TPU v7x, 32 devices: a whole 2x2x4 slice. The times are simulated.
32 devices in a mesh: fsdp: 16 (over z, y, x), dp: 2 (over core).
Axes of the slice: x: 2, y: 2, z: 4, core: 2. Of those that a mesh axis runs over, the one named last changes fastest.
Arguments:
- codons: int32 [16384], P(('fsdp', 'dp')), may hold values from 0 to 68
- masked: int32 [16384], P(('fsdp', 'dp')), may hold values from 0 to 1
- segments: int32 [16384], P(('fsdp', 'dp')), may hold values from 0 to 127, never falling along the last dimension, each value on 1 to 256 neighbouring positions
- inward: float32 [2, 768, 2304], P(None, 'fsdp'), may hold values from -0.21875 to 0.21875
- outward: float32 [2, 768, 768], P(None, 'fsdp'), may hold values from -0.875 to 0.875
- expand: float32 [2, 768, 3072], P(None, 'fsdp'), may hold values from -0.21875 to 0.21875
- shrink: float32 [2, 3072, 768], P(None, 'fsdp'), may hold values from -0.109375 to 0.109375
- codon_table: float32 [70, 768], P(None, 'fsdp'), may hold values from -0.21875 to 0.21875
- norm_params: float32 [5, 2, 768], P(None, None, 'fsdp'), may hold values from -0.9 to 2.5
- inward_first: float32 [2, 768, 2304], P(None, 'fsdp'), may hold values from -9.536743e-06 to 9.536743e-06
- inward_second: float32 [2, 768, 2304], P(None, 'fsdp'), may hold values from 9.143844e-12 to 3.7278746e-11
- outward_first: float32 [2, 768, 768], P(None, 'fsdp'), may hold values from -9.536743e-06 to 9.536743e-06
- outward_second: float32 [2, 768, 768], P(None, 'fsdp'), may hold values from 9.143844e-12 to 3.7278746e-11
- expand_first: float32 [2, 768, 3072], P(None, 'fsdp'), may hold values from -9.536743e-06 to 9.536743e-06
- expand_second: float32 [2, 768, 3072], P(None, 'fsdp'), may hold values from 9.143844e-12 to 3.7278746e-11
- shrink_first: float32 [2, 3072, 768], P(None, 'fsdp'), may hold values from -9.536743e-06 to 9.536743e-06
- shrink_second: float32 [2, 3072, 768], P(None, 'fsdp'), may hold values from 9.143844e-12 to 3.7278746e-11
- table_first: float32 [70, 768], P(None, 'fsdp'), may hold values from -9.536743e-06 to 9.536743e-06
- table_second: float32 [70, 768], P(None, 'fsdp'), may hold values from 9.143844e-12 to 3.7278746e-11
- norm_first: float32 [5, 2, 768], P(None, None, 'fsdp'), may hold values from -3.8146973e-05 to 3.8146973e-05
- norm_second: float32 [5, 2, 768], P(None, None, 'fsdp'), may hold values from 1.4770825e-10 to 5.978667e-10
Outputs:
- loss_sum: float32 [], replicated
- mask_count: float32 [], replicated
- grad_norm: float32 [], replicated
- inward_new: float32 [2, 768, 2304], P(None, 'fsdp')
- inward_moment: float32 [2, 768, 2304], P(None, 'fsdp')
- inward_square: float32 [2, 768, 2304], P(None, 'fsdp')
- outward_new: float32 [2, 768, 768], P(None, 'fsdp')
- outward_moment: float32 [2, 768, 768], P(None, 'fsdp')
- outward_square: float32 [2, 768, 768], P(None, 'fsdp')
- expand_new: float32 [2, 768, 3072], P(None, 'fsdp')
- expand_moment: float32 [2, 768, 3072], P(None, 'fsdp')
- expand_square: float32 [2, 768, 3072], P(None, 'fsdp')
- shrink_new: float32 [2, 3072, 768], P(None, 'fsdp')
- shrink_moment: float32 [2, 3072, 768], P(None, 'fsdp')
- shrink_square: float32 [2, 3072, 768], P(None, 'fsdp')
- table_new: float32 [70, 768], P(None, 'fsdp')
- table_moment: float32 [70, 768], P(None, 'fsdp')
- table_square: float32 [70, 768], P(None, 'fsdp')
- norm_new: float32 [5, 2, 768], P(None, None, 'fsdp')
- norm_moment: float32 [5, 2, 768], P(None, None, 'fsdp')
- norm_square: float32 [5, 2, 768], P(None, None, 'fsdp')
All inputs are finite; a program needn't handle non-finite values.
Results may differ from a plain program's by a relative error of at most 0.012.
The roundings to bfloat16 on the way count: a program that leaves them out, or rounds other values in their place, can miss the bound.
Values may be sent and summed in bfloat16 or wider, within the bound.
No kernel may reach another device: no remote copies, remote signals or barrier semaphores. Data moves between devices by JAX's collectives and lax.ppermute only.
A program may use at most 192 MiB of HBM per device.

v0:
```python
import jax
import jax.numpy as jnp
from jax import lax
from jax.sharding import PartitionSpec as P

HD = 64
V = 70
STEP = 10


NORM_EPS = 1e-05
BETA_ONE = 0.9
BETA_TWO = 0.95
ADAM_EPS = 1e-08
DECAY = 0.1
RATE_MATRIX = 0.05
RATE_VECTOR = 0.3
CLIP = 0.05


def rotary_tables(length, size):
    freq = 10000.0 ** (-jnp.arange(size // 2, dtype=jnp.float32) * 2.0 / size)
    angle = jnp.arange(length, dtype=jnp.float32)[:, None] * freq[None, :]
    return (jnp.cos(angle)[:, None, :], jnp.sin(angle)[:, None, :])


def rotate(value, cosine, sine):
    half = value.shape[-1] // 2
    first = value[..., :half]
    second = value[..., half:]
    return jnp.concatenate([first * cosine - second * sine, second * cosine + first * sine], -1)


def normalize(resid, gain, bias):
    mean = jnp.mean(resid, -1, keepdims=True)
    centred = resid - mean
    inverse = lax.rsqrt(jnp.mean(centred * centred, -1, keepdims=True) + NORM_EPS)
    unit = centred * inverse
    return (unit * gain + bias, unit, inverse)


def normalize_back(grad, unit, inverse, gain):
    scaled = grad * gain
    across = (
        scaled
        - jnp.mean(scaled, -1, keepdims=True)
        - unit * jnp.mean(scaled * unit, -1, keepdims=True)
    )
    return (across * inverse, jnp.sum(grad * unit, 0), jnp.sum(grad, 0))


def layer_pass(resid, weights, cosine, sine, same, kept_lse):
    w_in, w_out, w_up, w_down, gains = weights
    gains = gains.astype(jnp.float32)
    length = resid.shape[0]
    width = w_out.shape[0]
    heads = width // HD
    normed, unit_in, inverse_in = normalize(resid, gains[0, 0], gains[0, 1])
    normed_low = normed.astype(jnp.bfloat16)
    mixed = jnp.dot(normed_low, w_in, preferred_element_type=jnp.float32).reshape(
        length, 3, heads, HD
    )
    query = rotate(mixed[:, 0], cosine, sine).astype(jnp.bfloat16)
    keys = rotate(mixed[:, 1], cosine, sine).astype(jnp.bfloat16)
    values = mixed[:, 2].astype(jnp.bfloat16)
    scores = jnp.einsum("qhe,khe->hqk", query, keys, preferred_element_type=jnp.float32) * HD ** (
        -0.5
    )
    scores = jnp.where(same[None], scores, -1000000000.0)
    if kept_lse is None:
        top = jnp.max(scores, -1, keepdims=True)
        expo = jnp.exp(scores - top)
        total = jnp.sum(expo, -1, keepdims=True)
        probs = expo / total
        lse = top + jnp.log(total)
    else:
        probs = jnp.exp(scores - kept_lse)
        lse = kept_lse
    probs_low = probs.astype(jnp.bfloat16)
    attended = jnp.einsum("hqk,khe->qhe", probs_low, values, preferred_element_type=jnp.float32)
    attended = attended.astype(jnp.bfloat16).reshape(length, width)
    middle = resid + jnp.dot(attended, w_out, preferred_element_type=jnp.float32)
    normed_mid, unit_mid, inverse_mid = normalize(middle, gains[1, 0], gains[1, 1])
    normed_mid_low = normed_mid.astype(jnp.bfloat16)
    hidden = jnp.dot(normed_mid_low, w_up, preferred_element_type=jnp.float32)
    active = jax.nn.gelu(hidden).astype(jnp.bfloat16)
    output = middle + jnp.dot(active, w_down, preferred_element_type=jnp.float32)
    saved = (
        normed_low,
        unit_in,
        inverse_in,
        query,
        keys,
        values,
        probs,
        probs_low,
        attended,
        unit_mid,
        inverse_mid,
        normed_mid_low,
        hidden,
        active,
    )
    return (output, lse, saved)


def layer_back(resid, lse, weights, cosine, sine, same, grad_out):
    _, _, saved = layer_pass(resid, weights, cosine, sine, same, lse)
    (
        normed_low,
        unit_in,
        inverse_in,
        query,
        keys,
        values,
        probs,
        probs_low,
        attended,
        unit_mid,
        inverse_mid,
        normed_mid_low,
        hidden,
        active,
    ) = saved
    w_in, w_out, w_up, w_down, gains = weights
    gains = gains.astype(jnp.float32)
    length = resid.shape[0]
    width = w_out.shape[0]
    heads = width // HD
    branch_grad = grad_out.astype(jnp.bfloat16)
    grad_down = jnp.dot(active.T, branch_grad, preferred_element_type=jnp.float32)
    grad_active = jnp.dot(branch_grad, w_down.T, preferred_element_type=jnp.float32)
    _, gelu_back = jax.vjp(jax.nn.gelu, hidden)
    grad_hidden = gelu_back(grad_active)[0].astype(jnp.bfloat16)
    grad_up = jnp.dot(normed_mid_low.T, grad_hidden, preferred_element_type=jnp.float32)
    grad_normed_mid = jnp.dot(grad_hidden, w_up.T, preferred_element_type=jnp.float32)
    grad_middle, gain_mid, bias_mid = normalize_back(
        grad_normed_mid, unit_mid, inverse_mid, gains[1, 0]
    )
    grad_middle = grad_middle + grad_out
    attn_grad = grad_middle.astype(jnp.bfloat16)
    grad_wout = jnp.dot(attended.T, attn_grad, preferred_element_type=jnp.float32)
    grad_attended = jnp.dot(attn_grad, w_out.T, preferred_element_type=jnp.float32)
    grad_attended = grad_attended.astype(jnp.bfloat16).reshape(length, heads, HD)
    grad_probs = jnp.einsum(
        "qhe,khe->hqk", grad_attended, values, preferred_element_type=jnp.float32
    )
    grad_scores = probs * (grad_probs - jnp.sum(probs * grad_probs, -1, keepdims=True))
    grad_scores = grad_scores.astype(jnp.bfloat16)
    scale = HD ** (-0.5)
    grad_query = (
        jnp.einsum("hqk,khe->qhe", grad_scores, keys, preferred_element_type=jnp.float32) * scale
    )
    grad_keys = (
        jnp.einsum("hqk,qhe->khe", grad_scores, query, preferred_element_type=jnp.float32) * scale
    )
    grad_values = jnp.einsum(
        "hqk,qhe->khe", probs_low, grad_attended, preferred_element_type=jnp.float32
    )
    grad_mixed = jnp.stack(
        [rotate(grad_query, cosine, -sine), rotate(grad_keys, cosine, -sine), grad_values], 1
    )
    grad_mixed = grad_mixed.reshape(length, 3 * width).astype(jnp.bfloat16)
    grad_in = jnp.dot(normed_low.T, grad_mixed, preferred_element_type=jnp.float32)
    grad_normed = jnp.dot(grad_mixed, w_in.T, preferred_element_type=jnp.float32)
    grad_resid, gain_in, bias_in = normalize_back(grad_normed, unit_in, inverse_in, gains[0, 0])
    grad_gains = jnp.stack([jnp.stack([gain_in, bias_in]), jnp.stack([gain_mid, bias_mid])])
    return (grad_resid + grad_middle, grad_in, grad_wout, grad_up, grad_down, grad_gains)


def adam_step(master, grad, first, second, rate, decay):
    first = BETA_ONE * first + (1.0 - BETA_ONE) * grad
    second = BETA_TWO * second + (1.0 - BETA_TWO) * grad * grad
    fix_one = 1.0 - BETA_ONE**STEP
    fix_two = 1.0 - BETA_TWO**STEP
    update = first / fix_one / (jnp.sqrt(second / fix_two) + ADAM_EPS) + decay * master
    return (master - rate * update, first, second)


def body(
    codons,
    masked,
    segments,
    inward,
    outward,
    expand,
    shrink,
    codon_table,
    norm_params,
    inward_first,
    inward_second,
    outward_first,
    outward_second,
    expand_first,
    expand_second,
    shrink_first,
    shrink_second,
    table_first,
    table_second,
    norm_first,
    norm_second,
):
    layers = inward.shape[0]
    length = codons.shape[0]
    weight = masked.astype(jnp.float32)
    count = lax.psum(jnp.sum(weight), ("fsdp", "dp"))
    inputs = jnp.where(masked == 1, V - 1, codons)
    table_low, final_low = (
        lax.all_gather(codon_table.astype(jnp.bfloat16), "fsdp", axis=1, tiled=True),
        lax.all_gather(norm_params[2 * layers].astype(jnp.bfloat16), "fsdp", axis=1, tiled=True),
    )
    final_gain = final_low.astype(jnp.float32)
    cosine, sine = rotary_tables(length, HD)
    same = segments[:, None] == segments[None, :]
    vocab_ids = jnp.arange(V, dtype=jnp.int32)
    chosen = (inputs[:, None] == vocab_ids[None, :]).astype(jnp.bfloat16)
    start = jnp.dot(chosen, table_low, preferred_element_type=jnp.float32)
    layer_norms = norm_params[: 2 * layers].reshape((layers, 2) + norm_params.shape[1:])
    shards = (inward, outward, expand, shrink, layer_norms)

    def forward_step(resid, piece):
        w_in, w_out, w_up, w_down, gains = piece
        whole = (
            lax.all_gather(w_in.astype(jnp.bfloat16), "fsdp", axis=0, tiled=True),
            lax.all_gather(w_out.astype(jnp.bfloat16), "fsdp", axis=0, tiled=True),
            lax.all_gather(w_up.astype(jnp.bfloat16), "fsdp", axis=0, tiled=True),
            lax.all_gather(w_down.astype(jnp.bfloat16), "fsdp", axis=0, tiled=True),
            lax.all_gather(gains.astype(jnp.bfloat16), "fsdp", axis=2, tiled=True),
        )
        output, lse, _ = layer_pass(resid, whole, cosine, sine, same, None)
        return (output, (resid, lse))

    final_resid, kept = lax.scan(forward_step, start, shards)
    normed_out, unit_out, inverse_out = normalize(final_resid, final_gain[0], final_gain[1])
    head_in = normed_out.astype(jnp.bfloat16)
    logits = jnp.einsum("sd,vd->sv", head_in, table_low, preferred_element_type=jnp.float32)
    top = jnp.max(logits, -1, keepdims=True)
    lse_head = top + jnp.log(jnp.sum(jnp.exp(logits - top), -1, keepdims=True))
    targets = (codons[:, None] == vocab_ids[None, :]).astype(jnp.float32)
    picked = jnp.sum(logits * targets, -1)
    loss_local = jnp.sum((lse_head[:, 0] - picked) * weight)
    grad_logits = ((jnp.exp(logits - lse_head) - targets) * weight[:, None]).astype(jnp.bfloat16)
    grad_table = jnp.einsum("sv,sd->vd", grad_logits, head_in, preferred_element_type=jnp.float32)
    grad_head = jnp.dot(grad_logits, table_low, preferred_element_type=jnp.float32)
    grad_top, grad_final_gain, grad_final_bias = normalize_back(
        grad_head, unit_out, inverse_out, final_gain[0]
    )

    def backward_step(grad, item):
        piece, (resid, lse) = item
        w_in, w_out, w_up, w_down, gains = piece
        whole = (
            lax.all_gather(w_in.astype(jnp.bfloat16), "fsdp", axis=0, tiled=True),
            lax.all_gather(w_out.astype(jnp.bfloat16), "fsdp", axis=0, tiled=True),
            lax.all_gather(w_up.astype(jnp.bfloat16), "fsdp", axis=0, tiled=True),
            lax.all_gather(w_down.astype(jnp.bfloat16), "fsdp", axis=0, tiled=True),
            lax.all_gather(gains.astype(jnp.bfloat16), "fsdp", axis=2, tiled=True),
        )
        grad_resid, grad_in, grad_wout, grad_up, grad_down, grad_gains = layer_back(
            resid, lse, whole, cosine, sine, same, grad
        )
        shares = (
            lax.psum_scatter(grad_in, "fsdp", scatter_dimension=0, tiled=True),
            lax.psum_scatter(grad_wout, "fsdp", scatter_dimension=0, tiled=True),
            lax.psum_scatter(grad_up, "fsdp", scatter_dimension=0, tiled=True),
            lax.psum_scatter(grad_down, "fsdp", scatter_dimension=0, tiled=True),
            lax.psum_scatter(grad_gains, "fsdp", scatter_dimension=2, tiled=True),
        )
        return (grad_resid, shares)

    grad_start, layer_shares = lax.scan(backward_step, grad_top, (shards, kept), reverse=True)
    grad_table = grad_table + jnp.einsum(
        "sv,sd->vd", chosen, grad_start.astype(jnp.bfloat16), preferred_element_type=jnp.float32
    )
    table_share, final_share = (
        lax.psum_scatter(grad_table, "fsdp", scatter_dimension=1, tiled=True),
        lax.psum_scatter(
            jnp.stack([grad_final_gain, grad_final_bias]), "fsdp", scatter_dimension=1, tiled=True
        ),
    )
    share_in, share_out, share_up, share_down, share_norms = layer_shares
    share_in, share_out, share_up, share_down, share_norms, table_share, final_share = lax.psum(
        (share_in, share_out, share_up, share_down, share_norms, table_share, final_share), "dp"
    )
    norm_sums = jnp.concatenate(
        [share_norms.reshape((2 * layers,) + share_norms.shape[2:]), final_share[None]], 0
    )
    group = (share_in, share_out, share_up, share_down, table_share, norm_sums)
    squares = jnp.zeros((), jnp.float32)
    for grad in group:
        squares = squares + jnp.sum(grad * grad)
    loss_sum = lax.psum(loss_local, ("fsdp", "dp"))
    square_total = lax.psum(squares, "fsdp")
    grad_norm = jnp.sqrt(square_total) / count
    factor = CLIP / jnp.maximum(grad_norm, CLIP)
    masters = (inward, outward, expand, shrink, codon_table, norm_params)
    firsts = (inward_first, outward_first, expand_first, shrink_first, table_first, norm_first)
    seconds = (
        inward_second,
        outward_second,
        expand_second,
        shrink_second,
        table_second,
        norm_second,
    )
    result = [loss_sum, count, grad_norm]
    for index in range(6):
        rate = RATE_VECTOR if index == 5 else RATE_MATRIX
        decay = 0.0 if index == 5 else DECAY
        clipped = group[index] / count * factor
        result.extend(
            adam_step(masters[index], clipped, firsts[index], seconds[index], rate, decay)
        )
    return tuple(result)


def solution(mesh):
    in_specs = (
        P(("fsdp", "dp")),
        P(("fsdp", "dp")),
        P(("fsdp", "dp")),
        P(None, "fsdp", None),
        P(None, "fsdp", None),
        P(None, "fsdp", None),
        P(None, "fsdp", None),
        P(None, "fsdp"),
        P(None, None, "fsdp"),
        P(None, "fsdp", None),
        P(None, "fsdp", None),
        P(None, "fsdp", None),
        P(None, "fsdp", None),
        P(None, "fsdp", None),
        P(None, "fsdp", None),
        P(None, "fsdp", None),
        P(None, "fsdp", None),
        P(None, "fsdp"),
        P(None, "fsdp"),
        P(None, None, "fsdp"),
        P(None, None, "fsdp"),
    )
    out_specs = (
        P(),
        P(),
        P(),
        P(None, "fsdp", None),
        P(None, "fsdp", None),
        P(None, "fsdp", None),
        P(None, "fsdp", None),
        P(None, "fsdp", None),
        P(None, "fsdp", None),
        P(None, "fsdp", None),
        P(None, "fsdp", None),
        P(None, "fsdp", None),
        P(None, "fsdp", None),
        P(None, "fsdp", None),
        P(None, "fsdp", None),
        P(None, "fsdp"),
        P(None, "fsdp"),
        P(None, "fsdp"),
        P(None, None, "fsdp"),
        P(None, None, "fsdp"),
        P(None, None, "fsdp"),
    )
    return jax.shard_map(body, mesh=mesh, in_specs=in_specs, out_specs=out_specs, check_vma=False)
```

profile of v0, /device:TPU:0, one launch (start us, length us, event | category | flops | bytes accessed | tf_op | source)
XLA Modules:
  0.0 3370.6 jit_solution(12549617299005766116)
XLA Ops:
  11.5 43.4 %all_gather.66 = bf16[70,768]{0,1:T(8,128)(2,1)S(1)} all-gather(bf16[70,48]{0,1:T(8,128)(2,1)S(1)} %convert_element_type.300), channel_id=1, replica_groups=mesh['fsdp'=16,'dp'=2] {'fsdp'}, dimensions={1}, use_global_device_ids=true | all-gather | bytes 114240 | tf_op jit(solution)/shard_map/all_gather | solution.py:209
  54.9 37.8 %all-gather = bf16[1,2,768]{1,0,2:T(2,128)(2,1)S(1)} all-gather(bf16[1,2,48]{1,0,2:T(2,128)(2,1)S(1)} %copy.117), channel_id=2, replica_groups=mesh['fsdp'=16,'dp'=2] {'fsdp'}, dimensions={2}, use_global_device_ids=true | all-gather | bytes 3264 | tf_op jit(solution)/shard_map/all_gather | solution.py:210
  102.0 628.1 %while.44 = (s32[]{:T(128)}, f32[512,768]{1,0:T(8,128)S(1)}, f32[2,512,768]{2,1,0:T(8,128)}, f32[2,12,512,1]{2,1,3,0:T(8,128)S(1)}, bf16[2,2,2,48]{2,1,0,3:T(2,1...) while((s32[]{:T(128)}, f32[512,768]{1,0:T(8,128)S(1)}, ...), condition=%wide.region_7.8_spmd.clone.clone.clone, body=%wide.region_0.7_spmd.clone.clone.clone.sunk | while | flops 8119793664 | bytes 160984688 | solution.py:233
  124.7 41.3 %all-gather.42 = bf16[1,2,2,768]{2,1,0,3:T(2,128)(2,1)S(1)} all-gather(bf16[1,2,2,48]{2,1,0,3:T(2,128)(2,1)S(1)} %dynamic-slice_convert_fusion.21), channel_id=3, replica_groups=mesh['fsdp'=16,'dp'=2] {'fsdp'}, dimensions={3}, use_global_device_ids=true | all-gather | bytes 6528 | tf_op jit(solution)/shard_map/while/body/eval_jaxpr/all_gather | solution.py:228
  168.4 10.7 slice_reduce_fusion.12
  179.1 14.1 all-gather.60.cloned.1.call-done
  204.9 5.7 fusion.215
  210.6 41.1 %all-gather.62.cloned.1.call-done = bf16[1,768,768]{2,1,0:T(8,128)(2,1)} async-done(((bf16[1,48,768]{2,1,0:T(8,128)(2,1)}), bf16[1,768,768]{2,1,0:T(8,128)(2,1)}) %all-gather.62.cloned.1.call-update) | async-done | bytes 1179664 | tf_op jit(solution)/shard_map/while/body/eval_jaxpr/all_gather | solution.py:225
  254.5 80.4 %all-gather.64.cloned.1.call-done = bf16[1,768,3072]{2,1,0:T(8,128)(2,1)} async-done(((bf16[1,48,3072]{2,1,0:T(8,128)(2,1)}), bf16[1,768,3072]{2,1,0:T(8,128)(2,1)}) %all-gather.64.cloned.1.call-update) | async-done | bytes 4718608 | tf_op jit(solution)/shard_map/while/body/eval_jaxpr/all_gather | solution.py:226
  334.9 7.8 fusion.217
  342.7 74.9 %all-gather.66.cloned.1.call-done = bf16[1,3072,768]{2,1,0:T(8,128)(2,1)} async-done(((bf16[1,192,768]{2,1,0:T(8,128)(2,1)}), bf16[1,3072,768]{2,1,0:T(8,128)(2,1)}) %all-gather.66.cloned.1.call-update) | async-done | bytes 4718608 | tf_op jit(solution)/shard_map/while/body/eval_jaxpr/all_gather | solution.py:227
  417.6 6.0 fusion.218
  429.6 42.3 %all-gather.42 = bf16[1,2,2,768]{2,1,0,3:T(2,128)(2,1)S(1)} all-gather(bf16[1,2,2,48]{2,1,0,3:T(2,128)(2,1)S(1)} %dynamic-slice_convert_fusion.21), channel_id=3, replica_groups=mesh['fsdp'=16,'dp'=2] {'fsdp'}, dimensions={3}, use_global_device_ids=true | all-gather | bytes 6528 | tf_op jit(solution)/shard_map/while/body/eval_jaxpr/all_gather | solution.py:228
  474.3 10.7 slice_reduce_fusion.12
  485.0 14.3 all-gather.60.cloned.1.call-done
  511.1 5.7 fusion.215
  516.8 40.9 %all-gather.62.cloned.1.call-done = bf16[1,768,768]{2,1,0:T(8,128)(2,1)} async-done(((bf16[1,48,768]{2,1,0:T(8,128)(2,1)}), bf16[1,768,768]{2,1,0:T(8,128)(2,1)}) %all-gather.62.cloned.1.call-update) | async-done | bytes 1179664 | tf_op jit(solution)/shard_map/while/body/eval_jaxpr/all_gather | solution.py:225
  560.5 80.4 %all-gather.64.cloned.1.call-done = bf16[1,768,3072]{2,1,0:T(8,128)(2,1)} async-done(((bf16[1,48,3072]{2,1,0:T(8,128)(2,1)}), bf16[1,768,3072]{2,1,0:T(8,128)(2,1)}) %all-gather.64.cloned.1.call-update) | async-done | bytes 4718608 | tf_op jit(solution)/shard_map/while/body/eval_jaxpr/all_gather | solution.py:226
  640.8 7.8 fusion.217
  648.7 75.1 %all-gather.66.cloned.1.call-done = bf16[1,3072,768]{2,1,0:T(8,128)(2,1)} async-done(((bf16[1,192,768]{2,1,0:T(8,128)(2,1)}), bf16[1,3072,768]{2,1,0:T(8,128)(2,1)}) %all-gather.66.cloned.1.call-update) | async-done | bytes 4718608 | tf_op jit(solution)/shard_map/while/body/eval_jaxpr/all_gather | solution.py:227
  723.7 6.0 fusion.218
  743.1 2253.9 %while.45 = (s32[]{:T(128)}, f32[512,768]{1,0:T(8,128)}, f32[2,48,2304]{2,1,0:T(8,128)}, f32[2,48,768]{2,1,0:T(8,128)}, f32[2,48,3072]{2,1,0:T(8,128)}, /*index=...) while((s32[]{:T(128)}, f32[512,768]{1,0:T(8,128)}, ...), condition=%wide.region_38.39_spmd.clone.clone.clone, body=%wide.region_19.38_spmd.clone.clone.clone.sunk | while | flops 21894955008 | bytes 646272320 | solution.py:271
  749.4 42.1 %all-gather.47 = bf16[1,2,2,768]{2,1,0,3:T(2,128)(2,1)S(1)} all-gather(bf16[1,2,2,48]{2,1,0,3:T(2,128)(2,1)S(1)} %dynamic-slice_convert_fusion.26), channel_id=8, replica_groups=mesh['fsdp'=16,'dp'=2] {'fsdp'}, dimensions={3}, use_global_device_ids=true | all-gather | bytes 6528 | tf_op jit(solution)/shard_map/while/body/eval_jaxpr/all_gather | solution.py:257
  797.7 11.2 slice_reduce_fusion.13
  808.8 9.9 all-gather.68.cloned.1.call-done
  839.4 37.7 %all-gather.70.cloned.1.call-done = bf16[1,768,768]{2,1,0:T(8,128)(2,1)} async-done(((bf16[1,48,768]{2,1,0:T(8,128)(2,1)}), bf16[1,768,768]{2,1,0:T(8,128)(2,1)}) %all-gather.70.cloned.1.call-update) | async-done | bytes 1179664 | tf_op jit(solution)/shard_map/while/body/eval_jaxpr/all_gather | solution.py:254
  880.6 79.6 %all-gather.72.cloned.1.call-done = bf16[1,768,3072]{2,1,0:T(8,128)(2,1)} async-done(((bf16[1,48,3072]{2,1,0:T(8,128)(2,1)}), bf16[1,768,3072]{2,1,0:T(8,128)(2,1)}) %all-gather.72.cloned.1.call-update) | async-done | bytes 4718608 | tf_op jit(solution)/shard_map/while/body/eval_jaxpr/all_gather | solution.py:255
  960.2 8.6 fusion.245
  968.8 74.1 %all-gather.74.cloned.1.call-done = bf16[1,3072,768]{2,1,0:T(8,128)(2,1)} async-done(((bf16[1,192,768]{2,1,0:T(8,128)(2,1)}), bf16[1,3072,768]{2,1,0:T(8,128)(2,1)}) %all-gather.74.cloned.1.call-update) | async-done | bytes 4718608 | tf_op jit(solution)/shard_map/while/body/eval_jaxpr/all_gather | solution.py:256
  1042.9 9.6 fusion.246
  1061.6 8.9 convolution_bitcast_fusion.2
  1070.5 10.0 multiply_reduce_fusion.34
  1080.5 7.0 multiply_convert_fusion.9
  1108.0 7.3 fusion.247
  1115.7 10.7 fusion.250
  1127.1 7.4 fusion.249
  1139.0 85.1 %reduce-scatter.26.cloned.1.call-done = f32[48,4]{1,0:T(8,128)} async-done(((f32[768,4]{1,0:T(8,128)}), f32[48,4]{1,0:T(8,128)}) %reduce-scatter.26.cloned.1.call-update) | async-done | bytes 784 | tf_op jit(solution)/shard_map/while
  1225.1 131.4 %reduce-scatter.20.cloned.1.call-done = f32[48,768]{1,0:T(8,128)} async-done(((f32[768,768]{1,0:T(8,128)}), f32[48,768]{1,0:T(8,128)}) %reduce-scatter.20.cloned.1.call-update) | async-done | bytes 147472 | tf_op jit(solution)/shard_map/while/body/eval_jaxpr/reduce_scatter | solution.py:264
  1357.5 155.8 %reduce-scatter.18.cloned.1.call-done = f32[48,2304]{1,0:T(8,128)} async-done(((f32[768,2304]{1,0:T(8,128)}), f32[48,2304]{1,0:T(8,128)}) %reduce-scatter.18.cloned.1.call-update) | async-done | bytes 442384 | tf_op jit(solution)/shard_map/while/body/eval_jaxpr/reduce_scatter | solution.py:263
  1515.2 174.2 %reduce-scatter.24.cloned.1.call-done = f32[192,768]{1,0:T(8,128)} async-done(((f32[3072,768]{1,0:T(8,128)}), f32[192,768]{1,0:T(8,128)}) %reduce-scatter.24.cloned.1.call-update) | async-done | bytes 589840 | tf_op jit(solution)/shard_map/while/body/eval_jaxpr/reduce_scatter | solution.py:266
  1691.3 173.5 %reduce-scatter.22.cloned.1.call-done = f32[48,3072]{1,0:T(8,128)} async-done(((f32[768,3072]{1,0:T(8,128)}), f32[48,3072]{1,0:T(8,128)}) %reduce-scatter.22.cloned.1.call-update) | async-done | bytes 589840 | tf_op jit(solution)/shard_map/while/body/eval_jaxpr/reduce_scatter | solution.py:265
  1873.5 42.1 %all-gather.47 = bf16[1,2,2,768]{2,1,0,3:T(2,128)(2,1)S(1)} all-gather(bf16[1,2,2,48]{2,1,0,3:T(2,128)(2,1)S(1)} %dynamic-slice_convert_fusion.26), channel_id=8, replica_groups=mesh['fsdp'=16,'dp'=2] {'fsdp'}, dimensions={3}, use_global_device_ids=true | all-gather | bytes 6528 | tf_op jit(solution)/shard_map/while/body/eval_jaxpr/all_gather | solution.py:257
  1921.9 11.2 slice_reduce_fusion.13
  1933.0 10.0 all-gather.68.cloned.1.call-done
  1963.6 37.9 %all-gather.70.cloned.1.call-done = bf16[1,768,768]{2,1,0:T(8,128)(2,1)} async-done(((bf16[1,48,768]{2,1,0:T(8,128)(2,1)}), bf16[1,768,768]{2,1,0:T(8,128)(2,1)}) %all-gather.70.cloned.1.call-update) | async-done | bytes 1179664 | tf_op jit(solution)/shard_map/while/body/eval_jaxpr/all_gather | solution.py:254
  2005.1 79.4 %all-gather.72.cloned.1.call-done = bf16[1,768,3072]{2,1,0:T(8,128)(2,1)} async-done(((bf16[1,48,3072]{2,1,0:T(8,128)(2,1)}), bf16[1,768,3072]{2,1,0:T(8,128)(2,1)}) %all-gather.72.cloned.1.call-update) | async-done | bytes 4718608 | tf_op jit(solution)/shard_map/while/body/eval_jaxpr/all_gather | solution.py:255
  2084.5 8.6 fusion.245
  2093.0 74.3 %all-gather.74.cloned.1.call-done = bf16[1,3072,768]{2,1,0:T(8,128)(2,1)} async-done(((bf16[1,192,768]{2,1,0:T(8,128)(2,1)}), bf16[1,3072,768]{2,1,0:T(8,128)(2,1)}) %all-gather.74.cloned.1.call-update) | async-done | bytes 4718608 | tf_op jit(solution)/shard_map/while/body/eval_jaxpr/all_gather | solution.py:256
  2167.3 9.3 fusion.246
  2185.7 8.9 convolution_bitcast_fusion.2
  2194.7 10.3 multiply_reduce_fusion.34
  2205.0 7.0 multiply_convert_fusion.9
  2232.5 7.3 fusion.247
  2240.1 10.7 fusion.250
  2251.5 7.4 fusion.249
  2263.4 85.0 %reduce-scatter.26.cloned.1.call-done = f32[48,4]{1,0:T(8,128)} async-done(((f32[768,4]{1,0:T(8,128)}), f32[48,4]{1,0:T(8,128)}) %reduce-scatter.26.cloned.1.call-update) | async-done | bytes 784 | tf_op jit(solution)/shard_map/while
  2349.4 131.6 %reduce-scatter.20.cloned.1.call-done = f32[48,768]{1,0:T(8,128)} async-done(((f32[768,768]{1,0:T(8,128)}), f32[48,768]{1,0:T(8,128)}) %reduce-scatter.20.cloned.1.call-update) | async-done | bytes 147472 | tf_op jit(solution)/shard_map/while/body/eval_jaxpr/reduce_scatter | solution.py:264
  2482.0 155.6 %reduce-scatter.18.cloned.1.call-done = f32[48,2304]{1,0:T(8,128)} async-done(((f32[768,2304]{1,0:T(8,128)}), f32[48,2304]{1,0:T(8,128)}) %reduce-scatter.18.cloned.1.call-update) | async-done | bytes 442384 | tf_op jit(solution)/shard_map/while/body/eval_jaxpr/reduce_scatter | solution.py:263
  2639.4 174.5 %reduce-scatter.24.cloned.1.call-done = f32[192,768]{1,0:T(8,128)} async-done(((f32[3072,768]{1,0:T(8,128)}), f32[192,768]{1,0:T(8,128)}) %reduce-scatter.24.cloned.1.call-update) | async-done | bytes 589840 | tf_op jit(solution)/shard_map/while/body/eval_jaxpr/reduce_scatter | solution.py:266
  2815.9 173.8 %reduce-scatter.22.cloned.1.call-done = f32[48,3072]{1,0:T(8,128)} async-done(((f32[768,3072]{1,0:T(8,128)}), f32[48,3072]{1,0:T(8,128)}) %reduce-scatter.22.cloned.1.call-update) | async-done | bytes 589840 | tf_op jit(solution)/shard_map/while/body/eval_jaxpr/reduce_scatter | solution.py:265
  3001.3 122.3 %reduce-scatter.16.cloned.1.call-done = f32[48,2]{1,0:T(8,128)} async-done(((f32[768,2]{1,0:T(8,128)}), f32[48,2]{1,0:T(8,128)}) %reduce-scatter.16.cloned.1.call-update) | async-done | bytes 400
  3124.4 124.9 %reduce-scatter.14.cloned.1.call-done = f32[70,48]{0,1:T(8,128)} async-done(((f32[70,768]{0,1:T(8,128)}), f32[70,48]{0,1:T(8,128)}) %reduce-scatter.14.cloned.1.call-update) | async-done | bytes 13456 | tf_op jit(solution)/shard_map/reduce_scatter | solution.py:276
  3263.2 40.4 %all-reduce = (f32[]{:T(128)}, f32[]{:T(128)}) all-reduce(f32[]{:T(128)} %get-tuple-element.847, f32[]{:T(128)} %get-tuple-element.846), channel_id=1, replica_groups=mesh['fsdp'=16,'dp'=2] {'fsdp','dp'}, use_global_device_ids=true, to_apply=%region_14.15 | all-reduce | flops 2 | bytes 16 | tf_op jit(solution)/shard_map/psum | solution.py:292
  3303.6 40.5 %psum.79 = f32[]{:T(128)} all-reduce(f32[]{:T(128)S(6)} %add.426), channel_id=1, replica_groups=mesh['fsdp'=16,'dp'=2] {'fsdp'}, use_global_device_ids=true, to_apply=%region_56.57 | all-reduce | flops 1 | bytes 8 | tf_op jit(solution)/shard_map/psum | solution.py:293
  (561 shorter events, 259.8 us)
Async XLA Ops:
  8.0 90.2 %copy-start.39 = (f32[2,48,2304]{2,1,0:T(8,128)S(1)}, f32[2,48,2304]{2,1,0:T(8,128)}, u32[]{:S(2)}) copy-start(f32[2,48,2304]{2,1,0:T(8,128)} %param.28) | copy-start | bytes 2654212
  54.9 46.6 %copy-start.43 = (bf16[70,768]{0,1:T(8,128)(2,1)}, bf16[70,768]{0,1:T(8,128)(2,1)S(1)}, u32[]{:S(2)}) copy-start(bf16[70,768]{0,1:T(8,128)(2,1)S(1)} %all_gather.66) | copy-start | bytes 322564
  54.9 44.2 %copy-start.32 = (f32[2,48,3072]{2,1,0:T(8,128)S(1)}, f32[2,48,3072]{2,1,0:T(8,128)}, u32[]{:S(2)}) copy-start(f32[2,48,3072]{2,1,0:T(8,128)} %param.30) | copy-start | bytes 3538948
  118.7 74.6 %all-gather.60.cloned.1.call-start = ((), (), s32[]{:S(2)}) async-start(), calls=%async_computation.10 | async-start | bytes 3760128 | tf_op jit(solution)/shard_map/while/body/eval_jaxpr/all_gather | solution.py:224
  120.4 131.3 %all-gather.62.cloned.1.call-start = ((), (), s32[]{:S(2)}) async-start(), calls=%async_computation.11 | async-start | bytes 1253376 | tf_op jit(solution)/shard_map/while/body/eval_jaxpr/all_gather | solution.py:225
  121.1 213.7 %all-gather.64.cloned.1.call-start = ((), (), s32[]{:S(2)}) async-start(), calls=%async_computation.12 | async-start | bytes 5013504 | tf_op jit(solution)/shard_map/while/body/eval_jaxpr/all_gather | solution.py:226
  122.9 294.7 %all-gather.66.cloned.1.call-start = ((), (), s32[]{:S(2)}) async-start(), calls=%async_computation.13 | async-start | bytes 5013504 | tf_op jit(solution)/shard_map/while/body/eval_jaxpr/all_gather | solution.py:227
  423.6 75.8 %all-gather.60.cloned.1.call-start = ((), (), s32[]{:S(2)}) async-start(), calls=%async_computation.10 | async-start | bytes 3760128 | tf_op jit(solution)/shard_map/while/body/eval_jaxpr/all_gather | solution.py:224
  425.3 132.4 %all-gather.62.cloned.1.call-start = ((), (), s32[]{:S(2)}) async-start(), calls=%async_computation.11 | async-start | bytes 1253376 | tf_op jit(solution)/shard_map/while/body/eval_jaxpr/all_gather | solution.py:225
  426.0 214.8 %all-gather.64.cloned.1.call-start = ((), (), s32[]{:S(2)}) async-start(), calls=%async_computation.12 | async-start | bytes 5013504 | tf_op jit(solution)/shard_map/while/body/eval_jaxpr/all_gather | solution.py:226
  427.8 295.9 %all-gather.66.cloned.1.call-start = ((), (), s32[]{:S(2)}) async-start(), calls=%async_computation.13 | async-start | bytes 5013504 | tf_op jit(solution)/shard_map/while/body/eval_jaxpr/all_gather | solution.py:227
  743.2 48.2 %copy-start.28 = (bf16[2,48,768]{2,1,0:T(8,128)(2,1)}, bf16[2,48,768]{2,1,0:T(8,128)(2,1)S(1)}, u32[]{:S(2)}) copy-start(bf16[2,48,768]{2,1,0:T(8,128)(2,1)S(1)} %get-tuple-element.1347) | copy-start | bytes 442372 | tf_op jit(solution)/shard_map/while
  743.3 48.2 %copy-start.41 = (bf16[2,2,2,48]{2,1,0,3:T(2,128)(2,1)}, bf16[2,2,2,48]{2,1,0,3:T(2,128)(2,1)S(1)}, u32[]{:S(2)}) copy-start(bf16[2,2,2,48]{2,1,0,3:T(2,128)(2,1)S(1)} %get-tuple-element.1343) | copy-start | bytes 2308 | tf_op jit(solution)/shard_map/while
  743.3 49.8 %copy-start.57 = (f32[2,12,512,1]{2,1,3,0:T(8,128)}, f32[2,12,512,1]{2,1,3,0:T(8,128)S(1)}, u32[]{:S(2)}) copy-start(f32[2,12,512,1]{2,1,3,0:T(8,128)S(1)} %get-tuple-element.1345) | copy-start | bytes 147460 | tf_op jit(solution)/shard_map/while
  743.3 52.2 %copy-start.70 = (f32[32]{0:T(128)}, f32[32]{0:T(128)S(1)}, u32[]{:S(2)}) copy-start(f32[32]{0:T(128)S(1)} %get-tuple-element.1349) | copy-start | bytes 388 | tf_op jit(solution)/shard_map/while
  743.3 75.5 %all-gather.68.cloned.1.call-start = ((), (), s32[]{:S(2)}) async-start(), calls=%async_computation.14 | async-start | bytes 3760128 | tf_op jit(solution)/shard_map/while/body/eval_jaxpr/all_gather | solution.py:253
  745.0 132.0 %all-gather.70.cloned.1.call-start = ((), (), s32[]{:S(2)}) async-start(), calls=%async_computation.15 | async-start | bytes 1253376 | tf_op jit(solution)/shard_map/while/body/eval_jaxpr/all_gather | solution.py:254
  745.7 214.5 %all-gather.72.cloned.1.call-start = ((), (), s32[]{:S(2)}) async-start(), calls=%async_computation.16 | async-start | bytes 5013504 | tf_op jit(solution)/shard_map/while/body/eval_jaxpr/all_gather | solution.py:255
  747.5 295.4 %all-gather.74.cloned.1.call-start = ((), (), s32[]{:S(2)}) async-start(), calls=%async_computation.17 | async-start | bytes 5013504 | tf_op jit(solution)/shard_map/while/body/eval_jaxpr/all_gather | solution.py:256
  749.3 474.9 %reduce-scatter.26.cloned.1.call-start = ((), (), s32[]{:S(2)}) async-start(), calls=%async_computation.22 | async-start | bytes 417792 | tf_op jit(solution)/shard_map/while
  960.2 82.7 %copy-start.11 = (f32[512,768]{1,0:T(8,128)S(1)}, f32[512,768]{1,0:T(8,128)}, u32[]{:S(2)}) copy-start(f32[512,768]{1,0:T(8,128)} %get-tuple-element.1319) | copy-start | bytes 4718596 | tf_op jit(solution)/shard_map/while
  1104.0 252.5 %reduce-scatter.20.cloned.1.call-start = ((), (), s32[]{:S(2)}) async-start(), calls=%async_computation.19 | async-start | bytes 2506752 | tf_op jit(solution)/shard_map/while/body/eval_jaxpr/reduce_scatter | solution.py:264
  1107.4 405.9 %reduce-scatter.18.cloned.1.call-start = ((), (), s32[]{:S(2)}) async-start(), calls=%async_computation.18 | async-start | bytes 7520256 | tf_op jit(solution)/shard_map/while/body/eval_jaxpr/reduce_scatter | solution.py:263
  1115.4 573.9 %reduce-scatter.24.cloned.1.call-start = ((), (), s32[]{:S(2)}) async-start(), calls=%async_computation.21 | async-start | bytes 10027008 | tf_op jit(solution)/shard_map/while/body/eval_jaxpr/reduce_scatter | solution.py:266
  1126.4 738.4 %reduce-scatter.22.cloned.1.call-start = ((), (), s32[]{:S(2)}) async-start(), calls=%async_computation.20 | async-start | bytes 10027008 | tf_op jit(solution)/shard_map/while/body/eval_jaxpr/reduce_scatter | solution.py:265
  1135.9 89.2 %copy-start.78 = (f32[2,2,2,48]{3,2,1,0:T(2,128)S(1)}, f32[2,2,2,48]{3,2,1,0:T(2,128)}, u32[]{:S(2)}) copy-start(f32[2,2,2,48]{3,2,1,0:T(2,128)} %get-tuple-element.1324) | copy-start | bytes 4612 | tf_op jit(solution)/shard_map/while
  1135.9 220.7 %copy-start.52 = (f32[2,48,768]{2,1,0:T(8,128)S(1)}, f32[2,48,768]{2,1,0:T(8,128)}, u32[]{:S(2)}) copy-start(f32[2,48,768]{2,1,0:T(8,128)} %get-tuple-element.1321) | copy-start | bytes 884740 | tf_op jit(solution)/shard_map/while
  1139.0 725.8 %copy-start.36 = (f32[2,48,3072]{2,1,0:T(8,128)S(1)}, f32[2,48,3072]{2,1,0:T(8,128)}, u32[]{:S(2)}) copy-start(f32[2,48,3072]{2,1,0:T(8,128)} %get-tuple-element.1322) | copy-start | bytes 3538948 | tf_op jit(solution)/shard_map/while
  1225.1 640.8 %copy-start.79 = (f32[2,2,2,48]{3,2,1,0:T(2,128)}, f32[2,2,2,48]{3,2,1,0:T(2,128)S(1)}, u32[]{:S(2)}) copy-start(f32[2,2,2,48]{3,2,1,0:T(2,128)S(1)} %constant_dynamic-update-slice_fusion.4) | copy-start | bytes 4612 | tf_op jit(solution)/shard_map/while
  1357.5 155.9 %copy-start.53 = (f32[2,48,768]{2,1,0:T(8,128)}, f32[2,48,768]{2,1,0:T(8,128)S(1)}, u32[]{:S(2)}) copy-start(f32[2,48,768]{2,1,0:T(8,128)S(1)} %bitcast_dynamic-update-slice_fusion.15) | copy-start | bytes 884740 | tf_op jit(solution)/shard_map/while
  1513.3 353.6 %copy-start.29 = (bf16[2,48,768]{2,1,0:T(8,128)(2,1)S(1)}, bf16[2,48,768]{2,1,0:T(8,128)(2,1)}, u32[]{:S(2)}) copy-start(bf16[2,48,768]{2,1,0:T(8,128)(2,1)} %copy-done.28) | copy-start | bytes 442372 | tf_op jit(solution)/shard_map/while
  1513.3 353.6 %copy-start.42 = (bf16[2,2,2,48]{2,1,0,3:T(2,128)(2,1)S(1)}, bf16[2,2,2,48]{2,1,0,3:T(2,128)(2,1)}, u32[]{:S(2)}) copy-start(bf16[2,2,2,48]{2,1,0,3:T(2,128)(2,1)} %copy-done.41) | copy-start | bytes 2308 | tf_op jit(solution)/shard_map/while
  1513.3 353.6 %copy-start.58 = (f32[2,12,512,1]{2,1,3,0:T(8,128)S(1)}, f32[2,12,512,1]{2,1,3,0:T(8,128)}, u32[]{:S(2)}) copy-start(f32[2,12,512,1]{2,1,3,0:T(8,128)} %copy-done.57) | copy-start | bytes 147460 | tf_op jit(solution)/shard_map/while
  1513.3 353.6 %copy-start.71 = (f32[32]{0:T(128)S(1)}, f32[32]{0:T(128)}, u32[]{:S(2)}) copy-start(f32[32]{0:T(128)} %copy-done.70) | copy-start | bytes 388 | tf_op jit(solution)/shard_map/while
  1867.4 48.2 %copy-start.28 = (bf16[2,48,768]{2,1,0:T(8,128)(2,1)}, bf16[2,48,768]{2,1,0:T(8,128)(2,1)S(1)}, u32[]{:S(2)}) copy-start(bf16[2,48,768]{2,1,0:T(8,128)(2,1)S(1)} %get-tuple-element.1347) | copy-start | bytes 442372 | tf_op jit(solution)/shard_map/while
  1867.4 48.2 %copy-start.41 = (bf16[2,2,2,48]{2,1,0,3:T(2,128)(2,1)}, bf16[2,2,2,48]{2,1,0,3:T(2,128)(2,1)S(1)}, u32[]{:S(2)}) copy-start(bf16[2,2,2,48]{2,1,0,3:T(2,128)(2,1)S(1)} %get-tuple-element.1343) | copy-start | bytes 2308 | tf_op jit(solution)/shard_map/while
  1867.4 49.8 %copy-start.57 = (f32[2,12,512,1]{2,1,3,0:T(8,128)}, f32[2,12,512,1]{2,1,3,0:T(8,128)S(1)}, u32[]{:S(2)}) copy-start(f32[2,12,512,1]{2,1,3,0:T(8,128)S(1)} %get-tuple-element.1345) | copy-start | bytes 147460 | tf_op jit(solution)/shard_map/while
  1867.4 52.3 %copy-start.70 = (f32[32]{0:T(128)}, f32[32]{0:T(128)S(1)}, u32[]{:S(2)}) copy-start(f32[32]{0:T(128)S(1)} %get-tuple-element.1349) | copy-start | bytes 388 | tf_op jit(solution)/shard_map/while
  1867.4 75.6 %all-gather.68.cloned.1.call-start = ((), (), s32[]{:S(2)}) async-start(), calls=%async_computation.14 | async-start | bytes 3760128 | tf_op jit(solution)/shard_map/while/body/eval_jaxpr/all_gather | solution.py:253
  1869.1 132.3 %all-gather.70.cloned.1.call-start = ((), (), s32[]{:S(2)}) async-start(), calls=%async_computation.15 | async-start | bytes 1253376 | tf_op jit(solution)/shard_map/while/body/eval_jaxpr/all_gather | solution.py:254
  1869.9 214.6 %all-gather.72.cloned.1.call-start = ((), (), s32[]{:S(2)}) async-start(), calls=%async_computation.16 | async-start | bytes 5013504 | tf_op jit(solution)/shard_map/while/body/eval_jaxpr/all_gather | solution.py:255
  1871.7 295.7 %all-gather.74.cloned.1.call-start = ((), (), s32[]{:S(2)}) async-start(), calls=%async_computation.17 | async-start | bytes 5013504 | tf_op jit(solution)/shard_map/while/body/eval_jaxpr/all_gather | solution.py:256
  1873.4 475.0 %reduce-scatter.26.cloned.1.call-start = ((), (), s32[]{:S(2)}) async-start(), calls=%async_computation.22 | async-start | bytes 417792 | tf_op jit(solution)/shard_map/while
  2084.5 82.9 %copy-start.11 = (f32[512,768]{1,0:T(8,128)S(1)}, f32[512,768]{1,0:T(8,128)}, u32[]{:S(2)}) copy-start(f32[512,768]{1,0:T(8,128)} %get-tuple-element.1319) | copy-start | bytes 4718596 | tf_op jit(solution)/shard_map/while
  2228.5 252.6 %reduce-scatter.20.cloned.1.call-start = ((), (), s32[]{:S(2)}) async-start(), calls=%async_computation.19 | async-start | bytes 2506752 | tf_op jit(solution)/shard_map/while/body/eval_jaxpr/reduce_scatter | solution.py:264
  2231.8 405.8 %reduce-scatter.18.cloned.1.call-start = ((), (), s32[]{:S(2)}) async-start(), calls=%async_computation.18 | async-start | bytes 7520256 | tf_op jit(solution)/shard_map/while/body/eval_jaxpr/reduce_scatter | solution.py:263
  2239.8 574.1 %reduce-scatter.24.cloned.1.call-start = ((), (), s32[]{:S(2)}) async-start(), calls=%async_computation.21 | async-start | bytes 10027008 | tf_op jit(solution)/shard_map/while/body/eval_jaxpr/reduce_scatter | solution.py:266
  2250.8 738.9 %reduce-scatter.22.cloned.1.call-start = ((), (), s32[]{:S(2)}) async-start(), calls=%async_computation.20 | async-start | bytes 10027008 | tf_op jit(solution)/shard_map/while/body/eval_jaxpr/reduce_scatter | solution.py:265
  2260.3 89.1 %copy-start.78 = (f32[2,2,2,48]{3,2,1,0:T(2,128)S(1)}, f32[2,2,2,48]{3,2,1,0:T(2,128)}, u32[]{:S(2)}) copy-start(f32[2,2,2,48]{3,2,1,0:T(2,128)} %get-tuple-element.1324) | copy-start | bytes 4612 | tf_op jit(solution)/shard_map/while
  2260.3 220.8 %copy-start.52 = (f32[2,48,768]{2,1,0:T(8,128)S(1)}, f32[2,48,768]{2,1,0:T(8,128)}, u32[]{:S(2)}) copy-start(f32[2,48,768]{2,1,0:T(8,128)} %get-tuple-element.1321) | copy-start | bytes 884740 | tf_op jit(solution)/shard_map/while
  2263.4 726.3 %copy-start.36 = (f32[2,48,3072]{2,1,0:T(8,128)S(1)}, f32[2,48,3072]{2,1,0:T(8,128)}, u32[]{:S(2)}) copy-start(f32[2,48,3072]{2,1,0:T(8,128)} %get-tuple-element.1322) | copy-start | bytes 3538948 | tf_op jit(solution)/shard_map/while
  2349.4 641.4 %copy-start.79 = (f32[2,2,2,48]{3,2,1,0:T(2,128)}, f32[2,2,2,48]{3,2,1,0:T(2,128)S(1)}, u32[]{:S(2)}) copy-start(f32[2,2,2,48]{3,2,1,0:T(2,128)S(1)} %constant_dynamic-update-slice_fusion.4) | copy-start | bytes 4612 | tf_op jit(solution)/shard_map/while
  2481.9 155.6 %copy-start.53 = (f32[2,48,768]{2,1,0:T(8,128)}, f32[2,48,768]{2,1,0:T(8,128)S(1)}, u32[]{:S(2)}) copy-start(f32[2,48,768]{2,1,0:T(8,128)S(1)} %bitcast_dynamic-update-slice_fusion.15) | copy-start | bytes 884740 | tf_op jit(solution)/shard_map/while
  2637.6 354.3 %copy-start.29 = (bf16[2,48,768]{2,1,0:T(8,128)(2,1)S(1)}, bf16[2,48,768]{2,1,0:T(8,128)(2,1)}, u32[]{:S(2)}) copy-start(bf16[2,48,768]{2,1,0:T(8,128)(2,1)} %copy-done.28) | copy-start | bytes 442372 | tf_op jit(solution)/shard_map/while
  2637.6 354.3 %copy-start.42 = (bf16[2,2,2,48]{2,1,0,3:T(2,128)(2,1)S(1)}, bf16[2,2,2,48]{2,1,0,3:T(2,128)(2,1)}, u32[]{:S(2)}) copy-start(bf16[2,2,2,48]{2,1,0,3:T(2,128)(2,1)} %copy-done.41) | copy-start | bytes 2308 | tf_op jit(solution)/shard_map/while
  2637.6 354.3 %copy-start.58 = (f32[2,12,512,1]{2,1,3,0:T(8,128)S(1)}, f32[2,12,512,1]{2,1,3,0:T(8,128)}, u32[]{:S(2)}) copy-start(f32[2,12,512,1]{2,1,3,0:T(8,128)} %copy-done.57) | copy-start | bytes 147460 | tf_op jit(solution)/shard_map/while
  2637.6 354.3 %copy-start.71 = (f32[32]{0:T(128)S(1)}, f32[32]{0:T(128)}, u32[]{:S(2)}) copy-start(f32[32]{0:T(128)} %copy-done.70) | copy-start | bytes 388 | tf_op jit(solution)/shard_map/while
  2997.1 126.5 %reduce-scatter.16.cloned.1.call-start = ((), (), s32[]{:S(2)}) async-start(), calls=%async_computation.8 | async-start | bytes 417792
  2997.6 251.6 %reduce-scatter.14.cloned.1.call-start = ((), (), s32[]{:S(2)}) async-start(), calls=%async_computation.7 | async-start | bytes 417792 | tf_op jit(solution)/shard_map/reduce_scatter | solution.py:276
  3000.7 253.9 %all-reduce.5.cloned.1.call-start = ((), (), s32[]{:S(2)}) async-start(), calls=%async_computation.9 | async-start | bytes 7077888 | tf_op jit(solution)/shard_map/psum | solution.py:282
  3000.8 248.5 %copy-start.80 = (f32[2,2,2,48]{3,2,1,0:T(2,128)S(1)}, f32[2,2,2,48]{3,2,1,0:T(2,128)}, u32[]{:S(2)}) copy-start(f32[2,2,2,48]{3,2,1,0:T(2,128)} %get-tuple-element.500) | copy-start | bytes 4612
  3254.6 91.0 %copy-start.81 = (f32[5,2,48]{2,1,0:T(2,128)S(1)}, f32[5,2,48]{2,1,0:T(2,128)}, u32[]{:S(2)}) copy-start(f32[5,2,48]{2,1,0:T(2,128)} %param.33) | copy-start | bytes 5764
  3256.9 92.8 %copy-start.50 = (f32[2,48,768]{2,1,0:T(8,128)S(1)}, f32[2,48,768]{2,1,0:T(8,128)}, u32[]{:S(2)}) copy-start(f32[2,48,768]{2,1,0:T(8,128)} %param.29) | copy-start | bytes 884740
  3258.5 94.0 %copy-start.40 = (f32[2,48,2304]{2,1,0:T(8,128)S(1)}, f32[2,48,2304]{2,1,0:T(8,128)}, u32[]{:S(2)}) copy-start(f32[2,48,2304]{2,1,0:T(8,128)} %param.28) | copy-start | bytes 2654212
  (111 other events, 561.8 us)
Sparse Core Ops, SparseCore 0:
  123.2 69.9 all-gather.59
  197.0 54.6 all-gather.61
  255.5 79.3 all-gather.63
  338.5 79.0 all-gather.65
  427.9 71.4 all-gather.59
  503.0 54.6 all-gather.61
  561.5 79.3 all-gather.63
  644.6 79.0 all-gather.65
  747.9 70.8 all-gather.67
  822.4 54.6 all-gather.69
  880.8 79.3 all-gather.71
  963.8 79.0 all-gather.73
  1104.1 119.9 reduce-scatter.25
  1228.9 127.5 reduce-scatter.19
  1362.6 150.6 reduce-scatter.17
  1519.8 169.5 reduce-scatter.23
  1694.9 169.8 reduce-scatter.21
  1871.7 71.2 all-gather.67
  1946.8 54.6 all-gather.69
  2005.1 79.3 all-gather.71
  2088.2 79.0 all-gather.73
  2228.6 119.8 reduce-scatter.25
  2353.4 127.5 reduce-scatter.19
  2487.1 150.4 reduce-scatter.17
  2644.2 169.7 reduce-scatter.23
  2819.5 170.1 reduce-scatter.21
  3004.9 23.0 all-reduce.4
Sparse Core Ops, SparseCore 1:
  3002.9 120.6 reduce-scatter.15
  3128.7 120.5 reduce-scatter.13
where the time goes:
time: 3380 us; the launch traced here: 3370 us
  waiting for transfers between devices  2510 us (74%)
  blocking collectives  334 us (10%)
  matrix products  243 us (7%)
  local copies, waits for them, and re-layouts  153 us (5%)
  other arithmetic  78.4 us (2%)
    reduce_scatter x2, waiting for transfers between devices, backward_step(): lax.psum_scatter(grad_down, 'fsdp', scatter_dimension=0, tiled=True)  349 us
    reduce_scatter x2, waiting for transfers between devices, backward_step(): lax.psum_scatter(grad_up, 'fsdp', scatter_dimension=0, tiled=True)  347 us
    reduce_scatter x2, waiting for transfers between devices, backward_step(): lax.psum_scatter(grad_in, 'fsdp', scatter_dimension=0, tiled=True)  311 us
    reduce_scatter x2, waiting for transfers between devices, backward_step(): lax.psum_scatter(grad_wout, 'fsdp', scatter_dimension=0, tiled=True)  263 us
    while x28, waiting for transfers between devices  171 us
    all_gather x2, waiting for transfers between devices, forward_step(): lax.all_gather(w_up.astype(jnp.bfloat16), 'fsdp', axis=0, tiled=True)  161 us
    all_gather x2, waiting for transfers between devices, backward_step(): lax.all_gather(w_up.astype(jnp.bfloat16), 'fsdp', axis=0, tiled=True)  159 us
    all_gather x2, waiting for transfers between devices, forward_step(): lax.all_gather(w_down.astype(jnp.bfloat16), 'fsdp', axis=0, tiled=True)  150 us
  transfers between devices with their start and end apart: 29, of which 28 were waited for; matrix products, arithmetic and copies ran while one was open for 8% of the time, Pallas kernels for 0%

commit v1 on v0

v1 whole, which is shorter than its diff:
```python
import functools

import jax
import jax.numpy as jnp
from jax import lax
from jax.sharding import PartitionSpec as P

HD = 64
V = 70
STEP = 10


NORM_EPS = 1e-05
BETA_ONE = 0.9
BETA_TWO = 0.95
ADAM_EPS = 1e-08
DECAY = 0.1
RATE_MATRIX = 0.05
RATE_VECTOR = 0.3
CLIP = 0.05


def rotary_tables(length, size):
    freq = 10000.0 ** (-jnp.arange(size // 2, dtype=jnp.float32) * 2.0 / size)
    angle = jnp.arange(length, dtype=jnp.float32)[:, None] * freq[None, :]
    return (jnp.cos(angle)[:, None, :], jnp.sin(angle)[:, None, :])


def rotate(value, cosine, sine):
    half = value.shape[-1] // 2
    first = value[..., :half]
    second = value[..., half:]
    return jnp.concatenate([first * cosine - second * sine, second * cosine + first * sine], -1)


def normalize(resid, gain, bias):
    mean = jnp.mean(resid, -1, keepdims=True)
    centred = resid - mean
    inverse = lax.rsqrt(jnp.mean(centred * centred, -1, keepdims=True) + NORM_EPS)
    unit = centred * inverse
    return (unit * gain + bias, unit, inverse)


def normalize_back(grad, unit, inverse, gain):
    scaled = grad * gain
    across = (
        scaled
        - jnp.mean(scaled, -1, keepdims=True)
        - unit * jnp.mean(scaled * unit, -1, keepdims=True)
    )
    return (across * inverse, jnp.sum(grad * unit, 0), jnp.sum(grad, 0))


def layer_forward(resid, weights, cosine, sine, same):
    w_in, w_out, w_up, w_down, gains = weights
    length = resid.shape[0]
    width = w_out.shape[0]
    heads = width // HD
    normed, unit_in, inverse_in = normalize(resid, gains[0, 0], gains[0, 1])
    normed_low = normed.astype(jnp.bfloat16)
    mixed = dots(normed_low, w_in).reshape(length, 3, heads, HD)
    query = rotate(mixed[:, 0], cosine, sine).astype(jnp.bfloat16)
    keys = rotate(mixed[:, 1], cosine, sine).astype(jnp.bfloat16)
    values = mixed[:, 2].astype(jnp.bfloat16)
    scores = jnp.einsum("qhe,khe->hqk", query, keys, preferred_element_type=jnp.float32) * HD ** (
        -0.5
    )
    scores = jnp.where(same[None], scores, -1000000000.0)
    top = jnp.max(scores, -1, keepdims=True)
    expo = jnp.exp(scores - top)
    total = jnp.sum(expo, -1, keepdims=True)
    probs = expo / total
    probs_low = probs.astype(jnp.bfloat16)
    attended = jnp.einsum("hqk,khe->qhe", probs_low, values, preferred_element_type=jnp.float32)
    attended = attended.astype(jnp.bfloat16).reshape(length, width)
    middle = resid + dots(attended, [w_out])
    normed_mid, unit_mid, inverse_mid = normalize(middle, gains[1, 0], gains[1, 1])
    normed_mid_low = normed_mid.astype(jnp.bfloat16)
    hidden = dots(normed_mid_low, w_up)
    active = jax.nn.gelu(hidden).astype(jnp.bfloat16)
    output = middle
    width = w_down[0].shape[0]
    for part, w_part in enumerate(w_down):
        output = output + jnp.dot(
            active[:, part * width : (part + 1) * width],
            w_part,
            preferred_element_type=jnp.float32,
        )
    saved = (
        normed_low,
        unit_in,
        inverse_in,
        query,
        keys,
        values,
        probs,
        probs_low,
        attended,
        unit_mid,
        inverse_mid,
        normed_mid_low,
        hidden,
        active,
    )
    return (output, saved)


def dots(value, weights):
    return jnp.concatenate(
        [jnp.dot(value, w, preferred_element_type=jnp.float32) for w in weights], 1
    )


def dots_back(grad, weights):
    total, at = 0.0, 0
    for w in weights:
        part = grad[:, at : at + w.shape[1]]
        total = total + jnp.dot(part, w.T, preferred_element_type=jnp.float32)
        at += w.shape[1]
    return total


def layer_back(saved, weights, cosine, sine, grad_out):
    (
        normed_low,
        unit_in,
        inverse_in,
        query,
        keys,
        values,
        probs,
        probs_low,
        attended,
        unit_mid,
        inverse_mid,
        normed_mid_low,
        hidden,
        active,
    ) = saved
    w_in, w_out, w_up, w_down, gains = weights
    length = grad_out.shape[0]
    width = w_out.shape[0]
    heads = width // HD
    branch_grad = grad_out.astype(jnp.bfloat16)
    grad_down = jnp.dot(active.T, branch_grad, preferred_element_type=jnp.float32)
    grad_active = jnp.concatenate(
        [jnp.dot(branch_grad, w.T, preferred_element_type=jnp.float32) for w in w_down], 1
    )
    _, gelu_back = jax.vjp(jax.nn.gelu, hidden)
    grad_hidden = gelu_back(grad_active)[0].astype(jnp.bfloat16)
    grad_up = jnp.dot(normed_mid_low.T, grad_hidden, preferred_element_type=jnp.float32)
    grad_normed_mid = dots_back(grad_hidden, w_up)
    grad_middle, gain_mid, bias_mid = normalize_back(
        grad_normed_mid, unit_mid, inverse_mid, gains[1, 0]
    )
    grad_middle = grad_middle + grad_out
    attn_grad = grad_middle.astype(jnp.bfloat16)
    grad_wout = jnp.dot(attended.T, attn_grad, preferred_element_type=jnp.float32)
    grad_attended = jnp.dot(attn_grad, w_out.T, preferred_element_type=jnp.float32)
    grad_attended = grad_attended.astype(jnp.bfloat16).reshape(length, heads, HD)
    grad_probs = jnp.einsum(
        "qhe,khe->hqk", grad_attended, values, preferred_element_type=jnp.float32
    )
    grad_scores = probs * (grad_probs - jnp.sum(probs * grad_probs, -1, keepdims=True))
    grad_scores = grad_scores.astype(jnp.bfloat16)
    scale = HD ** (-0.5)
    grad_query = (
        jnp.einsum("hqk,khe->qhe", grad_scores, keys, preferred_element_type=jnp.float32) * scale
    )
    grad_keys = (
        jnp.einsum("hqk,qhe->khe", grad_scores, query, preferred_element_type=jnp.float32) * scale
    )
    grad_values = jnp.einsum(
        "hqk,qhe->khe", probs_low, grad_attended, preferred_element_type=jnp.float32
    )
    grad_mixed = jnp.stack(
        [rotate(grad_query, cosine, -sine), rotate(grad_keys, cosine, -sine), grad_values], 1
    )
    grad_mixed = grad_mixed.reshape(length, 3 * width).astype(jnp.bfloat16)
    grad_in = jnp.dot(normed_low.T, grad_mixed, preferred_element_type=jnp.float32)
    grad_normed = dots_back(grad_mixed, w_in)
    grad_resid, gain_in, bias_in = normalize_back(grad_normed, unit_in, inverse_in, gains[0, 0])
    grad_gains = [gain_in, bias_in, gain_mid, bias_mid]
    return (grad_resid + grad_middle, grad_in, grad_wout, grad_up, grad_down, grad_gains)


def adam_step(master, grad, first, second, rate, decay):
    first = BETA_ONE * first + (1.0 - BETA_ONE) * grad
    second = BETA_TWO * second + (1.0 - BETA_TWO) * grad * grad
    fix_one = 1.0 - BETA_ONE**STEP
    fix_two = 1.0 - BETA_TWO**STEP
    update = first / fix_one / (jnp.sqrt(second / fix_two) + ADAM_EPS) + decay * master
    return (master - rate * update, first, second)


def bits_of(size, swap):
    order = list(range(size.bit_length() - 1))
    if swap and len(order) > 1:
        order[0], order[1] = order[1], order[0]
    return order


def exchange(value, axis, size, bit=0):
    return lax.ppermute(value, axis, [(i, i ^ (1 << bit)) for i in range(size)])


def total_of(value, sizes):
    for axis, size in sizes:
        for bit in bits_of(size, False):
            value = value + exchange(value, axis, size, bit)
    return value


def scatter_sum(value, size, low, swap):
    levels = size.bit_length() - 1
    me = lax.axis_index("fsdp")
    rows, columns = value.shape[0] // size, value.shape[1]
    value = value.reshape((2,) * levels + (rows, columns))
    left = list(range(levels))[::-1]
    for bit in bits_of(size, swap):
        place = left.index(bit)
        left.remove(bit)
        mine = lax.rem(lax.div(me, 1 << bit), 2)
        send = lax.dynamic_index_in_dim(value, 1 - mine, place, keepdims=False)
        keep = lax.dynamic_index_in_dim(value, mine, place, keepdims=False)
        value = keep + exchange(send.astype(low), "fsdp", size, bit).astype(jnp.float32)
    return value


def reduce_matrix(grad, size, swap):
    core = lax.axis_index("dp")
    half = grad.shape[1] // 2
    send = lax.dynamic_slice_in_dim(grad, (1 - core) * half, half, 1)
    keep = lax.dynamic_slice_in_dim(grad, core * half, half, 1)
    grad = keep + exchange(send.astype(jnp.bfloat16), "dp", 2).astype(jnp.float32)
    return scatter_sum(grad, size, jnp.bfloat16, swap)


def both_halves(part):
    other = exchange(part, "dp", 2)
    first = lax.axis_index("dp") == 0
    return jnp.concatenate(
        [jnp.where(first, part, other), jnp.where(first, other, part)], 1
    )


def gather_halves(first, second):
    own = jnp.where(lax.axis_index("dp") == 0, first, second)
    own = lax.all_gather(own, "fsdp", axis=0, tiled=True)
    return lax.all_gather(own, "dp", axis=0, tiled=False)


def down_to_rows(shrink_shard, rows):
    return jnp.concatenate(
        [shrink_shard[at : at + rows] for at in range(0, shrink_shard.shape[0], rows)], 1
    )


def up_to_parts(expand_shard, size, rows, parts):
    r = expand_shard.shape[0]
    return expand_shard.reshape(r, size, parts, rows).transpose(0, 2, 1, 3).reshape(r, -1)


def up_from_parts(expand_shard, size, rows, parts):
    r = expand_shard.shape[0]
    return expand_shard.reshape(r, parts, size, rows).transpose(0, 2, 1, 3).reshape(r, -1)


def body(
    fsdp,
    codons,
    masked,
    segments,
    inward,
    outward,
    expand,
    shrink,
    codon_table,
    norm_params,
    inward_first,
    inward_second,
    outward_first,
    outward_second,
    expand_first,
    expand_second,
    shrink_first,
    shrink_second,
    table_first,
    table_second,
    norm_first,
    norm_second,
):
    layers = inward.shape[0]
    length = codons.shape[0]
    rows = inward.shape[1]
    width = rows * fsdp
    parts = shrink.shape[1] // rows
    low = jnp.bfloat16
    sizes = (("dp", 2), ("fsdp", fsdp))
    weight = masked.astype(jnp.float32)
    inputs = jnp.where(masked == 1, V - 1, codons)

    norms = norm_params.shape[0] * 2
    small = jnp.concatenate(
        [codon_table.astype(low), norm_params.astype(low).reshape(norms, rows)], 0
    ).T
    small = jnp.pad(small, ((0, 0), (0, -small.shape[1] % 128)))
    w_in, w_out = inward.astype(low), outward.astype(low)
    w_up = [up_to_parts(expand[l].astype(low), fsdp, rows, parts) for l in range(layers)]
    w_down = [down_to_rows(shrink[l].astype(low), rows) for l in range(layers)]
    half = (3 * width + width) // 2
    mixer = [jnp.concatenate([w_in[l], w_out[l]], 1) for l in range(layers)]
    whole = []
    first = gather_halves(
        jnp.concatenate([mixer[0][:, :half], small], 1),
        jnp.concatenate([mixer[0][:, half:], small], 1),
    )
    second = gather_halves(w_up[0], w_down[0])
    small = first[0, :, half:]
    whole.append((first[0, :, :half], first[1, :, :half], second[0], second[1]))
    for l in range(1, layers):
        cut = parts * width // 2
        later = gather_halves(
            jnp.concatenate([mixer[l], w_up[l][:, :cut]], 1),
            jnp.concatenate([w_up[l][:, cut:], w_down[l]], 1),
        )
        whole.append(
            (
                later[0, :, :half],
                later[0, :, half : 2 * half],
                jnp.concatenate([later[0, :, 2 * half :], later[1, :, :cut]], 1),
                later[1, :, cut:],
            )
        )
    table_low = small[:, :V].T
    gains = small[:, V : V + norms].T.astype(jnp.float32).reshape(-1, 2, width)
    weights = []
    for l in range(layers):
        left, right, up, down = whole[l]
        weights.append(
            (
                [left, right[:, : 3 * width - half]],
                right[:, 3 * width - half :],
                [up],
                [down[:, p * width : (p + 1) * width] for p in range(parts)],
                gains[2 * l : 2 * l + 2],
            )
        )

    cosine, sine = rotary_tables(length, HD)
    same = segments[:, None] == segments[None, :]
    vocab_ids = jnp.arange(V, dtype=jnp.int32)
    chosen = (inputs[:, None] == vocab_ids[None, :]).astype(low)
    resid = jnp.dot(chosen, table_low, preferred_element_type=jnp.float32)
    kept = []
    for l in range(layers):
        resid, saved = layer_forward(resid, weights[l], cosine, sine, same)
        kept.append(saved)
    final_gain = gains[2 * layers]
    normed_out, unit_out, inverse_out = normalize(resid, final_gain[0], final_gain[1])
    head_in = normed_out.astype(low)
    logits = jnp.einsum("sd,vd->sv", head_in, table_low, preferred_element_type=jnp.float32)
    top = jnp.max(logits, -1, keepdims=True)
    lse_head = top + jnp.log(jnp.sum(jnp.exp(logits - top), -1, keepdims=True))
    targets = (codons[:, None] == vocab_ids[None, :]).astype(jnp.float32)
    picked = jnp.sum(logits * targets, -1)
    loss_local = jnp.sum((lse_head[:, 0] - picked) * weight)
    scalars = total_of(jnp.stack([loss_local, jnp.sum(weight)])[None], sizes)
    loss_sum, count = scalars[0, 0], scalars[0, 1]
    grad_logits = ((jnp.exp(logits - lse_head) - targets) * weight[:, None]).astype(low)
    grad_table = jnp.einsum("sv,sd->vd", grad_logits, head_in, preferred_element_type=jnp.float32)
    grad_head = jnp.dot(grad_logits, table_low, preferred_element_type=jnp.float32)
    grad, grad_final_gain, grad_final_bias = normalize_back(
        grad_head, unit_out, inverse_out, final_gain[0]
    )
    grad_norms = [grad_final_gain, grad_final_bias]
    shares = [[None] * layers for _ in range(4)]
    for l in reversed(range(layers)):
        grad, grad_in, grad_wout, grad_up, grad_down, grad_gains = layer_back(
            kept[l], weights[l], cosine, sine, grad
        )
        grad_norms = grad_gains + grad_norms
        grad_down = jnp.concatenate(
            [grad_down[p * width : (p + 1) * width] for p in range(parts)], 1
        )
        for index, (value, swap) in enumerate(
            ((grad_in, False), (grad_wout, True), (grad_up, True), (grad_down, False))
        ):
            shares[index][l] = reduce_matrix(value, fsdp, swap)
    grad_table = grad_table + jnp.einsum(
        "sv,sd->vd", chosen, grad.astype(low), preferred_element_type=jnp.float32
    )
    grad_small = jnp.concatenate([grad_table, jnp.stack(grad_norms)], 0)
    grad_small = grad_small + exchange(grad_small, "dp", 2)
    grad_small = grad_small.reshape(V + norms, fsdp, rows).transpose(1, 0, 2)
    share_small = scatter_sum(grad_small.reshape(-1, rows), fsdp, jnp.float32, False)

    squares = jnp.zeros((), jnp.float32)
    for value in sum(shares, []):
        squares = squares + jnp.sum(value * value)
    squares = squares + 0.5 * jnp.sum(share_small * share_small)
    square_total = total_of(squares.reshape(1, 1), sizes)[0, 0]
    shares = [[both_halves(value) for value in group] for group in shares]
    share_in, share_out, share_up, share_down = shares
    share_up = [up_from_parts(value, fsdp, rows, parts) for value in share_up]
    share_down = [
        jnp.concatenate([value[:, p * width : (p + 1) * width] for p in range(parts)], 0)
        for value in share_down
    ]
    group = (
        jnp.stack(share_in),
        jnp.stack(share_out),
        jnp.stack(share_up),
        jnp.stack(share_down),
        share_small[:V],
        share_small[V:].reshape(-1, 2, rows),
    )
    grad_norm = jnp.sqrt(square_total) / count
    factor = CLIP / jnp.maximum(grad_norm, CLIP)
    masters = (inward, outward, expand, shrink, codon_table, norm_params)
    firsts = (inward_first, outward_first, expand_first, shrink_first, table_first, norm_first)
    seconds = (
        inward_second,
        outward_second,
        expand_second,
        shrink_second,
        table_second,
        norm_second,
    )
    result = [loss_sum, count, grad_norm]
    for index in range(6):
        rate = RATE_VECTOR if index == 5 else RATE_MATRIX
        decay = 0.0 if index == 5 else DECAY
        clipped = group[index] / count * factor
        result.extend(
            adam_step(masters[index], clipped, firsts[index], seconds[index], rate, decay)
        )
    return tuple(result)


def solution(mesh):
    in_specs = (
        P(("fsdp", "dp")),
        P(("fsdp", "dp")),
        P(("fsdp", "dp")),
        P(None, "fsdp", None),
        P(None, "fsdp", None),
        P(None, "fsdp", None),
        P(None, "fsdp", None),
        P(None, "fsdp"),
        P(None, None, "fsdp"),
        P(None, "fsdp", None),
        P(None, "fsdp", None),
        P(None, "fsdp", None),
        P(None, "fsdp", None),
        P(None, "fsdp", None),
        P(None, "fsdp", None),
        P(None, "fsdp", None),
        P(None, "fsdp", None),
        P(None, "fsdp"),
        P(None, "fsdp"),
        P(None, None, "fsdp"),
        P(None, None, "fsdp"),
    )
    out_specs = (
        P(),
        P(),
        P(),
        P(None, "fsdp", None),
        P(None, "fsdp", None),
        P(None, "fsdp", None),
        P(None, "fsdp", None),
        P(None, "fsdp", None),
        P(None, "fsdp", None),
        P(None, "fsdp", None),
        P(None, "fsdp", None),
        P(None, "fsdp", None),
        P(None, "fsdp", None),
        P(None, "fsdp", None),
        P(None, "fsdp", None),
        P(None, "fsdp"),
        P(None, "fsdp"),
        P(None, "fsdp"),
        P(None, None, "fsdp"),
        P(None, None, "fsdp"),
        P(None, None, "fsdp"),
    )
    step = functools.partial(body, mesh.shape["fsdp"])
    return jax.shard_map(step, mesh=mesh, in_specs=in_specs, out_specs=out_specs, check_vma=False)
```

time: 3380 us -> 913 us (0.27)
  waiting for transfers between devices: 2510 us -> 399 us
  blocking collectives: 334 us -> 0 us
  matrix products: 243 us -> 172 us
  starting transfers between devices: 1.64 us -> 63.9 us
  other arithmetic: 78.4 us -> 117 us
    reduce_scatter x9 -> x0, waiting for transfers between devices: 1400 us -> none  [the longest x2 349 us: backward_step(): lax.psum_scatter(grad_down, 'fsdp', scatter_dimension=0, tiled=True)]
    all_gather x16 -> x6, waiting for transfers between devices: 824 us -> 255 us  [the longest x3 245 us: gather_halves(): own = lax.all_gather(own, 'fsdp', axis=0, tiled=True)]
    all_gather x6 -> x0, blocking collectives: 249 us -> none  [the longest x2 84.2 us: backward_step(): lax.all_gather(gains.astype(jnp.bfloat16), 'fsdp', axis=2, tiled=True)]
    while x28 -> x0, waiting for transfers between devices: 171 us -> none
    ppermute x0 -> x63, waiting for transfers between devices: none -> 144 us  [exchange(): return lax.ppermute(value, axis, [(i, i ^ 1 << bit) for i in range(size)])]
    unnamed x4 -> x6, waiting for transfers between devices: 123 us -> 0.1 us
    psum x3 -> x0, blocking collectives: 84.9 us -> none  [the longest x1 40.5 us: body(): square_total = lax.psum(squares, 'fsdp')]
    ppermute x0 -> x63, starting transfers between devices: none -> 63.4 us  [exchange(): return lax.ppermute(value, axis, [(i, i ^ 1 << bit) for i in range(size)])]
  transfers between devices with their start and end apart: 29 -> 69, of which waited for: 28 -> 39; matrix products, arithmetic and copies ran while one was open for 8% -> 21% of each run, Pallas kernels for 0% -> 0%
where the time goes in v1:
time: 913 us; the launch traced here: 906 us
  waiting for transfers between devices  399 us (44%)
  matrix products  172 us (19%)
  local copies, waits for them, and re-layouts  126 us (14%)
  other arithmetic  117 us (13%)
  starting transfers between devices  63.9 us (7%)
  between operations  28.3 us (3%)
    all_gather x3, waiting for transfers between devices, gather_halves(): own = lax.all_gather(own, 'fsdp', axis=0, tiled=True)  245 us
    ppermute x63, waiting for transfers between devices, exchange(): return lax.ppermute(value, axis, [(i, i ^ 1 << bit) for i in range(size)])  144 us
    ppermute x63, starting transfers between devices, exchange(): return lax.ppermute(value, axis, [(i, i ^ 1 << bit) for i in range(size)])  63.4 us
    unnamed x260, local copies, waits for them, and re-layouts  24.5 us
    dot_general x8, matrix products, dots(): jnp.dot(value, w, preferred_element_type=jnp.float32)  22.6 us
    convert_element_type x8, local copies, waits for them, and re-layouts, reduce_matrix(): send.astype(jnp.bfloat16)  21.7 us
    add x8, other arithmetic, reduce_matrix(): keep + exchange(send.astype(jnp.bfloat16), 'dp', 2).astype(jnp.float32)  21.7 us
    sub x2, matrix products, layer_forward(): expo = jnp.exp(scores - top)  19.2 us
  transfers between devices with their start and end apart: 69, of which 39 were waited for; matrix products, arithmetic and copies ran while one was open for 21% of the time, Pallas kernels for 0%

profile of v1, /device:TPU:0, one launch (start us, length us, event | category | flops | bytes accessed | tf_op | source)
XLA Modules:
  0.0 906.4 jit_solution(9137213806273289884)
XLA Ops:
  19.3 59.0 %all-gather.10.cloned.1.call-done = bf16[768,1664]{1,0:T(8,128)(2,1)} async-done(((bf16[48,1664]{1,0:T(8,128)(2,1)}), bf16[768,1664]{1,0:T(8,128)(2,1)}) %all-gather.10.cloned.1.call-update) | async-done | bytes 2555920 | tf_op jit(solution)/shard_map/all_gather | solution.py:249
  78.4 82.7 %all-gather.12.cloned.1.call-done = bf16[768,3072]{1,0:T(8,128)(2,1)} async-done(((bf16[48,3072]{1,0:T(8,128)(2,1)}), bf16[768,3072]{1,0:T(8,128)(2,1)}) %all-gather.12.cloned.1.call-update) | async-done | bytes 4718608 | tf_op jit(solution)/shard_map/all_gather | solution.py:249
  161.5 103.0 %all-gather.14.cloned.1.call-done = bf16[768,4608]{1,0:T(8,128)(2,1)} async-done(((bf16[48,4608]{1,0:T(8,128)(2,1)}), bf16[768,4608]{1,0:T(8,128)(2,1)}) %all-gather.14.cloned.1.call-update) | async-done | bytes 7077904 | tf_op jit(solution)/shard_map/all_gather | solution.py:249
  269.2 9.8 %all-gather.16.cloned.1.call-done = bf16[1536,1664]{1,0:T(8,128)(2,1)} async-done(((bf16[768,1664]{1,0:T(8,128)(2,1)}), bf16[1536,1664]{1,0:T(8,128)(2,1)}) %all-gather.16.cloned.1.call-update) | async-done | bytes 5111824 | tf_op jit(solution)/shard_map/all_gather | solution.py:250
  289.2 6.6 copy.198
  299.6 8.7 fusion.236
  308.4 7.6 fusion.44
  317.3 10.3 %multiply_convert_fusion.3 = (bf16[512,3072]{1,0:T(8,128)(2,1)S(1)}, f32[512,3072]{1,0:T(8,128)}) fusion(bf16[1536,3072]{1,0:T(8,128)(2,1)} %all-gather.18.cloned.1.call-done, f32[512,768]{1,0:T(8,128)S(1)} %get-tuple-element.229, f32[768]{0:T(1024)S(1)} %get-tuple-element.92, f32[768]{0:T(1024)S(1)} %get-tuple-element.91, f32[512]{0:T(512)S(1)} %add_rsqrt_fusion.3, ...), kind=kOutput, calls=%fused_computation.36 | convolution fusion | flops 2432040960 | bytes 15738880 | tf_op jit(solution)/shard_map/dot_general | solution.py:110
  332.7 4.8 slice_bitcast_fusion
  337.5 5.8 slice_bitcast_fusion.3
  343.3 3.9 fusion.41
  350.6 6.2 copy.202
  360.7 10.5 %fusion.239 = (f32[12,512]{1,0:T(8,128)S(1)}, f32[12,512,512]{1,2,0:T(8,128)}) fusion(pred[512,512]{0,1:T(8,128)(4,1)} %broadcast_compare_fusion, bf16[512,12,32]{0,2,1:T(8,128)(2,1)} %get-tuple-element.209, bf16[512,12,32]{0,2,1:T(8,128)(2,1)} %get-tuple-element.210, bf16[512,12,32]{0,2,1:T(8,128)(2,1)} %get-tuple-element.162, ...), kind=kOutput, calls=%fused_computation.544 | convolution fusion | flops 418382336 | bytes 14442496 | tf_op jit(solution)/shard_map/sub | solution.py:70
  371.2 6.4 fusion.50
  379.3 3.7 multiply_convert_fusion.2
  397.1 5.4 fusion.17
  410.0 5.5 fusion.215
  415.6 5.3 fusion.246
  423.2 7.0 fusion.60
  430.2 9.4 %multiply_reduce_fusion.1 = (f32[12,512]{1,0:T(8,128)S(1)}, f32[12,512,512]{1,2,0:T(8,128)}) fusion(f32[12,512,512]{1,2,0:T(8,128)} %get-tuple-element.235, f32[12,512]{1,0:T(8,128)S(1)} %get-tuple-element.234, bf16[512,12,64]{0,2,1:T(8,128)(2,1)S(1)} %bitcast.421, f32[512,3,12,64]{0,3,2,1:T(8,128)} %bitcast.373), kind=kOutput, calls=%fused_computation.5 | convolution fusion | flops 412084224 | bytes 26787840 | tf_op jit(solution)/shard_map/qhe,khe->hqk/dot_general | solution.py:161
  439.6 6.8 multiply_convert_fusion.1
  459.5 4.7 fusion.10
  464.2 5.4 multiply_reduce_fusion.5
  475.3 4.9 fusion.244
  480.2 5.6 fusion.214
  485.8 5.2 fusion.245
  491.3 6.8 fusion.63
  498.1 9.5 %multiply_reduce_fusion = (f32[12,512]{1,0:T(8,128)S(1)}, f32[12,512,512]{1,2,0:T(8,128)}) fusion(f32[12,512,512]{1,2,0:T(8,128)} %get-tuple-element.227, f32[12,512]{1,0:T(8,128)S(1)} %copy-done.75, bf16[512,12,64]{0,2,1:T(8,128)(2,1)S(1)} %bitcast.423, f32[512,3,12,64]{0,3,2,1:T(8,128)} %bitcast.370), kind=kOutput, calls=%fused_computation.3 | convolution fusion | flops 412084224 | bytes 26787840 | tf_op jit(solution)/shard_map/qhe,khe->hqk/dot_general | solution.py:161
  507.7 6.8 multiply_convert_fusion
  521.9 4.9 fusion.243
  530.9 4.0 dynamic-slice_convert_fusion.2
  535.1 4.4 fusion.224
  540.2 3.7 copy-done.2
  546.0 4.0 dynamic-slice_convert_fusion.3
  550.0 4.4 fusion.225
  563.0 3.4 dynamic-slice_convert_fusion.4
  566.4 3.4 dynamic-slice_convert_fusion.5
  573.3 3.9 collective-permute-done.46
  609.4 6.0 collective-permute-done.21
  617.2 6.6 collective-permute-done.16
  625.4 3.6 collective-permute-done.22
  630.5 3.6 collective-permute-done.17
  635.1 3.3 collective-permute-done.23
  639.5 3.3 collective-permute-done.18
  672.4 4.4 convert_add_fusion
  676.8 6.1 copy.225
  687.0 3.7 convert_add_fusion.3
  694.2 5.7 convert_add_fusion.1
  699.9 6.4 copy.224
  715.1 18.2 %collective-permute-done.12 = bf16[2,2,48,1152]{3,2,0,1:T(8,128)(2,1)S(1)} collective-permute-done((bf16[2,2,48,1152]{3,2,0,1:T(8,128)(2,1)S(1)}, bf16[2,2,48,1152]{3,2,0,1:T(8,128)(2,1)S(1)}, u32[]{:S(2)}, u32[]{:S(2)}) %collective-permute-start.12) | collective-permute-done | bytes 442400 | tf_op jit(solution)/shard_map/ppermute | solution.py:204
  735.1 9.5 %collective-permute-done.7 = bf16[2,2,48,1152]{3,2,0,1:T(8,128)(2,1)S(1)} collective-permute-done((bf16[2,2,48,1152]{3,2,0,1:T(8,128)(2,1)S(1)}, bf16[2,2,48,1152]{3,2,0,1:T(8,128)(2,1)S(1)}, u32[]{:S(2)}, u32[]{:S(2)}) %collective-permute-start.7) | collective-permute-done | bytes 442400 | tf_op jit(solution)/shard_map/ppermute | solution.py:204
  745.4 5.1 collective-permute-done.13
  751.3 5.1 collective-permute-done.8
  758.9 6.4 collective-permute-done.14
  766.0 6.1 collective-permute-done.9
  789.1 5.6 collective-permute-done.32
  794.9 4.5 collective-permute-done.42
  799.7 6.8 collective-permute-done.27
  806.8 4.4 collective-permute-done.37
  814.7 9.0 collective-permute-done.28
  824.0 4.3 collective-permute-done.38
  829.4 5.5 collective-permute-done.44
  845.1 3.5 collective-permute-start.51
  865.3 4.1 multiply_subtract_fusion.2
  (653 shorter events, 273.7 us)
Async XLA Ops:
  7.2 71.1 %all-gather.10.cloned.1.call-start = ((), (), s32[]{:S(2)}) async-start(), calls=%async_computation | async-start | bytes 2715648 | tf_op jit(solution)/shard_map/all_gather | solution.py:249
  12.0 149.1 %all-gather.12.cloned.1.call-start = ((), (), s32[]{:S(2)}) async-start(), calls=%async_computation.1 | async-start | bytes 5013504 | tf_op jit(solution)/shard_map/all_gather | solution.py:249
  15.8 248.6 %all-gather.14.cloned.1.call-start = ((), (), s32[]{:S(2)}) async-start(), calls=%async_computation.2 | async-start | bytes 7520256 | tf_op jit(solution)/shard_map/all_gather | solution.py:249
  19.3 259.8 %all-gather.16.cloned.1.call-start = ((), (), s32[]{:S(2)}) async-start(), calls=%async_computation.3 | async-start | bytes 7667712 | tf_op jit(solution)/shard_map/all_gather | solution.py:250
  78.3 239.0 %all-gather.18.cloned.1.call-start = ((), (), s32[]{:S(2)}) async-start(), calls=%async_computation.4 | async-start | bytes 14155776 | tf_op jit(solution)/shard_map/all_gather | solution.py:250
  161.1 171.6 %all-gather.20.cloned.1.call-start = ((), (), s32[]{:S(2)}) async-start(), calls=%async_computation.5 | async-start | bytes 21233664 | tf_op jit(solution)/shard_map/all_gather | solution.py:250
  528.2 50.9 %collective-permute-start = (f32[1,2]{1,0:T(1,128)S(1)}, f32[1,2]{1,0:T(1,128)S(1)}, u32[]{:S(2)}, u32[]{:S(2)}) collective-permute-start(f32[1,2]{1,0:T(1,128)S(1)} %maximum_bitcast_fusion.11), channel_id=1, source_target_pairs={{0,1},{1,0},{2,3},{3,2},{4,5},{5,4},{6,7},{7,6},{8,9},{9,8},{10,11... | collective-permute-start | bytes 32 | tf_op jit(solution)/shard_map/ppermute | solution.py:204
  530.6 73.3 %collective-permute-start.20 = (bf16[768,384]{1,0:T(8,128)(2,1)}, bf16[768,384]{1,0:T(8,128)(2,1)}, u32[]{:S(2)}, u32[]{:S(2)}) collective-permute-start(bf16[768,384]{1,0:T(8,128)(2,1)} %dynamic-slice_convert_fusion.11), channel_id=1, source_target_pairs={{0,1},{1,0},{2,3},{3,2},{4,5},{5,4},{6,7},{7,6},{8,9},{9,8},{10,11... | collective-permute-start | bytes 1769480 | tf_op jit(solution)/shard_map/ppermute | solution.py:204
  534.9 127.2 %collective-permute-start.30 = (bf16[768,1536]{1,0:T(8,128)(2,1)}, bf16[768,1536]{1,0:T(8,128)(2,1)}, u32[]{:S(2)}, u32[]{:S(2)}) collective-permute-start(bf16[768,1536]{1,0:T(8,128)(2,1)} %dynamic-slice_convert_fusion.2), channel_id=1, source_target_pairs={{0,1},{1,0},{2,3},{3,2},{4,5},{5,4},{6,7},{7,6},{8,9},{9,8},{10,11... | collective-permute-start | bytes 7077896 | tf_op jit(solution)/shard_map/ppermute | solution.py:204
  545.6 124.8 %collective-permute-start.40 = (bf16[768,1536]{0,1:T(8,128)(2,1)}, bf16[768,1536]{0,1:T(8,128)(2,1)}, u32[]{:S(2)}, u32[]{:S(2)}) collective-permute-start(bf16[768,1536]{0,1:T(8,128)(2,1)} %dynamic-slice_convert_fusion), channel_id=1, source_target_pairs={{0,1},{1,0},{2,3},{3,2},{4,5},{5,4},{6,7},{7,6},{8,9},{9,8},{10,11... | collective-permute-start | bytes 7077896 | tf_op jit(solution)/shard_map/ppermute | solution.py:204
  562.7 7.2 collective-permute-start.45
  570.1 7.2 collective-permute-start.46
  577.3 4.7 collective-permute-start.47
  580.5 3.5 collective-permute-start.1
  582.1 14.9 %collective-permute-start.48 = (f32[2,80,48]{1,2,0:T(8,128)S(1)}, f32[2,80,48]{1,2,0:T(8,128)S(1)}, u32[]{:S(2)}, u32[]{:S(2)}) collective-permute-start(f32[2,80,48]{1,2,0:T(8,128)S(1)} %dynamic-slice_bitcast_fusion.2), channel_id=1, source_target_pairs={{0,8},{2,10},{4,12},{6,14},{8,0},{10,2},{12,4},{14,6},{16,24},{18,... | collective-permute-start | bytes 92168 | tf_op jit(solution)/shard_map/ppermute | solution.py:204
  592.5 4.4 collective-permute-start.4
  597.0 9.0 collective-permute-start.15
  597.1 5.0 collective-permute-start.49
  602.1 53.8 %collective-permute-start.10 = (bf16[768,1152]{1,0:T(8,128)(2,1)}, bf16[768,1152]{1,0:T(8,128)(2,1)}, u32[]{:S(2)}, u32[]{:S(2)}) collective-permute-start(bf16[768,1152]{1,0:T(8,128)(2,1)} %dynamic-slice_convert_fusion.4), channel_id=1, source_target_pairs={{0,1},{1,0},{2,3},{3,2},{4,5},{5,4},{6,7},{7,6},{8,9},{9,8},{10,11... | collective-permute-start | bytes 5308424 | tf_op jit(solution)/shard_map/ppermute | solution.py:204
  604.0 55.3 %collective-permute-start.5 = (bf16[768,1152]{1,0:T(8,128)(2,1)}, bf16[768,1152]{1,0:T(8,128)(2,1)S(1)}, u32[]{:S(2)}, u32[]{:S(2)}) collective-permute-start(bf16[768,1152]{1,0:T(8,128)(2,1)} %dynamic-slice_convert_fusion.5), channel_id=1, source_target_pairs={{0,1},{1,0},{2,3},{3,2},{4,5},{5,4},{6,7},{7,6},{8,9},{9,8},{10,11... | collective-permute-start | bytes 5308424 | tf_op jit(solution)/shard_map/ppermute | solution.py:204
  605.9 9.4 %collective-permute-start.21 = (bf16[2,2,2,48,384]{4,3,0,1,2:T(8,128)(2,1)S(1)}, bf16[2,2,2,48,384]{4,3,0,1,2:T(8,128)(2,1)S(1)}, u32[]{:S(2)}, u32[]{:S(2)}) collective-permute-start(bf16[2,2,2,48,384]{4,3,0,1,2:T(8,128)(2,1)S(1)} %fusion.155), channel_id=1, source_target_pairs={{0,4},{2,6},{4,0},{6,2},{8,12},{10,14},{12,8},{14,10},{16,20},{18,... | collective-permute-start | bytes 884744 | tf_op jit(solution)/shard_map/ppermute | solution.py:204
  615.4 8.5 collective-permute-start.16
  623.8 5.1 collective-permute-start.22
  628.9 5.1 collective-permute-start.17
  634.1 4.4 collective-permute-start.23
  638.4 4.4 collective-permute-start.18
  642.8 4.9 collective-permute-start.24
  647.7 4.9 collective-permute-start.19
  655.0 30.6 %collective-permute-start.25 = (bf16[768,1536]{1,0:T(8,128)(2,1)}, bf16[768,1536]{1,0:T(8,128)(2,1)}, u32[]{:S(2)}, u32[]{:S(2)}) collective-permute-start(bf16[768,1536]{1,0:T(8,128)(2,1)} %dynamic-slice_convert_fusion.3), channel_id=1, source_target_pairs={{0,1},{1,0},{2,3},{3,2},{4,5},{5,4},{6,7},{7,6},{8,9},{9,8},{10,11... | collective-permute-start | bytes 7077896 | tf_op jit(solution)/shard_map/ppermute | solution.py:204
  655.9 38.3 %collective-permute-start.35 = (bf16[768,1536]{0,1:T(8,128)(2,1)}, bf16[768,1536]{0,1:T(8,128)(2,1)}, u32[]{:S(2)}, u32[]{:S(2)}) collective-permute-start(bf16[768,1536]{0,1:T(8,128)(2,1)} %dynamic-slice_convert_fusion.1), channel_id=1, source_target_pairs={{0,1},{1,0},{2,3},{3,2},{4,5},{5,4},{6,7},{7,6},{8,9},{9,8},{10,11... | collective-permute-start | bytes 7077896 | tf_op jit(solution)/shard_map/ppermute | solution.py:204
  659.3 49.9 %collective-permute-start.11 = (bf16[2,2,2,48,1152]{4,3,0,1,2:T(8,128)(2,1)}, bf16[2,2,2,48,1152]{4,3,0,1,2:T(8,128)(2,1)}, u32[]{:S(2)}, u32[]{:S(2)}) collective-permute-start(bf16[2,2,2,48,1152]{4,3,0,1,2:T(8,128)(2,1)} %fusion.116), channel_id=1, source_target_pairs={{0,2},{2,0},{4,6},{6,4},{8,10},{10,8},{12,14},{14,12},{16,18},{18,... | collective-permute-start | bytes 2654216 | tf_op jit(solution)/shard_map/ppermute | solution.py:204
  663.4 48.2 %collective-permute-start.6 = (bf16[2,2,2,48,1152]{4,3,0,1,2:T(8,128)(2,1)}, bf16[2,2,2,48,1152]{4,3,0,1,2:T(8,128)(2,1)}, u32[]{:S(2)}, u32[]{:S(2)}) collective-permute-start(bf16[2,2,2,48,1152]{4,3,0,1,2:T(8,128)(2,1)} %fusion.115), channel_id=1, source_target_pairs={{0,2},{2,0},{4,6},{6,4},{8,10},{10,8},{12,14},{14,12},{16,18},{18,... | collective-permute-start | bytes 2654216 | tf_op jit(solution)/shard_map/ppermute | solution.py:204
  670.4 105.0 %collective-permute-start.31 = (bf16[2,2,2,48,1536]{4,3,0,1,2:T(8,128)(2,1)}, bf16[2,2,2,48,1536]{4,3,0,1,2:T(8,128)(2,1)}, u32[]{:S(2)}, u32[]{:S(2)}) collective-permute-start(bf16[2,2,2,48,1536]{4,3,0,1,2:T(8,128)(2,1)} %fusion.70), channel_id=1, source_target_pairs={{0,4},{2,6},{4,0},{6,2},{8,12},{10,14},{12,8},{14,10},{16,20},{18,... | collective-permute-start | bytes 3538952 | tf_op jit(solution)/shard_map/ppermute | solution.py:204
  685.7 92.7 %collective-permute-start.41 = (bf16[2,2,2,48,1536]{4,3,0,1,2:T(8,128)(2,1)}, bf16[2,2,2,48,1536]{4,3,0,1,2:T(8,128)(2,1)}, u32[]{:S(2)}, u32[]{:S(2)}) collective-permute-start(bf16[2,2,2,48,1536]{4,3,0,1,2:T(8,128)(2,1)} %fusion.71), channel_id=1, source_target_pairs={{0,2},{2,0},{4,6},{6,4},{8,10},{10,8},{12,14},{14,12},{16,18},{18,... | collective-permute-start | bytes 3538952 | tf_op jit(solution)/shard_map/ppermute | solution.py:204
  694.2 89.0 %collective-permute-start.26 = (bf16[2,2,2,48,1536]{4,3,0,1,2:T(8,128)(2,1)}, bf16[2,2,2,48,1536]{4,3,0,1,2:T(8,128)(2,1)}, u32[]{:S(2)}, u32[]{:S(2)}) collective-permute-start(bf16[2,2,2,48,1536]{4,3,0,1,2:T(8,128)(2,1)} %fusion.69), channel_id=1, source_target_pairs={{0,4},{2,6},{4,0},{6,2},{8,12},{10,14},{12,8},{14,10},{16,20},{18,... | collective-permute-start | bytes 3538952 | tf_op jit(solution)/shard_map/ppermute | solution.py:204
  709.1 76.7 %collective-permute-start.36 = (bf16[2,2,2,48,1536]{4,3,2,1,0:T(8,128)(2,1)}, bf16[2,2,2,48,1536]{4,3,2,1,0:T(8,128)(2,1)}, u32[]{:S(2)}, u32[]{:S(2)}) collective-permute-start(bf16[2,2,2,48,1536]{4,3,2,1,0:T(8,128)(2,1)} %fusion.68), channel_id=1, source_target_pairs={{0,2},{2,0},{4,6},{6,4},{8,10},{10,8},{12,14},{14,12},{16,18},{18,... | collective-permute-start | bytes 3538952 | tf_op jit(solution)/shard_map/ppermute | solution.py:204
  711.6 21.7 %collective-permute-start.12 = (bf16[2,2,48,1152]{3,2,0,1:T(8,128)(2,1)S(1)}, bf16[2,2,48,1152]{3,2,0,1:T(8,128)(2,1)S(1)}, u32[]{:S(2)}, u32[]{:S(2)}) collective-permute-start(bf16[2,2,48,1152]{3,2,0,1:T(8,128)(2,1)S(1)} %fusion.135), channel_id=1, source_target_pairs={{0,4},{2,6},{4,0},{6,2},{8,12},{10,14},{12,8},{14,10},{16,20},{18,... | collective-permute-start | bytes 1327112 | tf_op jit(solution)/shard_map/ppermute | solution.py:204
  733.2 11.3 %collective-permute-start.7 = (bf16[2,2,48,1152]{3,2,0,1:T(8,128)(2,1)S(1)}, bf16[2,2,48,1152]{3,2,0,1:T(8,128)(2,1)S(1)}, u32[]{:S(2)}, u32[]{:S(2)}) collective-permute-start(bf16[2,2,48,1152]{3,2,0,1:T(8,128)(2,1)S(1)} %fusion.134), channel_id=1, source_target_pairs={{0,4},{2,6},{4,0},{6,2},{8,12},{10,14},{12,8},{14,10},{16,20},{18,... | collective-permute-start | bytes 1327112 | tf_op jit(solution)/shard_map/ppermute | solution.py:204
  744.5 5.9 collective-permute-start.13
  750.5 5.9 collective-permute-start.8
  756.4 8.9 collective-permute-start.14
  765.3 6.8 collective-permute-start.9
  772.1 15.6 %collective-permute-start.56 = (f32[48,1152]{1,0:T(8,128)S(1)}, f32[48,1152]{1,0:T(8,128)S(1)}, u32[]{:S(2)}, u32[]{:S(2)}) collective-permute-start(f32[48,1152]{1,0:T(8,128)S(1)} %get-tuple-element.130), channel_id=1, source_target_pairs={{0,1},{1,0},{2,3},{3,2},{4,5},{5,4},{6,7},{7,6},{8,9},{9,8},{10,11... | collective-permute-start | bytes 663560 | tf_op jit(solution)/shard_map/ppermute | solution.py:204
  775.4 13.6 %collective-permute-start.55 = (f32[48,1152]{1,0:T(8,128)S(1)}, f32[48,1152]{1,0:T(8,128)S(1)}, u32[]{:S(2)}, u32[]{:S(2)}) collective-permute-start(f32[48,1152]{1,0:T(8,128)S(1)} %get-tuple-element.132), channel_id=1, source_target_pairs={{0,1},{1,0},{2,3},{3,2},{4,5},{5,4},{6,7},{7,6},{8,9},{9,8},{10,11... | collective-permute-start | bytes 663560 | tf_op jit(solution)/shard_map/ppermute | solution.py:204
  778.4 16.2 %collective-permute-start.32 = (bf16[2,2,48,1536]{3,2,0,1:T(8,128)(2,1)S(1)}, bf16[2,2,48,1536]{3,2,0,1:T(8,128)(2,1)S(1)}, u32[]{:S(2)}, u32[]{:S(2)}) collective-permute-start(bf16[2,2,48,1536]{3,2,0,1:T(8,128)(2,1)S(1)} %fusion.131), channel_id=1, source_target_pairs={{0,2},{2,0},{4,6},{6,4},{8,10},{10,8},{12,14},{14,12},{16,18},{18,... | collective-permute-start | bytes 1769480 | tf_op jit(solution)/shard_map/ppermute | solution.py:204
  783.2 16.3 %collective-permute-start.42 = (bf16[2,2,48,1536]{3,2,0,1:T(8,128)(2,1)S(1)}, bf16[2,2,48,1536]{3,2,0,1:T(8,128)(2,1)S(1)}, u32[]{:S(2)}, u32[]{:S(2)}) collective-permute-start(bf16[2,2,48,1536]{3,2,0,1:T(8,128)(2,1)S(1)} %fusion.133), channel_id=1, source_target_pairs={{0,4},{2,6},{4,0},{6,2},{8,12},{10,14},{12,8},{14,10},{16,20},{18,... | collective-permute-start | bytes 1769480 | tf_op jit(solution)/shard_map/ppermute | solution.py:204
  785.8 20.7 %collective-permute-start.27 = (bf16[2,2,48,1536]{3,2,0,1:T(8,128)(2,1)S(1)}, bf16[2,2,48,1536]{3,2,0,1:T(8,128)(2,1)S(1)}, u32[]{:S(2)}, u32[]{:S(2)}) collective-permute-start(bf16[2,2,48,1536]{3,2,0,1:T(8,128)(2,1)S(1)} %fusion.130), channel_id=1, source_target_pairs={{0,2},{2,0},{4,6},{6,4},{8,10},{10,8},{12,14},{14,12},{16,18},{18,... | collective-permute-start | bytes 1769480 | tf_op jit(solution)/shard_map/ppermute | solution.py:204
  787.7 23.4 %collective-permute-start.37 = (bf16[2,2,48,1536]{3,2,1,0:T(8,128)(2,1)S(1)}, bf16[2,2,48,1536]{3,2,1,0:T(8,128)(2,1)S(1)}, u32[]{:S(2)}, u32[]{:S(2)}) collective-permute-start(bf16[2,2,48,1536]{3,2,1,0:T(8,128)(2,1)S(1)} %fusion.132), channel_id=1, source_target_pairs={{0,4},{2,6},{4,0},{6,2},{8,12},{10,14},{12,8},{14,10},{16,20},{18,... | collective-permute-start | bytes 1769480 | tf_op jit(solution)/shard_map/ppermute | solution.py:204
  794.8 16.6 %collective-permute-start.33 = (bf16[2,48,1536]{2,1,0:T(8,128)(2,1)S(1)}, bf16[2,48,1536]{2,1,0:T(8,128)(2,1)S(1)}, u32[]{:S(2)}, u32[]{:S(2)}) collective-permute-start(bf16[2,48,1536]{2,1,0:T(8,128)(2,1)S(1)} %fusion.151), channel_id=1, source_target_pairs={{0,8},{2,10},{4,12},{6,14},{8,0},{10,2},{12,4},{14,6},{16,24},{18,... | collective-permute-start | bytes 884744 | tf_op jit(solution)/shard_map/ppermute | solution.py:204
  799.6 14.3 %collective-permute-start.43 = (bf16[2,48,1536]{2,1,0:T(8,128)(2,1)S(1)}, bf16[2,48,1536]{2,1,0:T(8,128)(2,1)S(1)}, u32[]{:S(2)}, u32[]{:S(2)}) collective-permute-start(bf16[2,48,1536]{2,1,0:T(8,128)(2,1)S(1)} %fusion.153), channel_id=1, source_target_pairs={{0,8},{2,10},{4,12},{6,14},{8,0},{10,2},{12,4},{14,6},{16,24},{18,... | collective-permute-start | bytes 884744 | tf_op jit(solution)/shard_map/ppermute | solution.py:204
  806.7 17.0 %collective-permute-start.28 = (bf16[2,48,1536]{2,1,0:T(8,128)(2,1)S(1)}, bf16[2,48,1536]{2,1,0:T(8,128)(2,1)S(1)}, u32[]{:S(2)}, u32[]{:S(2)}) collective-permute-start(bf16[2,48,1536]{2,1,0:T(8,128)(2,1)S(1)} %fusion.150), channel_id=1, source_target_pairs={{0,8},{2,10},{4,12},{6,14},{8,0},{10,2},{12,4},{14,6},{16,24},{18,... | collective-permute-start | bytes 884744 | tf_op jit(solution)/shard_map/ppermute | solution.py:204
  811.4 17.0 %collective-permute-start.38 = (bf16[2,48,1536]{2,1,0:T(8,128)(2,1)S(1)}, bf16[2,48,1536]{2,1,0:T(8,128)(2,1)S(1)}, u32[]{:S(2)}, u32[]{:S(2)}) collective-permute-start(bf16[2,48,1536]{2,1,0:T(8,128)(2,1)S(1)} %fusion.152), channel_id=1, source_target_pairs={{0,8},{2,10},{4,12},{6,14},{8,0},{10,2},{12,4},{14,6},{16,24},{18,... | collective-permute-start | bytes 884744 | tf_op jit(solution)/shard_map/ppermute | solution.py:204
  811.5 17.2 %collective-permute-start.34 = (bf16[48,1536]{1,0:T(8,128)(2,1)S(1)}, bf16[48,1536]{1,0:T(8,128)(2,1)S(1)}, u32[]{:S(2)}, u32[]{:S(2)}) collective-permute-start(bf16[48,1536]{1,0:T(8,128)(2,1)S(1)} %fusion.168), channel_id=1, source_target_pairs={{0,16},{2,18},{4,20},{6,22},{8,24},{10,26},{12,28},{14,30},{16,0},... | collective-permute-start | bytes 442376 | tf_op jit(solution)/shard_map/ppermute | solution.py:204
  814.0 21.0 %collective-permute-start.44 = (bf16[48,1536]{1,0:T(8,128)(2,1)S(1)}, bf16[48,1536]{1,0:T(8,128)(2,1)S(1)}, u32[]{:S(2)}, u32[]{:S(2)}) collective-permute-start(bf16[48,1536]{1,0:T(8,128)(2,1)S(1)} %fusion.170), channel_id=1, source_target_pairs={{0,16},{2,18},{4,20},{6,22},{8,24},{10,26},{12,28},{14,30},{16,0},... | collective-permute-start | bytes 442376 | tf_op jit(solution)/shard_map/ppermute | solution.py:204
  823.8 14.3 %collective-permute-start.29 = (bf16[48,1536]{1,0:T(8,128)(2,1)S(1)}, bf16[48,1536]{1,0:T(8,128)(2,1)S(1)}, u32[]{:S(2)}, u32[]{:S(2)}) collective-permute-start(bf16[48,1536]{1,0:T(8,128)(2,1)S(1)} %fusion.167), channel_id=1, source_target_pairs={{0,16},{2,18},{4,20},{6,22},{8,24},{10,26},{12,28},{14,30},{16,0},... | collective-permute-start | bytes 442376 | tf_op jit(solution)/shard_map/ppermute | solution.py:204
  828.5 11.3 %collective-permute-start.39 = (bf16[48,1536]{1,0:T(8,128)(2,1)S(1)}, bf16[48,1536]{1,0:T(8,128)(2,1)S(1)}, u32[]{:S(2)}, u32[]{:S(2)}) collective-permute-start(bf16[48,1536]{1,0:T(8,128)(2,1)S(1)} %fusion.169), channel_id=1, source_target_pairs={{0,16},{2,18},{4,20},{6,22},{8,24},{10,26},{12,28},{14,30},{16,0},... | collective-permute-start | bytes 442376 | tf_op jit(solution)/shard_map/ppermute | solution.py:204
  829.4 45.6 %collective-permute-start.60 = (f32[48,1536]{1,0:T(8,128)S(1)}, f32[48,1536]{1,0:T(8,128)}, u32[]{:S(2)}, u32[]{:S(2)}) collective-permute-start(f32[48,1536]{1,0:T(8,128)S(1)} %get-tuple-element.122), channel_id=1, source_target_pairs={{0,1},{1,0},{2,3},{3,2},{4,5},{5,4},{6,7},{7,6},{8,9},{9,8},{10,11... | collective-permute-start | bytes 884744 | tf_op jit(solution)/shard_map/ppermute | solution.py:204
  835.6 42.3 %collective-permute-start.62 = (f32[48,1536]{1,0:T(8,128)S(1)}, f32[48,1536]{1,0:T(8,128)}, u32[]{:S(2)}, u32[]{:S(2)}) collective-permute-start(f32[48,1536]{1,0:T(8,128)S(1)} %get-tuple-element.118), channel_id=1, source_target_pairs={{0,1},{1,0},{2,3},{3,2},{4,5},{5,4},{6,7},{7,6},{8,9},{9,8},{10,11... | collective-permute-start | bytes 884744 | tf_op jit(solution)/shard_map/ppermute | solution.py:204
  838.8 37.2 %collective-permute-start.59 = (f32[48,1536]{1,0:T(8,128)S(1)}, f32[48,1536]{1,0:T(8,128)}, u32[]{:S(2)}, u32[]{:S(2)}) collective-permute-start(f32[48,1536]{1,0:T(8,128)S(1)} %get-tuple-element.124), channel_id=1, source_target_pairs={{0,1},{1,0},{2,3},{3,2},{4,5},{5,4},{6,7},{7,6},{8,9},{9,8},{10,11... | collective-permute-start | bytes 884744 | tf_op jit(solution)/shard_map/ppermute | solution.py:204
  840.5 48.4 %collective-permute-start.61 = (f32[48,1536]{1,0:T(8,128)S(1)}, f32[48,1536]{1,0:T(8,128)}, u32[]{:S(2)}, u32[]{:S(2)}) collective-permute-start(f32[48,1536]{1,0:T(8,128)S(1)} %get-tuple-element.120), channel_id=1, source_target_pairs={{0,1},{1,0},{2,3},{3,2},{4,5},{5,4},{6,7},{7,6},{8,9},{9,8},{10,11... | collective-permute-start | bytes 884744 | tf_op jit(solution)/shard_map/ppermute | solution.py:204
  845.1 3.7 collective-permute-start.51
  849.5 3.6 collective-permute-start.52
  853.7 3.6 collective-permute-start.53
  857.9 4.5 collective-permute-start.54
  (130 other events, 1040.0 us)
Sparse Core Ops, SparseCore 0:
  12.1 66.0 all-gather.9
  81.7 79.4 all-gather.11
  164.5 99.9 all-gather.13
  265.9 13.1 all-gather.15
  280.5 23.0 all-gather.17
  304.9 27.5 all-gather.19

commit v2 on v1

v2 whole, which is shorter than its diff:
```python
import functools

import jax
import jax.numpy as jnp
from jax import lax
from jax.sharding import PartitionSpec as P

HD = 64
V = 70
STEP = 10


NORM_EPS = 1e-05
BETA_ONE = 0.9
BETA_TWO = 0.95
ADAM_EPS = 1e-08
DECAY = 0.1
RATE_MATRIX = 0.05
RATE_VECTOR = 0.3
CLIP = 0.05


def rotary_tables(length, size):
    freq = 10000.0 ** (-jnp.arange(size // 2, dtype=jnp.float32) * 2.0 / size)
    angle = jnp.arange(length, dtype=jnp.float32)[:, None] * freq[None, :]
    return (jnp.cos(angle)[:, None, :], jnp.sin(angle)[:, None, :])


def rotate(value, cosine, sine):
    half = value.shape[-1] // 2
    first = value[..., :half]
    second = value[..., half:]
    return jnp.concatenate([first * cosine - second * sine, second * cosine + first * sine], -1)


def normalize(resid, gain, bias):
    mean = jnp.mean(resid, -1, keepdims=True)
    centred = resid - mean
    inverse = lax.rsqrt(jnp.mean(centred * centred, -1, keepdims=True) + NORM_EPS)
    unit = centred * inverse
    return (unit * gain + bias, unit, inverse)


def normalize_back(grad, unit, inverse, gain):
    scaled = grad * gain
    across = (
        scaled
        - jnp.mean(scaled, -1, keepdims=True)
        - unit * jnp.mean(scaled * unit, -1, keepdims=True)
    )
    return (across * inverse, jnp.sum(grad * unit, 0), jnp.sum(grad, 0))


def dot(left, right):
    return jnp.dot(left, right, preferred_element_type=jnp.float32)


def cross(left, right):
    return jnp.dot(left.T, right, preferred_element_type=jnp.float32)


def in_order(own, other):
    first = lax.axis_index("dp") == 0
    return jnp.concatenate(
        [jnp.where(first, own, other), jnp.where(first, other, own)], 1
    )


def half_of(value, core):
    half = value.shape[1] // 2
    return lax.dynamic_slice_in_dim(value, core * half, half, 1)


def attention_forward(resid, mixer, gains, cosine, sine, same):
    (own_a, other_a), (own_b, other_b) = mixer
    length, width = resid.shape
    heads = width // HD
    half = width // 2
    w_query = in_order(own_a[:, :half], other_a[:, :half])
    w_keys = in_order(own_a[:, half:], other_a[:, half:])
    w_values = in_order(own_b[:, :half], other_b[:, :half])
    w_out = in_order(own_b[:, half:], other_b[:, half:])
    normed, unit_in, inverse_in = normalize(resid, gains[0, 0], gains[0, 1])
    normed_low = normed.astype(jnp.bfloat16)
    shape = (length, heads, HD)
    query = rotate(dot(normed_low, w_query).reshape(shape), cosine, sine).astype(jnp.bfloat16)
    keys = rotate(dot(normed_low, w_keys).reshape(shape), cosine, sine).astype(jnp.bfloat16)
    values = dot(normed_low, w_values).reshape(shape).astype(jnp.bfloat16)
    scores = jnp.einsum("qhe,khe->hqk", query, keys, preferred_element_type=jnp.float32) * HD ** (
        -0.5
    )
    scores = jnp.where(same[None], scores, -1000000000.0)
    top = jnp.max(scores, -1, keepdims=True)
    expo = jnp.exp(scores - top)
    total = jnp.sum(expo, -1, keepdims=True)
    probs = expo / total
    probs_low = probs.astype(jnp.bfloat16)
    attended = jnp.einsum("hqk,khe->qhe", probs_low, values, preferred_element_type=jnp.float32)
    attended = attended.astype(jnp.bfloat16).reshape(length, width)
    middle = resid + dot(attended, w_out)
    kept = (
        (w_query, w_keys, w_values, w_out),
        normed_low,
        unit_in,
        inverse_in,
        query,
        keys,
        values,
        probs,
        probs_low,
        attended,
    )
    return middle, kept


def hidden_forward(middle, ups, downs, gains):
    normed_mid, unit_mid, inverse_mid = normalize(middle, gains[1, 0], gains[1, 1])
    normed_mid_low = normed_mid.astype(jnp.bfloat16)
    hidden = [dot(normed_mid_low, w) for w in ups]
    active = [jax.nn.gelu(h).astype(jnp.bfloat16) for h in hidden]
    output = middle
    for a, w in zip(active, downs):
        output = output + dot(a, w)
    return output, (unit_mid, inverse_mid, normed_mid_low, hidden, active)


def adam_step(master, grad, first, second, rate, decay):
    first = BETA_ONE * first + (1.0 - BETA_ONE) * grad
    second = BETA_TWO * second + (1.0 - BETA_TWO) * grad * grad
    fix_one = 1.0 - BETA_ONE**STEP
    fix_two = 1.0 - BETA_TWO**STEP
    update = first / fix_one / (jnp.sqrt(second / fix_two) + ADAM_EPS) + decay * master
    return (master - rate * update, first, second)


def bits_of(size, swap):
    order = list(range(size.bit_length() - 1))
    if swap and len(order) > 1:
        order[0], order[1] = order[1], order[0]
    return order


def my_bit(bit):
    return lax.rem(lax.div(lax.axis_index("fsdp"), 1 << bit), 2)


class Links:
    def __init__(self, size):
        self.size = size
        self.live = []
        self.flying = []

    def add(self, stream):
        box = []
        link, rows = next(stream)
        self.live.append((stream, box, link, rows))
        return box

    def start(self):
        groups = {}
        for item in self.live:
            key = (str(item[2]), str(item[3].dtype), item[3].shape[1])
            groups.setdefault(key, []).append(item)
        self.flying = []
        for items in groups.values():
            link = items[0][2]
            rows = [item[3] for item in items]
            rows = rows[0] if len(rows) == 1 else jnp.concatenate(rows, 0)
            if link == "dp":
                got = lax.ppermute(rows, "dp", [(0, 1), (1, 0)])
            else:
                pairs = [(i, i ^ (1 << link)) for i in range(self.size)]
                got = lax.ppermute(rows, "fsdp", pairs)
            self.flying.append((items, got))

    def finish(self, tied=()):
        got, tied = lax.optimization_barrier(([g for _, g in self.flying], tied))
        self.live = []
        for (items, _), rows in zip(self.flying, got):
            at = 0
            for stream, box, _, sent in items:
                part = rows if len(items) == 1 else rows[at : at + sent.shape[0]]
                at += sent.shape[0]
                try:
                    link, following = stream.send(part)
                    self.live.append((stream, box, link, following))
                except StopIteration as end:
                    box.append(end.value)
        return tied

    def drain(self):
        while self.live:
            self.start()
            self.finish()


def gather_stream(shard, size, swap):
    columns = shard.shape[1]
    value, held = shard, []
    for bit in reversed(bits_of(size, swap)):
        got = yield bit, value.reshape(-1, columns)
        got = got.reshape(value.shape)
        low = my_bit(bit) == 0
        place = len([b for b in held if b > bit])
        held.append(bit)
        value = jnp.stack(
            [jnp.where(low, value, got), jnp.where(low, got, value)], place
        )
    value = value.reshape(-1, columns)
    other = yield "dp", value
    return value, other


def swap_stream(value):
    other = yield "dp", value
    return value, other


def scatter_steps(value, size, low, swap):
    levels = size.bit_length() - 1
    rows, columns = value.shape[0] // size, value.shape[1]
    value = value.reshape((2,) * levels + (rows, columns))
    left = list(range(levels))[::-1]
    for bit in bits_of(size, swap):
        place = left.index(bit)
        left.remove(bit)
        mine = my_bit(bit)
        send = lax.dynamic_index_in_dim(value, 1 - mine, place, keepdims=False)
        keep = lax.dynamic_index_in_dim(value, mine, place, keepdims=False)
        got = yield bit, send.astype(low).reshape(-1, columns)
        value = keep + got.reshape(keep.shape).astype(jnp.float32)
    return value


def tile_stream(send, keep, size, swap):
    got = yield "dp", send
    return (yield from scatter_steps(keep() + got.astype(jnp.float32), size, jnp.bfloat16, swap))


def small_stream(value, size, rows):
    got = yield "dp", value
    value = (value + got).reshape(-1, size, rows).transpose(1, 0, 2).reshape(-1, rows)
    return (yield from scatter_steps(value, size, jnp.float32, False))


def total_stream(value, size):
    for link in ["dp"] + bits_of(size, False):
        got = yield link, value
        value = value + got
    return value


def up_to_parts(expand_shard, size, rows, parts):
    r = expand_shard.shape[0]
    return expand_shard.reshape(r, size, parts, rows).transpose(0, 2, 1, 3).reshape(r, -1)


def up_from_parts(expand_shard, size, rows, parts):
    r = expand_shard.shape[0]
    return expand_shard.reshape(r, parts, size, rows).transpose(0, 2, 1, 3).reshape(r, -1)


def body(
    fsdp,
    codons,
    masked,
    segments,
    inward,
    outward,
    expand,
    shrink,
    codon_table,
    norm_params,
    inward_first,
    inward_second,
    outward_first,
    outward_second,
    expand_first,
    expand_second,
    shrink_first,
    shrink_second,
    table_first,
    table_second,
    norm_first,
    norm_second,
):
    layers = inward.shape[0]
    length = codons.shape[0]
    rows = inward.shape[1]
    width = rows * fsdp
    half = width // 2
    parts = shrink.shape[1] // rows
    low = jnp.bfloat16
    core = lax.axis_index("dp")
    weight = masked.astype(jnp.float32)
    inputs = jnp.where(masked == 1, V - 1, codons)
    links = Links(fsdp)

    norms = norm_params.shape[0] * 2
    small = jnp.concatenate(
        [codon_table.astype(low), norm_params.astype(low).reshape(norms, rows)], 0
    ).reshape(-1)
    small_size = small.shape[0]
    small = jnp.pad(small, (0, -small_size % (16 * width))).reshape(-1, width)

    def mixer_of(l):
        w_in, w_out = inward[l].astype(low), outward[l].astype(low)
        pieces = [half_of(w_in[:, p * width : (p + 1) * width], core) for p in range(3)]
        pieces.append(half_of(w_out, core))
        return jnp.concatenate(pieces[:2], 1), jnp.concatenate(pieces[2:], 1)

    def up_of(l):
        own = half_of(up_to_parts(expand[l].astype(low), fsdp, rows, parts), core)
        return own[:, :width], own[:, width:]

    def down_of(l):
        own = lax.dynamic_slice_in_dim(shrink[l].astype(low), core * 2 * rows, 2 * rows, 0)
        return own[:rows], own[rows:]

    def gather(pair):
        return [links.add(gather_stream(v, fsdp, swap)) for v, swap in zip(pair, (False, True))]

    late = jnp.concatenate(up_of(layers - 1) + down_of(layers - 1), 1)
    late = lax.all_gather(late, "fsdp", axis=0, tiled=True)
    mixers, ups, downs = [None] * layers, [None] * layers, [None] * layers
    table_box = links.add(gather_stream(small, fsdp, False))
    for l in range(layers):
        mixers[l] = gather(mixer_of(l))
        links.start()
        links.finish()
        if l < layers - 1:
            ups[l] = gather(up_of(l))
            links.start()
            links.finish()
            downs[l] = gather(down_of(l))
            links.start()
            links.finish()
    links.drain()
    late_box = links.add(swap_stream(late))
    links.drain()
    late, late_other = late_box[0]
    cut = lambda v, p: v[:, p * width : (p + 1) * width]
    ups[-1] = [[(cut(late, p), cut(late_other, p))] for p in (0, 1)]
    downs[-1] = [[(cut(late, p), cut(late_other, p))] for p in (2, 3)]
    pairs = lambda boxes: (boxes[0][0], boxes[1][0])
    own_first = lambda boxes: [b[0][0] for b in boxes] + [b[0][1] for b in boxes]
    small = table_box[0][0].reshape(fsdp, -1)[:, :small_size]
    small = small.reshape(fsdp, V + norms, rows).transpose(1, 0, 2).reshape(V + norms, width)
    table_low = small[:V]
    gains = small[V:].astype(jnp.float32).reshape(-1, 2, width)

    cosine, sine = rotary_tables(length, HD)
    same = segments[:, None] == segments[None, :]
    vocab_ids = jnp.arange(V, dtype=jnp.int32)
    chosen = (inputs[:, None] == vocab_ids[None, :]).astype(low)
    resid = dot(chosen, table_low)
    kept = []
    for l in range(layers):
        gain = gains[2 * l : 2 * l + 2]
        middle, kept_mixer = attention_forward(resid, pairs(mixers[l]), gain, cosine, sine, same)
        resid, kept_hidden = hidden_forward(middle, own_first(ups[l]), own_first(downs[l]), gain)
        kept.append((kept_mixer, kept_hidden))
    final_gain = gains[2 * layers]
    normed_out, unit_out, inverse_out = normalize(resid, final_gain[0], final_gain[1])
    head_in = normed_out.astype(low)
    logits = jnp.einsum("sd,vd->sv", head_in, table_low, preferred_element_type=jnp.float32)
    top = jnp.max(logits, -1, keepdims=True)
    lse_head = top + jnp.log(jnp.sum(jnp.exp(logits - top), -1, keepdims=True))
    targets = (codons[:, None] == vocab_ids[None, :]).astype(jnp.float32)
    picked = jnp.sum(logits * targets, -1)
    loss_local = jnp.sum((lse_head[:, 0] - picked) * weight)
    scalars = jnp.stack([loss_local, jnp.sum(weight)])
    scalars_box = links.add(total_stream(jnp.pad(scalars, (0, 126))[None], fsdp))
    grad_logits = ((jnp.exp(logits - lse_head) - targets) * weight[:, None]).astype(low)
    grad_table = cross(grad_logits, head_in)
    grad_head = dot(grad_logits, table_low)
    grad, grad_final_gain, grad_final_bias = normalize_back(
        grad_head, unit_out, inverse_out, final_gain[0]
    )

    def scatter(tiles):
        boxes = []
        for (theirs, own), swap in zip(tiles, (False, True)):
            make = lambda pairs: jnp.concatenate([cross(a, b) for a, b in pairs], 1)
            send = make(theirs).astype(low)
            keep = functools.partial(make, own)
            boxes.append(links.add(tile_stream(send, keep, fsdp, swap)))
        return boxes

    grad_norms = [grad_final_gain, grad_final_bias]
    shares = [[None] * layers for _ in range(3)]
    for l in reversed(range(layers)):
        (w_mix, normed_low, unit_in, inverse_in, query, keys, values, probs, probs_low, attended), (
            unit_mid, inverse_mid, normed_mid_low, hidden, active,
        ) = kept[l]
        up_tiles, down_tiles = own_first(ups[l]), own_first(downs[l])
        gain = gains[2 * l : 2 * l + 2]
        heads = width // HD
        branch = grad.astype(low)
        links.start()
        grad_hidden = []
        for h, w in zip(hidden, down_tiles):
            _, gelu_back = jax.vjp(jax.nn.gelu, h)
            grad_active = jnp.einsum("sd,fd->sf", branch, w, preferred_element_type=jnp.float32)
            grad_hidden.append(gelu_back(grad_active)[0].astype(low))
        grad_hidden, branch = links.finish((grad_hidden, branch))
        shares[2][l] = scatter(
            [([(active[2 + s], branch)], [(active[s], branch)]) for s in range(2)]
        )
        links.start()
        grad_normed = 0.0
        for g, w in zip(grad_hidden, up_tiles):
            grad_normed = grad_normed + jnp.einsum(
                "sf,df->sd", g, w, preferred_element_type=jnp.float32
            )
        grad_middle, gain_mid, bias_mid = normalize_back(
            grad_normed, unit_mid, inverse_mid, gain[1, 0]
        )
        grad_middle = grad_middle + grad
        grad_middle, grad_hidden = links.finish((grad_middle, grad_hidden))
        shares[1][l] = scatter(
            [
                ([(normed_mid_low, grad_hidden[2 + s])], [(normed_mid_low, grad_hidden[s])])
                for s in range(2)
            ]
        )
        links.start()
        attn_grad = grad_middle.astype(low)
        w_query, w_keys, w_values, w_out = w_mix
        grad_attended = jnp.einsum(
            "sd,ed->se", attn_grad, w_out, preferred_element_type=jnp.float32
        )
        grad_attended = grad_attended.astype(low).reshape(length, heads, HD)
        grad_probs = jnp.einsum(
            "qhe,khe->hqk", grad_attended, values, preferred_element_type=jnp.float32
        )
        grad_scores = probs * (grad_probs - jnp.sum(probs * grad_probs, -1, keepdims=True))
        grad_scores = grad_scores.astype(low)
        grad_scores, grad_attended, attn_grad = links.finish(
            (grad_scores, grad_attended, attn_grad)
        )
        links.start()
        scale = HD ** (-0.5)
        grad_query = (
            jnp.einsum("hqk,khe->qhe", grad_scores, keys, preferred_element_type=jnp.float32)
            * scale
        )
        grad_keys = (
            jnp.einsum("hqk,qhe->khe", grad_scores, query, preferred_element_type=jnp.float32)
            * scale
        )
        grad_values = jnp.einsum(
            "hqk,qhe->khe", probs_low, grad_attended, preferred_element_type=jnp.float32
        )
        flat = lambda v: v.reshape(length, width).astype(low)
        grad_query = flat(rotate(grad_query, cosine, -sine))
        grad_keys = flat(rotate(grad_keys, cosine, -sine))
        grad_values = flat(grad_values)
        grad_query, grad_keys, grad_values, attn_grad = links.finish(
            (grad_query, grad_keys, grad_values, attn_grad)
        )
        tiles = [([], []), ([], [])]
        for place, c in enumerate((1 - core, core)):
            g_q, g_k, g_v, g_o = (
                half_of(v, c) for v in (grad_query, grad_keys, grad_values, attn_grad)
            )
            tiles[0][place].append((normed_low, jnp.concatenate([g_q, g_k], 1)))
            tiles[1][place].extend([(normed_low, g_v), (attended, g_o)])
        shares[0][l] = scatter(tiles)
        links.start()
        grad_normed = 0.0
        for g, w in ((grad_query, w_query), (grad_keys, w_keys), (grad_values, w_values)):
            grad_normed = grad_normed + jnp.einsum(
                "se,de->sd", g, w, preferred_element_type=jnp.float32
            )
        grad_resid, gain_in, bias_in = normalize_back(
            grad_normed, unit_in, inverse_in, gain[0, 0]
        )
        grad = grad_resid + grad_middle
        grad_norms = [gain_in, bias_in, gain_mid, bias_mid] + grad_norms
        if l == 0:
            grad_table = grad_table + cross(chosen, grad.astype(low))
        grad, grad_table = links.finish((grad, grad_table))
    grad_small = jnp.concatenate([grad_table, jnp.stack(grad_norms)], 0)
    small_box = links.add(small_stream(grad_small, fsdp, rows))
    links.drain()

    share_small = small_box[0]
    shares = [[[box[0] for box in pair] for pair in group] for group in shares]
    squares = 0.5 * jnp.sum(share_small * share_small)
    for value in sum(sum(shares, []), []):
        squares = squares + jnp.sum(value * value)
    squares = jnp.pad(squares.reshape(1, 1), ((0, 0), (0, 127)))
    total_box = links.add(total_stream(squares, fsdp))
    swapped = [
        [links.add(swap_stream(jnp.concatenate(pair, 0))) for pair in group] for group in shares
    ]
    links.drain()
    square_total = total_box[0][0, 0]
    loss_sum, count = scalars_box[0][0, 0], scalars_box[0][0, 1]

    def tiles_of(box):
        own, other = box[0]
        first = core == 0
        ordered = (jnp.where(first, own, other), jnp.where(first, other, own))
        return [v[s * rows : (s + 1) * rows] for v in ordered for s in range(2)]

    share_in, share_out, share_up, share_down = [], [], [], []
    for l in range(layers):
        a_0, b_0, a_1, b_1 = tiles_of(swapped[0][l])
        side = lambda x, y: jnp.concatenate([x, y], 1)
        share_in.append(
            jnp.concatenate(
                [a_0[:, :half], a_1[:, :half], a_0[:, half:], a_1[:, half:], b_0[:, :half], b_1[:, :half]], 1
            )
        )
        share_out.append(side(b_0[:, half:], b_1[:, half:]))
        up = jnp.concatenate(tiles_of(swapped[1][l]), 1)
        share_up.append(up_from_parts(up, fsdp, rows, parts))
        share_down.append(jnp.concatenate(tiles_of(swapped[2][l]), 0))
    group = (
        jnp.stack(share_in),
        jnp.stack(share_out),
        jnp.stack(share_up),
        jnp.stack(share_down),
        share_small[:V],
        share_small[V:].reshape(-1, 2, rows),
    )
    grad_norm = jnp.sqrt(square_total) / count
    factor = CLIP / jnp.maximum(grad_norm, CLIP)
    masters = (inward, outward, expand, shrink, codon_table, norm_params)
    firsts = (inward_first, outward_first, expand_first, shrink_first, table_first, norm_first)
    seconds = (
        inward_second,
        outward_second,
        expand_second,
        shrink_second,
        table_second,
        norm_second,
    )
    result = [loss_sum, count, grad_norm]
    for index in range(6):
        rate = RATE_VECTOR if index == 5 else RATE_MATRIX
        decay = 0.0 if index == 5 else DECAY
        clipped = group[index] / count * factor
        result.extend(
            adam_step(masters[index], clipped, firsts[index], seconds[index], rate, decay)
        )
    return tuple(result)


def solution(mesh):
    in_specs = (
        P(("fsdp", "dp")),
        P(("fsdp", "dp")),
        P(("fsdp", "dp")),
        P(None, "fsdp", None),
        P(None, "fsdp", None),
        P(None, "fsdp", None),
        P(None, "fsdp", None),
        P(None, "fsdp"),
        P(None, None, "fsdp"),
        P(None, "fsdp", None),
        P(None, "fsdp", None),
        P(None, "fsdp", None),
        P(None, "fsdp", None),
        P(None, "fsdp", None),
        P(None, "fsdp", None),
        P(None, "fsdp", None),
        P(None, "fsdp", None),
        P(None, "fsdp"),
        P(None, "fsdp"),
        P(None, None, "fsdp"),
        P(None, None, "fsdp"),
    )
    out_specs = (
        P(),
        P(),
        P(),
        P(None, "fsdp", None),
        P(None, "fsdp", None),
        P(None, "fsdp", None),
        P(None, "fsdp", None),
        P(None, "fsdp", None),
        P(None, "fsdp", None),
        P(None, "fsdp", None),
        P(None, "fsdp", None),
        P(None, "fsdp", None),
        P(None, "fsdp", None),
        P(None, "fsdp", None),
        P(None, "fsdp", None),
        P(None, "fsdp"),
        P(None, "fsdp"),
        P(None, "fsdp"),
        P(None, None, "fsdp"),
        P(None, None, "fsdp"),
        P(None, None, "fsdp"),
    )
    step = functools.partial(body, mesh.shape["fsdp"])
    return jax.shard_map(step, mesh=mesh, in_specs=in_specs, out_specs=out_specs, check_vma=False)
```

time: 913 us -> 716 us (0.78)
  waiting for transfers between devices: 399 us -> 150 us
  matrix products: 172 us -> 200 us
  starting transfers between devices: 63.9 us -> 77.2 us
    all_gather x6 -> x1, waiting for transfers between devices: 255 us -> 0.01 us  [body(): late = lax.all_gather(late, 'fsdp', axis=0, tiled=True)]
    sub x2 -> x4, matrix products: 19.2 us -> 51.1 us  [the longest x2 29.4 us: body(): grad_probs - jnp.sum(probs * grad_probs, -1, keepdims=True)]
    convert_element_type x11 -> x9, other arithmetic: 28.6 us -> 3.33 us  [the longest x2 1.3 us: attention_forward(): normed_low = normed.astype(jnp.bfloat16)]
    add x43 -> x57, other arithmetic: 38.1 us -> 20.1 us  [the longest x39 11.1 us: scatter_steps(): value = keep + got.reshape(keep.shape).astype(jnp.float32)]
    another operation x14 -> x57, other arithmetic: 4.35 us -> 20.8 us  [the longest x49 14.6 us: gather_stream(): jnp.stack([jnp.where(low, value, got), jnp.where(low, got, value)], place)]
    squeeze x10 -> x0, local copies, waits for them, and re-layouts: 16.2 us -> none  [the longest x1 5.76 us: body(): later[0, :, half:2 * half]]
    concatenate x6 -> x49, other arithmetic: 7.77 us -> 23.8 us  [the longest x41 21.7 us: start(): rows = rows[0] if len(rows) == 1 else jnp.concatenate(rows, 0)]
    slice x17 -> x67, local copies, waits for them, and re-layouts: 11.3 us -> 26.5 us  [the longest x41 21 us: finish(): part = rows if len(items) == 1 else rows[at:at + sent.shape[0]]]
  transfers between devices with their start and end apart: 69 -> 78, of which waited for: 39 -> 30; matrix products, arithmetic and copies ran while one was open for 21% -> 45% of each run, Pallas kernels for 0% -> 0%
where the time goes in v2:
time: 716 us; the launch traced here: 703 us
  matrix products  200 us (28%)
  waiting for transfers between devices  150 us (21%)
  other arithmetic  123 us (17%)
  local copies, waits for them, and re-layouts  122 us (17%)
  starting transfers between devices  77.2 us (11%)
  between operations  30.4 us (4%)
    ppermute x62, waiting for transfers between devices, start(): got = lax.ppermute(rows, 'fsdp', pairs)  149 us
    ppermute x62, starting transfers between devices, start(): got = lax.ppermute(rows, 'fsdp', pairs)  75 us
    dot_general x26, matrix products, dot(): return jnp.dot(left, right, preferred_element_type=jnp.float32)  43.5 us
    dot_general x30, matrix products, cross(): return jnp.dot(left.T, right, preferred_element_type=jnp.float32)  34.7 us
    unnamed x626, local copies, waits for them, and re-layouts  32 us
    sub x2, matrix products, body(): grad_probs - jnp.sum(probs * grad_probs, -1, keepdims=True)  29.4 us
    sub x2, matrix products, attention_forward(): expo = jnp.exp(scores - top)  21.7 us
    concatenate x41, other arithmetic, start(): rows = rows[0] if len(rows) == 1 else jnp.concatenate(rows, 0)  21.7 us
  transfers between devices with their start and end apart: 78, of which 30 were waited for; matrix products, arithmetic and copies ran while one was open for 45% of the time, Pallas kernels for 0%

profile of v2, /device:TPU:0, one launch (start us, length us, event | category | flops | bytes accessed | tf_op | source)
XLA Modules:
  0.0 703.0 jit_solution(7557758886424443579)
XLA Ops:
  10.4 4.0 collective-permute-start.10
  18.3 3.0 collective-permute-start.2
  24.7 11.6 %collective-permute-done = bf16[112,768]{1,0:T(8,128)(2,1)} collective-permute-done((bf16[112,768]{1,0:T(8,128)(2,1)}, bf16[112,768]{1,0:T(8,128)(2,1)}, u32[]{:S(2)}, u32[]{:S(2)}) %collective-permute-start) | collective-permute-done | bytes 172064 | tf_op jit(solution)/shard_map/ppermute | solution.py:173
  39.8 9.2 %collective-permute-done.1 = bf16[224,768]{1,0:T(8,128)(2,1)S(1)} collective-permute-done((bf16[224,768]{1,0:T(8,128)(2,1)S(1)}, bf16[224,768]{1,0:T(8,128)(2,1)S(1)}, u32[]{:S(2)}, u32[]{:S(2)}) %collective-permute-start.1) | collective-permute-done | bytes 344096 | tf_op jit(solution)/shard_map/ppermute | solution.py:173
  53.7 11.0 %collective-permute-done.5 = bf16[192,768]{1,0:T(8,128)(2,1)S(1)} collective-permute-done((bf16[192,768]{1,0:T(8,128)(2,1)S(1)}, bf16[192,768]{1,0:T(8,128)(2,1)S(1)}, u32[]{:S(2)}, u32[]{:S(2)}) %collective-permute-start.5) | collective-permute-done | bytes 294944 | tf_op jit(solution)/shard_map/ppermute | solution.py:173
  74.0 12.5 %collective-permute-done.9 = bf16[192,768]{1,0:T(8,128)(2,1)S(1)} collective-permute-done((bf16[192,768]{1,0:T(8,128)(2,1)}, bf16[192,768]{1,0:T(8,128)(2,1)S(1)}, u32[]{:S(2)}, u32[]{:S(2)}) %collective-permute-start.9) | collective-permute-done | bytes 294944 | tf_op jit(solution)/shard_map/ppermute | solution.py:173
  86.5 8.0 %collective-permute-done.8 = bf16[576,768]{1,0:T(8,128)(2,1)S(1)} collective-permute-done((bf16[576,768]{1,0:T(8,128)(2,1)}, bf16[576,768]{1,0:T(8,128)(2,1)S(1)}, u32[]{:S(2)}, u32[]{:S(2)}) %collective-permute-start.8) | collective-permute-done | bytes 884768 | tf_op jit(solution)/shard_map/ppermute | solution.py:173
  94.4 6.2 collective-permute-done.7
  142.2 6.7 collective-permute-done.12
  163.3 3.6 broadcast_select_fusion.25
  169.6 2.4 copy.437
  183.5 10.5 %fusion.367 = (f32[12,512]{1,0:T(8,128)S(1)}, f32[12,512,512]{1,2,0:T(8,128)}) fusion(pred[512,512]{0,1:T(8,128)(4,1)S(1)} %copy-done.234, bf16[512,12,32]{0,2,1:T(8,128)(2,1)S(1)} %get-tuple-element.559, bf16[512,12,32]{0,2,1:T(8,128)(2,1)} %get-tuple-element.560, bf16[512,12,32]{0,2,1:T(8,128)(2,1)S(1)} %get-tuple-element.392, ...), kind=kOutput, calls=%fused_computation.924 | convolution fusion | flops 418382336 | bytes 14442496 | tf_op jit(solution)/shard_map/sub | solution.py:94
  194.0 6.1 fusion.86
  213.7 3.3 fusion.157
  217.0 2.2 fusion.331
  219.2 9.3 %collective-permute-done.20 = bf16[384,768]{1,0:T(8,128)(2,1)S(1)} collective-permute-done((bf16[384,768]{1,0:T(8,128)(2,1)S(1)}, bf16[384,768]{1,0:T(8,128)(2,1)S(1)}, u32[]{:S(2)}, u32[]{:S(2)}) %collective-permute-start.20) | collective-permute-done | bytes 589856 | tf_op jit(solution)/shard_map/ppermute | solution.py:173
  234.9 2.2 fusion.332
  237.8 2.6 fusion.163
  240.4 2.7 fusion.369
  245.1 3.3 broadcast_select_fusion.17
  251.1 2.3 copy.483
  253.4 2.3 fusion.194
  258.2 11.3 %fusion.370 = (f32[12,512]{1,0:T(8,128)}, f32[12,512,512]{1,2,0:T(8,128)}) fusion(pred[512,512]{0,1:T(8,128)(4,1)} %broadcast_compare_fusion, bf16[512,12,32]{0,2,1:T(8,128)(2,1)} %get-tuple-element.555, bf16[512,12,32]{0,2,1:T(8,128)(2,1)} %get-tuple-element.556, bf16[512,12,32]{0,2,1:T(8,128)(2,1)S(1)} %get-tuple-element.388, ...), kind=kOutput, calls=%fused_computation.927 | convolution fusion | flops 418382336 | bytes 14442496 | tf_op jit(solution)/shard_map/sub | solution.py:94
  269.4 5.9 fusion.92
  277.9 2.3 fusion.138
  283.3 2.5 fusion.116
  287.8 2.3 fusion.122
  290.2 2.6 fusion.372
  296.6 2.7 fusion.85
  299.4 3.0 fusion.78
  318.5 2.7 multiply_reduce_fusion.3
  322.9 2.4 convert_add_fusion.8
  325.3 2.4 convert_add_fusion.9
  332.1 2.3 copy.488
  334.4 2.3 dynamic-slice_convert_fusion.11
  344.2 14.6 %multiply_convert_fusion.1 = bf16[12,512,512]{1,2,0:T(8,128)(2,1)} fusion(bf16[512,12,64]{0,2,1:T(8,128)(2,1)} %bitcast.938, bf16[512,12,64]{0,2,1:T(8,128)(2,1)} %bitcast.935, f32[12,512,512]{1,2,0:T(8,128)} %get-tuple-element.583, f32[12,512]{1,0:T(8,128)S(1)} %copy-done.302), kind=kOutput, calls=%fused_computation.7 | convolution fusion | flops 824187392 | bytes 20471808 | tf_op jit(solution)/shard_map/sub | solution.py:437
  358.9 7.0 fusion.95
  382.0 17.9 %collective-permute-done.31 = bf16[576,768]{1,0:T(8,128)(2,1)S(1)} collective-permute-done((bf16[576,768]{1,0:T(8,128)(2,1)S(1)}, bf16[576,768]{1,0:T(8,128)(2,1)S(1)}, u32[]{:S(2)}, u32[]{:S(2)}) %collective-permute-start.31) | collective-permute-done | bytes 884768 | tf_op jit(solution)/shard_map/ppermute | solution.py:173
  401.1 4.1 collective-permute-start.33
  435.8 4.7 collective-permute-done.39
  442.0 2.3 collective-permute-done.40
  446.6 2.2 collective-permute-start.42
  452.5 2.2 fusion.167
  454.7 2.6 multiply_reduce_fusion.5
  459.7 2.4 convert_add_fusion.3
  462.1 2.4 convert_add_fusion.4
  469.1 2.3 copy.501
  471.4 2.3 dynamic-slice_convert_fusion.4
  480.7 14.8 %multiply_convert_fusion = bf16[12,512,512]{1,2,0:T(8,128)(2,1)} fusion(bf16[512,12,64]{0,2,1:T(8,128)(2,1)} %bitcast.936, bf16[512,12,64]{0,2,1:T(8,128)(2,1)} %bitcast.933, f32[12,512,512]{1,2,0:T(8,128)} %get-tuple-element.577, f32[12,512]{1,0:T(8,128)S(1)} %copy-done.301), kind=kOutput, calls=%fused_computation.4 | convolution fusion | flops 824187392 | bytes 20471808 | tf_op jit(solution)/shard_map/sub | solution.py:437
  495.6 7.0 fusion.89
  519.6 17.4 %collective-permute-done.51 = bf16[576,768]{1,0:T(8,128)(2,1)S(1)} collective-permute-done((bf16[576,768]{1,0:T(8,128)(2,1)S(1)}, bf16[576,768]{1,0:T(8,128)(2,1)S(1)}, u32[]{:S(2)}, u32[]{:S(2)}) %collective-permute-start.51) | collective-permute-done | bytes 884768 | tf_op jit(solution)/shard_map/ppermute | solution.py:173
  558.1 2.7 concatenate.1038
  570.8 2.3 collective-permute-start.57
  573.0 7.2 %collective-permute-done.57 = bf16[96,768]{1,0:T(8,128)(2,1)S(1)} collective-permute-done((bf16[96,768]{1,0:T(8,128)(2,1)S(1)}, bf16[96,768]{1,0:T(8,128)(2,1)S(1)}, u32[]{:S(2)}, u32[]{:S(2)}) %collective-permute-start.57) | collective-permute-done | bytes 147488 | tf_op jit(solution)/shard_map/ppermute | solution.py:173
  582.3 2.3 collective-permute-done.59
  589.5 2.3 collective-permute-start.62
  593.6 4.1 collective-permute-done.65
  604.7 2.8 collective-permute-done.67
  662.0 2.7 collective-permute-start.76
  666.7 2.8 stack_reshape.6
  681.1 2.9 multiply_subtract_fusion.3
  684.1 4.4 multiply_subtract_fusion.2
  688.6 3.2 multiply_subtract_fusion.1
  691.8 3.0 multiply_subtract_fusion
  (1288 shorter events, 353.9 us)
Async XLA Ops:
  7.2 230.0 %all-gather.2.cloned.1.call-start = ((), (), s32[]{:S(2)}) async-start(), calls=%async_computation | async-start | bytes 5013504 | tf_op jit(solution)/shard_map/all_gather | solution.py:324
  10.4 63.6 %collective-permute-start.10 = (bf16[96,768]{1,0:T(8,128)(2,1)}, bf16[96,768]{1,0:T(8,128)(2,1)}, u32[]{:S(2)}, u32[]{:S(2)}) collective-permute-start(bf16[96,768]{1,0:T(8,128)(2,1)} %maximum_maximum_fusion.3), channel_id=1, source_target_pairs={{0,16},{2,18},{4,20},{6,22},{8,24},{10,26},{12,28},{14,30},{16,0},... | collective-permute-start | bytes 442376 | tf_op jit(solution)/shard_map/ppermute | solution.py:173
  15.7 20.5 %collective-permute-start = (bf16[112,768]{1,0:T(8,128)(2,1)}, bf16[112,768]{1,0:T(8,128)(2,1)}, u32[]{:S(2)}, u32[]{:S(2)}) collective-permute-start(bf16[112,768]{1,0:T(8,128)(2,1)} %maximum_maximum_fusion.2), channel_id=1, source_target_pairs={{0,16},{2,18},{4,20},{6,22},{8,24},{10,26},{12,28},{14,30},{16,0},... | collective-permute-start | bytes 516104 | tf_op jit(solution)/shard_map/ppermute | solution.py:173
  18.3 21.5 %collective-permute-start.2 = (bf16[96,768]{1,0:T(8,128)(2,1)S(1)}, bf16[96,768]{1,0:T(8,128)(2,1)S(1)}, u32[]{:S(2)}, u32[]{:S(2)}) collective-permute-start(bf16[96,768]{1,0:T(8,128)(2,1)S(1)} %pad_maximum_fusion.143), channel_id=1, source_target_pairs={{0,16},{2,18},{4,20},{6,22},{8,24},{10,26},{12,28},{14,30},{16,0},... | collective-permute-start | bytes 442376 | tf_op jit(solution)/shard_map/ppermute | solution.py:173
  22.2 31.5 %collective-permute-start.6 = (bf16[96,768]{1,0:T(8,128)(2,1)}, bf16[96,768]{1,0:T(8,128)(2,1)}, u32[]{:S(2)}, u32[]{:S(2)}) collective-permute-start(bf16[96,768]{1,0:T(8,128)(2,1)} %dynamic-slice_bitcast_fusion), channel_id=1, source_target_pairs={{0,16},{2,18},{4,20},{6,22},{8,24},{10,26},{12,28},{14,30},{16,0},... | collective-permute-start | bytes 442376 | tf_op jit(solution)/shard_map/ppermute | solution.py:173
  38.9 10.1 %collective-permute-start.1 = (bf16[224,768]{1,0:T(8,128)(2,1)S(1)}, bf16[224,768]{1,0:T(8,128)(2,1)S(1)}, u32[]{:S(2)}, u32[]{:S(2)}) collective-permute-start(bf16[224,768]{1,0:T(8,128)(2,1)S(1)} %pad_maximum_fusion.82), channel_id=1, source_target_pairs={{0,8},{2,10},{4,12},{6,14},{8,0},{10,2},{12,4},{14,6},{16,24},{18,... | collective-permute-start | bytes 1032200 | tf_op jit(solution)/shard_map/ppermute | solution.py:173
  49.3 15.4 %collective-permute-start.3 = (bf16[256,768]{1,0:T(8,128)(2,1)S(1)}, bf16[256,768]{1,0:T(8,128)(2,1)S(1)}, u32[]{:S(2)}, u32[]{:S(2)}) collective-permute-start(bf16[256,768]{1,0:T(8,128)(2,1)S(1)} %pad_maximum_fusion.80), channel_id=1, source_target_pairs={{0,4},{2,6},{4,0},{6,2},{8,12},{10,14},{12,8},{14,10},{16,20},{18,... | collective-permute-start | bytes 1179656 | tf_op jit(solution)/shard_map/ppermute | solution.py:173
  51.1 13.6 %collective-permute-start.5 = (bf16[192,768]{1,0:T(8,128)(2,1)S(1)}, bf16[192,768]{1,0:T(8,128)(2,1)S(1)}, u32[]{:S(2)}, u32[]{:S(2)}) collective-permute-start(bf16[192,768]{1,0:T(8,128)(2,1)S(1)} %pad_maximum_fusion.85), channel_id=1, source_target_pairs={{0,8},{2,10},{4,12},{6,14},{8,0},{10,2},{12,4},{14,6},{16,24},{18,... | collective-permute-start | bytes 884744 | tf_op jit(solution)/shard_map/ppermute | solution.py:173
  51.2 13.5 %collective-permute-start.4 = (bf16[192,768]{1,0:T(8,128)(2,1)S(1)}, bf16[192,768]{1,0:T(8,128)(2,1)S(1)}, u32[]{:S(2)}, u32[]{:S(2)}) collective-permute-start(bf16[192,768]{1,0:T(8,128)(2,1)S(1)} %bitcast.1000), channel_id=1, source_target_pairs={{0,2},{2,0},{4,6},{6,4},{8,10},{10,8},{12,14},{14,12},{16,18},{18,... | collective-permute-start | bytes 884744 | tf_op jit(solution)/shard_map/ppermute | solution.py:173
  66.9 33.8 %collective-permute-start.7 = (bf16[704,768]{1,0:T(8,128)(2,1)}, bf16[704,768]{1,0:T(8,128)(2,1)}, u32[]{:S(2)}, u32[]{:S(2)}) collective-permute-start(bf16[704,768]{1,0:T(8,128)(2,1)} %pad_maximum_fusion.24), channel_id=1, source_target_pairs={{0,2},{2,0},{4,6},{6,4},{8,10},{10,8},{12,14},{14,12},{16,18},{18,... | collective-permute-start | bytes 3244040 | tf_op jit(solution)/shard_map/ppermute | solution.py:173
  69.3 25.1 %collective-permute-start.8 = (bf16[576,768]{1,0:T(8,128)(2,1)}, bf16[576,768]{1,0:T(8,128)(2,1)S(1)}, u32[]{:S(2)}, u32[]{:S(2)}) collective-permute-start(bf16[576,768]{1,0:T(8,128)(2,1)} %pad_maximum_fusion.25), channel_id=1, source_target_pairs={{0,4},{2,6},{4,0},{6,2},{8,12},{10,14},{12,8},{14,10},{16,20},{18,... | collective-permute-start | bytes 2654216 | tf_op jit(solution)/shard_map/ppermute | solution.py:173
  71.9 14.5 %collective-permute-start.9 = (bf16[192,768]{1,0:T(8,128)(2,1)}, bf16[192,768]{1,0:T(8,128)(2,1)S(1)}, u32[]{:S(2)}, u32[]{:S(2)}) collective-permute-start(bf16[192,768]{1,0:T(8,128)(2,1)} %pad_maximum_fusion.90), channel_id=1, source_target_pairs={{0,8},{2,10},{4,12},{6,14},{8,0},{10,2},{12,4},{14,6},{16,24},{18,... | collective-permute-start | bytes 884744 | tf_op jit(solution)/shard_map/ppermute | solution.py:173
  120.1 22.1 %collective-permute-start.14 = (bf16[192,768]{1,0:T(8,128)(2,1)}, bf16[192,768]{1,0:T(8,128)(2,1)}, u32[]{:S(2)}, u32[]{:S(2)}) collective-permute-start(bf16[192,768]{1,0:T(8,128)(2,1)} %pad_maximum_fusion.95), channel_id=1, source_target_pairs={{0,8},{2,10},{4,12},{6,14},{8,0},{10,2},{12,4},{14,6},{16,24},{18,... | collective-permute-start | bytes 884744 | tf_op jit(solution)/shard_map/ppermute | solution.py:173
  123.7 27.2 %collective-permute-start.11 = (bf16[1792,768]{1,0:T(8,128)(2,1)}, bf16[1792,768]{1,0:T(8,128)(2,1)}, u32[]{:S(2)}, u32[]{:S(2)}) collective-permute-start(bf16[1792,768]{1,0:T(8,128)(2,1)} %pad_maximum_fusion), channel_id=1, source_target_pairs={{0,1},{1,0},{2,3},{3,2},{4,5},{5,4},{6,7},{7,6},{8,9},{9,8},{10,11... | collective-permute-start | bytes 8257544 | tf_op jit(solution)/shard_map/ppermute | solution.py:170
  126.5 22.4 %collective-permute-start.12 = (bf16[576,768]{1,0:T(8,128)(2,1)}, bf16[576,768]{1,0:T(8,128)(2,1)}, u32[]{:S(2)}, u32[]{:S(2)}) collective-permute-start(bf16[576,768]{1,0:T(8,128)(2,1)} %pad_maximum_fusion.26), channel_id=1, source_target_pairs={{0,4},{2,6},{4,0},{6,2},{8,12},{10,14},{12,8},{14,10},{16,20},{18,... | collective-permute-start | bytes 2654216 | tf_op jit(solution)/shard_map/ppermute | solution.py:173
  128.5 22.4 %collective-permute-start.13 = (bf16[576,768]{1,0:T(8,128)(2,1)}, bf16[576,768]{1,0:T(8,128)(2,1)}, u32[]{:S(2)}, u32[]{:S(2)}) collective-permute-start(bf16[576,768]{1,0:T(8,128)(2,1)} %pad_maximum_fusion.27), channel_id=1, source_target_pairs={{0,2},{2,0},{4,6},{6,4},{8,10},{10,8},{12,14},{14,12},{16,18},{18,... | collective-permute-start | bytes 2654216 | tf_op jit(solution)/shard_map/ppermute | solution.py:173
  174.0 28.4 %collective-permute-start.17 = (bf16[576,768]{1,0:T(8,128)(2,1)}, bf16[576,768]{1,0:T(8,128)(2,1)}, u32[]{:S(2)}, u32[]{:S(2)}) collective-permute-start(bf16[576,768]{1,0:T(8,128)(2,1)} %pad_maximum_fusion.29), channel_id=1, source_target_pairs={{0,4},{2,6},{4,0},{6,2},{8,12},{10,14},{12,8},{14,10},{16,20},{18,... | collective-permute-start | bytes 2654216 | tf_op jit(solution)/shard_map/ppermute | solution.py:173
  176.8 25.6 %collective-permute-start.16 = (bf16[576,768]{1,0:T(8,128)(2,1)}, bf16[576,768]{1,0:T(8,128)(2,1)}, u32[]{:S(2)}, u32[]{:S(2)}) collective-permute-start(bf16[576,768]{1,0:T(8,128)(2,1)} %pad_maximum_fusion.28), channel_id=1, source_target_pairs={{0,2},{2,0},{4,6},{6,4},{8,10},{10,8},{12,14},{14,12},{16,18},{18,... | collective-permute-start | bytes 2654216 | tf_op jit(solution)/shard_map/ppermute | solution.py:173
  180.0 22.4 %collective-permute-start.15 = (bf16[1536,768]{1,0:T(8,128)(2,1)}, bf16[1536,768]{1,0:T(8,128)(2,1)}, u32[]{:S(2)}, u32[]{:S(2)}) collective-permute-start(bf16[1536,768]{1,0:T(8,128)(2,1)} %pad_maximum_fusion.1), channel_id=1, source_target_pairs={{0,1},{1,0},{2,3},{3,2},{4,5},{5,4},{6,7},{7,6},{8,9},{9,8},{10,11... | collective-permute-start | bytes 7077896 | tf_op jit(solution)/shard_map/ppermute | solution.py:170
  206.3 22.4 %collective-permute-start.18 = (bf16[1536,768]{1,0:T(8,128)(2,1)S(1)}, bf16[1536,768]{1,0:T(8,128)(2,1)S(1)}, u32[]{:S(2)}, u32[]{:S(2)}) collective-permute-start(bf16[1536,768]{1,0:T(8,128)(2,1)S(1)} %pad_maximum_fusion.2), channel_id=1, source_target_pairs={{0,1},{1,0},{2,3},{3,2},{4,5},{5,4},{6,7},{7,6},{8,9},{9,8},{10,11... | collective-permute-start | bytes 7077896 | tf_op jit(solution)/shard_map/ppermute | solution.py:170
  212.8 15.7 %collective-permute-start.20 = (bf16[384,768]{1,0:T(8,128)(2,1)S(1)}, bf16[384,768]{1,0:T(8,128)(2,1)S(1)}, u32[]{:S(2)}, u32[]{:S(2)}) collective-permute-start(bf16[384,768]{1,0:T(8,128)(2,1)S(1)} %bitcast.951), channel_id=1, source_target_pairs={{0,2},{2,0},{4,6},{6,4},{8,10},{10,8},{12,14},{14,12},{16,18},{18,... | collective-permute-start | bytes 1769480 | tf_op jit(solution)/shard_map/ppermute | solution.py:173
  213.3 15.4 %collective-permute-start.19 = (bf16[384,768]{1,0:T(8,128)(2,1)S(1)}, bf16[384,768]{1,0:T(8,128)(2,1)S(1)}, u32[]{:S(2)}, u32[]{:S(2)}) collective-permute-start(bf16[384,768]{1,0:T(8,128)(2,1)S(1)} %bitcast.949), channel_id=1, source_target_pairs={{0,4},{2,6},{4,0},{6,2},{8,12},{10,14},{12,8},{14,10},{16,20},{18,... | collective-permute-start | bytes 1769480 | tf_op jit(solution)/shard_map/ppermute | solution.py:173
  232.8 11.3 %collective-permute-start.21 = (bf16[1536,768]{1,0:T(8,128)(2,1)}, bf16[1536,768]{1,0:T(8,128)(2,1)}, u32[]{:S(2)}, u32[]{:S(2)}) collective-permute-start(bf16[1536,768]{1,0:T(8,128)(2,1)} %pad_maximum_fusion.3), channel_id=1, source_target_pairs={{0,1},{1,0},{2,3},{3,2},{4,5},{5,4},{6,7},{7,6},{8,9},{9,8},{10,11... | collective-permute-start | bytes 7077896 | tf_op jit(solution)/shard_map/ppermute | solution.py:170
  237.2 46.1 %collective-permute-start.22 = (bf16[768,3072]{1,0:T(8,128)(2,1)}, bf16[768,3072]{1,0:T(8,128)(2,1)}, u32[]{:S(2)}, u32[]{:S(2)}) collective-permute-start(bf16[768,3072]{1,0:T(8,128)(2,1)} %all-gather.2.cloned.1.call-done), channel_id=1, source_target_pairs={{0,1},{1,0},{2,3},{3,2},{4,5},{5,4},{6,7},{7,6},{8,9},{9,8},{10,11... | collective-permute-start | bytes 14155784 | tf_op jit(solution)/shard_map/ppermute | solution.py:170
  311.3 11.7 %collective-permute-start.25 = (bf16[1536,768]{1,0:T(8,128)(2,1)S(1)}, bf16[1536,768]{1,0:T(8,128)(2,1)S(1)}, u32[]{:S(2)}, u32[]{:S(2)}) collective-permute-start(bf16[1536,768]{1,0:T(8,128)(2,1)S(1)} %pad_maximum_fusion.4), channel_id=1, source_target_pairs={{0,1},{1,0},{2,3},{3,2},{4,5},{5,4},{6,7},{7,6},{8,9},{9,8},{10,11... | collective-permute-start | bytes 7077896 | tf_op jit(solution)/shard_map/ppermute | solution.py:170
  313.2 9.7 %collective-permute-start.24 = (f32[1,128]{1,0:T(1,128)S(1)}, f32[1,128]{1,0:T(1,128)S(1)}, u32[]{:S(2)}, u32[]{:S(2)}) collective-permute-start(f32[1,128]{1,0:T(1,128)S(1)} %fusion.485), channel_id=1, source_target_pairs={{0,2},{2,0},{4,6},{6,4},{8,10},{10,8},{12,14},{14,12},{16,18},{18,... | collective-permute-start | bytes 1544 | tf_op jit(solution)/shard_map/ppermute | solution.py:173
  329.1 29.7 %collective-permute-start.26 = (f32[1,128]{1,0:T(1,128)S(1)}, f32[1,128]{1,0:T(1,128)S(1)}, u32[]{:S(2)}, u32[]{:S(2)}) collective-permute-start(f32[1,128]{1,0:T(1,128)S(1)} %fusion.489), channel_id=1, source_target_pairs={{0,4},{2,6},{4,0},{6,2},{8,12},{10,14},{12,8},{14,10},{16,20},{18,... | collective-permute-start | bytes 1544 | tf_op jit(solution)/shard_map/ppermute | solution.py:173
  336.7 22.2 %collective-permute-start.27 = (bf16[384,768]{1,0:T(8,128)(2,1)}, bf16[384,768]{1,0:T(8,128)(2,1)}, u32[]{:S(2)}, u32[]{:S(2)}) collective-permute-start(bf16[384,768]{1,0:T(8,128)(2,1)} %bitcast.189), channel_id=1, source_target_pairs={{0,2},{2,0},{4,6},{6,4},{8,10},{10,8},{12,14},{14,12},{16,18},{18,... | collective-permute-start | bytes 1769480 | tf_op jit(solution)/shard_map/ppermute | solution.py:173
  339.4 19.5 %collective-permute-start.28 = (bf16[384,768]{1,0:T(8,128)(2,1)}, bf16[384,768]{1,0:T(8,128)(2,1)}, u32[]{:S(2)}, u32[]{:S(2)}) collective-permute-start(bf16[384,768]{1,0:T(8,128)(2,1)} %bitcast.191), channel_id=1, source_target_pairs={{0,4},{2,6},{4,0},{6,2},{8,12},{10,14},{12,8},{14,10},{16,20},{18,... | collective-permute-start | bytes 1769480 | tf_op jit(solution)/shard_map/ppermute | solution.py:173
  344.2 14.7 %collective-permute-start.29 = (bf16[1536,768]{1,0:T(8,128)(2,1)}, bf16[1536,768]{1,0:T(8,128)(2,1)}, u32[]{:S(2)}, u32[]{:S(2)}) collective-permute-start(bf16[1536,768]{1,0:T(8,128)(2,1)} %pad_maximum_fusion.5), channel_id=1, source_target_pairs={{0,1},{1,0},{2,3},{3,2},{4,5},{5,4},{6,7},{7,6},{8,9},{9,8},{10,11... | collective-permute-start | bytes 7077896 | tf_op jit(solution)/shard_map/ppermute | solution.py:170
  365.9 16.1 %collective-permute-start.30 = (f32[1,128]{1,0:T(1,128)S(1)}, f32[1,128]{1,0:T(1,128)S(1)}, u32[]{:S(2)}, u32[]{:S(2)}) collective-permute-start(f32[1,128]{1,0:T(1,128)S(1)} %add.860), channel_id=1, source_target_pairs={{0,8},{2,10},{4,12},{6,14},{8,0},{10,2},{12,4},{14,6},{16,24},{18,... | collective-permute-start | bytes 1544 | tf_op jit(solution)/shard_map/ppermute | solution.py:173
  378.1 21.8 %collective-permute-start.31 = (bf16[576,768]{1,0:T(8,128)(2,1)S(1)}, bf16[576,768]{1,0:T(8,128)(2,1)S(1)}, u32[]{:S(2)}, u32[]{:S(2)}) collective-permute-start(bf16[576,768]{1,0:T(8,128)(2,1)S(1)} %pad_maximum_fusion.30), channel_id=1, source_target_pairs={{0,4},{2,6},{4,0},{6,2},{8,12},{10,14},{12,8},{14,10},{16,20},{18,... | collective-permute-start | bytes 2654216 | tf_op jit(solution)/shard_map/ppermute | solution.py:173
  378.6 21.6 %collective-permute-start.32 = (bf16[576,768]{1,0:T(8,128)(2,1)S(1)}, bf16[576,768]{1,0:T(8,128)(2,1)S(1)}, u32[]{:S(2)}, u32[]{:S(2)}) collective-permute-start(bf16[576,768]{1,0:T(8,128)(2,1)S(1)} %pad_maximum_fusion.31), channel_id=1, source_target_pairs={{0,2},{2,0},{4,6},{6,4},{8,10},{10,8},{12,14},{14,12},{16,18},{18,... | collective-permute-start | bytes 2654216 | tf_op jit(solution)/shard_map/ppermute | solution.py:173
  401.1 18.0 %collective-permute-start.33 = (f32[1,128]{1,0:T(1,128)S(1)}, f32[1,128]{1,0:T(1,128)S(1)}, u32[]{:S(2)}, u32[]{:S(2)}) collective-permute-start(f32[1,128]{1,0:T(1,128)S(1)} %add.869), channel_id=1, source_target_pairs={{0,16},{2,18},{4,20},{6,22},{8,24},{10,26},{12,28},{14,30},{16,0},... | collective-permute-start | bytes 1544 | tf_op jit(solution)/shard_map/ppermute | solution.py:173
  406.8 12.4 %collective-permute-start.36 = (bf16[192,768]{1,0:T(8,128)(2,1)S(1)}, bf16[192,768]{1,0:T(8,128)(2,1)S(1)}, u32[]{:S(2)}, u32[]{:S(2)}) collective-permute-start(bf16[192,768]{1,0:T(8,128)(2,1)S(1)} %bitcast.1004), channel_id=1, source_target_pairs={{0,4},{2,6},{4,0},{6,2},{8,12},{10,14},{12,8},{14,10},{16,20},{18,... | collective-permute-start | bytes 884744 | tf_op jit(solution)/shard_map/ppermute | solution.py:173
  407.4 11.8 %collective-permute-start.34 = (bf16[192,768]{1,0:T(8,128)(2,1)S(1)}, bf16[192,768]{1,0:T(8,128)(2,1)S(1)}, u32[]{:S(2)}, u32[]{:S(2)}) collective-permute-start(bf16[192,768]{1,0:T(8,128)(2,1)S(1)} %pad_maximum_fusion.103), channel_id=1, source_target_pairs={{0,8},{2,10},{4,12},{6,14},{8,0},{10,2},{12,4},{14,6},{16,24},{18,... | collective-permute-start | bytes 884744 | tf_op jit(solution)/shard_map/ppermute | solution.py:173
  408.0 11.2 %collective-permute-start.35 = (bf16[192,768]{1,0:T(8,128)(2,1)S(1)}, bf16[192,768]{1,0:T(8,128)(2,1)S(1)}, u32[]{:S(2)}, u32[]{:S(2)}) collective-permute-start(bf16[192,768]{1,0:T(8,128)(2,1)S(1)} %bitcast.1002), channel_id=1, source_target_pairs={{0,2},{2,0},{4,6},{6,4},{8,10},{10,8},{12,14},{14,12},{16,18},{18,... | collective-permute-start | bytes 884744 | tf_op jit(solution)/shard_map/ppermute | solution.py:173
  426.3 9.5 %collective-permute-start.38 = (bf16[96,768]{1,0:T(8,128)(2,1)S(1)}, bf16[96,768]{1,0:T(8,128)(2,1)S(1)}, u32[]{:S(2)}, u32[]{:S(2)}) collective-permute-start(bf16[96,768]{1,0:T(8,128)(2,1)S(1)} %pad_maximum_fusion.158), channel_id=1, source_target_pairs={{0,16},{2,18},{4,20},{6,22},{8,24},{10,26},{12,28},{14,30},{16,0},... | collective-permute-start | bytes 442376 | tf_op jit(solution)/shard_map/ppermute | solution.py:173
  427.4 14.6 %collective-permute-start.41 = (bf16[384,768]{1,0:T(8,128)(2,1)S(1)}, bf16[384,768]{1,0:T(8,128)(2,1)S(1)}, u32[]{:S(2)}, u32[]{:S(2)}) collective-permute-start(bf16[384,768]{1,0:T(8,128)(2,1)S(1)} %bitcast.947), channel_id=1, source_target_pairs={{0,4},{2,6},{4,0},{6,2},{8,12},{10,14},{12,8},{14,10},{16,20},{18,... | collective-permute-start | bytes 1769480 | tf_op jit(solution)/shard_map/ppermute | solution.py:173
  430.0 14.3 %collective-permute-start.40 = (bf16[384,768]{1,0:T(8,128)(2,1)S(1)}, bf16[384,768]{1,0:T(8,128)(2,1)S(1)}, u32[]{:S(2)}, u32[]{:S(2)}) collective-permute-start(bf16[384,768]{1,0:T(8,128)(2,1)S(1)} %bitcast.950), channel_id=1, source_target_pairs={{0,2},{2,0},{4,6},{6,4},{8,10},{10,8},{12,14},{14,12},{16,18},{18,... | collective-permute-start | bytes 1769480 | tf_op jit(solution)/shard_map/ppermute | solution.py:173
  430.8 9.7 %collective-permute-start.39 = (bf16[192,768]{1,0:T(8,128)(2,1)S(1)}, bf16[192,768]{1,0:T(8,128)(2,1)S(1)}, u32[]{:S(2)}, u32[]{:S(2)}) collective-permute-start(bf16[192,768]{1,0:T(8,128)(2,1)S(1)} %pad_maximum_fusion.104), channel_id=1, source_target_pairs={{0,8},{2,10},{4,12},{6,14},{8,0},{10,2},{12,4},{14,6},{16,24},{18,... | collective-permute-start | bytes 884744 | tf_op jit(solution)/shard_map/ppermute | solution.py:173
  446.6 11.3 %collective-permute-start.42 = (bf16[96,768]{1,0:T(8,128)(2,1)S(1)}, bf16[96,768]{1,0:T(8,128)(2,1)S(1)}, u32[]{:S(2)}, u32[]{:S(2)}) collective-permute-start(bf16[96,768]{1,0:T(8,128)(2,1)S(1)} %pad_maximum_fusion.159), channel_id=1, source_target_pairs={{0,16},{2,18},{4,20},{6,22},{8,24},{10,26},{12,28},{14,30},{16,0},... | collective-permute-start | bytes 442376 | tf_op jit(solution)/shard_map/ppermute | solution.py:173
  450.1 9.6 %collective-permute-start.45 = (bf16[1536,768]{1,0:T(8,128)(2,1)S(1)}, bf16[1536,768]{1,0:T(8,128)(2,1)S(1)}, u32[]{:S(2)}, u32[]{:S(2)}) collective-permute-start(bf16[1536,768]{1,0:T(8,128)(2,1)S(1)} %pad_maximum_fusion.6), channel_id=1, source_target_pairs={{0,1},{1,0},{2,3},{3,2},{4,5},{5,4},{6,7},{7,6},{8,9},{9,8},{10,11... | collective-permute-start | bytes 7077896 | tf_op jit(solution)/shard_map/ppermute | solution.py:170
  450.3 9.5 %collective-permute-start.43 = (bf16[192,768]{1,0:T(8,128)(2,1)S(1)}, bf16[192,768]{1,0:T(8,128)(2,1)S(1)}, u32[]{:S(2)}, u32[]{:S(2)}) collective-permute-start(bf16[192,768]{1,0:T(8,128)(2,1)S(1)} %bitcast.1006), channel_id=1, source_target_pairs={{0,4},{2,6},{4,0},{6,2},{8,12},{10,14},{12,8},{14,10},{16,20},{18,... | collective-permute-start | bytes 884744 | tf_op jit(solution)/shard_map/ppermute | solution.py:173
  465.7 29.9 %collective-permute-start.46 = (bf16[192,768]{1,0:T(8,128)(2,1)}, bf16[192,768]{1,0:T(8,128)(2,1)}, u32[]{:S(2)}, u32[]{:S(2)}) collective-permute-start(bf16[192,768]{1,0:T(8,128)(2,1)} %pad_maximum_fusion.105), channel_id=1, source_target_pairs={{0,8},{2,10},{4,12},{6,14},{8,0},{10,2},{12,4},{14,6},{16,24},{18,... | collective-permute-start | bytes 884744 | tf_op jit(solution)/shard_map/ppermute | solution.py:173
  475.8 19.7 %collective-permute-start.47 = (bf16[384,768]{1,0:T(8,128)(2,1)}, bf16[384,768]{1,0:T(8,128)(2,1)}, u32[]{:S(2)}, u32[]{:S(2)}) collective-permute-start(bf16[384,768]{1,0:T(8,128)(2,1)} %bitcast.260), channel_id=1, source_target_pairs={{0,2},{2,0},{4,6},{6,4},{8,10},{10,8},{12,14},{14,12},{16,18},{18,... | collective-permute-start | bytes 1769480 | tf_op jit(solution)/shard_map/ppermute | solution.py:173
  477.1 18.4 %collective-permute-start.48 = (bf16[384,768]{1,0:T(8,128)(2,1)}, bf16[384,768]{1,0:T(8,128)(2,1)}, u32[]{:S(2)}, u32[]{:S(2)}) collective-permute-start(bf16[384,768]{1,0:T(8,128)(2,1)} %bitcast.262), channel_id=1, source_target_pairs={{0,4},{2,6},{4,0},{6,2},{8,12},{10,14},{12,8},{14,10},{16,20},{18,... | collective-permute-start | bytes 1769480 | tf_op jit(solution)/shard_map/ppermute | solution.py:173
  480.7 14.8 %collective-permute-start.49 = (bf16[1536,768]{1,0:T(8,128)(2,1)}, bf16[1536,768]{1,0:T(8,128)(2,1)}, u32[]{:S(2)}, u32[]{:S(2)}) collective-permute-start(bf16[1536,768]{1,0:T(8,128)(2,1)} %pad_maximum_fusion.7), channel_id=1, source_target_pairs={{0,1},{1,0},{2,3},{3,2},{4,5},{5,4},{6,7},{7,6},{8,9},{9,8},{10,11... | collective-permute-start | bytes 7077896 | tf_op jit(solution)/shard_map/ppermute | solution.py:170
  507.9 11.7 %collective-permute-start.50 = (bf16[96,768]{1,0:T(8,128)(2,1)S(1)}, bf16[96,768]{1,0:T(8,128)(2,1)S(1)}, u32[]{:S(2)}, u32[]{:S(2)}) collective-permute-start(bf16[96,768]{1,0:T(8,128)(2,1)S(1)} %pad_maximum_fusion.160), channel_id=1, source_target_pairs={{0,16},{2,18},{4,20},{6,22},{8,24},{10,26},{12,28},{14,30},{16,0},... | collective-permute-start | bytes 442376 | tf_op jit(solution)/shard_map/ppermute | solution.py:173
  515.2 21.8 %collective-permute-start.51 = (bf16[576,768]{1,0:T(8,128)(2,1)S(1)}, bf16[576,768]{1,0:T(8,128)(2,1)S(1)}, u32[]{:S(2)}, u32[]{:S(2)}) collective-permute-start(bf16[576,768]{1,0:T(8,128)(2,1)S(1)} %pad_maximum_fusion.32), channel_id=1, source_target_pairs={{0,4},{2,6},{4,0},{6,2},{8,12},{10,14},{12,8},{14,10},{16,20},{18,... | collective-permute-start | bytes 2654216 | tf_op jit(solution)/shard_map/ppermute | solution.py:173
  516.9 21.6 %collective-permute-start.52 = (bf16[576,768]{1,0:T(8,128)(2,1)S(1)}, bf16[576,768]{1,0:T(8,128)(2,1)S(1)}, u32[]{:S(2)}, u32[]{:S(2)}) collective-permute-start(bf16[576,768]{1,0:T(8,128)(2,1)S(1)} %pad_maximum_fusion.33), channel_id=1, source_target_pairs={{0,2},{2,0},{4,6},{6,4},{8,10},{10,8},{12,14},{14,12},{16,18},{18,... | collective-permute-start | bytes 2654216 | tf_op jit(solution)/shard_map/ppermute | solution.py:173
  542.4 13.1 %collective-permute-start.55 = (bf16[192,768]{1,0:T(8,128)(2,1)S(1)}, bf16[192,768]{1,0:T(8,128)(2,1)S(1)}, u32[]{:S(2)}, u32[]{:S(2)}) collective-permute-start(bf16[192,768]{1,0:T(8,128)(2,1)S(1)} %bitcast.1003), channel_id=1, source_target_pairs={{0,4},{2,6},{4,0},{6,2},{8,12},{10,14},{12,8},{14,10},{16,20},{18,... | collective-permute-start | bytes 884744 | tf_op jit(solution)/shard_map/ppermute | solution.py:173
  542.9 12.6 %collective-permute-start.53 = (bf16[192,768]{1,0:T(8,128)(2,1)S(1)}, bf16[192,768]{1,0:T(8,128)(2,1)S(1)}, u32[]{:S(2)}, u32[]{:S(2)}) collective-permute-start(bf16[192,768]{1,0:T(8,128)(2,1)S(1)} %pad_maximum_fusion.106), channel_id=1, source_target_pairs={{0,8},{2,10},{4,12},{6,14},{8,0},{10,2},{12,4},{14,6},{16,24},{18,... | collective-permute-start | bytes 884744 | tf_op jit(solution)/shard_map/ppermute | solution.py:173
  543.5 12.0 %collective-permute-start.54 = (bf16[192,768]{1,0:T(8,128)(2,1)S(1)}, bf16[192,768]{1,0:T(8,128)(2,1)S(1)}, u32[]{:S(2)}, u32[]{:S(2)}) collective-permute-start(bf16[192,768]{1,0:T(8,128)(2,1)S(1)} %bitcast.1001), channel_id=1, source_target_pairs={{0,2},{2,0},{4,6},{6,4},{8,10},{10,8},{12,14},{14,12},{16,18},{18,... | collective-permute-start | bytes 884744 | tf_op jit(solution)/shard_map/ppermute | solution.py:173
  560.9 19.4 %collective-permute-start.61 = (f32[80,768]{1,0:T(8,128)}, f32[80,768]{1,0:T(8,128)S(1)}, u32[]{:S(2)}, u32[]{:S(2)}) collective-permute-start(f32[80,768]{1,0:T(8,128)} %concatenate.1038), channel_id=1, source_target_pairs={{0,1},{1,0},{2,3},{3,2},{4,5},{5,4},{6,7},{7,6},{8,9},{9,8},{10,11... | collective-permute-start | bytes 737288 | tf_op jit(solution)/shard_map/ppermute | solution.py:170
  563.7 16.6 %collective-permute-start.58 = (bf16[192,768]{1,0:T(8,128)(2,1)S(1)}, bf16[192,768]{1,0:T(8,128)(2,1)S(1)}, u32[]{:S(2)}, u32[]{:S(2)}) collective-permute-start(bf16[192,768]{1,0:T(8,128)(2,1)S(1)} %pad_maximum_fusion.107), channel_id=1, source_target_pairs={{0,8},{2,10},{4,12},{6,14},{8,0},{10,2},{12,4},{14,6},{16,24},{18,... | collective-permute-start | bytes 884744 | tf_op jit(solution)/shard_map/ppermute | solution.py:173
  566.8 15.5 %collective-permute-start.60 = (bf16[384,768]{1,0:T(8,128)(2,1)S(1)}, bf16[384,768]{1,0:T(8,128)(2,1)S(1)}, u32[]{:S(2)}, u32[]{:S(2)}) collective-permute-start(bf16[384,768]{1,0:T(8,128)(2,1)S(1)} %bitcast.946), channel_id=1, source_target_pairs={{0,4},{2,6},{4,0},{6,2},{8,12},{10,14},{12,8},{14,10},{16,20},{18,... | collective-permute-start | bytes 1769480 | tf_op jit(solution)/shard_map/ppermute | solution.py:173
  569.4 15.2 %collective-permute-start.59 = (bf16[384,768]{1,0:T(8,128)(2,1)S(1)}, bf16[384,768]{1,0:T(8,128)(2,1)S(1)}, u32[]{:S(2)}, u32[]{:S(2)}) collective-permute-start(bf16[384,768]{1,0:T(8,128)(2,1)S(1)} %bitcast.948), channel_id=1, source_target_pairs={{0,2},{2,0},{4,6},{6,4},{8,10},{10,8},{12,14},{14,12},{16,18},{18,... | collective-permute-start | bytes 1769480 | tf_op jit(solution)/shard_map/ppermute | solution.py:173
  570.8 9.5 %collective-permute-start.57 = (bf16[96,768]{1,0:T(8,128)(2,1)S(1)}, bf16[96,768]{1,0:T(8,128)(2,1)S(1)}, u32[]{:S(2)}, u32[]{:S(2)}) collective-permute-start(bf16[96,768]{1,0:T(8,128)(2,1)S(1)} %pad_maximum_fusion.161), channel_id=1, source_target_pairs={{0,16},{2,18},{4,20},{6,22},{8,24},{10,26},{12,28},{14,30},{16,0},... | collective-permute-start | bytes 442376 | tf_op jit(solution)/shard_map/ppermute | solution.py:173
  586.6 11.3 %collective-permute-start.63 = (bf16[192,768]{1,0:T(8,128)(2,1)}, bf16[192,768]{1,0:T(8,128)(2,1)}, u32[]{:S(2)}, u32[]{:S(2)}) collective-permute-start(bf16[192,768]{1,0:T(8,128)(2,1)} %bitcast.326), channel_id=1, source_target_pairs={{0,4},{2,6},{4,0},{6,2},{8,12},{10,14},{12,8},{14,10},{16,20},{18,... | collective-permute-start | bytes 884744 | tf_op jit(solution)/shard_map/ppermute | solution.py:173
  587.1 10.8 %collective-permute-start.64 = (bf16[192,768]{1,0:T(8,128)(2,1)}, bf16[192,768]{1,0:T(8,128)(2,1)}, u32[]{:S(2)}, u32[]{:S(2)}) collective-permute-start(bf16[192,768]{1,0:T(8,128)(2,1)} %bitcast.329), channel_id=1, source_target_pairs={{0,2},{2,0},{4,6},{6,4},{8,10},{10,8},{12,14},{14,12},{16,18},{18,... | collective-permute-start | bytes 884744 | tf_op jit(solution)/shard_map/ppermute | solution.py:173
  626.9 23.1 %collective-permute-start.72 = (f32[576,768]{1,0:T(8,128)}, f32[576,768]{1,0:T(8,128)S(1)}, u32[]{:S(2)}, u32[]{:S(2)}) collective-permute-start(f32[576,768]{1,0:T(8,128)} %get-tuple-element.306), channel_id=1, source_target_pairs={{0,1},{1,0},{2,3},{3,2},{4,5},{5,4},{6,7},{7,6},{8,9},{9,8},{10,11... | collective-permute-start | bytes 5308424 | tf_op jit(solution)/shard_map/ppermute | solution.py:170
  629.0 9.3 %collective-permute-start.70 = (f32[80,48]{1,0:T(8,128)}, f32[80,48]{1,0:T(8,128)}, u32[]{:S(2)}, u32[]{:S(2)}) collective-permute-start(f32[80,48]{1,0:T(8,128)} %bitcast.1017), channel_id=1, source_target_pairs={{0,16},{2,18},{4,20},{6,22},{8,24},{10,26},{12,28},{14,30},{16,0},... | collective-permute-start | bytes 46088 | tf_op jit(solution)/shard_map/ppermute | solution.py:173
  662.0 11.9 %collective-permute-start.76 = (f32[1,128]{1,0:T(1,128)}, f32[1,128]{1,0:T(1,128)}, u32[]{:S(2)}, u32[]{:S(2)}) collective-permute-start(f32[1,128]{1,0:T(1,128)} %add.963), channel_id=1, source_target_pairs={{0,16},{2,18},{4,20},{6,22},{8,24},{10,26},{12,28},{14,30},{16,0},... | collective-permute-start | bytes 1544 | tf_op jit(solution)/shard_map/ppermute | solution.py:173
  (326 other events, 1893.0 us)
Sparse Core Ops, SparseCore 0:
  39.9 96.3 all-gather.1

commit v3 on v2

--- a/solution.py
+++ b/solution.py
@@ -3,6 +3,8 @@
 import jax
 import jax.numpy as jnp
 from jax import lax
+from jax.experimental import pallas as pl
+from jax.experimental.pallas import tpu as pltpu
 from jax.sharding import PartitionSpec as P
 
 HD = 64
@@ -20,17 +22,14 @@
 CLIP = 0.05
 
 
-def rotary_tables(length, size):
-    freq = 10000.0 ** (-jnp.arange(size // 2, dtype=jnp.float32) * 2.0 / size)
+def rotary_tables(length):
+    freq = 10000.0 ** (-jnp.arange(HD // 2, dtype=jnp.float32) * 2.0 / HD)
     angle = jnp.arange(length, dtype=jnp.float32)[:, None] * freq[None, :]
-    return (jnp.cos(angle)[:, None, :], jnp.sin(angle)[:, None, :])
-
-
-def rotate(value, cosine, sine):
-    half = value.shape[-1] // 2
-    first = value[..., :half]
-    second = value[..., half:]
-    return jnp.concatenate([first * cosine - second * sine, second * cosine + first * sine], -1)
+    cosine, sine = jnp.cos(angle), jnp.sin(angle)
+    return (
+        jnp.concatenate([cosine] * 4, 1),
+        jnp.concatenate([-sine, sine] * 2, 1),
+    )
 
 
 def normalize(resid, gain, bias):
@@ -48,80 +47,357 @@
         - jnp.mean(scaled, -1, keepdims=True)
         - unit * jnp.mean(scaled * unit, -1, keepdims=True)
     )
-    return (across * inverse, jnp.sum(grad * unit, 0), jnp.sum(grad, 0))
+    return (across * inverse, jnp.sum(grad * unit, 0, keepdims=True), jnp.sum(grad, 0, keepdims=True))
 
 
 def dot(left, right):
     return jnp.dot(left, right, preferred_element_type=jnp.float32)
 
 
+def dot_nt(left, right):
+    return lax.dot_general(
+        left, right, (((1,), (1,)), ((), ())), preferred_element_type=jnp.float32
+    )
+
+
 def cross(left, right):
-    return jnp.dot(left.T, right, preferred_element_type=jnp.float32)
-
-
-def in_order(own, other):
-    first = lax.axis_index("dp") == 0
-    return jnp.concatenate(
-        [jnp.where(first, own, other), jnp.where(first, other, own)], 1
-    )
-
-
-def half_of(value, core):
-    half = value.shape[1] // 2
-    return lax.dynamic_slice_in_dim(value, core * half, half, 1)
-
-
-def attention_forward(resid, mixer, gains, cosine, sine, same):
-    (own_a, other_a), (own_b, other_b) = mixer
+    return lax.dot_general(
+        left, right, (((0,), (0,)), ((), ())), preferred_element_type=jnp.float32
+    )
+
+
+VMEM_LIMIT = 56 * 1024 * 1024
+
+
+def call(kernel, out_shapes, ins, anys, scratch, flops, outs_any=0):
+    whole = pl.BlockSpec(memory_space=pltpu.VMEM)
+    left = pl.BlockSpec(memory_space=pl.ANY)
+    n = len(out_shapes)
+    return pl.pallas_call(
+        kernel,
+        out_shape=[jax.ShapeDtypeStruct(s, t) for s, t in out_shapes],
+        in_specs=[pl.BlockSpec(memory_space=pltpu.SMEM)]
+        + [whole] * len(ins)
+        + [left] * len(anys),
+        out_specs=[whole] * (n - outs_any) + [left] * outs_any,
+        scratch_shapes=scratch,
+        compiler_params=pltpu.CompilerParams(vmem_limit_bytes=VMEM_LIMIT),
+        cost_estimate=pl.CostEstimate(
+            flops=flops,
+            bytes_accessed=sum(x.size * x.dtype.itemsize for x in ins + anys),
+            transcendentals=0,
+        ),
+    )(lax.axis_index("dp").reshape(1).astype(jnp.int32), *ins, *anys)
+
+
+def fetch(sources, targets, sems):
+    copies = [pltpu.make_async_copy(s, t, sems.at[i]) for i, (s, t) in enumerate(zip(sources, targets))]
+    for c in copies:
+        c.start()
+    return copies
+
+
+def swap_halves(value):
+    lane = lax.broadcasted_iota(jnp.int32, value.shape, 1)
+    return jnp.where(
+        lax.rem(lane, HD) < HD // 2,
+        pltpu.roll(value, 128 - HD // 2, 1),
+        pltpu.roll(value, HD // 2, 1),
+    )
+
+
+def ordered(first, own, other):
+    return jnp.concatenate([jnp.where(first, own, other), jnp.where(first, other, own)], 1)
+
+
+def head_mask(shape, head):
+    lane = lax.broadcasted_iota(jnp.int32, shape, 1)
+    return (lane < HD) if head == 0 else (lane >= HD)
+
+
+def attention_forward_kernel(
+    core, resid, seg_col, seg_row, cosine, sine, gains, a_own, a_other, b_own, b_other,
+    middle, normed_low, query, keys, values, attended, lse,
+    w_a, w_b, mixed, same, sems,
+):
+    copies = fetch(
+        [a_own, a_other, b_own, b_other], [w_a.at[0], w_a.at[1], w_b.at[0], w_b.at[1]], sems
+    )
+    first = core[0] == 0
+    half = resid.shape[1] // 2
+    normed, _, _ = normalize(resid[...], gains[0:1], gains[1:2])
+    normed_low[...] = normed.astype(jnp.bfloat16)
+    same[...] = jnp.where(seg_col[...] == seg_row[...], 0.0, 1.0)
+    for place in range(2):
+        copies[place].wait()
+        mixed[...] = dot(normed_low[...], w_a[place])
+        for p in range(half // 128):
+            for part, target in ((0, query), (1, keys)):
+                x = mixed[:, part * half + p * 128 : part * half + (p + 1) * 128]
+                x = x * cosine[...] + swap_halves(x) * sine[...]
+                target[:, place * half + p * 128 : place * half + (p + 1) * 128] = x.astype(jnp.bfloat16)
+    for place in range(2):
+        copies[2 + place].wait()
+        values[:, place * half : (place + 1) * half] = dot(
+            normed_low[...], w_b[place, :, :half]
+        ).astype(jnp.bfloat16)
+
+    lse[...] = jnp.zeros_like(lse)
+
+    def pair(p, _):
+        columns = pl.ds(pl.multiple_of(p * 128, 128), 128)
+        q, k, v = query[:, columns], keys[:, columns], values[:, columns]
+        out = []
+        for head in range(2):
+            masked_q = jnp.where(head_mask(q.shape, head), q, jnp.zeros_like(q))
+            scores = dot_nt(masked_q, k) * HD ** (-0.5)
+            scores = jnp.where(same[...] > 0.5, -1000000000.0, scores)
+            top = jnp.max(scores, -1, keepdims=True)
+            expo = jnp.exp(scores - top)
+            total = jnp.sum(expo, -1, keepdims=True)
+            probs = (expo / total).astype(jnp.bfloat16)
+            out.append(dot(probs, v))
+            lane = lax.broadcasted_iota(jnp.int32, lse.shape, 1)
+            lse[...] = jnp.where(lane == 2 * p + head, top + jnp.log(total), lse[...])
+        attended[:, columns] = jnp.where(head_mask(out[0].shape, 0), out[0], out[1]).astype(jnp.bfloat16)
+        return 0
+
+    lax.fori_loop(0, resid.shape[1] // 128, pair, 0)
+    attended[...] = ordered(first, attended[:, :half], attended[:, half:])
+    out = ordered(
+        first, dot(attended[...], w_b[0, :, half:]), dot(attended[...], w_b[1, :, half:])
+    )
+    middle[...] = resid[...] + out
+
+
+def attention_forward(resid, mixer, gains, cosine, sine, segments):
+    (a_own, a_other), (b_own, b_other) = mixer
     length, width = resid.shape
-    heads = width // HD
+    low, full = jnp.bfloat16, jnp.float32
+    ins = [resid, segments[:, None], segments[None, :], cosine, sine, gains]
+    outs = [((length, width), full)] + [((length, width), low)] * 5 + [((length, 128), full)]
+    return call(
+        attention_forward_kernel,
+        outs,
+        ins,
+        [a_own, a_other, b_own, b_other],
+        [
+            pltpu.VMEM((2, width, width), low),
+            pltpu.VMEM((2, width, width), low),
+            pltpu.VMEM((length, width), full),
+            pltpu.VMEM((length, length), full),
+            pltpu.SemaphoreType.DMA((4,)),
+        ],
+        8 * length * width * width + 4 * length * length * width,
+    )
+
+
+GELU_SCALE = 0.7978845608028654
+GELU_CUBE = 0.044715
+
+
+def hidden_forward_kernel(
+    core, middle, gains, u0, u1, u2, u3, d0, d1, d2, d3,
+    output, normed_low, hidden, active, ups, downs, hidden_here, active_here, sems, out_sems,
+):
+    ins = fetch(
+        [u0, d0, u1, d1, u2, d2, u3, d3],
+        [w.at[t] for t in range(4) for w in (ups, downs)],
+        sems,
+    )
+    normed, _, _ = normalize(middle[...], gains[0:1], gains[1:2])
+    normed_low[...] = normed.astype(jnp.bfloat16)
+    outs = []
+    for t in range(4):
+        ins[2 * t].wait()
+        x = dot(normed_low[...], ups[t])
+        hidden_here[t] = x
+        inner = jnp.tanh(GELU_SCALE * (x + GELU_CUBE * (x * x * x)))
+        active_here[t] = (x * (0.5 * (1.0 + inner))).astype(jnp.bfloat16)
+        for here, there in ((hidden_here, hidden), (active_here, active)):
+            out = pltpu.make_async_copy(here.at[t], there.at[t], out_sems.at[len(outs)])
+            out.start()
+            outs.append(out)
+        ins[2 * t + 1].wait()
+        product = dot(active_here[t], downs[t])
+        output[...] = (middle[...] if t == 0 else output[...]) + product
+    for out in outs:
+        out.wait()
+
+
+def hidden_forward(middle, ups, downs, gains):
+    length, width = middle.shape
+    low, full = jnp.bfloat16, jnp.float32
+    many = (4, length, width)
+    outs = [((length, width), full), ((length, width), low), (many, full), (many, low)]
+    return call(
+        hidden_forward_kernel,
+        outs,
+        [middle, gains],
+        ups + downs,
+        [
+            pltpu.VMEM((4, width, width), low),
+            pltpu.VMEM((4, width, width), low),
+            pltpu.VMEM(many, full),
+            pltpu.VMEM(many, low),
+            pltpu.SemaphoreType.DMA((8,)),
+            pltpu.SemaphoreType.DMA((8,)),
+        ],
+        16 * length * width * width,
+        outs_any=2,
+    )
+
+
+def hidden_back_kernel(
+    core, grad, middle, gains, hidden, u0, u1, u2, u3, d0, d1, d2, d3,
+    grad_middle, grad_gains, grad_hidden, ups, downs, hidden_here, grad_here, total, sems, out_sems,
+):
+    ins = fetch(
+        [r for t, d, u in ((0, d0, u0), (1, d1, u1), (2, d2, u2), (3, d3, u3)) for r in (d, hidden.at[t], u)],
+        [w.at[t] for t in range(4) for w in (downs, hidden_here, ups)],
+        sems,
+    )
+    branch = grad[...].astype(jnp.bfloat16)
+    outs = []
+    for t in range(4):
+        ins[3 * t].wait()
+        grad_active = dot_nt(branch, downs[t])
+        ins[3 * t + 1].wait()
+        x = hidden_here[t]
+        inner = jnp.tanh(GELU_SCALE * (x + GELU_CUBE * (x * x * x)))
+        slope = 0.5 * (1.0 + inner) + (0.5 * GELU_SCALE) * x * (1.0 - inner * inner) * (
+            1.0 + (3.0 * GELU_CUBE) * (x * x)
+        )
+        grad_here[t] = (grad_active * slope).astype(jnp.bfloat16)
+        out = pltpu.make_async_copy(grad_here.at[t], grad_hidden.at[t], out_sems.at[t])
+        out.start()
+        outs.append(out)
+        ins[3 * t + 2].wait()
+        product = dot_nt(grad_here[t], ups[t])
+        total[...] = product if t == 0 else total[...] + product
+    _, unit, inverse = normalize(middle[...], gains[0:1], gains[1:2])
+    back, gain, bias = normalize_back(total[...], unit, inverse, gains[0:1])
+    grad_middle[...] = grad[...] + back
+    grad_gains[0:1] = gain
+    grad_gains[1:2] = bias
+    for out in outs:
+        out.wait()
+
+
+def hidden_back(grad, middle, hidden, ups, downs, gains):
+    length, width = middle.shape
+    low, full = jnp.bfloat16, jnp.float32
+    many = (4, length, width)
+    outs = [((length, width), full), ((2, width), full), (many, low)]
+    return call(
+        hidden_back_kernel,
+        outs,
+        [grad, middle, gains],
+        [hidden] + ups + downs,
+        [
+            pltpu.VMEM((4, width, width), low),
+            pltpu.VMEM((4, width, width), low),
+            pltpu.VMEM(many, full),
+            pltpu.VMEM(many, low),
+            pltpu.VMEM((length, width), full),
+            pltpu.SemaphoreType.DMA((12,)),
+            pltpu.SemaphoreType.DMA((4,)),
+        ],
+        16 * length * width * width,
+        outs_any=1,
+    )
+
+
+def attention_back_kernel(
+    core, grad_middle, resid, seg_col, seg_row, cosine, sine, gains, query, keys, values, lse,
+    a_own, a_other, b_own, b_other,
+    grad, grad_gains, grad_a, grad_b,
+    w_a, w_b, same, ga, gq, gk, gv, sems,
+):
+    copies = fetch(
+        [b_own, b_other, a_own, a_other], [w_b.at[0], w_b.at[1], w_a.at[0], w_a.at[1]], sems
+    )
+    low = jnp.bfloat16
+    first = core[0] == 0
+    width = resid.shape[1]
     half = width // 2
-    w_query = in_order(own_a[:, :half], other_a[:, :half])
-    w_keys = in_order(own_a[:, half:], other_a[:, half:])
-    w_values = in_order(own_b[:, :half], other_b[:, :half])
-    w_out = in_order(own_b[:, half:], other_b[:, half:])
-    normed, unit_in, inverse_in = normalize(resid, gains[0, 0], gains[0, 1])
-    normed_low = normed.astype(jnp.bfloat16)
-    shape = (length, heads, HD)
-    query = rotate(dot(normed_low, w_query).reshape(shape), cosine, sine).astype(jnp.bfloat16)
-    keys = rotate(dot(normed_low, w_keys).reshape(shape), cosine, sine).astype(jnp.bfloat16)
-    values = dot(normed_low, w_values).reshape(shape).astype(jnp.bfloat16)
-    scores = jnp.einsum("qhe,khe->hqk", query, keys, preferred_element_type=jnp.float32) * HD ** (
-        -0.5
-    )
-    scores = jnp.where(same[None], scores, -1000000000.0)
-    top = jnp.max(scores, -1, keepdims=True)
-    expo = jnp.exp(scores - top)
-    total = jnp.sum(expo, -1, keepdims=True)
-    probs = expo / total
-    probs_low = probs.astype(jnp.bfloat16)
-    attended = jnp.einsum("hqk,khe->qhe", probs_low, values, preferred_element_type=jnp.float32)
-    attended = attended.astype(jnp.bfloat16).reshape(length, width)
-    middle = resid + dot(attended, w_out)
-    kept = (
-        (w_query, w_keys, w_values, w_out),
-        normed_low,
-        unit_in,
-        inverse_in,
-        query,
-        keys,
-        values,
-        probs,
-        probs_low,
-        attended,
-    )
-    return middle, kept
-
-
-def hidden_forward(middle, ups, downs, gains):
-    normed_mid, unit_mid, inverse_mid = normalize(middle, gains[1, 0], gains[1, 1])
-    normed_mid_low = normed_mid.astype(jnp.bfloat16)
-    hidden = [dot(normed_mid_low, w) for w in ups]
-    active = [jax.nn.gelu(h).astype(jnp.bfloat16) for h in hidden]
-    output = middle
-    for a, w in zip(active, downs):
-        output = output + dot(a, w)
-    return output, (unit_mid, inverse_mid, normed_mid_low, hidden, active)
+    scale = HD ** (-0.5)
+    same[...] = jnp.where(seg_col[...] == seg_row[...], 0.0, 1.0)
+    attn_grad = grad_middle[...].astype(low)
+    left, right = attn_grad[:, :half], attn_grad[:, half:]
+    grad_b[0, :, half:] = jnp.where(first, left, right)
+    grad_b[1, :, half:] = jnp.where(first, right, left)
+    copies[0].wait()
+    copies[1].wait()
+    natural = dot_nt(grad_b[0, :, half:], w_b[0, :, half:]) + dot_nt(
+        grad_b[1, :, half:], w_b[1, :, half:]
+    )
+    natural = natural.astype(low)
+    ga[:, :half] = jnp.where(first, natural[:, :half], natural[:, half:])
+    ga[:, half:] = jnp.where(first, natural[:, half:], natural[:, :half])
+
+    def pair(p, _):
+        columns = pl.ds(pl.multiple_of(p * 128, 128), 128)
+        q, k, v, g = query[:, columns], keys[:, columns], values[:, columns], ga[:, columns]
+        out_q, out_k, out_v = [], [], []
+        for head in range(2):
+            mask = head_mask(q.shape, head)
+            zero = jnp.zeros_like(q)
+            scores = dot_nt(k, jnp.where(mask, q, zero)) * scale
+            scores = jnp.where(same[...] > 0.5, -1000000000.0, scores)
+            probs = jnp.exp(scores - lse[pl.ds(2 * p + head, 1), :])
+            grad_probs = dot_nt(v, jnp.where(mask, g, zero))
+            across = jnp.sum(probs * grad_probs, 0, keepdims=True)
+            grad_scores = (probs * (grad_probs - across)).astype(low)
+            out_k.append(dot(grad_scores, q))
+            out_q.append(cross(grad_scores, k))
+            out_v.append(dot(probs.astype(low), g))
+        for out, target in ((out_q, gq), (out_k, gk)):
+            x = jnp.where(head_mask(out[0].shape, 0), out[0], out[1]) * scale
+            x = x * cosine[...] - swap_halves(x) * sine[...]
+            target[:, columns] = x.astype(low)
+        gv[:, columns] = jnp.where(head_mask(out_v[0].shape, 0), out_v[0], out_v[1]).astype(low)
+        return 0
+
+    lax.fori_loop(0, width // 128, pair, 0)
+    for place in range(2):
+        columns = slice(place * half, (place + 1) * half)
+        grad_a[place, :, :half] = gq[:, columns]
+        grad_a[place, :, half:] = gk[:, columns]
+        grad_b[place, :, :half] = gv[:, columns]
+    copies[2].wait()
+    copies[3].wait()
+    total = dot_nt(grad_a[0], w_a[0]) + dot_nt(grad_a[1], w_a[1])
+    total = total + dot_nt(grad_b[0, :, :half], w_b[0, :, :half])
+    total = total + dot_nt(grad_b[1, :, :half], w_b[1, :, :half])
+    _, unit, inverse = normalize(resid[...], gains[0:1], gains[1:2])
+    back, gain, bias = normalize_back(total, unit, inverse, gains[0:1])
+    grad[...] = grad_middle[...] + back
+    grad_gains[0:1] = gain
+    grad_gains[1:2] = bias
+
+
+def attention_back(grad_middle, resid, mixer, gains, cosine, sine, segments, query, keys, values, lse):
+    (a_own, a_other), (b_own, b_other) = mixer
+    length, width = resid.shape
+    low, full = jnp.bfloat16, jnp.float32
+    outs = [((length, width), full), ((2, width), full)] + [((2, length, width), low)] * 2
+    ins = [grad_middle, resid, segments[:, None], segments[None, :], cosine, sine, gains]
+    ins += [query, keys, values, lse.T[: width // HD]]
+    return call(
+        attention_back_kernel,
+        outs,
+        ins,
+        [a_own, a_other, b_own, b_other],
+        [
+            pltpu.VMEM((2, width, width), low),
+            pltpu.VMEM((2, width, width), low),
+            pltpu.VMEM((length, length), full),
+        ]
+        + [pltpu.VMEM((length, width), low)] * 4
+        + [pltpu.SemaphoreType.DMA((4,))],
+        8 * length * width * width + 10 * length * length * width,
+    )
 
 
 def adam_step(master, grad, first, second, rate, decay):
@@ -248,6 +524,11 @@
         got = yield link, value
         value = value + got
     return value
+
+
+def half_of(value, core):
+    half = value.shape[1] // 2
+    return lax.dynamic_slice_in_dim(value, core * half, half, 1)
 
 
 def up_to_parts(expand_shard, size, rows, parts):
@@ -349,17 +630,21 @@
     table_low = small[:V]
     gains = small[V:].astype(jnp.float32).reshape(-1, 2, width)
 
-    cosine, sine = rotary_tables(length, HD)
-    same = segments[:, None] == segments[None, :]
+    cosine, sine = rotary_tables(length)
     vocab_ids = jnp.arange(V, dtype=jnp.int32)
     chosen = (inputs[:, None] == vocab_ids[None, :]).astype(low)
     resid = dot(chosen, table_low)
     kept = []
     for l in range(layers):
         gain = gains[2 * l : 2 * l + 2]
-        middle, kept_mixer = attention_forward(resid, pairs(mixers[l]), gain, cosine, sine, same)
-        resid, kept_hidden = hidden_forward(middle, own_first(ups[l]), own_first(downs[l]), gain)
-        kept.append((kept_mixer, kept_hidden))
+        middle, *saved = attention_forward(
+            resid, pairs(mixers[l]), gain[0], cosine, sine, segments
+        )
+        output, *saved_mid = hidden_forward(
+            middle, own_first(ups[l]), own_first(downs[l]), gain[1]
+        )
+        kept.append((resid, saved, middle, saved_mid))
+        resid = output
     final_gain = gains[2 * layers]
     normed_out, unit_out, inverse_out = normalize(resid, final_gain[0], final_gain[1])
     head_in = normed_out.astype(low)
@@ -387,36 +672,20 @@
             boxes.append(links.add(tile_stream(send, keep, fsdp, swap)))
         return boxes
 
-    grad_norms = [grad_final_gain, grad_final_bias]
+    grad_norms = [jnp.concatenate([grad_final_gain, grad_final_bias], 0)]
     shares = [[None] * layers for _ in range(3)]
     for l in reversed(range(layers)):
-        (w_mix, normed_low, unit_in, inverse_in, query, keys, values, probs, probs_low, attended), (
-            unit_mid, inverse_mid, normed_mid_low, hidden, active,
-        ) = kept[l]
-        up_tiles, down_tiles = own_first(ups[l]), own_first(downs[l])
+        resid, (normed_low, query, keys, values, attended, lse), middle, saved_mid = kept[l]
+        normed_mid_low, hidden, active = saved_mid
         gain = gains[2 * l : 2 * l + 2]
-        heads = width // HD
         branch = grad.astype(low)
-        links.start()
-        grad_hidden = []
-        for h, w in zip(hidden, down_tiles):
-            _, gelu_back = jax.vjp(jax.nn.gelu, h)
-            grad_active = jnp.einsum("sd,fd->sf", branch, w, preferred_element_type=jnp.float32)
-            grad_hidden.append(gelu_back(grad_active)[0].astype(low))
-        grad_hidden, branch = links.finish((grad_hidden, branch))
         shares[2][l] = scatter(
             [([(active[2 + s], branch)], [(active[s], branch)]) for s in range(2)]
         )
         links.start()
-        grad_normed = 0.0
-        for g, w in zip(grad_hidden, up_tiles):
-            grad_normed = grad_normed + jnp.einsum(
-                "sf,df->sd", g, w, preferred_element_type=jnp.float32
-            )
-        grad_middle, gain_mid, bias_mid = normalize_back(
-            grad_normed, unit_mid, inverse_mid, gain[1, 0]
-        )
-        grad_middle = grad_middle + grad
+        grad_middle, gains_mid, grad_hidden = hidden_back(
+            grad, middle, hidden, own_first(ups[l]), own_first(downs[l]), gain[1]
+        )
         grad_middle, grad_hidden = links.finish((grad_middle, grad_hidden))
         shares[1][l] = scatter(
             [
@@ -425,63 +694,25 @@
             ]
         )
         links.start()
-        attn_grad = grad_middle.astype(low)
-        w_query, w_keys, w_values, w_out = w_mix
-        grad_attended = jnp.einsum(
-            "sd,ed->se", attn_grad, w_out, preferred_element_type=jnp.float32
-        )
-        grad_attended = grad_attended.astype(low).reshape(length, heads, HD)
-        grad_probs = jnp.einsum(
-            "qhe,khe->hqk", grad_attended, values, preferred_element_type=jnp.float32
-        )
-        grad_scores = probs * (grad_probs - jnp.sum(probs * grad_probs, -1, keepdims=True))
-        grad_scores = grad_scores.astype(low)
-        grad_scores, grad_attended, attn_grad = links.finish(
-            (grad_scores, grad_attended, attn_grad)
-        )
+        links.finish()
         links.start()
-        scale = HD ** (-0.5)
-        grad_query = (
-            jnp.einsum("hqk,khe->qhe", grad_scores, keys, preferred_element_type=jnp.float32)
-            * scale
-        )
-        grad_keys = (
-            jnp.einsum("hqk,qhe->khe", grad_scores, query, preferred_element_type=jnp.float32)
-            * scale
-        )
-        grad_values = jnp.einsum(
-            "hqk,qhe->khe", probs_low, grad_attended, preferred_element_type=jnp.float32
-        )
-        flat = lambda v: v.reshape(length, width).astype(low)
-        grad_query = flat(rotate(grad_query, cosine, -sine))
-        grad_keys = flat(rotate(grad_keys, cosine, -sine))
-        grad_values = flat(grad_values)
-        grad_query, grad_keys, grad_values, attn_grad = links.finish(
-            (grad_query, grad_keys, grad_values, attn_grad)
-        )
-        tiles = [([], []), ([], [])]
-        for place, c in enumerate((1 - core, core)):
-            g_q, g_k, g_v, g_o = (
-                half_of(v, c) for v in (grad_query, grad_keys, grad_values, attn_grad)
-            )
-            tiles[0][place].append((normed_low, jnp.concatenate([g_q, g_k], 1)))
-            tiles[1][place].extend([(normed_low, g_v), (attended, g_o)])
-        shares[0][l] = scatter(tiles)
-        links.start()
-        grad_normed = 0.0
-        for g, w in ((grad_query, w_query), (grad_keys, w_keys), (grad_values, w_values)):
-            grad_normed = grad_normed + jnp.einsum(
-                "se,de->sd", g, w, preferred_element_type=jnp.float32
-            )
-        grad_resid, gain_in, bias_in = normalize_back(
-            grad_normed, unit_in, inverse_in, gain[0, 0]
-        )
-        grad = grad_resid + grad_middle
-        grad_norms = [gain_in, bias_in, gain_mid, bias_mid] + grad_norms
+        grad, gains_in, grad_a, grad_b = attention_back(
+            grad_middle, resid, pairs(mixers[l]), gain[0], cosine, sine, segments,
+            query, keys, values, lse,
+        )
+        grad_norms = [gains_in, gains_mid] + grad_norms
         if l == 0:
             grad_table = grad_table + cross(chosen, grad.astype(low))
-        grad, grad_table = links.finish((grad, grad_table))
-    grad_small = jnp.concatenate([grad_table, jnp.stack(grad_norms)], 0)
+        grad, grad_a, grad_b, grad_table = links.finish((grad, grad_a, grad_b, grad_table))
+        split = lambda g: (normed_low, g[:, : width // 2])
+        outer = lambda g: (attended, g[:, width // 2 :])
+        shares[0][l] = scatter(
+            [
+                ([(normed_low, grad_a[1])], [(normed_low, grad_a[0])]),
+                ([split(grad_b[1]), outer(grad_b[1])], [split(grad_b[0]), outer(grad_b[0])]),
+            ]
+        )
+    grad_small = jnp.concatenate([grad_table] + grad_norms, 0)
     small_box = links.add(small_stream(grad_small, fsdp, rows))
     links.drain()
 

time: 716 us -> 718 us (level)
  matrix products: 200 us -> 45.5 us
  Pallas kernels: 0 us -> 140 us
  waiting for transfers between devices: 150 us -> 186 us
  other arithmetic: 123 us -> 112 us
  local copies, waits for them, and re-layouts: 122 us -> 113 us
    pallas_call x0 -> x8, Pallas kernels: none -> 140 us  [call(): pl.pallas_call(kernel, out_shape=[jax.ShapeDtypeStruct(s, t) for s, t in...]
    dot_general x62 -> x30, matrix products: 105 us -> 42.2 us  [cross(): lax.dot_general(left, right, (((0,), (0,)), ((), ())), preferred_element_...]
    sub x4 -> x0, matrix products: 51.1 us -> none  [the longest x2 29.4 us: body(): grad_probs - jnp.sum(probs * grad_probs, -1, keepdims=True)]
    dot_general x26 -> x2, matrix products: 43.5 us -> 2.94 us  [dot(): return jnp.dot(left, right, preferred_element_type=jnp.float32)]
    ppermute x62 -> x56, waiting for transfers between devices: 149 us -> 186 us  [start(): got = lax.ppermute(rows, 'fsdp', pairs)]
    slice x7 -> x13, local copies, waits for them, and re-layouts: 2.06 us -> 12.1 us  [the longest x2 6.73 us: body(): cut = lambda v, p: v[:, p * width:(p + 1) * width]]
    convert_element_type x4 -> x0, local copies, waits for them, and re-layouts: 9.22 us -> none  [the longest x2 4.64 us: attention_forward(): values = dot(normed_low, w_values).reshape(shape).astype(jnp.bfloat16)]
    another operation x49 -> x59, other arithmetic: 14.6 us -> 9.49 us  [gather_stream(): jnp.stack([jnp.where(low, value, got), jnp.where(low, got, value)], place)]
  transfers between devices with their start and end apart: 78 -> 71, of which waited for: 30 -> 28; matrix products, arithmetic and copies ran while one was open for 45% -> 18% of each run, Pallas kernels for 0% -> 18%
where the time goes in v3:
time: 718 us; the launch traced here: 706 us
  waiting for transfers between devices  186 us (26%)
  Pallas kernels  140 us (19%)
  local copies, waits for them, and re-layouts  113 us (16%)
  other arithmetic  112 us (16%)
  starting transfers between devices  79.4 us (11%)
  matrix products  45.5 us (6%)
  between operations  29.1 us (4%)
    ppermute x56, waiting for transfers between devices, start(): got = lax.ppermute(rows, 'fsdp', pairs)  186 us
    pallas_call x8, Pallas kernels, call(): pl.pallas_call(kernel, out_shape=[jax.ShapeDtypeStruct(s, t) for s, t in...  140 us
    ppermute x56, starting transfers between devices, start(): got = lax.ppermute(rows, 'fsdp', pairs)  77.3 us
    dot_general x30, matrix products, cross(): lax.dot_general(left, right, (((0,), (0,)), ((), ())), preferred_element_...  42.2 us
    unnamed x372, local copies, waits for them, and re-layouts  34.6 us
    slice x52, local copies, waits for them, and re-layouts, finish(): part = rows if len(items) == 1 else rows[at:at + sent.shape[0]]  25.6 us
    concatenate x40, other arithmetic, start(): rows = rows[0] if len(rows) == 1 else jnp.concatenate(rows, 0)  20.5 us
    sub x6, other arithmetic, adam_step(): return (master - rate * update, first, second)  16.6 us
  transfers between devices with their start and end apart: 71, of which 28 were waited for; matrix products, arithmetic and copies ran while one was open for 18% of the time, Pallas kernels for 18%

profile of v3, /device:TPU:0, one launch (start us, length us, event | category | flops | bytes accessed | tf_op | source)
XLA Modules:
  0.0 705.9 jit_solution(9295021523521302870)
XLA Ops:
  10.3 4.0 collective-permute-start.10
  17.6 3.0 collective-permute-start.2
  23.2 9.9 %collective-permute-done = bf16[112,768]{1,0:T(8,128)(2,1)} collective-permute-done((bf16[112,768]{1,0:T(8,128)(2,1)S(1)}, bf16[112,768]{1,0:T(8,128)(2,1)}, u32[]{:S(2)}, u32[]{:S(2)}) %collective-permute-start) | collective-permute-done | bytes 172064 | tf_op jit(solution)/shard_map/ppermute | solution.py:449
  36.6 7.6 %collective-permute-done.1 = bf16[224,768]{1,0:T(8,128)(2,1)S(1)} collective-permute-done((bf16[224,768]{1,0:T(8,128)(2,1)S(1)}, bf16[224,768]{1,0:T(8,128)(2,1)S(1)}, u32[]{:S(2)}, u32[]{:S(2)}) %collective-permute-start.1) | collective-permute-done | bytes 344096 | tf_op jit(solution)/shard_map/ppermute | solution.py:449
  50.8 3.6 collective-permute-start.6
  54.4 8.4 %collective-permute-done.6 = bf16[96,768]{1,0:T(8,128)(2,1)} collective-permute-done((bf16[96,768]{1,0:T(8,128)(2,1)S(1)}, bf16[96,768]{1,0:T(8,128)(2,1)}, u32[]{:S(2)}, u32[]{:S(2)}) %collective-permute-start.6) | collective-permute-done | bytes 147488 | tf_op jit(solution)/shard_map/ppermute | solution.py:449
  70.7 4.1 collective-permute-start.9
  74.8 9.5 %collective-permute-done.9 = bf16[192,768]{1,0:T(8,128)(2,1)S(1)} collective-permute-done((bf16[192,768]{1,0:T(8,128)(2,1)S(1)}, bf16[192,768]{1,0:T(8,128)(2,1)S(1)}, u32[]{:S(2)}, u32[]{:S(2)}) %collective-permute-start.9) | collective-permute-done | bytes 294944 | tf_op jit(solution)/shard_map/ppermute | solution.py:449
  84.3 9.4 %collective-permute-done.8 = bf16[576,768]{1,0:T(8,128)(2,1)S(1)} collective-permute-done((bf16[576,768]{1,0:T(8,128)(2,1)S(1)}, bf16[576,768]{1,0:T(8,128)(2,1)S(1)}, u32[]{:S(2)}, u32[]{:S(2)}) %collective-permute-start.8) | collective-permute-done | bytes 884768 | tf_op jit(solution)/shard_map/ppermute | solution.py:449
  93.7 7.1 %collective-permute-done.7 = bf16[704,768]{1,0:T(8,128)(2,1)S(1)} collective-permute-done((bf16[704,768]{1,0:T(8,128)(2,1)S(1)}, bf16[704,768]{1,0:T(8,128)(2,1)S(1)}, u32[]{:S(2)}, u32[]{:S(2)}) %collective-permute-start.7) | collective-permute-done | bytes 1081376 | tf_op jit(solution)/shard_map/ppermute | solution.py:449
  111.4 3.7 collective-permute-start.14
  115.2 9.7 %collective-permute-done.14 = bf16[192,768]{1,0:T(8,128)(2,1)S(1)} collective-permute-done((bf16[192,768]{1,0:T(8,128)(2,1)S(1)}, bf16[192,768]{1,0:T(8,128)(2,1)S(1)}, u32[]{:S(2)}, u32[]{:S(2)}) %collective-permute-start.14) | collective-permute-done | bytes 294944 | tf_op jit(solution)/shard_map/ppermute | solution.py:449
  124.8 12.7 %collective-permute-done.12 = bf16[576,768]{1,0:T(8,128)(2,1)S(1)} collective-permute-done((bf16[576,768]{1,0:T(8,128)(2,1)S(1)}, bf16[576,768]{1,0:T(8,128)(2,1)S(1)}, u32[]{:S(2)}, u32[]{:S(2)}) %collective-permute-start.12) | collective-permute-done | bytes 884768 | tf_op jit(solution)/shard_map/ppermute | solution.py:449
  146.4 19.5 %collective-permute-done.16 = bf16[576,768]{1,0:T(8,128)(2,1)S(1)} collective-permute-done((bf16[576,768]{1,0:T(8,128)(2,1)S(1)}, bf16[576,768]{1,0:T(8,128)(2,1)S(1)}, u32[]{:S(2)}, u32[]{:S(2)}) %collective-permute-start.16) | collective-permute-done | bytes 884768 | tf_op jit(solution)/shard_map/ppermute | solution.py:449
  173.6 2.8 pad_maximum_fusion.81
  185.4 12.8 %collective-permute-done.19 = bf16[384,768]{1,0:T(8,128)(2,1)} collective-permute-done((bf16[384,768]{1,0:T(8,128)(2,1)}, bf16[384,768]{1,0:T(8,128)(2,1)}, u32[]{:S(2)}, u32[]{:S(2)}) %collective-permute-start.19) | collective-permute-done | bytes 589856 | tf_op jit(solution)/shard_map/ppermute | solution.py:449
  208.2 3.3 fusion.164
  211.6 17.9 %shard_map.364 = (f32[512,768]{1,0:T(8,128)}, bf16[512,768]{1,0:T(8,128)(2,1)}, bf16[512,768]{1,0:T(8,128)(2,1)}, bf16[512,768]{1,0:T(8,128)(2,1)}, bf16[512,768...) custom-call(s32[1]{0:T(128)} %bitcast.core, f32[512,768]{1,0:T(8,128)} %fusion.79.resid, ...), custom_call_target="tpu_custom_call" | custom-call | flops 3221225472 | bytes 6825984 | tf_op jit(solution)/shard_map/pallas_call | solution.py:76
  231.1 2.2 fusion.163
  233.3 3.2 fusion.166
  236.4 12.6 %shard_map.365 = (f32[512,768]{1,0:T(8,128)}, bf16[512,768]{1,0:T(8,128)(2,1)}, f32[4,512,768]{2,1,0:T(8,128)}, bf16[4,512,768]{2,1,0:T(8,128)(2,1)}) custom-call(s32[1]{0:T(128)} %bitcast.core, f32[512,768]{1,0:T(8,128)} %get-tuple-element.142.middle, f32[2,768]{1,0:T(2,128)} %slice.747.gains, bf16[768,768]{1,0:T(8,128)(2,1)} %bitcast.800, ...), custom_call_target="tpu_custom_call" | custom-call | flops 4831838208 | bytes 11016192 | tf_op jit(solution)/shard_map/pallas_call | solution.py:76
  249.1 3.2 fusion.165
  252.2 17.6 %shard_map.366 = (f32[512,768]{1,0:T(8,128)}, bf16[512,768]{1,0:T(8,128)(2,1)}, bf16[512,768]{1,0:T(8,128)(2,1)}, bf16[512,768]{1,0:T(8,128)(2,1)}, bf16[512,768...) custom-call(s32[1]{0:T(128)} %bitcast.core, f32[512,768]{1,0:T(8,128)} %get-tuple-element.150.resid, ...), custom_call_target="tpu_custom_call" | custom-call | flops 3221225472 | bytes 6825984 | tf_op jit(solution)/shard_map/pallas_call | solution.py:76
  269.9 4.5 fusion.162
  274.4 12.6 %shard_map.367 = (f32[512,768]{1,0:T(8,128)}, bf16[512,768]{1,0:T(8,128)(2,1)}, f32[4,512,768]{2,1,0:T(8,128)}, bf16[4,512,768]{2,1,0:T(8,128)(2,1)}) custom-call(s32[1]{0:T(128)} %bitcast.core, f32[512,768]{1,0:T(8,128)} %get-tuple-element.153.middle, f32[2,768]{1,0:T(2,128)} %slice.767.gains, bf16[768,768]{1,0:T(8,128)(2,1)} %get-tuple-element.326.u0, ...), custom_call_target="tpu_custom_call" | custom-call | flops 4831838208 | bytes 11016192 | tf_op jit(solution)/shard_map/pallas_call | solution.py:76
  298.2 16.8 %shard_map.368 = (f32[512,768]{1,0:T(8,128)}, f32[2,768]{1,0:T(2,128)}, bf16[4,512,768]{2,1,0:T(8,128)(2,1)}) custom-call(s32[1]{0:T(128)} %bitcast.core, f32[512,768]{1,0:T(8,128)} %get-tuple-element.317.grad, f32[512,768]{1,0:T(8,128)} %get-tuple-element.153.middle, f32[2,768]{1,0:T(2,128)} %slice.767.gains, f32[4,512,768]{2,1,0:T(8,128)} %get-tuple-element.156.hidden, ...), custom_call_target="tpu_custom_call" | custom-call | flops 4831838208 | bytes 18880512 | tf_op jit(solution)/shard_map/pallas_call | solution.py:76
  315.1 2.5 convolution_convert_fusion.6
  321.6 2.5 convert_add_fusion.9
  336.2 3.4 collective-permute-done.25
  339.6 4.8 collective-permute-done.27
  344.4 2.3 convert_add_fusion.6
  346.8 3.2 convert_add_fusion.7
  359.8 22.9 %shard_map.369 = (f32[512,768]{1,0:T(8,128)}, f32[2,768]{1,0:T(2,128)}, bf16[2,512,768]{2,1,0:T(8,128)(2,1)}, bf16[2,512,768]{2,1,0:T(8,128)(2,1)}) custom-call(s32[1]{0:T(128)} %bitcast.core, f32[512,768]{1,0:T(8,128)} %get-tuple-element.167.grad_middle, f32[512,768]{1,0:T(8,128)} %get-tuple-element.150.resid, s32[512,1]{1,0:T(8,128)} %copy.446.seg_col, ...), custom_call_target="tpu_custom_call" | custom-call | flops 4429185024 | bytes 10782720 | tf_op jit(solution)/shard_map/pallas_call | solution.py:76
  393.4 3.4 pad_maximum_fusion
  407.2 16.6 %shard_map.370 = (f32[512,768]{1,0:T(8,128)}, f32[2,768]{1,0:T(2,128)}, bf16[4,512,768]{2,1,0:T(8,128)(2,1)}) custom-call(s32[1]{0:T(128)} %bitcast.core, f32[512,768]{1,0:T(8,128)} %get-tuple-element.183.grad, f32[512,768]{1,0:T(8,128)} %get-tuple-element.142.middle, f32[2,768]{1,0:T(2,128)} %slice.747.gains, f32[4,512,768]{2,1,0:T(8,128)} %get-tuple-element.184.hidden, ...), custom_call_target="tpu_custom_call" | custom-call | flops 4831838208 | bytes 18880512 | tf_op jit(solution)/shard_map/pallas_call | solution.py:76
  428.6 2.2 convert_add_fusion.5
  430.9 2.2 convert_add_fusion.4
  442.4 2.9 convert_add_fusion.3
  450.6 23.3 %shard_map.371 = (f32[512,768]{1,0:T(8,128)}, f32[2,768]{1,0:T(2,128)}, bf16[2,512,768]{2,1,0:T(8,128)(2,1)}, bf16[2,512,768]{2,1,0:T(8,128)(2,1)}) custom-call(s32[1]{0:T(128)} %bitcast.core, f32[512,768]{1,0:T(8,128)} %get-tuple-element.199.grad_middle, f32[512,768]{1,0:T(8,128)} %fusion.79.resid, s32[512,1]{1,0:T(8,128)} %copy.446.seg_col, ...), custom_call_target="tpu_custom_call" | custom-call | flops 4429185024 | bytes 10782720 | tf_op jit(solution)/shard_map/pallas_call | solution.py:76
  474.0 2.2 collective-permute-done.41
  477.1 2.3 convert_add_fusion.1
  479.5 2.3 convert_add_fusion.2
  481.8 2.2 fusion.171
  491.2 2.5 collective-permute-start.43
  494.9 5.3 collective-permute-done.43
  500.1 16.2 %collective-permute-done.44 = bf16[768,768]{1,0:T(8,128)(2,1)S(1)} collective-permute-done((bf16[768,768]{1,0:T(8,128)(2,1)S(1)}, bf16[768,768]{1,0:T(8,128)(2,1)S(1)}, u32[]{:S(2)}, u32[]{:S(2)}) %collective-permute-start.44) | collective-permute-done | bytes 1179680 | tf_op jit(solution)/shard_map/ppermute | solution.py:449
  518.2 4.3 concatenate.952
  537.8 6.5 collective-permute-done.48
  544.4 5.6 collective-permute-done.46
  558.4 2.2 collective-permute-start.51
  563.1 10.4 %collective-permute-done.55 = f32[640,48]{0,1:T(8,128)S(1)} collective-permute-done((f32[640,48]{0,1:T(8,128)S(1)}, f32[640,48]{0,1:T(8,128)S(1)}, u32[]{:S(2)}, u32[]{:S(2)}) %collective-permute-start.55) | collective-permute-done | bytes 122912 | tf_op jit(solution)/shard_map/ppermute | solution.py:449
  575.8 2.2 bitcast_add_fusion.1
  583.8 2.2 collective-permute-start.56
  589.5 5.6 collective-permute-done.59
  598.5 2.8 collective-permute-start.60
  601.7 6.2 collective-permute-done.61
  609.1 3.0 collective-permute-start.63
  612.1 4.8 collective-permute-done.63
  664.0 2.7 collective-permute-done.68
  669.6 2.6 stack_reshape.6
  683.8 3.1 multiply_subtract_fusion.3
  687.0 4.4 multiply_subtract_fusion.2
  691.5 3.2 multiply_subtract_fusion.1
  694.7 3.0 multiply_subtract_fusion
  (948 shorter events, 255.0 us)
Async XLA Ops:
  7.2 176.6 %all-gather.2.cloned.1.call-start = ((), (), s32[]{:S(2)}) async-start(), calls=%async_computation | async-start | bytes 5013504 | tf_op jit(solution)/shard_map/all_gather | solution.py:605
  10.3 64.5 %collective-permute-start.10 = (bf16[96,768]{1,0:T(8,128)(2,1)}, bf16[96,768]{1,0:T(8,128)(2,1)}, u32[]{:S(2)}, u32[]{:S(2)}) collective-permute-start(bf16[96,768]{1,0:T(8,128)(2,1)} %maximum_maximum_fusion.2), channel_id=1, source_target_pairs={{0,16},{2,18},{4,20},{6,22},{8,24},{10,26},{12,28},{14,30},{16,0},... | collective-permute-start | bytes 442376 | tf_op jit(solution)/shard_map/ppermute | solution.py:449
  15.0 18.1 %collective-permute-start = (bf16[112,768]{1,0:T(8,128)(2,1)S(1)}, bf16[112,768]{1,0:T(8,128)(2,1)}, u32[]{:S(2)}, u32[]{:S(2)}) collective-permute-start(bf16[112,768]{1,0:T(8,128)(2,1)S(1)} %maximum_maximum_fusion.1), channel_id=1, source_target_pairs={{0,16},{2,18},{4,20},{6,22},{8,24},{10,26},{12,28},{14,30},{16,0},... | collective-permute-start | bytes 516104 | tf_op jit(solution)/shard_map/ppermute | solution.py:449
  17.6 19.0 %collective-permute-start.2 = (bf16[96,768]{1,0:T(8,128)(2,1)S(1)}, bf16[96,768]{1,0:T(8,128)(2,1)}, u32[]{:S(2)}, u32[]{:S(2)}) collective-permute-start(bf16[96,768]{1,0:T(8,128)(2,1)S(1)} %pad_maximum_fusion.87), channel_id=1, source_target_pairs={{0,16},{2,18},{4,20},{6,22},{8,24},{10,26},{12,28},{14,30},{16,0},... | collective-permute-start | bytes 442376 | tf_op jit(solution)/shard_map/ppermute | solution.py:449
  35.7 8.5 %collective-permute-start.1 = (bf16[224,768]{1,0:T(8,128)(2,1)S(1)}, bf16[224,768]{1,0:T(8,128)(2,1)S(1)}, u32[]{:S(2)}, u32[]{:S(2)}) collective-permute-start(bf16[224,768]{1,0:T(8,128)(2,1)S(1)} %pad_maximum_fusion.49), channel_id=1, source_target_pairs={{0,8},{2,10},{4,12},{6,14},{8,0},{10,2},{12,4},{14,6},{16,24},{18,... | collective-permute-start | bytes 1032200 | tf_op jit(solution)/shard_map/ppermute | solution.py:449
  45.5 19.0 %collective-permute-start.3 = (bf16[256,768]{1,0:T(8,128)(2,1)S(1)}, bf16[256,768]{1,0:T(8,128)(2,1)S(1)}, u32[]{:S(2)}, u32[]{:S(2)}) collective-permute-start(bf16[256,768]{1,0:T(8,128)(2,1)S(1)} %pad_maximum_fusion.47), channel_id=1, source_target_pairs={{0,4},{2,6},{4,0},{6,2},{8,12},{10,14},{12,8},{14,10},{16,20},{18,... | collective-permute-start | bytes 1179656 | tf_op jit(solution)/shard_map/ppermute | solution.py:449
  47.6 16.8 %collective-permute-start.5 = (bf16[192,768]{1,0:T(8,128)(2,1)}, bf16[192,768]{1,0:T(8,128)(2,1)S(1)}, u32[]{:S(2)}, u32[]{:S(2)}) collective-permute-start(bf16[192,768]{1,0:T(8,128)(2,1)} %pad_maximum_fusion.52), channel_id=1, source_target_pairs={{0,8},{2,10},{4,12},{6,14},{8,0},{10,2},{12,4},{14,6},{16,24},{18,... | collective-permute-start | bytes 884744 | tf_op jit(solution)/shard_map/ppermute | solution.py:449
  49.3 15.1 %collective-permute-start.4 = (bf16[192,768]{1,0:T(8,128)(2,1)S(1)}, bf16[192,768]{1,0:T(8,128)(2,1)S(1)}, u32[]{:S(2)}, u32[]{:S(2)}) collective-permute-start(bf16[192,768]{1,0:T(8,128)(2,1)S(1)} %bitcast.1004), channel_id=1, source_target_pairs={{0,2},{2,0},{4,6},{6,4},{8,10},{10,8},{12,14},{14,12},{16,18},{18,... | collective-permute-start | bytes 884744 | tf_op jit(solution)/shard_map/ppermute | solution.py:449
  50.8 12.0 %collective-permute-start.6 = (bf16[96,768]{1,0:T(8,128)(2,1)S(1)}, bf16[96,768]{1,0:T(8,128)(2,1)}, u32[]{:S(2)}, u32[]{:S(2)}) collective-permute-start(bf16[96,768]{1,0:T(8,128)(2,1)S(1)} %dynamic-slice_bitcast_fusion), channel_id=1, source_target_pairs={{0,16},{2,18},{4,20},{6,22},{8,24},{10,26},{12,28},{14,30},{16,0},... | collective-permute-start | bytes 442376 | tf_op jit(solution)/shard_map/ppermute | solution.py:449
  67.4 33.4 %collective-permute-start.7 = (bf16[704,768]{1,0:T(8,128)(2,1)S(1)}, bf16[704,768]{1,0:T(8,128)(2,1)S(1)}, u32[]{:S(2)}, u32[]{:S(2)}) collective-permute-start(bf16[704,768]{1,0:T(8,128)(2,1)S(1)} %pad_maximum_fusion.20), channel_id=1, source_target_pairs={{0,2},{2,0},{4,6},{6,4},{8,10},{10,8},{12,14},{14,12},{16,18},{18,... | collective-permute-start | bytes 3244040 | tf_op jit(solution)/shard_map/ppermute | solution.py:449
  69.0 24.7 %collective-permute-start.8 = (bf16[576,768]{1,0:T(8,128)(2,1)S(1)}, bf16[576,768]{1,0:T(8,128)(2,1)S(1)}, u32[]{:S(2)}, u32[]{:S(2)}) collective-permute-start(bf16[576,768]{1,0:T(8,128)(2,1)S(1)} %pad_maximum_fusion.21), channel_id=1, source_target_pairs={{0,4},{2,6},{4,0},{6,2},{8,12},{10,14},{12,8},{14,10},{16,20},{18,... | collective-permute-start | bytes 2654216 | tf_op jit(solution)/shard_map/ppermute | solution.py:449
  70.7 13.6 %collective-permute-start.9 = (bf16[192,768]{1,0:T(8,128)(2,1)S(1)}, bf16[192,768]{1,0:T(8,128)(2,1)S(1)}, u32[]{:S(2)}, u32[]{:S(2)}) collective-permute-start(bf16[192,768]{1,0:T(8,128)(2,1)S(1)} %pad_maximum_fusion.57), channel_id=1, source_target_pairs={{0,8},{2,10},{4,12},{6,14},{8,0},{10,2},{12,4},{14,6},{16,24},{18,... | collective-permute-start | bytes 884744 | tf_op jit(solution)/shard_map/ppermute | solution.py:449
  105.7 31.8 %collective-permute-start.11 = (bf16[1792,768]{1,0:T(8,128)(2,1)S(1)}, bf16[1792,768]{1,0:T(8,128)(2,1)S(1)}, u32[]{:S(2)}, u32[]{:S(2)}) collective-permute-start(bf16[1792,768]{1,0:T(8,128)(2,1)S(1)} %pad_maximum_fusion.1), channel_id=1, source_target_pairs={{0,1},{1,0},{2,3},{3,2},{4,5},{5,4},{6,7},{7,6},{8,9},{9,8},{10,11... | collective-permute-start | bytes 8257544 | tf_op jit(solution)/shard_map/ppermute | solution.py:446
  107.1 30.4 %collective-permute-start.12 = (bf16[576,768]{1,0:T(8,128)(2,1)S(1)}, bf16[576,768]{1,0:T(8,128)(2,1)S(1)}, u32[]{:S(2)}, u32[]{:S(2)}) collective-permute-start(bf16[576,768]{1,0:T(8,128)(2,1)S(1)} %pad_maximum_fusion.22), channel_id=1, source_target_pairs={{0,4},{2,6},{4,0},{6,2},{8,12},{10,14},{12,8},{14,10},{16,20},{18,... | collective-permute-start | bytes 2654216 | tf_op jit(solution)/shard_map/ppermute | solution.py:449
  107.7 29.8 %collective-permute-start.13 = (bf16[576,768]{1,0:T(8,128)(2,1)S(1)}, bf16[576,768]{1,0:T(8,128)(2,1)S(1)}, u32[]{:S(2)}, u32[]{:S(2)}) collective-permute-start(bf16[576,768]{1,0:T(8,128)(2,1)S(1)} %pad_maximum_fusion.23), channel_id=1, source_target_pairs={{0,2},{2,0},{4,6},{6,4},{8,10},{10,8},{12,14},{14,12},{16,18},{18,... | collective-permute-start | bytes 2654216 | tf_op jit(solution)/shard_map/ppermute | solution.py:449
  111.4 13.5 %collective-permute-start.14 = (bf16[192,768]{1,0:T(8,128)(2,1)S(1)}, bf16[192,768]{1,0:T(8,128)(2,1)S(1)}, u32[]{:S(2)}, u32[]{:S(2)}) collective-permute-start(bf16[192,768]{1,0:T(8,128)(2,1)S(1)} %pad_maximum_fusion.62), channel_id=1, source_target_pairs={{0,8},{2,10},{4,12},{6,14},{8,0},{10,2},{12,4},{14,6},{16,24},{18,... | collective-permute-start | bytes 884744 | tf_op jit(solution)/shard_map/ppermute | solution.py:449
  142.5 25.0 %collective-permute-start.15 = (bf16[1536,768]{1,0:T(8,128)(2,1)S(1)}, bf16[1536,768]{1,0:T(8,128)(2,1)S(1)}, u32[]{:S(2)}, u32[]{:S(2)}) collective-permute-start(bf16[1536,768]{1,0:T(8,128)(2,1)S(1)} %pad_maximum_fusion.2), channel_id=1, source_target_pairs={{0,1},{1,0},{2,3},{3,2},{4,5},{5,4},{6,7},{7,6},{8,9},{9,8},{10,11... | collective-permute-start | bytes 7077896 | tf_op jit(solution)/shard_map/ppermute | solution.py:446
  143.8 22.1 %collective-permute-start.16 = (bf16[576,768]{1,0:T(8,128)(2,1)S(1)}, bf16[576,768]{1,0:T(8,128)(2,1)S(1)}, u32[]{:S(2)}, u32[]{:S(2)}) collective-permute-start(bf16[576,768]{1,0:T(8,128)(2,1)S(1)} %pad_maximum_fusion.24), channel_id=1, source_target_pairs={{0,2},{2,0},{4,6},{6,4},{8,10},{10,8},{12,14},{14,12},{16,18},{18,... | collective-permute-start | bytes 2654216 | tf_op jit(solution)/shard_map/ppermute | solution.py:449
  145.7 21.8 %collective-permute-start.17 = (bf16[576,768]{1,0:T(8,128)(2,1)S(1)}, bf16[576,768]{1,0:T(8,128)(2,1)S(1)}, u32[]{:S(2)}, u32[]{:S(2)}) collective-permute-start(bf16[576,768]{1,0:T(8,128)(2,1)S(1)} %pad_maximum_fusion.25), channel_id=1, source_target_pairs={{0,4},{2,6},{4,0},{6,2},{8,12},{10,14},{12,8},{14,10},{16,20},{18,... | collective-permute-start | bytes 2654216 | tf_op jit(solution)/shard_map/ppermute | solution.py:449
  170.9 27.4 %collective-permute-start.18 = (bf16[1536,768]{1,0:T(8,128)(2,1)}, bf16[1536,768]{1,0:T(8,128)(2,1)}, u32[]{:S(2)}, u32[]{:S(2)}) collective-permute-start(bf16[1536,768]{1,0:T(8,128)(2,1)} %pad_maximum_fusion.3), channel_id=1, source_target_pairs={{0,1},{1,0},{2,3},{3,2},{4,5},{5,4},{6,7},{7,6},{8,9},{9,8},{10,11... | collective-permute-start | bytes 7077896 | tf_op jit(solution)/shard_map/ppermute | solution.py:446
  182.1 16.0 %collective-permute-start.19 = (bf16[384,768]{1,0:T(8,128)(2,1)}, bf16[384,768]{1,0:T(8,128)(2,1)}, u32[]{:S(2)}, u32[]{:S(2)}) collective-permute-start(bf16[384,768]{1,0:T(8,128)(2,1)} %bitcast.168), channel_id=1, source_target_pairs={{0,4},{2,6},{4,0},{6,2},{8,12},{10,14},{12,8},{14,10},{16,20},{18,... | collective-permute-start | bytes 1769480 | tf_op jit(solution)/shard_map/ppermute | solution.py:449
  182.6 15.7 %collective-permute-start.20 = (bf16[384,768]{1,0:T(8,128)(2,1)}, bf16[384,768]{1,0:T(8,128)(2,1)}, u32[]{:S(2)}, u32[]{:S(2)}) collective-permute-start(bf16[384,768]{1,0:T(8,128)(2,1)} %bitcast.175), channel_id=1, source_target_pairs={{0,2},{2,0},{4,6},{6,4},{8,10},{10,8},{12,14},{14,12},{16,18},{18,... | collective-permute-start | bytes 1769480 | tf_op jit(solution)/shard_map/ppermute | solution.py:449
  183.8 86.0 %collective-permute-start.22 = (bf16[768,3072]{1,0:T(8,128)(2,1)}, bf16[768,3072]{1,0:T(8,128)(2,1)}, u32[]{:S(2)}, u32[]{:S(2)}) collective-permute-start(bf16[768,3072]{1,0:T(8,128)(2,1)} %all-gather.2.cloned.1.call-done), channel_id=1, source_target_pairs={{0,1},{1,0},{2,3},{3,2},{4,5},{5,4},{6,7},{7,6},{8,9},{9,8},{10,11... | collective-permute-start | bytes 14155784 | tf_op jit(solution)/shard_map/ppermute | solution.py:446
  203.4 45.6 %collective-permute-start.21 = (bf16[1536,768]{1,0:T(8,128)(2,1)}, bf16[1536,768]{1,0:T(8,128)(2,1)}, u32[]{:S(2)}, u32[]{:S(2)}) collective-permute-start(bf16[1536,768]{1,0:T(8,128)(2,1)} %pad_maximum_fusion.4), channel_id=1, source_target_pairs={{0,1},{1,0},{2,3},{3,2},{4,5},{5,4},{6,7},{7,6},{8,9},{9,8},{10,11... | collective-permute-start | bytes 7077896 | tf_op jit(solution)/shard_map/ppermute | solution.py:446
  296.2 18.8 %collective-permute-start.24 = (bf16[1536,768]{1,0:T(8,128)(2,1)S(1)}, bf16[1536,768]{1,0:T(8,128)(2,1)S(1)}, u32[]{:S(2)}, u32[]{:S(2)}) collective-permute-start(bf16[1536,768]{1,0:T(8,128)(2,1)S(1)} %pad_maximum_fusion.5), channel_id=1, source_target_pairs={{0,1},{1,0},{2,3},{3,2},{4,5},{5,4},{6,7},{7,6},{8,9},{9,8},{10,11... | collective-permute-start | bytes 7077896 | tf_op jit(solution)/shard_map/ppermute | solution.py:446
  298.2 16.9 %collective-permute-start.23 = (f32[1,128]{1,0:T(1,128)S(1)}, f32[1,128]{1,0:T(1,128)S(1)}, u32[]{:S(2)}, u32[]{:S(2)}) collective-permute-start(f32[1,128]{1,0:T(1,128)S(1)} %fusion.128), channel_id=1, source_target_pairs={{0,1},{1,0},{2,3},{3,2},{4,5},{5,4},{6,7},{7,6},{8,9},{9,8},{10,11... | collective-permute-start | bytes 1544 | tf_op jit(solution)/shard_map/ppermute | solution.py:446
  321.2 23.3 %collective-permute-start.28 = (bf16[1536,768]{1,0:T(8,128)(2,1)}, bf16[1536,768]{1,0:T(8,128)(2,1)}, u32[]{:S(2)}, u32[]{:S(2)}) collective-permute-start(bf16[1536,768]{1,0:T(8,128)(2,1)} %pad_maximum_fusion.6), channel_id=1, source_target_pairs={{0,1},{1,0},{2,3},{3,2},{4,5},{5,4},{6,7},{7,6},{8,9},{9,8},{10,11... | collective-permute-start | bytes 7077896 | tf_op jit(solution)/shard_map/ppermute | solution.py:446
  324.2 15.4 %collective-permute-start.26 = (bf16[384,768]{1,0:T(8,128)(2,1)S(1)}, bf16[384,768]{1,0:T(8,128)(2,1)S(1)}, u32[]{:S(2)}, u32[]{:S(2)}) collective-permute-start(bf16[384,768]{1,0:T(8,128)(2,1)S(1)} %bitcast.968), channel_id=1, source_target_pairs={{0,2},{2,0},{4,6},{6,4},{8,10},{10,8},{12,14},{14,12},{16,18},{18,... | collective-permute-start | bytes 1769480 | tf_op jit(solution)/shard_map/ppermute | solution.py:449
  329.3 15.1 %collective-permute-start.27 = (bf16[384,768]{1,0:T(8,128)(2,1)S(1)}, bf16[384,768]{1,0:T(8,128)(2,1)}, u32[]{:S(2)}, u32[]{:S(2)}) collective-permute-start(bf16[384,768]{1,0:T(8,128)(2,1)S(1)} %bitcast.969), channel_id=1, source_target_pairs={{0,4},{2,6},{4,0},{6,2},{8,12},{10,14},{12,8},{14,10},{16,20},{18,... | collective-permute-start | bytes 1769480 | tf_op jit(solution)/shard_map/ppermute | solution.py:449
  331.7 7.9 %collective-permute-start.25 = (f32[1,128]{1,0:T(1,128)S(1)}, f32[1,128]{1,0:T(1,128)S(1)}, u32[]{:S(2)}, u32[]{:S(2)}) collective-permute-start(f32[1,128]{1,0:T(1,128)S(1)} %fusion.232), channel_id=1, source_target_pairs={{0,2},{2,0},{4,6},{6,4},{8,10},{10,8},{12,14},{14,12},{16,18},{18,... | collective-permute-start | bytes 1544 | tf_op jit(solution)/shard_map/ppermute | solution.py:449
  354.4 28.3 %collective-permute-start.30 = (bf16[576,768]{1,0:T(8,128)(2,1)S(1)}, bf16[576,768]{1,0:T(8,128)(2,1)S(1)}, u32[]{:S(2)}, u32[]{:S(2)}) collective-permute-start(bf16[576,768]{1,0:T(8,128)(2,1)S(1)} %pad_maximum_fusion.26), channel_id=1, source_target_pairs={{0,4},{2,6},{4,0},{6,2},{8,12},{10,14},{12,8},{14,10},{16,20},{18,... | collective-permute-start | bytes 2654216 | tf_op jit(solution)/shard_map/ppermute | solution.py:449
  355.7 27.0 %collective-permute-start.31 = (bf16[576,768]{1,0:T(8,128)(2,1)S(1)}, bf16[576,768]{1,0:T(8,128)(2,1)S(1)}, u32[]{:S(2)}, u32[]{:S(2)}) collective-permute-start(bf16[576,768]{1,0:T(8,128)(2,1)S(1)} %pad_maximum_fusion.27), channel_id=1, source_target_pairs={{0,2},{2,0},{4,6},{6,4},{8,10},{10,8},{12,14},{14,12},{16,18},{18,... | collective-permute-start | bytes 2654216 | tf_op jit(solution)/shard_map/ppermute | solution.py:449
  359.1 23.5 %collective-permute-start.29 = (f32[1,128]{1,0:T(1,128)S(1)}, f32[1,128]{1,0:T(1,128)S(1)}, u32[]{:S(2)}, u32[]{:S(2)}) collective-permute-start(f32[1,128]{1,0:T(1,128)S(1)} %fusion.241), channel_id=1, source_target_pairs={{0,4},{2,6},{4,0},{6,2},{8,12},{10,14},{12,8},{14,10},{16,20},{18,... | collective-permute-start | bytes 1544 | tf_op jit(solution)/shard_map/ppermute | solution.py:449
  396.9 28.8 %collective-permute-start.36 = (bf16[3072,768]{1,0:T(8,128)(2,1)}, bf16[3072,768]{1,0:T(8,128)(2,1)}, u32[]{:S(2)}, u32[]{:S(2)}) collective-permute-start(bf16[3072,768]{1,0:T(8,128)(2,1)} %pad_maximum_fusion), channel_id=1, source_target_pairs={{0,1},{1,0},{2,3},{3,2},{4,5},{5,4},{6,7},{7,6},{8,9},{9,8},{10,11... | collective-permute-start | bytes 14155784 | tf_op jit(solution)/shard_map/ppermute | solution.py:446
  398.7 26.9 %collective-permute-start.32 = (f32[1,128]{1,0:T(1,128)S(1)}, f32[1,128]{1,0:T(1,128)S(1)}, u32[]{:S(2)}, u32[]{:S(2)}) collective-permute-start(f32[1,128]{1,0:T(1,128)S(1)} %add.562), channel_id=1, source_target_pairs={{0,8},{2,10},{4,12},{6,14},{8,0},{10,2},{12,4},{14,6},{16,24},{18,... | collective-permute-start | bytes 1544 | tf_op jit(solution)/shard_map/ppermute | solution.py:449
  401.0 24.6 %collective-permute-start.35 = (bf16[192,768]{1,0:T(8,128)(2,1)S(1)}, bf16[192,768]{1,0:T(8,128)(2,1)S(1)}, u32[]{:S(2)}, u32[]{:S(2)}) collective-permute-start(bf16[192,768]{1,0:T(8,128)(2,1)S(1)} %bitcast.1006), channel_id=1, source_target_pairs={{0,4},{2,6},{4,0},{6,2},{8,12},{10,14},{12,8},{14,10},{16,20},{18,... | collective-permute-start | bytes 884744 | tf_op jit(solution)/shard_map/ppermute | solution.py:449
  403.1 22.5 %collective-permute-start.33 = (bf16[192,768]{1,0:T(8,128)(2,1)S(1)}, bf16[192,768]{1,0:T(8,128)(2,1)S(1)}, u32[]{:S(2)}, u32[]{:S(2)}) collective-permute-start(bf16[192,768]{1,0:T(8,128)(2,1)S(1)} %pad_maximum_fusion.70), channel_id=1, source_target_pairs={{0,8},{2,10},{4,12},{6,14},{8,0},{10,2},{12,4},{14,6},{16,24},{18,... | collective-permute-start | bytes 884744 | tf_op jit(solution)/shard_map/ppermute | solution.py:449
  406.1 19.6 %collective-permute-start.34 = (bf16[192,768]{1,0:T(8,128)(2,1)S(1)}, bf16[192,768]{1,0:T(8,128)(2,1)S(1)}, u32[]{:S(2)}, u32[]{:S(2)}) collective-permute-start(bf16[192,768]{1,0:T(8,128)(2,1)S(1)} %bitcast.1007), channel_id=1, source_target_pairs={{0,2},{2,0},{4,6},{6,4},{8,10},{10,8},{12,14},{14,12},{16,18},{18,... | collective-permute-start | bytes 884744 | tf_op jit(solution)/shard_map/ppermute | solution.py:449
  433.1 16.7 %collective-permute-start.37 = (f32[1,128]{1,0:T(1,128)S(1)}, f32[1,128]{1,0:T(1,128)S(1)}, u32[]{:S(2)}, u32[]{:S(2)}) collective-permute-start(f32[1,128]{1,0:T(1,128)S(1)} %add.568), channel_id=1, source_target_pairs={{0,16},{2,18},{4,20},{6,22},{8,24},{10,26},{12,28},{14,30},{16,0},... | collective-permute-start | bytes 1544 | tf_op jit(solution)/shard_map/ppermute | solution.py:449
  436.0 38.0 %collective-permute-start.38 = (bf16[96,768]{1,0:T(8,128)(2,1)}, bf16[96,768]{1,0:T(8,128)(2,1)}, u32[]{:S(2)}, u32[]{:S(2)}) collective-permute-start(bf16[96,768]{1,0:T(8,128)(2,1)} %pad_maximum_fusion.102), channel_id=1, source_target_pairs={{0,16},{2,18},{4,20},{6,22},{8,24},{10,26},{12,28},{14,30},{16,0},... | collective-permute-start | bytes 442376 | tf_op jit(solution)/shard_map/ppermute | solution.py:449
  438.7 38.4 %collective-permute-start.42 = (bf16[1536,768]{1,0:T(8,128)(2,1)}, bf16[1536,768]{1,0:T(8,128)(2,1)}, u32[]{:S(2)}, u32[]{:S(2)}) collective-permute-start(bf16[1536,768]{1,0:T(8,128)(2,1)} %pad_maximum_fusion.7), channel_id=1, source_target_pairs={{0,1},{1,0},{2,3},{3,2},{4,5},{5,4},{6,7},{7,6},{8,9},{9,8},{10,11... | collective-permute-start | bytes 7077896 | tf_op jit(solution)/shard_map/ppermute | solution.py:446
  439.8 34.1 %collective-permute-start.40 = (bf16[768,768]{1,0:T(8,128)(2,1)}, bf16[768,768]{1,0:T(8,128)(2,1)}, u32[]{:S(2)}, u32[]{:S(2)}) collective-permute-start(bf16[768,768]{1,0:T(8,128)(2,1)} %pad_maximum_fusion.16), channel_id=1, source_target_pairs={{0,2},{2,0},{4,6},{6,4},{8,10},{10,8},{12,14},{14,12},{16,18},{18,... | collective-permute-start | bytes 3538952 | tf_op jit(solution)/shard_map/ppermute | solution.py:449
  447.8 28.3 %collective-permute-start.41 = (bf16[768,768]{1,0:T(8,128)(2,1)}, bf16[768,768]{1,0:T(8,128)(2,1)S(1)}, u32[]{:S(2)}, u32[]{:S(2)}) collective-permute-start(bf16[768,768]{1,0:T(8,128)(2,1)} %pad_maximum_fusion.17), channel_id=1, source_target_pairs={{0,4},{2,6},{4,0},{6,2},{8,12},{10,14},{12,8},{14,10},{16,20},{18,... | collective-permute-start | bytes 3538952 | tf_op jit(solution)/shard_map/ppermute | solution.py:449
  449.8 24.1 %collective-permute-start.39 = (bf16[192,768]{1,0:T(8,128)(2,1)}, bf16[192,768]{1,0:T(8,128)(2,1)S(1)}, u32[]{:S(2)}, u32[]{:S(2)}) collective-permute-start(bf16[192,768]{1,0:T(8,128)(2,1)} %pad_maximum_fusion.71), channel_id=1, source_target_pairs={{0,8},{2,10},{4,12},{6,14},{8,0},{10,2},{12,4},{14,6},{16,24},{18,... | collective-permute-start | bytes 884744 | tf_op jit(solution)/shard_map/ppermute | solution.py:449
  489.0 27.3 %collective-permute-start.44 = (bf16[768,768]{1,0:T(8,128)(2,1)S(1)}, bf16[768,768]{1,0:T(8,128)(2,1)S(1)}, u32[]{:S(2)}, u32[]{:S(2)}) collective-permute-start(bf16[768,768]{1,0:T(8,128)(2,1)S(1)} %pad_maximum_fusion.18), channel_id=1, source_target_pairs={{0,4},{2,6},{4,0},{6,2},{8,12},{10,14},{12,8},{14,10},{16,20},{18,... | collective-permute-start | bytes 3538952 | tf_op jit(solution)/shard_map/ppermute | solution.py:449
  490.0 27.2 %collective-permute-start.45 = (bf16[768,768]{1,0:T(8,128)(2,1)S(1)}, bf16[768,768]{1,0:T(8,128)(2,1)}, u32[]{:S(2)}, u32[]{:S(2)}) collective-permute-start(bf16[768,768]{1,0:T(8,128)(2,1)S(1)} %pad_maximum_fusion.19), channel_id=1, source_target_pairs={{0,2},{2,0},{4,6},{6,4},{8,10},{10,8},{12,14},{14,12},{16,18},{18,... | collective-permute-start | bytes 3538952 | tf_op jit(solution)/shard_map/ppermute | solution.py:449
  491.2 8.9 %collective-permute-start.43 = (bf16[96,768]{1,0:T(8,128)(2,1)S(1)}, bf16[96,768]{1,0:T(8,128)(2,1)S(1)}, u32[]{:S(2)}, u32[]{:S(2)}) collective-permute-start(bf16[96,768]{1,0:T(8,128)(2,1)S(1)} %pad_maximum_fusion.103), channel_id=1, source_target_pairs={{0,16},{2,18},{4,20},{6,22},{8,24},{10,26},{12,28},{14,30},{16,0},... | collective-permute-start | bytes 442376 | tf_op jit(solution)/shard_map/ppermute | solution.py:449
  522.5 15.3 %collective-permute-start.50 = (f32[80,768]{1,0:T(8,128)}, f32[80,768]{1,0:T(8,128)S(1)}, u32[]{:S(2)}, u32[]{:S(2)}) collective-permute-start(f32[80,768]{1,0:T(8,128)} %concatenate.952), channel_id=1, source_target_pairs={{0,1},{1,0},{2,3},{3,2},{4,5},{5,4},{6,7},{7,6},{8,9},{9,8},{10,11... | collective-permute-start | bytes 737288 | tf_op jit(solution)/shard_map/ppermute | solution.py:446
  525.4 12.5 %collective-permute-start.47 = (bf16[192,768]{1,0:T(8,128)(2,1)S(1)}, bf16[192,768]{1,0:T(8,128)(2,1)S(1)}, u32[]{:S(2)}, u32[]{:S(2)}) collective-permute-start(bf16[192,768]{1,0:T(8,128)(2,1)S(1)} %bitcast.1005), channel_id=1, source_target_pairs={{0,2},{2,0},{4,6},{6,4},{8,10},{10,8},{12,14},{14,12},{16,18},{18,... | collective-permute-start | bytes 884744 | tf_op jit(solution)/shard_map/ppermute | solution.py:449
  532.0 18.0 %collective-permute-start.49 = (bf16[1536,768]{1,0:T(8,128)(2,1)S(1)}, bf16[1536,768]{1,0:T(8,128)(2,1)S(1)}, u32[]{:S(2)}, u32[]{:S(2)}) collective-permute-start(bf16[1536,768]{1,0:T(8,128)(2,1)S(1)} %maximum_maximum_fusion), channel_id=1, source_target_pairs={{0,1},{1,0},{2,3},{3,2},{4,5},{5,4},{6,7},{7,6},{8,9},{9,8},{10,11... | collective-permute-start | bytes 7077896 | tf_op jit(solution)/shard_map/ppermute | solution.py:446
  534.5 15.5 %collective-permute-start.46 = (bf16[384,768]{1,0:T(8,128)(2,1)S(1)}, bf16[384,768]{1,0:T(8,128)(2,1)S(1)}, u32[]{:S(2)}, u32[]{:S(2)}) collective-permute-start(bf16[384,768]{1,0:T(8,128)(2,1)S(1)} %pad_maximum_fusion.44), channel_id=1, source_target_pairs={{0,8},{2,10},{4,12},{6,14},{8,0},{10,2},{12,4},{14,6},{16,24},{18,... | collective-permute-start | bytes 1769480 | tf_op jit(solution)/shard_map/ppermute | solution.py:449
  535.5 8.8 %collective-permute-start.48 = (bf16[192,768]{1,0:T(8,128)(2,1)S(1)}, bf16[192,768]{1,0:T(8,128)(2,1)S(1)}, u32[]{:S(2)}, u32[]{:S(2)}) collective-permute-start(bf16[192,768]{1,0:T(8,128)(2,1)S(1)} %bitcast.1008), channel_id=1, source_target_pairs={{0,4},{2,6},{4,0},{6,2},{8,12},{10,14},{12,8},{14,10},{16,20},{18,... | collective-permute-start | bytes 884744 | tf_op jit(solution)/shard_map/ppermute | solution.py:449
  551.9 21.6 %collective-permute-start.52 = (bf16[192,768]{1,0:T(8,128)(2,1)}, bf16[192,768]{1,0:T(8,128)(2,1)}, u32[]{:S(2)}, u32[]{:S(2)}) collective-permute-start(bf16[192,768]{1,0:T(8,128)(2,1)} %pad_maximum_fusion.73), channel_id=1, source_target_pairs={{0,8},{2,10},{4,12},{6,14},{8,0},{10,2},{12,4},{14,6},{16,24},{18,... | collective-permute-start | bytes 884744 | tf_op jit(solution)/shard_map/ppermute | solution.py:449
  555.6 17.9 %collective-permute-start.54 = (bf16[384,768]{1,0:T(8,128)(2,1)}, bf16[384,768]{1,0:T(8,128)(2,1)}, u32[]{:S(2)}, u32[]{:S(2)}) collective-permute-start(bf16[384,768]{1,0:T(8,128)(2,1)} %bitcast.329), channel_id=1, source_target_pairs={{0,4},{2,6},{4,0},{6,2},{8,12},{10,14},{12,8},{14,10},{16,20},{18,... | collective-permute-start | bytes 1769480 | tf_op jit(solution)/shard_map/ppermute | solution.py:449
  556.7 16.9 %collective-permute-start.53 = (bf16[384,768]{1,0:T(8,128)(2,1)}, bf16[384,768]{1,0:T(8,128)(2,1)}, u32[]{:S(2)}, u32[]{:S(2)}) collective-permute-start(bf16[384,768]{1,0:T(8,128)(2,1)} %bitcast.326), channel_id=1, source_target_pairs={{0,2},{2,0},{4,6},{6,4},{8,10},{10,8},{12,14},{14,12},{16,18},{18,... | collective-permute-start | bytes 1769480 | tf_op jit(solution)/shard_map/ppermute | solution.py:449
  558.4 15.1 %collective-permute-start.51 = (bf16[192,768]{1,0:T(8,128)(2,1)}, bf16[192,768]{1,0:T(8,128)(2,1)S(1)}, u32[]{:S(2)}, u32[]{:S(2)}) collective-permute-start(bf16[192,768]{1,0:T(8,128)(2,1)} %pad_maximum_fusion.72), channel_id=1, source_target_pairs={{0,16},{2,18},{4,20},{6,22},{8,24},{10,26},{12,28},{14,30},{16,0},... | collective-permute-start | bytes 884744 | tf_op jit(solution)/shard_map/ppermute | solution.py:449
  562.1 11.4 %collective-permute-start.55 = (f32[640,48]{0,1:T(8,128)S(1)}, f32[640,48]{0,1:T(8,128)S(1)}, u32[]{:S(2)}, u32[]{:S(2)}) collective-permute-start(f32[640,48]{0,1:T(8,128)S(1)} %reshape.3897), channel_id=1, source_target_pairs={{0,2},{2,0},{4,6},{6,4},{8,10},{10,8},{12,14},{14,12},{16,18},{18,... | collective-permute-start | bytes 368648 | tf_op jit(solution)/shard_map/ppermute | solution.py:449
  583.8 11.3 %collective-permute-start.56 = (bf16[96,768]{1,0:T(8,128)(2,1)}, bf16[96,768]{1,0:T(8,128)(2,1)}, u32[]{:S(2)}, u32[]{:S(2)}) collective-permute-start(bf16[96,768]{1,0:T(8,128)(2,1)} %pad_maximum_fusion.104), channel_id=1, source_target_pairs={{0,16},{2,18},{4,20},{6,22},{8,24},{10,26},{12,28},{14,30},{16,0},... | collective-permute-start | bytes 442376 | tf_op jit(solution)/shard_map/ppermute | solution.py:449
  586.0 9.1 %collective-permute-start.58 = (bf16[192,768]{1,0:T(8,128)(2,1)}, bf16[192,768]{1,0:T(8,128)(2,1)}, u32[]{:S(2)}, u32[]{:S(2)}) collective-permute-start(bf16[192,768]{1,0:T(8,128)(2,1)} %bitcast.344), channel_id=1, source_target_pairs={{0,2},{2,0},{4,6},{6,4},{8,10},{10,8},{12,14},{14,12},{16,18},{18,... | collective-permute-start | bytes 884744 | tf_op jit(solution)/shard_map/ppermute | solution.py:449
  587.0 8.1 %collective-permute-start.57 = (bf16[192,768]{1,0:T(8,128)(2,1)}, bf16[192,768]{1,0:T(8,128)(2,1)}, u32[]{:S(2)}, u32[]{:S(2)}) collective-permute-start(bf16[192,768]{1,0:T(8,128)(2,1)} %bitcast.341), channel_id=1, source_target_pairs={{0,4},{2,6},{4,0},{6,2},{8,12},{10,14},{12,8},{14,10},{16,20},{18,... | collective-permute-start | bytes 884744 | tf_op jit(solution)/shard_map/ppermute | solution.py:449
  598.5 9.5 %collective-permute-start.60 = (bf16[192,768]{1,0:T(8,128)(2,1)S(1)}, bf16[192,768]{1,0:T(8,128)(2,1)S(1)}, u32[]{:S(2)}, u32[]{:S(2)}) collective-permute-start(bf16[192,768]{1,0:T(8,128)(2,1)S(1)} %pad_maximum_fusion.74), channel_id=1, source_target_pairs={{0,8},{2,10},{4,12},{6,14},{8,0},{10,2},{12,4},{14,6},{16,24},{18,... | collective-permute-start | bytes 884744 | tf_op jit(solution)/shard_map/ppermute | solution.py:449
  608.1 8.8 %collective-permute-start.62 = (bf16[96,768]{1,0:T(8,128)(2,1)S(1)}, bf16[96,768]{1,0:T(8,128)(2,1)S(1)}, u32[]{:S(2)}, u32[]{:S(2)}) collective-permute-start(bf16[96,768]{1,0:T(8,128)(2,1)S(1)} %pad_maximum_fusion.105), channel_id=1, source_target_pairs={{0,16},{2,18},{4,20},{6,22},{8,24},{10,26},{12,28},{14,30},{16,0},... | collective-permute-start | bytes 442376 | tf_op jit(solution)/shard_map/ppermute | solution.py:449
  629.8 25.3 %collective-permute-start.65 = (f32[576,768]{1,0:T(8,128)}, f32[576,768]{1,0:T(8,128)S(1)}, u32[]{:S(2)}, u32[]{:S(2)}) collective-permute-start(f32[576,768]{1,0:T(8,128)} %get-tuple-element.290), channel_id=1, source_target_pairs={{0,1},{1,0},{2,3},{3,2},{4,5},{5,4},{6,7},{7,6},{8,9},{9,8},{10,11... | collective-permute-start | bytes 5308424 | tf_op jit(solution)/shard_map/ppermute | solution.py:446
  667.2 9.3 %collective-permute-start.69 = (f32[1,128]{1,0:T(1,128)}, f32[1,128]{1,0:T(1,128)}, u32[]{:S(2)}, u32[]{:S(2)}) collective-permute-start(f32[1,128]{1,0:T(1,128)} %add.644), channel_id=1, source_target_pairs={{0,16},{2,18},{4,20},{6,22},{8,24},{10,26},{12,28},{14,30},{16,0},... | collective-permute-start | bytes 1544 | tf_op jit(solution)/shard_map/ppermute | solution.py:449
  (198 other events, 987.0 us)
Sparse Core Ops, SparseCore 0:
  36.7 102.3 all-gather.1

commit v4 on v3

v4 whole, which is shorter than its diff:
```python
import functools

import jax
import jax.numpy as jnp
from jax import lax
from jax.experimental import pallas as pl
from jax.experimental.pallas import tpu as pltpu
from jax.sharding import PartitionSpec as P

HD = 64
V = 70
STEP = 10


NORM_EPS = 1e-05
BETA_ONE = 0.9
BETA_TWO = 0.95
ADAM_EPS = 1e-08
DECAY = 0.1
RATE_MATRIX = 0.05
RATE_VECTOR = 0.3
CLIP = 0.05


def rotary_tables(length):
    freq = 10000.0 ** (-jnp.arange(HD // 2, dtype=jnp.float32) * 2.0 / HD)
    angle = jnp.arange(length, dtype=jnp.float32)[:, None] * freq[None, :]
    cosine, sine = jnp.cos(angle), jnp.sin(angle)
    return (
        jnp.concatenate([cosine] * 4, 1),
        jnp.concatenate([-sine, sine] * 2, 1),
    )


def normalize(resid, gain, bias):
    mean = jnp.mean(resid, -1, keepdims=True)
    centred = resid - mean
    inverse = lax.rsqrt(jnp.mean(centred * centred, -1, keepdims=True) + NORM_EPS)
    unit = centred * inverse
    return (unit * gain + bias, unit, inverse)


def normalize_back(grad, unit, inverse, gain):
    scaled = grad * gain
    across = (
        scaled
        - jnp.mean(scaled, -1, keepdims=True)
        - unit * jnp.mean(scaled * unit, -1, keepdims=True)
    )
    return (across * inverse, jnp.sum(grad * unit, 0, keepdims=True), jnp.sum(grad, 0, keepdims=True))


def dot(left, right):
    return jnp.dot(left, right, preferred_element_type=jnp.float32)


def dot_nt(left, right):
    return lax.dot_general(
        left, right, (((1,), (1,)), ((), ())), preferred_element_type=jnp.float32
    )


def cross(left, right):
    return lax.dot_general(
        left, right, (((0,), (0,)), ((), ())), preferred_element_type=jnp.float32
    )


VMEM_LIMIT = 56 * 1024 * 1024
LOW, FULL = jnp.bfloat16, jnp.float32


def call(kernel, scalars, out_shapes, ins, anys, scratch, flops, outs_any=0):
    whole = pl.BlockSpec(memory_space=pltpu.VMEM)
    left = pl.BlockSpec(memory_space=pl.ANY)
    n = len(out_shapes)
    return pl.pallas_call(
        kernel,
        out_shape=[jax.ShapeDtypeStruct(s, t) for s, t in out_shapes],
        in_specs=[pl.BlockSpec(memory_space=pltpu.SMEM)]
        + [whole] * len(ins)
        + [left] * len(anys),
        out_specs=[whole] * (n - outs_any) + [left] * outs_any,
        scratch_shapes=scratch,
        compiler_params=pltpu.CompilerParams(vmem_limit_bytes=VMEM_LIMIT),
        cost_estimate=pl.CostEstimate(
            flops=flops,
            bytes_accessed=sum(x.size * x.dtype.itemsize for x in ins + anys),
            transcendentals=0,
        ),
    )(scalars, *ins, *anys)


def fetch(sources, targets, sems):
    copies = [
        pltpu.make_async_copy(s, t, sems.at[i]) for i, (s, t) in enumerate(zip(sources, targets))
    ]
    for c in copies:
        c.start()
    return copies


def tile_of(ref, t, width):
    return ref.at[t] if len(ref.shape) == 3 else ref.at[:, t * width : (t + 1) * width]


def swap_halves(value):
    lane = lax.broadcasted_iota(jnp.int32, value.shape, 1)
    return jnp.where(
        lax.rem(lane, HD) < HD // 2,
        pltpu.roll(value, 128 - HD // 2, 1),
        pltpu.roll(value, HD // 2, 1),
    )


def ordered(first, own, other):
    return jnp.concatenate([jnp.where(first, own, other), jnp.where(first, other, own)], 1)


def head_mask(shape, head):
    lane = lax.broadcasted_iota(jnp.int32, shape, 1)
    return (lane < HD) if head == 0 else (lane >= HD)


def attention_forward_kernel(
    place_of, resid, seg_col, seg_row, cosine, sine, gains, own, other,
    middle, query, keys, values, lse, pack,
    w_a, w_b, mixed, same, sems,
):
    width = resid.shape[1]
    half = width // 2
    copies = fetch(
        [tile_of(r, t, width) for t in range(2) for r in (own, other)],
        [w.at[place] for w in (w_a, w_b) for place in range(2)],
        sems,
    )
    first = place_of[0] == 0
    normed, _, _ = normalize(resid[...], gains[0:1], gains[1:2])
    normed_low, attended = pack.at[0], pack.at[1]
    normed_low[...] = normed.astype(LOW)
    same[...] = jnp.where(seg_col[...] == seg_row[...], 0.0, 1.0)
    for place in range(2):
        copies[place].wait()
        mixed[...] = dot(normed_low[...], w_a[place])
        for p in range(half // 128):
            for part, target in ((0, query), (1, keys)):
                x = mixed[:, part * half + p * 128 : part * half + (p + 1) * 128]
                x = x * cosine[...] + swap_halves(x) * sine[...]
                target[:, place * half + p * 128 : place * half + (p + 1) * 128] = x.astype(LOW)
    for place in range(2):
        copies[2 + place].wait()
        values[:, place * half : (place + 1) * half] = dot(
            normed_low[...], w_b[place, :, :half]
        ).astype(LOW)

    lse[...] = jnp.zeros_like(lse)

    def pair(p, _):
        columns = pl.ds(pl.multiple_of(p * 128, 128), 128)
        q, k, v = query[:, columns], keys[:, columns], values[:, columns]
        out = []
        for head in range(2):
            masked_q = jnp.where(head_mask(q.shape, head), q, jnp.zeros_like(q))
            scores = dot_nt(masked_q, k) * HD ** (-0.5)
            scores = jnp.where(same[...] > 0.5, -1000000000.0, scores)
            top = jnp.max(scores, -1, keepdims=True)
            expo = jnp.exp(scores - top)
            total = jnp.sum(expo, -1, keepdims=True)
            probs = (expo / total).astype(LOW)
            out.append(dot(probs, v))
            lane = lax.broadcasted_iota(jnp.int32, lse.shape, 1)
            lse[...] = jnp.where(lane == 2 * p + head, top + jnp.log(total), lse[...])
        attended[:, columns] = jnp.where(head_mask(out[0].shape, 0), out[0], out[1]).astype(LOW)
        return 0

    lax.fori_loop(0, width // 128, pair, 0)
    attended[...] = ordered(first, attended[:, :half], attended[:, half:])
    out = ordered(
        first, dot(attended[...], w_b[0, :, half:]), dot(attended[...], w_b[1, :, half:])
    )
    middle[...] = resid[...] + out


def attention_forward(place, resid, mixer, gains, cosine, sine, segments):
    length, width = resid.shape
    one = (length, width)
    outs = [(one, FULL)] + [(one, LOW)] * 3 + [((length, 128), FULL), ((2,) + one, LOW)]
    return call(
        attention_forward_kernel,
        place,
        outs,
        [resid, segments[:, None], segments[None, :], cosine, sine, gains],
        list(mixer),
        [
            pltpu.VMEM((2, width, width), LOW),
            pltpu.VMEM((2, width, width), LOW),
            pltpu.VMEM(one, FULL),
            pltpu.VMEM((length, length), FULL),
            pltpu.SemaphoreType.DMA((4,)),
        ],
        8 * length * width * width + 4 * length * length * width,
    )


GELU_SCALE = 0.7978845608028654
GELU_CUBE = 0.044715


def hidden_tiles(own, other, width):
    ups = [tile_of(r, t, width) for r in (own, other) for t in (0, 1)]
    downs = [tile_of(r, t, width) for r in (own, other) for t in (2, 3)]
    return ups, downs


def hidden_forward_kernel(
    place_of, middle, gains, own, other,
    output, active, pack, hidden, ups, downs, hidden_here, sems, out_sems,
):
    u, d = hidden_tiles(own, other, middle.shape[1])
    ins = fetch(
        [r for t in range(4) for r in (u[t], d[t])],
        [w.at[t] for t in range(4) for w in (ups, downs)],
        sems,
    )
    normed, _, _ = normalize(middle[...], gains[0:1], gains[1:2])
    pack[0] = normed.astype(LOW)
    outs = []
    for t in range(4):
        ins[2 * t].wait()
        x = dot(pack[0], ups[t])
        hidden_here[t] = x
        out = pltpu.make_async_copy(hidden_here.at[t], hidden.at[t], out_sems.at[t])
        out.start()
        outs.append(out)
        inner = jnp.tanh(GELU_SCALE * (x + GELU_CUBE * (x * x * x)))
        target = active.at[t] if t < 2 else pack.at[t - 1]
        target[...] = (x * (0.5 * (1.0 + inner))).astype(LOW)
        ins[2 * t + 1].wait()
        product = dot(target[...], downs[t])
        output[...] = (middle[...] if t == 0 else output[...]) + product
    for out in outs:
        out.wait()


def hidden_forward(place, middle, pair, gains):
    length, width = middle.shape
    one = (length, width)
    outs = [(one, FULL), ((2,) + one, LOW), ((3,) + one, LOW), ((4,) + one, FULL)]
    return call(
        hidden_forward_kernel,
        place,
        outs,
        [middle, gains],
        list(pair),
        [
            pltpu.VMEM((4, width, width), LOW),
            pltpu.VMEM((4, width, width), LOW),
            pltpu.VMEM((4,) + one, FULL),
            pltpu.SemaphoreType.DMA((8,)),
            pltpu.SemaphoreType.DMA((4,)),
        ],
        16 * length * width * width,
        outs_any=1,
    )


def hidden_back_kernel(
    place_of, grad, branch, middle, gains, hidden, own, other,
    grad_middle, grad_gains, grad_own, grad_other, ups, downs, hidden_here, total, sems,
):
    u, d = hidden_tiles(own, other, middle.shape[1])
    ins = fetch(
        [r for t in range(4) for r in (d[t], hidden.at[t], u[t])],
        [w.at[t] for t in range(4) for w in (downs, hidden_here, ups)],
        sems,
    )
    for t in range(4):
        ins[3 * t].wait()
        grad_active = dot_nt(branch[...], downs[t])
        ins[3 * t + 1].wait()
        x = hidden_here[t]
        inner = jnp.tanh(GELU_SCALE * (x + GELU_CUBE * (x * x * x)))
        slope = 0.5 * (1.0 + inner) + (0.5 * GELU_SCALE) * x * (1.0 - inner * inner) * (
            1.0 + (3.0 * GELU_CUBE) * (x * x)
        )
        target = grad_own.at[t] if t < 2 else grad_other.at[t - 2]
        target[...] = (grad_active * slope).astype(LOW)
        ins[3 * t + 2].wait()
        product = dot_nt(target[...], ups[t])
        total[...] = product if t == 0 else total[...] + product
    _, unit, inverse = normalize(middle[...], gains[0:1], gains[1:2])
    back, gain, bias = normalize_back(total[...], unit, inverse, gains[0:1])
    grad_middle[...] = grad[...] + back
    grad_gains[0:1] = gain
    grad_gains[1:2] = bias


def hidden_back(place, grad, branch, middle, hidden, pair, gains):
    length, width = middle.shape
    one = (length, width)
    outs = [(one, FULL), ((2, width), FULL), ((2,) + one, LOW), ((2,) + one, LOW)]
    return call(
        hidden_back_kernel,
        place,
        outs,
        [grad, branch, middle, gains],
        [hidden] + list(pair),
        [
            pltpu.VMEM((4, width, width), LOW),
            pltpu.VMEM((4, width, width), LOW),
            pltpu.VMEM((4,) + one, FULL),
            pltpu.VMEM(one, FULL),
            pltpu.SemaphoreType.DMA((12,)),
        ],
        16 * length * width * width,
    )


def attention_back_kernel(
    place_of, grad_middle, resid, seg_col, seg_row, cosine, sine, gains, query, keys, values, lse,
    own, other,
    grad, branch, grad_gains, grad_own, grad_other,
    w_a, w_b, same, ga, gq, gk, gv, sems,
):
    width = resid.shape[1]
    half = width // 2
    copies = fetch(
        [tile_of(r, t, width) for t in (1, 0) for r in (own, other)],
        [w.at[place] for w in (w_b, w_a) for place in range(2)],
        sems,
    )
    first = place_of[0] == 0
    scale = HD ** (-0.5)
    grads = (grad_own, grad_other)
    same[...] = jnp.where(seg_col[...] == seg_row[...], 0.0, 1.0)
    attn_grad = grad_middle[...].astype(LOW)
    left, right = attn_grad[:, :half], attn_grad[:, half:]
    grad_own[1, :, half:] = jnp.where(first, left, right)
    grad_other[1, :, half:] = jnp.where(first, right, left)
    copies[0].wait()
    copies[1].wait()
    natural = dot_nt(grad_own[1, :, half:], w_b[0, :, half:]) + dot_nt(
        grad_other[1, :, half:], w_b[1, :, half:]
    )
    natural = natural.astype(LOW)
    ga[:, :half] = jnp.where(first, natural[:, :half], natural[:, half:])
    ga[:, half:] = jnp.where(first, natural[:, half:], natural[:, :half])

    def pair(p, _):
        columns = pl.ds(pl.multiple_of(p * 128, 128), 128)
        q, k, v, g = query[:, columns], keys[:, columns], values[:, columns], ga[:, columns]
        out_q, out_k, out_v = [], [], []
        for head in range(2):
            mask = head_mask(q.shape, head)
            zero = jnp.zeros_like(q)
            scores = dot_nt(k, jnp.where(mask, q, zero)) * scale
            scores = jnp.where(same[...] > 0.5, -1000000000.0, scores)
            probs = jnp.exp(scores - lse[pl.ds(2 * p + head, 1), :])
            grad_probs = dot_nt(v, jnp.where(mask, g, zero))
            across = jnp.sum(probs * grad_probs, 0, keepdims=True)
            grad_scores = (probs * (grad_probs - across)).astype(LOW)
            out_k.append(dot(grad_scores, q))
            out_q.append(cross(grad_scores, k))
            out_v.append(dot(probs.astype(LOW), g))
        for out, target in ((out_q, gq), (out_k, gk)):
            x = jnp.where(head_mask(out[0].shape, 0), out[0], out[1]) * scale
            x = x * cosine[...] - swap_halves(x) * sine[...]
            target[:, columns] = x.astype(LOW)
        gv[:, columns] = jnp.where(head_mask(out_v[0].shape, 0), out_v[0], out_v[1]).astype(LOW)
        return 0

    lax.fori_loop(0, width // 128, pair, 0)
    for place in range(2):
        columns = slice(place * half, (place + 1) * half)
        grads[place][0, :, :half] = gq[:, columns]
        grads[place][0, :, half:] = gk[:, columns]
        grads[place][1, :, :half] = gv[:, columns]
    copies[2].wait()
    copies[3].wait()
    total = dot_nt(grad_own[0], w_a[0]) + dot_nt(grad_other[0], w_a[1])
    total = total + dot_nt(grad_own[1, :, :half], w_b[0, :, :half])
    total = total + dot_nt(grad_other[1, :, :half], w_b[1, :, :half])
    _, unit, inverse = normalize(resid[...], gains[0:1], gains[1:2])
    back, gain, bias = normalize_back(total, unit, inverse, gains[0:1])
    back = grad_middle[...] + back
    grad[...] = back
    branch[...] = back.astype(LOW)
    grad_gains[0:1] = gain
    grad_gains[1:2] = bias


def attention_back(place, grad_middle, resid, mixer, gains, cosine, sine, segments, query, keys, values, lse):
    length, width = resid.shape
    one = (length, width)
    outs = [(one, FULL), (one, LOW), ((2, width), FULL)] + [((2,) + one, LOW)] * 2
    ins = [grad_middle, resid, segments[:, None], segments[None, :], cosine, sine, gains]
    ins += [query, keys, values, lse.T[: width // HD]]
    return call(
        attention_back_kernel,
        place,
        outs,
        ins,
        list(mixer),
        [
            pltpu.VMEM((2, width, width), LOW),
            pltpu.VMEM((2, width, width), LOW),
            pltpu.VMEM((length, length), FULL),
        ]
        + [pltpu.VMEM(one, LOW)] * 4
        + [pltpu.SemaphoreType.DMA((4,))],
        8 * length * width * width + 10 * length * length * width,
    )


def adam_step(master, grad, first, second, rate, decay):
    first = BETA_ONE * first + (1.0 - BETA_ONE) * grad
    second = BETA_TWO * second + (1.0 - BETA_TWO) * grad * grad
    fix_one = 1.0 - BETA_ONE**STEP
    fix_two = 1.0 - BETA_TWO**STEP
    update = first / fix_one / (jnp.sqrt(second / fix_two) + ADAM_EPS) + decay * master
    return (master - rate * update, first, second)


def swap_cores(value):
    return lax.ppermute(value, "dp", [(0, 1), (1, 0)])


def across(value, mask, size):
    return lax.ppermute(value, "fsdp", [(i, i ^ mask) for i in range(size)])


def tie(*values):
    return lax.optimization_barrier(values)


def total_of(value, size):
    value = value + swap_cores(value)
    for bit in range(size.bit_length() - 1):
        value = value + across(value, 1 << bit, size)
    return value


X, Y = 1, 2
Z = (4, 8, 12)


def place_kernel(parts, place_of, quarter, from_x, from_y, far_a, far_b, mixer, hidden, small, sems):
    x, y, z = place_of[1], place_of[2], place_of[3]
    rows = (parts[0] - parts[2]) // 3
    for xor_z in range(4):
        for xor_y in range(2):
            for xor_x in range(2):
                index = (z ^ xor_z) * 4 + (y ^ xor_y) * 2 + (x ^ xor_x)
                for h in range(2):
                    at = xor_z * parts[h]
                    if xor_x and xor_y:
                        source = (far_a, far_b)[h]
                    else:
                        source = from_x if xor_x else from_y if xor_y else quarter
                        at += h * 4 * parts[0]
                    for j in range(3):
                        target = mixer.at[h] if j == 0 else hidden.at[2 * (j - 1) + h]
                        pltpu.make_async_copy(
                            source.at[pl.ds(at + j * rows, rows)],
                            target.at[pl.ds(pl.multiple_of(index * rows, 16), rows)],
                            sems.at[h * 3 + j],
                        ).start()
                    if h == 0:
                        pltpu.make_async_copy(
                            source.at[pl.ds(at + 3 * rows, parts[2])],
                            small.at[pl.ds(pl.multiple_of(index * parts[2], 16), parts[2])],
                            sems.at[6],
                        ).start()
    for h in range(2):
        for j in range(3):
            target = mixer.at[h] if j == 0 else hidden.at[2 * (j - 1) + h]
            pltpu.make_async_copy(target, target, sems.at[h * 3 + j]).wait()
    pltpu.make_async_copy(small, small, sems.at[6]).wait()


def gather_blocks(place, shard_a, shard_b, small, size):
    rows, width = shard_a.shape[0] // 3, shard_a.shape[1]
    shard_a = jnp.concatenate([shard_a, small], 0)
    parts = (shard_a.shape[0], shard_b.shape[0], small.shape[0])
    shard = jnp.concatenate([shard_a, shard_b], 0)
    got = [across(shard, mask, size) for mask in Z]
    (got,) = tie(got)
    got = [shard] + got
    quarter = jnp.concatenate([g[: parts[0]] for g in got] + [g[parts[0] :] for g in got], 0)
    from_x, from_y = tie(across(quarter, X, size), across(quarter, Y, size))
    cut = 4 * parts[0]
    far_a, far_b = tie(across(from_y[:cut], X, size), across(from_x[cut:], Y, size))
    return call(
        functools.partial(place_kernel, parts),
        place,
        [
            ((2, width, width), LOW),
            ((4, width, width), LOW),
            ((size * parts[2], width), LOW),
        ],
        [],
        [quarter, from_x, from_y, far_a, far_b],
        [pltpu.SemaphoreType.DMA((7,))],
        0,
        outs_any=3,
    )


def round_kernel(jobs, n_ins, counts, *refs):
    new, once, twice, done = counts
    place_of, ins = refs[0], refs[1 : 1 + n_ins]
    rest = list(refs[1 + n_ins :])
    pop = lambda present, n=1: [rest.pop(0) for _ in range(n)] if present else [None] * n
    (keep_once,), (keep_twice,) = pop(once), pop(twice)
    from_x, from_y = pop(once or twice, 2)
    keep_done, *from_z = pop(done, 4)
    to_x, to_y = pop(new or once, 2)
    (out_once,), (out_twice,) = pop(new), pop(once)
    out_done, *to_z = pop(twice, 4)
    share, squares = pop(done, 2)
    (tile,) = pop(new)
    rows = (out_once if new else out_twice if once else out_done if twice else share).shape[-2]
    rows = rows // (8 if new else 4 if once else 1)
    bits, z = (place_of[1], place_of[2]), place_of[3]
    to, came = (to_x, to_y), (from_x, from_y)

    def block(index):
        if isinstance(index, int):
            return pl.ds(index * rows, rows)
        return pl.ds(pl.multiple_of(index * rows, 16), rows)

    def factor(spec):
        which, index, low, high = spec
        ref = ins[which] if index is None else ins[which].at[index]
        return ref[...] if low is None else ref[:, low:high]

    for p in range(new):
        for s in range(2):
            for low, high, products in jobs[2 * p + s]:
                total = None
                for left, right in products:
                    product = cross(factor(left), factor(right))
                    total = product if total is None else total + product
                tile[:, low:high] = total
            for zz in range(4):
                for other in range(2):
                    at = zz * 2 + other
                    index = lambda bit: zz * 4 + (other * 2 + bit if s == 0 else bit * 2 + other)
                    to[s][block(p * 8 + at), :] = tile[block(index(1 - bits[s])), :].astype(LOW)
                    out_once[p, s, block(at), :] = tile[block(index(bits[s])), :]
    for p in range(once):
        for s in range(2):
            for zz in range(4):
                for bit in range(2):
                    at = zz * 2 + (bits[1 - s] if bit else 1 - bits[1 - s])
                    value = keep_once[p, s, block(at), :] + came[s][block(p * 8 + at), :].astype(FULL)
                    if bit:
                        out_twice[p, s, block(zz), :] = value
                    else:
                        to[1 - s][block(new * 8 + p * 4 + zz), :] = value.astype(LOW)
    for p in range(twice):
        for s in range(2):
            for xor in range(4):
                at = jnp.bitwise_xor(z, xor)
                value = keep_twice[p, s, block(at), :] + came[1 - s][
                    block(once * 8 + p * 4 + at), :
                ].astype(FULL)
                if xor == 0:
                    out_done[p, s] = value
                else:
                    to_z[xor - 1][block(2 * p + s), :] = value.astype(LOW)
    if done:
        squares[...] = jnp.zeros_like(squares)
    for p in range(done):
        for s in range(2):
            value = keep_done[p, s]
            for f in from_z:
                value = value + f[block(2 * p + s), :].astype(FULL)
            share[p, s] = value
            squares[...] += jnp.sum(value * value, 0, keepdims=True)


class Rounds:
    def __init__(self, place, rows, width):
        self.place, self.rows, self.width = place, rows, width
        self.counts = (0, 0, 0, 0)
        self.kept = [None] * 3
        self.came = None
        self.came_z = None
        self.shares, self.squares = [], []
        self.flying = []

    def step(self, chunk):
        rows, width = self.rows, self.width
        new, once, twice, done = counts = (len(chunk),) + self.counts[:3]
        arrays, jobs = [], []

        def number(spec):
            array, *place = spec
            for i, known in enumerate(arrays):
                if known is array:
                    return (i, *place)
            arrays.append(array)
            return (len(arrays) - 1, *place)

        for pair in chunk:
            for tile in pair:
                jobs.append(
                    [(a, b, [(number(l), number(r)) for l, r in ps]) for a, b, ps in tile]
                )
        ins = list(arrays)
        if once:
            ins.append(self.kept[0])
        if twice:
            ins.append(self.kept[1])
        if once or twice:
            ins += self.came
        if done:
            ins += [self.kept[2]] + self.came_z
        outs = []
        if new or once:
            outs += [(((new * 8 + once * 4) * rows, width), LOW)] * 2
        if new:
            outs.append(((new, 2, 8 * rows, width), FULL))
        if once:
            outs.append(((once, 2, 4 * rows, width), FULL))
        if twice:
            outs.append(((twice, 2, rows, width), FULL))
            outs += [((twice * 2 * rows, width), LOW)] * 3
        if done:
            outs += [((done, 2, rows, width), FULL), ((1, width), FULL)]
        length = 2 * arrays[0].shape[-2] if new else 0
        got = call(
            functools.partial(round_kernel, jobs, len(arrays), counts),
            self.place,
            outs,
            ins,
            [],
            [pltpu.VMEM((16 * rows, width), FULL)] if new else [],
            4 * new * length * width * width,
        )
        got = list(got)
        self.flying, self.kept, self.counts = [], [None] * 3, counts
        if new or once:
            self.flying += [across(got.pop(0), X, 16), across(got.pop(0), Y, 16)]
        if new:
            self.kept[0] = got.pop(0)
        if once:
            self.kept[1] = got.pop(0)
        if twice:
            self.kept[2] = got.pop(0)
            self.flying += [across(got.pop(0), mask, 16) for mask in Z]
        if done:
            self.shares.append(got[0])
            self.squares.append(got[1])

    def finish(self, *ties):
        flying, ties = tie(self.flying, ties)
        self.came = self.came_z = None
        if self.counts[0] or self.counts[1]:
            self.came, flying = flying[:2], flying[2:]
        if self.counts[2]:
            self.came_z = flying
        return ties

    def left(self):
        return any(self.counts[:3])


class PlainRounds:
    def __init__(self):
        self.shares, self.squares = [], []

    def step(self, chunk):
        def factor(spec):
            array, index, low, high = spec
            array = array if index is None else array[index]
            return array if low is None else array[:, low:high]

        def summed(tile):
            parts = [sum(cross(factor(l), factor(r)) for l, r in ps) for _, _, ps in tile]
            return lax.psum_scatter(
                jnp.concatenate(parts, 1), "fsdp", scatter_dimension=0, tiled=True
            )

        share = jnp.stack([jnp.stack([summed(tile) for tile in pair]) for pair in chunk])
        self.shares.append(share)
        self.squares.append(jnp.sum(share * share, (0, 1, 2))[None])

    def finish(self, *ties):
        return ties

    def left(self):
        return False


def small_steps(value, place, size, rows):
    (got,) = yield [swap_cores(value)]
    value = (value + got).reshape(-1, 4, 2, 2, rows).transpose(1, 2, 3, 0, 4)
    for bit in range(2):
        axis = 2 - bit
        send = lax.dynamic_index_in_dim(value, 1 - place[1 + bit], axis, keepdims=False)
        keep = lax.dynamic_index_in_dim(value, place[1 + bit], axis, keepdims=False)
        (got,) = yield [across(send, 1 << bit, size)]
        value = keep + got
    take = lambda xor: lax.dynamic_index_in_dim(value, place[3] ^ xor, 0, keepdims=False)
    got = yield [across(take(mask // 4), mask, size) for mask in Z]
    return take(0) + (got[0] + (got[1] + got[2]))


def up_to_parts(expand_shard, size, rows, parts):
    r = expand_shard.shape[0]
    return expand_shard.reshape(r, size, parts, rows).transpose(0, 2, 1, 3).reshape(r, -1)


def up_from_parts(expand_shard, size, rows, parts):
    r = expand_shard.shape[0]
    return expand_shard.reshape(r, parts, size, rows).transpose(0, 2, 1, 3).reshape(r, -1)


def half_of(value, core):
    half = value.shape[1] // 2
    return lax.dynamic_slice_in_dim(value, core * half, half, 1)


def body(
    fsdp,
    codons,
    masked,
    segments,
    inward,
    outward,
    expand,
    shrink,
    codon_table,
    norm_params,
    inward_first,
    inward_second,
    outward_first,
    outward_second,
    expand_first,
    expand_second,
    shrink_first,
    shrink_second,
    table_first,
    table_second,
    norm_first,
    norm_second,
):
    layers = inward.shape[0]
    length = codons.shape[0]
    rows = inward.shape[1]
    width = rows * fsdp
    half = width // 2
    parts = shrink.shape[1] // rows
    fast = fsdp == 16 and rows % 16 == 0
    core, index = lax.axis_index("dp"), lax.axis_index("fsdp")
    bit = lambda b: lax.rem(lax.div(index, b), 2)
    place = jnp.stack([core, bit(1), bit(2), lax.div(index, 4)]).astype(jnp.int32)
    weight = masked.astype(FULL)
    inputs = jnp.where(masked == 1, V - 1, codons)

    def tiles_of(l):
        w_in, w_out = inward[l].astype(LOW), outward[l].astype(LOW)
        pieces = [half_of(w_in[:, p * width : (p + 1) * width], core) for p in range(3)]
        pieces.append(half_of(w_out, core))
        mixer = [jnp.concatenate(pieces[:2], 1), jnp.concatenate(pieces[2:], 1)]
        up = half_of(up_to_parts(expand[l].astype(LOW), fsdp, rows, parts), core)
        down = lax.dynamic_slice_in_dim(shrink[l].astype(LOW), core * 2 * rows, 2 * rows, 0)
        return mixer + [up[:, :width], up[:, width:], down[:rows], down[rows:]]

    norms = norm_params.shape[0] * 2
    small = jnp.concatenate(
        [codon_table.astype(LOW), norm_params.astype(LOW).reshape(norms, rows)], 0
    )
    mixers, hiddens = [None] * layers, [None] * layers
    plain = list(range(1, layers)) if fast else list(range(layers))
    sides = [jnp.concatenate(tiles_of(l), 1) for l in plain]
    if fast:
        tiles = tiles_of(0)
        flat = small.reshape(-1)
        flat = jnp.pad(flat, (0, -flat.shape[0] % (16 * width))).reshape(-1, width)
        shard_a = jnp.concatenate(tiles[0::2], 0)
        shard_b = jnp.concatenate(tiles[1::2], 0)
        sides, shard_a = tie(sides, shard_a)
    for l, side in zip(plain, sides):
        own = lax.all_gather(side, "fsdp", axis=0, tiled=True)
        mixers[l], hiddens[l] = own[:, : 2 * width], own[:, 2 * width :]
    if fast:
        mixers[0], hiddens[0], blocks = gather_blocks(place, shard_a, shard_b, flat, fsdp)
        blocks = blocks.reshape(fsdp, -1)[:, : small.size].reshape(fsdp, V + norms, rows)
        small = blocks.transpose(1, 0, 2).reshape(V + norms, width)
    else:
        small = lax.all_gather(small, "fsdp", axis=1, tiled=True)
    mixers = [(own, swap_cores(own)) for own in mixers]
    hiddens = [(own, swap_cores(own)) for own in hiddens]
    table_low = small[:V]
    gains = small[V:].astype(FULL).reshape(-1, 2, width)

    cosine, sine = rotary_tables(length)
    vocab_ids = jnp.arange(V, dtype=jnp.int32)
    chosen = (inputs[:, None] == vocab_ids[None, :]).astype(LOW)
    resid = dot(chosen, table_low)
    kept = []
    for l in range(layers):
        gain = gains[2 * l : 2 * l + 2]
        middle, query, keys, values, lse, pack = attention_forward(
            place, resid, mixers[l], gain[0], cosine, sine, segments
        )
        if l > 0:
            middle, came = tie(middle, kept[-1][-1])
            kept[-1] = kept[-1][:-1] + (came,)
        pack_came = swap_cores(pack)
        output, active, pack_mid, hidden = hidden_forward(place, middle, hiddens[l], gain[1])
        output, pack_came = tie(output, pack_came)
        kept.append(
            (resid, query, keys, values, lse, pack, pack_came, middle, hidden, active, pack_mid)
            + (swap_cores(pack_mid),)
        )
        resid = output
    final_gain = gains[2 * layers]
    normed_out, unit_out, inverse_out = normalize(resid, final_gain[0], final_gain[1])
    head_in = normed_out.astype(LOW)
    logits = jnp.einsum("sd,vd->sv", head_in, table_low, preferred_element_type=FULL)
    top = jnp.max(logits, -1, keepdims=True)
    lse_head = top + jnp.log(jnp.sum(jnp.exp(logits - top), -1, keepdims=True))
    targets = (codons[:, None] == vocab_ids[None, :]).astype(FULL)
    picked = jnp.sum(logits * targets, -1)
    loss_local = jnp.sum((lse_head[:, 0] - picked) * weight)
    grad_logits = ((jnp.exp(logits - lse_head) - targets) * weight[:, None]).astype(LOW)
    grad_table = cross(grad_logits, head_in)
    grad_head = dot(grad_logits, table_low)
    grad, grad_final_gain, grad_final_bias = normalize_back(
        grad_head, unit_out, inverse_out, final_gain[0]
    )
    branch = grad.astype(LOW)
    grad_norms = [grad_final_gain, grad_final_bias]
    grad, branch, came = tie(grad, branch, kept[-1][-1])
    kept[-1] = kept[-1][:-1] + (came,)

    rounds = Rounds(place, rows, width) if fast else PlainRounds()
    whole = lambda array, i=None: (array, i, None, None)
    tile = lambda left, right, other_left, other_right: [
        (0, width, [(left, right), (other_left, other_right)])
    ]
    chunk = []
    for l in reversed(range(layers)):
        (resid, query, keys, values, lse, pack, pack_came, middle, hidden, active, pack_mid, mid_came) = kept[l]
        gain = gains[2 * l : 2 * l + 2]
        branch_came = swap_cores(branch)
        chunk.append(
            [
                tile(
                    whole(active, s), whole(branch), whole(mid_came, 1 + s), whole(branch_came)
                )
                for s in range(2)
            ]
        )
        rounds.step(chunk)
        grad_middle, gains_mid, up_own, up_other = hidden_back(
            place, grad, branch, middle, hidden, hiddens[l], gain[1]
        )
        grad_middle, up_own, up_came = rounds.finish(grad_middle, up_own, swap_cores(up_other))
        rounds.step(
            [
                [
                    tile(
                        whole(pack_mid, 0), whole(up_own, s), whole(mid_came, 0), whole(up_came, s)
                    )
                    for s in range(2)
                ]
            ]
        )
        grad, branch, gains_in, mix_own, mix_other = attention_back(
            place, grad_middle, resid, mixers[l], gain[0], cosine, sine, segments,
            query, keys, values, lse,
        )
        grad_norms = [gains_in, gains_mid] + grad_norms
        grad, branch, mix_own, mix_came = rounds.finish(
            grad, branch, mix_own, swap_cores(mix_other)
        )
        products = lambda i, a, b: [
            ((pack, i, None, None), (mix_own, 1, a, b)),
            ((pack_came, i, None, None), (mix_came, 1, a, b)),
        ]
        chunk = [
            [
                tile(whole(pack, 0), whole(mix_own, 0), whole(pack_came, 0), whole(mix_came, 0)),
                [(0, half, products(0, 0, half)), (half, width, products(1, half, width))],
            ]
        ]
    grad_table = grad_table + cross(chosen, branch)
    grad_small = jnp.concatenate([grad_table] + grad_norms, 0)
    if fast:
        steps = small_steps(grad_small, place, fsdp, rows)
        messages = steps.send(next(steps))
        rounds.step(chunk)
        share_small = None
        while rounds.left() or share_small is None:
            ((messages,),) = (rounds.finish(messages),)
            try:
                messages = steps.send(messages) if share_small is None else []
            except StopIteration as end:
                share_small, messages = end.value, []
            if rounds.left():
                rounds.step([])
    else:
        rounds.step(chunk)
        share_small = lax.psum_scatter(
            grad_small + swap_cores(grad_small), "fsdp", scatter_dimension=1, tiled=True
        )

    squares = 0.5 * jnp.sum(share_small * share_small)
    for value in rounds.squares:
        squares = squares + jnp.sum(value)
    totals = jnp.stack([loss_local, jnp.sum(weight), squares])
    totals = total_of(jnp.pad(totals, (0, 125))[None], fsdp)
    loss_sum, count, square_total = totals[0, 0], totals[0, 1], totals[0, 2]

    both = []
    for share in rounds.shares:
        other = swap_cores(share)
        first = core == 0
        both.append((jnp.where(first, share, other), jnp.where(first, other, share)))
    share_in, share_out, share_up, share_down = ([None] * layers for _ in range(4))
    side = lambda *values: jnp.concatenate(values, 1)
    for l in range(layers):
        at = 2 * (layers - 1 - l)
        down, up, mix = (at, at and 1), (at + 1, 0), (at + 2, 0)
        tiles = lambda where: [both[where[0]][c][where[1], s] for c in range(2) for s in range(2)]
        a_0, b_0, a_1, b_1 = tiles(mix)
        share_in[l] = side(
            a_0[:, :half], a_1[:, :half], a_0[:, half:], a_1[:, half:], b_0[:, :half], b_1[:, :half]
        )
        share_out[l] = side(b_0[:, half:], b_1[:, half:])
        share_up[l] = up_from_parts(side(*tiles(up)), fsdp, rows, parts)
        share_down[l] = jnp.concatenate(tiles(down), 0)
    group = (
        jnp.stack(share_in),
        jnp.stack(share_out),
        jnp.stack(share_up),
        jnp.stack(share_down),
        share_small[:V],
        share_small[V:].reshape(-1, 2, rows),
    )
    grad_norm = jnp.sqrt(square_total) / count
    factor = CLIP / jnp.maximum(grad_norm, CLIP)
    masters = (inward, outward, expand, shrink, codon_table, norm_params)
    firsts = (inward_first, outward_first, expand_first, shrink_first, table_first, norm_first)
    seconds = (
        inward_second,
        outward_second,
        expand_second,
        shrink_second,
        table_second,
        norm_second,
    )
    result = [loss_sum, count, grad_norm]
    for index in range(6):
        rate = RATE_VECTOR if index == 5 else RATE_MATRIX
        decay = 0.0 if index == 5 else DECAY
        clipped = group[index] / count * factor
        result.extend(
            adam_step(masters[index], clipped, firsts[index], seconds[index], rate, decay)
        )
    return tuple(result)


def solution(mesh):
    in_specs = (
        P(("fsdp", "dp")),
        P(("fsdp", "dp")),
        P(("fsdp", "dp")),
        P(None, "fsdp", None),
        P(None, "fsdp", None),
        P(None, "fsdp", None),
        P(None, "fsdp", None),
        P(None, "fsdp"),
        P(None, None, "fsdp"),
        P(None, "fsdp", None),
        P(None, "fsdp", None),
        P(None, "fsdp", None),
        P(None, "fsdp", None),
        P(None, "fsdp", None),
        P(None, "fsdp", None),
        P(None, "fsdp", None),
        P(None, "fsdp", None),
        P(None, "fsdp"),
        P(None, "fsdp"),
        P(None, None, "fsdp"),
        P(None, None, "fsdp"),
    )
    out_specs = (
        P(),
        P(),
        P(),
        P(None, "fsdp", None),
        P(None, "fsdp", None),
        P(None, "fsdp", None),
        P(None, "fsdp", None),
        P(None, "fsdp", None),
        P(None, "fsdp", None),
        P(None, "fsdp", None),
        P(None, "fsdp", None),
        P(None, "fsdp", None),
        P(None, "fsdp", None),
        P(None, "fsdp", None),
        P(None, "fsdp", None),
        P(None, "fsdp"),
        P(None, "fsdp"),
        P(None, "fsdp"),
        P(None, None, "fsdp"),
        P(None, None, "fsdp"),
        P(None, None, "fsdp"),
    )
    step = functools.partial(body, mesh.shape["fsdp"])
    return jax.shard_map(step, mesh=mesh, in_specs=in_specs, out_specs=out_specs, check_vma=False)
```

time: 718 us -> 911 us (1.27)
  Pallas kernels: 140 us -> 437 us
  other arithmetic: 112 us -> 41.3 us
  waiting for transfers between devices: 186 us -> 246 us
  local copies, waits for them, and re-layouts: 113 us -> 66.9 us
  matrix products: 45.5 us -> 5.11 us
    pallas_call x8 -> x17, Pallas kernels: 140 us -> 437 us  [call(): pl.pallas_call(kernel, out_shape=[jax.ShapeDtypeStruct(s, t) for s, t in...]
    ppermute x70 -> x64, waiting for transfers between devices: 186 us -> 246 us  [the longest x43 245 us: across(): return lax.ppermute(value, 'fsdp', [(i, i ^ mask) for i in range(size)])]
    dot_general x30 -> x2, matrix products: 42.2 us -> 1.83 us  [cross(): lax.dot_general(left, right, (((0,), (0,)), ((), ())), preferred_element_...]
    concatenate x44 -> x2, other arithmetic: 22.2 us -> 0.78 us  [the longest x1 0.7 us: body(): shard_a = jnp.concatenate(tiles[0::2], 0)]
    slice x71 -> x20, local copies, waits for them, and re-layouts: 33.2 us -> 13 us  [the longest x2 8.07 us: body(): mixers[l], hiddens[l] = (own[:, :2 * width], own[:, 2 * width:])]
    add x53 -> x8, other arithmetic: 18.4 us -> 4.85 us  [the longest x4 1.35 us: total_of(): value = value + across(value, 1 << bit, size)]
    unnamed x372 -> x214, local copies, waits for them, and re-layouts: 34.6 us -> 23 us
    unnamed x12 -> x2, other arithmetic: 11.2 us -> 0.02 us
  transfers between devices with their start and end apart: 71 -> 65, of which waited for: 28 -> 27; matrix products, arithmetic and copies ran while one was open for 18% -> 8% of each run, Pallas kernels for 18% -> 42%
where the time goes in v4:
time: 911 us; the launch traced here: 900 us
  Pallas kernels  437 us (48%)
  waiting for transfers between devices  246 us (27%)
  starting transfers between devices  81.1 us (9%)
  local copies, waits for them, and re-layouts  66.9 us (7%)
  other arithmetic  41.3 us (5%)
  between operations  22.4 us (2%)
    pallas_call x17, Pallas kernels, call(): pl.pallas_call(kernel, out_shape=[jax.ShapeDtypeStruct(s, t) for s, t in...  437 us
    ppermute x43, waiting for transfers between devices, across(): return lax.ppermute(value, 'fsdp', [(i, i ^ mask) for i in range(size)])  245 us
    ppermute x43, starting transfers between devices, across(): return lax.ppermute(value, 'fsdp', [(i, i ^ mask) for i in range(size)])  77.5 us
    unnamed x214, local copies, waits for them, and re-layouts  23 us
  transfers between devices with their start and end apart: 65, of which 27 were waited for; matrix products, arithmetic and copies ran while one was open for 8% of the time, Pallas kernels for 42%

profile of v4, /device:TPU:0, one launch (start us, length us, event | category | flops | bytes accessed | tf_op | source)
XLA Modules:
  0.0 900.2 jit_solution(4431253558233858134)
XLA Ops:
  28.0 5.0 collective-permute-start.2
  33.7 14.8 %collective-permute-done.2 = bf16[304,768]{1,0:T(8,128)(2,1)S(1)} collective-permute-done((bf16[304,768]{1,0:T(8,128)(2,1)S(1)}, bf16[304,768]{1,0:T(8,128)(2,1)S(1)}, u32[]{:S(2)}, u32[]{:S(2)}) %collective-permute-start.2) | collective-permute-done | bytes 466976 | tf_op jit(solution)/shard_map/ppermute | solution.py:429
  48.5 43.5 %collective-permute-done.1 = bf16[304,768]{1,0:T(8,128)(2,1)S(1)} collective-permute-done((bf16[304,768]{1,0:T(8,128)(2,1)S(1)}, bf16[304,768]{1,0:T(8,128)(2,1)S(1)}, u32[]{:S(2)}, u32[]{:S(2)}) %collective-permute-start.1) | collective-permute-done | bytes 466976 | tf_op jit(solution)/shard_map/ppermute | solution.py:429
  93.1 1.6 collective-permute-start.4
  96.3 62.6 %collective-permute-done.4.from_y = bf16[1216,768]{1,0:T(8,128)(2,1)S(1)} collective-permute-done((bf16[1216,768]{1,0:T(8,128)(2,1)S(1)}, bf16[1216,768]{1,0:T(8,128)(2,1)S(1)}, u32[]{:S(2)}, u32[]{:S(2)}) %collective-permute-start.4) | collective-permute-done | bytes 1867808 | tf_op jit(solution)/shard_map/ppermute | solution.py:429
  158.9 3.1 collective-permute-done.3.from_x
  163.1 1.8 collective-permute-start.5
  166.9 12.3 %collective-permute-done.6.far_b = bf16[576,768]{1,0:T(8,128)(2,1)} collective-permute-done((bf16[576,768]{1,0:T(8,128)(2,1)}, bf16[576,768]{1,0:T(8,128)(2,1)}, u32[]{:S(2)}, u32[]{:S(2)}) %collective-permute-start.6) | collective-permute-done | bytes 884768 | tf_op jit(solution)/shard_map/ppermute | solution.py:429
  179.2 228.2 %shard_map.364 = (bf16[2,768,768]{2,1,0:T(8,128)(2,1)}, bf16[4,768,768]{2,1,0:T(8,128)(2,1)}, bf16[256,768]{1,0:T(8,128)(2,1)}) custom-call(s32[4]{0:T(128)} %pad_add_fusion.place_of.refs_0_, bf16[1216,768]{1,0:T(8,128)(2,1)} %copy-done.11, bf16[1216,768]{1,0:T(8,128)(2,1)} %copy-done.5, bf16[1216,768]{1,0:T(8,128)(2,1)} %copy-done.4, ...), custom_call_target="tpu_custom_call" | custom-call | bytes 7471104 | tf_op jit(solution)/shard_map/pallas_call | solution.py:77
  408.9 4.8 slice.440.own
  417.6 3.3 slice.438.own
  422.6 1.6 fusion.10.resid
  424.2 17.6 %shard_map.365 = (f32[512,768]{1,0:T(8,128)}, bf16[512,768]{1,0:T(8,128)(2,1)}, bf16[512,768]{1,0:T(8,128)(2,1)}, bf16[512,768]{1,0:T(8,128)(2,1)}, f32[512,128]{1,0:T(8,128)}, /*index=5*/bf16[2,512,768]{2,1,0:T(8,128)(2,1)}) custom-call(s32[4]{0:T(128)} %pad_add_fusion.place_of.refs_0_, f32[512,768]{1,0:T(8,128)} %fusion.10.resid, s32[512,1]{1,0:T(8,128)} %copy.77.seg_col, ...), custom_call_target="tpu_custom_call" | custom-call | flops 3221225472 | bytes 6825984 | tf_op jit(solution)/shard_map/pallas_call | solution.py:77
  442.6 13.4 %shard_map.366 = (f32[512,768]{1,0:T(8,128)}, bf16[2,512,768]{2,1,0:T(8,128)(2,1)}, bf16[3,512,768]{2,1,0:T(8,128)(2,1)}, f32[4,512,768]{2,1,0:T(8,128)}) custom-call(s32[4]{0:T(128)} %pad_add_fusion.place_of.refs_0_, f32[512,768]{1,0:T(8,128)} %get-tuple-element.186.middle, f32[2,768]{1,0:T(2,128)} %slice.362.gains, ...), custom_call_target="tpu_custom_call" | custom-call | flops 4831838208 | bytes 11016192 | tf_op jit(solution)/shard_map/pallas_call | solution.py:77
  457.2 17.8 %shard_map.367 = (f32[512,768]{1,0:T(8,128)}, bf16[512,768]{1,0:T(8,128)(2,1)}, bf16[512,768]{1,0:T(8,128)(2,1)}, bf16[512,768]{1,0:T(8,128)(2,1)}, f32[512,128]{1,0:T(8,128)}, /*index=5*/bf16[2,512,768]{2,1,0:T(8,128)(2,1)}) custom-call(s32[4]{0:T(128)} %pad_add_fusion.place_of.refs_0_, f32[512,768]{1,0:T(8,128)} %get-tuple-element.190.resid, ...), custom_call_target="tpu_custom_call" | custom-call | flops 3221225472 | bytes 6825984 | tf_op jit(solution)/shard_map/pallas_call | solution.py:77
  479.7 13.3 %shard_map.368 = (f32[512,768]{1,0:T(8,128)}, bf16[2,512,768]{2,1,0:T(8,128)(2,1)}, bf16[3,512,768]{2,1,0:T(8,128)(2,1)}, f32[4,512,768]{2,1,0:T(8,128)}) custom-call(s32[4]{0:T(128)} %pad_add_fusion.place_of.refs_0_, f32[512,768]{1,0:T(8,128)} %get-tuple-element.194.middle, f32[2,768]{1,0:T(2,128)} %slice.367.gains, bf16[768,3072]{1,0:T(8,128)(2,1)} %slice.440.own, ...), custom_call_target="tpu_custom_call" | custom-call | flops 4831838208 | bytes 11016192 | tf_op jit(solution)/shard_map/pallas_call | solution.py:77
  493.0 1.7 reduce_sum.144
  498.9 1.6 fusion.27
  501.4 17.6 %shard_map.370 = (f32[512,768]{1,0:T(8,128)}, f32[2,768]{1,0:T(2,128)}, bf16[2,512,768]{2,1,0:T(8,128)(2,1)}, bf16[2,512,768]{2,1,0:T(8,128)(2,1)}) custom-call(s32[4]{0:T(128)} %pad_add_fusion.place_of.refs_0_, f32[512,768]{1,0:T(8,128)} %get-tuple-element.204.grad, bf16[512,768]{1,0:T(8,128)(2,1)} %copy-done.7, f32[512,768]{1,0:T(8,128)} %get-tuple-element.194.middle, ...), custom_call_target="tpu_custom_call" | custom-call | flops 4831838208 | bytes 19666944 | tf_op jit(solution)/shard_map/pallas_call | solution.py:77
  520.1 7.0 shard_map.369
  529.0 1.8 copy.82
  532.1 10.9 %collective-permute-done.16.refs_6_ = bf16[384,768]{1,0:T(8,128)(2,1)} collective-permute-done((bf16[384,768]{1,0:T(8,128)(2,1)}, bf16[384,768]{1,0:T(8,128)(2,1)}, u32[]{:S(2)}, u32[]{:S(2)}) %collective-permute-start.16) | collective-permute-done | bytes 589856 | tf_op jit(solution)/shard_map/ppermute | solution.py:429
  544.2 23.5 %shard_map.372 = (f32[512,768]{1,0:T(8,128)}, bf16[512,768]{1,0:T(8,128)(2,1)}, f32[2,768]{1,0:T(2,128)}, bf16[2,512,768]{2,1,0:T(8,128)(2,1)}, bf16[2,512,768]{2,1,0:T(8,128)(2,1)}) custom-call(s32[4]{0:T(128)} %pad_add_fusion.place_of.refs_0_, f32[512,768]{1,0:T(8,128)} %get-tuple-element.216.grad_middle, f32[512,768]{1,0:T(8,128)} %get-tuple-element.190.resid, ...), custom_call_target="tpu_custom_call" | custom-call | flops 4429185024 | bytes 10782720 | tf_op jit(solution)/shard_map/pallas_call | solution.py:77
  567.9 9.5 %shard_map.371 = (bf16[576,768]{1,0:T(8,128)(2,1)}, bf16[576,768]{1,0:T(8,128)(2,1)}, f32[1,2,384,768]{3,2,1,0:T(8,128)}, f32[1,2,192,768]{3,2,1,0:T(8,128)}) custom-call(s32[4]{0:T(128)} %pad_add_fusion.place_of.refs_0_, bf16[3,512,768]{2,1,0:T(8,128)(2,1)} %get-tuple-element.198.refs_1_, bf16[2,512,768]{2,1,0:T(8,128)(2,1)} %get-tuple-element.209.refs_2_, ...), custom_call_target="tpu_custom_call" | custom-call | flops 2415919104 | bytes 11403264 | tf_op jit(solution)/shard_map/pallas_call | solution.py:77
  578.3 21.3 %collective-permute-done.19.refs_11_ = bf16[576,768]{1,0:T(8,128)(2,1)S(1)} collective-permute-done((bf16[576,768]{1,0:T(8,128)(2,1)}, bf16[576,768]{1,0:T(8,128)(2,1)S(1)}, u32[]{:S(2)}, u32[]{:S(2)}) %collective-permute-start.19) | collective-permute-done | bytes 884768 | tf_op jit(solution)/shard_map/ppermute | solution.py:429
  600.0 18.3 %shard_map.374 = (f32[512,768]{1,0:T(8,128)}, f32[2,768]{1,0:T(2,128)}, bf16[2,512,768]{2,1,0:T(8,128)(2,1)}, bf16[2,512,768]{2,1,0:T(8,128)(2,1)}) custom-call(s32[4]{0:T(128)} %pad_add_fusion.place_of.refs_0_, f32[512,768]{1,0:T(8,128)} %get-tuple-element.240.grad, bf16[512,768]{1,0:T(8,128)(2,1)} %get-tuple-element.229.refs_6_.branch, ...), custom_call_target="tpu_custom_call" | custom-call | flops 4831838208 | bytes 19666944 | tf_op jit(solution)/shard_map/pallas_call | solution.py:77
  618.4 15.3 %shard_map.373 = (bf16[960,768]{1,0:T(8,128)(2,1)}, bf16[960,768]{1,0:T(8,128)(2,1)}, f32[2,2,384,768]{3,2,1,0:T(8,128)}, f32[1,2,192,768]{3,2,1,0:T(8,128)}, f3...) custom-call(s32[4]{0:T(128)} %pad_add_fusion.place_of.refs_0_, ...), custom_call_target="tpu_custom_call" | custom-call | flops 4831838208 | bytes 17104896 | tf_op jit(solution)/shard_map/pallas_call | solution.py:77
  636.6 4.3 collective-permute-start.26
  641.6 5.9 collective-permute-start.27
  647.5 1.8 copy.84
  651.3 17.5 %collective-permute-done.23.refs_7_ = bf16[960,768]{1,0:T(8,128)(2,1)} collective-permute-done((bf16[960,768]{1,0:T(8,128)(2,1)}, bf16[960,768]{1,0:T(8,128)(2,1)}, u32[]{:S(2)}, u32[]{:S(2)}) %collective-permute-start.23) | collective-permute-done | bytes 1474592 | tf_op jit(solution)/shard_map/ppermute | solution.py:429
  669.9 23.0 %shard_map.376 = (f32[512,768]{1,0:T(8,128)}, bf16[512,768]{1,0:T(8,128)(2,1)}, f32[2,768]{1,0:T(2,128)}, bf16[2,512,768]{2,1,0:T(8,128)(2,1)}, bf16[2,512,768]{2,1,0:T(8,128)(2,1)}) custom-call(s32[4]{0:T(128)} %pad_add_fusion.place_of.refs_0_, f32[512,768]{1,0:T(8,128)} %get-tuple-element.260.grad_middle, f32[512,768]{1,0:T(8,128)} %fusion.10.resid, ...), custom_call_target="tpu_custom_call" | custom-call | flops 4429185024 | bytes 10782720 | tf_op jit(solution)/shard_map/pallas_call | solution.py:77
  693.0 12.2 %shard_map.375 = (bf16[768,768]{1,0:T(8,128)(2,1)}, bf16[768,768]{1,0:T(8,128)(2,1)}, f32[1,2,384,768]{3,2,1,0:T(8,128)}, f32[2,2,192,768]{3,2,1,0:T(8,128)}, f3...) custom-call(s32[4]{0:T(128)} %pad_add_fusion.place_of.refs_0_, ...), custom_call_target="tpu_custom_call" | custom-call | flops 2415919104 | bytes 17448960 | tf_op jit(solution)/shard_map/pallas_call | solution.py:77
  707.7 4.2 collective-permute-start.32
  712.1 6.3 collective-permute-start.33
  718.4 3.7 collective-permute-done.32.refs_11_
  722.2 11.6 %collective-permute-done.29.refs_7_ = bf16[768,768]{1,0:T(8,128)(2,1)S(1)} collective-permute-done((bf16[768,768]{1,0:T(8,128)(2,1)}, bf16[768,768]{1,0:T(8,128)(2,1)S(1)}, u32[]{:S(2)}, u32[]{:S(2)}) %collective-permute-start.29) | collective-permute-done | bytes 1179680 | tf_op jit(solution)/shard_map/ppermute | solution.py:429
  735.8 11.3 %shard_map.377 = (bf16[576,768]{1,0:T(8,128)(2,1)}, bf16[576,768]{1,0:T(8,128)(2,1)}, f32[1,2,384,768]{3,2,1,0:T(8,128)}, f32[1,2,192,768]{3,2,1,0:T(8,128)}, f3...) custom-call(s32[4]{0:T(128)} %pad_add_fusion.place_of.refs_0_, ...), custom_call_target="tpu_custom_call" | custom-call | flops 2415919104 | bytes 14106624 | tf_op jit(solution)/shard_map/pallas_call | solution.py:77
  749.3 1.6 convolution_add_fusion
  752.0 4.3 collective-permute-start.39
  758.4 8.3 collective-permute-done.38.refs_6_
  767.3 9.8 %collective-permute-done.39.refs_7_ = bf16[192,768]{1,0:T(8,128)(2,1)} collective-permute-done((bf16[192,768]{1,0:T(8,128)(2,1)}, bf16[192,768]{1,0:T(8,128)(2,1)}, u32[]{:S(2)}, u32[]{:S(2)}) %collective-permute-start.39) | collective-permute-done | bytes 294944 | tf_op jit(solution)/shard_map/ppermute | solution.py:429
  779.0 1.7 collective-permute-start.47
  780.8 4.6 shard_map.378
  789.5 6.4 collective-permute-start.44
  800.7 8.5 collective-permute-done.45.refs_6_
  809.5 2.3 collective-permute-start.51
  812.9 1.6 collective-permute-start.53
  814.5 2.7 shard_map.379
  818.3 1.6 collective-permute-start.49
  820.0 1.7 collective-permute-start.50
  825.0 5.7 collective-permute-done.49.refs_3_
  831.4 2.0 shard_map.380
  844.9 2.5 collective-permute-done.55
  848.7 1.7 collective-permute-start.56
  850.4 1.8 collective-permute-done.56
  852.2 2.1 collective-permute-start.57
  855.9 2.9 collective-permute-start.58
  860.0 2.6 stack_reshape.7
  872.1 3.1 multiply_subtract_fusion
  877.9 2.6 stack_reshape.6
  880.6 4.9 multiply_subtract_fusion.1
  887.6 1.8 multiply_subtract_fusion.3
  889.4 2.6 multiply_subtract_fusion.2
  (453 shorter events, 111.4 us)
Async XLA Ops:
  7.2 401.7 %all-gather.2.cloned.1.call-start = ((), (), s32[]{:S(2)}) async-start(), calls=%async_computation | async-start | bytes 7520256 | tf_op jit(solution)/shard_map/all_gather | solution.py:787
  28.0 20.5 %collective-permute-start.2 = (bf16[304,768]{1,0:T(8,128)(2,1)S(1)}, bf16[304,768]{1,0:T(8,128)(2,1)S(1)}, u32[]{:S(2)}, u32[]{:S(2)}) collective-permute-start(bf16[304,768]{1,0:T(8,128)(2,1)S(1)} %constant_dynamic-update-slice_fusion.6), channel_id=1, source_target_pairs={{0,24},{2,26},{4,28},{6,30},{8,16},{10,18},{12,20},{14,22},{16,8},... | collective-permute-start | bytes 1400840 | tf_op jit(solution)/shard_map/ppermute | solution.py:429
  33.1 58.9 %collective-permute-start.1 = (bf16[304,768]{1,0:T(8,128)(2,1)S(1)}, bf16[304,768]{1,0:T(8,128)(2,1)S(1)}, u32[]{:S(2)}, u32[]{:S(2)}) collective-permute-start(bf16[304,768]{1,0:T(8,128)(2,1)S(1)} %constant_dynamic-update-slice_fusion.6), channel_id=1, source_target_pairs={{0,16},{2,18},{4,20},{6,22},{8,24},{10,26},{12,28},{14,30},{16,0},... | collective-permute-start | bytes 1400840 | tf_op jit(solution)/shard_map/ppermute | solution.py:429
  33.1 58.9 %collective-permute-start = (bf16[304,768]{1,0:T(8,128)(2,1)S(1)}, bf16[304,768]{1,0:T(8,128)(2,1)S(1)}, u32[]{:S(2)}, u32[]{:S(2)}) collective-permute-start(bf16[304,768]{1,0:T(8,128)(2,1)S(1)} %constant_dynamic-update-slice_fusion.6), channel_id=1, source_target_pairs={{0,8},{2,10},{4,12},{6,14},{8,0},{10,2},{12,4},{14,6},{16,24},{18,... | collective-permute-start | bytes 1400840 | tf_op jit(solution)/shard_map/ppermute | solution.py:429
  93.1 65.8 %collective-permute-start.4 = (bf16[1216,768]{1,0:T(8,128)(2,1)S(1)}, bf16[1216,768]{1,0:T(8,128)(2,1)S(1)}, u32[]{:S(2)}, u32[]{:S(2)}) collective-permute-start(bf16[1216,768]{1,0:T(8,128)(2,1)S(1)} %slice_dynamic-update-slice_fusion.3.quarter), channel_id=1, source_target_pairs={{0,4},{2,6},{4,0},{6,2},{8,12},{10,14},{12,8},{14,10},{16,20},{18,... | collective-permute-start | bytes 5603336 | tf_op jit(solution)/shard_map/ppermute | solution.py:429
  94.7 67.3 %collective-permute-start.3 = (bf16[1216,768]{1,0:T(8,128)(2,1)S(1)}, bf16[1216,768]{1,0:T(8,128)(2,1)S(1)}, u32[]{:S(2)}, u32[]{:S(2)}) collective-permute-start(bf16[1216,768]{1,0:T(8,128)(2,1)S(1)} %slice_dynamic-update-slice_fusion.3.quarter), channel_id=1, source_target_pairs={{0,2},{2,0},{4,6},{6,4},{8,10},{10,8},{12,14},{14,12},{16,18},{18,... | collective-permute-start | bytes 5603336 | tf_op jit(solution)/shard_map/ppermute | solution.py:429
  163.1 16.2 %collective-permute-start.5 = (bf16[640,768]{1,0:T(8,128)(2,1)}, bf16[640,768]{1,0:T(8,128)(2,1)}, u32[]{:S(2)}, u32[]{:S(2)}) collective-permute-start(bf16[640,768]{1,0:T(8,128)(2,1)} %slice.353), channel_id=1, source_target_pairs={{0,2},{2,0},{4,6},{6,4},{8,10},{10,8},{12,14},{14,12},{16,18},{18,... | collective-permute-start | bytes 2949128 | tf_op jit(solution)/shard_map/ppermute | solution.py:429
  165.9 13.4 %collective-permute-start.6 = (bf16[576,768]{1,0:T(8,128)(2,1)}, bf16[576,768]{1,0:T(8,128)(2,1)}, u32[]{:S(2)}, u32[]{:S(2)}) collective-permute-start(bf16[576,768]{1,0:T(8,128)(2,1)} %slice.354), channel_id=1, source_target_pairs={{0,4},{2,6},{4,0},{6,2},{8,12},{10,14},{12,8},{14,10},{16,20},{18,... | collective-permute-start | bytes 2654216 | tf_op jit(solution)/shard_map/ppermute | solution.py:429
  407.4 35.2 %collective-permute-start.8 = (bf16[4,768,768]{2,1,0:T(8,128)(2,1)}, bf16[4,768,768]{2,1,0:T(8,128)(2,1)}, u32[]{:S(2)}, u32[]{:S(2)}) collective-permute-start(bf16[4,768,768]{2,1,0:T(8,128)(2,1)} %get-tuple-element.187.own), channel_id=1, source_target_pairs={{0,1},{1,0},{2,3},{3,2},{4,5},{5,4},{6,7},{7,6},{8,9},{9,8},{10,11... | collective-permute-start | bytes 14155784 | tf_op jit(solution)/shard_map/ppermute | solution.py:425
  407.5 16.7 %collective-permute-start.7 = (bf16[2,768,768]{2,1,0:T(8,128)(2,1)}, bf16[2,768,768]{2,1,0:T(8,128)(2,1)}, u32[]{:S(2)}, u32[]{:S(2)}) collective-permute-start(bf16[2,768,768]{2,1,0:T(8,128)(2,1)} %get-tuple-element.185.own), channel_id=1, source_target_pairs={{0,1},{1,0},{2,3},{3,2},{4,5},{5,4},{6,7},{7,6},{8,9},{9,8},{10,11... | collective-permute-start | bytes 7077896 | tf_op jit(solution)/shard_map/ppermute | solution.py:425
  413.7 64.6 %collective-permute-start.12 = (bf16[768,3072]{1,0:T(8,128)(2,1)}, bf16[768,3072]{1,0:T(8,128)(2,1)}, u32[]{:S(2)}, u32[]{:S(2)}) collective-permute-start(bf16[768,3072]{1,0:T(8,128)(2,1)} %slice.440.own), channel_id=1, source_target_pairs={{0,1},{1,0},{2,3},{3,2},{4,5},{5,4},{6,7},{7,6},{8,9},{9,8},{10,11... | collective-permute-start | bytes 14155784 | tf_op jit(solution)/shard_map/ppermute | solution.py:425
  420.9 36.3 %collective-permute-start.10 = (bf16[768,1536]{1,0:T(8,128)(2,1)}, bf16[768,1536]{1,0:T(8,128)(2,1)}, u32[]{:S(2)}, u32[]{:S(2)}) collective-permute-start(bf16[768,1536]{1,0:T(8,128)(2,1)} %slice.438.own), channel_id=1, source_target_pairs={{0,1},{1,0},{2,3},{3,2},{4,5},{5,4},{6,7},{7,6},{8,9},{9,8},{10,11... | collective-permute-start | bytes 7077896 | tf_op jit(solution)/shard_map/ppermute | solution.py:425
  441.8 15.4 %collective-permute-start.9 = (bf16[2,512,768]{2,1,0:T(8,128)(2,1)}, bf16[2,512,768]{2,1,0:T(8,128)(2,1)}, u32[]{:S(2)}, u32[]{:S(2)}) collective-permute-start(bf16[2,512,768]{2,1,0:T(8,128)(2,1)} %get-tuple-element.189.refs_1_), channel_id=1, source_target_pairs={{0,1},{1,0},{2,3},{3,2},{4,5},{5,4},{6,7},{7,6},{8,9},{9,8},{10,11... | collective-permute-start | bytes 4718600 | tf_op jit(solution)/shard_map/ppermute | solution.py:425
  456.0 22.2 %collective-permute-start.11 = (bf16[3,512,768]{2,1,0:T(8,128)(2,1)}, bf16[3,512,768]{2,1,0:T(8,128)(2,1)S(1)}, u32[]{:S(2)}, u32[]{:S(2)}) collective-permute-start(bf16[3,512,768]{2,1,0:T(8,128)(2,1)} %get-tuple-element.193.refs_1_), channel_id=1, source_target_pairs={{0,1},{1,0},{2,3},{3,2},{4,5},{5,4},{6,7},{7,6},{8,9},{9,8},{10,11... | collective-permute-start | bytes 7077896 | tf_op jit(solution)/shard_map/ppermute | solution.py:425
  475.0 17.9 %collective-permute-start.13 = (bf16[2,512,768]{2,1,0:T(8,128)(2,1)}, bf16[2,512,768]{2,1,0:T(8,128)(2,1)}, u32[]{:S(2)}, u32[]{:S(2)}) collective-permute-start(bf16[2,512,768]{2,1,0:T(8,128)(2,1)} %get-tuple-element.196.refs_1_), channel_id=1, source_target_pairs={{0,1},{1,0},{2,3},{3,2},{4,5},{5,4},{6,7},{7,6},{8,9},{9,8},{10,11... | collective-permute-start | bytes 4718600 | tf_op jit(solution)/shard_map/ppermute | solution.py:425
  494.7 5.9 collective-permute-start.14
  500.5 18.7 %collective-permute-start.15 = (bf16[512,768]{1,0:T(8,128)(2,1)S(1)}, bf16[512,768]{1,0:T(8,128)(2,1)S(1)}, u32[]{:S(2)}, u32[]{:S(2)}) collective-permute-start(bf16[512,768]{1,0:T(8,128)(2,1)S(1)} %get-tuple-element.200.refs_2_.branch), channel_id=1, source_target_pairs={{0,1},{1,0},{2,3},{3,2},{4,5},{5,4},{6,7},{7,6},{8,9},{9,8},{10,11... | collective-permute-start | bytes 2359304 | tf_op jit(solution)/shard_map/ppermute | solution.py:425
  519.0 25.2 %collective-permute-start.18 = (bf16[2,512,768]{2,1,0:T(8,128)(2,1)}, bf16[2,512,768]{2,1,0:T(8,128)(2,1)S(1)}, u32[]{:S(2)}, u32[]{:S(2)}) collective-permute-start(bf16[2,512,768]{2,1,0:T(8,128)(2,1)} %get-tuple-element.208), channel_id=1, source_target_pairs={{0,1},{1,0},{2,3},{3,2},{4,5},{5,4},{6,7},{7,6},{8,9},{9,8},{10,11... | collective-permute-start | bytes 4718600 | tf_op jit(solution)/shard_map/ppermute | solution.py:425
  527.1 16.0 %collective-permute-start.16 = (bf16[384,768]{1,0:T(8,128)(2,1)}, bf16[384,768]{1,0:T(8,128)(2,1)}, u32[]{:S(2)}, u32[]{:S(2)}) collective-permute-start(bf16[384,768]{1,0:T(8,128)(2,1)} %get-tuple-element.202), channel_id=1, source_target_pairs={{0,2},{2,0},{4,6},{6,4},{8,10},{10,8},{12,14},{14,12},{16,18},{18,... | collective-permute-start | bytes 1769480 | tf_op jit(solution)/shard_map/ppermute | solution.py:429
  528.5 15.7 %collective-permute-start.17 = (bf16[384,768]{1,0:T(8,128)(2,1)}, bf16[384,768]{1,0:T(8,128)(2,1)}, u32[]{:S(2)}, u32[]{:S(2)}) collective-permute-start(bf16[384,768]{1,0:T(8,128)(2,1)} %get-tuple-element.203), channel_id=1, source_target_pairs={{0,4},{2,6},{4,0},{6,2},{8,12},{10,14},{12,8},{14,10},{16,20},{18,... | collective-permute-start | bytes 1769480 | tf_op jit(solution)/shard_map/ppermute | solution.py:429
  567.8 32.1 %collective-permute-start.21 = (bf16[2,512,768]{2,1,0:T(8,128)(2,1)}, bf16[2,512,768]{2,1,0:T(8,128)(2,1)S(1)}, u32[]{:S(2)}, u32[]{:S(2)}) collective-permute-start(bf16[2,512,768]{2,1,0:T(8,128)(2,1)} %get-tuple-element.224), channel_id=1, source_target_pairs={{0,1},{1,0},{2,3},{3,2},{4,5},{5,4},{6,7},{7,6},{8,9},{9,8},{10,11... | collective-permute-start | bytes 4718600 | tf_op jit(solution)/shard_map/ppermute | solution.py:425
  577.4 22.2 %collective-permute-start.19 = (bf16[576,768]{1,0:T(8,128)(2,1)}, bf16[576,768]{1,0:T(8,128)(2,1)S(1)}, u32[]{:S(2)}, u32[]{:S(2)}) collective-permute-start(bf16[576,768]{1,0:T(8,128)(2,1)} %get-tuple-element.214), channel_id=1, source_target_pairs={{0,2},{2,0},{4,6},{6,4},{8,10},{10,8},{12,14},{14,12},{16,18},{18,... | collective-permute-start | bytes 2654216 | tf_op jit(solution)/shard_map/ppermute | solution.py:429
  577.9 22.0 %collective-permute-start.20 = (bf16[576,768]{1,0:T(8,128)(2,1)}, bf16[576,768]{1,0:T(8,128)(2,1)S(1)}, u32[]{:S(2)}, u32[]{:S(2)}) collective-permute-start(bf16[576,768]{1,0:T(8,128)(2,1)} %get-tuple-element.215), channel_id=1, source_target_pairs={{0,4},{2,6},{4,0},{6,2},{8,12},{10,14},{12,8},{14,10},{16,20},{18,... | collective-permute-start | bytes 2654216 | tf_op jit(solution)/shard_map/ppermute | solution.py:429
  599.9 18.5 %collective-permute-start.22 = (bf16[512,768]{1,0:T(8,128)(2,1)S(1)}, bf16[512,768]{1,0:T(8,128)(2,1)}, u32[]{:S(2)}, u32[]{:S(2)}) collective-permute-start(bf16[512,768]{1,0:T(8,128)(2,1)S(1)} %copy-done.28), channel_id=1, source_target_pairs={{0,1},{1,0},{2,3},{3,2},{4,5},{5,4},{6,7},{7,6},{8,9},{9,8},{10,11... | collective-permute-start | bytes 2359304 | tf_op jit(solution)/shard_map/ppermute | solution.py:425
  618.3 33.0 %collective-permute-start.28 = (bf16[2,512,768]{2,1,0:T(8,128)(2,1)}, bf16[2,512,768]{2,1,0:T(8,128)(2,1)S(1)}, u32[]{:S(2)}, u32[]{:S(2)}) collective-permute-start(bf16[2,512,768]{2,1,0:T(8,128)(2,1)} %get-tuple-element.244), channel_id=1, source_target_pairs={{0,1},{1,0},{2,3},{3,2},{4,5},{5,4},{6,7},{7,6},{8,9},{9,8},{10,11... | collective-permute-start | bytes 4718600 | tf_op jit(solution)/shard_map/ppermute | solution.py:425
  633.7 35.0 %collective-permute-start.23 = (bf16[960,768]{1,0:T(8,128)(2,1)}, bf16[960,768]{1,0:T(8,128)(2,1)}, u32[]{:S(2)}, u32[]{:S(2)}) collective-permute-start(bf16[960,768]{1,0:T(8,128)(2,1)} %get-tuple-element.235), channel_id=1, source_target_pairs={{0,2},{2,0},{4,6},{6,4},{8,10},{10,8},{12,14},{14,12},{16,18},{18,... | collective-permute-start | bytes 4423688 | tf_op jit(solution)/shard_map/ppermute | solution.py:429
  635.2 34.7 %collective-permute-start.24 = (bf16[960,768]{1,0:T(8,128)(2,1)}, bf16[960,768]{1,0:T(8,128)(2,1)}, u32[]{:S(2)}, u32[]{:S(2)}) collective-permute-start(bf16[960,768]{1,0:T(8,128)(2,1)} %get-tuple-element.236), channel_id=1, source_target_pairs={{0,4},{2,6},{4,0},{6,2},{8,12},{10,14},{12,8},{14,10},{16,20},{18,... | collective-permute-start | bytes 4423688 | tf_op jit(solution)/shard_map/ppermute | solution.py:429
  635.6 6.0 collective-permute-start.25
  636.6 14.7 %collective-permute-start.26 = (bf16[96,768]{1,0:T(8,128)(2,1)}, bf16[96,768]{1,0:T(8,128)(2,1)}, u32[]{:S(2)}, u32[]{:S(2)}) collective-permute-start(bf16[96,768]{1,0:T(8,128)(2,1)} %get-tuple-element.238), channel_id=1, source_target_pairs={{0,16},{2,18},{4,20},{6,22},{8,24},{10,26},{12,28},{14,30},{16,0},... | collective-permute-start | bytes 442376 | tf_op jit(solution)/shard_map/ppermute | solution.py:429
  641.6 9.6 %collective-permute-start.27 = (bf16[96,768]{1,0:T(8,128)(2,1)}, bf16[96,768]{1,0:T(8,128)(2,1)}, u32[]{:S(2)}, u32[]{:S(2)}) collective-permute-start(bf16[96,768]{1,0:T(8,128)(2,1)} %get-tuple-element.239), channel_id=1, source_target_pairs={{0,24},{2,26},{4,28},{6,30},{8,16},{10,18},{12,20},{14,22},{16,8},... | collective-permute-start | bytes 442376 | tf_op jit(solution)/shard_map/ppermute | solution.py:429
  692.9 41.2 %collective-permute-start.34 = (bf16[2,512,768]{2,1,0:T(8,128)(2,1)}, bf16[2,512,768]{2,1,0:T(8,128)(2,1)S(1)}, u32[]{:S(2)}, u32[]{:S(2)}) collective-permute-start(bf16[2,512,768]{2,1,0:T(8,128)(2,1)} %get-tuple-element.267), channel_id=1, source_target_pairs={{0,1},{1,0},{2,3},{3,2},{4,5},{5,4},{6,7},{7,6},{8,9},{9,8},{10,11... | collective-permute-start | bytes 4718600 | tf_op jit(solution)/shard_map/ppermute | solution.py:425
  705.1 28.6 %collective-permute-start.29 = (bf16[768,768]{1,0:T(8,128)(2,1)}, bf16[768,768]{1,0:T(8,128)(2,1)S(1)}, u32[]{:S(2)}, u32[]{:S(2)}) collective-permute-start(bf16[768,768]{1,0:T(8,128)(2,1)} %get-tuple-element.255), channel_id=1, source_target_pairs={{0,2},{2,0},{4,6},{6,4},{8,10},{10,8},{12,14},{14,12},{16,18},{18,... | collective-permute-start | bytes 3538952 | tf_op jit(solution)/shard_map/ppermute | solution.py:429
  705.8 28.3 %collective-permute-start.30 = (bf16[768,768]{1,0:T(8,128)(2,1)}, bf16[768,768]{1,0:T(8,128)(2,1)S(1)}, u32[]{:S(2)}, u32[]{:S(2)}) collective-permute-start(bf16[768,768]{1,0:T(8,128)(2,1)} %get-tuple-element.256), channel_id=1, source_target_pairs={{0,4},{2,6},{4,0},{6,2},{8,12},{10,14},{12,8},{14,10},{16,20},{18,... | collective-permute-start | bytes 3538952 | tf_op jit(solution)/shard_map/ppermute | solution.py:429
  706.2 5.9 collective-permute-start.31
  707.7 14.5 %collective-permute-start.32 = (bf16[96,768]{1,0:T(8,128)(2,1)}, bf16[96,768]{1,0:T(8,128)(2,1)S(1)}, u32[]{:S(2)}, u32[]{:S(2)}) collective-permute-start(bf16[96,768]{1,0:T(8,128)(2,1)} %get-tuple-element.258), channel_id=1, source_target_pairs={{0,16},{2,18},{4,20},{6,22},{8,24},{10,26},{12,28},{14,30},{16,0},... | collective-permute-start | bytes 442376 | tf_op jit(solution)/shard_map/ppermute | solution.py:429
  712.1 10.1 %collective-permute-start.33 = (bf16[96,768]{1,0:T(8,128)(2,1)}, bf16[96,768]{1,0:T(8,128)(2,1)S(1)}, u32[]{:S(2)}, u32[]{:S(2)}) collective-permute-start(bf16[96,768]{1,0:T(8,128)(2,1)} %get-tuple-element.259), channel_id=1, source_target_pairs={{0,24},{2,26},{4,28},{6,30},{8,16},{10,18},{12,20},{14,22},{16,8},... | collective-permute-start | bytes 442376 | tf_op jit(solution)/shard_map/ppermute | solution.py:429
  747.1 30.1 %collective-permute-start.36 = (bf16[576,768]{1,0:T(8,128)(2,1)}, bf16[576,768]{1,0:T(8,128)(2,1)S(1)}, u32[]{:S(2)}, u32[]{:S(2)}) collective-permute-start(bf16[576,768]{1,0:T(8,128)(2,1)} %get-tuple-element.284), channel_id=1, source_target_pairs={{0,2},{2,0},{4,6},{6,4},{8,10},{10,8},{12,14},{14,12},{16,18},{18,... | collective-permute-start | bytes 2654216 | tf_op jit(solution)/shard_map/ppermute | solution.py:429
  748.5 29.3 %collective-permute-start.37 = (bf16[576,768]{1,0:T(8,128)(2,1)}, bf16[576,768]{1,0:T(8,128)(2,1)}, u32[]{:S(2)}, u32[]{:S(2)}) collective-permute-start(bf16[576,768]{1,0:T(8,128)(2,1)} %get-tuple-element.285), channel_id=1, source_target_pairs={{0,4},{2,6},{4,0},{6,2},{8,12},{10,14},{12,8},{14,10},{16,20},{18,... | collective-permute-start | bytes 2654216 | tf_op jit(solution)/shard_map/ppermute | solution.py:429
  751.0 5.4 collective-permute-start.35
  751.0 15.6 %collective-permute-start.38 = (bf16[192,768]{1,0:T(8,128)(2,1)}, bf16[192,768]{1,0:T(8,128)(2,1)S(1)}, u32[]{:S(2)}, u32[]{:S(2)}) collective-permute-start(bf16[192,768]{1,0:T(8,128)(2,1)} %get-tuple-element.286), channel_id=1, source_target_pairs={{0,8},{2,10},{4,12},{6,14},{8,0},{10,2},{12,4},{14,6},{16,24},{18,... | collective-permute-start | bytes 884744 | tf_op jit(solution)/shard_map/ppermute | solution.py:429
  752.0 25.1 %collective-permute-start.39 = (bf16[192,768]{1,0:T(8,128)(2,1)}, bf16[192,768]{1,0:T(8,128)(2,1)}, u32[]{:S(2)}, u32[]{:S(2)}) collective-permute-start(bf16[192,768]{1,0:T(8,128)(2,1)} %get-tuple-element.287), channel_id=1, source_target_pairs={{0,16},{2,18},{4,20},{6,22},{8,24},{10,26},{12,28},{14,30},{16,0},... | collective-permute-start | bytes 884744 | tf_op jit(solution)/shard_map/ppermute | solution.py:429
  756.3 20.8 %collective-permute-start.40 = (bf16[192,768]{1,0:T(8,128)(2,1)}, bf16[192,768]{1,0:T(8,128)(2,1)}, u32[]{:S(2)}, u32[]{:S(2)}) collective-permute-start(bf16[192,768]{1,0:T(8,128)(2,1)} %get-tuple-element.288), channel_id=1, source_target_pairs={{0,24},{2,26},{4,28},{6,30},{8,16},{10,18},{12,20},{14,22},{16,8},... | collective-permute-start | bytes 884744 | tf_op jit(solution)/shard_map/ppermute | solution.py:429
  766.7 10.5 %collective-permute-start.41 = (f32[4,2,80,48]{2,3,1,0:T(8,128)S(1)}, f32[4,2,80,48]{2,3,1,0:T(8,128)S(1)}, u32[]{:S(2)}, u32[]{:S(2)}) collective-permute-start(f32[4,2,80,48]{2,3,1,0:T(8,128)S(1)} %dynamic-slice_bitcast_fusion), channel_id=1, source_target_pairs={{0,2},{2,0},{4,6},{6,4},{8,10},{10,8},{12,14},{14,12},{16,18},{18,... | collective-permute-start | bytes 368648 | tf_op jit(solution)/shard_map/ppermute | solution.py:429
  777.1 18.8 %collective-permute-start.63 = (f32[1,2,48,768]{3,2,1,0:T(8,128)S(1)}, f32[1,2,48,768]{3,2,1,0:T(8,128)}, u32[]{:S(2)}, u32[]{:S(2)}) collective-permute-start(f32[1,2,48,768]{3,2,1,0:T(8,128)S(1)} %copy-done.38), channel_id=1, source_target_pairs={{0,1},{1,0},{2,3},{3,2},{4,5},{5,4},{6,7},{7,6},{8,9},{9,8},{10,11... | collective-permute-start | bytes 884744 | tf_op jit(solution)/shard_map/ppermute | solution.py:425
  779.0 17.8 %collective-permute-start.47 = (f32[4,80,48]{1,2,0:T(8,128)S(1)}, f32[4,80,48]{1,2,0:T(8,128)S(1)}, u32[]{:S(2)}, u32[]{:S(2)}) collective-permute-start(f32[4,80,48]{1,2,0:T(8,128)S(1)} %dynamic-slice_bitcast_fusion.1), channel_id=1, source_target_pairs={{0,4},{2,6},{4,0},{6,2},{8,12},{10,14},{12,8},{14,10},{16,20},{18,... | collective-permute-start | bytes 184328 | tf_op jit(solution)/shard_map/ppermute | solution.py:429
  785.4 23.7 %collective-permute-start.42 = (bf16[192,768]{1,0:T(8,128)(2,1)}, bf16[192,768]{1,0:T(8,128)(2,1)S(1)}, u32[]{:S(2)}, u32[]{:S(2)}) collective-permute-start(bf16[192,768]{1,0:T(8,128)(2,1)} %get-tuple-element.298), channel_id=1, source_target_pairs={{0,2},{2,0},{4,6},{6,4},{8,10},{10,8},{12,14},{14,12},{16,18},{18,... | collective-permute-start | bytes 884744 | tf_op jit(solution)/shard_map/ppermute | solution.py:429
  786.5 22.7 %collective-permute-start.43 = (bf16[192,768]{1,0:T(8,128)(2,1)}, bf16[192,768]{1,0:T(8,128)(2,1)S(1)}, u32[]{:S(2)}, u32[]{:S(2)}) collective-permute-start(bf16[192,768]{1,0:T(8,128)(2,1)} %get-tuple-element.299), channel_id=1, source_target_pairs={{0,4},{2,6},{4,0},{6,2},{8,12},{10,14},{12,8},{14,10},{16,20},{18,... | collective-permute-start | bytes 884744 | tf_op jit(solution)/shard_map/ppermute | solution.py:429
  789.5 11.1 %collective-permute-start.44 = (bf16[96,768]{1,0:T(8,128)(2,1)}, bf16[96,768]{1,0:T(8,128)(2,1)S(1)}, u32[]{:S(2)}, u32[]{:S(2)}) collective-permute-start(bf16[96,768]{1,0:T(8,128)(2,1)} %get-tuple-element.300), channel_id=1, source_target_pairs={{0,8},{2,10},{4,12},{6,14},{8,0},{10,2},{12,4},{14,6},{16,24},{18,... | collective-permute-start | bytes 442376 | tf_op jit(solution)/shard_map/ppermute | solution.py:429
  795.9 13.2 %collective-permute-start.45 = (bf16[96,768]{1,0:T(8,128)(2,1)}, bf16[96,768]{1,0:T(8,128)(2,1)S(1)}, u32[]{:S(2)}, u32[]{:S(2)}) collective-permute-start(bf16[96,768]{1,0:T(8,128)(2,1)} %get-tuple-element.301), channel_id=1, source_target_pairs={{0,16},{2,18},{4,20},{6,22},{8,24},{10,26},{12,28},{14,30},{16,0},... | collective-permute-start | bytes 442376 | tf_op jit(solution)/shard_map/ppermute | solution.py:429
  796.8 12.3 %collective-permute-start.46 = (bf16[96,768]{1,0:T(8,128)(2,1)}, bf16[96,768]{1,0:T(8,128)(2,1)S(1)}, u32[]{:S(2)}, u32[]{:S(2)}) collective-permute-start(bf16[96,768]{1,0:T(8,128)(2,1)} %get-tuple-element.302), channel_id=1, source_target_pairs={{0,24},{2,26},{4,28},{6,30},{8,16},{10,18},{12,20},{14,22},{16,8},... | collective-permute-start | bytes 442376 | tf_op jit(solution)/shard_map/ppermute | solution.py:429
  809.5 10.5 %collective-permute-start.51 = (f32[80,48]{1,0:T(8,128)S(1)}, f32[80,48]{1,0:T(8,128)S(1)}, u32[]{:S(2)}, u32[]{:S(2)}) collective-permute-start(f32[80,48]{1,0:T(8,128)S(1)} %bitcast.160), channel_id=1, source_target_pairs={{0,8},{2,10},{4,12},{6,14},{8,0},{10,2},{12,4},{14,6},{16,24},{18,... | collective-permute-start | bytes 46088 | tf_op jit(solution)/shard_map/ppermute | solution.py:429
  812.1 12.2 %collective-permute-start.52 = (f32[80,48]{1,0:T(8,128)S(1)}, f32[80,48]{1,0:T(8,128)S(1)}, u32[]{:S(2)}, u32[]{:S(2)}) collective-permute-start(f32[80,48]{1,0:T(8,128)S(1)} %bitcast.159), channel_id=1, source_target_pairs={{0,16},{2,18},{4,20},{6,22},{8,24},{10,26},{12,28},{14,30},{16,0},... | collective-permute-start | bytes 46088 | tf_op jit(solution)/shard_map/ppermute | solution.py:429
  812.9 11.5 %collective-permute-start.53 = (f32[80,48]{1,0:T(8,128)S(1)}, f32[80,48]{1,0:T(8,128)}, u32[]{:S(2)}, u32[]{:S(2)}) collective-permute-start(f32[80,48]{1,0:T(8,128)S(1)} %bitcast.158), channel_id=1, source_target_pairs={{0,24},{2,26},{4,28},{6,30},{8,16},{10,18},{12,20},{14,22},{16,8},... | collective-permute-start | bytes 46088 | tf_op jit(solution)/shard_map/ppermute | solution.py:429
  817.2 7.8 collective-permute-start.48
  818.3 12.4 %collective-permute-start.49 = (bf16[96,768]{1,0:T(8,128)(2,1)}, bf16[96,768]{1,0:T(8,128)(2,1)S(1)}, u32[]{:S(2)}, u32[]{:S(2)}) collective-permute-start(bf16[96,768]{1,0:T(8,128)(2,1)} %get-tuple-element.312), channel_id=1, source_target_pairs={{0,16},{2,18},{4,20},{6,22},{8,24},{10,26},{12,28},{14,30},{16,0},... | collective-permute-start | bytes 442376 | tf_op jit(solution)/shard_map/ppermute | solution.py:429
  820.0 10.7 %collective-permute-start.50 = (bf16[96,768]{1,0:T(8,128)(2,1)}, bf16[96,768]{1,0:T(8,128)(2,1)S(1)}, u32[]{:S(2)}, u32[]{:S(2)}) collective-permute-start(bf16[96,768]{1,0:T(8,128)(2,1)} %get-tuple-element.313), channel_id=1, source_target_pairs={{0,24},{2,26},{4,28},{6,30},{8,16},{10,18},{12,20},{14,22},{16,8},... | collective-permute-start | bytes 442376 | tf_op jit(solution)/shard_map/ppermute | solution.py:429
  824.3 20.6 %collective-permute-start.62 = (f32[1,2,48,768]{3,2,1,0:T(8,128)S(1)}, f32[1,2,48,768]{3,2,1,0:T(8,128)S(1)}, u32[]{:S(2)}, u32[]{:S(2)}) collective-permute-start(f32[1,2,48,768]{3,2,1,0:T(8,128)S(1)} %copy-done.36), channel_id=1, source_target_pairs={{0,1},{1,0},{2,3},{3,2},{4,5},{5,4},{6,7},{7,6},{8,9},{9,8},{10,11... | collective-permute-start | bytes 884744 | tf_op jit(solution)/shard_map/ppermute | solution.py:425
  843.8 3.5 collective-permute-start.55
  848.7 3.5 collective-permute-start.56
  852.2 3.6 collective-permute-start.57
  855.9 7.3 collective-permute-start.58
  862.6 6.6 collective-permute-start.60
  862.6 12.6 %collective-permute-start.61 = (f32[1,2,48,768]{3,2,1,0:T(8,128)}, f32[1,2,48,768]{3,2,1,0:T(8,128)S(1)}, u32[]{:S(2)}, u32[]{:S(2)}) collective-permute-start(f32[1,2,48,768]{3,2,1,0:T(8,128)} %get-tuple-element.328), channel_id=1, source_target_pairs={{0,1},{1,0},{2,3},{3,2},{4,5},{5,4},{6,7},{7,6},{8,9},{9,8},{10,11... | collective-permute-start | bytes 884744 | tf_op jit(solution)/shard_map/ppermute | solution.py:425
  863.1 22.3 %collective-permute-start.59 = (f32[1,2,48,768]{3,2,1,0:T(8,128)}, f32[1,2,48,768]{3,2,1,0:T(8,128)}, u32[]{:S(2)}, u32[]{:S(2)}) collective-permute-start(f32[1,2,48,768]{3,2,1,0:T(8,128)} %get-tuple-element.326), channel_id=1, source_target_pairs={{0,1},{1,0},{2,3},{3,2},{4,5},{5,4},{6,7},{7,6},{8,9},{9,8},{10,11... | collective-permute-start | bytes 884744 | tf_op jit(solution)/shard_map/ppermute | solution.py:425
  (93 other events, 975.5 us)
Sparse Core Ops, SparseCore 0:
  25.7 150.5 all-gather.1

commit v5 on v4

--- a/solution.py
+++ b/solution.py
@@ -442,68 +442,6 @@
 
 X, Y = 1, 2
 Z = (4, 8, 12)
-
-
-def place_kernel(parts, place_of, quarter, from_x, from_y, far_a, far_b, mixer, hidden, small, sems):
-    x, y, z = place_of[1], place_of[2], place_of[3]
-    rows = (parts[0] - parts[2]) // 3
-    for xor_z in range(4):
-        for xor_y in range(2):
-            for xor_x in range(2):
-                index = (z ^ xor_z) * 4 + (y ^ xor_y) * 2 + (x ^ xor_x)
-                for h in range(2):
-                    at = xor_z * parts[h]
-                    if xor_x and xor_y:
-                        source = (far_a, far_b)[h]
-                    else:
-                        source = from_x if xor_x else from_y if xor_y else quarter
-                        at += h * 4 * parts[0]
-                    for j in range(3):
-                        target = mixer.at[h] if j == 0 else hidden.at[2 * (j - 1) + h]
-                        pltpu.make_async_copy(
-                            source.at[pl.ds(at + j * rows, rows)],
-                            target.at[pl.ds(pl.multiple_of(index * rows, 16), rows)],
-                            sems.at[h * 3 + j],
-                        ).start()
-                    if h == 0:
-                        pltpu.make_async_copy(
-                            source.at[pl.ds(at + 3 * rows, parts[2])],
-                            small.at[pl.ds(pl.multiple_of(index * parts[2], 16), parts[2])],
-                            sems.at[6],
-                        ).start()
-    for h in range(2):
-        for j in range(3):
-            target = mixer.at[h] if j == 0 else hidden.at[2 * (j - 1) + h]
-            pltpu.make_async_copy(target, target, sems.at[h * 3 + j]).wait()
-    pltpu.make_async_copy(small, small, sems.at[6]).wait()
-
-
-def gather_blocks(place, shard_a, shard_b, small, size):
-    rows, width = shard_a.shape[0] // 3, shard_a.shape[1]
-    shard_a = jnp.concatenate([shard_a, small], 0)
-    parts = (shard_a.shape[0], shard_b.shape[0], small.shape[0])
-    shard = jnp.concatenate([shard_a, shard_b], 0)
-    got = [across(shard, mask, size) for mask in Z]
-    (got,) = tie(got)
-    got = [shard] + got
-    quarter = jnp.concatenate([g[: parts[0]] for g in got] + [g[parts[0] :] for g in got], 0)
-    from_x, from_y = tie(across(quarter, X, size), across(quarter, Y, size))
-    cut = 4 * parts[0]
-    far_a, far_b = tie(across(from_y[:cut], X, size), across(from_x[cut:], Y, size))
-    return call(
-        functools.partial(place_kernel, parts),
-        place,
-        [
-            ((2, width, width), LOW),
-            ((4, width, width), LOW),
-            ((size * parts[2], width), LOW),
-        ],
-        [],
-        [quarter, from_x, from_y, far_a, far_b],
-        [pltpu.SemaphoreType.DMA((7,))],
-        0,
-        outs_any=3,
-    )
 
 
 def round_kernel(jobs, n_ins, counts, *refs):
@@ -590,7 +528,7 @@
         self.shares, self.squares = [], []
         self.flying = []
 
-    def step(self, chunk):
+    def step(self, chunk, *ties):
         rows, width = self.rows, self.width
         new, once, twice, done = counts = (len(chunk),) + self.counts[:3]
         arrays, jobs = [], []
@@ -639,8 +577,14 @@
             [pltpu.VMEM((16 * rows, width), FULL)] if new else [],
             4 * new * length * width * width,
         )
-        got = list(got)
         self.flying, self.kept, self.counts = [], [None] * 3, counts
+        if done:
+            *got, share, square = got
+            self.squares.append(square)
+        if not (new or once or twice):
+            self.shares.append((share, swap_cores(share)))
+            return ties
+        got, ties = tie(list(got), ties)
         if new or once:
             self.flying += [across(got.pop(0), X, 16), across(got.pop(0), Y, 16)]
         if new:
@@ -651,11 +595,16 @@
             self.kept[2] = got.pop(0)
             self.flying += [across(got.pop(0), mask, 16) for mask in Z]
         if done:
-            self.shares.append(got[0])
-            self.squares.append(got[1])
+            self.shares.append((share, swap_cores(share)))
+        return ties
 
     def finish(self, *ties):
+        if self.counts[3]:
+            share, other = self.shares[-1]
+            self.flying.append(other)
         flying, ties = tie(self.flying, ties)
+        if self.counts[3]:
+            self.shares[-1] = (share, flying.pop())
         self.came = self.came_z = None
         if self.counts[0] or self.counts[1]:
             self.came, flying = flying[:2], flying[2:]
@@ -671,7 +620,7 @@
     def __init__(self):
         self.shares, self.squares = [], []
 
-    def step(self, chunk):
+    def step(self, chunk, *ties):
         def factor(spec):
             array, index, low, high = spec
             array = array if index is None else array[index]
@@ -684,8 +633,9 @@
             )
 
         share = jnp.stack([jnp.stack([summed(tile) for tile in pair]) for pair in chunk])
-        self.shares.append(share)
+        self.shares.append((share, swap_cores(share)))
         self.squares.append(jnp.sum(share * share, (0, 1, 2))[None])
+        return ties
 
     def finish(self, *ties):
         return ties
@@ -773,27 +723,18 @@
     small = jnp.concatenate(
         [codon_table.astype(LOW), norm_params.astype(LOW).reshape(norms, rows)], 0
     )
-    mixers, hiddens = [None] * layers, [None] * layers
-    plain = list(range(1, layers)) if fast else list(range(layers))
-    sides = [jnp.concatenate(tiles_of(l), 1) for l in plain]
-    if fast:
-        tiles = tiles_of(0)
-        flat = small.reshape(-1)
-        flat = jnp.pad(flat, (0, -flat.shape[0] % (16 * width))).reshape(-1, width)
-        shard_a = jnp.concatenate(tiles[0::2], 0)
-        shard_b = jnp.concatenate(tiles[1::2], 0)
-        sides, shard_a = tie(sides, shard_a)
-    for l, side in zip(plain, sides):
-        own = lax.all_gather(side, "fsdp", axis=0, tiled=True)
-        mixers[l], hiddens[l] = own[:, : 2 * width], own[:, 2 * width :]
-    if fast:
-        mixers[0], hiddens[0], blocks = gather_blocks(place, shard_a, shard_b, flat, fsdp)
-        blocks = blocks.reshape(fsdp, -1)[:, : small.size].reshape(fsdp, V + norms, rows)
-        small = blocks.transpose(1, 0, 2).reshape(V + norms, width)
-    else:
-        small = lax.all_gather(small, "fsdp", axis=1, tiled=True)
-    mixers = [(own, swap_cores(own)) for own in mixers]
-    hiddens = [(own, swap_cores(own)) for own in hiddens]
+    small = jnp.pad(small.T, ((0, 0), (0, -small.shape[0] % 128)))
+    sides = jnp.concatenate([small] + sum([tiles_of(l) for l in range(layers)], []), 1)
+    sides = lax.all_gather(sides, "fsdp", axis=0, tiled=True)
+    cut = small.shape[1]
+    small = sides[:, : V + norms].T
+    mixers, hiddens = [], []
+    for l in range(layers):
+        own = sides[:, cut : cut + 2 * width]
+        mixers.append((own, swap_cores(own)))
+        own = sides[:, cut + 2 * width : cut + 6 * width]
+        hiddens.append((own, swap_cores(own)))
+        cut += 6 * width
     table_low = small[:V]
     gains = small[V:].astype(FULL).reshape(-1, 2, width)
 
@@ -856,12 +797,13 @@
                 for s in range(2)
             ]
         )
-        rounds.step(chunk)
+        grad, branch = rounds.step(chunk, grad, branch)
         grad_middle, gains_mid, up_own, up_other = hidden_back(
             place, grad, branch, middle, hidden, hiddens[l], gain[1]
         )
-        grad_middle, up_own, up_came = rounds.finish(grad_middle, up_own, swap_cores(up_other))
-        rounds.step(
+        grad_middle, up_own, up_other = rounds.finish(grad_middle, up_own, up_other)
+        up_came = swap_cores(up_other)
+        (grad_middle,) = rounds.step(
             [
                 [
                     tile(
@@ -869,16 +811,16 @@
                     )
                     for s in range(2)
                 ]
-            ]
+            ],
+            grad_middle,
         )
         grad, branch, gains_in, mix_own, mix_other = attention_back(
             place, grad_middle, resid, mixers[l], gain[0], cosine, sine, segments,
             query, keys, values, lse,
         )
         grad_norms = [gains_in, gains_mid] + grad_norms
-        grad, branch, mix_own, mix_came = rounds.finish(
-            grad, branch, mix_own, swap_cores(mix_other)
-        )
+        grad, branch, mix_own, mix_other = rounds.finish(grad, branch, mix_own, mix_other)
+        mix_came = swap_cores(mix_other)
         products = lambda i, a, b: [
             ((pack, i, None, None), (mix_own, 1, a, b)),
             ((pack_came, i, None, None), (mix_came, 1, a, b)),
@@ -918,8 +860,7 @@
     loss_sum, count, square_total = totals[0, 0], totals[0, 1], totals[0, 2]
 
     both = []
-    for share in rounds.shares:
-        other = swap_cores(share)
+    for share, other in rounds.shares:
         first = core == 0
         both.append((jnp.where(first, share, other), jnp.where(first, other, share)))
     share_in, share_out, share_up, share_down = ([None] * layers for _ in range(4))

time: 911 us -> 664 us (0.73)
  Pallas kernels: 437 us -> 207 us
  starting transfers between devices: 81.1 us -> 54.1 us
    pallas_call x17 -> x16, Pallas kernels: 437 us -> 207 us  [call(): pl.pallas_call(kernel, out_shape=[jax.ShapeDtypeStruct(s, t) for s, t in...]
    ppermute x43 -> x36, waiting for transfers between devices: 245 us -> 57 us  [across(): return lax.ppermute(value, 'fsdp', [(i, i ^ mask) for i in range(size)])]
    all_gather x1, waiting for transfers between devices: 0.01 us -> 172 us  [body(): sides = lax.all_gather(sides, 'fsdp', axis=0, tiled=True)]
    ppermute x43 -> x36, starting transfers between devices: 77.5 us -> 50.3 us  [across(): return lax.ppermute(value, 'fsdp', [(i, i ^ mask) for i in range(size)])]
    ppermute x21, waiting for transfers between devices: 1.11 us -> 14.7 us  [swap_cores(): return lax.ppermute(value, 'dp', [(0, 1), (1, 0)])]
    unnamed x214 -> x174, local copies, waits for them, and re-layouts: 23 us -> 25.3 us
  transfers between devices with their start and end apart: 65 -> 58, of which waited for: 27 -> 15; matrix products, arithmetic and copies ran while one was open for 8% -> 11% of each run, Pallas kernels for 42% -> 24%
where the time goes in v5:
time: 664 us; the launch traced here: 653 us
  waiting for transfers between devices  243 us (37%)
  Pallas kernels  207 us (31%)
  local copies, waits for them, and re-layouts  75.6 us (11%)
  starting transfers between devices  54.1 us (8%)
  other arithmetic  43.9 us (7%)
  between operations  22.1 us (3%)
  matrix products  6.76 us (1%)
    pallas_call x16, Pallas kernels, call(): pl.pallas_call(kernel, out_shape=[jax.ShapeDtypeStruct(s, t) for s, t in...  207 us
    all_gather x1, waiting for transfers between devices, body(): sides = lax.all_gather(sides, 'fsdp', axis=0, tiled=True)  172 us
    ppermute x36, waiting for transfers between devices, across(): return lax.ppermute(value, 'fsdp', [(i, i ^ mask) for i in range(size)])  57 us
    ppermute x36, starting transfers between devices, across(): return lax.ppermute(value, 'fsdp', [(i, i ^ mask) for i in range(size)])  50.3 us
    unnamed x174, local copies, waits for them, and re-layouts  25.3 us
    sub x6, other arithmetic, adam_step(): return (master - rate * update, first, second)  16 us
    ppermute x21, waiting for transfers between devices, swap_cores(): return lax.ppermute(value, 'dp', [(0, 1), (1, 0)])  14.7 us
  transfers between devices with their start and end apart: 58, of which 15 were waited for; matrix products, arithmetic and copies ran while one was open for 11% of the time, Pallas kernels for 24%

profile of v5, /device:TPU:0, one launch (start us, length us, event | category | flops | bytes accessed | tf_op | source)
XLA Modules:
  0.0 653.3 jit_solution(12233331277818927783)
XLA Ops:
  12.9 2.1 reshape.152
  17.0 2.1 reshape.151
  24.6 171.6 %all-gather.2.cloned.1.call-done = bf16[768,9344]{1,0:T(8,128)(2,1)} async-done(((bf16[48,9344]{1,0:T(8,128)(2,1)}), bf16[768,9344]{1,0:T(8,128)(2,1)}) %all-gather.2.cloned.1.call-update) | async-done | bytes 14352400 | tf_op jit(solution)/shard_map/all_gather | solution.py:728
  196.2 8.2 %fusion.36 = (bf16[768,3072]{1,0:T(8,128)(2,1)}, bf16[768,3072]{1,0:T(8,128)(2,1)}) fusion(bf16[768,9344]{1,0:T(8,128)(2,1)} %all-gather.2.cloned.1.call-done), kind=kLoop, calls=%fused_computation.161 | loop fusion | bytes 18874368 | tf_op jit(solution)/shard_map/slice | solution.py:735
  204.5 4.8 fusion.37
  217.4 1.6 fusion.10.resid
  219.1 17.8 %shard_map.364 = (f32[512,768]{1,0:T(8,128)}, bf16[512,768]{1,0:T(8,128)(2,1)}, bf16[512,768]{1,0:T(8,128)(2,1)}, bf16[512,768]{1,0:T(8,128)(2,1)}, f32[512,128]{1,0:T(8,128)}, /*index=5*/bf16[2,512,768]{2,1,0:T(8,128)(2,1)}) custom-call(s32[4]{0:T(128)} %pad_add_fusion.place_of.refs_0_, f32[512,768]{1,0:T(8,128)} %fusion.10.resid, s32[512,1]{1,0:T(8,128)} %copy.84.seg_col, ...), custom_call_target="tpu_custom_call" | custom-call | flops 3221225472 | bytes 6825984 | tf_op jit(solution)/shard_map/pallas_call | solution.py:77
  237.7 13.4 %shard_map.365 = (f32[512,768]{1,0:T(8,128)}, bf16[2,512,768]{2,1,0:T(8,128)(2,1)}, bf16[3,512,768]{2,1,0:T(8,128)(2,1)}, f32[4,512,768]{2,1,0:T(8,128)}) custom-call(s32[4]{0:T(128)} %pad_add_fusion.place_of.refs_0_, f32[512,768]{1,0:T(8,128)} %get-tuple-element.216.middle, f32[2,768]{1,0:T(2,128)} %copy.86.gains, ...), custom_call_target="tpu_custom_call" | custom-call | flops 4831838208 | bytes 11016192 | tf_op jit(solution)/shard_map/pallas_call | solution.py:77
  252.4 18.1 %shard_map.366 = (f32[512,768]{1,0:T(8,128)}, bf16[512,768]{1,0:T(8,128)(2,1)}, bf16[512,768]{1,0:T(8,128)(2,1)}, bf16[512,768]{1,0:T(8,128)(2,1)}, f32[512,128]{1,0:T(8,128)}, /*index=5*/bf16[2,512,768]{2,1,0:T(8,128)(2,1)}) custom-call(s32[4]{0:T(128)} %pad_add_fusion.place_of.refs_0_, f32[512,768]{1,0:T(8,128)} %get-tuple-element.219.resid, ...), custom_call_target="tpu_custom_call" | custom-call | flops 3221225472 | bytes 6825984 | tf_op jit(solution)/shard_map/pallas_call | solution.py:77
  271.9 13.2 %shard_map.367 = (f32[512,768]{1,0:T(8,128)}, bf16[2,512,768]{2,1,0:T(8,128)(2,1)}, bf16[3,512,768]{2,1,0:T(8,128)(2,1)}, f32[4,512,768]{2,1,0:T(8,128)}) custom-call(s32[4]{0:T(128)} %pad_add_fusion.place_of.refs_0_, f32[512,768]{1,0:T(8,128)} %get-tuple-element.222.middle, f32[2,768]{1,0:T(2,128)} %copy.89.gains, ...), custom_call_target="tpu_custom_call" | custom-call | flops 4831838208 | bytes 11016192 | tf_op jit(solution)/shard_map/pallas_call | solution.py:77
  285.2 1.7 reduce_sum.144
  291.1 1.7 fusion.35
  292.9 2.2 collective-permute-done.8.refs_4_
  296.0 7.3 %shard_map.368 = (bf16[384,768]{1,0:T(8,128)(2,1)}, bf16[384,768]{1,0:T(8,128)(2,1)}, f32[1,2,384,768]{3,2,1,0:T(8,128)}) custom-call(s32[4]{0:T(128)} %pad_add_fusion.place_of.refs_0_, bf16[2,512,768]{2,1,0:T(8,128)(2,1)} %get-tuple-element.227.refs_1_, bf16[512,768]{1,0:T(8,128)(2,1)} %copy-done.5, bf16[3,512,768]{2,1,0:T(8,128)(2,1)} %copy-done.10, ...), custom_call_target="tpu_custom_call" | custom-call | flops 2415919104 | bytes 5505024 | tf_op jit(solution)/shard_map/pallas_call | solution.py:77
  303.3 1.4 collective-permute-start.9
  305.3 17.2 %shard_map.369 = (f32[512,768]{1,0:T(8,128)}, f32[2,768]{1,0:T(2,128)}, bf16[2,512,768]{2,1,0:T(8,128)(2,1)}, bf16[2,512,768]{2,1,0:T(8,128)(2,1)}) custom-call(s32[4]{0:T(128)} %pad_add_fusion.place_of.refs_0_, f32[512,768]{1,0:T(8,128)} %get-tuple-element.236.grad, bf16[512,768]{1,0:T(8,128)(2,1)} %copy-done.5, f32[512,768]{1,0:T(8,128)} %get-tuple-element.222.middle, ...), custom_call_target="tpu_custom_call" | custom-call | flops 4831838208 | bytes 19666944 | tf_op jit(solution)/shard_map/pallas_call | solution.py:77
  322.6 3.6 collective-permute-done.11.refs_4_
  327.5 9.6 %shard_map.370 = (bf16[576,768]{1,0:T(8,128)(2,1)}, bf16[576,768]{1,0:T(8,128)(2,1)}, f32[1,2,384,768]{3,2,1,0:T(8,128)}, f32[1,2,192,768]{3,2,1,0:T(8,128)}) custom-call(s32[4]{0:T(128)} %pad_add_fusion.place_of.refs_0_, bf16[3,512,768]{2,1,0:T(8,128)(2,1)} %get-tuple-element.226.refs_1_, bf16[2,512,768]{2,1,0:T(8,128)(2,1)} %get-tuple-element.242.refs_2_, ...), custom_call_target="tpu_custom_call" | custom-call | flops 2415919104 | bytes 11403264 | tf_op jit(solution)/shard_map/pallas_call | solution.py:77
  337.1 1.5 collective-permute-start.12
  339.8 22.6 %shard_map.371 = (f32[512,768]{1,0:T(8,128)}, bf16[512,768]{1,0:T(8,128)(2,1)}, f32[2,768]{1,0:T(2,128)}, bf16[2,512,768]{2,1,0:T(8,128)(2,1)}, bf16[2,512,768]{2,1,0:T(8,128)(2,1)}) custom-call(s32[4]{0:T(128)} %pad_add_fusion.place_of.refs_0_, f32[512,768]{1,0:T(8,128)} %get-tuple-element.254.grad_middle, f32[512,768]{1,0:T(8,128)} %get-tuple-element.219.resid, ...), custom_call_target="tpu_custom_call" | custom-call | flops 4429185024 | bytes 10782720 | tf_op jit(solution)/shard_map/pallas_call | solution.py:77
  363.1 4.2 collective-permute-done.15.refs_8_
  368.8 15.3 %shard_map.372 = (bf16[960,768]{1,0:T(8,128)(2,1)}, bf16[960,768]{1,0:T(8,128)(2,1)}, f32[2,2,384,768]{3,2,1,0:T(8,128)}, f32[1,2,192,768]{3,2,1,0:T(8,128)}, f3...) custom-call(s32[4]{0:T(128)} %pad_add_fusion.place_of.refs_0_, ...), custom_call_target="tpu_custom_call" | custom-call | flops 4831838208 | bytes 17104896 | tf_op jit(solution)/shard_map/pallas_call | solution.py:77
  384.1 1.5 collective-permute-start.16
  386.1 2.0 collective-permute-start.19
  388.1 2.4 collective-permute-start.20
  390.5 17.6 %shard_map.373 = (f32[512,768]{1,0:T(8,128)}, f32[2,768]{1,0:T(2,128)}, bf16[2,512,768]{2,1,0:T(8,128)(2,1)}, bf16[2,512,768]{2,1,0:T(8,128)(2,1)}) custom-call(s32[4]{0:T(128)} %pad_add_fusion.place_of.refs_0_, f32[512,768]{1,0:T(8,128)} %get-tuple-element.287.grad, bf16[512,768]{1,0:T(8,128)(2,1)} %get-tuple-element.288.refs_6_.branch, ...), custom_call_target="tpu_custom_call" | custom-call | flops 4831838208 | bytes 19666944 | tf_op jit(solution)/shard_map/pallas_call | solution.py:77
  408.2 10.4 %collective-permute-done.16.refs_7_ = bf16[960,768]{1,0:T(8,128)(2,1)S(1)} collective-permute-done((bf16[960,768]{1,0:T(8,128)(2,1)}, bf16[960,768]{1,0:T(8,128)(2,1)S(1)}, u32[]{:S(2)}, u32[]{:S(2)}) %collective-permute-start.16) | collective-permute-done | bytes 1474592 | tf_op jit(solution)/shard_map/ppermute | solution.py:429
  419.8 3.6 collective-permute-done.21.refs_4_
  424.6 12.1 %shard_map.374 = (bf16[768,768]{1,0:T(8,128)(2,1)}, bf16[768,768]{1,0:T(8,128)(2,1)}, f32[1,2,384,768]{3,2,1,0:T(8,128)}, f32[2,2,192,768]{3,2,1,0:T(8,128)}, f3...) custom-call(s32[4]{0:T(128)} %pad_add_fusion.place_of.refs_0_, ...), custom_call_target="tpu_custom_call" | custom-call | flops 2415919104 | bytes 17448960 | tf_op jit(solution)/shard_map/pallas_call | solution.py:77
  437.4 1.5 collective-permute-start.23
  440.6 2.0 collective-permute-start.25
  442.6 2.4 collective-permute-start.26
  446.0 22.8 %shard_map.375 = (f32[512,768]{1,0:T(8,128)}, bf16[512,768]{1,0:T(8,128)(2,1)}, f32[2,768]{1,0:T(2,128)}, bf16[2,512,768]{2,1,0:T(8,128)(2,1)}, bf16[2,512,768]{2,1,0:T(8,128)(2,1)}) custom-call(s32[4]{0:T(128)} %pad_add_fusion.place_of.refs_0_, f32[512,768]{1,0:T(8,128)} %get-tuple-element.318.grad_middle, f32[512,768]{1,0:T(8,128)} %fusion.10.resid, ...), custom_call_target="tpu_custom_call" | custom-call | flops 4429185024 | bytes 10782720 | tf_op jit(solution)/shard_map/pallas_call | solution.py:77
  470.5 1.4 copy.109
  471.9 1.4 copy.106
  476.2 1.9 fusion.28
  479.3 1.6 convolution_add_fusion
  480.9 3.4 concatenate.62
  485.5 11.2 %shard_map.376 = (bf16[576,768]{1,0:T(8,128)(2,1)}, bf16[576,768]{1,0:T(8,128)(2,1)}, f32[1,2,384,768]{3,2,1,0:T(8,128)}, f32[1,2,192,768]{3,2,1,0:T(8,128)}, f3...) custom-call(s32[4]{0:T(128)} %pad_add_fusion.place_of.refs_0_, ...), custom_call_target="tpu_custom_call" | custom-call | flops 2415919104 | bytes 14106624 | tf_op jit(solution)/shard_map/pallas_call | solution.py:77
  501.7 21.4 %collective-permute-done.36 = f32[4,2,80,48]{2,3,1,0:T(8,128)S(1)} collective-permute-done((f32[4,2,80,48]{2,3,1,0:T(8,128)S(1)}, f32[4,2,80,48]{2,3,1,0:T(8,128)S(1)}, u32[]{:S(2)}, u32[]{:S(2)}) %collective-permute-start.36) | collective-permute-done | bytes 122912 | tf_op jit(solution)/shard_map/ppermute | solution.py:429
  524.9 9.0 %collective-permute-done.34.refs_8_ = bf16[192,768]{1,0:T(8,128)(2,1)} collective-permute-done((bf16[192,768]{1,0:T(8,128)(2,1)}, bf16[192,768]{1,0:T(8,128)(2,1)}, u32[]{:S(2)}, u32[]{:S(2)}) %collective-permute-start.34) | collective-permute-done | bytes 294944 | tf_op jit(solution)/shard_map/ppermute | solution.py:429
  534.9 4.6 shard_map.377
  540.7 4.1 collective-permute-start.39
  545.8 1.5 collective-permute-start.37
  551.5 1.8 collective-permute-start.41
  554.5 2.9 stack_reshape.7
  557.4 6.9 %collective-permute-done.40.refs_6_ = bf16[96,768]{1,0:T(8,128)(2,1)} collective-permute-done((bf16[96,768]{1,0:T(8,128)(2,1)}, bf16[96,768]{1,0:T(8,128)(2,1)}, u32[]{:S(2)}, u32[]{:S(2)}) %collective-permute-start.40) | collective-permute-done | bytes 147488 | tf_op jit(solution)/shard_map/ppermute | solution.py:429
  564.3 2.6 shard_map.378
  568.1 3.7 collective-permute-start.48
  572.4 1.9 collective-permute-start.44
  580.2 2.0 collective-permute-start.46
  583.1 1.9 collective-permute-start.50
  585.7 3.5 collective-permute-done.50
  590.0 2.0 shard_map.379
  601.6 1.5 collective-permute-start.52
  608.0 2.1 collective-permute-done.53
  610.1 4.1 collective-permute-start.54
  615.9 2.3 collective-permute-start.55
  619.4 2.6 stack_reshape.6
  624.1 1.5 multiply_subtract_fusion.4
  625.6 5.4 multiply_subtract_fusion
  631.1 3.1 multiply_subtract_fusion.1
  639.7 1.7 multiply_subtract_fusion.3
  641.5 3.6 multiply_subtract_fusion.2
  (371 shorter events, 92.8 us)
Async XLA Ops:
  7.2 189.0 %all-gather.2.cloned.1.call-start = ((), (), s32[]{:S(2)}) async-start(), calls=%async_computation | async-start | bytes 15249408 | tf_op jit(solution)/shard_map/all_gather | solution.py:728
  204.5 33.2 %collective-permute-start.1 = (bf16[768,3072]{1,0:T(8,128)(2,1)}, bf16[768,3072]{1,0:T(8,128)(2,1)}, u32[]{:S(2)}, u32[]{:S(2)}) collective-permute-start(bf16[768,3072]{1,0:T(8,128)(2,1)} %get-tuple-element.466.own), channel_id=1, source_target_pairs={{0,1},{1,0},{2,3},{3,2},{4,5},{5,4},{6,7},{7,6},{8,9},{9,8},{10,11... | collective-permute-start | bytes 14155784 | tf_op jit(solution)/shard_map/ppermute | solution.py:425
  209.3 9.7 %collective-permute-start = (bf16[768,1536]{1,0:T(8,128)(2,1)}, bf16[768,1536]{1,0:T(8,128)(2,1)}, u32[]{:S(2)}, u32[]{:S(2)}) collective-permute-start(bf16[768,1536]{1,0:T(8,128)(2,1)} %get-tuple-element.468.own), channel_id=1, source_target_pairs={{0,1},{1,0},{2,3},{3,2},{4,5},{5,4},{6,7},{7,6},{8,9},{9,8},{10,11... | collective-permute-start | bytes 7077896 | tf_op jit(solution)/shard_map/ppermute | solution.py:425
  210.8 61.0 %collective-permute-start.5 = (bf16[768,3072]{1,0:T(8,128)(2,1)}, bf16[768,3072]{1,0:T(8,128)(2,1)}, u32[]{:S(2)}, u32[]{:S(2)}) collective-permute-start(bf16[768,3072]{1,0:T(8,128)(2,1)} %get-tuple-element.465.own), channel_id=1, source_target_pairs={{0,1},{1,0},{2,3},{3,2},{4,5},{5,4},{6,7},{7,6},{8,9},{9,8},{10,11... | collective-permute-start | bytes 14155784 | tf_op jit(solution)/shard_map/ppermute | solution.py:425
  213.7 76.1 %copy-start.57 = (f32[512]{0:T(512)}, f32[512]{0:T(512)S(1)}, u32[]{:S(2)}) copy-start(f32[512]{0:T(512)S(1)} %get-tuple-element.533) | copy-start | bytes 6148
  213.7 38.7 %collective-permute-start.3 = (bf16[768,1536]{1,0:T(8,128)(2,1)}, bf16[768,1536]{1,0:T(8,128)(2,1)}, u32[]{:S(2)}, u32[]{:S(2)}) collective-permute-start(bf16[768,1536]{1,0:T(8,128)(2,1)} %get-tuple-element.467.own), channel_id=1, source_target_pairs={{0,1},{1,0},{2,3},{3,2},{4,5},{5,4},{6,7},{7,6},{8,9},{9,8},{10,11... | collective-permute-start | bytes 7077896 | tf_op jit(solution)/shard_map/ppermute | solution.py:425
  236.8 15.5 %collective-permute-start.2 = (bf16[2,512,768]{2,1,0:T(8,128)(2,1)}, bf16[2,512,768]{2,1,0:T(8,128)(2,1)S(1)}, u32[]{:S(2)}, u32[]{:S(2)}) collective-permute-start(bf16[2,512,768]{2,1,0:T(8,128)(2,1)} %get-tuple-element.218.refs_1_), channel_id=1, source_target_pairs={{0,1},{1,0},{2,3},{3,2},{4,5},{5,4},{6,7},{7,6},{8,9},{9,8},{10,11... | collective-permute-start | bytes 4718600 | tf_op jit(solution)/shard_map/ppermute | solution.py:425
  251.1 20.8 %collective-permute-start.4 = (bf16[3,512,768]{2,1,0:T(8,128)(2,1)}, bf16[3,512,768]{2,1,0:T(8,128)(2,1)}, u32[]{:S(2)}, u32[]{:S(2)}) collective-permute-start(bf16[3,512,768]{2,1,0:T(8,128)(2,1)} %get-tuple-element.221.refs_1_), channel_id=1, source_target_pairs={{0,1},{1,0},{2,3},{3,2},{4,5},{5,4},{6,7},{7,6},{8,9},{9,8},{10,11... | collective-permute-start | bytes 7077896 | tf_op jit(solution)/shard_map/ppermute | solution.py:425
  252.4 18.3 %copy-start.14 = (f32[2,768]{0,1:T(8,128)S(1)}, f32[2,768]{0,1:T(8,128)}, u32[]{:S(2)}) copy-start(f32[2,768]{0,1:T(8,128)} %get-tuple-element.493) | copy-start | bytes 18436
  270.5 14.6 %collective-permute-start.6 = (bf16[2,512,768]{2,1,0:T(8,128)(2,1)}, bf16[2,512,768]{2,1,0:T(8,128)(2,1)}, u32[]{:S(2)}, u32[]{:S(2)}) collective-permute-start(bf16[2,512,768]{2,1,0:T(8,128)(2,1)} %get-tuple-element.224.refs_1_), channel_id=1, source_target_pairs={{0,1},{1,0},{2,3},{3,2},{4,5},{5,4},{6,7},{7,6},{8,9},{9,8},{10,11... | collective-permute-start | bytes 4718600 | tf_op jit(solution)/shard_map/ppermute | solution.py:425
  286.8 6.0 collective-permute-start.7
  292.8 2.3 collective-permute-start.8
  303.3 19.3 %collective-permute-start.9 = (bf16[384,768]{1,0:T(8,128)(2,1)}, bf16[384,768]{1,0:T(8,128)(2,1)S(1)}, u32[]{:S(2)}, u32[]{:S(2)}) collective-permute-start(bf16[384,768]{1,0:T(8,128)(2,1)} %get-tuple-element.234), channel_id=1, source_target_pairs={{0,2},{2,0},{4,6},{6,4},{8,10},{10,8},{12,14},{14,12},{16,18},{18,... | collective-permute-start | bytes 1769480 | tf_op jit(solution)/shard_map/ppermute | solution.py:429
  304.7 17.8 %collective-permute-start.10 = (bf16[384,768]{1,0:T(8,128)(2,1)}, bf16[384,768]{1,0:T(8,128)(2,1)S(1)}, u32[]{:S(2)}, u32[]{:S(2)}) collective-permute-start(bf16[384,768]{1,0:T(8,128)(2,1)} %get-tuple-element.235), channel_id=1, source_target_pairs={{0,4},{2,6},{4,0},{6,2},{8,12},{10,14},{12,8},{14,10},{16,20},{18,... | collective-permute-start | bytes 1769480 | tf_op jit(solution)/shard_map/ppermute | solution.py:429
  322.6 3.7 collective-permute-start.11
  337.1 25.4 %collective-permute-start.12 = (bf16[576,768]{1,0:T(8,128)(2,1)}, bf16[576,768]{1,0:T(8,128)(2,1)S(1)}, u32[]{:S(2)}, u32[]{:S(2)}) collective-permute-start(bf16[576,768]{1,0:T(8,128)(2,1)} %get-tuple-element.252), channel_id=1, source_target_pairs={{0,2},{2,0},{4,6},{6,4},{8,10},{10,8},{12,14},{14,12},{16,18},{18,... | collective-permute-start | bytes 2654216 | tf_op jit(solution)/shard_map/ppermute | solution.py:429
  338.5 24.0 %collective-permute-start.13 = (bf16[576,768]{1,0:T(8,128)(2,1)}, bf16[576,768]{1,0:T(8,128)(2,1)}, u32[]{:S(2)}, u32[]{:S(2)}) collective-permute-start(bf16[576,768]{1,0:T(8,128)(2,1)} %get-tuple-element.253), channel_id=1, source_target_pairs={{0,4},{2,6},{4,0},{6,2},{8,12},{10,14},{12,8},{14,10},{16,20},{18,... | collective-permute-start | bytes 2654216 | tf_op jit(solution)/shard_map/ppermute | solution.py:429
  362.5 4.8 collective-permute-start.14
  362.6 4.7 collective-permute-start.15
  384.1 34.6 %collective-permute-start.16 = (bf16[960,768]{1,0:T(8,128)(2,1)}, bf16[960,768]{1,0:T(8,128)(2,1)S(1)}, u32[]{:S(2)}, u32[]{:S(2)}) collective-permute-start(bf16[960,768]{1,0:T(8,128)(2,1)} %get-tuple-element.282), channel_id=1, source_target_pairs={{0,2},{2,0},{4,6},{6,4},{8,10},{10,8},{12,14},{14,12},{16,18},{18,... | collective-permute-start | bytes 4423688 | tf_op jit(solution)/shard_map/ppermute | solution.py:429
  385.6 34.3 %collective-permute-start.17 = (bf16[960,768]{1,0:T(8,128)(2,1)}, bf16[960,768]{1,0:T(8,128)(2,1)S(1)}, u32[]{:S(2)}, u32[]{:S(2)}) collective-permute-start(bf16[960,768]{1,0:T(8,128)(2,1)} %get-tuple-element.283), channel_id=1, source_target_pairs={{0,4},{2,6},{4,0},{6,2},{8,12},{10,14},{12,8},{14,10},{16,20},{18,... | collective-permute-start | bytes 4423688 | tf_op jit(solution)/shard_map/ppermute | solution.py:429
  386.1 22.0 %collective-permute-start.18 = (bf16[96,768]{1,0:T(8,128)(2,1)}, bf16[96,768]{1,0:T(8,128)(2,1)S(1)}, u32[]{:S(2)}, u32[]{:S(2)}) collective-permute-start(bf16[96,768]{1,0:T(8,128)(2,1)} %get-tuple-element.284), channel_id=1, source_target_pairs={{0,8},{2,10},{4,12},{6,14},{8,0},{10,2},{12,4},{14,6},{16,24},{18,... | collective-permute-start | bytes 442376 | tf_op jit(solution)/shard_map/ppermute | solution.py:429
  386.1 22.1 %collective-permute-start.19 = (bf16[96,768]{1,0:T(8,128)(2,1)}, bf16[96,768]{1,0:T(8,128)(2,1)S(1)}, u32[]{:S(2)}, u32[]{:S(2)}) collective-permute-start(bf16[96,768]{1,0:T(8,128)(2,1)} %get-tuple-element.285), channel_id=1, source_target_pairs={{0,16},{2,18},{4,20},{6,22},{8,24},{10,26},{12,28},{14,30},{16,0},... | collective-permute-start | bytes 442376 | tf_op jit(solution)/shard_map/ppermute | solution.py:429
  388.1 20.1 %collective-permute-start.20 = (bf16[96,768]{1,0:T(8,128)(2,1)}, bf16[96,768]{1,0:T(8,128)(2,1)S(1)}, u32[]{:S(2)}, u32[]{:S(2)}) collective-permute-start(bf16[96,768]{1,0:T(8,128)(2,1)} %get-tuple-element.286), channel_id=1, source_target_pairs={{0,24},{2,26},{4,28},{6,30},{8,16},{10,18},{12,20},{14,22},{16,8},... | collective-permute-start | bytes 442376 | tf_op jit(solution)/shard_map/ppermute | solution.py:429
  419.8 3.6 collective-permute-start.21
  436.8 32.1 %collective-permute-start.22 = (bf16[768,768]{1,0:T(8,128)(2,1)}, bf16[768,768]{1,0:T(8,128)(2,1)S(1)}, u32[]{:S(2)}, u32[]{:S(2)}) collective-permute-start(bf16[768,768]{1,0:T(8,128)(2,1)} %get-tuple-element.312), channel_id=1, source_target_pairs={{0,2},{2,0},{4,6},{6,4},{8,10},{10,8},{12,14},{14,12},{16,18},{18,... | collective-permute-start | bytes 3538952 | tf_op jit(solution)/shard_map/ppermute | solution.py:429
  437.4 31.5 %collective-permute-start.23 = (bf16[768,768]{1,0:T(8,128)(2,1)}, bf16[768,768]{1,0:T(8,128)(2,1)}, u32[]{:S(2)}, u32[]{:S(2)}) collective-permute-start(bf16[768,768]{1,0:T(8,128)(2,1)} %get-tuple-element.313), channel_id=1, source_target_pairs={{0,4},{2,6},{4,0},{6,2},{8,12},{10,14},{12,8},{14,10},{16,20},{18,... | collective-permute-start | bytes 3538952 | tf_op jit(solution)/shard_map/ppermute | solution.py:429
  438.9 7.1 %collective-permute-start.24 = (bf16[96,768]{1,0:T(8,128)(2,1)}, bf16[96,768]{1,0:T(8,128)(2,1)S(1)}, u32[]{:S(2)}, u32[]{:S(2)}) collective-permute-start(bf16[96,768]{1,0:T(8,128)(2,1)} %get-tuple-element.314), channel_id=1, source_target_pairs={{0,8},{2,10},{4,12},{6,14},{8,0},{10,2},{12,4},{14,6},{16,24},{18,... | collective-permute-start | bytes 442376 | tf_op jit(solution)/shard_map/ppermute | solution.py:429
  440.6 28.2 %collective-permute-start.25 = (bf16[96,768]{1,0:T(8,128)(2,1)}, bf16[96,768]{1,0:T(8,128)(2,1)S(1)}, u32[]{:S(2)}, u32[]{:S(2)}) collective-permute-start(bf16[96,768]{1,0:T(8,128)(2,1)} %get-tuple-element.315), channel_id=1, source_target_pairs={{0,16},{2,18},{4,20},{6,22},{8,24},{10,26},{12,28},{14,30},{16,0},... | collective-permute-start | bytes 442376 | tf_op jit(solution)/shard_map/ppermute | solution.py:429
  442.6 26.3 %collective-permute-start.26 = (bf16[96,768]{1,0:T(8,128)(2,1)}, bf16[96,768]{1,0:T(8,128)(2,1)S(1)}, u32[]{:S(2)}, u32[]{:S(2)}) collective-permute-start(bf16[96,768]{1,0:T(8,128)(2,1)} %get-tuple-element.316), channel_id=1, source_target_pairs={{0,24},{2,26},{4,28},{6,30},{8,16},{10,18},{12,20},{14,22},{16,8},... | collective-permute-start | bytes 442376 | tf_op jit(solution)/shard_map/ppermute | solution.py:429
  446.0 22.8 %copy-start.45 = (bf16[96,768]{1,0:T(8,128)(2,1)}, bf16[96,768]{1,0:T(8,128)(2,1)S(1)}, u32[]{:S(2)}) copy-start(bf16[96,768]{1,0:T(8,128)(2,1)S(1)} %collective-permute-done.24.refs_10_) | copy-start | bytes 442372
  446.0 22.9 %collective-permute-start.27 = (f32[1,2,48,768]{3,2,1,0:T(8,128)}, f32[1,2,48,768]{3,2,1,0:T(8,128)S(1)}, u32[]{:S(2)}, u32[]{:S(2)}) collective-permute-start(f32[1,2,48,768]{3,2,1,0:T(8,128)} %get-tuple-element.317), channel_id=1, source_target_pairs={{0,1},{1,0},{2,3},{3,2},{4,5},{5,4},{6,7},{7,6},{8,9},{9,8},{10,11... | collective-permute-start | bytes 884744 | tf_op jit(solution)/shard_map/ppermute | solution.py:425
  470.0 14.3 %collective-permute-start.29 = (bf16[2,512,768]{2,1,0:T(8,128)(2,1)}, bf16[2,512,768]{2,1,0:T(8,128)(2,1)S(1)}, u32[]{:S(2)}, u32[]{:S(2)}) collective-permute-start(bf16[2,512,768]{2,1,0:T(8,128)(2,1)} %get-tuple-element.333), channel_id=1, source_target_pairs={{0,1},{1,0},{2,3},{3,2},{4,5},{5,4},{6,7},{7,6},{8,9},{9,8},{10,11... | collective-permute-start | bytes 4718600 | tf_op jit(solution)/shard_map/ppermute | solution.py:425
  484.3 14.5 %collective-permute-start.28 = (f32[80,768]{1,0:T(8,128)}, f32[80,768]{1,0:T(8,128)S(1)}, u32[]{:S(2)}, u32[]{:S(2)}) collective-permute-start(f32[80,768]{1,0:T(8,128)} %concatenate.62), channel_id=1, source_target_pairs={{0,1},{1,0},{2,3},{3,2},{4,5},{5,4},{6,7},{7,6},{8,9},{9,8},{10,11... | collective-permute-start | bytes 737288 | tf_op jit(solution)/shard_map/ppermute | solution.py:425
  496.6 37.3 %collective-permute-start.30 = (bf16[576,768]{1,0:T(8,128)(2,1)}, bf16[576,768]{1,0:T(8,128)(2,1)S(1)}, u32[]{:S(2)}, u32[]{:S(2)}) collective-permute-start(bf16[576,768]{1,0:T(8,128)(2,1)} %get-tuple-element.350), channel_id=1, source_target_pairs={{0,2},{2,0},{4,6},{6,4},{8,10},{10,8},{12,14},{14,12},{16,18},{18,... | collective-permute-start | bytes 2654216 | tf_op jit(solution)/shard_map/ppermute | solution.py:429
  497.3 36.7 %collective-permute-start.31 = (bf16[576,768]{1,0:T(8,128)(2,1)}, bf16[576,768]{1,0:T(8,128)(2,1)}, u32[]{:S(2)}, u32[]{:S(2)}) collective-permute-start(bf16[576,768]{1,0:T(8,128)(2,1)} %get-tuple-element.351), channel_id=1, source_target_pairs={{0,4},{2,6},{4,0},{6,2},{8,12},{10,14},{12,8},{14,10},{16,20},{18,... | collective-permute-start | bytes 2654216 | tf_op jit(solution)/shard_map/ppermute | solution.py:429
  499.7 24.6 %copy-start.65 = (f32[1,768]{1,0:T(1,128)S(1)}, f32[1,768]{1,0:T(1,128)}, u32[]{:S(2)}) copy-start(f32[1,768]{1,0:T(1,128)} %get-tuple-element.398) | copy-start | bytes 9220
  499.9 23.6 %collective-permute-start.32 = (bf16[192,768]{1,0:T(8,128)(2,1)}, bf16[192,768]{1,0:T(8,128)(2,1)S(1)}, u32[]{:S(2)}, u32[]{:S(2)}) collective-permute-start(bf16[192,768]{1,0:T(8,128)(2,1)} %get-tuple-element.352), channel_id=1, source_target_pairs={{0,8},{2,10},{4,12},{6,14},{8,0},{10,2},{12,4},{14,6},{16,24},{18,... | collective-permute-start | bytes 884744 | tf_op jit(solution)/shard_map/ppermute | solution.py:429
  500.0 23.1 %collective-permute-start.36 = (f32[4,2,80,48]{2,3,1,0:T(8,128)S(1)}, f32[4,2,80,48]{2,3,1,0:T(8,128)S(1)}, u32[]{:S(2)}, u32[]{:S(2)}) collective-permute-start(f32[4,2,80,48]{2,3,1,0:T(8,128)S(1)} %dynamic-slice_bitcast_fusion), channel_id=1, source_target_pairs={{0,2},{2,0},{4,6},{6,4},{8,10},{10,8},{12,14},{14,12},{16,18},{18,... | collective-permute-start | bytes 368648 | tf_op jit(solution)/shard_map/ppermute | solution.py:429
  500.7 24.2 %collective-permute-start.33 = (bf16[192,768]{1,0:T(8,128)(2,1)}, bf16[192,768]{1,0:T(8,128)(2,1)}, u32[]{:S(2)}, u32[]{:S(2)}) collective-permute-start(bf16[192,768]{1,0:T(8,128)(2,1)} %get-tuple-element.353), channel_id=1, source_target_pairs={{0,16},{2,18},{4,20},{6,22},{8,24},{10,26},{12,28},{14,30},{16,0},... | collective-permute-start | bytes 884744 | tf_op jit(solution)/shard_map/ppermute | solution.py:429
  523.1 10.8 %collective-permute-start.34 = (bf16[192,768]{1,0:T(8,128)(2,1)}, bf16[192,768]{1,0:T(8,128)(2,1)}, u32[]{:S(2)}, u32[]{:S(2)}) collective-permute-start(bf16[192,768]{1,0:T(8,128)(2,1)} %get-tuple-element.354), channel_id=1, source_target_pairs={{0,24},{2,26},{4,28},{6,30},{8,16},{10,18},{12,20},{14,22},{16,8},... | collective-permute-start | bytes 884744 | tf_op jit(solution)/shard_map/ppermute | solution.py:429
  523.6 10.4 %collective-permute-start.35 = (f32[1,2,48,768]{3,2,1,0:T(8,128)}, f32[1,2,48,768]{3,2,1,0:T(8,128)}, u32[]{:S(2)}, u32[]{:S(2)}) collective-permute-start(f32[1,2,48,768]{3,2,1,0:T(8,128)} %get-tuple-element.355), channel_id=1, source_target_pairs={{0,1},{1,0},{2,3},{3,2},{4,5},{5,4},{6,7},{7,6},{8,9},{9,8},{10,11... | collective-permute-start | bytes 884744 | tf_op jit(solution)/shard_map/ppermute | solution.py:425
  524.9 19.9 %copy-start.40 = (f32[1,2,48,768]{3,2,1,0:T(8,128)S(1)}, f32[1,2,48,768]{3,2,1,0:T(8,128)}, u32[]{:S(2)}) copy-start(f32[1,2,48,768]{3,2,1,0:T(8,128)} %get-tuple-element.355) | copy-start | bytes 884740
  540.2 10.8 %collective-permute-start.43 = (f32[4,80,48]{1,2,0:T(8,128)}, f32[4,80,48]{1,2,0:T(8,128)}, u32[]{:S(2)}, u32[]{:S(2)}) collective-permute-start(f32[4,80,48]{1,2,0:T(8,128)} %dynamic-slice_bitcast_fusion.1), channel_id=1, source_target_pairs={{0,4},{2,6},{4,0},{6,2},{8,12},{10,14},{12,8},{14,10},{16,20},{18,... | collective-permute-start | bytes 184328 | tf_op jit(solution)/shard_map/ppermute | solution.py:429
  540.7 10.8 %collective-permute-start.39 = (bf16[96,768]{1,0:T(8,128)(2,1)}, bf16[96,768]{1,0:T(8,128)(2,1)}, u32[]{:S(2)}, u32[]{:S(2)}) collective-permute-start(bf16[96,768]{1,0:T(8,128)(2,1)} %get-tuple-element.374), channel_id=1, source_target_pairs={{0,8},{2,10},{4,12},{6,14},{8,0},{10,2},{12,4},{14,6},{16,24},{18,... | collective-permute-start | bytes 442376 | tf_op jit(solution)/shard_map/ppermute | solution.py:429
  545.8 18.5 %collective-permute-start.37 = (bf16[192,768]{1,0:T(8,128)(2,1)}, bf16[192,768]{1,0:T(8,128)(2,1)}, u32[]{:S(2)}, u32[]{:S(2)}) collective-permute-start(bf16[192,768]{1,0:T(8,128)(2,1)} %get-tuple-element.372), channel_id=1, source_target_pairs={{0,2},{2,0},{4,6},{6,4},{8,10},{10,8},{12,14},{14,12},{16,18},{18,... | collective-permute-start | bytes 884744 | tf_op jit(solution)/shard_map/ppermute | solution.py:429
  547.3 17.0 %collective-permute-start.38 = (bf16[192,768]{1,0:T(8,128)(2,1)}, bf16[192,768]{1,0:T(8,128)(2,1)}, u32[]{:S(2)}, u32[]{:S(2)}) collective-permute-start(bf16[192,768]{1,0:T(8,128)(2,1)} %get-tuple-element.373), channel_id=1, source_target_pairs={{0,4},{2,6},{4,0},{6,2},{8,12},{10,14},{12,8},{14,10},{16,20},{18,... | collective-permute-start | bytes 884744 | tf_op jit(solution)/shard_map/ppermute | solution.py:429
  547.9 16.4 %collective-permute-start.42 = (f32[2,2,48,768]{3,2,1,0:T(8,128)}, f32[2,2,48,768]{3,2,1,0:T(8,128)}, u32[]{:S(2)}, u32[]{:S(2)}) collective-permute-start(f32[2,2,48,768]{3,2,1,0:T(8,128)} %get-tuple-element.377), channel_id=1, source_target_pairs={{0,1},{1,0},{2,3},{3,2},{4,5},{5,4},{6,7},{7,6},{8,9},{9,8},{10,11... | collective-permute-start | bytes 1769480 | tf_op jit(solution)/shard_map/ppermute | solution.py:425
  551.0 13.3 %collective-permute-start.40 = (bf16[96,768]{1,0:T(8,128)(2,1)}, bf16[96,768]{1,0:T(8,128)(2,1)}, u32[]{:S(2)}, u32[]{:S(2)}) collective-permute-start(bf16[96,768]{1,0:T(8,128)(2,1)} %get-tuple-element.375), channel_id=1, source_target_pairs={{0,16},{2,18},{4,20},{6,22},{8,24},{10,26},{12,28},{14,30},{16,0},... | collective-permute-start | bytes 442376 | tf_op jit(solution)/shard_map/ppermute | solution.py:429
  551.5 12.7 %collective-permute-start.41 = (bf16[96,768]{1,0:T(8,128)(2,1)}, bf16[96,768]{1,0:T(8,128)(2,1)}, u32[]{:S(2)}, u32[]{:S(2)}) collective-permute-start(bf16[96,768]{1,0:T(8,128)(2,1)} %get-tuple-element.376), channel_id=1, source_target_pairs={{0,24},{2,26},{4,28},{6,30},{8,16},{10,18},{12,20},{14,22},{16,8},... | collective-permute-start | bytes 442376 | tf_op jit(solution)/shard_map/ppermute | solution.py:429
  568.1 12.1 %collective-permute-start.48 = (f32[80,48]{1,0:T(8,128)S(1)}, f32[80,48]{1,0:T(8,128)S(1)}, u32[]{:S(2)}, u32[]{:S(2)}) collective-permute-start(f32[80,48]{1,0:T(8,128)S(1)} %bitcast.152), channel_id=1, source_target_pairs={{0,8},{2,10},{4,12},{6,14},{8,0},{10,2},{12,4},{14,6},{16,24},{18,... | collective-permute-start | bytes 46088 | tf_op jit(solution)/shard_map/ppermute | solution.py:429
  571.8 11.3 %collective-permute-start.49 = (f32[80,48]{1,0:T(8,128)S(1)}, f32[80,48]{1,0:T(8,128)S(1)}, u32[]{:S(2)}, u32[]{:S(2)}) collective-permute-start(f32[80,48]{1,0:T(8,128)S(1)} %bitcast.151), channel_id=1, source_target_pairs={{0,16},{2,18},{4,20},{6,22},{8,24},{10,26},{12,28},{14,30},{16,0},... | collective-permute-start | bytes 46088 | tf_op jit(solution)/shard_map/ppermute | solution.py:429
  572.4 16.8 %collective-permute-start.44 = (bf16[96,768]{1,0:T(8,128)(2,1)}, bf16[96,768]{1,0:T(8,128)(2,1)S(1)}, u32[]{:S(2)}, u32[]{:S(2)}) collective-permute-start(bf16[96,768]{1,0:T(8,128)(2,1)} %get-tuple-element.390), channel_id=1, source_target_pairs={{0,8},{2,10},{4,12},{6,14},{8,0},{10,2},{12,4},{14,6},{16,24},{18,... | collective-permute-start | bytes 442376 | tf_op jit(solution)/shard_map/ppermute | solution.py:429
  574.3 14.9 %collective-permute-start.45 = (bf16[96,768]{1,0:T(8,128)(2,1)}, bf16[96,768]{1,0:T(8,128)(2,1)S(1)}, u32[]{:S(2)}, u32[]{:S(2)}) collective-permute-start(bf16[96,768]{1,0:T(8,128)(2,1)} %get-tuple-element.391), channel_id=1, source_target_pairs={{0,16},{2,18},{4,20},{6,22},{8,24},{10,26},{12,28},{14,30},{16,0},... | collective-permute-start | bytes 442376 | tf_op jit(solution)/shard_map/ppermute | solution.py:429
  574.8 14.5 %collective-permute-start.47 = (f32[1,2,48,768]{3,2,1,0:T(8,128)}, f32[1,2,48,768]{3,2,1,0:T(8,128)S(1)}, u32[]{:S(2)}, u32[]{:S(2)}) collective-permute-start(f32[1,2,48,768]{3,2,1,0:T(8,128)} %get-tuple-element.393), channel_id=1, source_target_pairs={{0,1},{1,0},{2,3},{3,2},{4,5},{5,4},{6,7},{7,6},{8,9},{9,8},{10,11... | collective-permute-start | bytes 884744 | tf_op jit(solution)/shard_map/ppermute | solution.py:425
  578.9 20.3 %copy-start.37 = (f32[1,2,48,768]{3,2,1,0:T(8,128)S(1)}, f32[1,2,48,768]{3,2,1,0:T(8,128)}, u32[]{:S(2)}) copy-start(f32[1,2,48,768]{3,2,1,0:T(8,128)} %get-tuple-element.393) | copy-start | bytes 884740
  580.2 9.1 %collective-permute-start.46 = (bf16[96,768]{1,0:T(8,128)(2,1)S(1)}, bf16[96,768]{1,0:T(8,128)(2,1)S(1)}, u32[]{:S(2)}, u32[]{:S(2)}) collective-permute-start(bf16[96,768]{1,0:T(8,128)(2,1)S(1)} %copy-done.72), channel_id=1, source_target_pairs={{0,24},{2,26},{4,28},{6,30},{8,16},{10,18},{12,20},{14,22},{16,8},... | collective-permute-start | bytes 442376 | tf_op jit(solution)/shard_map/ppermute | solution.py:429
  583.1 6.1 collective-permute-start.50
  599.1 1.1 collective-permute-start.51
  601.6 3.5 collective-permute-start.52
  606.5 3.5 collective-permute-start.53
  610.1 5.8 collective-permute-start.54
  614.6 23.0 %collective-permute-start.56 = (f32[1,2,48,768]{3,2,1,0:T(8,128)}, f32[1,2,48,768]{3,2,1,0:T(8,128)}, u32[]{:S(2)}, u32[]{:S(2)}) collective-permute-start(f32[1,2,48,768]{3,2,1,0:T(8,128)} %get-tuple-element.406), channel_id=1, source_target_pairs={{0,1},{1,0},{2,3},{3,2},{4,5},{5,4},{6,7},{7,6},{8,9},{9,8},{10,11... | collective-permute-start | bytes 884744 | tf_op jit(solution)/shard_map/ppermute | solution.py:425
  615.9 6.1 collective-permute-start.55
  (67 other events, 339.4 us)
Sparse Core Ops, SparseCore 0:
  24.8 171.4 all-gather.1

commit v6 on v5

--- a/solution.py
+++ b/solution.py
@@ -100,8 +100,18 @@
     return copies
 
 
-def tile_of(ref, t, width):
-    return ref.at[t] if len(ref.shape) == 3 else ref.at[:, t * width : (t + 1) * width]
+def tile_of(ref, core, at):
+    return ref.at[:, core, :, at : at + ref.shape[0] * ref.shape[2]]
+
+
+def matrix(ref, place, low=None, high=None):
+    value = ref[place] if low is None else ref[place, :, :, low:high]
+    return value.reshape(-1, value.shape[-1])
+
+
+def tile_scratch(count, weights):
+    blocks, _, rows, _ = weights.shape
+    return pltpu.VMEM((count, blocks, rows, blocks * rows), LOW)
 
 
 def swap_halves(value):
@@ -123,14 +133,14 @@
 
 
 def attention_forward_kernel(
-    place_of, resid, seg_col, seg_row, cosine, sine, gains, own, other,
+    base, place_of, resid, seg_col, seg_row, cosine, sine, gains, weights,
     middle, query, keys, values, lse, pack,
     w_a, w_b, mixed, same, sems,
 ):
     width = resid.shape[1]
     half = width // 2
     copies = fetch(
-        [tile_of(r, t, width) for t in range(2) for r in (own, other)],
+        [tile_of(weights, c, base + t * width) for t in range(2) for c in (place_of[0], 1 - place_of[0])],
         [w.at[place] for w in (w_a, w_b) for place in range(2)],
         sems,
     )
@@ -141,7 +151,7 @@
     same[...] = jnp.where(seg_col[...] == seg_row[...], 0.0, 1.0)
     for place in range(2):
         copies[place].wait()
-        mixed[...] = dot(normed_low[...], w_a[place])
+        mixed[...] = dot(normed_low[...], matrix(w_a, place))
         for p in range(half // 128):
             for part, target in ((0, query), (1, keys)):
                 x = mixed[:, part * half + p * 128 : part * half + (p + 1) * 128]
@@ -150,7 +160,7 @@
     for place in range(2):
         copies[2 + place].wait()
         values[:, place * half : (place + 1) * half] = dot(
-            normed_low[...], w_b[place, :, :half]
+            normed_low[...], matrix(w_b, place, 0, half)
         ).astype(LOW)
 
     lse[...] = jnp.zeros_like(lse)
@@ -176,24 +186,26 @@
     lax.fori_loop(0, width // 128, pair, 0)
     attended[...] = ordered(first, attended[:, :half], attended[:, half:])
     out = ordered(
-        first, dot(attended[...], w_b[0, :, half:]), dot(attended[...], w_b[1, :, half:])
+        first,
+        dot(attended[...], matrix(w_b, 0, half, width)),
+        dot(attended[...], matrix(w_b, 1, half, width)),
     )
     middle[...] = resid[...] + out
 
 
-def attention_forward(place, resid, mixer, gains, cosine, sine, segments):
+def attention_forward(place, resid, weights, base, gains, cosine, sine, segments):
     length, width = resid.shape
     one = (length, width)
     outs = [(one, FULL)] + [(one, LOW)] * 3 + [((length, 128), FULL), ((2,) + one, LOW)]
     return call(
-        attention_forward_kernel,
+        functools.partial(attention_forward_kernel, base),
         place,
         outs,
         [resid, segments[:, None], segments[None, :], cosine, sine, gains],
-        list(mixer),
+        [weights],
         [
-            pltpu.VMEM((2, width, width), LOW),
-            pltpu.VMEM((2, width, width), LOW),
+            tile_scratch(2, weights),
+            tile_scratch(2, weights),
             pltpu.VMEM(one, FULL),
             pltpu.VMEM((length, length), FULL),
             pltpu.SemaphoreType.DMA((4,)),
@@ -206,17 +218,19 @@
 GELU_CUBE = 0.044715
 
 
-def hidden_tiles(own, other, width):
-    ups = [tile_of(r, t, width) for r in (own, other) for t in (0, 1)]
-    downs = [tile_of(r, t, width) for r in (own, other) for t in (2, 3)]
-    return ups, downs
+def hidden_tiles(weights, core, base, width):
+    tiles = [
+        [tile_of(weights, c, base + t * width) for c in (core, 1 - core) for t in pair]
+        for pair in ((2, 3), (4, 5))
+    ]
+    return tiles[0], tiles[1]
 
 
 def hidden_forward_kernel(
-    place_of, middle, gains, own, other,
+    base, place_of, middle, gains, weights,
     output, active, pack, hidden, ups, downs, hidden_here, sems, out_sems,
 ):
-    u, d = hidden_tiles(own, other, middle.shape[1])
+    u, d = hidden_tiles(weights, place_of[0], base, middle.shape[1])
     ins = fetch(
         [r for t in range(4) for r in (u[t], d[t])],
         [w.at[t] for t in range(4) for w in (ups, downs)],
@@ -227,7 +241,7 @@
     outs = []
     for t in range(4):
         ins[2 * t].wait()
-        x = dot(pack[0], ups[t])
+        x = dot(pack[0], matrix(ups, t))
         hidden_here[t] = x
         out = pltpu.make_async_copy(hidden_here.at[t], hidden.at[t], out_sems.at[t])
         out.start()
@@ -236,25 +250,25 @@
         target = active.at[t] if t < 2 else pack.at[t - 1]
         target[...] = (x * (0.5 * (1.0 + inner))).astype(LOW)
         ins[2 * t + 1].wait()
-        product = dot(target[...], downs[t])
+        product = dot(target[...], matrix(downs, t))
         output[...] = (middle[...] if t == 0 else output[...]) + product
     for out in outs:
         out.wait()
 
 
-def hidden_forward(place, middle, pair, gains):
+def hidden_forward(place, middle, weights, base, gains):
     length, width = middle.shape
     one = (length, width)
     outs = [(one, FULL), ((2,) + one, LOW), ((3,) + one, LOW), ((4,) + one, FULL)]
     return call(
-        hidden_forward_kernel,
+        functools.partial(hidden_forward_kernel, base),
         place,
         outs,
         [middle, gains],
-        list(pair),
+        [weights],
         [
-            pltpu.VMEM((4, width, width), LOW),
-            pltpu.VMEM((4, width, width), LOW),
+            tile_scratch(4, weights),
+            tile_scratch(4, weights),
             pltpu.VMEM((4,) + one, FULL),
             pltpu.SemaphoreType.DMA((8,)),
             pltpu.SemaphoreType.DMA((4,)),
@@ -265,10 +279,10 @@
 
 
 def hidden_back_kernel(
-    place_of, grad, branch, middle, gains, hidden, own, other,
+    base, place_of, grad, branch, middle, gains, hidden, weights,
     grad_middle, grad_gains, grad_own, grad_other, ups, downs, hidden_here, total, sems,
 ):
-    u, d = hidden_tiles(own, other, middle.shape[1])
+    u, d = hidden_tiles(weights, place_of[0], base, middle.shape[1])
     ins = fetch(
         [r for t in range(4) for r in (d[t], hidden.at[t], u[t])],
         [w.at[t] for t in range(4) for w in (downs, hidden_here, ups)],
@@ -276,7 +290,7 @@
     )
     for t in range(4):
         ins[3 * t].wait()
-        grad_active = dot_nt(branch[...], downs[t])
+        grad_active = dot_nt(branch[...], matrix(downs, t))
         ins[3 * t + 1].wait()
         x = hidden_here[t]
         inner = jnp.tanh(GELU_SCALE * (x + GELU_CUBE * (x * x * x)))
@@ -286,7 +300,7 @@
         target = grad_own.at[t] if t < 2 else grad_other.at[t - 2]
         target[...] = (grad_active * slope).astype(LOW)
         ins[3 * t + 2].wait()
-        product = dot_nt(target[...], ups[t])
+        product = dot_nt(target[...], matrix(ups, t))
         total[...] = product if t == 0 else total[...] + product
     _, unit, inverse = normalize(middle[...], gains[0:1], gains[1:2])
     back, gain, bias = normalize_back(total[...], unit, inverse, gains[0:1])
@@ -295,19 +309,19 @@
     grad_gains[1:2] = bias
 
 
-def hidden_back(place, grad, branch, middle, hidden, pair, gains):
+def hidden_back(place, grad, branch, middle, hidden, weights, base, gains):
     length, width = middle.shape
     one = (length, width)
     outs = [(one, FULL), ((2, width), FULL), ((2,) + one, LOW), ((2,) + one, LOW)]
     return call(
-        hidden_back_kernel,
+        functools.partial(hidden_back_kernel, base),
         place,
         outs,
         [grad, branch, middle, gains],
-        [hidden] + list(pair),
+        [hidden, weights],
         [
-            pltpu.VMEM((4, width, width), LOW),
-            pltpu.VMEM((4, width, width), LOW),
+            tile_scratch(4, weights),
+            tile_scratch(4, weights),
             pltpu.VMEM((4,) + one, FULL),
             pltpu.VMEM(one, FULL),
             pltpu.SemaphoreType.DMA((12,)),
@@ -317,15 +331,15 @@
 
 
 def attention_back_kernel(
-    place_of, grad_middle, resid, seg_col, seg_row, cosine, sine, gains, query, keys, values, lse,
-    own, other,
+    base, place_of, grad_middle, resid, seg_col, seg_row, cosine, sine, gains, query, keys, values, lse,
+    weights,
     grad, branch, grad_gains, grad_own, grad_other,
     w_a, w_b, same, ga, gq, gk, gv, sems,
 ):
     width = resid.shape[1]
     half = width // 2
     copies = fetch(
-        [tile_of(r, t, width) for t in (1, 0) for r in (own, other)],
+        [tile_of(weights, c, base + t * width) for t in (1, 0) for c in (place_of[0], 1 - place_of[0])],
         [w.at[place] for w in (w_b, w_a) for place in range(2)],
         sems,
     )
@@ -339,8 +353,8 @@
     grad_other[1, :, half:] = jnp.where(first, right, left)
     copies[0].wait()
     copies[1].wait()
-    natural = dot_nt(grad_own[1, :, half:], w_b[0, :, half:]) + dot_nt(
-        grad_other[1, :, half:], w_b[1, :, half:]
+    natural = dot_nt(grad_own[1, :, half:], matrix(w_b, 0, half, width)) + dot_nt(
+        grad_other[1, :, half:], matrix(w_b, 1, half, width)
     )
     natural = natural.astype(LOW)
     ga[:, :half] = jnp.where(first, natural[:, :half], natural[:, half:])
@@ -377,9 +391,9 @@
         grads[place][1, :, :half] = gv[:, columns]
     copies[2].wait()
     copies[3].wait()
-    total = dot_nt(grad_own[0], w_a[0]) + dot_nt(grad_other[0], w_a[1])
-    total = total + dot_nt(grad_own[1, :, :half], w_b[0, :, :half])
-    total = total + dot_nt(grad_other[1, :, :half], w_b[1, :, :half])
+    total = dot_nt(grad_own[0], matrix(w_a, 0)) + dot_nt(grad_other[0], matrix(w_a, 1))
+    total = total + dot_nt(grad_own[1, :, :half], matrix(w_b, 0, 0, half))
+    total = total + dot_nt(grad_other[1, :, :half], matrix(w_b, 1, 0, half))
     _, unit, inverse = normalize(resid[...], gains[0:1], gains[1:2])
     back, gain, bias = normalize_back(total, unit, inverse, gains[0:1])
     back = grad_middle[...] + back
@@ -389,21 +403,21 @@
     grad_gains[1:2] = bias
 
 
-def attention_back(place, grad_middle, resid, mixer, gains, cosine, sine, segments, query, keys, values, lse):
+def attention_back(place, grad_middle, resid, weights, base, gains, cosine, sine, segments, query, keys, values, lse):
     length, width = resid.shape
     one = (length, width)
     outs = [(one, FULL), (one, LOW), ((2, width), FULL)] + [((2,) + one, LOW)] * 2
     ins = [grad_middle, resid, segments[:, None], segments[None, :], cosine, sine, gains]
     ins += [query, keys, values, lse.T[: width // HD]]
     return call(
-        attention_back_kernel,
+        functools.partial(attention_back_kernel, base),
         place,
         outs,
         ins,
-        list(mixer),
+        [weights],
         [
-            pltpu.VMEM((2, width, width), LOW),
-            pltpu.VMEM((2, width, width), LOW),
+            tile_scratch(2, weights),
+            tile_scratch(2, weights),
             pltpu.VMEM((length, length), FULL),
         ]
         + [pltpu.VMEM(one, LOW)] * 4
@@ -421,6 +435,59 @@
     return (master - rate * update, first, second)
 
 
+def optimizer_kernel(chunks, layers, place_of, scale, *refs):
+    n = (len(refs) - 25) // 2
+    own, other, up, masters = refs[:n], refs[n : 2 * n], refs[2 * n], refs[2 * n + 1 : 2 * n + 13]
+    outs = refs[2 * n + 13 :]
+    first = place_of[0] == 0
+    count, factor = scale[0], scale[1]
+
+    def step(which, at, grad):
+        master, moment, square = (masters[3 * which + i][at] for i in range(3))
+        clipped = grad / count * factor
+        values = adam_step(master, clipped, moment, square, RATE_MATRIX, DECAY)
+        for i in range(3):
+            outs[3 * which + i][at] = values[i]
+
+    def tile(where, s, core):
+        a, b = own[where[0]][where[1], s], other[where[0]][where[1], s]
+        return jnp.where(first, a, b) if core == 0 else jnp.where(first, b, a)
+
+    rows, width = own[0].shape[-2:]
+    half = width // 2
+    for l in range(layers):
+        mixer, down = chunks[l]
+        for core in range(2):
+            columns = lambda p: pl.ds(p * width + core * half, half)
+            value = tile(mixer, 0, core)
+            step(0, (l, slice(None), columns(0)), value[:, :half])
+            step(0, (l, slice(None), columns(1)), value[:, half:])
+            value = tile(mixer, 1, core)
+            step(0, (l, slice(None), columns(2)), value[:, :half])
+            step(1, (l, slice(None), columns(0)), value[:, half:])
+            for s in range(2):
+                at = (l, pl.ds((2 * core + s) * rows, rows), slice(None))
+                step(3, at, tile(down, s, core))
+        step(2, l, up[l])
+
+
+def optimizer(place, scale, chunks, own, other, up, masters):
+    ins = list(own) + list(other) + [up] + list(masters)
+    whole = pl.BlockSpec(memory_space=pltpu.VMEM)
+    return pl.pallas_call(
+        functools.partial(optimizer_kernel, chunks, up.shape[0]),
+        out_shape=[jax.ShapeDtypeStruct(m.shape, m.dtype) for m in masters],
+        in_specs=[pl.BlockSpec(memory_space=pltpu.SMEM)] * 2 + [whole] * len(ins),
+        out_specs=[whole] * len(masters),
+        compiler_params=pltpu.CompilerParams(vmem_limit_bytes=VMEM_LIMIT),
+        cost_estimate=pl.CostEstimate(
+            flops=20 * sum(m.size for m in masters),
+            bytes_accessed=8 * sum(m.size for m in masters),
+            transcendentals=0,
+        ),
+    )(place, scale, *ins)
+
+
 def swap_cores(value):
     return lax.ppermute(value, "dp", [(0, 1), (1, 0)])
 
@@ -435,8 +502,14 @@
 
 def total_of(value, size):
     value = value + swap_cores(value)
-    for bit in range(size.bit_length() - 1):
-        value = value + across(value, 1 << bit, size)
+    bit = 1
+    while bit < size:
+        if 2 * bit < size:
+            a, b, c = (across(value, m * bit, size) for m in (1, 2, 3))
+            value = (value + a) + (b + c)
+        else:
+            value = value + across(value, bit, size)
+        bit *= 4
     return value
 
 
@@ -444,33 +517,58 @@
 Z = (4, 8, 12)
 
 
-def round_kernel(jobs, n_ins, counts, *refs):
+SMALL = 128
+
+
+def round_kernel(jobs, small_job, n_ins, counts, smalls, last, *refs):
     new, once, twice, done = counts
+    small_new, small_once, small_twice, small_done = smalls
     place_of, ins = refs[0], refs[1 : 1 + n_ins]
     rest = list(refs[1 + n_ins :])
     pop = lambda present, n=1: [rest.pop(0) for _ in range(n)] if present else [None] * n
-    (keep_once,), (keep_twice,) = pop(once), pop(twice)
+    (keep_once,), (small_keep_once,) = pop(once), pop(small_once)
+    (keep_twice,), (small_keep_twice,) = pop(twice), pop(small_twice)
     from_x, from_y = pop(once or twice, 2)
-    keep_done, *from_z = pop(done, 4)
+    (keep_done,), (small_keep_done,) = pop(done), pop(small_done)
+    from_z = pop(done, 3)
+    (squares_in,), (sums,) = pop(done), pop(last)
     to_x, to_y = pop(new or once, 2)
-    (out_once,), (out_twice,) = pop(new), pop(once)
-    out_done, *to_z = pop(twice, 4)
-    share, squares = pop(done, 2)
-    (tile,) = pop(new)
+    (out_once,), (small_out_once,) = pop(new), pop(small_new)
+    (out_twice,), (small_out_twice,) = pop(once), pop(small_once)
+    (out_done,), (small_out_done,) = pop(twice), pop(small_twice)
+    to_z = pop(twice, 3)
+    (share,), (small_share,), (squares,) = pop(done), pop(small_done), pop(done)
+    (totals,) = pop(last)
+    (tile,), (small_tile,) = pop(new), pop(small_new)
     rows = (out_once if new else out_twice if once else out_done if twice else share).shape[-2]
     rows = rows // (8 if new else 4 if once else 1)
     bits, z = (place_of[1], place_of[2]), place_of[3]
     to, came = (to_x, to_y), (from_x, from_y)
 
-    def block(index):
+    def block(index, size=rows):
         if isinstance(index, int):
-            return pl.ds(index * rows, rows)
-        return pl.ds(pl.multiple_of(index * rows, 16), rows)
+            return pl.ds(index * size, size)
+        return pl.ds(pl.multiple_of(index * size, 16), size)
 
     def factor(spec):
         which, index, low, high = spec
         ref = ins[which] if index is None else ins[which].at[index]
         return ref[...] if low is None else ref[:, low:high]
+
+    def put_small(ref, start, group, side, value):
+        for q in range(rows // 16):
+            lanes = side * (rows // 16) + q
+            ref[pl.ds(start + group * 16, 16), lanes * SMALL : (lanes + 1) * SMALL] = value[
+                q * 16 : (q + 1) * 16
+            ].astype(LOW)
+
+    def take_small(ref, start, group, side):
+        parts = []
+        for q in range(rows // 16):
+            lanes = side * (rows // 16) + q
+            at = pl.ds(pl.multiple_of(start + group * 16, 16), 16)
+            parts.append(ref[at, lanes * SMALL : (lanes + 1) * SMALL])
+        return jnp.concatenate(parts, 0).astype(FULL)
 
     for p in range(new):
         for s in range(2):
@@ -486,6 +584,25 @@
                     index = lambda bit: zz * 4 + (other * 2 + bit if s == 0 else bit * 2 + other)
                     to[s][block(p * 8 + at), :] = tile[block(index(1 - bits[s])), :].astype(LOW)
                     out_once[p, s, block(at), :] = tile[block(index(bits[s])), :]
+    if small_new:
+        products, norms, norms_came = small_job
+        total = None
+        for left, right in products:
+            product = cross(factor(left), factor(right))
+            total = product if total is None else total + product
+        norms = ins[norms][...] + ins[norms_came][...]
+        high = norms.astype(LOW)
+        shape = (norms.shape[0], SMALL)
+        column = lax.broadcasted_iota(jnp.int32, shape, 1) - V
+        pick = jnp.where(lax.broadcasted_iota(jnp.int32, shape, 0) == column, 1.0, 0.0).astype(LOW)
+        total = total + (cross(high, pick) + cross((norms - high.astype(FULL)).astype(LOW), pick))
+        small_tile[...] = total
+        for zz in range(4):
+            for other in range(2):
+                index = lambda bit: zz * 4 + other * 2 + bit
+                send = small_tile[block(index(1 - bits[0])), :]
+                put_small(to_x, (new * 8 + once * 4) * rows, other * 2 + zz // 2, zz % 2, send)
+                small_out_once[block(zz * 2 + other), :] = small_tile[block(index(bits[0])), :]
     for p in range(once):
         for s in range(2):
             for zz in range(4):
@@ -496,6 +613,17 @@
                         out_twice[p, s, block(zz), :] = value
                     else:
                         to[1 - s][block(new * 8 + p * 4 + zz), :] = value.astype(LOW)
+    if small_once:
+        start = (once * 8 + twice * 4) * rows
+        for zz in range(4):
+            for bit in range(2):
+                other = bits[1] if bit else 1 - bits[1]
+                value = small_keep_once[block(zz * 2 + other), :]
+                value = value + take_small(from_x, start, other * 2 + zz // 2, zz % 2)
+                if bit:
+                    small_out_twice[block(zz), :] = value
+                else:
+                    put_small(to_y, (new * 8 + once * 4) * rows, zz, 0, value)
     for p in range(twice):
         for s in range(2):
             for xor in range(4):
@@ -507,8 +635,17 @@
                     out_done[p, s] = value
                 else:
                     to_z[xor - 1][block(2 * p + s), :] = value.astype(LOW)
+    if small_twice:
+        for xor in range(4):
+            at = jnp.bitwise_xor(z, xor)
+            value = small_keep_twice[block(at), :]
+            value = value + take_small(from_y, (once * 8 + twice * 4) * rows, at, 0)
+            if xor == 0:
+                small_out_done[...] = value
+            else:
+                put_small(to_z[xor - 1], twice * 2 * rows, 0, 0, value)
     if done:
-        squares[...] = jnp.zeros_like(squares)
+        squares[...] = squares_in[...]
     for p in range(done):
         for s in range(2):
             value = keep_done[p, s]
@@ -516,21 +653,35 @@
                 value = value + f[block(2 * p + s), :].astype(FULL)
             share[p, s] = value
             squares[...] += jnp.sum(value * value, 0, keepdims=True)
+    if small_done:
+        value = small_keep_done[...]
+        for f in from_z:
+            value = value + take_small(f, done * 2 * rows, 0, 0)
+        small_share[...] = value
+    if last:
+        total = jnp.sum(squares[...], 1, keepdims=True)
+        if small_done:
+            square = jnp.sum(jnp.sum(value * value, 0, keepdims=True), 1, keepdims=True)
+            total = total + jnp.where(place_of[0] == 0, square, jnp.zeros_like(square))
+        lane = lax.broadcasted_iota(jnp.int32, sums.shape, 1)
+        totals[...] = jnp.where(lane == 2, total, sums[...])
 
 
 class Rounds:
-    def __init__(self, place, rows, width):
-        self.place, self.rows, self.width = place, rows, width
-        self.counts = (0, 0, 0, 0)
-        self.kept = [None] * 3
-        self.came = None
-        self.came_z = None
-        self.shares, self.squares = [], []
-        self.flying = []
-
-    def step(self, chunk, *ties):
+    def __init__(self, place, rows, width, sums):
+        self.place, self.rows, self.width, self.sums = place, rows, width, sums
+        self.counts, self.smalls = (0,) * 4, (False,) * 4
+        self.kept, self.small_kept = [None] * 3, [None] * 3
+        self.came = self.came_z = self.totals = None
+        self.shares, self.others, self.small_share = [], [], None
+        self.squares = jnp.zeros((1, width), FULL)
+        self.flying, self.swapping = [], 0
+
+    def step(self, chunk, *ties, small=None):
         rows, width = self.rows, self.width
         new, once, twice, done = counts = (len(chunk),) + self.counts[:3]
+        smalls = (small is not None,) + self.smalls[:3]
+        last = not (new or once or twice)
         arrays, jobs = [], []
 
         def number(spec):
@@ -546,74 +697,93 @@
                 jobs.append(
                     [(a, b, [(number(l), number(r)) for l, r in ps]) for a, b, ps in tile]
                 )
+        small_job = None
+        if small is not None:
+            products, norms, norms_came = small
+            small_job = [(number(l), number(r)) for l, r in products]
+            small_job = (small_job, number((norms,))[0], number((norms_came,))[0])
         ins = list(arrays)
-        if once:
-            ins.append(self.kept[0])
-        if twice:
-            ins.append(self.kept[1])
+        for stage in range(2):
+            ins += [self.kept[stage]] * (counts[1 + stage] > 0)
+            ins += [self.small_kept[stage]] * smalls[1 + stage]
         if once or twice:
             ins += self.came
         if done:
-            ins += [self.kept[2]] + self.came_z
+            ins += [self.kept[2]] + [self.small_kept[2]] * smalls[3] + self.came_z + [self.squares]
+        ins += [self.sums] * last
         outs = []
         if new or once:
-            outs += [(((new * 8 + once * 4) * rows, width), LOW)] * 2
-        if new:
-            outs.append(((new, 2, 8 * rows, width), FULL))
-        if once:
-            outs.append(((once, 2, 4 * rows, width), FULL))
+            for added in (64 * smalls[0], 64 * smalls[1]):
+                outs.append((((new * 8 + once * 4) * rows + added, width), LOW))
+        for stage, blocks in enumerate((8, 4, 1)):
+            if counts[stage]:
+                outs.append(((counts[stage], 2, blocks * rows, width), FULL))
+            if smalls[stage]:
+                outs.append(((blocks * rows, SMALL), FULL))
         if twice:
-            outs.append(((twice, 2, rows, width), FULL))
-            outs += [((twice * 2 * rows, width), LOW)] * 3
+            outs += [((twice * 2 * rows + 16 * smalls[2], width), LOW)] * 3
         if done:
-            outs += [((done, 2, rows, width), FULL), ((1, width), FULL)]
+            outs.append(((done, 2, rows, width), FULL))
+            outs += [((rows, SMALL), FULL)] * smalls[3]
+            outs.append(((1, width), FULL))
+        outs += [((1, SMALL), FULL)] * last
         length = 2 * arrays[0].shape[-2] if new else 0
-        got = call(
-            functools.partial(round_kernel, jobs, len(arrays), counts),
-            self.place,
-            outs,
-            ins,
-            [],
-            [pltpu.VMEM((16 * rows, width), FULL)] if new else [],
-            4 * new * length * width * width,
+        scratch = [pltpu.VMEM((16 * rows, width), FULL)] if new else []
+        scratch += [pltpu.VMEM((16 * rows, SMALL), FULL)] * smalls[0]
+        got = list(
+            call(
+                functools.partial(
+                    round_kernel, jobs, small_job, len(arrays), counts, smalls, last
+                ),
+                self.place,
+                outs,
+                ins,
+                [],
+                scratch,
+                4 * new * length * width * width,
+            )
         )
-        self.flying, self.kept, self.counts = [], [None] * 3, counts
+        if last:
+            self.totals = got.pop()
         if done:
-            *got, share, square = got
-            self.squares.append(square)
-        if not (new or once or twice):
-            self.shares.append((share, swap_cores(share)))
+            self.squares = got.pop()
+            if smalls[3]:
+                self.small_share = got.pop()
+            self.shares.append(got.pop())
+        self.counts, self.smalls = counts, smalls
+        self.kept, self.small_kept = [None] * 3, [None] * 3
+        if last:
             return ties
-        got, ties = tie(list(got), ties)
-        if new or once:
-            self.flying += [across(got.pop(0), X, 16), across(got.pop(0), Y, 16)]
-        if new:
-            self.kept[0] = got.pop(0)
-        if once:
-            self.kept[1] = got.pop(0)
-        if twice:
-            self.kept[2] = got.pop(0)
-            self.flying += [across(got.pop(0), mask, 16) for mask in Z]
-        if done:
-            self.shares.append((share, swap_cores(share)))
+        got, ties = tie(got, ties)
+        to = [got.pop(0) for _ in range(2)] if new or once else []
+        for stage in range(3):
+            if counts[stage]:
+                self.kept[stage] = got.pop(0)
+            if smalls[stage]:
+                self.small_kept[stage] = got.pop(0)
+        self.flying = [across(v, mask, 16) for v, mask in zip(to, (X, Y))]
+        self.flying += [across(v, mask, 16) for v, mask in zip(got, Z)]
+        self.swapping = 0
+        while len(self.flying) < 5 and len(self.others) + self.swapping < len(self.shares):
+            self.flying.append(swap_cores(self.shares[len(self.others) + self.swapping]))
+            self.swapping += 1
         return ties
 
     def finish(self, *ties):
-        if self.counts[3]:
-            share, other = self.shares[-1]
-            self.flying.append(other)
         flying, ties = tie(self.flying, ties)
-        if self.counts[3]:
-            self.shares[-1] = (share, flying.pop())
         self.came = self.came_z = None
         if self.counts[0] or self.counts[1]:
             self.came, flying = flying[:2], flying[2:]
         if self.counts[2]:
-            self.came_z = flying
+            self.came_z, flying = flying[:3], flying[3:]
+        self.others += flying
         return ties
 
     def left(self):
         return any(self.counts[:3])
+
+    def swap_rest(self):
+        self.others += [swap_cores(v) for v in self.shares[len(self.others) :]]
 
 
 class PlainRounds:
@@ -642,20 +812,6 @@
 
     def left(self):
         return False
-
-
-def small_steps(value, place, size, rows):
-    (got,) = yield [swap_cores(value)]
-    value = (value + got).reshape(-1, 4, 2, 2, rows).transpose(1, 2, 3, 0, 4)
-    for bit in range(2):
-        axis = 2 - bit
-        send = lax.dynamic_index_in_dim(value, 1 - place[1 + bit], axis, keepdims=False)
-        keep = lax.dynamic_index_in_dim(value, place[1 + bit], axis, keepdims=False)
-        (got,) = yield [across(send, 1 << bit, size)]
-        value = keep + got
-    take = lambda xor: lax.dynamic_index_in_dim(value, place[3] ^ xor, 0, keepdims=False)
-    got = yield [across(take(mask // 4), mask, size) for mask in Z]
-    return take(0) + (got[0] + (got[1] + got[2]))
 
 
 def up_to_parts(expand_shard, size, rows, parts):
@@ -703,7 +859,7 @@
     width = rows * fsdp
     half = width // 2
     parts = shrink.shape[1] // rows
-    fast = fsdp == 16 and rows % 16 == 0
+    fast = fsdp == 16 and rows == 48
     core, index = lax.axis_index("dp"), lax.axis_index("fsdp")
     bit = lambda b: lax.rem(lax.div(index, b), 2)
     place = jnp.stack([core, bit(1), bit(2), lax.div(index, 4)]).astype(jnp.int32)
@@ -724,35 +880,33 @@
         [codon_table.astype(LOW), norm_params.astype(LOW).reshape(norms, rows)], 0
     )
     small = jnp.pad(small.T, ((0, 0), (0, -small.shape[0] % 128)))
-    sides = jnp.concatenate([small] + sum([tiles_of(l) for l in range(layers)], []), 1)
-    sides = lax.all_gather(sides, "fsdp", axis=0, tiled=True)
-    cut = small.shape[1]
-    small = sides[:, : V + norms].T
-    mixers, hiddens = [], []
-    for l in range(layers):
-        own = sides[:, cut : cut + 2 * width]
-        mixers.append((own, swap_cores(own)))
-        own = sides[:, cut + 2 * width : cut + 6 * width]
-        hiddens.append((own, swap_cores(own)))
-        cut += 6 * width
+    weights = jnp.concatenate([small] + sum([tiles_of(l) for l in range(layers)], []), 1)
+    weights = lax.all_gather(weights, ("fsdp", "dp"), axis=0, tiled=True)
+    weights = weights.reshape(fsdp, 2, rows, -1)
+    if not fast:
+        weights = weights.transpose(1, 0, 2, 3).reshape(1, 2, width, -1)
+    small = weights[:, 0, :, : V + norms].reshape(width, V + norms).T
+    base = lambda l: weights.shape[3] - (layers - l) * 6 * width
     table_low = small[:V]
     gains = small[V:].astype(FULL).reshape(-1, 2, width)
 
     cosine, sine = rotary_tables(length)
     vocab_ids = jnp.arange(V, dtype=jnp.int32)
-    chosen = (inputs[:, None] == vocab_ids[None, :]).astype(LOW)
-    resid = dot(chosen, table_low)
+    chosen = (inputs[:, None] == jnp.arange(SMALL, dtype=jnp.int32)[None, :]).astype(LOW)
+    resid = dot(chosen, jnp.pad(table_low, ((0, SMALL - V), (0, 0))))
     kept = []
     for l in range(layers):
         gain = gains[2 * l : 2 * l + 2]
         middle, query, keys, values, lse, pack = attention_forward(
-            place, resid, mixers[l], gain[0], cosine, sine, segments
+            place, resid, weights, base(l), gain[0], cosine, sine, segments
         )
         if l > 0:
             middle, came = tie(middle, kept[-1][-1])
             kept[-1] = kept[-1][:-1] + (came,)
         pack_came = swap_cores(pack)
-        output, active, pack_mid, hidden = hidden_forward(place, middle, hiddens[l], gain[1])
+        output, active, pack_mid, hidden = hidden_forward(
+            place, middle, weights, base(l), gain[1]
+        )
         output, pack_came = tie(output, pack_came)
         kept.append(
             (resid, query, keys, values, lse, pack, pack_came, middle, hidden, active, pack_mid)
@@ -769,8 +923,11 @@
     picked = jnp.sum(logits * targets, -1)
     loss_local = jnp.sum((lse_head[:, 0] - picked) * weight)
     grad_logits = ((jnp.exp(logits - lse_head) - targets) * weight[:, None]).astype(LOW)
-    grad_table = cross(grad_logits, head_in)
     grad_head = dot(grad_logits, table_low)
+    grad_logits = jnp.pad(grad_logits, ((0, 0), (0, SMALL - V)))
+    early = (head_in, grad_logits, chosen)
+    early_came = [swap_cores(v) for v in early]
+    sums = jnp.pad(jnp.stack([loss_local, jnp.sum(weight)]), (0, SMALL - 2))[None]
     grad, grad_final_gain, grad_final_bias = normalize_back(
         grad_head, unit_out, inverse_out, final_gain[0]
     )
@@ -779,7 +936,7 @@
     grad, branch, came = tie(grad, branch, kept[-1][-1])
     kept[-1] = kept[-1][:-1] + (came,)
 
-    rounds = Rounds(place, rows, width) if fast else PlainRounds()
+    rounds = Rounds(place, rows, width, sums) if fast else PlainRounds()
     whole = lambda array, i=None: (array, i, None, None)
     tile = lambda left, right, other_left, other_right: [
         (0, width, [(left, right), (other_left, other_right)])
@@ -799,9 +956,11 @@
         )
         grad, branch = rounds.step(chunk, grad, branch)
         grad_middle, gains_mid, up_own, up_other = hidden_back(
-            place, grad, branch, middle, hidden, hiddens[l], gain[1]
+            place, grad, branch, middle, hidden, weights, base(l), gain[1]
         )
-        grad_middle, up_own, up_other = rounds.finish(grad_middle, up_own, up_other)
+        grad_middle, up_own, up_other, early_came = rounds.finish(
+            grad_middle, up_own, up_other, early_came
+        )
         up_came = swap_cores(up_other)
         (grad_middle,) = rounds.step(
             [
@@ -815,7 +974,7 @@
             grad_middle,
         )
         grad, branch, gains_in, mix_own, mix_other = attention_back(
-            place, grad_middle, resid, mixers[l], gain[0], cosine, sine, segments,
+            place, grad_middle, resid, weights, base(l), gain[0], cosine, sine, segments,
             query, keys, values, lse,
         )
         grad_norms = [gains_in, gains_mid] + grad_norms
@@ -831,59 +990,66 @@
                 [(0, half, products(0, 0, half)), (half, width, products(1, half, width))],
             ]
         ]
-    grad_table = grad_table + cross(chosen, branch)
-    grad_small = jnp.concatenate([grad_table] + grad_norms, 0)
+    norm_rows = -(-norms // 16) * 16
+    grad_norms = jnp.concatenate(grad_norms + [jnp.zeros((norm_rows - norms, width), FULL)], 0)
+    branch_came, norms_came = swap_cores(branch), swap_cores(grad_norms)
+    products = [(whole(early[0]), whole(early[1])), (whole(early_came[0]), whole(early_came[1]))]
+    products += [(whole(branch), whole(early[2])), (whole(branch_came), whole(early_came[2]))]
     if fast:
-        steps = small_steps(grad_small, place, fsdp, rows)
-        messages = steps.send(next(steps))
-        rounds.step(chunk)
-        share_small = None
-        while rounds.left() or share_small is None:
-            ((messages,),) = (rounds.finish(messages),)
-            try:
-                messages = steps.send(messages) if share_small is None else []
-            except StopIteration as end:
-                share_small, messages = end.value, []
-            if rounds.left():
-                rounds.step([])
+        rounds.step(chunk, small=(products, grad_norms, norms_came))
+        while rounds.left():
+            rounds.finish()
+            rounds.step([])
+        rounds.swap_rest()
+        share_small = rounds.small_share
+        small_other = swap_cores(share_small)
+        totals, rest = tie(rounds.totals, [rounds.others, small_other])
+        share_small = jnp.where(core == 0, share_small, small_other)
     else:
         rounds.step(chunk)
-        share_small = lax.psum_scatter(
-            grad_small + swap_cores(grad_small), "fsdp", scatter_dimension=1, tiled=True
+        table = sum(cross(l[0], r[0]) for l, r in products)
+        table = table + jnp.pad((grad_norms + norms_came).T, ((0, 0), (V, SMALL - V - norm_rows)))
+        table = jnp.where(core == 0, table, swap_cores(table))
+        share_small = lax.psum_scatter(table, "fsdp", scatter_dimension=0, tiled=True)
+        squares = jnp.sum(share_small * share_small) * (core == 0)
+        for value in rounds.squares:
+            squares = squares + jnp.sum(value)
+        totals = sums + jnp.where(jnp.arange(SMALL) == 2, squares, 0.0)[None]
+    totals = total_of(totals, fsdp)
+    loss_sum, count, square_total = totals[0, 0], totals[0, 1], totals[0, 2]
+    share_small = share_small[:, : V + norms].T
+
+    shares = list(zip(rounds.shares, rounds.others)) if fast else rounds.shares
+    places = [(2 * (layers - 1 - l), 0 if l == layers - 1 else 1) for l in range(layers)]
+
+    def tiles_at(chunk, pair):
+        own, other = (v[pair] for v in shares[chunk])
+        ordered = (jnp.where(core == 0, own, other), jnp.where(core == 0, other, own))
+        return [v[s] for v in ordered for s in range(2)]
+
+    share_up = jnp.stack(
+        [
+            up_from_parts(jnp.concatenate(tiles_at(at + 1, 0), 1), fsdp, rows, parts)
+            for at, _ in places
+        ]
+    )
+    share_small = (share_small[:V], share_small[V:].reshape(-1, 2, rows))
+    if not fast:
+        share_in, share_out, share_down = [], [], []
+        side = lambda *values: jnp.concatenate(values, 1)
+        for at, pair in places:
+            a_0, b_0, a_1, b_1 = tiles_at(at + 2, 0)
+            share_in.append(
+                side(
+                    a_0[:, :half], a_1[:, :half], a_0[:, half:],
+                    a_1[:, half:], b_0[:, :half], b_1[:, :half],
+                )
+            )
+            share_out.append(side(b_0[:, half:], b_1[:, half:]))
+            share_down.append(jnp.concatenate(tiles_at(at, pair), 0))
+        share_in, share_out, share_down = (
+            jnp.stack(v) for v in (share_in, share_out, share_down)
         )
-
-    squares = 0.5 * jnp.sum(share_small * share_small)
-    for value in rounds.squares:
-        squares = squares + jnp.sum(value)
-    totals = jnp.stack([loss_local, jnp.sum(weight), squares])
-    totals = total_of(jnp.pad(totals, (0, 125))[None], fsdp)
-    loss_sum, count, square_total = totals[0, 0], totals[0, 1], totals[0, 2]
-
-    both = []
-    for share, other in rounds.shares:
-        first = core == 0
-        both.append((jnp.where(first, share, other), jnp.where(first, other, share)))
-    share_in, share_out, share_up, share_down = ([None] * layers for _ in range(4))
-    side = lambda *values: jnp.concatenate(values, 1)
-    for l in range(layers):
-        at = 2 * (layers - 1 - l)
-        down, up, mix = (at, at and 1), (at + 1, 0), (at + 2, 0)
-        tiles = lambda where: [both[where[0]][c][where[1], s] for c in range(2) for s in range(2)]
-        a_0, b_0, a_1, b_1 = tiles(mix)
-        share_in[l] = side(
-            a_0[:, :half], a_1[:, :half], a_0[:, half:], a_1[:, half:], b_0[:, :half], b_1[:, :half]
-        )
-        share_out[l] = side(b_0[:, half:], b_1[:, half:])
-        share_up[l] = up_from_parts(side(*tiles(up)), fsdp, rows, parts)
-        share_down[l] = jnp.concatenate(tiles(down), 0)
-    group = (
-        jnp.stack(share_in),
-        jnp.stack(share_out),
-        jnp.stack(share_up),
-        jnp.stack(share_down),
-        share_small[:V],
-        share_small[V:].reshape(-1, 2, rows),
-    )
     grad_norm = jnp.sqrt(square_total) / count
     factor = CLIP / jnp.maximum(grad_norm, CLIP)
     masters = (inward, outward, expand, shrink, codon_table, norm_params)
@@ -896,15 +1062,27 @@
         table_second,
         norm_second,
     )
-    result = [loss_sum, count, grad_norm]
-    for index in range(6):
-        rate = RATE_VECTOR if index == 5 else RATE_MATRIX
-        decay = 0.0 if index == 5 else DECAY
-        clipped = group[index] / count * factor
-        result.extend(
+    if fast:
+        matrices = [v for group in zip(masters[:4], firsts[:4], seconds[:4]) for v in group]
+        chunks = [((at + 2, 0), (at, pair)) for at, pair in places]
+        own, other = zip(*shares)
+        scale = jnp.stack([count, factor])
+        values = list(optimizer(place, scale, chunks, own, other, share_up, matrices))
+    else:
+        values = []
+        for index, grad in enumerate((share_in, share_out, share_up, share_down)):
+            clipped = grad / count * factor
+            values.extend(
+                adam_step(
+                    masters[index], clipped, firsts[index], seconds[index], RATE_MATRIX, DECAY
+                )
+            )
+    for index, rate, decay in ((4, RATE_MATRIX, DECAY), (5, RATE_VECTOR, 0.0)):
+        clipped = share_small[index - 4] / count * factor
+        values.extend(
             adam_step(masters[index], clipped, firsts[index], seconds[index], rate, decay)
         )
-    return tuple(result)
+    return (loss_sum, count, grad_norm, *values)
 
 
 def solution(mesh):

time: 664 us -> 605 us (0.911); the launches traced: 653 us -> 601 us
  local copies, waits for them, and re-layouts: 75.6 us -> 37 us
  Pallas kernels: 207 us -> 230 us
  other arithmetic: 43.9 us -> 22.6 us
    slice x12 -> x6, local copies, waits for them, and re-layouts: 17.3 us -> 1.04 us  [the longest x1 0.95 us: body(): small = weights[:, 0, :, :V + norms].reshape(width, V + norms).T]
    sub x6 -> x2, other arithmetic: 16 us -> 1.91 us  [adam_step(): return (master - rate * update, first, second)]
    pallas_call x16, Pallas kernels: 207 us -> 219 us  [call(): pl.pallas_call(kernel, out_shape=[jax.ShapeDtypeStruct(s, t) for s, t in...]
    pallas_call x0 -> x1, Pallas kernels: none -> 10.9 us  [optimizer(): pl.pallas_call(functools.partial(optimizer_kernel, chunks, up.shape[0]),...]
    unnamed x174 -> x164, local copies, waits for them, and re-layouts: 25.3 us -> 14.9 us
    ppermute x36 -> x33, waiting for transfers between devices: 57 us -> 52.2 us  [across(): return lax.ppermute(value, 'fsdp', [(i, i ^ mask) for i in range(size)])]
    ppermute x36 -> x33, starting transfers between devices: 50.3 us -> 47.6 us  [across(): return lax.ppermute(value, 'fsdp', [(i, i ^ mask) for i in range(size)])]
    ppermute x21 -> x22, waiting for transfers between devices: 14.7 us -> 14.6 us  [swap_cores(): return lax.ppermute(value, 'dp', [(0, 1), (1, 0)])]
  transfers between devices with their start and end apart: 58 -> 56, of which waited for: 15 -> 16; matrix products, arithmetic and copies ran while one was open for 11% -> 5% of each run, Pallas kernels for 24% -> 24%
where the time goes in v6:
time: 605 us; the launch traced here: 601 us
  waiting for transfers between devices  237 us (39%)
  Pallas kernels  230 us (38%)
  starting transfers between devices  52.3 us (9%)
  local copies, waits for them, and re-layouts  37 us (6%)
  other arithmetic  22.6 us (4%)
  between operations  18.2 us (3%)
    pallas_call x16, Pallas kernels, call(): pl.pallas_call(kernel, out_shape=[jax.ShapeDtypeStruct(s, t) for s, t in...  219 us
    all_gather x1, waiting for transfers between devices, body(): weights = lax.all_gather(weights, ('fsdp', 'dp'), axis=0, tiled=True)  171 us
    ppermute x33, waiting for transfers between devices, across(): return lax.ppermute(value, 'fsdp', [(i, i ^ mask) for i in range(size)])  52.2 us
    ppermute x33, starting transfers between devices, across(): return lax.ppermute(value, 'fsdp', [(i, i ^ mask) for i in range(size)])  47.6 us
    unnamed x164, local copies, waits for them, and re-layouts  14.9 us
    ppermute x22, waiting for transfers between devices, swap_cores(): return lax.ppermute(value, 'dp', [(0, 1), (1, 0)])  14.6 us
  transfers between devices with their start and end apart: 56, of which 16 were waited for; matrix products, arithmetic and copies ran while one was open for 5% of the time, Pallas kernels for 24%

profile of v6, /device:TPU:0, one launch (start us, length us, event | category | flops | bytes accessed | tf_op | source)
XLA Modules:
  0.0 601.1 jit_solution(5576629648826551956)
XLA Ops:
  7.3 1.3 convert.16
  11.3 2.1 reshape.175
  15.4 1.4 reshape.176
  22.4 1.3 pad_maximum_fusion.1
  23.7 170.6 %all-gather.2.cloned.1.call-done = bf16[1536,9344]{1,0:T(8,128)(2,1)} async-done(((bf16[48,9344]{1,0:T(8,128)(2,1)}), bf16[1536,9344]{1,0:T(8,128)(2,1)}) %all-gather.2.cloned.1.call-update) | async-done | bytes 28704784 | tf_op jit(solution)/shard_map/all_gather | solution.py:884
  196.1 1.5 fusion.3.resid
  197.6 17.7 %shard_map.364 = (f32[512,768]{1,0:T(8,128)}, bf16[512,768]{1,0:T(8,128)(2,1)}, bf16[512,768]{1,0:T(8,128)(2,1)}, bf16[512,768]{1,0:T(8,128)(2,1)}, f32[512,128]{1,0:T(8,128)}, /*index=5*/bf16[2,512,768]{2,1,0:T(8,128)(2,1)}) custom-call(s32[4]{0:T(128)} %pad_add_fusion.place_of.refs_0_, f32[512,768]{1,0:T(8,128)} %fusion.3.resid, s32[512,1]{1,0:T(8,128)} %copy.86.seg_col, ...), custom_call_target="tpu_custom_call" | custom-call | flops 3221225472 | bytes 30812160 | tf_op jit(solution)/shard_map/pallas_call | solution.py:77
  215.6 13.2 %shard_map.365 = (f32[512,768]{1,0:T(8,128)}, bf16[2,512,768]{2,1,0:T(8,128)(2,1)}, bf16[3,512,768]{2,1,0:T(8,128)(2,1)}, f32[4,512,768]{2,1,0:T(8,128)}) custom-call(s32[4]{0:T(128)} %pad_add_fusion.place_of.refs_0_, f32[512,768]{1,0:T(8,128)} %get-tuple-element.236.middle, f32[2,768]{1,0:T(2,128)} %get-tuple-element.494.gains, ...), custom_call_target="tpu_custom_call" | custom-call | flops 4831838208 | bytes 30283776 | tf_op jit(solution)/shard_map/pallas_call | solution.py:77
  229.2 26.7 %shard_map.366 = (f32[512,768]{1,0:T(8,128)}, bf16[512,768]{1,0:T(8,128)(2,1)}, bf16[512,768]{1,0:T(8,128)(2,1)}, bf16[512,768]{1,0:T(8,128)(2,1)}, f32[512,128]{1,0:T(8,128)}, /*index=5*/bf16[2,512,768]{2,1,0:T(8,128)(2,1)}) custom-call(s32[4]{0:T(128)} %pad_add_fusion.place_of.refs_0_, f32[512,768]{1,0:T(8,128)} %get-tuple-element.239.resid, ...), custom_call_target="tpu_custom_call" | custom-call | flops 3221225472 | bytes 30812160 | tf_op jit(solution)/shard_map/pallas_call | solution.py:77
  256.3 14.2 %shard_map.367 = (f32[512,768]{1,0:T(8,128)}, bf16[2,512,768]{2,1,0:T(8,128)(2,1)}, bf16[3,512,768]{2,1,0:T(8,128)(2,1)}, f32[4,512,768]{2,1,0:T(8,128)}) custom-call(s32[4]{0:T(128)} %pad_add_fusion.place_of.refs_0_, f32[512,768]{1,0:T(8,128)} %get-tuple-element.242.middle, f32[2,768]{1,0:T(2,128)} %get-tuple-element.492.gains, ...), custom_call_target="tpu_custom_call" | custom-call | flops 4831838208 | bytes 30283776 | tf_op jit(solution)/shard_map/pallas_call | solution.py:77
  272.0 1.6 reduce_sum.90
  275.9 1.3 multiply_reduce_fusion
  277.2 1.7 fusion.25
  279.5 1.8 collective-permute-done.4.refs_4_
  282.1 7.3 %shard_map.368 = (bf16[384,768]{1,0:T(8,128)(2,1)}, bf16[384,768]{1,0:T(8,128)(2,1)}, f32[1,2,384,768]{3,2,1,0:T(8,128)}) custom-call(s32[4]{0:T(128)} %pad_add_fusion.place_of.refs_0_, bf16[2,512,768]{2,1,0:T(8,128)(2,1)} %get-tuple-element.244.refs_1_, bf16[512,768]{1,0:T(8,128)(2,1)} %copy-done.4, bf16[3,512,768]{2,1,0:T(8,128)(2,1)} %collective-permute-done.3.refs_3_, ...), custom_call_target="tpu_custom_call" | custom-call | flops 2415919104 | bytes 5505024 | tf_op jit(solution)/shard_map/pallas_call | solution.py:77
  289.4 1.4 collective-permute-start.5
  292.3 17.3 %shard_map.369 = (f32[512,768]{1,0:T(8,128)}, f32[2,768]{1,0:T(2,128)}, bf16[2,512,768]{2,1,0:T(8,128)(2,1)}, bf16[2,512,768]{2,1,0:T(8,128)(2,1)}) custom-call(s32[4]{0:T(128)} %pad_add_fusion.place_of.refs_0_, f32[512,768]{1,0:T(8,128)} %get-tuple-element.255.grad, bf16[512,768]{1,0:T(8,128)(2,1)} %copy-done.4, f32[512,768]{1,0:T(8,128)} %get-tuple-element.242.middle, ...), custom_call_target="tpu_custom_call" | custom-call | flops 4831838208 | bytes 38934528 | tf_op jit(solution)/shard_map/pallas_call | solution.py:77
  310.3 3.6 collective-permute-done.10.refs_4_
  315.1 9.6 %shard_map.370 = (bf16[576,768]{1,0:T(8,128)(2,1)}, bf16[576,768]{1,0:T(8,128)(2,1)}, f32[1,2,384,768]{3,2,1,0:T(8,128)}, f32[1,2,192,768]{3,2,1,0:T(8,128)}) custom-call(s32[4]{0:T(128)} %pad_add_fusion.place_of.refs_0_, bf16[3,512,768]{2,1,0:T(8,128)(2,1)} %get-tuple-element.243.refs_1_, bf16[2,512,768]{2,1,0:T(8,128)(2,1)} %get-tuple-element.261.refs_2_, ...), custom_call_target="tpu_custom_call" | custom-call | flops 2415919104 | bytes 11403264 | tf_op jit(solution)/shard_map/pallas_call | solution.py:77
  324.7 1.5 collective-permute-start.11
  327.6 22.6 %shard_map.371 = (f32[512,768]{1,0:T(8,128)}, bf16[512,768]{1,0:T(8,128)(2,1)}, f32[2,768]{1,0:T(2,128)}, bf16[2,512,768]{2,1,0:T(8,128)(2,1)}, bf16[2,512,768]{2,1,0:T(8,128)(2,1)}) custom-call(s32[4]{0:T(128)} %pad_add_fusion.place_of.refs_0_, f32[512,768]{1,0:T(8,128)} %get-tuple-element.273.grad_middle, f32[512,768]{1,0:T(8,128)} %get-tuple-element.239.resid, ...), custom_call_target="tpu_custom_call" | custom-call | flops 4429185024 | bytes 34768896 | tf_op jit(solution)/shard_map/pallas_call | solution.py:77
  350.8 4.2 collective-permute-done.14.refs_8_
  356.5 15.2 %shard_map.372 = (bf16[960,768]{1,0:T(8,128)(2,1)}, bf16[960,768]{1,0:T(8,128)(2,1)}, f32[2,2,384,768]{3,2,1,0:T(8,128)}, f32[1,2,192,768]{3,2,1,0:T(8,128)}, f3...) custom-call(s32[4]{0:T(128)} %pad_add_fusion.place_of.refs_0_, ...), custom_call_target="tpu_custom_call" | custom-call | flops 4831838208 | bytes 17104896 | tf_op jit(solution)/shard_map/pallas_call | solution.py:77
  371.7 1.5 collective-permute-start.15
  373.8 1.9 collective-permute-start.18
  375.7 2.5 collective-permute-start.19
  378.2 17.7 %shard_map.373 = (f32[512,768]{1,0:T(8,128)}, f32[2,768]{1,0:T(2,128)}, bf16[2,512,768]{2,1,0:T(8,128)(2,1)}, bf16[2,512,768]{2,1,0:T(8,128)(2,1)}) custom-call(s32[4]{0:T(128)} %pad_add_fusion.place_of.refs_0_, f32[512,768]{1,0:T(8,128)} %get-tuple-element.306.grad, bf16[512,768]{1,0:T(8,128)(2,1)} %get-tuple-element.307.refs_6_.branch, ...), custom_call_target="tpu_custom_call" | custom-call | flops 4831838208 | bytes 38934528 | tf_op jit(solution)/shard_map/pallas_call | solution.py:77
  395.9 10.4 %collective-permute-done.15.refs_7_ = bf16[960,768]{1,0:T(8,128)(2,1)S(1)} collective-permute-done((bf16[960,768]{1,0:T(8,128)(2,1)}, bf16[960,768]{1,0:T(8,128)(2,1)S(1)}, u32[]{:S(2)}, u32[]{:S(2)}) %collective-permute-start.15) | collective-permute-done | bytes 1474592 | tf_op jit(solution)/shard_map/ppermute | solution.py:496
  407.4 3.6 collective-permute-done.20.refs_4_
  412.2 12.2 %shard_map.374 = (bf16[768,768]{1,0:T(8,128)(2,1)}, bf16[768,768]{1,0:T(8,128)(2,1)}, f32[1,2,384,768]{3,2,1,0:T(8,128)}, f32[2,2,192,768]{3,2,1,0:T(8,128)}, f3...) custom-call(s32[4]{0:T(128)} %pad_add_fusion.place_of.refs_0_, ...), custom_call_target="tpu_custom_call" | custom-call | flops 2415919104 | bytes 17452032 | tf_op jit(solution)/shard_map/pallas_call | solution.py:77
  425.1 1.5 collective-permute-start.22
  427.3 1.9 collective-permute-start.24
  429.2 2.5 collective-permute-start.25
  431.7 22.8 %shard_map.375 = (f32[512,768]{1,0:T(8,128)}, bf16[512,768]{1,0:T(8,128)(2,1)}, f32[2,768]{1,0:T(2,128)}, bf16[2,512,768]{2,1,0:T(8,128)(2,1)}, bf16[2,512,768]{2,1,0:T(8,128)(2,1)}) custom-call(s32[4]{0:T(128)} %pad_add_fusion.place_of.refs_0_, f32[512,768]{1,0:T(8,128)} %get-tuple-element.339.grad_middle, f32[512,768]{1,0:T(8,128)} %fusion.3.resid, ...), custom_call_target="tpu_custom_call" | custom-call | flops 4429185024 | bytes 34768896 | tf_op jit(solution)/shard_map/pallas_call | solution.py:77
  456.8 2.7 concatenate.44.refs_13_
  459.6 1.4 collective-permute-done.28.refs_14_
  462.4 13.2 %shard_map.376 = (bf16[640,768]{1,0:T(8,128)(2,1)}, bf16[576,768]{1,0:T(8,128)(2,1)}, f32[1,2,384,768]{3,2,1,0:T(8,128)}, f32[384,128]{1,0:T(8,128)}, f32[1,2,19...) custom-call(s32[4]{0:T(128)} %pad_add_fusion.place_of.refs_0_, ...), custom_call_target="tpu_custom_call" | custom-call | flops 2415919104 | bytes 17878016 | tf_op jit(solution)/shard_map/pallas_call | solution.py:77
  476.3 1.4 collective-permute-start.30
  477.7 1.9 collective-permute-start.32
  479.7 2.4 collective-permute-start.33
  482.1 9.7 %collective-permute-done.31.refs_7_ = bf16[192,768]{1,0:T(8,128)(2,1)S(1)} collective-permute-done((bf16[192,768]{1,0:T(8,128)(2,1)}, bf16[192,768]{1,0:T(8,128)(2,1)S(1)}, u32[]{:S(2)}, u32[]{:S(2)}) %collective-permute-start.31) | collective-permute-done | bytes 294944 | tf_op jit(solution)/shard_map/ppermute | solution.py:496
  491.9 9.5 %collective-permute-done.32.refs_8_ = bf16[192,768]{1,0:T(8,128)(2,1)S(1)} collective-permute-done((bf16[192,768]{1,0:T(8,128)(2,1)}, bf16[192,768]{1,0:T(8,128)(2,1)S(1)}, u32[]{:S(2)}, u32[]{:S(2)}) %collective-permute-start.32) | collective-permute-done | bytes 294944 | tf_op jit(solution)/shard_map/ppermute | solution.py:496
  502.8 4.9 shard_map.377
  508.3 1.5 collective-permute-start.34
  509.8 5.4 collective-permute-start.36
  515.5 2.1 collective-permute-start.38
  517.6 2.3 collective-permute-done.36.refs_6_
  519.8 7.5 %collective-permute-done.37.refs_7_ = bf16[96,768]{1,0:T(8,128)(2,1)S(1)} collective-permute-done((bf16[96,768]{1,0:T(8,128)(2,1)}, bf16[96,768]{1,0:T(8,128)(2,1)S(1)}, u32[]{:S(2)}, u32[]{:S(2)}) %collective-permute-start.37) | collective-permute-done | bytes 147488 | tf_op jit(solution)/shard_map/ppermute | solution.py:496
  528.3 2.8 shard_map.378
  531.1 2.6 collective-permute-start.39
  533.8 2.4 collective-permute-start.41
  536.1 1.9 fusion.17.refs_7_
  539.6 8.6 %collective-permute-done.40.refs_4_ = bf16[112,768]{1,0:T(8,128)(2,1)S(1)} collective-permute-done((bf16[112,768]{1,0:T(8,128)(2,1)}, bf16[112,768]{1,0:T(8,128)(2,1)S(1)}, u32[]{:S(2)}, u32[]{:S(2)}) %collective-permute-start.40) | collective-permute-done | bytes 172064 | tf_op jit(solution)/shard_map/ppermute | solution.py:496
  549.0 2.0 shard_map.379
  552.4 1.9 maximum_bitcast_fusion.1
  554.4 1.8 stack_reshape.7
  559.8 1.2 collective-permute-start.50
  561.0 1.5 collective-permute-start.51
  562.5 3.0 maximum_bitcast_fusion
  565.5 1.8 stack_reshape.6
  567.5 3.2 collective-permute-start.52
  570.7 2.4 collective-permute-start.54
  578.9 1.3 multiply_subtract_fusion
  582.0 10.9 %shard_map.380 = (f32[2,48,2304]{2,1,0:T(8,128)}, f32[2,48,2304]{2,1,0:T(8,128)}, f32[2,48,2304]{2,1,0:T(8,128)}, f32[2,48,768]{2,1,0:T(8,128)}, f32[2,48,768]{2...) custom-call(s32[4]{0:T(128)} %pad_add_fusion.place_of.refs_0_, ...), custom_call_target="tpu_custom_call" | custom-call | flops 53084160 | bytes 21233664 | tf_op jit(solution)/shard_map/pallas_call | solution.py:477
  (321 shorter events, 49.8 us)
Async XLA Ops:
  7.2 187.1 %all-gather.2.cloned.1.call-start = ((), (), s32[]{:S(2)}) async-start(), calls=%async_computation | async-start | bytes 29601792 | tf_op jit(solution)/shard_map/all_gather | solution.py:884
  215.3 13.9 %collective-permute-start = (bf16[2,512,768]{2,1,0:T(8,128)(2,1)}, bf16[2,512,768]{2,1,0:T(8,128)(2,1)S(1)}, u32[]{:S(2)}, u32[]{:S(2)}) collective-permute-start(bf16[2,512,768]{2,1,0:T(8,128)(2,1)} %get-tuple-element.235.refs_1_), channel_id=1, source_target_pairs={{0,1},{1,0},{2,3},{3,2},{4,5},{5,4},{6,7},{7,6},{8,9},{9,8},{10,11... | collective-permute-start | bytes 4718600 | tf_op jit(solution)/shard_map/ppermute | solution.py:492
  228.9 27.4 %collective-permute-start.1 = (bf16[3,512,768]{2,1,0:T(8,128)(2,1)}, bf16[3,512,768]{2,1,0:T(8,128)(2,1)S(1)}, u32[]{:S(2)}, u32[]{:S(2)}) collective-permute-start(bf16[3,512,768]{2,1,0:T(8,128)(2,1)} %get-tuple-element.237.refs_1_), channel_id=1, source_target_pairs={{0,1},{1,0},{2,3},{3,2},{4,5},{5,4},{6,7},{7,6},{8,9},{9,8},{10,11... | collective-permute-start | bytes 7077896 | tf_op jit(solution)/shard_map/ppermute | solution.py:492
  229.2 26.7 %copy-start.6 = (bf16[2,512,768]{2,1,0:T(8,128)(2,1)}, bf16[2,512,768]{2,1,0:T(8,128)(2,1)S(1)}, u32[]{:S(2)}) copy-start(bf16[2,512,768]{2,1,0:T(8,128)(2,1)S(1)} %collective-permute-done.refs_3_) | copy-start | bytes 4718596
  255.9 14.9 %collective-permute-start.2 = (bf16[2,512,768]{2,1,0:T(8,128)(2,1)}, bf16[2,512,768]{2,1,0:T(8,128)(2,1)S(1)}, u32[]{:S(2)}, u32[]{:S(2)}) collective-permute-start(bf16[2,512,768]{2,1,0:T(8,128)(2,1)} %get-tuple-element.240.refs_1_), channel_id=1, source_target_pairs={{0,1},{1,0},{2,3},{3,2},{4,5},{5,4},{6,7},{7,6},{8,9},{9,8},{10,11... | collective-permute-start | bytes 4718600 | tf_op jit(solution)/shard_map/ppermute | solution.py:492
  270.5 8.5 %collective-permute-start.3 = (bf16[3,512,768]{2,1,0:T(8,128)(2,1)}, bf16[3,512,768]{2,1,0:T(8,128)(2,1)}, u32[]{:S(2)}, u32[]{:S(2)}) collective-permute-start(bf16[3,512,768]{2,1,0:T(8,128)(2,1)} %get-tuple-element.243.refs_1_), channel_id=1, source_target_pairs={{0,1},{1,0},{2,3},{3,2},{4,5},{5,4},{6,7},{7,6},{8,9},{9,8},{10,11... | collective-permute-start | bytes 7077896 | tf_op jit(solution)/shard_map/ppermute | solution.py:492
  279.0 2.3 collective-permute-start.4
  279.2 30.5 %collective-permute-start.7 = (bf16[512,768]{1,0:T(8,128)(2,1)S(1)}, bf16[512,768]{1,0:T(8,128)(2,1)S(1)}, u32[]{:S(2)}, u32[]{:S(2)}) collective-permute-start(bf16[512,768]{1,0:T(8,128)(2,1)S(1)} %add_convert_fusion.refs_5_), channel_id=1, source_target_pairs={{0,1},{1,0},{2,3},{3,2},{4,5},{5,4},{6,7},{7,6},{8,9},{9,8},{10,11... | collective-permute-start | bytes 2359304 | tf_op jit(solution)/shard_map/ppermute | solution.py:492
  289.4 20.3 %collective-permute-start.5 = (bf16[384,768]{1,0:T(8,128)(2,1)}, bf16[384,768]{1,0:T(8,128)(2,1)S(1)}, u32[]{:S(2)}, u32[]{:S(2)}) collective-permute-start(bf16[384,768]{1,0:T(8,128)(2,1)} %get-tuple-element.253), channel_id=1, source_target_pairs={{0,2},{2,0},{4,6},{6,4},{8,10},{10,8},{12,14},{14,12},{16,18},{18,... | collective-permute-start | bytes 1769480 | tf_op jit(solution)/shard_map/ppermute | solution.py:496
  290.9 18.9 %collective-permute-start.6 = (bf16[384,768]{1,0:T(8,128)(2,1)}, bf16[384,768]{1,0:T(8,128)(2,1)S(1)}, u32[]{:S(2)}, u32[]{:S(2)}) collective-permute-start(bf16[384,768]{1,0:T(8,128)(2,1)} %get-tuple-element.254), channel_id=1, source_target_pairs={{0,4},{2,6},{4,0},{6,2},{8,12},{10,14},{12,8},{14,10},{16,20},{18,... | collective-permute-start | bytes 1769480 | tf_op jit(solution)/shard_map/ppermute | solution.py:496
  291.6 18.0 %copy-start.28 = (bf16[512,128]{1,0:T(8,128)(2,1)}, bf16[512,128]{1,0:T(8,128)(2,1)S(1)}, u32[]{:S(2)}) copy-start(bf16[512,128]{1,0:T(8,128)(2,1)S(1)} %fusion.2.refs_10_) | copy-start | bytes 393220
  291.6 18.0 %collective-permute-start.9 = (bf16[512,128]{1,0:T(8,128)(2,1)S(1)}, bf16[512,128]{1,0:T(8,128)(2,1)S(1)}, u32[]{:S(2)}, u32[]{:S(2)}) collective-permute-start(bf16[512,128]{1,0:T(8,128)(2,1)S(1)} %fusion.2.refs_10_), channel_id=1, source_target_pairs={{0,1},{1,0},{2,3},{3,2},{4,5},{5,4},{6,7},{7,6},{8,9},{9,8},{10,11... | collective-permute-start | bytes 393224 | tf_op jit(solution)/shard_map/ppermute | solution.py:492
  291.7 17.9 %copy-start.29 = (bf16[512,128]{1,0:T(8,128)(2,1)}, bf16[512,128]{1,0:T(8,128)(2,1)S(1)}, u32[]{:S(2)}) copy-start(bf16[512,128]{1,0:T(8,128)(2,1)S(1)} %pad.18.refs_6_) | copy-start | bytes 393220
  291.7 17.9 %collective-permute-start.8 = (bf16[512,128]{1,0:T(8,128)(2,1)S(1)}, bf16[512,128]{1,0:T(8,128)(2,1)S(1)}, u32[]{:S(2)}, u32[]{:S(2)}) collective-permute-start(bf16[512,128]{1,0:T(8,128)(2,1)S(1)} %pad.18.refs_6_), channel_id=1, source_target_pairs={{0,1},{1,0},{2,3},{3,2},{4,5},{5,4},{6,7},{7,6},{8,9},{9,8},{10,11... | collective-permute-start | bytes 393224 | tf_op jit(solution)/shard_map/ppermute | solution.py:492
  310.3 16.5 %copy-start.38 = (f32[512,128]{1,0:T(8,128)S(1)}, f32[512,128]{1,0:T(8,128)}, u32[]{:S(2)}) copy-start(f32[512,128]{1,0:T(8,128)} %get-tuple-element.277) | copy-start | bytes 786436
  310.3 3.6 collective-permute-start.10
  324.7 25.4 %collective-permute-start.11 = (bf16[576,768]{1,0:T(8,128)(2,1)}, bf16[576,768]{1,0:T(8,128)(2,1)S(1)}, u32[]{:S(2)}, u32[]{:S(2)}) collective-permute-start(bf16[576,768]{1,0:T(8,128)(2,1)} %get-tuple-element.271), channel_id=1, source_target_pairs={{0,2},{2,0},{4,6},{6,4},{8,10},{10,8},{12,14},{14,12},{16,18},{18,... | collective-permute-start | bytes 2654216 | tf_op jit(solution)/shard_map/ppermute | solution.py:496
  326.3 23.9 %collective-permute-start.12 = (bf16[576,768]{1,0:T(8,128)(2,1)}, bf16[576,768]{1,0:T(8,128)(2,1)S(1)}, u32[]{:S(2)}, u32[]{:S(2)}) collective-permute-start(bf16[576,768]{1,0:T(8,128)(2,1)} %get-tuple-element.272), channel_id=1, source_target_pairs={{0,4},{2,6},{4,0},{6,2},{8,12},{10,14},{12,8},{14,10},{16,20},{18,... | collective-permute-start | bytes 2654216 | tf_op jit(solution)/shard_map/ppermute | solution.py:496
  350.2 4.8 collective-permute-start.13
  350.3 4.7 collective-permute-start.14
  371.7 34.6 %collective-permute-start.15 = (bf16[960,768]{1,0:T(8,128)(2,1)}, bf16[960,768]{1,0:T(8,128)(2,1)S(1)}, u32[]{:S(2)}, u32[]{:S(2)}) collective-permute-start(bf16[960,768]{1,0:T(8,128)(2,1)} %get-tuple-element.301), channel_id=1, source_target_pairs={{0,2},{2,0},{4,6},{6,4},{8,10},{10,8},{12,14},{14,12},{16,18},{18,... | collective-permute-start | bytes 4423688 | tf_op jit(solution)/shard_map/ppermute | solution.py:496
  373.2 34.3 %collective-permute-start.16 = (bf16[960,768]{1,0:T(8,128)(2,1)}, bf16[960,768]{1,0:T(8,128)(2,1)S(1)}, u32[]{:S(2)}, u32[]{:S(2)}) collective-permute-start(bf16[960,768]{1,0:T(8,128)(2,1)} %get-tuple-element.302), channel_id=1, source_target_pairs={{0,4},{2,6},{4,0},{6,2},{8,12},{10,14},{12,8},{14,10},{16,20},{18,... | collective-permute-start | bytes 4423688 | tf_op jit(solution)/shard_map/ppermute | solution.py:496
  373.8 22.1 %collective-permute-start.17 = (bf16[96,768]{1,0:T(8,128)(2,1)}, bf16[96,768]{1,0:T(8,128)(2,1)S(1)}, u32[]{:S(2)}, u32[]{:S(2)}) collective-permute-start(bf16[96,768]{1,0:T(8,128)(2,1)} %get-tuple-element.303), channel_id=1, source_target_pairs={{0,8},{2,10},{4,12},{6,14},{8,0},{10,2},{12,4},{14,6},{16,24},{18,... | collective-permute-start | bytes 442376 | tf_op jit(solution)/shard_map/ppermute | solution.py:496
  373.8 22.1 %collective-permute-start.18 = (bf16[96,768]{1,0:T(8,128)(2,1)}, bf16[96,768]{1,0:T(8,128)(2,1)S(1)}, u32[]{:S(2)}, u32[]{:S(2)}) collective-permute-start(bf16[96,768]{1,0:T(8,128)(2,1)} %get-tuple-element.304), channel_id=1, source_target_pairs={{0,16},{2,18},{4,20},{6,22},{8,24},{10,26},{12,28},{14,30},{16,0},... | collective-permute-start | bytes 442376 | tf_op jit(solution)/shard_map/ppermute | solution.py:496
  375.7 20.2 %collective-permute-start.19 = (bf16[96,768]{1,0:T(8,128)(2,1)}, bf16[96,768]{1,0:T(8,128)(2,1)S(1)}, u32[]{:S(2)}, u32[]{:S(2)}) collective-permute-start(bf16[96,768]{1,0:T(8,128)(2,1)} %get-tuple-element.305), channel_id=1, source_target_pairs={{0,24},{2,26},{4,28},{6,30},{8,16},{10,18},{12,20},{14,22},{16,8},... | collective-permute-start | bytes 442376 | tf_op jit(solution)/shard_map/ppermute | solution.py:496
  395.8 15.8 %copy-start.47 = (bf16[96,768]{1,0:T(8,128)(2,1)}, bf16[96,768]{1,0:T(8,128)(2,1)S(1)}, u32[]{:S(2)}) copy-start(bf16[96,768]{1,0:T(8,128)(2,1)S(1)} %collective-permute-done.17.refs_10_) | copy-start | bytes 442372
  407.4 3.6 collective-permute-start.20
  424.4 30.1 %collective-permute-start.21 = (bf16[768,768]{1,0:T(8,128)(2,1)}, bf16[768,768]{1,0:T(8,128)(2,1)S(1)}, u32[]{:S(2)}, u32[]{:S(2)}) collective-permute-start(bf16[768,768]{1,0:T(8,128)(2,1)} %get-tuple-element.334), channel_id=1, source_target_pairs={{0,2},{2,0},{4,6},{6,4},{8,10},{10,8},{12,14},{14,12},{16,18},{18,... | collective-permute-start | bytes 3538952 | tf_op jit(solution)/shard_map/ppermute | solution.py:496
  425.1 29.5 %collective-permute-start.22 = (bf16[768,768]{1,0:T(8,128)(2,1)}, bf16[768,768]{1,0:T(8,128)(2,1)S(1)}, u32[]{:S(2)}, u32[]{:S(2)}) collective-permute-start(bf16[768,768]{1,0:T(8,128)(2,1)} %get-tuple-element.335), channel_id=1, source_target_pairs={{0,4},{2,6},{4,0},{6,2},{8,12},{10,14},{12,8},{14,10},{16,20},{18,... | collective-permute-start | bytes 3538952 | tf_op jit(solution)/shard_map/ppermute | solution.py:496
  427.3 27.2 %collective-permute-start.23 = (bf16[96,768]{1,0:T(8,128)(2,1)}, bf16[96,768]{1,0:T(8,128)(2,1)S(1)}, u32[]{:S(2)}, u32[]{:S(2)}) collective-permute-start(bf16[96,768]{1,0:T(8,128)(2,1)} %get-tuple-element.336), channel_id=1, source_target_pairs={{0,8},{2,10},{4,12},{6,14},{8,0},{10,2},{12,4},{14,6},{16,24},{18,... | collective-permute-start | bytes 442376 | tf_op jit(solution)/shard_map/ppermute | solution.py:496
  427.3 27.2 %collective-permute-start.24 = (bf16[96,768]{1,0:T(8,128)(2,1)}, bf16[96,768]{1,0:T(8,128)(2,1)S(1)}, u32[]{:S(2)}, u32[]{:S(2)}) collective-permute-start(bf16[96,768]{1,0:T(8,128)(2,1)} %get-tuple-element.337), channel_id=1, source_target_pairs={{0,16},{2,18},{4,20},{6,22},{8,24},{10,26},{12,28},{14,30},{16,0},... | collective-permute-start | bytes 442376 | tf_op jit(solution)/shard_map/ppermute | solution.py:496
  429.2 25.3 %collective-permute-start.25 = (bf16[96,768]{1,0:T(8,128)(2,1)}, bf16[96,768]{1,0:T(8,128)(2,1)S(1)}, u32[]{:S(2)}, u32[]{:S(2)}) collective-permute-start(bf16[96,768]{1,0:T(8,128)(2,1)} %get-tuple-element.338), channel_id=1, source_target_pairs={{0,24},{2,26},{4,28},{6,30},{8,16},{10,18},{12,20},{14,22},{16,8},... | collective-permute-start | bytes 442376 | tf_op jit(solution)/shard_map/ppermute | solution.py:496
  431.7 24.5 %copy-start.67 = (f32[768]{0:T(1024)S(1)}, f32[768]{0:T(1024)}, u32[]{:S(2)}) copy-start(f32[768]{0:T(1024)} %get-tuple-element.452) | copy-start | bytes 9220
  455.7 5.3 collective-permute-start.26
  455.7 5.3 collective-permute-start.27
  459.5 1.4 collective-permute-start.28
  475.7 25.8 %collective-permute-start.29 = (bf16[640,768]{1,0:T(8,128)(2,1)}, bf16[640,768]{1,0:T(8,128)(2,1)S(1)}, u32[]{:S(2)}, u32[]{:S(2)}) collective-permute-start(bf16[640,768]{1,0:T(8,128)(2,1)} %get-tuple-element.379), channel_id=1, source_target_pairs={{0,2},{2,0},{4,6},{6,4},{8,10},{10,8},{12,14},{14,12},{16,18},{18,... | collective-permute-start | bytes 2949128 | tf_op jit(solution)/shard_map/ppermute | solution.py:496
  476.3 25.1 %collective-permute-start.30 = (bf16[576,768]{1,0:T(8,128)(2,1)}, bf16[576,768]{1,0:T(8,128)(2,1)S(1)}, u32[]{:S(2)}, u32[]{:S(2)}) collective-permute-start(bf16[576,768]{1,0:T(8,128)(2,1)} %get-tuple-element.380), channel_id=1, source_target_pairs={{0,4},{2,6},{4,0},{6,2},{8,12},{10,14},{12,8},{14,10},{16,20},{18,... | collective-permute-start | bytes 2654216 | tf_op jit(solution)/shard_map/ppermute | solution.py:496
  477.7 14.1 %collective-permute-start.31 = (bf16[192,768]{1,0:T(8,128)(2,1)}, bf16[192,768]{1,0:T(8,128)(2,1)S(1)}, u32[]{:S(2)}, u32[]{:S(2)}) collective-permute-start(bf16[192,768]{1,0:T(8,128)(2,1)} %get-tuple-element.381), channel_id=1, source_target_pairs={{0,8},{2,10},{4,12},{6,14},{8,0},{10,2},{12,4},{14,6},{16,24},{18,... | collective-permute-start | bytes 884744 | tf_op jit(solution)/shard_map/ppermute | solution.py:496
  477.7 23.7 %collective-permute-start.32 = (bf16[192,768]{1,0:T(8,128)(2,1)}, bf16[192,768]{1,0:T(8,128)(2,1)S(1)}, u32[]{:S(2)}, u32[]{:S(2)}) collective-permute-start(bf16[192,768]{1,0:T(8,128)(2,1)} %get-tuple-element.382), channel_id=1, source_target_pairs={{0,16},{2,18},{4,20},{6,22},{8,24},{10,26},{12,28},{14,30},{16,0},... | collective-permute-start | bytes 884744 | tf_op jit(solution)/shard_map/ppermute | solution.py:496
  479.7 21.7 %collective-permute-start.33 = (bf16[192,768]{1,0:T(8,128)(2,1)}, bf16[192,768]{1,0:T(8,128)(2,1)S(1)}, u32[]{:S(2)}, u32[]{:S(2)}) collective-permute-start(bf16[192,768]{1,0:T(8,128)(2,1)} %get-tuple-element.383), channel_id=1, source_target_pairs={{0,24},{2,26},{4,28},{6,30},{8,16},{10,18},{12,20},{14,22},{16,8},... | collective-permute-start | bytes 884744 | tf_op jit(solution)/shard_map/ppermute | solution.py:496
  502.8 17.0 %copy-start.35 = (f32[1,2,48,768]{3,2,1,0:T(8,128)S(1)}, f32[1,2,48,768]{3,2,1,0:T(8,128)}, u32[]{:S(2)}) copy-start(f32[1,2,48,768]{3,2,1,0:T(8,128)} %get-tuple-element.423.refs_0_) | copy-start | bytes 884740
  502.8 24.5 %copy-start.15 = (f32[1,2,48,768]{3,2,1,0:T(8,128)S(1)}, f32[1,2,48,768]{3,2,1,0:T(8,128)}, u32[]{:S(2)}) copy-start(f32[1,2,48,768]{3,2,1,0:T(8,128)} %get-tuple-element.424.refs_1_) | copy-start | bytes 884740
  507.7 19.7 %collective-permute-start.35 = (bf16[256,768]{1,0:T(8,128)(2,1)}, bf16[256,768]{1,0:T(8,128)(2,1)S(1)}, u32[]{:S(2)}, u32[]{:S(2)}) collective-permute-start(bf16[256,768]{1,0:T(8,128)(2,1)} %get-tuple-element.402), channel_id=1, source_target_pairs={{0,4},{2,6},{4,0},{6,2},{8,12},{10,14},{12,8},{14,10},{16,20},{18,... | collective-permute-start | bytes 1179656 | tf_op jit(solution)/shard_map/ppermute | solution.py:496
  508.3 19.0 %collective-permute-start.34 = (bf16[192,768]{1,0:T(8,128)(2,1)}, bf16[192,768]{1,0:T(8,128)(2,1)S(1)}, u32[]{:S(2)}, u32[]{:S(2)}) collective-permute-start(bf16[192,768]{1,0:T(8,128)(2,1)} %get-tuple-element.401), channel_id=1, source_target_pairs={{0,2},{2,0},{4,6},{6,4},{8,10},{10,8},{12,14},{14,12},{16,18},{18,... | collective-permute-start | bytes 884744 | tf_op jit(solution)/shard_map/ppermute | solution.py:496
  509.8 10.0 %collective-permute-start.36 = (bf16[96,768]{1,0:T(8,128)(2,1)}, bf16[96,768]{1,0:T(8,128)(2,1)S(1)}, u32[]{:S(2)}, u32[]{:S(2)}) collective-permute-start(bf16[96,768]{1,0:T(8,128)(2,1)} %get-tuple-element.403), channel_id=1, source_target_pairs={{0,8},{2,10},{4,12},{6,14},{8,0},{10,2},{12,4},{14,6},{16,24},{18,... | collective-permute-start | bytes 442376 | tf_op jit(solution)/shard_map/ppermute | solution.py:496
  515.2 12.1 %collective-permute-start.37 = (bf16[96,768]{1,0:T(8,128)(2,1)}, bf16[96,768]{1,0:T(8,128)(2,1)S(1)}, u32[]{:S(2)}, u32[]{:S(2)}) collective-permute-start(bf16[96,768]{1,0:T(8,128)(2,1)} %get-tuple-element.404), channel_id=1, source_target_pairs={{0,16},{2,18},{4,20},{6,22},{8,24},{10,26},{12,28},{14,30},{16,0},... | collective-permute-start | bytes 442376 | tf_op jit(solution)/shard_map/ppermute | solution.py:496
  515.5 11.8 %collective-permute-start.38 = (bf16[96,768]{1,0:T(8,128)(2,1)}, bf16[96,768]{1,0:T(8,128)(2,1)S(1)}, u32[]{:S(2)}, u32[]{:S(2)}) collective-permute-start(bf16[96,768]{1,0:T(8,128)(2,1)} %get-tuple-element.405), channel_id=1, source_target_pairs={{0,24},{2,26},{4,28},{6,30},{8,16},{10,18},{12,20},{14,22},{16,8},... | collective-permute-start | bytes 442376 | tf_op jit(solution)/shard_map/ppermute | solution.py:496
  519.8 18.2 %collective-permute-start.42 = (f32[1,2,48,768]{3,2,1,0:T(8,128)S(1)}, f32[1,2,48,768]{3,2,1,0:T(8,128)S(1)}, u32[]{:S(2)}, u32[]{:S(2)}) collective-permute-start(f32[1,2,48,768]{3,2,1,0:T(8,128)S(1)} %copy-done.35), channel_id=1, source_target_pairs={{0,1},{1,0},{2,3},{3,2},{4,5},{5,4},{6,7},{7,6},{8,9},{9,8},{10,11... | collective-permute-start | bytes 884744 | tf_op jit(solution)/shard_map/ppermute | solution.py:492
  527.3 10.7 %collective-permute-start.43 = (f32[1,2,48,768]{3,2,1,0:T(8,128)S(1)}, f32[1,2,48,768]{3,2,1,0:T(8,128)S(1)}, u32[]{:S(2)}, u32[]{:S(2)}) collective-permute-start(f32[1,2,48,768]{3,2,1,0:T(8,128)S(1)} %copy-done.15), channel_id=1, source_target_pairs={{0,1},{1,0},{2,3},{3,2},{4,5},{5,4},{6,7},{7,6},{8,9},{9,8},{10,11... | collective-permute-start | bytes 884744 | tf_op jit(solution)/shard_map/ppermute | solution.py:492
  531.1 8.6 %collective-permute-start.39 = (bf16[112,768]{1,0:T(8,128)(2,1)}, bf16[112,768]{1,0:T(8,128)(2,1)S(1)}, u32[]{:S(2)}, u32[]{:S(2)}) collective-permute-start(bf16[112,768]{1,0:T(8,128)(2,1)} %get-tuple-element.420), channel_id=1, source_target_pairs={{0,8},{2,10},{4,12},{6,14},{8,0},{10,2},{12,4},{14,6},{16,24},{18,... | collective-permute-start | bytes 516104 | tf_op jit(solution)/shard_map/ppermute | solution.py:496
  533.7 14.6 %collective-permute-start.40 = (bf16[112,768]{1,0:T(8,128)(2,1)}, bf16[112,768]{1,0:T(8,128)(2,1)S(1)}, u32[]{:S(2)}, u32[]{:S(2)}) collective-permute-start(bf16[112,768]{1,0:T(8,128)(2,1)} %get-tuple-element.421), channel_id=1, source_target_pairs={{0,16},{2,18},{4,20},{6,22},{8,24},{10,26},{12,28},{14,30},{16,0},... | collective-permute-start | bytes 516104 | tf_op jit(solution)/shard_map/ppermute | solution.py:496
  533.8 14.5 %collective-permute-start.41 = (bf16[112,768]{1,0:T(8,128)(2,1)}, bf16[112,768]{1,0:T(8,128)(2,1)S(1)}, u32[]{:S(2)}, u32[]{:S(2)}) collective-permute-start(bf16[112,768]{1,0:T(8,128)(2,1)} %get-tuple-element.422), channel_id=1, source_target_pairs={{0,24},{2,26},{4,28},{6,30},{8,16},{10,18},{12,20},{14,22},{16,8},... | collective-permute-start | bytes 516104 | tf_op jit(solution)/shard_map/ppermute | solution.py:496
  538.0 19.3 %collective-permute-start.44 = (f32[2,2,48,768]{3,2,1,0:T(8,128)}, f32[2,2,48,768]{3,2,1,0:T(8,128)}, u32[]{:S(2)}, u32[]{:S(2)}) collective-permute-start(f32[2,2,48,768]{3,2,1,0:T(8,128)} %get-tuple-element.432.refs_2_), channel_id=1, source_target_pairs={{0,1},{1,0},{2,3},{3,2},{4,5},{5,4},{6,7},{7,6},{8,9},{9,8},{10,11... | collective-permute-start | bytes 1769480 | tf_op jit(solution)/shard_map/ppermute | solution.py:492
  538.0 18.2 %collective-permute-start.45 = (f32[1,2,48,768]{3,2,1,0:T(8,128)}, f32[1,2,48,768]{3,2,1,0:T(8,128)}, u32[]{:S(2)}, u32[]{:S(2)}) collective-permute-start(f32[1,2,48,768]{3,2,1,0:T(8,128)} %get-tuple-element.433.refs_3_), channel_id=1, source_target_pairs={{0,1},{1,0},{2,3},{3,2},{4,5},{5,4},{6,7},{7,6},{8,9},{9,8},{10,11... | collective-permute-start | bytes 884744 | tf_op jit(solution)/shard_map/ppermute | solution.py:492
  551.0 5.2 collective-permute-start.47
  551.0 6.3 %collective-permute-start.46 = (f32[1,2,48,768]{3,2,1,0:T(8,128)}, f32[1,2,48,768]{3,2,1,0:T(8,128)}, u32[]{:S(2)}, u32[]{:S(2)}) collective-permute-start(f32[1,2,48,768]{3,2,1,0:T(8,128)} %get-tuple-element.434.refs_4_), channel_id=1, source_target_pairs={{0,1},{1,0},{2,3},{3,2},{4,5},{5,4},{6,7},{7,6},{8,9},{9,8},{10,11... | collective-permute-start | bytes 884744 | tf_op jit(solution)/shard_map/ppermute | solution.py:492
  557.4 1.7 collective-permute-start.48
  559.0 8.4 %collective-permute-start.49 = (f32[1,128]{1,0:T(1,128)S(1)}, f32[1,128]{1,0:T(1,128)S(1)}, u32[]{:S(2)}, u32[]{:S(2)}) collective-permute-start(f32[1,128]{1,0:T(1,128)S(1)} %add.116), channel_id=1, source_target_pairs={{0,2},{2,0},{4,6},{6,4},{8,10},{10,8},{12,14},{14,12},{16,18},{18,... | collective-permute-start | bytes 1544 | tf_op jit(solution)/shard_map/ppermute | solution.py:496
  559.8 7.7 %collective-permute-start.50 = (f32[1,128]{1,0:T(1,128)S(1)}, f32[1,128]{1,0:T(1,128)S(1)}, u32[]{:S(2)}, u32[]{:S(2)}) collective-permute-start(f32[1,128]{1,0:T(1,128)S(1)} %add.116), channel_id=1, source_target_pairs={{0,4},{2,6},{4,0},{6,2},{8,12},{10,14},{12,8},{14,10},{16,20},{18,... | collective-permute-start | bytes 1544 | tf_op jit(solution)/shard_map/ppermute | solution.py:496
  561.0 6.4 %collective-permute-start.51 = (f32[1,128]{1,0:T(1,128)S(1)}, f32[1,128]{1,0:T(1,128)S(1)}, u32[]{:S(2)}, u32[]{:S(2)}) collective-permute-start(f32[1,128]{1,0:T(1,128)S(1)} %add.116), channel_id=1, source_target_pairs={{0,6},{2,4},{4,2},{6,0},{8,14},{10,12},{12,10},{14,8},{16,22},{18,... | collective-permute-start | bytes 1544 | tf_op jit(solution)/shard_map/ppermute | solution.py:496
  567.5 6.8 %collective-permute-start.52 = (f32[1,128]{1,0:T(1,128)S(1)}, f32[1,128]{1,0:T(1,128)S(1)}, u32[]{:S(2)}, u32[]{:S(2)}) collective-permute-start(f32[1,128]{1,0:T(1,128)S(1)} %add_add_fusion.1), channel_id=1, source_target_pairs={{0,8},{2,10},{4,12},{6,14},{8,0},{10,2},{12,4},{14,6},{16,24},{18,... | collective-permute-start | bytes 1544 | tf_op jit(solution)/shard_map/ppermute | solution.py:496
  570.7 4.4 collective-permute-start.53
  570.7 5.3 collective-permute-start.54
  (67 other events, 316.4 us)
Sparse Core Ops, SparseCore 0:
  20.0 174.2 all-gather.1

commit v7 on v6

--- a/solution.py
+++ b/solution.py
@@ -70,22 +70,95 @@
 LOW, FULL = jnp.bfloat16, jnp.float32
 
 
-def call(kernel, scalars, out_shapes, ins, anys, scratch, flops, outs_any=0):
+class Lazy:
+    def __init__(self, source, target, sem):
+        self.copy = pltpu.make_async_copy(source, target, sem)
+        self.copy.start()
+        self.here, self.shape = target, target.shape
+
+    def ready(self):
+        if self.copy is not None:
+            self.copy.wait()
+            self.copy = None
+        return self.here
+
+    def __getitem__(self, at):
+        return self.ready()[at]
+
+    @property
+    def at(self):
+        return self.ready().at
+
+
+class Sent:
+    def __init__(self, here, there, sems):
+        self.here, self.there, self.sems = here, there, sems
+        self.shape, self.at = here.shape, here.at
+        self.copies = []
+
+    def __getitem__(self, at):
+        return self.here[at]
+
+    def __setitem__(self, at, value):
+        self.here[at] = value
+
+    def send(self, index=None):
+        here, there = self.here, self.there
+        if index is not None:
+            here, there = here.at[index], there.at[index]
+        copy = pltpu.make_async_copy(here, there, self.sems.at[len(self.copies)])
+        copy.start()
+        self.copies.append(copy)
+
+
+def ready(*inputs):
+    for value in inputs:
+        if isinstance(value, Lazy):
+            value.ready()
+
+
+def call(kernel, scalars, outs, ins, anys=(), scratch=(), flops=0, sent=()):
     whole = pl.BlockSpec(memory_space=pltpu.VMEM)
     left = pl.BlockSpec(memory_space=pl.ANY)
-    n = len(out_shapes)
+    large = [x.size >= 1 << 16 for x in ins]
+    buffers = [pltpu.VMEM(x.shape, x.dtype) for x, lazy in zip(ins, large) if lazy]
+    buffers += [pltpu.VMEM(*outs[i]) for i in sent]
+
+    def body(scalars, *refs):
+        refs = list(refs)
+        take = lambda n: [refs.pop(0) for _ in range(n)]
+        sources, any_refs, out_refs = take(len(ins)), take(len(anys)), take(len(outs))
+        here, here_out = take(sum(large)), take(len(sent))
+        extra, (sems, out_sems) = refs[:-2], refs[-2:]
+        values = []
+        for source, lazy in zip(sources, large):
+            at = sum(isinstance(v, Lazy) for v in values)
+            values.append(Lazy(source, here[at], sems.at[at]) if lazy else source)
+        for n, i in enumerate(sent):
+            out_refs[i] = Sent(here_out[n], out_refs[i], out_sems.at[n])
+        kernel(scalars, values, any_refs, out_refs, *extra)
+        ready(*values)
+        for i in sent:
+            for copy in out_refs[i].copies:
+                copy.wait()
+
     return pl.pallas_call(
-        kernel,
-        out_shape=[jax.ShapeDtypeStruct(s, t) for s, t in out_shapes],
+        body,
+        out_shape=[jax.ShapeDtypeStruct(s, t) for s, t in outs],
         in_specs=[pl.BlockSpec(memory_space=pltpu.SMEM)]
-        + [whole] * len(ins)
+        + [left if lazy else whole for lazy in large]
         + [left] * len(anys),
-        out_specs=[whole] * (n - outs_any) + [left] * outs_any,
-        scratch_shapes=scratch,
+        out_specs=[left if i in sent else whole for i in range(len(outs))],
+        scratch_shapes=buffers
+        + list(scratch)
+        + [
+            pltpu.SemaphoreType.DMA((max(sum(large), 1),)),
+            pltpu.SemaphoreType.DMA((max(len(sent), 1), 4)),
+        ],
         compiler_params=pltpu.CompilerParams(vmem_limit_bytes=VMEM_LIMIT),
         cost_estimate=pl.CostEstimate(
             flops=flops,
-            bytes_accessed=sum(x.size * x.dtype.itemsize for x in ins + anys),
+            bytes_accessed=sum(x.size * x.dtype.itemsize for x in list(ins) + list(anys)),
             transcendentals=0,
         ),
     )(scalars, *ins, *anys)
@@ -132,15 +205,15 @@
     return (lane < HD) if head == 0 else (lane >= HD)
 
 
-def attention_forward_kernel(
-    base, place_of, resid, seg_col, seg_row, cosine, sine, gains, weights,
-    middle, query, keys, values, lse, pack,
-    w_a, w_b, mixed, same, sems,
-):
+def attention_forward_kernel(base, place_of, ins, anys, outs, w_a, w_b, mixed, bias, sems):
+    resid, seg_col, seg_row, cosine, sine, gains = ins
+    middle, query, keys, values, lse, pack = outs
+    (weights,) = anys
     width = resid.shape[1]
     half = width // 2
+    cores = (place_of[0], 1 - place_of[0])
     copies = fetch(
-        [tile_of(weights, c, base + t * width) for t in range(2) for c in (place_of[0], 1 - place_of[0])],
+        [tile_of(weights, c, base + t * width) for t in range(2) for c in cores],
         [w.at[place] for w in (w_a, w_b) for place in range(2)],
         sems,
     )
@@ -148,20 +221,25 @@
     normed, _, _ = normalize(resid[...], gains[0:1], gains[1:2])
     normed_low, attended = pack.at[0], pack.at[1]
     normed_low[...] = normed.astype(LOW)
-    same[...] = jnp.where(seg_col[...] == seg_row[...], 0.0, 1.0)
+    pack.send(0)
+    bias[...] = jnp.where(seg_col[...] == seg_row[...], 0.0, -1000000000.0)
     for place in range(2):
         copies[place].wait()
         mixed[...] = dot(normed_low[...], matrix(w_a, place))
         for p in range(half // 128):
-            for part, target in ((0, query), (1, keys)):
+            for part, target, scale in ((0, query, HD ** (-0.5)), (1, keys, 1.0)):
                 x = mixed[:, part * half + p * 128 : part * half + (p + 1) * 128]
                 x = x * cosine[...] + swap_halves(x) * sine[...]
-                target[:, place * half + p * 128 : place * half + (p + 1) * 128] = x.astype(LOW)
+                x = (x * scale if scale != 1.0 else x).astype(LOW)
+                target[:, place * half + p * 128 : place * half + (p + 1) * 128] = x
+    query.send()
+    keys.send()
     for place in range(2):
         copies[2 + place].wait()
         values[:, place * half : (place + 1) * half] = dot(
             normed_low[...], matrix(w_b, place, 0, half)
         ).astype(LOW)
+    values.send()
 
     lse[...] = jnp.zeros_like(lse)
 
@@ -171,12 +249,11 @@
         out = []
         for head in range(2):
             masked_q = jnp.where(head_mask(q.shape, head), q, jnp.zeros_like(q))
-            scores = dot_nt(masked_q, k) * HD ** (-0.5)
-            scores = jnp.where(same[...] > 0.5, -1000000000.0, scores)
+            scores = dot_nt(masked_q, k) + bias[...]
             top = jnp.max(scores, -1, keepdims=True)
             expo = jnp.exp(scores - top)
             total = jnp.sum(expo, -1, keepdims=True)
-            probs = (expo / total).astype(LOW)
+            probs = (expo * (1.0 / total)).astype(LOW)
             out.append(dot(probs, v))
             lane = lax.broadcasted_iota(jnp.int32, lse.shape, 1)
             lse[...] = jnp.where(lane == 2 * p + head, top + jnp.log(total), lse[...])
@@ -185,6 +262,7 @@
 
     lax.fori_loop(0, width // 128, pair, 0)
     attended[...] = ordered(first, attended[:, :half], attended[:, half:])
+    pack.send(1)
     out = ordered(
         first,
         dot(attended[...], matrix(w_b, 0, half, width)),
@@ -196,11 +274,10 @@
 def attention_forward(place, resid, weights, base, gains, cosine, sine, segments):
     length, width = resid.shape
     one = (length, width)
-    outs = [(one, FULL)] + [(one, LOW)] * 3 + [((length, 128), FULL), ((2,) + one, LOW)]
     return call(
         functools.partial(attention_forward_kernel, base),
         place,
-        outs,
+        [(one, FULL)] + [(one, LOW)] * 3 + [((length, 128), FULL), ((2,) + one, LOW)],
         [resid, segments[:, None], segments[None, :], cosine, sine, gains],
         [weights],
         [
@@ -211,6 +288,7 @@
             pltpu.SemaphoreType.DMA((4,)),
         ],
         8 * length * width * width + 4 * length * length * width,
+        sent=(1, 2, 3, 5),
     )
 
 
@@ -226,81 +304,78 @@
     return tiles[0], tiles[1]
 
 
-def hidden_forward_kernel(
-    base, place_of, middle, gains, weights,
-    output, active, pack, hidden, ups, downs, hidden_here, sems, out_sems,
-):
-    u, d = hidden_tiles(weights, place_of[0], base, middle.shape[1])
-    ins = fetch(
+def hidden_forward_kernel(base, place_of, ins, anys, outs, ups, downs, sems):
+    middle, gains = ins
+    output, active, pack, hidden = outs
+    u, d = hidden_tiles(anys[0], place_of[0], base, middle.shape[1])
+    copies = fetch(
         [r for t in range(4) for r in (u[t], d[t])],
         [w.at[t] for t in range(4) for w in (ups, downs)],
         sems,
     )
     normed, _, _ = normalize(middle[...], gains[0:1], gains[1:2])
     pack[0] = normed.astype(LOW)
-    outs = []
+    pack.send(0)
     for t in range(4):
-        ins[2 * t].wait()
+        copies[2 * t].wait()
         x = dot(pack[0], matrix(ups, t))
-        hidden_here[t] = x
-        out = pltpu.make_async_copy(hidden_here.at[t], hidden.at[t], out_sems.at[t])
-        out.start()
-        outs.append(out)
-        inner = jnp.tanh(GELU_SCALE * (x + GELU_CUBE * (x * x * x)))
-        target = active.at[t] if t < 2 else pack.at[t - 1]
-        target[...] = (x * (0.5 * (1.0 + inner))).astype(LOW)
-        ins[2 * t + 1].wait()
-        product = dot(target[...], matrix(downs, t))
+        hidden[t] = x
+        hidden.send(t)
+        inner = jnp.tanh(x * (GELU_SCALE + (GELU_SCALE * GELU_CUBE) * (x * x)))
+        value = x * 0.5
+        value = (value + value * inner).astype(LOW)
+        target, at = (active, t) if t < 2 else (pack, t - 1)
+        target[at] = value
+        target.send(at)
+        copies[2 * t + 1].wait()
+        product = dot(value, matrix(downs, t))
         output[...] = (middle[...] if t == 0 else output[...]) + product
-    for out in outs:
-        out.wait()
 
 
 def hidden_forward(place, middle, weights, base, gains):
     length, width = middle.shape
     one = (length, width)
-    outs = [(one, FULL), ((2,) + one, LOW), ((3,) + one, LOW), ((4,) + one, FULL)]
     return call(
         functools.partial(hidden_forward_kernel, base),
         place,
-        outs,
+        [(one, FULL), ((2,) + one, LOW), ((3,) + one, LOW), ((4,) + one, FULL)],
         [middle, gains],
         [weights],
         [
             tile_scratch(4, weights),
             tile_scratch(4, weights),
-            pltpu.VMEM((4,) + one, FULL),
             pltpu.SemaphoreType.DMA((8,)),
-            pltpu.SemaphoreType.DMA((4,)),
         ],
         16 * length * width * width,
-        outs_any=1,
-    )
-
-
-def hidden_back_kernel(
-    base, place_of, grad, branch, middle, gains, hidden, weights,
-    grad_middle, grad_gains, grad_own, grad_other, ups, downs, hidden_here, total, sems,
-):
+        sent=(1, 2, 3),
+    )
+
+
+def hidden_back_kernel(base, place_of, ins, anys, outs, ups, downs, hidden_here, total, sems):
+    branch, grad, middle, gains = ins
+    hidden, weights = anys
+    grad_middle, grad_gains, grad_own, grad_other = outs
     u, d = hidden_tiles(weights, place_of[0], base, middle.shape[1])
-    ins = fetch(
+    copies = fetch(
         [r for t in range(4) for r in (d[t], hidden.at[t], u[t])],
         [w.at[t] for t in range(4) for w in (downs, hidden_here, ups)],
         sems,
     )
     for t in range(4):
-        ins[3 * t].wait()
+        copies[3 * t].wait()
         grad_active = dot_nt(branch[...], matrix(downs, t))
-        ins[3 * t + 1].wait()
+        copies[3 * t + 1].wait()
         x = hidden_here[t]
-        inner = jnp.tanh(GELU_SCALE * (x + GELU_CUBE * (x * x * x)))
-        slope = 0.5 * (1.0 + inner) + (0.5 * GELU_SCALE) * x * (1.0 - inner * inner) * (
-            1.0 + (3.0 * GELU_CUBE) * (x * x)
-        )
-        target = grad_own.at[t] if t < 2 else grad_other.at[t - 2]
-        target[...] = (grad_active * slope).astype(LOW)
-        ins[3 * t + 2].wait()
-        product = dot_nt(target[...], matrix(ups, t))
+        square = x * x
+        inner = jnp.tanh(x * (GELU_SCALE + (GELU_SCALE * GELU_CUBE) * square))
+        slope = x * (GELU_SCALE + (3.0 * GELU_SCALE * GELU_CUBE) * square)
+        slope = (0.5 + 0.5 * inner) * (1.0 + slope * (1.0 - inner))
+        value = (grad_active * slope).astype(LOW)
+        target = grad_own if t < 2 else grad_other
+        target[t % 2] = value
+        target.send(t % 2)
+        copies[3 * t + 2].wait()
+        product = dot_nt(value, matrix(ups, t))
         total[...] = product if t == 0 else total[...] + product
     _, unit, inverse = normalize(middle[...], gains[0:1], gains[1:2])
     back, gain, bias = normalize_back(total[...], unit, inverse, gains[0:1])
@@ -312,12 +387,11 @@
 def hidden_back(place, grad, branch, middle, hidden, weights, base, gains):
     length, width = middle.shape
     one = (length, width)
-    outs = [(one, FULL), ((2, width), FULL), ((2,) + one, LOW), ((2,) + one, LOW)]
     return call(
         functools.partial(hidden_back_kernel, base),
         place,
-        outs,
-        [grad, branch, middle, gains],
+        [(one, FULL), ((2, width), FULL), ((2,) + one, LOW), ((2,) + one, LOW)],
+        [branch, grad, middle, gains],
         [hidden, weights],
         [
             tile_scratch(4, weights),
@@ -327,26 +401,25 @@
             pltpu.SemaphoreType.DMA((12,)),
         ],
         16 * length * width * width,
-    )
-
-
-def attention_back_kernel(
-    base, place_of, grad_middle, resid, seg_col, seg_row, cosine, sine, gains, query, keys, values, lse,
-    weights,
-    grad, branch, grad_gains, grad_own, grad_other,
-    w_a, w_b, same, ga, gq, gk, gv, sems,
-):
+        sent=(2, 3),
+    )
+
+
+def attention_back_kernel(base, place_of, ins, anys, outs, w_a, w_b, bias, ga, gq, gk, gv, sems):
+    grad_middle, query, keys, values, lse, seg_col, seg_row, cosine, sine, gains, resid = ins
+    (weights,) = anys
+    grad, branch, grad_gains, grad_own, grad_other = outs
     width = resid.shape[1]
     half = width // 2
+    cores = (place_of[0], 1 - place_of[0])
     copies = fetch(
-        [tile_of(weights, c, base + t * width) for t in (1, 0) for c in (place_of[0], 1 - place_of[0])],
+        [tile_of(weights, c, base + t * width) for t in (1, 0) for c in cores],
         [w.at[place] for w in (w_b, w_a) for place in range(2)],
         sems,
     )
     first = place_of[0] == 0
-    scale = HD ** (-0.5)
     grads = (grad_own, grad_other)
-    same[...] = jnp.where(seg_col[...] == seg_row[...], 0.0, 1.0)
+    bias[...] = jnp.where(seg_col[...] == seg_row[...], 0.0, -1000000000.0)
     attn_grad = grad_middle[...].astype(LOW)
     left, right = attn_grad[:, :half], attn_grad[:, half:]
     grad_own[1, :, half:] = jnp.where(first, left, right)
@@ -359,6 +432,7 @@
     natural = natural.astype(LOW)
     ga[:, :half] = jnp.where(first, natural[:, :half], natural[:, half:])
     ga[:, half:] = jnp.where(first, natural[:, half:], natural[:, :half])
+    ready(query, keys, values, lse, cosine, sine)
 
     def pair(p, _):
         columns = pl.ds(pl.multiple_of(p * 128, 128), 128)
@@ -367,8 +441,7 @@
         for head in range(2):
             mask = head_mask(q.shape, head)
             zero = jnp.zeros_like(q)
-            scores = dot_nt(k, jnp.where(mask, q, zero)) * scale
-            scores = jnp.where(same[...] > 0.5, -1000000000.0, scores)
+            scores = dot_nt(k, jnp.where(mask, q, zero)) + bias[...]
             probs = jnp.exp(scores - lse[pl.ds(2 * p + head, 1), :])
             grad_probs = dot_nt(v, jnp.where(mask, g, zero))
             across = jnp.sum(probs * grad_probs, 0, keepdims=True)
@@ -376,44 +449,44 @@
             out_k.append(dot(grad_scores, q))
             out_q.append(cross(grad_scores, k))
             out_v.append(dot(probs.astype(LOW), g))
-        for out, target in ((out_q, gq), (out_k, gk)):
-            x = jnp.where(head_mask(out[0].shape, 0), out[0], out[1]) * scale
+        for out, target, scale in ((out_q, gq, HD ** (-0.5)), (out_k, gk, 1.0)):
+            x = jnp.where(head_mask(out[0].shape, 0), out[0], out[1])
+            x = x * scale if scale != 1.0 else x
             x = x * cosine[...] - swap_halves(x) * sine[...]
             target[:, columns] = x.astype(LOW)
         gv[:, columns] = jnp.where(head_mask(out_v[0].shape, 0), out_v[0], out_v[1]).astype(LOW)
         return 0
 
     lax.fori_loop(0, width // 128, pair, 0)
-    for place in range(2):
+    for place in (1, 0):
         columns = slice(place * half, (place + 1) * half)
         grads[place][0, :, :half] = gq[:, columns]
         grads[place][0, :, half:] = gk[:, columns]
         grads[place][1, :, :half] = gv[:, columns]
+        grads[place].send()
     copies[2].wait()
     copies[3].wait()
     total = dot_nt(grad_own[0], matrix(w_a, 0)) + dot_nt(grad_other[0], matrix(w_a, 1))
     total = total + dot_nt(grad_own[1, :, :half], matrix(w_b, 0, 0, half))
     total = total + dot_nt(grad_other[1, :, :half], matrix(w_b, 1, 0, half))
     _, unit, inverse = normalize(resid[...], gains[0:1], gains[1:2])
-    back, gain, bias = normalize_back(total, unit, inverse, gains[0:1])
+    back, gain, bias_grad = normalize_back(total, unit, inverse, gains[0:1])
     back = grad_middle[...] + back
     grad[...] = back
     branch[...] = back.astype(LOW)
     grad_gains[0:1] = gain
-    grad_gains[1:2] = bias
+    grad_gains[1:2] = bias_grad
 
 
 def attention_back(place, grad_middle, resid, weights, base, gains, cosine, sine, segments, query, keys, values, lse):
     length, width = resid.shape
     one = (length, width)
-    outs = [(one, FULL), (one, LOW), ((2, width), FULL)] + [((2,) + one, LOW)] * 2
-    ins = [grad_middle, resid, segments[:, None], segments[None, :], cosine, sine, gains]
-    ins += [query, keys, values, lse.T[: width // HD]]
     return call(
         functools.partial(attention_back_kernel, base),
         place,
-        outs,
-        ins,
+        [(one, FULL), (one, LOW), ((2, width), FULL)] + [((2,) + one, LOW)] * 2,
+        [grad_middle, query, keys, values, lse.T[: width // HD]]
+        + [segments[:, None], segments[None, :], cosine, sine, gains, resid],
         [weights],
         [
             tile_scratch(2, weights),
@@ -423,6 +496,7 @@
         + [pltpu.VMEM(one, LOW)] * 4
         + [pltpu.SemaphoreType.DMA((4,))],
         8 * length * width * width + 10 * length * length * width,
+        sent=(3, 4),
     )
 
 
@@ -520,11 +594,10 @@
 SMALL = 128
 
 
-def round_kernel(jobs, small_job, n_ins, counts, smalls, last, *refs):
+def round_kernel(jobs, small_job, n_ins, counts, smalls, last, place_of, ins, anys, outs, *scratch):
     new, once, twice, done = counts
     small_new, small_once, small_twice, small_done = smalls
-    place_of, ins = refs[0], refs[1 : 1 + n_ins]
-    rest = list(refs[1 + n_ins :])
+    rest = list(ins[n_ins:]) + list(outs) + list(scratch)
     pop = lambda present, n=1: [rest.pop(0) for _ in range(n)] if present else [None] * n
     (keep_once,), (small_keep_once,) = pop(once), pop(small_once)
     (keep_twice,), (small_keep_twice,) = pop(twice), pop(small_twice)
@@ -585,12 +658,12 @@
                     to[s][block(p * 8 + at), :] = tile[block(index(1 - bits[s])), :].astype(LOW)
                     out_once[p, s, block(at), :] = tile[block(index(bits[s])), :]
     if small_new:
-        products, norms, norms_came = small_job
+        products, norms_at = small_job
         total = None
         for left, right in products:
             product = cross(factor(left), factor(right))
             total = product if total is None else total + product
-        norms = ins[norms][...] + ins[norms_came][...]
+        norms = jnp.concatenate([ins[mine][...] + ins[theirs][...] for mine, theirs in norms_at], 0)
         high = norms.astype(LOW)
         shape = (norms.shape[0], SMALL)
         column = lax.broadcasted_iota(jnp.int32, shape, 1) - V
@@ -699,9 +772,10 @@
                 )
         small_job = None
         if small is not None:
-            products, norms, norms_came = small
-            small_job = [(number(l), number(r)) for l, r in products]
-            small_job = (small_job, number((norms,))[0], number((norms_came,))[0])
+            small_job = (
+                [(number(l), number(r)) for l, r in small[0]],
+                [(number((a,))[0], number((b,))[0]) for a, b in small[1]],
+            )
         ins = list(arrays)
         for stage in range(2):
             ins += [self.kept[stage]] * (counts[1 + stage] > 0)
@@ -962,6 +1036,9 @@
             grad_middle, up_own, up_other, early_came
         )
         up_came = swap_cores(up_other)
+        if l == 0:
+            norms_early = jnp.concatenate([gains_mid] + grad_norms, 0)
+            norms_early = (norms_early, swap_cores(norms_early))
         (grad_middle,) = rounds.step(
             [
                 [
@@ -990,13 +1067,12 @@
                 [(0, half, products(0, 0, half)), (half, width, products(1, half, width))],
             ]
         ]
-    norm_rows = -(-norms // 16) * 16
-    grad_norms = jnp.concatenate(grad_norms + [jnp.zeros((norm_rows - norms, width), FULL)], 0)
-    branch_came, norms_came = swap_cores(branch), swap_cores(grad_norms)
+    late = (grad_norms[0], swap_cores(grad_norms[0]))
+    branch_came = swap_cores(branch)
     products = [(whole(early[0]), whole(early[1])), (whole(early_came[0]), whole(early_came[1]))]
     products += [(whole(branch), whole(early[2])), (whole(branch_came), whole(early_came[2]))]
     if fast:
-        rounds.step(chunk, small=(products, grad_norms, norms_came))
+        rounds.step(chunk, small=(products, [late, norms_early]))
         while rounds.left():
             rounds.finish()
             rounds.step([])
@@ -1008,7 +1084,10 @@
     else:
         rounds.step(chunk)
         table = sum(cross(l[0], r[0]) for l, r in products)
-        table = table + jnp.pad((grad_norms + norms_came).T, ((0, 0), (V, SMALL - V - norm_rows)))
+        table = table + jnp.pad(
+            jnp.concatenate([a + b for a, b in (late, norms_early)], 0).T,
+            ((0, 0), (V, SMALL - V - norms)),
+        )
         table = jnp.where(core == 0, table, swap_cores(table))
         share_small = lax.psum_scatter(table, "fsdp", scatter_dimension=0, tiled=True)
         squares = jnp.sum(share_small * share_small) * (core == 0)

time: 605 us -> 610 us (level)
    ppermute x22 -> x23, waiting for transfers between devices: 14.6 us -> 15.7 us  [swap_cores(): return lax.ppermute(value, 'dp', [(0, 1), (1, 0)])]
    unnamed x164 -> x166, local copies, waits for them, and re-layouts: 14.9 us -> 14.3 us
  transfers between devices with their start and end apart: 56 -> 57, of which waited for: 16 -> 16; matrix products, arithmetic and copies ran while one was open for 5% -> 5% of each run, Pallas kernels for 24% -> 24%
where the time goes in v7:
time: 610 us; the launch traced here: 601 us
  waiting for transfers between devices  239 us (39%)
  Pallas kernels  231 us (38%)
  starting transfers between devices  53.1 us (9%)
  local copies, waits for them, and re-layouts  34.6 us (6%)
  other arithmetic  22.4 us (4%)
  between operations  18.5 us (3%)
    pallas_call x16, Pallas kernels, call(): pl.pallas_call(body, out_shape=[jax.ShapeDtypeStruct(s, t) for s, t in ou...  220 us
    all_gather x1, waiting for transfers between devices, body(): weights = lax.all_gather(weights, ('fsdp', 'dp'), axis=0, tiled=True)  171 us
    ppermute x33, waiting for transfers between devices, across(): return lax.ppermute(value, 'fsdp', [(i, i ^ mask) for i in range(size)])  52.3 us
    ppermute x33, starting transfers between devices, across(): return lax.ppermute(value, 'fsdp', [(i, i ^ mask) for i in range(size)])  47.8 us
    ppermute x23, waiting for transfers between devices, swap_cores(): return lax.ppermute(value, 'dp', [(0, 1), (1, 0)])  15.7 us
    unnamed x166, local copies, waits for them, and re-layouts  14.3 us
  transfers between devices with their start and end apart: 57, of which 16 were waited for; matrix products, arithmetic and copies ran while one was open for 5% of the time, Pallas kernels for 24%

profile of v7, /device:TPU:0, one launch (start us, length us, event | category | flops | bytes accessed | tf_op | source)
XLA Modules:
  0.0 601.3 jit_solution(6459424588698913811)
XLA Ops:
  7.3 1.3 convert.16
  11.3 2.1 reshape.175
  15.4 1.4 reshape.176
  23.7 170.6 %all-gather.2.cloned.1.call-done = bf16[1536,9344]{1,0:T(8,128)(2,1)} async-done(((bf16[48,9344]{1,0:T(8,128)(2,1)}), bf16[1536,9344]{1,0:T(8,128)(2,1)}) %all-gather.2.cloned.1.call-update) | async-done | bytes 28704784 | tf_op jit(solution)/shard_map/all_gather | solution.py:958
  196.1 1.5 fusion.3.refs_0_.refs_10_
  197.6 18.6 %shard_map.364 = (f32[512,768]{1,0:T(8,128)}, bf16[512,768]{1,0:T(8,128)(2,1)}, bf16[512,768]{1,0:T(8,128)(2,1)}, bf16[512,768]{1,0:T(8,128)(2,1)}, f32[512,128]{1,0:T(8,128)}, /*index=5*/bf16[2,512,768]{2,1,0:T(8,128)(2,1)}) custom-call(s32[4]{0:T(128)} %pad_add_fusion.scalars.place_of, f32[512,768]{1,0:T(8,128)} %fusion.3.refs_0_.refs_10_, ...), custom_call_target="tpu_custom_call" | custom-call | flops 3221225472 | bytes 30812160 | tf_op jit(solution)/shard_map/pallas_call | solution.py:145
  216.5 12.3 %shard_map.365 = (f32[512,768]{1,0:T(8,128)}, bf16[2,512,768]{2,1,0:T(8,128)(2,1)}, bf16[3,512,768]{2,1,0:T(8,128)(2,1)}, f32[4,512,768]{2,1,0:T(8,128)}) custom-call(s32[4]{0:T(128)} %pad_add_fusion.scalars.place_of, f32[512,768]{1,0:T(8,128)} %get-tuple-element.236.refs_0_.refs_2_, f32[2,768]{1,0:T(2,128)} %get-tuple-element.494.refs_1_.refs_3_, ...), custom_call_target="tpu_custom_call" | custom-call | flops 4831838208 | bytes 30283776 | tf_op jit(solution)/shard_map/pallas_call | solution.py:145
  229.2 27.9 %shard_map.366 = (f32[512,768]{1,0:T(8,128)}, bf16[512,768]{1,0:T(8,128)(2,1)}, bf16[512,768]{1,0:T(8,128)(2,1)}, bf16[512,768]{1,0:T(8,128)(2,1)}, f32[512,128]{1,0:T(8,128)}, /*index=5*/bf16[2,512,768]{2,1,0:T(8,128)(2,1)}) custom-call(s32[4]{0:T(128)} %pad_add_fusion.scalars.place_of, f32[512,768]{1,0:T(8,128)} %get-tuple-element.239.refs_0_.refs_10_, ...), custom_call_target="tpu_custom_call" | custom-call | flops 3221225472 | bytes 30812160 | tf_op jit(solution)/shard_map/pallas_call | solution.py:145
  257.5 12.4 %shard_map.367 = (f32[512,768]{1,0:T(8,128)}, bf16[2,512,768]{2,1,0:T(8,128)(2,1)}, bf16[3,512,768]{2,1,0:T(8,128)(2,1)}, f32[4,512,768]{2,1,0:T(8,128)}) custom-call(s32[4]{0:T(128)} %pad_add_fusion.scalars.place_of, f32[512,768]{1,0:T(8,128)} %get-tuple-element.242.refs_0_.refs_2_, f32[2,768]{1,0:T(2,128)} %get-tuple-element.492.refs_1_.refs_3_, ...), custom_call_target="tpu_custom_call" | custom-call | flops 4831838208 | bytes 30283776 | tf_op jit(solution)/shard_map/pallas_call | solution.py:145
  271.5 1.6 reduce_sum.90
  275.4 1.3 multiply_reduce_fusion
  276.7 1.7 fusion.25
  278.9 1.8 collective-permute-done.4.refs_3_
  281.6 8.0 %shard_map.368 = (bf16[384,768]{1,0:T(8,128)(2,1)}, bf16[384,768]{1,0:T(8,128)(2,1)}, f32[1,2,384,768]{3,2,1,0:T(8,128)}) custom-call(s32[4]{0:T(128)} %pad_add_fusion.scalars.place_of, bf16[2,512,768]{2,1,0:T(8,128)(2,1)} %get-tuple-element.244.refs_0_, bf16[512,768]{1,0:T(8,128)(2,1)} %copy-done.4, bf16[3,512,768]{2,1,0:T(8,128)(2,1)} %collective-permute-done.3.refs_2_, ...), custom_call_target="tpu_custom_call" | custom-call | flops 2415919104 | bytes 5505024 | tf_op jit(solution)/shard_map/pallas_call | solution.py:145
  289.6 1.5 collective-permute-start.5
  292.5 17.0 %shard_map.369 = (f32[512,768]{1,0:T(8,128)}, f32[2,768]{1,0:T(2,128)}, bf16[2,512,768]{2,1,0:T(8,128)(2,1)}, bf16[2,512,768]{2,1,0:T(8,128)(2,1)}) custom-call(s32[4]{0:T(128)} %pad_add_fusion.scalars.place_of, bf16[512,768]{1,0:T(8,128)(2,1)} %copy-done.4, f32[512,768]{1,0:T(8,128)} %get-tuple-element.256.refs_1_, ...), custom_call_target="tpu_custom_call" | custom-call | flops 4831838208 | bytes 38934528 | tf_op jit(solution)/shard_map/pallas_call | solution.py:145
  309.8 3.6 collective-permute-done.10.refs_3_
  314.6 9.7 %shard_map.370 = (bf16[576,768]{1,0:T(8,128)(2,1)}, bf16[576,768]{1,0:T(8,128)(2,1)}, f32[1,2,384,768]{3,2,1,0:T(8,128)}, f32[1,2,192,768]{3,2,1,0:T(8,128)}) custom-call(s32[4]{0:T(128)} %pad_add_fusion.scalars.place_of, bf16[3,512,768]{2,1,0:T(8,128)(2,1)} %get-tuple-element.243.refs_0_, bf16[2,512,768]{2,1,0:T(8,128)(2,1)} %get-tuple-element.261.refs_1_, ...), custom_call_target="tpu_custom_call" | custom-call | flops 2415919104 | bytes 11403264 | tf_op jit(solution)/shard_map/pallas_call | solution.py:145
  324.4 1.5 collective-permute-start.11
  327.2 22.7 %shard_map.371 = (f32[512,768]{1,0:T(8,128)}, bf16[512,768]{1,0:T(8,128)(2,1)}, f32[2,768]{1,0:T(2,128)}, bf16[2,512,768]{2,1,0:T(8,128)(2,1)}, bf16[2,512,768]{2,1,0:T(8,128)(2,1)}) custom-call(s32[4]{0:T(128)} %pad_add_fusion.scalars.place_of, f32[512,768]{1,0:T(8,128)} %get-tuple-element.273.refs_0_, bf16[512,768]{1,0:T(8,128)(2,1)} %get-tuple-element.274.refs_1_, ...), custom_call_target="tpu_custom_call" | custom-call | flops 4429185024 | bytes 34768896 | tf_op jit(solution)/shard_map/pallas_call | solution.py:145
  350.5 4.2 collective-permute-done.14.refs_7_
  356.2 14.1 %shard_map.372 = (bf16[960,768]{1,0:T(8,128)(2,1)}, bf16[960,768]{1,0:T(8,128)(2,1)}, f32[2,2,384,768]{3,2,1,0:T(8,128)}, f32[1,2,192,768]{3,2,1,0:T(8,128)}, f3...) custom-call(s32[4]{0:T(128)} %pad_add_fusion.scalars.place_of, ...), custom_call_target="tpu_custom_call" | custom-call | flops 4831838208 | bytes 17104896 | tf_op jit(solution)/shard_map/pallas_call | solution.py:145
  370.3 1.5 collective-permute-start.15
  372.4 1.9 collective-permute-start.18
  374.3 2.4 collective-permute-start.19
  376.8 17.4 %shard_map.373 = (f32[512,768]{1,0:T(8,128)}, f32[2,768]{1,0:T(2,128)}, bf16[2,512,768]{2,1,0:T(8,128)(2,1)}, bf16[2,512,768]{2,1,0:T(8,128)(2,1)}) custom-call(s32[4]{0:T(128)} %pad_add_fusion.scalars.place_of, bf16[512,768]{1,0:T(8,128)(2,1)} %get-tuple-element.306.refs_5_.refs_0_, f32[512,768]{1,0:T(8,128)} %get-tuple-element.307.refs_1_, ...), custom_call_target="tpu_custom_call" | custom-call | flops 4831838208 | bytes 38934528 | tf_op jit(solution)/shard_map/pallas_call | solution.py:145
  394.3 10.6 %collective-permute-done.15.refs_6_ = bf16[960,768]{1,0:T(8,128)(2,1)S(1)} collective-permute-done((bf16[960,768]{1,0:T(8,128)(2,1)}, bf16[960,768]{1,0:T(8,128)(2,1)S(1)}, u32[]{:S(2)}, u32[]{:S(2)}) %collective-permute-start.15) | collective-permute-done | bytes 1474592 | tf_op jit(solution)/shard_map/ppermute | solution.py:570
  406.0 3.6 collective-permute-done.20.refs_3_
  410.7 11.0 %shard_map.374 = (bf16[768,768]{1,0:T(8,128)(2,1)}, bf16[768,768]{1,0:T(8,128)(2,1)}, f32[1,2,384,768]{3,2,1,0:T(8,128)}, f32[2,2,192,768]{3,2,1,0:T(8,128)}, f3...) custom-call(s32[4]{0:T(128)} %pad_add_fusion.scalars.place_of, ...), custom_call_target="tpu_custom_call" | custom-call | flops 2415919104 | bytes 17452032 | tf_op jit(solution)/shard_map/pallas_call | solution.py:145
  422.4 1.5 collective-permute-start.22
  424.6 1.9 collective-permute-start.24
  426.6 2.4 collective-permute-start.25
  429.0 22.8 %shard_map.375 = (f32[512,768]{1,0:T(8,128)}, bf16[512,768]{1,0:T(8,128)(2,1)}, f32[2,768]{1,0:T(2,128)}, bf16[2,512,768]{2,1,0:T(8,128)(2,1)}, bf16[2,512,768]{2,1,0:T(8,128)(2,1)}) custom-call(s32[4]{0:T(128)} %pad_add_fusion.scalars.place_of, f32[512,768]{1,0:T(8,128)} %get-tuple-element.339.refs_0_, bf16[512,768]{1,0:T(8,128)(2,1)} %get-tuple-element.340.refs_1_, ...), custom_call_target="tpu_custom_call" | custom-call | flops 4429185024 | bytes 34768896 | tf_op jit(solution)/shard_map/pallas_call | solution.py:145
  453.6 1.4 concatenate.44.refs_14_
  455.5 2.4 collective-permute-done.29.refs_15_
  459.3 13.6 %shard_map.376 = (bf16[640,768]{1,0:T(8,128)(2,1)}, bf16[576,768]{1,0:T(8,128)(2,1)}, f32[1,2,384,768]{3,2,1,0:T(8,128)}, f32[384,128]{1,0:T(8,128)}, f32[1,2,19...) custom-call(s32[4]{0:T(128)} %pad_add_fusion.scalars.place_of, ...), custom_call_target="tpu_custom_call" | custom-call | flops 2415919104 | bytes 17841152 | tf_op jit(solution)/shard_map/pallas_call | solution.py:145
  473.5 1.4 collective-permute-start.31
  474.9 2.0 collective-permute-start.33
  476.9 2.4 collective-permute-start.34
  479.3 9.7 %collective-permute-done.32.refs_6_ = bf16[192,768]{1,0:T(8,128)(2,1)S(1)} collective-permute-done((bf16[192,768]{1,0:T(8,128)(2,1)}, bf16[192,768]{1,0:T(8,128)(2,1)S(1)}, u32[]{:S(2)}, u32[]{:S(2)}) %collective-permute-start.32) | collective-permute-done | bytes 294944 | tf_op jit(solution)/shard_map/ppermute | solution.py:570
  489.0 9.6 %collective-permute-done.33.refs_7_ = bf16[192,768]{1,0:T(8,128)(2,1)S(1)} collective-permute-done((bf16[192,768]{1,0:T(8,128)(2,1)}, bf16[192,768]{1,0:T(8,128)(2,1)S(1)}, u32[]{:S(2)}, u32[]{:S(2)}) %collective-permute-start.33) | collective-permute-done | bytes 294944 | tf_op jit(solution)/shard_map/ppermute | solution.py:570
  500.0 5.8 shard_map.377
  506.5 1.4 collective-permute-start.35
  507.9 5.4 collective-permute-start.37
  513.6 2.1 collective-permute-start.39
  515.7 2.3 collective-permute-done.37.refs_5_
  518.0 7.5 %collective-permute-done.38.refs_6_ = bf16[96,768]{1,0:T(8,128)(2,1)S(1)} collective-permute-done((bf16[96,768]{1,0:T(8,128)(2,1)}, bf16[96,768]{1,0:T(8,128)(2,1)S(1)}, u32[]{:S(2)}, u32[]{:S(2)}) %collective-permute-start.38) | collective-permute-done | bytes 147488 | tf_op jit(solution)/shard_map/ppermute | solution.py:570
  526.4 3.6 shard_map.378
  530.0 2.7 collective-permute-start.40
  532.8 2.3 collective-permute-start.42
  535.2 1.9 fusion.17.refs_6_
  538.7 8.6 %collective-permute-done.41.refs_3_ = bf16[112,768]{1,0:T(8,128)(2,1)S(1)} collective-permute-done((bf16[112,768]{1,0:T(8,128)(2,1)}, bf16[112,768]{1,0:T(8,128)(2,1)S(1)}, u32[]{:S(2)}, u32[]{:S(2)}) %collective-permute-start.41) | collective-permute-done | bytes 172064 | tf_op jit(solution)/shard_map/ppermute | solution.py:570
  548.0 2.8 shard_map.379
  552.5 1.7 maximum_bitcast_fusion.1
  554.3 1.8 stack_reshape.7
  559.6 1.3 collective-permute-start.51
  560.9 1.5 collective-permute-start.52
  562.4 3.0 maximum_bitcast_fusion
  565.4 1.8 stack_reshape.6
  567.4 3.2 collective-permute-start.53
  570.6 2.4 collective-permute-start.55
  578.8 1.3 multiply_subtract_fusion
  580.1 1.3 pad_maximum_fusion.3.scale
  582.0 10.9 %shard_map.380 = (f32[2,48,2304]{2,1,0:T(8,128)}, f32[2,48,2304]{2,1,0:T(8,128)}, f32[2,48,2304]{2,1,0:T(8,128)}, f32[2,48,768]{2,1,0:T(8,128)}, f32[2,48,768]{2...) custom-call(s32[4]{0:T(128)} %pad_add_fusion.scalars.place_of, ...), custom_call_target="tpu_custom_call" | custom-call | flops 53084160 | bytes 21233664 | tf_op jit(solution)/shard_map/pallas_call | solution.py:551
  (324 shorter events, 49.5 us)
Async XLA Ops:
  7.2 187.1 %all-gather.2.cloned.1.call-start = ((), (), s32[]{:S(2)}) async-start(), calls=%async_computation | async-start | bytes 29601792 | tf_op jit(solution)/shard_map/all_gather | solution.py:958
  216.2 13.0 %collective-permute-start = (bf16[2,512,768]{2,1,0:T(8,128)(2,1)}, bf16[2,512,768]{2,1,0:T(8,128)(2,1)S(1)}, u32[]{:S(2)}, u32[]{:S(2)}) collective-permute-start(bf16[2,512,768]{2,1,0:T(8,128)(2,1)} %get-tuple-element.235.refs_0_), channel_id=1, source_target_pairs={{0,1},{1,0},{2,3},{3,2},{4,5},{5,4},{6,7},{7,6},{8,9},{9,8},{10,11... | collective-permute-start | bytes 4718600 | tf_op jit(solution)/shard_map/ppermute | solution.py:566
  228.8 28.6 %collective-permute-start.1 = (bf16[3,512,768]{2,1,0:T(8,128)(2,1)}, bf16[3,512,768]{2,1,0:T(8,128)(2,1)S(1)}, u32[]{:S(2)}, u32[]{:S(2)}) collective-permute-start(bf16[3,512,768]{2,1,0:T(8,128)(2,1)} %get-tuple-element.237.refs_0_), channel_id=1, source_target_pairs={{0,1},{1,0},{2,3},{3,2},{4,5},{5,4},{6,7},{7,6},{8,9},{9,8},{10,11... | collective-permute-start | bytes 7077896 | tf_op jit(solution)/shard_map/ppermute | solution.py:566
  229.2 27.9 %copy-start.6 = (bf16[2,512,768]{2,1,0:T(8,128)(2,1)}, bf16[2,512,768]{2,1,0:T(8,128)(2,1)S(1)}, u32[]{:S(2)}) copy-start(bf16[2,512,768]{2,1,0:T(8,128)(2,1)S(1)} %collective-permute-done.refs_2_) | copy-start | bytes 4718596
  257.1 13.2 %collective-permute-start.2 = (bf16[2,512,768]{2,1,0:T(8,128)(2,1)}, bf16[2,512,768]{2,1,0:T(8,128)(2,1)S(1)}, u32[]{:S(2)}, u32[]{:S(2)}) collective-permute-start(bf16[2,512,768]{2,1,0:T(8,128)(2,1)} %get-tuple-element.240.refs_0_), channel_id=1, source_target_pairs={{0,1},{1,0},{2,3},{3,2},{4,5},{5,4},{6,7},{7,6},{8,9},{9,8},{10,11... | collective-permute-start | bytes 4718600 | tf_op jit(solution)/shard_map/ppermute | solution.py:566
  270.0 8.5 %collective-permute-start.3 = (bf16[3,512,768]{2,1,0:T(8,128)(2,1)}, bf16[3,512,768]{2,1,0:T(8,128)(2,1)}, u32[]{:S(2)}, u32[]{:S(2)}) collective-permute-start(bf16[3,512,768]{2,1,0:T(8,128)(2,1)} %get-tuple-element.243.refs_0_), channel_id=1, source_target_pairs={{0,1},{1,0},{2,3},{3,2},{4,5},{5,4},{6,7},{7,6},{8,9},{9,8},{10,11... | collective-permute-start | bytes 7077896 | tf_op jit(solution)/shard_map/ppermute | solution.py:566
  278.4 2.3 collective-permute-start.4
  278.7 31.0 %collective-permute-start.7 = (bf16[512,768]{1,0:T(8,128)(2,1)S(1)}, bf16[512,768]{1,0:T(8,128)(2,1)S(1)}, u32[]{:S(2)}, u32[]{:S(2)}) collective-permute-start(bf16[512,768]{1,0:T(8,128)(2,1)S(1)} %add_convert_fusion.refs_4_), channel_id=1, source_target_pairs={{0,1},{1,0},{2,3},{3,2},{4,5},{5,4},{6,7},{7,6},{8,9},{9,8},{10,11... | collective-permute-start | bytes 2359304 | tf_op jit(solution)/shard_map/ppermute | solution.py:566
  289.6 20.1 %collective-permute-start.5 = (bf16[384,768]{1,0:T(8,128)(2,1)}, bf16[384,768]{1,0:T(8,128)(2,1)S(1)}, u32[]{:S(2)}, u32[]{:S(2)}) collective-permute-start(bf16[384,768]{1,0:T(8,128)(2,1)} %get-tuple-element.253), channel_id=1, source_target_pairs={{0,2},{2,0},{4,6},{6,4},{8,10},{10,8},{12,14},{14,12},{16,18},{18,... | collective-permute-start | bytes 1769480 | tf_op jit(solution)/shard_map/ppermute | solution.py:570
  291.1 18.6 %collective-permute-start.6 = (bf16[384,768]{1,0:T(8,128)(2,1)}, bf16[384,768]{1,0:T(8,128)(2,1)S(1)}, u32[]{:S(2)}, u32[]{:S(2)}) collective-permute-start(bf16[384,768]{1,0:T(8,128)(2,1)} %get-tuple-element.254), channel_id=1, source_target_pairs={{0,4},{2,6},{4,0},{6,2},{8,12},{10,14},{12,8},{14,10},{16,20},{18,... | collective-permute-start | bytes 1769480 | tf_op jit(solution)/shard_map/ppermute | solution.py:570
  291.8 17.7 %copy-start.28 = (bf16[512,128]{1,0:T(8,128)(2,1)}, bf16[512,128]{1,0:T(8,128)(2,1)S(1)}, u32[]{:S(2)}) copy-start(bf16[512,128]{1,0:T(8,128)(2,1)S(1)} %fusion.2.refs_9_) | copy-start | bytes 393220
  291.9 17.8 %collective-permute-start.9 = (bf16[512,128]{1,0:T(8,128)(2,1)S(1)}, bf16[512,128]{1,0:T(8,128)(2,1)S(1)}, u32[]{:S(2)}, u32[]{:S(2)}) collective-permute-start(bf16[512,128]{1,0:T(8,128)(2,1)S(1)} %fusion.2.refs_9_), channel_id=1, source_target_pairs={{0,1},{1,0},{2,3},{3,2},{4,5},{5,4},{6,7},{7,6},{8,9},{9,8},{10,11... | collective-permute-start | bytes 393224 | tf_op jit(solution)/shard_map/ppermute | solution.py:566
  292.0 17.6 %copy-start.29 = (bf16[512,128]{1,0:T(8,128)(2,1)}, bf16[512,128]{1,0:T(8,128)(2,1)S(1)}, u32[]{:S(2)}) copy-start(bf16[512,128]{1,0:T(8,128)(2,1)S(1)} %pad.18.refs_5_) | copy-start | bytes 393220
  292.0 17.6 %collective-permute-start.8 = (bf16[512,128]{1,0:T(8,128)(2,1)S(1)}, bf16[512,128]{1,0:T(8,128)(2,1)S(1)}, u32[]{:S(2)}, u32[]{:S(2)}) collective-permute-start(bf16[512,128]{1,0:T(8,128)(2,1)S(1)} %pad.18.refs_5_), channel_id=1, source_target_pairs={{0,1},{1,0},{2,3},{3,2},{4,5},{5,4},{6,7},{7,6},{8,9},{9,8},{10,11... | collective-permute-start | bytes 393224 | tf_op jit(solution)/shard_map/ppermute | solution.py:566
  309.7 16.7 %copy-start.38 = (f32[512,128]{1,0:T(8,128)S(1)}, f32[512,128]{1,0:T(8,128)}, u32[]{:S(2)}) copy-start(f32[512,128]{1,0:T(8,128)} %get-tuple-element.277) | copy-start | bytes 786436
  309.7 3.7 collective-permute-start.10
  324.4 25.5 %collective-permute-start.11 = (bf16[576,768]{1,0:T(8,128)(2,1)}, bf16[576,768]{1,0:T(8,128)(2,1)S(1)}, u32[]{:S(2)}, u32[]{:S(2)}) collective-permute-start(bf16[576,768]{1,0:T(8,128)(2,1)} %get-tuple-element.271), channel_id=1, source_target_pairs={{0,2},{2,0},{4,6},{6,4},{8,10},{10,8},{12,14},{14,12},{16,18},{18,... | collective-permute-start | bytes 2654216 | tf_op jit(solution)/shard_map/ppermute | solution.py:570
  325.9 24.0 %collective-permute-start.12 = (bf16[576,768]{1,0:T(8,128)(2,1)}, bf16[576,768]{1,0:T(8,128)(2,1)S(1)}, u32[]{:S(2)}, u32[]{:S(2)}) collective-permute-start(bf16[576,768]{1,0:T(8,128)(2,1)} %get-tuple-element.272), channel_id=1, source_target_pairs={{0,4},{2,6},{4,0},{6,2},{8,12},{10,14},{12,8},{14,10},{16,20},{18,... | collective-permute-start | bytes 2654216 | tf_op jit(solution)/shard_map/ppermute | solution.py:570
  349.9 4.8 collective-permute-start.13
  350.0 4.7 collective-permute-start.14
  370.3 34.6 %collective-permute-start.15 = (bf16[960,768]{1,0:T(8,128)(2,1)}, bf16[960,768]{1,0:T(8,128)(2,1)S(1)}, u32[]{:S(2)}, u32[]{:S(2)}) collective-permute-start(bf16[960,768]{1,0:T(8,128)(2,1)} %get-tuple-element.301), channel_id=1, source_target_pairs={{0,2},{2,0},{4,6},{6,4},{8,10},{10,8},{12,14},{14,12},{16,18},{18,... | collective-permute-start | bytes 4423688 | tf_op jit(solution)/shard_map/ppermute | solution.py:570
  371.8 34.2 %collective-permute-start.16 = (bf16[960,768]{1,0:T(8,128)(2,1)}, bf16[960,768]{1,0:T(8,128)(2,1)S(1)}, u32[]{:S(2)}, u32[]{:S(2)}) collective-permute-start(bf16[960,768]{1,0:T(8,128)(2,1)} %get-tuple-element.302), channel_id=1, source_target_pairs={{0,4},{2,6},{4,0},{6,2},{8,12},{10,14},{12,8},{14,10},{16,20},{18,... | collective-permute-start | bytes 4423688 | tf_op jit(solution)/shard_map/ppermute | solution.py:570
  372.4 21.8 %collective-permute-start.17 = (bf16[96,768]{1,0:T(8,128)(2,1)}, bf16[96,768]{1,0:T(8,128)(2,1)S(1)}, u32[]{:S(2)}, u32[]{:S(2)}) collective-permute-start(bf16[96,768]{1,0:T(8,128)(2,1)} %get-tuple-element.303), channel_id=1, source_target_pairs={{0,8},{2,10},{4,12},{6,14},{8,0},{10,2},{12,4},{14,6},{16,24},{18,... | collective-permute-start | bytes 442376 | tf_op jit(solution)/shard_map/ppermute | solution.py:570
  372.4 21.9 %collective-permute-start.18 = (bf16[96,768]{1,0:T(8,128)(2,1)}, bf16[96,768]{1,0:T(8,128)(2,1)S(1)}, u32[]{:S(2)}, u32[]{:S(2)}) collective-permute-start(bf16[96,768]{1,0:T(8,128)(2,1)} %get-tuple-element.304), channel_id=1, source_target_pairs={{0,16},{2,18},{4,20},{6,22},{8,24},{10,26},{12,28},{14,30},{16,0},... | collective-permute-start | bytes 442376 | tf_op jit(solution)/shard_map/ppermute | solution.py:570
  374.3 19.9 %collective-permute-start.19 = (bf16[96,768]{1,0:T(8,128)(2,1)}, bf16[96,768]{1,0:T(8,128)(2,1)S(1)}, u32[]{:S(2)}, u32[]{:S(2)}) collective-permute-start(bf16[96,768]{1,0:T(8,128)(2,1)} %get-tuple-element.305), channel_id=1, source_target_pairs={{0,24},{2,26},{4,28},{6,30},{8,16},{10,18},{12,20},{14,22},{16,8},... | collective-permute-start | bytes 442376 | tf_op jit(solution)/shard_map/ppermute | solution.py:570
  406.0 3.6 collective-permute-start.20
  421.7 30.2 %collective-permute-start.21 = (bf16[768,768]{1,0:T(8,128)(2,1)}, bf16[768,768]{1,0:T(8,128)(2,1)S(1)}, u32[]{:S(2)}, u32[]{:S(2)}) collective-permute-start(bf16[768,768]{1,0:T(8,128)(2,1)} %get-tuple-element.334), channel_id=1, source_target_pairs={{0,2},{2,0},{4,6},{6,4},{8,10},{10,8},{12,14},{14,12},{16,18},{18,... | collective-permute-start | bytes 3538952 | tf_op jit(solution)/shard_map/ppermute | solution.py:570
  422.4 29.5 %collective-permute-start.22 = (bf16[768,768]{1,0:T(8,128)(2,1)}, bf16[768,768]{1,0:T(8,128)(2,1)S(1)}, u32[]{:S(2)}, u32[]{:S(2)}) collective-permute-start(bf16[768,768]{1,0:T(8,128)(2,1)} %get-tuple-element.335), channel_id=1, source_target_pairs={{0,4},{2,6},{4,0},{6,2},{8,12},{10,14},{12,8},{14,10},{16,20},{18,... | collective-permute-start | bytes 3538952 | tf_op jit(solution)/shard_map/ppermute | solution.py:570
  424.6 27.2 %collective-permute-start.23 = (bf16[96,768]{1,0:T(8,128)(2,1)}, bf16[96,768]{1,0:T(8,128)(2,1)S(1)}, u32[]{:S(2)}, u32[]{:S(2)}) collective-permute-start(bf16[96,768]{1,0:T(8,128)(2,1)} %get-tuple-element.336), channel_id=1, source_target_pairs={{0,8},{2,10},{4,12},{6,14},{8,0},{10,2},{12,4},{14,6},{16,24},{18,... | collective-permute-start | bytes 442376 | tf_op jit(solution)/shard_map/ppermute | solution.py:570
  424.6 27.3 %collective-permute-start.24 = (bf16[96,768]{1,0:T(8,128)(2,1)}, bf16[96,768]{1,0:T(8,128)(2,1)S(1)}, u32[]{:S(2)}, u32[]{:S(2)}) collective-permute-start(bf16[96,768]{1,0:T(8,128)(2,1)} %get-tuple-element.337), channel_id=1, source_target_pairs={{0,16},{2,18},{4,20},{6,22},{8,24},{10,26},{12,28},{14,30},{16,0},... | collective-permute-start | bytes 442376 | tf_op jit(solution)/shard_map/ppermute | solution.py:570
  426.6 25.3 %collective-permute-start.25 = (bf16[96,768]{1,0:T(8,128)(2,1)}, bf16[96,768]{1,0:T(8,128)(2,1)S(1)}, u32[]{:S(2)}, u32[]{:S(2)}) collective-permute-start(bf16[96,768]{1,0:T(8,128)(2,1)} %get-tuple-element.338), channel_id=1, source_target_pairs={{0,24},{2,26},{4,28},{6,30},{8,16},{10,18},{12,20},{14,22},{16,8},... | collective-permute-start | bytes 442376 | tf_op jit(solution)/shard_map/ppermute | solution.py:570
  429.0 24.6 %copy-start.68 = (f32[768]{0:T(1024)S(1)}, f32[768]{0:T(1024)}, u32[]{:S(2)}) copy-start(f32[768]{0:T(1024)} %get-tuple-element.452) | copy-start | bytes 9220
  453.1 4.8 collective-permute-start.26
  453.1 4.8 collective-permute-start.27
  455.0 2.9 collective-permute-start.29
  455.0 2.8 collective-permute-start.28
  472.8 25.8 %collective-permute-start.30 = (bf16[640,768]{1,0:T(8,128)(2,1)}, bf16[640,768]{1,0:T(8,128)(2,1)S(1)}, u32[]{:S(2)}, u32[]{:S(2)}) collective-permute-start(bf16[640,768]{1,0:T(8,128)(2,1)} %get-tuple-element.379), channel_id=1, source_target_pairs={{0,2},{2,0},{4,6},{6,4},{8,10},{10,8},{12,14},{14,12},{16,18},{18,... | collective-permute-start | bytes 2949128 | tf_op jit(solution)/shard_map/ppermute | solution.py:570
  473.5 25.1 %collective-permute-start.31 = (bf16[576,768]{1,0:T(8,128)(2,1)}, bf16[576,768]{1,0:T(8,128)(2,1)S(1)}, u32[]{:S(2)}, u32[]{:S(2)}) collective-permute-start(bf16[576,768]{1,0:T(8,128)(2,1)} %get-tuple-element.380), channel_id=1, source_target_pairs={{0,4},{2,6},{4,0},{6,2},{8,12},{10,14},{12,8},{14,10},{16,20},{18,... | collective-permute-start | bytes 2654216 | tf_op jit(solution)/shard_map/ppermute | solution.py:570
  474.9 14.1 %collective-permute-start.32 = (bf16[192,768]{1,0:T(8,128)(2,1)}, bf16[192,768]{1,0:T(8,128)(2,1)S(1)}, u32[]{:S(2)}, u32[]{:S(2)}) collective-permute-start(bf16[192,768]{1,0:T(8,128)(2,1)} %get-tuple-element.381), channel_id=1, source_target_pairs={{0,8},{2,10},{4,12},{6,14},{8,0},{10,2},{12,4},{14,6},{16,24},{18,... | collective-permute-start | bytes 884744 | tf_op jit(solution)/shard_map/ppermute | solution.py:570
  474.9 23.7 %collective-permute-start.33 = (bf16[192,768]{1,0:T(8,128)(2,1)}, bf16[192,768]{1,0:T(8,128)(2,1)S(1)}, u32[]{:S(2)}, u32[]{:S(2)}) collective-permute-start(bf16[192,768]{1,0:T(8,128)(2,1)} %get-tuple-element.382), channel_id=1, source_target_pairs={{0,16},{2,18},{4,20},{6,22},{8,24},{10,26},{12,28},{14,30},{16,0},... | collective-permute-start | bytes 884744 | tf_op jit(solution)/shard_map/ppermute | solution.py:570
  476.9 21.7 %collective-permute-start.34 = (bf16[192,768]{1,0:T(8,128)(2,1)}, bf16[192,768]{1,0:T(8,128)(2,1)S(1)}, u32[]{:S(2)}, u32[]{:S(2)}) collective-permute-start(bf16[192,768]{1,0:T(8,128)(2,1)} %get-tuple-element.383), channel_id=1, source_target_pairs={{0,24},{2,26},{4,28},{6,30},{8,16},{10,18},{12,20},{14,22},{16,8},... | collective-permute-start | bytes 884744 | tf_op jit(solution)/shard_map/ppermute | solution.py:570
  500.0 17.9 %copy-start.35 = (f32[1,2,48,768]{3,2,1,0:T(8,128)S(1)}, f32[1,2,48,768]{3,2,1,0:T(8,128)}, u32[]{:S(2)}) copy-start(f32[1,2,48,768]{3,2,1,0:T(8,128)} %get-tuple-element.423.refs_0_) | copy-start | bytes 884740
  500.0 25.4 %copy-start.15 = (f32[1,2,48,768]{3,2,1,0:T(8,128)S(1)}, f32[1,2,48,768]{3,2,1,0:T(8,128)}, u32[]{:S(2)}) copy-start(f32[1,2,48,768]{3,2,1,0:T(8,128)} %get-tuple-element.424.refs_1_) | copy-start | bytes 884740
  505.8 19.7 %collective-permute-start.36 = (bf16[256,768]{1,0:T(8,128)(2,1)}, bf16[256,768]{1,0:T(8,128)(2,1)S(1)}, u32[]{:S(2)}, u32[]{:S(2)}) collective-permute-start(bf16[256,768]{1,0:T(8,128)(2,1)} %get-tuple-element.402), channel_id=1, source_target_pairs={{0,4},{2,6},{4,0},{6,2},{8,12},{10,14},{12,8},{14,10},{16,20},{18,... | collective-permute-start | bytes 1179656 | tf_op jit(solution)/shard_map/ppermute | solution.py:570
  506.5 19.0 %collective-permute-start.35 = (bf16[192,768]{1,0:T(8,128)(2,1)}, bf16[192,768]{1,0:T(8,128)(2,1)S(1)}, u32[]{:S(2)}, u32[]{:S(2)}) collective-permute-start(bf16[192,768]{1,0:T(8,128)(2,1)} %get-tuple-element.401), channel_id=1, source_target_pairs={{0,2},{2,0},{4,6},{6,4},{8,10},{10,8},{12,14},{14,12},{16,18},{18,... | collective-permute-start | bytes 884744 | tf_op jit(solution)/shard_map/ppermute | solution.py:570
  507.9 10.0 %collective-permute-start.37 = (bf16[96,768]{1,0:T(8,128)(2,1)}, bf16[96,768]{1,0:T(8,128)(2,1)S(1)}, u32[]{:S(2)}, u32[]{:S(2)}) collective-permute-start(bf16[96,768]{1,0:T(8,128)(2,1)} %get-tuple-element.403), channel_id=1, source_target_pairs={{0,8},{2,10},{4,12},{6,14},{8,0},{10,2},{12,4},{14,6},{16,24},{18,... | collective-permute-start | bytes 442376 | tf_op jit(solution)/shard_map/ppermute | solution.py:570
  513.3 12.1 %collective-permute-start.38 = (bf16[96,768]{1,0:T(8,128)(2,1)}, bf16[96,768]{1,0:T(8,128)(2,1)S(1)}, u32[]{:S(2)}, u32[]{:S(2)}) collective-permute-start(bf16[96,768]{1,0:T(8,128)(2,1)} %get-tuple-element.404), channel_id=1, source_target_pairs={{0,16},{2,18},{4,20},{6,22},{8,24},{10,26},{12,28},{14,30},{16,0},... | collective-permute-start | bytes 442376 | tf_op jit(solution)/shard_map/ppermute | solution.py:570
  513.6 11.8 %collective-permute-start.39 = (bf16[96,768]{1,0:T(8,128)(2,1)}, bf16[96,768]{1,0:T(8,128)(2,1)S(1)}, u32[]{:S(2)}, u32[]{:S(2)}) collective-permute-start(bf16[96,768]{1,0:T(8,128)(2,1)} %get-tuple-element.405), channel_id=1, source_target_pairs={{0,24},{2,26},{4,28},{6,30},{8,16},{10,18},{12,20},{14,22},{16,8},... | collective-permute-start | bytes 442376 | tf_op jit(solution)/shard_map/ppermute | solution.py:570
  517.9 19.1 %collective-permute-start.43 = (f32[1,2,48,768]{3,2,1,0:T(8,128)S(1)}, f32[1,2,48,768]{3,2,1,0:T(8,128)S(1)}, u32[]{:S(2)}, u32[]{:S(2)}) collective-permute-start(f32[1,2,48,768]{3,2,1,0:T(8,128)S(1)} %copy-done.35), channel_id=1, source_target_pairs={{0,1},{1,0},{2,3},{3,2},{4,5},{5,4},{6,7},{7,6},{8,9},{9,8},{10,11... | collective-permute-start | bytes 884744 | tf_op jit(solution)/shard_map/ppermute | solution.py:566
  525.5 11.6 %collective-permute-start.44 = (f32[1,2,48,768]{3,2,1,0:T(8,128)S(1)}, f32[1,2,48,768]{3,2,1,0:T(8,128)S(1)}, u32[]{:S(2)}, u32[]{:S(2)}) collective-permute-start(f32[1,2,48,768]{3,2,1,0:T(8,128)S(1)} %copy-done.15), channel_id=1, source_target_pairs={{0,1},{1,0},{2,3},{3,2},{4,5},{5,4},{6,7},{7,6},{8,9},{9,8},{10,11... | collective-permute-start | bytes 884744 | tf_op jit(solution)/shard_map/ppermute | solution.py:566
  530.0 8.6 %collective-permute-start.40 = (bf16[112,768]{1,0:T(8,128)(2,1)}, bf16[112,768]{1,0:T(8,128)(2,1)S(1)}, u32[]{:S(2)}, u32[]{:S(2)}) collective-permute-start(bf16[112,768]{1,0:T(8,128)(2,1)} %get-tuple-element.420), channel_id=1, source_target_pairs={{0,8},{2,10},{4,12},{6,14},{8,0},{10,2},{12,4},{14,6},{16,24},{18,... | collective-permute-start | bytes 516104 | tf_op jit(solution)/shard_map/ppermute | solution.py:570
  532.7 14.6 %collective-permute-start.41 = (bf16[112,768]{1,0:T(8,128)(2,1)}, bf16[112,768]{1,0:T(8,128)(2,1)S(1)}, u32[]{:S(2)}, u32[]{:S(2)}) collective-permute-start(bf16[112,768]{1,0:T(8,128)(2,1)} %get-tuple-element.421), channel_id=1, source_target_pairs={{0,16},{2,18},{4,20},{6,22},{8,24},{10,26},{12,28},{14,30},{16,0},... | collective-permute-start | bytes 516104 | tf_op jit(solution)/shard_map/ppermute | solution.py:570
  532.8 14.5 %collective-permute-start.42 = (bf16[112,768]{1,0:T(8,128)(2,1)}, bf16[112,768]{1,0:T(8,128)(2,1)S(1)}, u32[]{:S(2)}, u32[]{:S(2)}) collective-permute-start(bf16[112,768]{1,0:T(8,128)(2,1)} %get-tuple-element.422), channel_id=1, source_target_pairs={{0,24},{2,26},{4,28},{6,30},{8,16},{10,18},{12,20},{14,22},{16,8},... | collective-permute-start | bytes 516104 | tf_op jit(solution)/shard_map/ppermute | solution.py:570
  537.0 20.2 %collective-permute-start.45 = (f32[2,2,48,768]{3,2,1,0:T(8,128)}, f32[2,2,48,768]{3,2,1,0:T(8,128)}, u32[]{:S(2)}, u32[]{:S(2)}) collective-permute-start(f32[2,2,48,768]{3,2,1,0:T(8,128)} %get-tuple-element.432.refs_2_), channel_id=1, source_target_pairs={{0,1},{1,0},{2,3},{3,2},{4,5},{5,4},{6,7},{7,6},{8,9},{9,8},{10,11... | collective-permute-start | bytes 1769480 | tf_op jit(solution)/shard_map/ppermute | solution.py:566
  537.1 19.1 %collective-permute-start.46 = (f32[1,2,48,768]{3,2,1,0:T(8,128)}, f32[1,2,48,768]{3,2,1,0:T(8,128)}, u32[]{:S(2)}, u32[]{:S(2)}) collective-permute-start(f32[1,2,48,768]{3,2,1,0:T(8,128)} %get-tuple-element.433.refs_3_), channel_id=1, source_target_pairs={{0,1},{1,0},{2,3},{3,2},{4,5},{5,4},{6,7},{7,6},{8,9},{9,8},{10,11... | collective-permute-start | bytes 884744 | tf_op jit(solution)/shard_map/ppermute | solution.py:566
  550.8 5.3 collective-permute-start.48
  550.9 6.3 %collective-permute-start.47 = (f32[1,2,48,768]{3,2,1,0:T(8,128)}, f32[1,2,48,768]{3,2,1,0:T(8,128)}, u32[]{:S(2)}, u32[]{:S(2)}) collective-permute-start(f32[1,2,48,768]{3,2,1,0:T(8,128)} %get-tuple-element.434.refs_4_), channel_id=1, source_target_pairs={{0,1},{1,0},{2,3},{3,2},{4,5},{5,4},{6,7},{7,6},{8,9},{9,8},{10,11... | collective-permute-start | bytes 884744 | tf_op jit(solution)/shard_map/ppermute | solution.py:566
  557.2 1.7 collective-permute-start.49
  558.9 8.4 %collective-permute-start.50 = (f32[1,128]{1,0:T(1,128)S(1)}, f32[1,128]{1,0:T(1,128)S(1)}, u32[]{:S(2)}, u32[]{:S(2)}) collective-permute-start(f32[1,128]{1,0:T(1,128)S(1)} %add.116), channel_id=1, source_target_pairs={{0,2},{2,0},{4,6},{6,4},{8,10},{10,8},{12,14},{14,12},{16,18},{18,... | collective-permute-start | bytes 1544 | tf_op jit(solution)/shard_map/ppermute | solution.py:570
  559.6 7.7 %collective-permute-start.51 = (f32[1,128]{1,0:T(1,128)S(1)}, f32[1,128]{1,0:T(1,128)S(1)}, u32[]{:S(2)}, u32[]{:S(2)}) collective-permute-start(f32[1,128]{1,0:T(1,128)S(1)} %add.116), channel_id=1, source_target_pairs={{0,4},{2,6},{4,0},{6,2},{8,12},{10,14},{12,8},{14,10},{16,20},{18,... | collective-permute-start | bytes 1544 | tf_op jit(solution)/shard_map/ppermute | solution.py:570
  560.9 6.4 %collective-permute-start.52 = (f32[1,128]{1,0:T(1,128)S(1)}, f32[1,128]{1,0:T(1,128)S(1)}, u32[]{:S(2)}, u32[]{:S(2)}) collective-permute-start(f32[1,128]{1,0:T(1,128)S(1)} %add.116), channel_id=1, source_target_pairs={{0,6},{2,4},{4,2},{6,0},{8,14},{10,12},{12,10},{14,8},{16,22},{18,... | collective-permute-start | bytes 1544 | tf_op jit(solution)/shard_map/ppermute | solution.py:570
  567.4 6.8 %collective-permute-start.53 = (f32[1,128]{1,0:T(1,128)S(1)}, f32[1,128]{1,0:T(1,128)S(1)}, u32[]{:S(2)}, u32[]{:S(2)}) collective-permute-start(f32[1,128]{1,0:T(1,128)S(1)} %add_add_fusion.1), channel_id=1, source_target_pairs={{0,8},{2,10},{4,12},{6,14},{8,0},{10,2},{12,4},{14,6},{16,24},{18,... | collective-permute-start | bytes 1544 | tf_op jit(solution)/shard_map/ppermute | solution.py:570
  570.6 4.4 collective-permute-start.54
  570.6 5.3 collective-permute-start.55
  (69 other events, 344.4 us)
Sparse Core Ops, SparseCore 0:
  20.0 174.2 all-gather.1

commit v8 on v7

--- a/solution.py
+++ b/solution.py
@@ -70,26 +70,6 @@
 LOW, FULL = jnp.bfloat16, jnp.float32
 
 
-class Lazy:
-    def __init__(self, source, target, sem):
-        self.copy = pltpu.make_async_copy(source, target, sem)
-        self.copy.start()
-        self.here, self.shape = target, target.shape
-
-    def ready(self):
-        if self.copy is not None:
-            self.copy.wait()
-            self.copy = None
-        return self.here
-
-    def __getitem__(self, at):
-        return self.ready()[at]
-
-    @property
-    def at(self):
-        return self.ready().at
-
-
 class Sent:
     def __init__(self, here, there, sems):
         self.here, self.there, self.sems = here, there, sems
@@ -111,33 +91,18 @@
         self.copies.append(copy)
 
 
-def ready(*inputs):
-    for value in inputs:
-        if isinstance(value, Lazy):
-            value.ready()
-
-
 def call(kernel, scalars, outs, ins, anys=(), scratch=(), flops=0, sent=()):
     whole = pl.BlockSpec(memory_space=pltpu.VMEM)
     left = pl.BlockSpec(memory_space=pl.ANY)
-    large = [x.size >= 1 << 16 for x in ins]
-    buffers = [pltpu.VMEM(x.shape, x.dtype) for x, lazy in zip(ins, large) if lazy]
-    buffers += [pltpu.VMEM(*outs[i]) for i in sent]
 
     def body(scalars, *refs):
         refs = list(refs)
         take = lambda n: [refs.pop(0) for _ in range(n)]
-        sources, any_refs, out_refs = take(len(ins)), take(len(anys)), take(len(outs))
-        here, here_out = take(sum(large)), take(len(sent))
-        extra, (sems, out_sems) = refs[:-2], refs[-2:]
-        values = []
-        for source, lazy in zip(sources, large):
-            at = sum(isinstance(v, Lazy) for v in values)
-            values.append(Lazy(source, here[at], sems.at[at]) if lazy else source)
+        in_refs, any_refs, out_refs = take(len(ins)), take(len(anys)), take(len(outs))
+        here = take(len(sent))
         for n, i in enumerate(sent):
-            out_refs[i] = Sent(here_out[n], out_refs[i], out_sems.at[n])
-        kernel(scalars, values, any_refs, out_refs, *extra)
-        ready(*values)
+            out_refs[i] = Sent(here[n], out_refs[i], refs[-1].at[n])
+        kernel(scalars, in_refs, any_refs, out_refs, *(refs[:-1] if sent else refs))
         for i in sent:
             for copy in out_refs[i].copies:
                 copy.wait()
@@ -146,15 +111,12 @@
         body,
         out_shape=[jax.ShapeDtypeStruct(s, t) for s, t in outs],
         in_specs=[pl.BlockSpec(memory_space=pltpu.SMEM)]
-        + [left if lazy else whole for lazy in large]
+        + [whole] * len(ins)
         + [left] * len(anys),
         out_specs=[left if i in sent else whole for i in range(len(outs))],
-        scratch_shapes=buffers
+        scratch_shapes=[pltpu.VMEM(*outs[i]) for i in sent]
         + list(scratch)
-        + [
-            pltpu.SemaphoreType.DMA((max(sum(large), 1),)),
-            pltpu.SemaphoreType.DMA((max(len(sent), 1), 4)),
-        ],
+        + [pltpu.SemaphoreType.DMA((len(sent), 5))] * (len(sent) > 0),
         compiler_params=pltpu.CompilerParams(vmem_limit_bytes=VMEM_LIMIT),
         cost_estimate=pl.CostEstimate(
             flops=flops,
@@ -164,9 +126,10 @@
     )(scalars, *ins, *anys)
 
 
-def fetch(sources, targets, sems):
+def fetch(sources, targets, sems, first=0):
     copies = [
-        pltpu.make_async_copy(s, t, sems.at[i]) for i, (s, t) in enumerate(zip(sources, targets))
+        pltpu.make_async_copy(s, t, sems.at[first + i])
+        for i, (s, t) in enumerate(zip(sources, targets))
     ]
     for c in copies:
         c.start()
@@ -221,7 +184,6 @@
     normed, _, _ = normalize(resid[...], gains[0:1], gains[1:2])
     normed_low, attended = pack.at[0], pack.at[1]
     normed_low[...] = normed.astype(LOW)
-    pack.send(0)
     bias[...] = jnp.where(seg_col[...] == seg_row[...], 0.0, -1000000000.0)
     for place in range(2):
         copies[place].wait()
@@ -232,19 +194,16 @@
                 x = x * cosine[...] + swap_halves(x) * sine[...]
                 x = (x * scale if scale != 1.0 else x).astype(LOW)
                 target[:, place * half + p * 128 : place * half + (p + 1) * 128] = x
-    query.send()
-    keys.send()
     for place in range(2):
         copies[2 + place].wait()
         values[:, place * half : (place + 1) * half] = dot(
             normed_low[...], matrix(w_b, place, 0, half)
         ).astype(LOW)
-    values.send()
 
     lse[...] = jnp.zeros_like(lse)
 
-    def pair(p, _):
-        columns = pl.ds(pl.multiple_of(p * 128, 128), 128)
+    for p in range(width // 128):
+        columns = slice(p * 128, (p + 1) * 128)
         q, k, v = query[:, columns], keys[:, columns], values[:, columns]
         out = []
         for head in range(2):
@@ -258,11 +217,7 @@
             lane = lax.broadcasted_iota(jnp.int32, lse.shape, 1)
             lse[...] = jnp.where(lane == 2 * p + head, top + jnp.log(total), lse[...])
         attended[:, columns] = jnp.where(head_mask(out[0].shape, 0), out[0], out[1]).astype(LOW)
-        return 0
-
-    lax.fori_loop(0, width // 128, pair, 0)
     attended[...] = ordered(first, attended[:, :half], attended[:, half:])
-    pack.send(1)
     out = ordered(
         first,
         dot(attended[...], matrix(w_b, 0, half, width)),
@@ -288,7 +243,6 @@
             pltpu.SemaphoreType.DMA((4,)),
         ],
         8 * length * width * width + 4 * length * length * width,
-        sent=(1, 2, 3, 5),
     )
 
 
@@ -296,39 +250,69 @@
 GELU_CUBE = 0.044715
 
 
-def hidden_tiles(weights, core, base, width):
-    tiles = [
-        [tile_of(weights, c, base + t * width) for c in (core, 1 - core) for t in pair]
-        for pair in ((2, 3), (4, 5))
+def fetch_hidden(weights, base, ups, downs, sems):
+    blocks, _, rows, _ = weights.shape
+    width = blocks * rows
+    half, some = width // 2, max(blocks // 4, 1)
+    copies = {}
+    for t in range(4):
+        copies[0, t] = fetch(
+            [tile_of(weights, t // 2, base + (2 + t % 2) * width)], [ups.at[t]], sems, t
+        )
+        if blocks >= 4 or t == 0:
+            sources, targets = [], []
+            for core in range(2):
+                for j in range(4):
+                    at = base + 4 * width + j * half
+                    sources.append(weights.at[pl.ds(t * some, some), core, :, at : at + half])
+                    targets.append(
+                        downs.at[pl.ds(t * some, some), j, :, core * half : (core + 1) * half]
+                    )
+            copies[1, t] = fetch(sources, targets, sems, 4 + 8 * t)
+
+    def wait(which, t):
+        for copy in copies.pop((which, t), []):
+            copy.wait()
+
+    return wait
+
+
+def rows_of(downs, t):
+    blocks, parts, rows, width = downs.shape
+    if blocks >= 4:
+        some = blocks // 4
+        return downs[t * some : (t + 1) * some].reshape(some * parts * rows, width)
+    return downs[0, t]
+
+
+def hidden_scratch(weights):
+    blocks, _, rows, _ = weights.shape
+    return [
+        tile_scratch(4, weights),
+        pltpu.VMEM((blocks, 4, rows, blocks * rows), LOW),
+        pltpu.SemaphoreType.DMA((36,)),
     ]
-    return tiles[0], tiles[1]
 
 
 def hidden_forward_kernel(base, place_of, ins, anys, outs, ups, downs, sems):
     middle, gains = ins
-    output, active, pack, hidden = outs
-    u, d = hidden_tiles(anys[0], place_of[0], base, middle.shape[1])
-    copies = fetch(
-        [r for t in range(4) for r in (u[t], d[t])],
-        [w.at[t] for t in range(4) for w in (ups, downs)],
-        sems,
-    )
+    output, pack, hidden = outs
+    wait = fetch_hidden(anys[0], base, ups, downs, sems)
     normed, _, _ = normalize(middle[...], gains[0:1], gains[1:2])
     pack[0] = normed.astype(LOW)
     pack.send(0)
     for t in range(4):
-        copies[2 * t].wait()
+        wait(0, t)
         x = dot(pack[0], matrix(ups, t))
         hidden[t] = x
         hidden.send(t)
         inner = jnp.tanh(x * (GELU_SCALE + (GELU_SCALE * GELU_CUBE) * (x * x)))
         value = x * 0.5
         value = (value + value * inner).astype(LOW)
-        target, at = (active, t) if t < 2 else (pack, t - 1)
-        target[at] = value
-        target.send(at)
-        copies[2 * t + 1].wait()
-        product = dot(value, matrix(downs, t))
+        pack[1 + t] = value
+        pack.send(1 + t)
+        wait(1, t)
+        product = dot(value, rows_of(downs, t))
         output[...] = (middle[...] if t == 0 else output[...]) + product
 
 
@@ -338,43 +322,42 @@
     return call(
         functools.partial(hidden_forward_kernel, base),
         place,
-        [(one, FULL), ((2,) + one, LOW), ((3,) + one, LOW), ((4,) + one, FULL)],
+        [(one, FULL), ((5,) + one, LOW), ((4,) + one, FULL)],
         [middle, gains],
         [weights],
-        [
-            tile_scratch(4, weights),
-            tile_scratch(4, weights),
-            pltpu.SemaphoreType.DMA((8,)),
-        ],
+        hidden_scratch(weights),
         16 * length * width * width,
-        sent=(1, 2, 3),
-    )
-
-
-def hidden_back_kernel(base, place_of, ins, anys, outs, ups, downs, hidden_here, total, sems):
+        sent=(1, 2),
+    )
+
+
+def hidden_back_kernel(base, place_of, ins, anys, outs, ups, downs, sems, hidden_here, total, own_sems):
     branch, grad, middle, gains = ins
     hidden, weights = anys
     grad_middle, grad_gains, grad_own, grad_other = outs
-    u, d = hidden_tiles(weights, place_of[0], base, middle.shape[1])
-    copies = fetch(
-        [r for t in range(4) for r in (d[t], hidden.at[t], u[t])],
-        [w.at[t] for t in range(4) for w in (downs, hidden_here, ups)],
-        sems,
-    )
+    wait = fetch_hidden(weights, base, ups, downs, sems)
+    copies = fetch([hidden.at[t] for t in range(4)], [hidden_here.at[t] for t in range(4)], own_sems)
     for t in range(4):
-        copies[3 * t].wait()
-        grad_active = dot_nt(branch[...], matrix(downs, t))
-        copies[3 * t + 1].wait()
+        wait(1, t)
+        grad_active = dot_nt(branch[...], rows_of(downs, t))
+        copies[t].wait()
         x = hidden_here[t]
         square = x * x
         inner = jnp.tanh(x * (GELU_SCALE + (GELU_SCALE * GELU_CUBE) * square))
         slope = x * (GELU_SCALE + (3.0 * GELU_SCALE * GELU_CUBE) * square)
         slope = (0.5 + 0.5 * inner) * (1.0 + slope * (1.0 - inner))
         value = (grad_active * slope).astype(LOW)
-        target = grad_own if t < 2 else grad_other
-        target[t % 2] = value
-        target.send(t % 2)
-        copies[3 * t + 2].wait()
+        mine = place_of[0] == t // 2
+
+        @pl.when(mine)
+        def _():
+            grad_own[t % 2] = value
+
+        @pl.when(jnp.logical_not(mine))
+        def _():
+            grad_other[t % 2] = value
+
+        wait(0, t)
         product = dot_nt(value, matrix(ups, t))
         total[...] = product if t == 0 else total[...] + product
     _, unit, inverse = normalize(middle[...], gains[0:1], gains[1:2])
@@ -393,22 +376,20 @@
         [(one, FULL), ((2, width), FULL), ((2,) + one, LOW), ((2,) + one, LOW)],
         [branch, grad, middle, gains],
         [hidden, weights],
-        [
-            tile_scratch(4, weights),
-            tile_scratch(4, weights),
+        hidden_scratch(weights)
+        + [
             pltpu.VMEM((4,) + one, FULL),
             pltpu.VMEM(one, FULL),
-            pltpu.SemaphoreType.DMA((12,)),
+            pltpu.SemaphoreType.DMA((4,)),
         ],
         16 * length * width * width,
-        sent=(2, 3),
     )
 
 
 def attention_back_kernel(base, place_of, ins, anys, outs, w_a, w_b, bias, ga, gq, gk, gv, sems):
     grad_middle, query, keys, values, lse, seg_col, seg_row, cosine, sine, gains, resid = ins
     (weights,) = anys
-    grad, branch, grad_gains, grad_own, grad_other = outs
+    grad, branch, branch_own, branch_other, grad_gains, grad_own, grad_other = outs
     width = resid.shape[1]
     half = width // 2
     cores = (place_of[0], 1 - place_of[0])
@@ -432,17 +413,16 @@
     natural = natural.astype(LOW)
     ga[:, :half] = jnp.where(first, natural[:, :half], natural[:, half:])
     ga[:, half:] = jnp.where(first, natural[:, half:], natural[:, :half])
-    ready(query, keys, values, lse, cosine, sine)
-
-    def pair(p, _):
-        columns = pl.ds(pl.multiple_of(p * 128, 128), 128)
+
+    for p in range(width // 128):
+        columns = slice(p * 128, (p + 1) * 128)
         q, k, v, g = query[:, columns], keys[:, columns], values[:, columns], ga[:, columns]
         out_q, out_k, out_v = [], [], []
         for head in range(2):
             mask = head_mask(q.shape, head)
             zero = jnp.zeros_like(q)
             scores = dot_nt(k, jnp.where(mask, q, zero)) + bias[...]
-            probs = jnp.exp(scores - lse[pl.ds(2 * p + head, 1), :])
+            probs = jnp.exp(scores - lse[2 * p + head : 2 * p + head + 1, :])
             grad_probs = dot_nt(v, jnp.where(mask, g, zero))
             across = jnp.sum(probs * grad_probs, 0, keepdims=True)
             grad_scores = (probs * (grad_probs - across)).astype(LOW)
@@ -455,15 +435,11 @@
             x = x * cosine[...] - swap_halves(x) * sine[...]
             target[:, columns] = x.astype(LOW)
         gv[:, columns] = jnp.where(head_mask(out_v[0].shape, 0), out_v[0], out_v[1]).astype(LOW)
-        return 0
-
-    lax.fori_loop(0, width // 128, pair, 0)
     for place in (1, 0):
         columns = slice(place * half, (place + 1) * half)
         grads[place][0, :, :half] = gq[:, columns]
         grads[place][0, :, half:] = gk[:, columns]
         grads[place][1, :, :half] = gv[:, columns]
-        grads[place].send()
     copies[2].wait()
     copies[3].wait()
     total = dot_nt(grad_own[0], matrix(w_a, 0)) + dot_nt(grad_other[0], matrix(w_a, 1))
@@ -473,7 +449,10 @@
     back, gain, bias_grad = normalize_back(total, unit, inverse, gains[0:1])
     back = grad_middle[...] + back
     grad[...] = back
-    branch[...] = back.astype(LOW)
+    back = back.astype(LOW)
+    branch[...] = back
+    branch_own[...] = jnp.where(first, back[:, :half], back[:, half:])
+    branch_other[...] = jnp.where(first, back[:, half:], back[:, :half])
     grad_gains[0:1] = gain
     grad_gains[1:2] = bias_grad
 
@@ -484,7 +463,10 @@
     return call(
         functools.partial(attention_back_kernel, base),
         place,
-        [(one, FULL), (one, LOW), ((2, width), FULL)] + [((2,) + one, LOW)] * 2,
+        [(one, FULL), (one, LOW)]
+        + [((length, width // 2), LOW)] * 2
+        + [((2, width), FULL)]
+        + [((2,) + one, LOW)] * 2,
         [grad_middle, query, keys, values, lse.T[: width // HD]]
         + [segments[:, None], segments[None, :], cosine, sine, gains, resid],
         [weights],
@@ -496,7 +478,6 @@
         + [pltpu.VMEM(one, LOW)] * 4
         + [pltpu.SemaphoreType.DMA((4,))],
         8 * length * width * width + 10 * length * length * width,
-        sent=(3, 4),
     )
 
 
@@ -510,9 +491,9 @@
 
 
 def optimizer_kernel(chunks, layers, place_of, scale, *refs):
-    n = (len(refs) - 25) // 2
-    own, other, up, masters = refs[:n], refs[n : 2 * n], refs[2 * n], refs[2 * n + 1 : 2 * n + 13]
-    outs = refs[2 * n + 13 :]
+    n = (len(refs) - 24) // 2
+    own, other, masters = refs[:n], refs[n : 2 * n], refs[2 * n : 2 * n + 12]
+    outs = refs[2 * n + 12 :]
     first = place_of[0] == 0
     count, factor = scale[0], scale[1]
 
@@ -530,7 +511,7 @@
     rows, width = own[0].shape[-2:]
     half = width // 2
     for l in range(layers):
-        mixer, down = chunks[l]
+        mixer, up, down = chunks[l]
         for core in range(2):
             columns = lambda p: pl.ds(p * width + core * half, half)
             value = tile(mixer, 0, core)
@@ -540,16 +521,18 @@
             step(0, (l, slice(None), columns(2)), value[:, :half])
             step(1, (l, slice(None), columns(0)), value[:, half:])
             for s in range(2):
-                at = (l, pl.ds((2 * core + s) * rows, rows), slice(None))
-                step(3, at, tile(down, s, core))
-        step(2, l, up[l])
-
-
-def optimizer(place, scale, chunks, own, other, up, masters):
-    ins = list(own) + list(other) + [up] + list(masters)
+                step(2, (l, slice(None), pl.ds((2 * core + s) * width, width)), tile(up, s, core))
+                value = tile(down, s, core)
+                for j in range(2):
+                    at = (l, pl.ds((2 * s + j) * rows, rows), columns(0))
+                    step(3, at, value[:, j * half : (j + 1) * half])
+
+
+def optimizer(place, scale, chunks, own, other, masters):
+    ins = list(own) + list(other) + list(masters)
     whole = pl.BlockSpec(memory_space=pltpu.VMEM)
     return pl.pallas_call(
-        functools.partial(optimizer_kernel, chunks, up.shape[0]),
+        functools.partial(optimizer_kernel, chunks, len(chunks)),
         out_shape=[jax.ShapeDtypeStruct(m.shape, m.dtype) for m in masters],
         in_specs=[pl.BlockSpec(memory_space=pltpu.SMEM)] * 2 + [whole] * len(ins),
         out_specs=[whole] * len(masters),
@@ -560,6 +543,26 @@
             transcendentals=0,
         ),
     )(place, scale, *ins)
+
+
+def pack_kernel(layers, place_of, ins, anys, outs):
+    inward, outward, expand, shrink, small = ins
+    (out,) = outs
+    first = place_of[0] == 0
+    rows = inward.shape[1]
+    width = inward.shape[2] // 3
+    half = width // 2
+    at = small.shape[1]
+    out[:, :at] = small[...]
+    for l in range(layers):
+        sources = [inward[l, :, p * width : (p + 1) * width] for p in range(3)] + [outward[l]]
+        sources.append(expand[l])
+        sources += [shrink[l, j * rows : (j + 1) * rows] for j in range(shrink.shape[1] // rows)]
+        for value in sources:
+            part = value.shape[1] // 2
+            value = jnp.where(first, value[:, :part], value[:, part:])
+            out[:, at : at + part] = value.astype(LOW)
+            at += part
 
 
 def swap_cores(value):
@@ -612,7 +615,7 @@
     to_z = pop(twice, 3)
     (share,), (small_share,), (squares,) = pop(done), pop(small_done), pop(done)
     (totals,) = pop(last)
-    (tile,), (small_tile,) = pop(new), pop(small_new)
+    (tile,), (unit,), (small_tile,) = pop(new), pop(new), pop(small_new)
     rows = (out_once if new else out_twice if once else out_done if twice else share).shape[-2]
     rows = rows // (8 if new else 4 if once else 1)
     bits, z = (place_of[1], place_of[2]), place_of[3]
@@ -643,26 +646,38 @@
             parts.append(ref[at, lanes * SMALL : (lanes + 1) * SMALL])
         return jnp.concatenate(parts, 0).astype(FULL)
 
+    def summed(products):
+        total = None
+        for left, right in products:
+            product = cross(factor(left), factor(right))
+            total = product if total is None else total + product
+        return total
+
     for p in range(new):
+        if len(jobs[p]) == 4:
+            for quarter, products in enumerate(jobs[p]):
+                unit[...] = summed(products)
+                half = unit.shape[1]
+                for index in range(4):
+                    for s in range(2):
+                        for j in range(2):
+                            tile[s, block(quarter * 4 + index), j * half : (j + 1) * half] = unit[
+                                block(index * 4 + 2 * s + j), :
+                            ]
+        else:
+            for s in range(2):
+                for low, high, products in jobs[p][s]:
+                    tile[s, :, low:high] = summed(products)
         for s in range(2):
-            for low, high, products in jobs[2 * p + s]:
-                total = None
-                for left, right in products:
-                    product = cross(factor(left), factor(right))
-                    total = product if total is None else total + product
-                tile[:, low:high] = total
             for zz in range(4):
                 for other in range(2):
                     at = zz * 2 + other
                     index = lambda bit: zz * 4 + (other * 2 + bit if s == 0 else bit * 2 + other)
-                    to[s][block(p * 8 + at), :] = tile[block(index(1 - bits[s])), :].astype(LOW)
-                    out_once[p, s, block(at), :] = tile[block(index(bits[s])), :]
+                    to[s][block(p * 8 + at), :] = tile[s, block(index(1 - bits[s])), :].astype(LOW)
+                    out_once[p, s, block(at), :] = tile[s, block(index(bits[s])), :]
     if small_new:
         products, norms_at = small_job
-        total = None
-        for left, right in products:
-            product = cross(factor(left), factor(right))
-            total = product if total is None else total + product
+        total = summed(products)
         norms = jnp.concatenate([ins[mine][...] + ins[theirs][...] for mine, theirs in norms_at], 0)
         high = norms.astype(LOW)
         shape = (norms.shape[0], SMALL)
@@ -765,11 +780,12 @@
             arrays.append(array)
             return (len(arrays) - 1, *place)
 
+        numbered = lambda products: [(number(l), number(r)) for l, r in products]
         for pair in chunk:
-            for tile in pair:
-                jobs.append(
-                    [(a, b, [(number(l), number(r)) for l, r in ps]) for a, b, ps in tile]
-                )
+            if len(pair) == 4:
+                jobs.append([numbered(products) for products in pair])
+            else:
+                jobs.append([[(a, b, numbered(ps)) for a, b, ps in tile] for tile in pair])
         small_job = None
         if small is not None:
             small_job = (
@@ -802,7 +818,10 @@
             outs.append(((1, width), FULL))
         outs += [((1, SMALL), FULL)] * last
         length = 2 * arrays[0].shape[-2] if new else 0
-        scratch = [pltpu.VMEM((16 * rows, width), FULL)] if new else []
+        scratch = []
+        if new:
+            scratch.append(pltpu.VMEM((2, 16 * rows, width), FULL))
+            scratch.append(pltpu.VMEM((16 * rows, width // 2), FULL))
         scratch += [pltpu.VMEM((16 * rows, SMALL), FULL)] * smalls[0]
         got = list(
             call(
@@ -870,13 +889,18 @@
             array = array if index is None else array[index]
             return array if low is None else array[:, low:high]
 
-        def summed(tile):
-            parts = [sum(cross(factor(l), factor(r)) for l, r in ps) for _, _, ps in tile]
-            return lax.psum_scatter(
-                jnp.concatenate(parts, 1), "fsdp", scatter_dimension=0, tiled=True
-            )
-
-        share = jnp.stack([jnp.stack([summed(tile) for tile in pair]) for pair in chunk])
+        summed = lambda products: sum(cross(factor(l), factor(r)) for l, r in products)
+        scatter = lambda v: lax.psum_scatter(v, "fsdp", scatter_dimension=0, tiled=True)
+        shares = []
+        for pair in chunk:
+            if len(pair) == 4:
+                v = scatter(jnp.concatenate([summed(products) for products in pair], 0))
+                v = v.reshape(2, 2, -1, v.shape[1])
+                shares.append(jnp.concatenate([v[:, 0], v[:, 1]], 2))
+            else:
+                tiles = [jnp.concatenate([summed(ps) for _, _, ps in t], 1) for t in pair]
+                shares.append(jnp.stack([scatter(t) for t in tiles]))
+        share = jnp.stack(shares)
         self.shares.append((share, swap_cores(share)))
         self.squares.append(jnp.sum(share * share, (0, 1, 2))[None])
         return ties
@@ -886,16 +910,6 @@
 
     def left(self):
         return False
-
-
-def up_to_parts(expand_shard, size, rows, parts):
-    r = expand_shard.shape[0]
-    return expand_shard.reshape(r, size, parts, rows).transpose(0, 2, 1, 3).reshape(r, -1)
-
-
-def up_from_parts(expand_shard, size, rows, parts):
-    r = expand_shard.shape[0]
-    return expand_shard.reshape(r, parts, size, rows).transpose(0, 2, 1, 3).reshape(r, -1)
 
 
 def half_of(value, core):
@@ -932,7 +946,6 @@
     rows = inward.shape[1]
     width = rows * fsdp
     half = width // 2
-    parts = shrink.shape[1] // rows
     fast = fsdp == 16 and rows == 48
     core, index = lax.axis_index("dp"), lax.axis_index("fsdp")
     bit = lambda b: lax.rem(lax.div(index, b), 2)
@@ -940,25 +953,28 @@
     weight = masked.astype(FULL)
     inputs = jnp.where(masked == 1, V - 1, codons)
 
-    def tiles_of(l):
-        w_in, w_out = inward[l].astype(LOW), outward[l].astype(LOW)
-        pieces = [half_of(w_in[:, p * width : (p + 1) * width], core) for p in range(3)]
-        pieces.append(half_of(w_out, core))
-        mixer = [jnp.concatenate(pieces[:2], 1), jnp.concatenate(pieces[2:], 1)]
-        up = half_of(up_to_parts(expand[l].astype(LOW), fsdp, rows, parts), core)
-        down = lax.dynamic_slice_in_dim(shrink[l].astype(LOW), core * 2 * rows, 2 * rows, 0)
-        return mixer + [up[:, :width], up[:, width:], down[:rows], down[rows:]]
-
     norms = norm_params.shape[0] * 2
     small = jnp.concatenate(
         [codon_table.astype(LOW), norm_params.astype(LOW).reshape(norms, rows)], 0
     )
     small = jnp.pad(small.T, ((0, 0), (0, -small.shape[0] % 128)))
-    weights = jnp.concatenate([small] + sum([tiles_of(l) for l in range(layers)], []), 1)
+    (weights,) = call(
+        functools.partial(pack_kernel, layers),
+        place,
+        [((rows, small.shape[1] + layers * 6 * width), LOW)],
+        [inward, outward, expand, shrink, small],
+    )
     weights = lax.all_gather(weights, ("fsdp", "dp"), axis=0, tiled=True)
     weights = weights.reshape(fsdp, 2, rows, -1)
     if not fast:
-        weights = weights.transpose(1, 0, 2, 3).reshape(1, 2, width, -1)
+        columns = [weights[:, :, :, : small.shape[1]]]
+        for at in range(small.shape[1], weights.shape[3], 6 * width):
+            columns.append(weights[:, :, :, at : at + 4 * width])
+            quarter = weights[:, :, :, at + 4 * width : at + 6 * width]
+            quarter = quarter.reshape(fsdp, 2, rows, 4, half).transpose(1, 0, 3, 2, 4)
+            quarter = quarter.reshape(2, 4, width, half).transpose(0, 2, 1, 3)
+            columns.append(quarter.reshape(2, fsdp, rows, 2 * width).transpose(1, 0, 2, 3))
+        weights = jnp.concatenate(columns, 3).transpose(1, 0, 2, 3).reshape(1, 2, width, -1)
     small = weights[:, 0, :, : V + norms].reshape(width, V + norms).T
     base = lambda l: weights.shape[3] - (layers - l) * 6 * width
     table_low = small[:V]
@@ -978,12 +994,12 @@
             middle, came = tie(middle, kept[-1][-1])
             kept[-1] = kept[-1][:-1] + (came,)
         pack_came = swap_cores(pack)
-        output, active, pack_mid, hidden = hidden_forward(
+        output, pack_mid, hidden = hidden_forward(
             place, middle, weights, base(l), gain[1]
         )
         output, pack_came = tie(output, pack_came)
         kept.append(
-            (resid, query, keys, values, lse, pack, pack_came, middle, hidden, active, pack_mid)
+            (resid, query, keys, values, lse, pack, pack_came, middle, hidden, pack_mid)
             + (swap_cores(pack_mid),)
         )
         resid = output
@@ -1006,6 +1022,7 @@
         grad_head, unit_out, inverse_out, final_gain[0]
     )
     branch = grad.astype(LOW)
+    branch_own, branch_other = half_of(branch, core), half_of(branch, 1 - core)
     grad_norms = [grad_final_gain, grad_final_bias]
     grad, branch, came = tie(grad, branch, kept[-1][-1])
     kept[-1] = kept[-1][:-1] + (came,)
@@ -1017,15 +1034,16 @@
     ]
     chunk = []
     for l in reversed(range(layers)):
-        (resid, query, keys, values, lse, pack, pack_came, middle, hidden, active, pack_mid, mid_came) = kept[l]
+        (resid, query, keys, values, lse, pack, pack_came, middle, hidden, pack_mid, mid_came) = kept[l]
         gain = gains[2 * l : 2 * l + 2]
-        branch_came = swap_cores(branch)
+        branch_came = swap_cores(branch_other)
         chunk.append(
             [
-                tile(
-                    whole(active, s), whole(branch), whole(mid_came, 1 + s), whole(branch_came)
-                )
-                for s in range(2)
+                [
+                    (whole(pack_mid, 1 + t), whole(branch_own)),
+                    (whole(mid_came, 1 + t), whole(branch_came)),
+                ]
+                for t in range(4)
             ]
         )
         grad, branch = rounds.step(chunk, grad, branch)
@@ -1050,12 +1068,14 @@
             ],
             grad_middle,
         )
-        grad, branch, gains_in, mix_own, mix_other = attention_back(
+        grad, branch, branch_own, branch_other, gains_in, mix_own, mix_other = attention_back(
             place, grad_middle, resid, weights, base(l), gain[0], cosine, sine, segments,
             query, keys, values, lse,
         )
         grad_norms = [gains_in, gains_mid] + grad_norms
-        grad, branch, mix_own, mix_other = rounds.finish(grad, branch, mix_own, mix_other)
+        grad, branch, branch_own, branch_other, mix_own, mix_other = rounds.finish(
+            grad, branch, branch_own, branch_other, mix_own, mix_other
+        )
         mix_came = swap_cores(mix_other)
         products = lambda i, a, b: [
             ((pack, i, None, None), (mix_own, 1, a, b)),
@@ -1106,15 +1126,9 @@
         ordered = (jnp.where(core == 0, own, other), jnp.where(core == 0, other, own))
         return [v[s] for v in ordered for s in range(2)]
 
-    share_up = jnp.stack(
-        [
-            up_from_parts(jnp.concatenate(tiles_at(at + 1, 0), 1), fsdp, rows, parts)
-            for at, _ in places
-        ]
-    )
     share_small = (share_small[:V], share_small[V:].reshape(-1, 2, rows))
     if not fast:
-        share_in, share_out, share_down = [], [], []
+        share_in, share_out, share_up, share_down = [], [], [], []
         side = lambda *values: jnp.concatenate(values, 1)
         for at, pair in places:
             a_0, b_0, a_1, b_1 = tiles_at(at + 2, 0)
@@ -1125,9 +1139,20 @@
                 )
             )
             share_out.append(side(b_0[:, half:], b_1[:, half:]))
-            share_down.append(jnp.concatenate(tiles_at(at, pair), 0))
-        share_in, share_out, share_down = (
-            jnp.stack(v) for v in (share_in, share_out, share_down)
+            share_up.append(side(*tiles_at(at + 1, 0)))
+            a_0, b_0, a_1, b_1 = tiles_at(at, pair)
+            share_down.append(
+                jnp.concatenate(
+                    [
+                        side(x[:, j * half : (j + 1) * half], y[:, j * half : (j + 1) * half])
+                        for x, y in ((a_0, a_1), (b_0, b_1))
+                        for j in range(2)
+                    ],
+                    0,
+                )
+            )
+        share_in, share_out, share_up, share_down = (
+            jnp.stack(v) for v in (share_in, share_out, share_up, share_down)
         )
     grad_norm = jnp.sqrt(square_total) / count
     factor = CLIP / jnp.maximum(grad_norm, CLIP)
@@ -1143,10 +1168,10 @@
     )
     if fast:
         matrices = [v for group in zip(masters[:4], firsts[:4], seconds[:4]) for v in group]
-        chunks = [((at + 2, 0), (at, pair)) for at, pair in places]
+        chunks = [((at + 2, 0), (at + 1, 0), (at, pair)) for at, pair in places]
         own, other = zip(*shares)
         scale = jnp.stack([count, factor])
-        values = list(optimizer(place, scale, chunks, own, other, share_up, matrices))
+        values = list(optimizer(place, scale, chunks, own, other, matrices))
     else:
         values = []
         for index, grad in enumerate((share_in, share_out, share_up, share_down)):

time: 610 us -> 602 us (0.987)
  local copies, waits for them, and re-layouts: 34.6 us -> 20.3 us
  waiting for transfers between devices: 239 us -> 250 us
    ppermute x23, waiting for transfers between devices: 15.7 us -> 24.7 us  [swap_cores(): return lax.ppermute(value, 'dp', [(0, 1), (1, 0)])]
    unnamed x166 -> x134, local copies, waits for them, and re-layouts: 14.3 us -> 11.7 us
    pallas_call x16 -> x17, Pallas kernels: 220 us -> 221 us  [call(): pl.pallas_call(body, out_shape=[jax.ShapeDtypeStruct(s, t) for s, t in ou...]
  transfers between devices with their start and end apart: 57 -> 57, of which waited for: 16 -> 22; matrix products, arithmetic and copies ran while one was open for 5% -> 3% of each run, Pallas kernels for 24% -> 22%
where the time goes in v8:
time: 602 us; the launch traced here: 593 us
  waiting for transfers between devices  250 us (42%)
  Pallas kernels  231 us (38%)
  starting transfers between devices  53.4 us (9%)
  local copies, waits for them, and re-layouts  20.3 us (3%)
  between operations  17.7 us (3%)
  other arithmetic  17.3 us (3%)
    pallas_call x17, Pallas kernels, call(): pl.pallas_call(body, out_shape=[jax.ShapeDtypeStruct(s, t) for s, t in ou...  221 us
    all_gather x1, waiting for transfers between devices, body(): weights = lax.all_gather(weights, ('fsdp', 'dp'), axis=0, tiled=True)  171 us
    ppermute x33, waiting for transfers between devices, across(): return lax.ppermute(value, 'fsdp', [(i, i ^ mask) for i in range(size)])  53.7 us
    ppermute x33, starting transfers between devices, across(): return lax.ppermute(value, 'fsdp', [(i, i ^ mask) for i in range(size)])  48.2 us
    ppermute x23, waiting for transfers between devices, swap_cores(): return lax.ppermute(value, 'dp', [(0, 1), (1, 0)])  24.7 us
  transfers between devices with their start and end apart: 57, of which 22 were waited for; matrix products, arithmetic and copies ran while one was open for 3% of the time, Pallas kernels for 22%

profile of v8, /device:TPU:0, one launch (start us, length us, event | category | flops | bytes accessed | tf_op | source)
XLA Modules:
  0.0 593.0 jit_solution(16369943714473185920)
XLA Ops:
  10.1 3.1 shard_map.364
  15.1 1.3 pad_maximum_fusion
  16.4 171.3 %all-gather.2.cloned.1.call-done = bf16[1536,9344]{1,0:T(8,128)(2,1)} async-done(((bf16[48,9344]{1,0:T(8,128)(2,1)}), bf16[1536,9344]{1,0:T(8,128)(2,1)}) %all-gather.2.cloned.1.call-update) | async-done | bytes 28704784 | tf_op jit(solution)/shard_map/all_gather | solution.py:967
  189.4 1.6 fusion.3.refs_0_.refs_10_
  190.9 14.0 %shard_map.365 = (f32[512,768]{1,0:T(8,128)}, bf16[512,768]{1,0:T(8,128)(2,1)}, bf16[512,768]{1,0:T(8,128)(2,1)}, bf16[512,768]{1,0:T(8,128)(2,1)}, f32[512,128]{1,0:T(8,128)}, /*index=5*/bf16[2,512,768]{2,1,0:T(8,128)(2,1)}) custom-call(s32[4]{0:T(128)} %pad_add_fusion.scalars.place_of, f32[512,768]{1,0:T(8,128)} %fusion.3.refs_0_.refs_10_, ...), custom_call_target="tpu_custom_call" | custom-call | flops 3221225472 | bytes 30812160 | tf_op jit(solution)/shard_map/pallas_call | solution.py:110
  205.0 12.8 %shard_map.366 = (f32[512,768]{1,0:T(8,128)}, bf16[5,512,768]{2,1,0:T(8,128)(2,1)}, f32[4,512,768]{2,1,0:T(8,128)}) custom-call(s32[4]{0:T(128)} %pad_add_fusion.scalars.place_of, f32[512,768]{1,0:T(8,128)} %get-tuple-element.238.refs_0_.refs_2_, f32[2,768]{1,0:T(2,128)} %get-tuple-element.474.refs_1_.refs_3_, bf16[16,2,48,9344]{3,2,1,0:T(8,128)(2,1)} %bitcast.28), custom_call_target="tpu_custom_call" | custom-call | flops 4831838208 | bytes 30283776 | tf_op jit(solution)/shard_map/pallas_call | solution.py:110
  218.3 7.8 %collective-permute-done.refs_2_ = bf16[2,512,768]{2,1,0:T(8,128)(2,1)S(1)} collective-permute-done((bf16[2,512,768]{2,1,0:T(8,128)(2,1)S(1)}, bf16[2,512,768]{2,1,0:T(8,128)(2,1)S(1)}, u32[]{:S(2)}, u32[]{:S(2)}) %collective-permute-start) | collective-permute-done | bytes 1572896 | tf_op jit(solution)/shard_map/ppermute | solution.py:569
  227.2 14.1 %shard_map.367 = (f32[512,768]{1,0:T(8,128)}, bf16[512,768]{1,0:T(8,128)(2,1)}, bf16[512,768]{1,0:T(8,128)(2,1)}, bf16[512,768]{1,0:T(8,128)(2,1)}, f32[512,128]{1,0:T(8,128)}, /*index=5*/bf16[2,512,768]{2,1,0:T(8,128)(2,1)}) custom-call(s32[4]{0:T(128)} %pad_add_fusion.scalars.place_of, f32[512,768]{1,0:T(8,128)} %get-tuple-element.241.refs_0_.refs_10_, ...), custom_call_target="tpu_custom_call" | custom-call | flops 3221225472 | bytes 30812160 | tf_op jit(solution)/shard_map/pallas_call | solution.py:110
  241.6 13.8 %shard_map.368 = (f32[512,768]{1,0:T(8,128)}, bf16[5,512,768]{2,1,0:T(8,128)(2,1)}, f32[4,512,768]{2,1,0:T(8,128)}) custom-call(s32[4]{0:T(128)} %pad_add_fusion.scalars.place_of, f32[512,768]{1,0:T(8,128)} %get-tuple-element.244.refs_0_.refs_2_, f32[2,768]{1,0:T(2,128)} %get-tuple-element.472.refs_1_.refs_3_, bf16[16,2,48,9344]{3,2,1,0:T(8,128)(2,1)} %bitcast.30), custom_call_target="tpu_custom_call" | custom-call | flops 4831838208 | bytes 30283776 | tf_op jit(solution)/shard_map/pallas_call | solution.py:110
  255.9 1.6 reduce_sum.90
  260.3 1.3 multiply_reduce_fusion
  261.6 1.7 fusion.21
  264.8 1.2 collective-permute-done.4.refs_3_
  266.8 8.8 %shard_map.369 = (bf16[384,768]{1,0:T(8,128)(2,1)}, bf16[384,768]{1,0:T(8,128)(2,1)}, f32[1,2,384,768]{3,2,1,0:T(8,128)}) custom-call(s32[4]{0:T(128)} %pad_add_fusion.scalars.place_of, bf16[5,512,768]{2,1,0:T(8,128)(2,1)} %get-tuple-element.245.refs_0_, bf16[512,384]{1,0:T(8,128)(2,1)} %get-tuple-element.471.refs_1_, ...), custom_call_target="tpu_custom_call" | custom-call | flops 2415919104 | bytes 8650752 | tf_op jit(solution)/shard_map/pallas_call | solution.py:110
  275.6 1.4 collective-permute-start.5
  278.4 22.6 %shard_map.370 = (f32[512,768]{1,0:T(8,128)}, f32[2,768]{1,0:T(2,128)}, bf16[2,512,768]{2,1,0:T(8,128)(2,1)}, bf16[2,512,768]{2,1,0:T(8,128)(2,1)}) custom-call(s32[4]{0:T(128)} %pad_add_fusion.scalars.place_of, bf16[512,768]{1,0:T(8,128)(2,1)} %copy-done.3, f32[512,768]{1,0:T(8,128)} %get-tuple-element.257.refs_1_, ...), custom_call_target="tpu_custom_call" | custom-call | flops 4831838208 | bytes 38934528 | tf_op jit(solution)/shard_map/pallas_call | solution.py:110
  301.7 3.6 collective-permute-done.10.refs_3_
  306.5 10.3 %shard_map.371 = (bf16[576,768]{1,0:T(8,128)(2,1)}, bf16[576,768]{1,0:T(8,128)(2,1)}, f32[1,2,384,768]{3,2,1,0:T(8,128)}, f32[1,2,192,768]{3,2,1,0:T(8,128)}) custom-call(s32[4]{0:T(128)} %pad_add_fusion.scalars.place_of, bf16[5,512,768]{2,1,0:T(8,128)(2,1)} %get-tuple-element.245.refs_0_, bf16[2,512,768]{2,1,0:T(8,128)(2,1)} %get-tuple-element.262.refs_1_, ...), custom_call_target="tpu_custom_call" | custom-call | flops 2415919104 | bytes 14548992 | tf_op jit(solution)/shard_map/pallas_call | solution.py:110
  316.8 1.5 collective-permute-start.11
  319.6 22.9 %shard_map.372 = (f32[512,768]{1,0:T(8,128)}, bf16[512,768]{1,0:T(8,128)(2,1)}, bf16[512,384]{1,0:T(8,128)(2,1)}, bf16[512,384]{1,0:T(8,128)(2,1)}, f32[2,768]{1...) custom-call(s32[4]{0:T(128)} %pad_add_fusion.scalars.place_of, ...), custom_call_target="tpu_custom_call" | custom-call | flops 4429185024 | bytes 34768896 | tf_op jit(solution)/shard_map/pallas_call | solution.py:110
  343.2 3.7 collective-permute-done.14.refs_7_
  348.7 17.1 %shard_map.373 = (bf16[960,768]{1,0:T(8,128)(2,1)}, bf16[960,768]{1,0:T(8,128)(2,1)}, f32[2,2,384,768]{3,2,1,0:T(8,128)}, f32[1,2,192,768]{3,2,1,0:T(8,128)}, f3...) custom-call(s32[4]{0:T(128)} %pad_add_fusion.scalars.place_of, ...), custom_call_target="tpu_custom_call" | custom-call | flops 4831838208 | bytes 20250624 | tf_op jit(solution)/shard_map/pallas_call | solution.py:110
  365.9 1.5 collective-permute-start.15
  368.0 1.9 collective-permute-start.18
  369.9 2.4 collective-permute-start.19
  372.3 22.8 %shard_map.374 = (f32[512,768]{1,0:T(8,128)}, f32[2,768]{1,0:T(2,128)}, bf16[2,512,768]{2,1,0:T(8,128)(2,1)}, bf16[2,512,768]{2,1,0:T(8,128)(2,1)}) custom-call(s32[4]{0:T(128)} %pad_add_fusion.scalars.place_of, bf16[512,768]{1,0:T(8,128)(2,1)} %get-tuple-element.310.refs_0_, f32[512,768]{1,0:T(8,128)} %get-tuple-element.311.refs_1_, ...), custom_call_target="tpu_custom_call" | custom-call | flops 4831838208 | bytes 38934528 | tf_op jit(solution)/shard_map/pallas_call | solution.py:110
  395.2 5.2 collective-permute-done.15.refs_6_
  401.6 3.6 collective-permute-done.20.refs_3_
  406.3 13.0 %shard_map.375 = (bf16[768,768]{1,0:T(8,128)(2,1)}, bf16[768,768]{1,0:T(8,128)(2,1)}, f32[1,2,384,768]{3,2,1,0:T(8,128)}, f32[2,2,192,768]{3,2,1,0:T(8,128)}, f3...) custom-call(s32[4]{0:T(128)} %pad_add_fusion.scalars.place_of, ...), custom_call_target="tpu_custom_call" | custom-call | flops 2415919104 | bytes 20597760 | tf_op jit(solution)/shard_map/pallas_call | solution.py:110
  420.0 1.5 collective-permute-start.22
  422.2 1.9 collective-permute-start.24
  424.2 2.5 collective-permute-start.25
  426.6 22.6 %shard_map.376 = (f32[512,768]{1,0:T(8,128)}, bf16[512,768]{1,0:T(8,128)(2,1)}, bf16[512,384]{1,0:T(8,128)(2,1)}, bf16[512,384]{1,0:T(8,128)(2,1)}, f32[2,768]{1...) custom-call(s32[4]{0:T(128)} %pad_add_fusion.scalars.place_of, ...), custom_call_target="tpu_custom_call" | custom-call | flops 4429185024 | bytes 34768896 | tf_op jit(solution)/shard_map/pallas_call | solution.py:110
  451.0 1.3 concatenate.15.refs_14_
  452.9 2.4 collective-permute-done.29.refs_15_
  456.7 13.1 %shard_map.377 = (bf16[640,768]{1,0:T(8,128)(2,1)}, bf16[576,768]{1,0:T(8,128)(2,1)}, f32[1,2,384,768]{3,2,1,0:T(8,128)}, f32[384,128]{1,0:T(8,128)}, f32[1,2,19...) custom-call(s32[4]{0:T(128)} %pad_add_fusion.scalars.place_of, ...), custom_call_target="tpu_custom_call" | custom-call | flops 2415919104 | bytes 17841152 | tf_op jit(solution)/shard_map/pallas_call | solution.py:110
  470.4 1.4 collective-permute-start.31
  471.8 2.0 collective-permute-start.33
  473.7 2.4 collective-permute-start.34
  476.2 9.7 %collective-permute-done.32.refs_6_ = bf16[192,768]{1,0:T(8,128)(2,1)S(1)} collective-permute-done((bf16[192,768]{1,0:T(8,128)(2,1)}, bf16[192,768]{1,0:T(8,128)(2,1)S(1)}, u32[]{:S(2)}, u32[]{:S(2)}) %collective-permute-start.32) | collective-permute-done | bytes 294944 | tf_op jit(solution)/shard_map/ppermute | solution.py:573
  485.9 9.6 %collective-permute-done.33.refs_7_ = bf16[192,768]{1,0:T(8,128)(2,1)S(1)} collective-permute-done((bf16[192,768]{1,0:T(8,128)(2,1)}, bf16[192,768]{1,0:T(8,128)(2,1)S(1)}, u32[]{:S(2)}, u32[]{:S(2)}) %collective-permute-start.33) | collective-permute-done | bytes 294944 | tf_op jit(solution)/shard_map/ppermute | solution.py:573
  496.9 4.9 shard_map.378
  501.8 5.4 collective-permute-start.37
  507.8 1.5 collective-permute-start.35
  510.5 1.8 collective-permute-start.39
  512.3 10.2 %collective-permute-done.38.refs_6_ = bf16[96,768]{1,0:T(8,128)(2,1)S(1)} collective-permute-done((bf16[96,768]{1,0:T(8,128)(2,1)}, bf16[96,768]{1,0:T(8,128)(2,1)S(1)}, u32[]{:S(2)}, u32[]{:S(2)}) %collective-permute-start.38) | collective-permute-done | bytes 147488 | tf_op jit(solution)/shard_map/ppermute | solution.py:573
  523.9 2.8 shard_map.379
  526.8 3.2 collective-permute-start.40
  530.4 2.1 collective-permute-start.42
  532.4 1.9 fusion.13.refs_6_
  534.3 3.7 collective-permute-done.40.refs_2_
  538.1 7.7 %collective-permute-done.41.refs_3_ = bf16[112,768]{1,0:T(8,128)(2,1)S(1)} collective-permute-done((bf16[112,768]{1,0:T(8,128)(2,1)}, bf16[112,768]{1,0:T(8,128)(2,1)S(1)}, u32[]{:S(2)}, u32[]{:S(2)}) %collective-permute-start.41) | collective-permute-done | bytes 172064 | tf_op jit(solution)/shard_map/ppermute | solution.py:573
  546.5 2.0 shard_map.380
  549.0 1.3 collective-permute-done.48
  552.9 1.4 collective-permute-start.51
  554.3 1.5 collective-permute-start.52
  556.5 2.3 collective-permute-done.52
  558.8 3.4 collective-permute-start.53
  562.6 2.0 collective-permute-start.55
  565.4 1.3 collective-permute-done.54
  566.6 1.3 collective-permute-done.55
  570.8 1.3 multiply_subtract_fusion
  572.1 1.3 pad_maximum_fusion.2.scale
  574.0 10.8 %shard_map.381 = (f32[2,48,2304]{2,1,0:T(8,128)}, f32[2,48,2304]{2,1,0:T(8,128)}, f32[2,48,2304]{2,1,0:T(8,128)}, f32[2,48,768]{2,1,0:T(8,128)}, f32[2,48,768]{2...) custom-call(s32[4]{0:T(128)} %pad_add_fusion.scalars.place_of, ...), custom_call_target="tpu_custom_call" | custom-call | flops 53084160 | bytes 21233664 | tf_op jit(solution)/shard_map/pallas_call | solution.py:534
  (260 shorter events, 41.9 us)
Async XLA Ops:
  7.2 180.4 %all-gather.2.cloned.1.call-start = ((), (), s32[]{:S(2)}) async-start(), calls=%async_computation | async-start | bytes 29601792 | tf_op jit(solution)/shard_map/all_gather | solution.py:967
  217.7 23.9 %collective-permute-start.1 = (bf16[5,512,768]{2,1,0:T(8,128)(2,1)}, bf16[5,512,768]{2,1,0:T(8,128)(2,1)S(1)}, u32[]{:S(2)}, u32[]{:S(2)}) collective-permute-start(bf16[5,512,768]{2,1,0:T(8,128)(2,1)} %get-tuple-element.239.refs_4_.refs_0_), channel_id=1, source_target_pairs={{0,1},{1,0},{2,3},{3,2},{4,5},{5,4},{6,7},{7,6},{8,9},{9,8},{10,11... | collective-permute-start | bytes 11796488 | tf_op jit(solution)/shard_map/ppermute | solution.py:569
  218.1 8.0 %collective-permute-start = (bf16[2,512,768]{2,1,0:T(8,128)(2,1)S(1)}, bf16[2,512,768]{2,1,0:T(8,128)(2,1)S(1)}, u32[]{:S(2)}, u32[]{:S(2)}) collective-permute-start(bf16[2,512,768]{2,1,0:T(8,128)(2,1)S(1)} %copy-done.4), channel_id=1, source_target_pairs={{0,1},{1,0},{2,3},{3,2},{4,5},{5,4},{6,7},{7,6},{8,9},{9,8},{10,11... | collective-permute-start | bytes 4718600 | tf_op jit(solution)/shard_map/ppermute | solution.py:569
  241.4 14.5 %collective-permute-start.2 = (bf16[2,512,768]{2,1,0:T(8,128)(2,1)}, bf16[2,512,768]{2,1,0:T(8,128)(2,1)}, u32[]{:S(2)}, u32[]{:S(2)}) collective-permute-start(bf16[2,512,768]{2,1,0:T(8,128)(2,1)} %get-tuple-element.242.refs_0_), channel_id=1, source_target_pairs={{0,1},{1,0},{2,3},{3,2},{4,5},{5,4},{6,7},{7,6},{8,9},{9,8},{10,11... | collective-permute-start | bytes 4718600 | tf_op jit(solution)/shard_map/ppermute | solution.py:569
  255.5 9.3 %collective-permute-start.3 = (bf16[5,512,768]{2,1,0:T(8,128)(2,1)}, bf16[5,512,768]{2,1,0:T(8,128)(2,1)}, u32[]{:S(2)}, u32[]{:S(2)}) collective-permute-start(bf16[5,512,768]{2,1,0:T(8,128)(2,1)} %get-tuple-element.245.refs_0_), channel_id=1, source_target_pairs={{0,1},{1,0},{2,3},{3,2},{4,5},{5,4},{6,7},{7,6},{8,9},{9,8},{10,11... | collective-permute-start | bytes 11796488 | tf_op jit(solution)/shard_map/ppermute | solution.py:569
  264.3 1.7 collective-permute-start.4
  264.6 36.5 %collective-permute-start.7 = (bf16[512,768]{1,0:T(8,128)(2,1)S(1)}, bf16[512,768]{1,0:T(8,128)(2,1)S(1)}, u32[]{:S(2)}, u32[]{:S(2)}) collective-permute-start(bf16[512,768]{1,0:T(8,128)(2,1)S(1)} %add_convert_fusion.refs_4_), channel_id=1, source_target_pairs={{0,1},{1,0},{2,3},{3,2},{4,5},{5,4},{6,7},{7,6},{8,9},{9,8},{10,11... | collective-permute-start | bytes 2359304 | tf_op jit(solution)/shard_map/ppermute | solution.py:569
  275.6 25.5 %collective-permute-start.5 = (bf16[384,768]{1,0:T(8,128)(2,1)}, bf16[384,768]{1,0:T(8,128)(2,1)S(1)}, u32[]{:S(2)}, u32[]{:S(2)}) collective-permute-start(bf16[384,768]{1,0:T(8,128)(2,1)} %get-tuple-element.254), channel_id=1, source_target_pairs={{0,2},{2,0},{4,6},{6,4},{8,10},{10,8},{12,14},{14,12},{16,18},{18,... | collective-permute-start | bytes 1769480 | tf_op jit(solution)/shard_map/ppermute | solution.py:573
  277.0 24.1 %collective-permute-start.6 = (bf16[384,768]{1,0:T(8,128)(2,1)}, bf16[384,768]{1,0:T(8,128)(2,1)S(1)}, u32[]{:S(2)}, u32[]{:S(2)}) collective-permute-start(bf16[384,768]{1,0:T(8,128)(2,1)} %get-tuple-element.255), channel_id=1, source_target_pairs={{0,4},{2,6},{4,0},{6,2},{8,12},{10,14},{12,8},{14,10},{16,20},{18,... | collective-permute-start | bytes 1769480 | tf_op jit(solution)/shard_map/ppermute | solution.py:573
  277.8 23.3 %collective-permute-start.9 = (bf16[512,128]{1,0:T(8,128)(2,1)S(1)}, bf16[512,128]{1,0:T(8,128)(2,1)S(1)}, u32[]{:S(2)}, u32[]{:S(2)}) collective-permute-start(bf16[512,128]{1,0:T(8,128)(2,1)S(1)} %fusion.2.refs_9_), channel_id=1, source_target_pairs={{0,1},{1,0},{2,3},{3,2},{4,5},{5,4},{6,7},{7,6},{8,9},{9,8},{10,11... | collective-permute-start | bytes 393224 | tf_op jit(solution)/shard_map/ppermute | solution.py:569
  277.9 23.2 %collective-permute-start.8 = (bf16[512,128]{1,0:T(8,128)(2,1)S(1)}, bf16[512,128]{1,0:T(8,128)(2,1)S(1)}, u32[]{:S(2)}, u32[]{:S(2)}) collective-permute-start(bf16[512,128]{1,0:T(8,128)(2,1)S(1)} %pad.18.refs_5_), channel_id=1, source_target_pairs={{0,1},{1,0},{2,3},{3,2},{4,5},{5,4},{6,7},{7,6},{8,9},{9,8},{10,11... | collective-permute-start | bytes 393224 | tf_op jit(solution)/shard_map/ppermute | solution.py:569
  301.7 3.6 collective-permute-start.10
  316.8 25.7 %collective-permute-start.11 = (bf16[576,768]{1,0:T(8,128)(2,1)}, bf16[576,768]{1,0:T(8,128)(2,1)S(1)}, u32[]{:S(2)}, u32[]{:S(2)}) collective-permute-start(bf16[576,768]{1,0:T(8,128)(2,1)} %get-tuple-element.272), channel_id=1, source_target_pairs={{0,2},{2,0},{4,6},{6,4},{8,10},{10,8},{12,14},{14,12},{16,18},{18,... | collective-permute-start | bytes 2654216 | tf_op jit(solution)/shard_map/ppermute | solution.py:573
  318.3 24.2 %collective-permute-start.12 = (bf16[576,768]{1,0:T(8,128)(2,1)}, bf16[576,768]{1,0:T(8,128)(2,1)S(1)}, u32[]{:S(2)}, u32[]{:S(2)}) collective-permute-start(bf16[576,768]{1,0:T(8,128)(2,1)} %get-tuple-element.273), channel_id=1, source_target_pairs={{0,4},{2,6},{4,0},{6,2},{8,12},{10,14},{12,8},{14,10},{16,20},{18,... | collective-permute-start | bytes 2654216 | tf_op jit(solution)/shard_map/ppermute | solution.py:573
  342.6 4.3 collective-permute-start.13
  342.7 4.2 collective-permute-start.14
  365.9 34.6 %collective-permute-start.15 = (bf16[960,768]{1,0:T(8,128)(2,1)}, bf16[960,768]{1,0:T(8,128)(2,1)S(1)}, u32[]{:S(2)}, u32[]{:S(2)}) collective-permute-start(bf16[960,768]{1,0:T(8,128)(2,1)} %get-tuple-element.305), channel_id=1, source_target_pairs={{0,2},{2,0},{4,6},{6,4},{8,10},{10,8},{12,14},{14,12},{16,18},{18,... | collective-permute-start | bytes 4423688 | tf_op jit(solution)/shard_map/ppermute | solution.py:573
  367.3 34.3 %collective-permute-start.16 = (bf16[960,768]{1,0:T(8,128)(2,1)}, bf16[960,768]{1,0:T(8,128)(2,1)S(1)}, u32[]{:S(2)}, u32[]{:S(2)}) collective-permute-start(bf16[960,768]{1,0:T(8,128)(2,1)} %get-tuple-element.306), channel_id=1, source_target_pairs={{0,4},{2,6},{4,0},{6,2},{8,12},{10,14},{12,8},{14,10},{16,20},{18,... | collective-permute-start | bytes 4423688 | tf_op jit(solution)/shard_map/ppermute | solution.py:573
  368.0 27.2 %collective-permute-start.17 = (bf16[96,768]{1,0:T(8,128)(2,1)}, bf16[96,768]{1,0:T(8,128)(2,1)S(1)}, u32[]{:S(2)}, u32[]{:S(2)}) collective-permute-start(bf16[96,768]{1,0:T(8,128)(2,1)} %get-tuple-element.307), channel_id=1, source_target_pairs={{0,8},{2,10},{4,12},{6,14},{8,0},{10,2},{12,4},{14,6},{16,24},{18,... | collective-permute-start | bytes 442376 | tf_op jit(solution)/shard_map/ppermute | solution.py:573
  368.0 27.2 %collective-permute-start.18 = (bf16[96,768]{1,0:T(8,128)(2,1)}, bf16[96,768]{1,0:T(8,128)(2,1)S(1)}, u32[]{:S(2)}, u32[]{:S(2)}) collective-permute-start(bf16[96,768]{1,0:T(8,128)(2,1)} %get-tuple-element.308), channel_id=1, source_target_pairs={{0,16},{2,18},{4,20},{6,22},{8,24},{10,26},{12,28},{14,30},{16,0},... | collective-permute-start | bytes 442376 | tf_op jit(solution)/shard_map/ppermute | solution.py:573
  369.9 25.3 %collective-permute-start.19 = (bf16[96,768]{1,0:T(8,128)(2,1)}, bf16[96,768]{1,0:T(8,128)(2,1)S(1)}, u32[]{:S(2)}, u32[]{:S(2)}) collective-permute-start(bf16[96,768]{1,0:T(8,128)(2,1)} %get-tuple-element.309), channel_id=1, source_target_pairs={{0,24},{2,26},{4,28},{6,30},{8,16},{10,18},{12,20},{14,22},{16,8},... | collective-permute-start | bytes 442376 | tf_op jit(solution)/shard_map/ppermute | solution.py:573
  401.6 3.6 collective-permute-start.20
  419.3 30.0 %collective-permute-start.21 = (bf16[768,768]{1,0:T(8,128)(2,1)}, bf16[768,768]{1,0:T(8,128)(2,1)S(1)}, u32[]{:S(2)}, u32[]{:S(2)}) collective-permute-start(bf16[768,768]{1,0:T(8,128)(2,1)} %get-tuple-element.338), channel_id=1, source_target_pairs={{0,2},{2,0},{4,6},{6,4},{8,10},{10,8},{12,14},{14,12},{16,18},{18,... | collective-permute-start | bytes 3538952 | tf_op jit(solution)/shard_map/ppermute | solution.py:573
  420.0 29.3 %collective-permute-start.22 = (bf16[768,768]{1,0:T(8,128)(2,1)}, bf16[768,768]{1,0:T(8,128)(2,1)S(1)}, u32[]{:S(2)}, u32[]{:S(2)}) collective-permute-start(bf16[768,768]{1,0:T(8,128)(2,1)} %get-tuple-element.339), channel_id=1, source_target_pairs={{0,4},{2,6},{4,0},{6,2},{8,12},{10,14},{12,8},{14,10},{16,20},{18,... | collective-permute-start | bytes 3538952 | tf_op jit(solution)/shard_map/ppermute | solution.py:573
  422.2 27.0 %collective-permute-start.23 = (bf16[96,768]{1,0:T(8,128)(2,1)}, bf16[96,768]{1,0:T(8,128)(2,1)S(1)}, u32[]{:S(2)}, u32[]{:S(2)}) collective-permute-start(bf16[96,768]{1,0:T(8,128)(2,1)} %get-tuple-element.340), channel_id=1, source_target_pairs={{0,8},{2,10},{4,12},{6,14},{8,0},{10,2},{12,4},{14,6},{16,24},{18,... | collective-permute-start | bytes 442376 | tf_op jit(solution)/shard_map/ppermute | solution.py:573
  422.2 27.0 %collective-permute-start.24 = (bf16[96,768]{1,0:T(8,128)(2,1)}, bf16[96,768]{1,0:T(8,128)(2,1)S(1)}, u32[]{:S(2)}, u32[]{:S(2)}) collective-permute-start(bf16[96,768]{1,0:T(8,128)(2,1)} %get-tuple-element.341), channel_id=1, source_target_pairs={{0,16},{2,18},{4,20},{6,22},{8,24},{10,26},{12,28},{14,30},{16,0},... | collective-permute-start | bytes 442376 | tf_op jit(solution)/shard_map/ppermute | solution.py:573
  424.2 25.1 %collective-permute-start.25 = (bf16[96,768]{1,0:T(8,128)(2,1)}, bf16[96,768]{1,0:T(8,128)(2,1)S(1)}, u32[]{:S(2)}, u32[]{:S(2)}) collective-permute-start(bf16[96,768]{1,0:T(8,128)(2,1)} %get-tuple-element.342), channel_id=1, source_target_pairs={{0,24},{2,26},{4,28},{6,30},{8,16},{10,18},{12,20},{14,22},{16,8},... | collective-permute-start | bytes 442376 | tf_op jit(solution)/shard_map/ppermute | solution.py:573
  450.5 4.8 collective-permute-start.26
  450.5 4.8 collective-permute-start.27
  452.3 2.9 collective-permute-start.29
  452.4 2.9 collective-permute-start.28
  469.8 25.7 %collective-permute-start.30 = (bf16[640,768]{1,0:T(8,128)(2,1)}, bf16[640,768]{1,0:T(8,128)(2,1)S(1)}, u32[]{:S(2)}, u32[]{:S(2)}) collective-permute-start(bf16[640,768]{1,0:T(8,128)(2,1)} %get-tuple-element.383), channel_id=1, source_target_pairs={{0,2},{2,0},{4,6},{6,4},{8,10},{10,8},{12,14},{14,12},{16,18},{18,... | collective-permute-start | bytes 2949128 | tf_op jit(solution)/shard_map/ppermute | solution.py:573
  470.4 25.1 %collective-permute-start.31 = (bf16[576,768]{1,0:T(8,128)(2,1)}, bf16[576,768]{1,0:T(8,128)(2,1)S(1)}, u32[]{:S(2)}, u32[]{:S(2)}) collective-permute-start(bf16[576,768]{1,0:T(8,128)(2,1)} %get-tuple-element.384), channel_id=1, source_target_pairs={{0,4},{2,6},{4,0},{6,2},{8,12},{10,14},{12,8},{14,10},{16,20},{18,... | collective-permute-start | bytes 2654216 | tf_op jit(solution)/shard_map/ppermute | solution.py:573
  471.8 14.1 %collective-permute-start.32 = (bf16[192,768]{1,0:T(8,128)(2,1)}, bf16[192,768]{1,0:T(8,128)(2,1)S(1)}, u32[]{:S(2)}, u32[]{:S(2)}) collective-permute-start(bf16[192,768]{1,0:T(8,128)(2,1)} %get-tuple-element.385), channel_id=1, source_target_pairs={{0,8},{2,10},{4,12},{6,14},{8,0},{10,2},{12,4},{14,6},{16,24},{18,... | collective-permute-start | bytes 884744 | tf_op jit(solution)/shard_map/ppermute | solution.py:573
  471.8 23.7 %collective-permute-start.33 = (bf16[192,768]{1,0:T(8,128)(2,1)}, bf16[192,768]{1,0:T(8,128)(2,1)S(1)}, u32[]{:S(2)}, u32[]{:S(2)}) collective-permute-start(bf16[192,768]{1,0:T(8,128)(2,1)} %get-tuple-element.386), channel_id=1, source_target_pairs={{0,16},{2,18},{4,20},{6,22},{8,24},{10,26},{12,28},{14,30},{16,0},... | collective-permute-start | bytes 884744 | tf_op jit(solution)/shard_map/ppermute | solution.py:573
  473.7 21.7 %collective-permute-start.34 = (bf16[192,768]{1,0:T(8,128)(2,1)}, bf16[192,768]{1,0:T(8,128)(2,1)S(1)}, u32[]{:S(2)}, u32[]{:S(2)}) collective-permute-start(bf16[192,768]{1,0:T(8,128)(2,1)} %get-tuple-element.387), channel_id=1, source_target_pairs={{0,24},{2,26},{4,28},{6,30},{8,16},{10,18},{12,20},{14,22},{16,8},... | collective-permute-start | bytes 884744 | tf_op jit(solution)/shard_map/ppermute | solution.py:573
  501.8 8.7 %collective-permute-start.37 = (bf16[96,768]{1,0:T(8,128)(2,1)}, bf16[96,768]{1,0:T(8,128)(2,1)S(1)}, u32[]{:S(2)}, u32[]{:S(2)}) collective-permute-start(bf16[96,768]{1,0:T(8,128)(2,1)} %get-tuple-element.407), channel_id=1, source_target_pairs={{0,8},{2,10},{4,12},{6,14},{8,0},{10,2},{12,4},{14,6},{16,24},{18,... | collective-permute-start | bytes 442376 | tf_op jit(solution)/shard_map/ppermute | solution.py:573
  507.2 15.9 %collective-permute-start.36 = (bf16[256,768]{1,0:T(8,128)(2,1)}, bf16[256,768]{1,0:T(8,128)(2,1)S(1)}, u32[]{:S(2)}, u32[]{:S(2)}) collective-permute-start(bf16[256,768]{1,0:T(8,128)(2,1)} %get-tuple-element.406), channel_id=1, source_target_pairs={{0,4},{2,6},{4,0},{6,2},{8,12},{10,14},{12,8},{14,10},{16,20},{18,... | collective-permute-start | bytes 1179656 | tf_op jit(solution)/shard_map/ppermute | solution.py:573
  507.8 15.3 %collective-permute-start.35 = (bf16[192,768]{1,0:T(8,128)(2,1)}, bf16[192,768]{1,0:T(8,128)(2,1)S(1)}, u32[]{:S(2)}, u32[]{:S(2)}) collective-permute-start(bf16[192,768]{1,0:T(8,128)(2,1)} %get-tuple-element.405), channel_id=1, source_target_pairs={{0,2},{2,0},{4,6},{6,4},{8,10},{10,8},{12,14},{14,12},{16,18},{18,... | collective-permute-start | bytes 884744 | tf_op jit(solution)/shard_map/ppermute | solution.py:573
  509.3 21.1 %collective-permute-start.43 = (f32[1,2,48,768]{3,2,1,0:T(8,128)S(1)}, f32[1,2,48,768]{3,2,1,0:T(8,128)S(1)}, u32[]{:S(2)}, u32[]{:S(2)}) collective-permute-start(f32[1,2,48,768]{3,2,1,0:T(8,128)S(1)} %copy-done.27), channel_id=1, source_target_pairs={{0,1},{1,0},{2,3},{3,2},{4,5},{5,4},{6,7},{7,6},{8,9},{9,8},{10,11... | collective-permute-start | bytes 884744 | tf_op jit(solution)/shard_map/ppermute | solution.py:569
  509.3 13.2 %collective-permute-start.38 = (bf16[96,768]{1,0:T(8,128)(2,1)}, bf16[96,768]{1,0:T(8,128)(2,1)S(1)}, u32[]{:S(2)}, u32[]{:S(2)}) collective-permute-start(bf16[96,768]{1,0:T(8,128)(2,1)} %get-tuple-element.408), channel_id=1, source_target_pairs={{0,16},{2,18},{4,20},{6,22},{8,24},{10,26},{12,28},{14,30},{16,0},... | collective-permute-start | bytes 442376 | tf_op jit(solution)/shard_map/ppermute | solution.py:573
  510.5 12.0 %collective-permute-start.39 = (bf16[96,768]{1,0:T(8,128)(2,1)}, bf16[96,768]{1,0:T(8,128)(2,1)S(1)}, u32[]{:S(2)}, u32[]{:S(2)}) collective-permute-start(bf16[96,768]{1,0:T(8,128)(2,1)} %get-tuple-element.409), channel_id=1, source_target_pairs={{0,24},{2,26},{4,28},{6,30},{8,16},{10,18},{12,20},{14,22},{16,8},... | collective-permute-start | bytes 442376 | tf_op jit(solution)/shard_map/ppermute | solution.py:573
  522.5 11.8 %collective-permute-start.44 = (f32[1,2,48,768]{3,2,1,0:T(8,128)S(1)}, f32[1,2,48,768]{3,2,1,0:T(8,128)S(1)}, u32[]{:S(2)}, u32[]{:S(2)}) collective-permute-start(f32[1,2,48,768]{3,2,1,0:T(8,128)S(1)} %copy-done.28), channel_id=1, source_target_pairs={{0,1},{1,0},{2,3},{3,2},{4,5},{5,4},{6,7},{7,6},{8,9},{9,8},{10,11... | collective-permute-start | bytes 884744 | tf_op jit(solution)/shard_map/ppermute | solution.py:569
  522.6 27.8 %collective-permute-start.45 = (f32[2,2,48,768]{3,2,1,0:T(8,128)}, f32[2,2,48,768]{3,2,1,0:T(8,128)S(1)}, u32[]{:S(2)}, u32[]{:S(2)}) collective-permute-start(f32[2,2,48,768]{3,2,1,0:T(8,128)} %get-tuple-element.436.refs_2_), channel_id=1, source_target_pairs={{0,1},{1,0},{2,3},{3,2},{4,5},{5,4},{6,7},{7,6},{8,9},{9,8},{10,11... | collective-permute-start | bytes 1769480 | tf_op jit(solution)/shard_map/ppermute | solution.py:569
  523.9 46.9 %copy-start.53 = (f32[70,48]{0,1:T(8,128)S(1)}, f32[70,48]{0,1:T(8,128)}, u32[]{:S(2)}) copy-start(f32[70,48]{0,1:T(8,128)} %param.28) | copy-start | bytes 40324
  523.9 46.9 %copy-start.56 = (f32[70,48]{0,1:T(8,128)S(1)}, f32[70,48]{0,1:T(8,128)}, u32[]{:S(2)}) copy-start(f32[70,48]{0,1:T(8,128)} %param.38) | copy-start | bytes 40324
  523.9 46.9 %copy-start.57 = (f32[70,48]{0,1:T(8,128)S(1)}, f32[70,48]{0,1:T(8,128)}, u32[]{:S(2)}) copy-start(f32[70,48]{0,1:T(8,128)} %param.39) | copy-start | bytes 40324
  523.9 49.5 %copy-start.58 = (f32[5,2,48]{2,1,0:T(2,128)S(1)}, f32[5,2,48]{2,1,0:T(2,128)}, u32[]{:S(2)}) copy-start(f32[5,2,48]{2,1,0:T(2,128)} %param.29) | copy-start | bytes 5764
  523.9 49.5 %copy-start.63 = (f32[5,2,48]{2,1,0:T(2,128)S(1)}, f32[5,2,48]{2,1,0:T(2,128)}, u32[]{:S(2)}) copy-start(f32[5,2,48]{2,1,0:T(2,128)} %param.40) | copy-start | bytes 5764
  523.9 49.5 %copy-start.64 = (f32[5,2,48]{2,1,0:T(2,128)S(1)}, f32[5,2,48]{2,1,0:T(2,128)}, u32[]{:S(2)}) copy-start(f32[5,2,48]{2,1,0:T(2,128)} %param.41) | copy-start | bytes 5764
  526.8 11.3 %collective-permute-start.40 = (bf16[112,768]{1,0:T(8,128)(2,1)}, bf16[112,768]{1,0:T(8,128)(2,1)S(1)}, u32[]{:S(2)}, u32[]{:S(2)}) collective-permute-start(bf16[112,768]{1,0:T(8,128)(2,1)} %get-tuple-element.424), channel_id=1, source_target_pairs={{0,8},{2,10},{4,12},{6,14},{8,0},{10,2},{12,4},{14,6},{16,24},{18,... | collective-permute-start | bytes 516104 | tf_op jit(solution)/shard_map/ppermute | solution.py:573
  530.0 15.7 %collective-permute-start.41 = (bf16[112,768]{1,0:T(8,128)(2,1)}, bf16[112,768]{1,0:T(8,128)(2,1)S(1)}, u32[]{:S(2)}, u32[]{:S(2)}) collective-permute-start(bf16[112,768]{1,0:T(8,128)(2,1)} %get-tuple-element.425), channel_id=1, source_target_pairs={{0,16},{2,18},{4,20},{6,22},{8,24},{10,26},{12,28},{14,30},{16,0},... | collective-permute-start | bytes 516104 | tf_op jit(solution)/shard_map/ppermute | solution.py:573
  530.4 43.6 %copy-start.29 = (f32[1,2,48,768]{3,2,1,0:T(8,128)}, f32[1,2,48,768]{3,2,1,0:T(8,128)S(1)}, u32[]{:S(2)}) copy-start(f32[1,2,48,768]{3,2,1,0:T(8,128)S(1)} %collective-permute-done.43.refs_5_) | copy-start | bytes 884740
  530.4 15.4 %collective-permute-start.42 = (bf16[112,768]{1,0:T(8,128)(2,1)}, bf16[112,768]{1,0:T(8,128)(2,1)S(1)}, u32[]{:S(2)}, u32[]{:S(2)}) collective-permute-start(bf16[112,768]{1,0:T(8,128)(2,1)} %get-tuple-element.426), channel_id=1, source_target_pairs={{0,24},{2,26},{4,28},{6,30},{8,16},{10,18},{12,20},{14,22},{16,8},... | collective-permute-start | bytes 516104 | tf_op jit(solution)/shard_map/ppermute | solution.py:573
  534.3 16.0 %collective-permute-start.46 = (f32[1,2,48,768]{3,2,1,0:T(8,128)}, f32[1,2,48,768]{3,2,1,0:T(8,128)S(1)}, u32[]{:S(2)}, u32[]{:S(2)}) collective-permute-start(f32[1,2,48,768]{3,2,1,0:T(8,128)} %get-tuple-element.437.refs_3_), channel_id=1, source_target_pairs={{0,1},{1,0},{2,3},{3,2},{4,5},{5,4},{6,7},{7,6},{8,9},{9,8},{10,11... | collective-permute-start | bytes 884744 | tf_op jit(solution)/shard_map/ppermute | solution.py:569
  548.5 1.9 collective-permute-start.47
  548.5 1.8 collective-permute-start.48
  550.4 1.3 collective-permute-start.49
  552.4 3.5 collective-permute-start.50
  552.9 3.5 collective-permute-start.51
  554.3 4.4 collective-permute-start.52
  558.8 6.6 %collective-permute-start.53 = (f32[1,128]{1,0:T(1,128)S(1)}, f32[1,128]{1,0:T(1,128)S(1)}, u32[]{:S(2)}, u32[]{:S(2)}) collective-permute-start(f32[1,128]{1,0:T(1,128)S(1)} %add_add_fusion.1), channel_id=1, source_target_pairs={{0,8},{2,10},{4,12},{6,14},{8,0},{10,2},{12,4},{14,6},{16,24},{18,... | collective-permute-start | bytes 1544 | tf_op jit(solution)/shard_map/ppermute | solution.py:573
  562.2 4.4 collective-permute-start.54
  562.6 5.3 collective-permute-start.55
  (60 other events, 481.4 us)
Sparse Core Ops, SparseCore 0:
  13.3 174.2 all-gather.1

commit v9 on v8

--- a/solution.py
+++ b/solution.py
@@ -66,7 +66,17 @@
     )
 
 
-VMEM_LIMIT = 56 * 1024 * 1024
+def granted(shapes, margin):
+    total = margin << 20
+    for shape, kind in shapes:
+        size = jnp.dtype(kind).itemsize
+        *lead, rows, lanes = (1,) + tuple(shape)
+        for n in lead:
+            size *= n
+        total += size * (-(-rows // 16) * 16) * (-(-lanes // 128) * 128)
+    return min(total, 60 << 20)
+
+
 LOW, FULL = jnp.bfloat16, jnp.float32
 
 
@@ -91,7 +101,7 @@
         self.copies.append(copy)
 
 
-def call(kernel, scalars, outs, ins, anys=(), scratch=(), flops=0, sent=()):
+def call(kernel, scalars, outs, ins, anys=(), scratch=(), flops=0, sent=(), margin=6):
     whole = pl.BlockSpec(memory_space=pltpu.VMEM)
     left = pl.BlockSpec(memory_space=pl.ANY)
 
@@ -107,6 +117,8 @@
             for copy in out_refs[i].copies:
                 copy.wait()
 
+    held = [(x.shape, x.dtype) for x in ins] + list(outs)
+    held += [(x.shape, x.dtype) for x in scratch if x.memory_space == pltpu.VMEM]
     return pl.pallas_call(
         body,
         out_shape=[jax.ShapeDtypeStruct(s, t) for s, t in outs],
@@ -117,7 +129,7 @@
         scratch_shapes=[pltpu.VMEM(*outs[i]) for i in sent]
         + list(scratch)
         + [pltpu.SemaphoreType.DMA((len(sent), 5))] * (len(sent) > 0),
-        compiler_params=pltpu.CompilerParams(vmem_limit_bytes=VMEM_LIMIT),
+        compiler_params=pltpu.CompilerParams(vmem_limit_bytes=granted(held, margin)),
         cost_estimate=pl.CostEstimate(
             flops=flops,
             bytes_accessed=sum(x.size * x.dtype.itemsize for x in list(ins) + list(anys)),
@@ -250,21 +262,22 @@
 GELU_CUBE = 0.044715
 
 
-def fetch_hidden(weights, base, ups, downs, sems):
+def fetch_hidden(weights, base, order, ups, downs, sems):
     blocks, _, rows, _ = weights.shape
     width = blocks * rows
     half, some = width // 2, max(blocks // 4, 1)
     copies = {}
-    for t in range(4):
+    for t, (core_of, within) in enumerate(order):
         copies[0, t] = fetch(
-            [tile_of(weights, t // 2, base + (2 + t % 2) * width)], [ups.at[t]], sems, t
+            [tile_of(weights, core_of, base + (2 + within) * width)], [ups.at[t]], sems, t
         )
         if blocks >= 4 or t == 0:
             sources, targets = [], []
+            first = (2 * core_of + within) * some if blocks >= 4 else 0
             for core in range(2):
                 for j in range(4):
                     at = base + 4 * width + j * half
-                    sources.append(weights.at[pl.ds(t * some, some), core, :, at : at + half])
+                    sources.append(weights.at[pl.ds(first, some), core, :, at : at + half])
                     targets.append(
                         downs.at[pl.ds(t * some, some), j, :, core * half : (core + 1) * half]
                     )
@@ -277,12 +290,12 @@
     return wait
 
 
-def rows_of(downs, t):
+def rows_of(downs, t, order):
     blocks, parts, rows, width = downs.shape
     if blocks >= 4:
         some = blocks // 4
         return downs[t * some : (t + 1) * some].reshape(some * parts * rows, width)
-    return downs[0, t]
+    return downs[0, 2 * order[t][0] + order[t][1]]
 
 
 def hidden_scratch(weights):
@@ -297,7 +310,8 @@
 def hidden_forward_kernel(base, place_of, ins, anys, outs, ups, downs, sems):
     middle, gains = ins
     output, pack, hidden = outs
-    wait = fetch_hidden(anys[0], base, ups, downs, sems)
+    order = [(t // 2, t % 2) for t in range(4)]
+    wait = fetch_hidden(anys[0], base, order, ups, downs, sems)
     normed, _, _ = normalize(middle[...], gains[0:1], gains[1:2])
     pack[0] = normed.astype(LOW)
     pack.send(0)
@@ -312,7 +326,7 @@
         pack[1 + t] = value
         pack.send(1 + t)
         wait(1, t)
-        product = dot(value, rows_of(downs, t))
+        product = dot(value, rows_of(downs, t, order))
         output[...] = (middle[...] if t == 0 else output[...]) + product
 
 
@@ -335,11 +349,14 @@
     branch, grad, middle, gains = ins
     hidden, weights = anys
     grad_middle, grad_gains, grad_own, grad_other = outs
-    wait = fetch_hidden(weights, base, ups, downs, sems)
-    copies = fetch([hidden.at[t] for t in range(4)], [hidden_here.at[t] for t in range(4)], own_sems)
+    order = [(core, t) for core in (place_of[0], 1 - place_of[0]) for t in range(2)]
+    wait = fetch_hidden(weights, base, order, ups, downs, sems)
+    copies = fetch(
+        [hidden.at[2 * core + t] for core, t in order], [hidden_here.at[t] for t in range(4)], own_sems
+    )
     for t in range(4):
         wait(1, t)
-        grad_active = dot_nt(branch[...], rows_of(downs, t))
+        grad_active = dot_nt(branch[...], rows_of(downs, t, order))
         copies[t].wait()
         x = hidden_here[t]
         square = x * x
@@ -347,16 +364,7 @@
         slope = x * (GELU_SCALE + (3.0 * GELU_SCALE * GELU_CUBE) * square)
         slope = (0.5 + 0.5 * inner) * (1.0 + slope * (1.0 - inner))
         value = (grad_active * slope).astype(LOW)
-        mine = place_of[0] == t // 2
-
-        @pl.when(mine)
-        def _():
-            grad_own[t % 2] = value
-
-        @pl.when(jnp.logical_not(mine))
-        def _():
-            grad_other[t % 2] = value
-
+        (grad_own if t < 2 else grad_other)[t % 2] = value
         wait(0, t)
         product = dot_nt(value, matrix(ups, t))
         total[...] = product if t == 0 else total[...] + product
@@ -417,6 +425,7 @@
     for p in range(width // 128):
         columns = slice(p * 128, (p + 1) * 128)
         q, k, v, g = query[:, columns], keys[:, columns], values[:, columns], ga[:, columns]
+        flipped = k.T
         out_q, out_k, out_v = [], [], []
         for head in range(2):
             mask = head_mask(q.shape, head)
@@ -427,11 +436,11 @@
             across = jnp.sum(probs * grad_probs, 0, keepdims=True)
             grad_scores = (probs * (grad_probs - across)).astype(LOW)
             out_k.append(dot(grad_scores, q))
-            out_q.append(cross(grad_scores, k))
+            out_q.append(dot(flipped[head * HD : (head + 1) * HD], grad_scores))
             out_v.append(dot(probs.astype(LOW), g))
-        for out, target, scale in ((out_q, gq, HD ** (-0.5)), (out_k, gk, 1.0)):
-            x = jnp.where(head_mask(out[0].shape, 0), out[0], out[1])
-            x = x * scale if scale != 1.0 else x
+        out_q = jnp.concatenate(out_q, 0).T * HD ** (-0.5)
+        out_k = jnp.where(head_mask(out_k[0].shape, 0), out_k[0], out_k[1])
+        for x, target in ((out_q, gq), (out_k, gk)):
             x = x * cosine[...] - swap_halves(x) * sine[...]
             target[:, columns] = x.astype(LOW)
         gv[:, columns] = jnp.where(head_mask(out_v[0].shape, 0), out_v[0], out_v[1]).astype(LOW)
@@ -484,25 +493,32 @@
 def adam_step(master, grad, first, second, rate, decay):
     first = BETA_ONE * first + (1.0 - BETA_ONE) * grad
     second = BETA_TWO * second + (1.0 - BETA_TWO) * grad * grad
-    fix_one = 1.0 - BETA_ONE**STEP
-    fix_two = 1.0 - BETA_TWO**STEP
-    update = first / fix_one / (jnp.sqrt(second / fix_two) + ADAM_EPS) + decay * master
+    fix_one = 1.0 / (1.0 - BETA_ONE**STEP)
+    fix_two = 1.0 / (1.0 - BETA_TWO**STEP)
+    update = first * fix_one / (jnp.sqrt(second * fix_two) + ADAM_EPS) + decay * master
     return (master - rate * update, first, second)
 
 
-def optimizer_kernel(chunks, layers, place_of, scale, *refs):
-    n = (len(refs) - 24) // 2
-    own, other, masters = refs[:n], refs[n : 2 * n], refs[2 * n : 2 * n + 12]
-    outs = refs[2 * n + 12 :]
+def scale_of(totals):
+    count = totals[0:1, 1:2]
+    grad_norm = jnp.sqrt(totals[0:1, 2:3]) / count
+    return grad_norm, CLIP / jnp.maximum(grad_norm, CLIP) / count
+
+
+def optimizer_kernel(chunks, place_of, ins, anys, outs):
+    totals, small_own, small_other, *rest = ins
+    n = (len(rest) - 18) // 2
+    own, other, masters = rest[:n], rest[n : 2 * n], rest[2 * n :]
+    layers = len(chunks)
     first = place_of[0] == 0
-    count, factor = scale[0], scale[1]
-
-    def step(which, at, grad):
+    grad_norm, scale = scale_of(totals[...])
+    outs[0][...] = grad_norm
+
+    def step(which, at, grad, rate=RATE_MATRIX, decay=DECAY):
         master, moment, square = (masters[3 * which + i][at] for i in range(3))
-        clipped = grad / count * factor
-        values = adam_step(master, clipped, moment, square, RATE_MATRIX, DECAY)
+        values = adam_step(master, grad * scale, moment, square, rate, decay)
         for i in range(3):
-            outs[3 * which + i][at] = values[i]
+            outs[1 + 3 * which + i][at] = values[i]
 
     def tile(where, s, core):
         a, b = own[where[0]][where[1], s], other[where[0]][where[1], s]
@@ -526,23 +542,20 @@
                 for j in range(2):
                     at = (l, pl.ds((2 * s + j) * rows, rows), columns(0))
                     step(3, at, value[:, j * half : (j + 1) * half])
-
-
-def optimizer(place, scale, chunks, own, other, masters):
-    ins = list(own) + list(other) + list(masters)
-    whole = pl.BlockSpec(memory_space=pltpu.VMEM)
-    return pl.pallas_call(
-        functools.partial(optimizer_kernel, chunks, len(chunks)),
-        out_shape=[jax.ShapeDtypeStruct(m.shape, m.dtype) for m in masters],
-        in_specs=[pl.BlockSpec(memory_space=pltpu.SMEM)] * 2 + [whole] * len(ins),
-        out_specs=[whole] * len(masters),
-        compiler_params=pltpu.CompilerParams(vmem_limit_bytes=VMEM_LIMIT),
-        cost_estimate=pl.CostEstimate(
-            flops=20 * sum(m.size for m in masters),
-            bytes_accessed=8 * sum(m.size for m in masters),
-            transcendentals=0,
-        ),
-    )(place, scale, *ins)
+    small = jnp.where(first, small_own[...], small_other[...]).T
+    step(4, (slice(None), slice(None)), small[:V])
+    for n in range(masters[15].shape[0]):
+        step(5, n, small[V + 2 * n : V + 2 * n + 2], RATE_VECTOR, 0.0)
+
+
+def optimizer(place, totals, small, chunks, own, other, masters):
+    return call(
+        functools.partial(optimizer_kernel, chunks),
+        place,
+        [((1, 1), FULL)] + [(m.shape, m.dtype) for m in masters],
+        [totals, *small, *own, *other, *masters],
+        flops=20 * sum(m.size for m in masters),
+    )
 
 
 def pack_kernel(layers, place_of, ins, anys, outs):
@@ -990,18 +1003,8 @@
         middle, query, keys, values, lse, pack = attention_forward(
             place, resid, weights, base(l), gain[0], cosine, sine, segments
         )
-        if l > 0:
-            middle, came = tie(middle, kept[-1][-1])
-            kept[-1] = kept[-1][:-1] + (came,)
-        pack_came = swap_cores(pack)
-        output, pack_mid, hidden = hidden_forward(
-            place, middle, weights, base(l), gain[1]
-        )
-        output, pack_came = tie(output, pack_came)
-        kept.append(
-            (resid, query, keys, values, lse, pack, pack_came, middle, hidden, pack_mid)
-            + (swap_cores(pack_mid),)
-        )
+        output, pack_mid, hidden = hidden_forward(place, middle, weights, base(l), gain[1])
+        kept.append((resid, query, keys, values, lse, pack, middle, hidden, pack_mid))
         resid = output
     final_gain = gains[2 * layers]
     normed_out, unit_out, inverse_out = normalize(resid, final_gain[0], final_gain[1])
@@ -1024,8 +1027,9 @@
     branch = grad.astype(LOW)
     branch_own, branch_other = half_of(branch, core), half_of(branch, 1 - core)
     grad_norms = [grad_final_gain, grad_final_bias]
-    grad, branch, came = tie(grad, branch, kept[-1][-1])
-    kept[-1] = kept[-1][:-1] + (came,)
+    mid_came = [swap_cores(saved[-1]) for saved in kept]
+    pack_came = [swap_cores(saved[5]) for saved in kept]
+    grad, branch, mid_came[-1] = tie(grad, branch, mid_came[-1])
 
     rounds = Rounds(place, rows, width, sums) if fast else PlainRounds()
     whole = lambda array, i=None: (array, i, None, None)
@@ -1034,14 +1038,14 @@
     ]
     chunk = []
     for l in reversed(range(layers)):
-        (resid, query, keys, values, lse, pack, pack_came, middle, hidden, pack_mid, mid_came) = kept[l]
+        resid, query, keys, values, lse, pack, middle, hidden, pack_mid = kept[l]
         gain = gains[2 * l : 2 * l + 2]
         branch_came = swap_cores(branch_other)
         chunk.append(
             [
                 [
                     (whole(pack_mid, 1 + t), whole(branch_own)),
-                    (whole(mid_came, 1 + t), whole(branch_came)),
+                    (whole(mid_came[l], 1 + t), whole(branch_came)),
                 ]
                 for t in range(4)
             ]
@@ -1061,7 +1065,7 @@
             [
                 [
                     tile(
-                        whole(pack_mid, 0), whole(up_own, s), whole(mid_came, 0), whole(up_came, s)
+                        whole(pack_mid, 0), whole(up_own, s), whole(mid_came[l], 0), whole(up_came, s)
                     )
                     for s in range(2)
                 ]
@@ -1073,17 +1077,19 @@
             query, keys, values, lse,
         )
         grad_norms = [gains_in, gains_mid] + grad_norms
-        grad, branch, branch_own, branch_other, mix_own, mix_other = rounds.finish(
-            grad, branch, branch_own, branch_other, mix_own, mix_other
+        grad, branch, branch_own, branch_other, mix_own, mix_other, mid_came, pack_came = (
+            rounds.finish(
+                grad, branch, branch_own, branch_other, mix_own, mix_other, mid_came, pack_came
+            )
         )
         mix_came = swap_cores(mix_other)
         products = lambda i, a, b: [
             ((pack, i, None, None), (mix_own, 1, a, b)),
-            ((pack_came, i, None, None), (mix_came, 1, a, b)),
+            ((pack_came[l], i, None, None), (mix_came, 1, a, b)),
         ]
         chunk = [
             [
-                tile(whole(pack, 0), whole(mix_own, 0), whole(pack_came, 0), whole(mix_came, 0)),
+                tile(whole(pack, 0), whole(mix_own, 0), whole(pack_came[l], 0), whole(mix_came, 0)),
                 [(0, half, products(0, 0, half)), (half, width, products(1, half, width))],
             ]
         ]
@@ -1099,8 +1105,7 @@
         rounds.swap_rest()
         share_small = rounds.small_share
         small_other = swap_cores(share_small)
-        totals, rest = tie(rounds.totals, [rounds.others, small_other])
-        share_small = jnp.where(core == 0, share_small, small_other)
+        totals = rounds.totals
     else:
         rounds.step(chunk)
         table = sum(cross(l[0], r[0]) for l, r in products)
@@ -1115,9 +1120,6 @@
             squares = squares + jnp.sum(value)
         totals = sums + jnp.where(jnp.arange(SMALL) == 2, squares, 0.0)[None]
     totals = total_of(totals, fsdp)
-    loss_sum, count, square_total = totals[0, 0], totals[0, 1], totals[0, 2]
-    share_small = share_small[:, : V + norms].T
-
     shares = list(zip(rounds.shares, rounds.others)) if fast else rounds.shares
     places = [(2 * (layers - 1 - l), 0 if l == layers - 1 else 1) for l in range(layers)]
 
@@ -1126,7 +1128,6 @@
         ordered = (jnp.where(core == 0, own, other), jnp.where(core == 0, other, own))
         return [v[s] for v in ordered for s in range(2)]
 
-    share_small = (share_small[:V], share_small[V:].reshape(-1, 2, rows))
     if not fast:
         share_in, share_out, share_up, share_down = [], [], [], []
         side = lambda *values: jnp.concatenate(values, 1)
@@ -1154,8 +1155,6 @@
         share_in, share_out, share_up, share_down = (
             jnp.stack(v) for v in (share_in, share_out, share_up, share_down)
         )
-    grad_norm = jnp.sqrt(square_total) / count
-    factor = CLIP / jnp.maximum(grad_norm, CLIP)
     masters = (inward, outward, expand, shrink, codon_table, norm_params)
     firsts = (inward_first, outward_first, expand_first, shrink_first, table_first, norm_first)
     seconds = (
@@ -1167,26 +1166,24 @@
         norm_second,
     )
     if fast:
-        matrices = [v for group in zip(masters[:4], firsts[:4], seconds[:4]) for v in group]
         chunks = [((at + 2, 0), (at + 1, 0), (at, pair)) for at, pair in places]
         own, other = zip(*shares)
-        scale = jnp.stack([count, factor])
-        values = list(optimizer(place, scale, chunks, own, other, matrices))
+        states = [v for group in zip(masters, firsts, seconds) for v in group]
+        grad_norm, *values = optimizer(
+            place, totals, (share_small, small_other), chunks, own, other, states
+        )
     else:
+        grad_norm, scale = scale_of(totals)
+        share_small = share_small[:, : V + norms].T
+        grads = (share_in, share_out, share_up, share_down)
+        grads += (share_small[:V], share_small[V:].reshape(-1, 2, rows))
         values = []
-        for index, grad in enumerate((share_in, share_out, share_up, share_down)):
-            clipped = grad / count * factor
+        for index, grad in enumerate(grads):
+            rate, decay = (RATE_VECTOR, 0.0) if index == 5 else (RATE_MATRIX, DECAY)
             values.extend(
-                adam_step(
-                    masters[index], clipped, firsts[index], seconds[index], RATE_MATRIX, DECAY
-                )
+                adam_step(masters[index], grad * scale.reshape(()), firsts[index], seconds[index], rate, decay)
             )
-    for index, rate, decay in ((4, RATE_MATRIX, DECAY), (5, RATE_VECTOR, 0.0)):
-        clipped = share_small[index - 4] / count * factor
-        values.extend(
-            adam_step(masters[index], clipped, firsts[index], seconds[index], rate, decay)
-        )
-    return (loss_sum, count, grad_norm, *values)
+    return (totals[0, 0], totals[0, 1], grad_norm.reshape(()), *values)
 
 
 def solution(mesh):

time: 602 us -> 637 us (1.058)
  local copies, waits for them, and re-layouts: 20.3 us -> 114 us
  Pallas kernels: 231 us -> 189 us
  waiting for transfers between devices: 250 us -> 238 us
    unnamed x134 -> x296, local copies, waits for them, and re-layouts: 11.7 us -> 105 us
    pallas_call x17 -> x18, Pallas kernels: 221 us -> 189 us  [call(): pl.pallas_call(body, out_shape=[jax.ShapeDtypeStruct(s, t) for s, t in ou...]
    pallas_call x1 -> x0, Pallas kernels: 10.8 us -> none  [optimizer(): pl.pallas_call(functools.partial(optimizer_kernel, chunks, len(chunks)),...]
    ppermute x23, waiting for transfers between devices: 24.7 us -> 15.1 us  [swap_cores(): return lax.ppermute(value, 'dp', [(0, 1), (1, 0)])]
  transfers between devices with their start and end apart: 57 -> 57, of which waited for: 22 -> 20; matrix products, arithmetic and copies ran while one was open for 3% -> 4% of each run, Pallas kernels for 22% -> 13%
where the time goes in v9:
time: 637 us; the launch traced here: 625 us
  waiting for transfers between devices  238 us (37%)
  Pallas kernels  189 us (30%)
  local copies, waits for them, and re-layouts  114 us (18%)
  starting transfers between devices  51.7 us (8%)
  between operations  15.5 us (2%)
  other arithmetic  13.2 us (2%)
    pallas_call x18, Pallas kernels, call(): pl.pallas_call(body, out_shape=[jax.ShapeDtypeStruct(s, t) for s, t in ou...  189 us
    all_gather x1, waiting for transfers between devices, body(): weights = lax.all_gather(weights, ('fsdp', 'dp'), axis=0, tiled=True)  172 us
    unnamed x296, local copies, waits for them, and re-layouts  105 us
    ppermute x33, waiting for transfers between devices, across(): return lax.ppermute(value, 'fsdp', [(i, i ^ mask) for i in range(size)])  50.6 us
    ppermute x33, starting transfers between devices, across(): return lax.ppermute(value, 'fsdp', [(i, i ^ mask) for i in range(size)])  47.2 us
    ppermute x23, waiting for transfers between devices, swap_cores(): return lax.ppermute(value, 'dp', [(0, 1), (1, 0)])  15.1 us
  transfers between devices with their start and end apart: 57, of which 20 were waited for; matrix products, arithmetic and copies ran while one was open for 4% of the time, Pallas kernels for 13%

profile of v9, /device:TPU:0, one launch (start us, length us, event | category | flops | bytes accessed | tf_op | source)
XLA Modules:
  0.0 625.4 jit_solution(4684318210630338138)
XLA Ops:
  13.7 1.6 shard_map.364
  17.7 172.1 %all-gather.2.cloned.1.call-done = bf16[1536,9344]{1,0:T(8,128)(2,1)} async-done(((bf16[48,9344]{1,0:T(8,128)(2,1)}), bf16[1536,9344]{1,0:T(8,128)(2,1)}) %all-gather.2.cloned.1.call-update) | async-done | bytes 28704784 | tf_op jit(solution)/shard_map/all_gather | solution.py:980
  191.4 12.1 %shard_map.365 = (f32[512,768]{1,0:T(8,128)S(1)}, bf16[512,768]{1,0:T(8,128)(2,1)S(1)}, bf16[512,768]{1,0:T(8,128)(2,1)S(1)}, bf16[512,768]{1,0:T(8,128)(2,1)S(1...) custom-call(s32[4]{0:T(128)S(1)} %pad_add_fusion.scalars, f32[512,768]{1,0:T(8,128)S(1)} %fusion.3.refs_0_.refs_10_, ...), custom_call_target="tpu_custom_call" | custom-call | flops 3221225472 | bytes 30812160 | tf_op jit(solution)/shard_map/pallas_call | solution.py:122
  206.0 12.7 %shard_map.366 = (f32[512,768]{1,0:T(8,128)S(1)}, bf16[5,512,768]{2,1,0:T(8,128)(2,1)}, f32[4,512,768]{2,1,0:T(8,128)S(1)}) custom-call(s32[4]{0:T(128)S(1)} %pad_add_fusion.scalars, f32[512,768]{1,0:T(8,128)S(1)} %get-tuple-element.242.refs_0_.refs_2_, f32[2,768]{1,0:T(2,128)S(1)} %get-tuple-element.518.refs_1_.refs_3_, bf16[16,2,48,9344]{3,2,1,0:T(8,128)(2,1)} %bitcast.33), custom_call_target="tpu_custom_call" | custom-call | flops 4831838208 | bytes 30283776 | tf_op jit(solution)/shard_map/pallas_call | solution.py:122
  218.8 13.1 %shard_map.367 = (f32[512,768]{1,0:T(8,128)S(1)}, bf16[512,768]{1,0:T(8,128)(2,1)S(1)}, bf16[512,768]{1,0:T(8,128)(2,1)S(1)}, bf16[512,768]{1,0:T(8,128)(2,1)S(1...) custom-call(s32[4]{0:T(128)S(1)} %pad_add_fusion.scalars, f32[512,768]{1,0:T(8,128)S(1)} %get-tuple-element.244.refs_0_.refs_10_, ...), custom_call_target="tpu_custom_call" | custom-call | flops 3221225472 | bytes 30812160 | tf_op jit(solution)/shard_map/pallas_call | solution.py:122
  235.2 21.9 %shard_map.368 = (f32[512,768]{1,0:T(8,128)S(1)}, bf16[5,512,768]{2,1,0:T(8,128)(2,1)}, f32[4,512,768]{2,1,0:T(8,128)S(1)}) custom-call(s32[4]{0:T(128)S(1)} %pad_add_fusion.scalars, f32[512,768]{1,0:T(8,128)S(1)} %get-tuple-element.246.refs_0_.refs_2_, f32[2,768]{1,0:T(2,128)S(1)} %get-tuple-element.516.refs_1_.refs_3_, bf16[16,2,48,9344]{3,2,1,0:T(8,128)(2,1)} %bitcast.35), custom_call_target="tpu_custom_call" | custom-call | flops 4831838208 | bytes 30283776 | tf_op jit(solution)/shard_map/pallas_call | solution.py:122
  257.2 2.6 copy-done.13
  263.9 1.6 fusion.18
  265.5 1.7 copy.58
  272.0 2.2 multiply_reduce_fusion
  276.7 7.1 %shard_map.369 = (bf16[384,768]{1,0:T(8,128)(2,1)S(1)}, bf16[384,768]{1,0:T(8,128)(2,1)S(1)}, f32[1,2,384,768]{3,2,1,0:T(8,128)S(1)}) custom-call(s32[4]{0:T(128)S(1)} %pad_add_fusion.scalars, bf16[5,512,768]{2,1,0:T(8,128)(2,1)} %get-tuple-element.247.refs_0_, bf16[512,384]{1,0:T(8,128)(2,1)S(1)} %get-tuple-element.515.refs_1_, ...), custom_call_target="tpu_custom_call" | custom-call | flops 2415919104 | bytes 8650752 | tf_op jit(solution)/shard_map/pallas_call | solution.py:122
  283.8 1.5 collective-permute-start.2
  287.6 14.3 %shard_map.370 = (f32[512,768]{1,0:T(8,128)S(1)}, f32[2,768]{1,0:T(2,128)S(1)}, bf16[2,512,768]{2,1,0:T(8,128)(2,1)S(1)}, bf16[2,512,768]{2,1,0:T(8,128)(2,1)S(1)}) custom-call(s32[4]{0:T(128)S(1)} %pad_add_fusion.scalars, bf16[512,768]{1,0:T(8,128)(2,1)S(1)} %get-tuple-element.257.refs_0_, f32[512,768]{1,0:T(8,128)S(1)} %get-tuple-element.258.refs_1_, ...), custom_call_target="tpu_custom_call" | custom-call | flops 4831838208 | bytes 38934528 | tf_op jit(solution)/shard_map/pallas_call | solution.py:122
  306.2 3.3 collective-permute-done.7.refs_3_
  309.5 7.4 %shard_map.371 = (bf16[576,768]{1,0:T(8,128)(2,1)}, bf16[576,768]{1,0:T(8,128)(2,1)}, f32[1,2,384,768]{3,2,1,0:T(8,128)S(1)}, f32[1,2,192,768]{3,2,1,0:T(8,128)S(1)}) custom-call(s32[4]{0:T(128)S(1)} %pad_add_fusion.scalars, bf16[5,512,768]{2,1,0:T(8,128)(2,1)} %get-tuple-element.247.refs_0_, bf16[2,512,768]{2,1,0:T(8,128)(2,1)S(1)} %get-tuple-element.263.refs_1_, ...), custom_call_target="tpu_custom_call" | custom-call | flops 2415919104 | bytes 14548992 | tf_op jit(solution)/shard_map/pallas_call | solution.py:122
  316.9 1.5 copy-done.21
  319.4 1.4 collective-permute-start.8
  323.1 1.4 copy-done.9
  324.5 1.4 copy-done.28
  330.0 18.2 %shard_map.372 = (f32[512,768]{1,0:T(8,128)S(1)}, bf16[512,768]{1,0:T(8,128)(2,1)S(1)}, bf16[512,384]{1,0:T(8,128)(2,1)S(1)}, bf16[512,384]{1,0:T(8,128)(2,1)S(1...) custom-call(s32[4]{0:T(128)S(1)} %pad_add_fusion.scalars, ...), custom_call_target="tpu_custom_call" | custom-call | flops 4429185024 | bytes 34768896 | tf_op jit(solution)/shard_map/pallas_call | solution.py:122
  350.9 3.1 collective-permute-done.14.refs_7_
  355.7 14.8 %shard_map.373 = (bf16[960,768]{1,0:T(8,128)(2,1)S(1)}, bf16[960,768]{1,0:T(8,128)(2,1)S(1)}, f32[2,2,384,768]{3,2,1,0:T(8,128)}, f32[1,2,192,768]{3,2,1,0:T(8,1...) custom-call(s32[4]{0:T(128)S(1)} %pad_add_fusion.scalars, ...), custom_call_target="tpu_custom_call" | custom-call | flops 4831838208 | bytes 20250624 | tf_op jit(solution)/shard_map/pallas_call | solution.py:122
  370.5 1.4 collective-permute-start.15
  372.7 1.9 collective-permute-start.18
  374.6 2.4 collective-permute-start.19
  379.6 14.3 %shard_map.374 = (f32[512,768]{1,0:T(8,128)S(1)}, f32[2,768]{1,0:T(2,128)S(1)}, bf16[2,512,768]{2,1,0:T(8,128)(2,1)S(1)}, bf16[2,512,768]{2,1,0:T(8,128)(2,1)S(1)}) custom-call(s32[4]{0:T(128)S(1)} %pad_add_fusion.scalars, bf16[512,768]{1,0:T(8,128)(2,1)S(1)} %copy-done.64, f32[512,768]{1,0:T(8,128)S(1)} %copy-done.26, f32[512,768]{1,0:T(8,128)S(1)} %copy-done.7, ...), custom_call_target="tpu_custom_call" | custom-call | flops 4831838208 | bytes 38934528 | tf_op jit(solution)/shard_map/pallas_call | solution.py:122
  396.9 8.2 %collective-permute-done.15.refs_6_ = bf16[960,768]{1,0:T(8,128)(2,1)S(1)} collective-permute-done((bf16[960,768]{1,0:T(8,128)(2,1)S(1)}, bf16[960,768]{1,0:T(8,128)(2,1)S(1)}, u32[]{:S(2)}, u32[]{:S(2)}) %collective-permute-start.15) | collective-permute-done | bytes 1474592 | tf_op jit(solution)/shard_map/ppermute | solution.py:586
  407.4 3.4 collective-permute-done.20.refs_3_
  410.8 1.4 copy-done.32
  416.2 9.9 %shard_map.375 = (bf16[768,768]{1,0:T(8,128)(2,1)}, bf16[768,768]{1,0:T(8,128)(2,1)}, f32[1,2,384,768]{3,2,1,0:T(8,128)S(1)}, f32[2,2,192,768]{3,2,1,0:T(8,128)}...) custom-call(s32[4]{0:T(128)S(1)} %pad_add_fusion.scalars, ...), custom_call_target="tpu_custom_call" | custom-call | flops 2415919104 | bytes 20597760 | tf_op jit(solution)/shard_map/pallas_call | solution.py:122
  431.4 1.4 collective-permute-start.21
  435.2 2.0 collective-permute-start.24
  437.1 2.4 collective-permute-start.25
  439.6 1.4 copy-done.24
  444.4 20.4 %shard_map.376 = (f32[512,768]{1,0:T(8,128)}, bf16[512,768]{1,0:T(8,128)(2,1)}, bf16[512,384]{1,0:T(8,128)(2,1)}, bf16[512,384]{1,0:T(8,128)(2,1)}, f32[2,768]{1...) custom-call(s32[4]{0:T(128)S(1)} %pad_add_fusion.scalars, f32[512,768]{1,0:T(8,128)S(1)} %copy-done.24, ...), custom_call_target="tpu_custom_call" | custom-call | flops 4429185024 | bytes 34768896 | tf_op jit(solution)/shard_map/pallas_call | solution.py:122
  473.3 1.4 copy-done.30
  484.4 10.0 %shard_map.377 = (bf16[640,768]{1,0:T(8,128)(2,1)S(1)}, bf16[576,768]{1,0:T(8,128)(2,1)S(1)}, f32[1,2,384,768]{3,2,1,0:T(8,128)}, f32[384,128]{1,0:T(8,128)S(1)}...) custom-call(s32[4]{0:T(128)S(1)} %pad_add_fusion.scalars, ...), custom_call_target="tpu_custom_call" | custom-call | flops 2415919104 | bytes 17841152 | tf_op jit(solution)/shard_map/pallas_call | solution.py:122
  496.4 2.0 collective-permute-start.33
  498.3 2.4 collective-permute-start.34
  500.7 9.5 %collective-permute-done.32.refs_6_ = bf16[192,768]{1,0:T(8,128)(2,1)S(1)} collective-permute-done((bf16[192,768]{1,0:T(8,128)(2,1)S(1)}, bf16[192,768]{1,0:T(8,128)(2,1)S(1)}, u32[]{:S(2)}, u32[]{:S(2)}) %collective-permute-start.32) | collective-permute-done | bytes 294944 | tf_op jit(solution)/shard_map/ppermute | solution.py:586
  510.3 9.6 %collective-permute-done.33.refs_7_ = bf16[192,768]{1,0:T(8,128)(2,1)S(1)} collective-permute-done((bf16[192,768]{1,0:T(8,128)(2,1)S(1)}, bf16[192,768]{1,0:T(8,128)(2,1)S(1)}, u32[]{:S(2)}, u32[]{:S(2)}) %collective-permute-start.33) | collective-permute-done | bytes 294944 | tf_op jit(solution)/shard_map/ppermute | solution.py:586
  519.9 1.7 copy-done.22
  521.5 1.9 shard_map.378
  523.4 1.5 collective-permute-start.36
  524.9 5.5 collective-permute-start.37
  531.3 2.4 collective-permute-done.37.refs_5_
  533.7 2.9 collective-permute-start.39
  536.6 6.6 %collective-permute-done.38.refs_6_ = bf16[96,768]{1,0:T(8,128)(2,1)S(1)} collective-permute-done((bf16[96,768]{1,0:T(8,128)(2,1)S(1)}, bf16[96,768]{1,0:T(8,128)(2,1)S(1)}, u32[]{:S(2)}, u32[]{:S(2)}) %collective-permute-start.38) | collective-permute-done | bytes 147488 | tf_op jit(solution)/shard_map/ppermute | solution.py:586
  544.8 2.3 collective-permute-start.40
  547.4 2.1 collective-permute-start.42
  552.3 1.7 collective-permute-done.40.refs_2_
  554.0 8.0 %collective-permute-done.41.refs_3_ = bf16[112,768]{1,0:T(8,128)(2,1)S(1)} collective-permute-done((bf16[112,768]{1,0:T(8,128)(2,1)S(1)}, bf16[112,768]{1,0:T(8,128)(2,1)S(1)}, u32[]{:S(2)}, u32[]{:S(2)}) %collective-permute-start.41) | collective-permute-done | bytes 172064 | tf_op jit(solution)/shard_map/ppermute | solution.py:586
  567.7 1.5 collective-permute-start.48
  570.1 2.0 collective-permute-done.48
  572.1 2.4 collective-permute-start.49
  574.5 1.4 copy.64.refs_25_
  576.6 1.4 copy.65.refs_26_
  578.0 1.8 collective-permute-start.51
  579.8 1.4 copy.66.refs_27_
  581.8 1.6 collective-permute-done.51
  604.4 7.6 %shard_map.381 = (f32[1,1]{1,0:T(1,128)}, f32[2,48,2304]{2,1,0:T(8,128)}, f32[2,48,2304]{2,1,0:T(8,128)}, f32[2,48,2304]{2,1,0:T(8,128)}, f32[2,48,768]{2,1,0:T(...) custom-call(s32[4]{0:T(128)S(1)} %pad_add_fusion.scalars, ...), custom_call_target="tpu_custom_call" | custom-call | flops 53314560 | bytes 14251520 | tf_op jit(solution)/shard_map/pallas_call | solution.py:122
  613.8 1.5 copy.67
  615.2 1.5 copy.68
  616.7 1.5 copy.69
  (417 shorter events, 125.1 us)
Async XLA Ops:
  7.2 182.6 %all-gather.2.cloned.1.call-start = ((), (), s32[]{:S(2)}) async-start(), calls=%async_computation | async-start | bytes 29601792 | tf_op jit(solution)/shard_map/all_gather | solution.py:980
  17.0 201.8 %copy-start.2 = (f32[512,128]{1,0:T(8,128)}, f32[512,128]{1,0:T(8,128)S(1)}, u32[]{:S(2)}) copy-start(f32[512,128]{1,0:T(8,128)S(1)} %get-tuple-element.530.refs_3_.refs_7_) | copy-start | bytes 786436
  17.0 201.8 %copy-start.4 = (f32[512,128]{1,0:T(8,128)}, f32[512,128]{1,0:T(8,128)S(1)}, u32[]{:S(2)}) copy-start(f32[512,128]{1,0:T(8,128)S(1)} %get-tuple-element.531.refs_4_.refs_8_) | copy-start | bytes 786436
  17.7 185.8 %copy-start.136 = (s32[512]{0:T(512)}, s32[512]{0:T(512)S(1)}, u32[]{:S(2)}) copy-start(s32[512]{0:T(512)S(1)} %get-tuple-element.521) | copy-start | bytes 6148
  259.8 16.3 %collective-permute-start = (bf16[5,512,768]{2,1,0:T(8,128)(2,1)}, bf16[5,512,768]{2,1,0:T(8,128)(2,1)}, u32[]{:S(2)}, u32[]{:S(2)}) collective-permute-start(bf16[5,512,768]{2,1,0:T(8,128)(2,1)} %get-tuple-element.247.refs_0_), channel_id=1, source_target_pairs={{0,1},{1,0},{2,3},{3,2},{4,5},{5,4},{6,7},{7,6},{8,9},{9,8},{10,11... | collective-permute-start | bytes 11796488 | tf_op jit(solution)/shard_map/ppermute | solution.py:582
  274.9 1.8 collective-permute-start.1
  275.2 75.0 %collective-permute-start.10 = (bf16[5,512,768]{2,1,0:T(8,128)(2,1)}, bf16[5,512,768]{2,1,0:T(8,128)(2,1)}, u32[]{:S(2)}, u32[]{:S(2)}) collective-permute-start(bf16[5,512,768]{2,1,0:T(8,128)(2,1)} %get-tuple-element.243.refs_4_.refs_0_), channel_id=1, source_target_pairs={{0,1},{1,0},{2,3},{3,2},{4,5},{5,4},{6,7},{7,6},{8,9},{9,8},{10,11... | collective-permute-start | bytes 11796488 | tf_op jit(solution)/shard_map/ppermute | solution.py:582
  275.9 28.5 %collective-permute-start.4 = (bf16[512,768]{1,0:T(8,128)(2,1)S(1)}, bf16[512,768]{1,0:T(8,128)(2,1)S(1)}, u32[]{:S(2)}, u32[]{:S(2)}) collective-permute-start(bf16[512,768]{1,0:T(8,128)(2,1)S(1)} %copy-done.1), channel_id=1, source_target_pairs={{0,1},{1,0},{2,3},{3,2},{4,5},{5,4},{6,7},{7,6},{8,9},{9,8},{10,11... | collective-permute-start | bytes 2359304 | tf_op jit(solution)/shard_map/ppermute | solution.py:582
  283.8 21.5 %collective-permute-start.2 = (bf16[384,768]{1,0:T(8,128)(2,1)S(1)}, bf16[384,768]{1,0:T(8,128)(2,1)S(1)}, u32[]{:S(2)}, u32[]{:S(2)}) collective-permute-start(bf16[384,768]{1,0:T(8,128)(2,1)S(1)} %get-tuple-element.255), channel_id=1, source_target_pairs={{0,2},{2,0},{4,6},{6,4},{8,10},{10,8},{12,14},{14,12},{16,18},{18,... | collective-permute-start | bytes 1769480 | tf_op jit(solution)/shard_map/ppermute | solution.py:586
  285.3 20.0 %collective-permute-start.3 = (bf16[384,768]{1,0:T(8,128)(2,1)S(1)}, bf16[384,768]{1,0:T(8,128)(2,1)S(1)}, u32[]{:S(2)}, u32[]{:S(2)}) collective-permute-start(bf16[384,768]{1,0:T(8,128)(2,1)S(1)} %get-tuple-element.256), channel_id=1, source_target_pairs={{0,4},{2,6},{4,0},{6,2},{8,12},{10,14},{12,8},{14,10},{16,20},{18,... | collective-permute-start | bytes 1769480 | tf_op jit(solution)/shard_map/ppermute | solution.py:586
  286.1 1.4 collective-permute-start.6
  287.5 16.2 %collective-permute-start.5 = (bf16[512,128]{1,0:T(8,128)(2,1)S(1)}, bf16[512,128]{1,0:T(8,128)(2,1)S(1)}, u32[]{:S(2)}, u32[]{:S(2)}) collective-permute-start(bf16[512,128]{1,0:T(8,128)(2,1)S(1)} %pad.18.refs_5_), channel_id=1, source_target_pairs={{0,1},{1,0},{2,3},{3,2},{4,5},{5,4},{6,7},{7,6},{8,9},{9,8},{10,11... | collective-permute-start | bytes 393224 | tf_op jit(solution)/shard_map/ppermute | solution.py:582
  305.3 4.2 collective-permute-start.7
  305.7 44.5 %collective-permute-start.12 = (bf16[2,512,768]{2,1,0:T(8,128)(2,1)}, bf16[2,512,768]{2,1,0:T(8,128)(2,1)}, u32[]{:S(2)}, u32[]{:S(2)}) collective-permute-start(bf16[2,512,768]{2,1,0:T(8,128)(2,1)} %get-tuple-element.245.refs_0_), channel_id=1, source_target_pairs={{0,1},{1,0},{2,3},{3,2},{4,5},{5,4},{6,7},{7,6},{8,9},{9,8},{10,11... | collective-permute-start | bytes 4718600 | tf_op jit(solution)/shard_map/ppermute | solution.py:582
  305.8 44.4 %collective-permute-start.11 = (bf16[2,512,768]{2,1,0:T(8,128)(2,1)}, bf16[2,512,768]{2,1,0:T(8,128)(2,1)}, u32[]{:S(2)}, u32[]{:S(2)}) collective-permute-start(bf16[2,512,768]{2,1,0:T(8,128)(2,1)} %get-tuple-element.241.refs_0_), channel_id=1, source_target_pairs={{0,1},{1,0},{2,3},{3,2},{4,5},{5,4},{6,7},{7,6},{8,9},{9,8},{10,11... | collective-permute-start | bytes 4718600 | tf_op jit(solution)/shard_map/ppermute | solution.py:582
  319.4 30.8 %collective-permute-start.8 = (bf16[576,768]{1,0:T(8,128)(2,1)}, bf16[576,768]{1,0:T(8,128)(2,1)}, u32[]{:S(2)}, u32[]{:S(2)}) collective-permute-start(bf16[576,768]{1,0:T(8,128)(2,1)} %get-tuple-element.273), channel_id=1, source_target_pairs={{0,2},{2,0},{4,6},{6,4},{8,10},{10,8},{12,14},{14,12},{16,18},{18,... | collective-permute-start | bytes 2654216 | tf_op jit(solution)/shard_map/ppermute | solution.py:586
  320.8 29.5 %collective-permute-start.9 = (bf16[576,768]{1,0:T(8,128)(2,1)}, bf16[576,768]{1,0:T(8,128)(2,1)}, u32[]{:S(2)}, u32[]{:S(2)}) collective-permute-start(bf16[576,768]{1,0:T(8,128)(2,1)} %get-tuple-element.274), channel_id=1, source_target_pairs={{0,4},{2,6},{4,0},{6,2},{8,12},{10,14},{12,8},{14,10},{16,20},{18,... | collective-permute-start | bytes 2654216 | tf_op jit(solution)/shard_map/ppermute | solution.py:586
  350.3 4.4 collective-permute-start.13
  350.4 3.6 collective-permute-start.14
  370.5 34.6 %collective-permute-start.15 = (bf16[960,768]{1,0:T(8,128)(2,1)S(1)}, bf16[960,768]{1,0:T(8,128)(2,1)S(1)}, u32[]{:S(2)}, u32[]{:S(2)}) collective-permute-start(bf16[960,768]{1,0:T(8,128)(2,1)S(1)} %get-tuple-element.306), channel_id=1, source_target_pairs={{0,2},{2,0},{4,6},{6,4},{8,10},{10,8},{12,14},{14,12},{16,18},{18,... | collective-permute-start | bytes 4423688 | tf_op jit(solution)/shard_map/ppermute | solution.py:586
  372.0 34.3 %collective-permute-start.16 = (bf16[960,768]{1,0:T(8,128)(2,1)S(1)}, bf16[960,768]{1,0:T(8,128)(2,1)S(1)}, u32[]{:S(2)}, u32[]{:S(2)}) collective-permute-start(bf16[960,768]{1,0:T(8,128)(2,1)S(1)} %get-tuple-element.307), channel_id=1, source_target_pairs={{0,4},{2,6},{4,0},{6,2},{8,12},{10,14},{12,8},{14,10},{16,20},{18,... | collective-permute-start | bytes 4423688 | tf_op jit(solution)/shard_map/ppermute | solution.py:586
  372.7 24.2 %collective-permute-start.17 = (bf16[96,768]{1,0:T(8,128)(2,1)S(1)}, bf16[96,768]{1,0:T(8,128)(2,1)S(1)}, u32[]{:S(2)}, u32[]{:S(2)}) collective-permute-start(bf16[96,768]{1,0:T(8,128)(2,1)S(1)} %get-tuple-element.308), channel_id=1, source_target_pairs={{0,8},{2,10},{4,12},{6,14},{8,0},{10,2},{12,4},{14,6},{16,24},{18,... | collective-permute-start | bytes 442376 | tf_op jit(solution)/shard_map/ppermute | solution.py:586
  372.7 24.2 %collective-permute-start.18 = (bf16[96,768]{1,0:T(8,128)(2,1)S(1)}, bf16[96,768]{1,0:T(8,128)(2,1)S(1)}, u32[]{:S(2)}, u32[]{:S(2)}) collective-permute-start(bf16[96,768]{1,0:T(8,128)(2,1)S(1)} %get-tuple-element.309), channel_id=1, source_target_pairs={{0,16},{2,18},{4,20},{6,22},{8,24},{10,26},{12,28},{14,30},{16,0},... | collective-permute-start | bytes 442376 | tf_op jit(solution)/shard_map/ppermute | solution.py:586
  374.6 22.3 %collective-permute-start.19 = (bf16[96,768]{1,0:T(8,128)(2,1)S(1)}, bf16[96,768]{1,0:T(8,128)(2,1)S(1)}, u32[]{:S(2)}, u32[]{:S(2)}) collective-permute-start(bf16[96,768]{1,0:T(8,128)(2,1)S(1)} %get-tuple-element.310), channel_id=1, source_target_pairs={{0,24},{2,26},{4,28},{6,30},{8,16},{10,18},{12,20},{14,22},{16,8},... | collective-permute-start | bytes 442376 | tf_op jit(solution)/shard_map/ppermute | solution.py:586
  407.4 3.4 collective-permute-start.20
  431.4 37.1 %collective-permute-start.21 = (bf16[768,768]{1,0:T(8,128)(2,1)}, bf16[768,768]{1,0:T(8,128)(2,1)}, u32[]{:S(2)}, u32[]{:S(2)}) collective-permute-start(bf16[768,768]{1,0:T(8,128)(2,1)} %get-tuple-element.339), channel_id=1, source_target_pairs={{0,2},{2,0},{4,6},{6,4},{8,10},{10,8},{12,14},{14,12},{16,18},{18,... | collective-permute-start | bytes 3538952 | tf_op jit(solution)/shard_map/ppermute | solution.py:586
  432.9 35.7 %collective-permute-start.22 = (bf16[768,768]{1,0:T(8,128)(2,1)}, bf16[768,768]{1,0:T(8,128)(2,1)}, u32[]{:S(2)}, u32[]{:S(2)}) collective-permute-start(bf16[768,768]{1,0:T(8,128)(2,1)} %get-tuple-element.340), channel_id=1, source_target_pairs={{0,4},{2,6},{4,0},{6,2},{8,12},{10,14},{12,8},{14,10},{16,20},{18,... | collective-permute-start | bytes 3538952 | tf_op jit(solution)/shard_map/ppermute | solution.py:586
  435.2 31.3 %collective-permute-start.23 = (bf16[96,768]{1,0:T(8,128)(2,1)}, bf16[96,768]{1,0:T(8,128)(2,1)S(1)}, u32[]{:S(2)}, u32[]{:S(2)}) collective-permute-start(bf16[96,768]{1,0:T(8,128)(2,1)} %copy-done.127), channel_id=1, source_target_pairs={{0,8},{2,10},{4,12},{6,14},{8,0},{10,2},{12,4},{14,6},{16,24},{18,... | collective-permute-start | bytes 442376 | tf_op jit(solution)/shard_map/ppermute | solution.py:586
  435.2 32.0 %collective-permute-start.24 = (bf16[96,768]{1,0:T(8,128)(2,1)}, bf16[96,768]{1,0:T(8,128)(2,1)S(1)}, u32[]{:S(2)}, u32[]{:S(2)}) collective-permute-start(bf16[96,768]{1,0:T(8,128)(2,1)} %copy-done.126), channel_id=1, source_target_pairs={{0,16},{2,18},{4,20},{6,22},{8,24},{10,26},{12,28},{14,30},{16,0},... | collective-permute-start | bytes 442376 | tf_op jit(solution)/shard_map/ppermute | solution.py:586
  437.1 30.7 %collective-permute-start.25 = (bf16[96,768]{1,0:T(8,128)(2,1)}, bf16[96,768]{1,0:T(8,128)(2,1)S(1)}, u32[]{:S(2)}, u32[]{:S(2)}) collective-permute-start(bf16[96,768]{1,0:T(8,128)(2,1)} %copy-done.125), channel_id=1, source_target_pairs={{0,24},{2,26},{4,28},{6,30},{8,16},{10,18},{12,20},{14,22},{16,8},... | collective-permute-start | bytes 442376 | tf_op jit(solution)/shard_map/ppermute | solution.py:586
  468.5 4.8 collective-permute-start.26
  468.5 4.8 collective-permute-start.27
  469.8 2.2 collective-permute-start.29
  470.6 2.8 collective-permute-start.28
  494.4 48.8 %copy-start.74 = (f32[1,2,48,768]{3,2,1,0:T(8,128)}, f32[1,2,48,768]{3,2,1,0:T(8,128)S(1)}, u32[]{:S(2)}) copy-start(f32[1,2,48,768]{3,2,1,0:T(8,128)S(1)} %get-tuple-element.430.refs_4_) | copy-start | bytes 884740
  494.4 25.4 %collective-permute-start.30 = (bf16[640,768]{1,0:T(8,128)(2,1)S(1)}, bf16[640,768]{1,0:T(8,128)(2,1)S(1)}, u32[]{:S(2)}, u32[]{:S(2)}) collective-permute-start(bf16[640,768]{1,0:T(8,128)(2,1)S(1)} %get-tuple-element.385), channel_id=1, source_target_pairs={{0,2},{2,0},{4,6},{6,4},{8,10},{10,8},{12,14},{14,12},{16,18},{18,... | collective-permute-start | bytes 2949128 | tf_op jit(solution)/shard_map/ppermute | solution.py:586
  495.8 24.0 %collective-permute-start.31 = (bf16[576,768]{1,0:T(8,128)(2,1)S(1)}, bf16[576,768]{1,0:T(8,128)(2,1)S(1)}, u32[]{:S(2)}, u32[]{:S(2)}) collective-permute-start(bf16[576,768]{1,0:T(8,128)(2,1)S(1)} %get-tuple-element.386), channel_id=1, source_target_pairs={{0,4},{2,6},{4,0},{6,2},{8,12},{10,14},{12,8},{14,10},{16,20},{18,... | collective-permute-start | bytes 2654216 | tf_op jit(solution)/shard_map/ppermute | solution.py:586
  496.4 13.9 %collective-permute-start.32 = (bf16[192,768]{1,0:T(8,128)(2,1)S(1)}, bf16[192,768]{1,0:T(8,128)(2,1)S(1)}, u32[]{:S(2)}, u32[]{:S(2)}) collective-permute-start(bf16[192,768]{1,0:T(8,128)(2,1)S(1)} %get-tuple-element.387), channel_id=1, source_target_pairs={{0,8},{2,10},{4,12},{6,14},{8,0},{10,2},{12,4},{14,6},{16,24},{18,... | collective-permute-start | bytes 884744 | tf_op jit(solution)/shard_map/ppermute | solution.py:586
  496.4 23.5 %collective-permute-start.33 = (bf16[192,768]{1,0:T(8,128)(2,1)S(1)}, bf16[192,768]{1,0:T(8,128)(2,1)S(1)}, u32[]{:S(2)}, u32[]{:S(2)}) collective-permute-start(bf16[192,768]{1,0:T(8,128)(2,1)S(1)} %get-tuple-element.388), channel_id=1, source_target_pairs={{0,16},{2,18},{4,20},{6,22},{8,24},{10,26},{12,28},{14,30},{16,0},... | collective-permute-start | bytes 884744 | tf_op jit(solution)/shard_map/ppermute | solution.py:586
  498.3 21.5 %collective-permute-start.34 = (bf16[192,768]{1,0:T(8,128)(2,1)S(1)}, bf16[192,768]{1,0:T(8,128)(2,1)S(1)}, u32[]{:S(2)}, u32[]{:S(2)}) collective-permute-start(bf16[192,768]{1,0:T(8,128)(2,1)S(1)} %get-tuple-element.389), channel_id=1, source_target_pairs={{0,24},{2,26},{4,28},{6,30},{8,16},{10,18},{12,20},{14,22},{16,8},... | collective-permute-start | bytes 884744 | tf_op jit(solution)/shard_map/ppermute | solution.py:586
  523.4 19.9 %collective-permute-start.36 = (bf16[256,768]{1,0:T(8,128)(2,1)S(1)}, bf16[256,768]{1,0:T(8,128)(2,1)S(1)}, u32[]{:S(2)}, u32[]{:S(2)}) collective-permute-start(bf16[256,768]{1,0:T(8,128)(2,1)S(1)} %get-tuple-element.408), channel_id=1, source_target_pairs={{0,4},{2,6},{4,0},{6,2},{8,12},{10,14},{12,8},{14,10},{16,20},{18,... | collective-permute-start | bytes 1179656 | tf_op jit(solution)/shard_map/ppermute | solution.py:586
  524.9 8.8 %collective-permute-start.37 = (bf16[96,768]{1,0:T(8,128)(2,1)S(1)}, bf16[96,768]{1,0:T(8,128)(2,1)S(1)}, u32[]{:S(2)}, u32[]{:S(2)}) collective-permute-start(bf16[96,768]{1,0:T(8,128)(2,1)S(1)} %get-tuple-element.409), channel_id=1, source_target_pairs={{0,8},{2,10},{4,12},{6,14},{8,0},{10,2},{12,4},{14,6},{16,24},{18,... | collective-permute-start | bytes 442376 | tf_op jit(solution)/shard_map/ppermute | solution.py:586
  530.4 12.9 %collective-permute-start.35 = (bf16[192,768]{1,0:T(8,128)(2,1)S(1)}, bf16[192,768]{1,0:T(8,128)(2,1)S(1)}, u32[]{:S(2)}, u32[]{:S(2)}) collective-permute-start(bf16[192,768]{1,0:T(8,128)(2,1)S(1)} %get-tuple-element.407), channel_id=1, source_target_pairs={{0,2},{2,0},{4,6},{6,4},{8,10},{10,8},{12,14},{14,12},{16,18},{18,... | collective-permute-start | bytes 884744 | tf_op jit(solution)/shard_map/ppermute | solution.py:586
  531.0 12.2 %collective-permute-start.38 = (bf16[96,768]{1,0:T(8,128)(2,1)S(1)}, bf16[96,768]{1,0:T(8,128)(2,1)S(1)}, u32[]{:S(2)}, u32[]{:S(2)}) collective-permute-start(bf16[96,768]{1,0:T(8,128)(2,1)S(1)} %get-tuple-element.410), channel_id=1, source_target_pairs={{0,16},{2,18},{4,20},{6,22},{8,24},{10,26},{12,28},{14,30},{16,0},... | collective-permute-start | bytes 442376 | tf_op jit(solution)/shard_map/ppermute | solution.py:586
  531.3 18.2 %collective-permute-start.43 = (f32[1,2,48,768]{3,2,1,0:T(8,128)S(1)}, f32[1,2,48,768]{3,2,1,0:T(8,128)S(1)}, u32[]{:S(2)}, u32[]{:S(2)}) collective-permute-start(f32[1,2,48,768]{3,2,1,0:T(8,128)S(1)} %copy-done.72), channel_id=1, source_target_pairs={{0,1},{1,0},{2,3},{3,2},{4,5},{5,4},{6,7},{7,6},{8,9},{9,8},{10,11... | collective-permute-start | bytes 884744 | tf_op jit(solution)/shard_map/ppermute | solution.py:582
  533.7 9.5 %collective-permute-start.39 = (bf16[96,768]{1,0:T(8,128)(2,1)S(1)}, bf16[96,768]{1,0:T(8,128)(2,1)S(1)}, u32[]{:S(2)}, u32[]{:S(2)}) collective-permute-start(bf16[96,768]{1,0:T(8,128)(2,1)S(1)} %get-tuple-element.411), channel_id=1, source_target_pairs={{0,24},{2,26},{4,28},{6,30},{8,16},{10,18},{12,20},{14,22},{16,8},... | collective-permute-start | bytes 442376 | tf_op jit(solution)/shard_map/ppermute | solution.py:586
  543.2 8.4 %collective-permute-start.44 = (f32[1,2,48,768]{3,2,1,0:T(8,128)S(1)}, f32[1,2,48,768]{3,2,1,0:T(8,128)S(1)}, u32[]{:S(2)}, u32[]{:S(2)}) collective-permute-start(f32[1,2,48,768]{3,2,1,0:T(8,128)S(1)} %get-tuple-element.430.refs_4_), channel_id=1, source_target_pairs={{0,1},{1,0},{2,3},{3,2},{4,5},{5,4},{6,7},{7,6},{8,9},{9,8},{10,11... | collective-permute-start | bytes 884744 | tf_op jit(solution)/shard_map/ppermute | solution.py:582
  543.3 41.5 %copy-start.15 = (f32[2,48,3072]{2,1,0:T(8,128)S(1)}, f32[2,48,3072]{2,1,0:T(8,128)}, u32[]{:S(2)}) copy-start(f32[2,48,3072]{2,1,0:T(8,128)} %refs_19_.1) | copy-start | bytes 3538948
  543.3 41.5 %copy-start.17 = (f32[2,192,768]{2,1,0:T(8,128)S(1)}, f32[2,192,768]{2,1,0:T(8,128)}, u32[]{:S(2)}) copy-start(f32[2,192,768]{2,1,0:T(8,128)} %refs_22_.1) | copy-start | bytes 3538948
  543.3 41.5 %copy-start.19 = (f32[2,48,2304]{2,1,0:T(8,128)S(1)}, f32[2,48,2304]{2,1,0:T(8,128)}, u32[]{:S(2)}) copy-start(f32[2,48,2304]{2,1,0:T(8,128)} %refs_13_.1) | copy-start | bytes 2654212
  544.8 9.2 %collective-permute-start.40 = (bf16[112,768]{1,0:T(8,128)(2,1)S(1)}, bf16[112,768]{1,0:T(8,128)(2,1)S(1)}, u32[]{:S(2)}, u32[]{:S(2)}) collective-permute-start(bf16[112,768]{1,0:T(8,128)(2,1)S(1)} %get-tuple-element.426), channel_id=1, source_target_pairs={{0,8},{2,10},{4,12},{6,14},{8,0},{10,2},{12,4},{14,6},{16,24},{18,... | collective-permute-start | bytes 516104 | tf_op jit(solution)/shard_map/ppermute | solution.py:586
  547.2 14.9 %collective-permute-start.41 = (bf16[112,768]{1,0:T(8,128)(2,1)S(1)}, bf16[112,768]{1,0:T(8,128)(2,1)S(1)}, u32[]{:S(2)}, u32[]{:S(2)}) collective-permute-start(bf16[112,768]{1,0:T(8,128)(2,1)S(1)} %get-tuple-element.427), channel_id=1, source_target_pairs={{0,16},{2,18},{4,20},{6,22},{8,24},{10,26},{12,28},{14,30},{16,0},... | collective-permute-start | bytes 516104 | tf_op jit(solution)/shard_map/ppermute | solution.py:586
  547.4 14.6 %collective-permute-start.42 = (bf16[112,768]{1,0:T(8,128)(2,1)S(1)}, bf16[112,768]{1,0:T(8,128)(2,1)S(1)}, u32[]{:S(2)}, u32[]{:S(2)}) collective-permute-start(bf16[112,768]{1,0:T(8,128)(2,1)S(1)} %get-tuple-element.428), channel_id=1, source_target_pairs={{0,24},{2,26},{4,28},{6,30},{8,16},{10,18},{12,20},{14,22},{16,8},... | collective-permute-start | bytes 516104 | tf_op jit(solution)/shard_map/ppermute | solution.py:586
  550.2 34.5 %collective-permute-start.53 = (f32[2,2,48,768]{3,2,1,0:T(8,128)}, f32[2,2,48,768]{3,2,1,0:T(8,128)}, u32[]{:S(2)}, u32[]{:S(2)}) collective-permute-start(f32[2,2,48,768]{3,2,1,0:T(8,128)} %get-tuple-element.437.refs_5_), channel_id=1, source_target_pairs={{0,1},{1,0},{2,3},{3,2},{4,5},{5,4},{6,7},{7,6},{8,9},{9,8},{10,11... | collective-permute-start | bytes 1769480 | tf_op jit(solution)/shard_map/ppermute | solution.py:582
  564.6 1.1 collective-permute-start.45
  565.7 3.5 collective-permute-start.46
  566.6 3.5 collective-permute-start.47
  567.7 4.4 collective-permute-start.48
  572.1 9.1 %collective-permute-start.49 = (f32[1,128]{1,0:T(1,128)S(1)}, f32[1,128]{1,0:T(1,128)}, u32[]{:S(2)}, u32[]{:S(2)}) collective-permute-start(f32[1,128]{1,0:T(1,128)S(1)} %add_add_fusion.1), channel_id=1, source_target_pairs={{0,8},{2,10},{4,12},{6,14},{8,0},{10,2},{12,4},{14,6},{16,24},{18,... | collective-permute-start | bytes 1544 | tf_op jit(solution)/shard_map/ppermute | solution.py:586
  576.0 5.8 collective-permute-start.50
  578.0 5.4 collective-permute-start.51
  581.2 3.5 collective-permute-start.54
  581.3 3.5 collective-permute-start.55
  581.8 3.0 collective-permute-start.52
  (138 other events, 688.9 us)
Sparse Core Ops, SparseCore 0:
  15.4 174.2 all-gather.1

commit v10 on v9

--- a/solution.py
+++ b/solution.py
@@ -74,7 +74,7 @@
         for n in lead:
             size *= n
         total += size * (-(-rows // 16) * 16) * (-(-lanes // 128) * 128)
-    return min(total, 60 << 20)
+    return min(max(total, 50 << 20), 60 << 20)
 
 
 LOW, FULL = jnp.bfloat16, jnp.float32

time: 637 us -> 592 us (0.929)
  local copies, waits for them, and re-layouts: 114 us -> 47.7 us
  Pallas kernels: 189 us -> 207 us
  waiting for transfers between devices: 238 us -> 245 us
    unnamed x296 -> x170, local copies, waits for them, and re-layouts: 105 us -> 43.4 us
    pallas_call x18, Pallas kernels: 189 us -> 207 us  [call(): pl.pallas_call(body, out_shape=[jax.ShapeDtypeStruct(s, t) for s, t in ou...]
  transfers between devices with their start and end apart: 57 -> 57, of which waited for: 20 -> 24; matrix products, arithmetic and copies ran while one was open for 4% -> 3% of each run, Pallas kernels for 13% -> 17%
where the time goes in v10:
time: 592 us; the launch traced here: 582 us
  waiting for transfers between devices  245 us (41%)
  Pallas kernels  207 us (35%)
  starting transfers between devices  51 us (9%)
  local copies, waits for them, and re-layouts  47.7 us (8%)
  between operations  15.1 us (3%)
  other arithmetic  11.7 us (2%)
    pallas_call x18, Pallas kernels, call(): pl.pallas_call(body, out_shape=[jax.ShapeDtypeStruct(s, t) for s, t in ou...  207 us
    all_gather x1, waiting for transfers between devices, body(): weights = lax.all_gather(weights, ('fsdp', 'dp'), axis=0, tiled=True)  172 us
    ppermute x33, waiting for transfers between devices, across(): return lax.ppermute(value, 'fsdp', [(i, i ^ mask) for i in range(size)])  55.2 us
    ppermute x33, starting transfers between devices, across(): return lax.ppermute(value, 'fsdp', [(i, i ^ mask) for i in range(size)])  46.5 us
    unnamed x170, local copies, waits for them, and re-layouts  43.4 us
    ppermute x23, waiting for transfers between devices, swap_cores(): return lax.ppermute(value, 'dp', [(0, 1), (1, 0)])  17.2 us
  transfers between devices with their start and end apart: 57, of which 24 were waited for; matrix products, arithmetic and copies ran while one was open for 3% of the time, Pallas kernels for 17%

profile of v10, /device:TPU:0, one launch (start us, length us, event | category | flops | bytes accessed | tf_op | source)
XLA Modules:
  0.0 582.3 jit_solution(6749231055598218206)
XLA Ops:
  9.0 1.3 copy-done.3
  12.4 2.4 shard_map.364
  17.1 172.2 %all-gather.2.cloned.1.call-done = bf16[1536,9344]{1,0:T(8,128)(2,1)} async-done(((bf16[48,9344]{1,0:T(8,128)(2,1)}), bf16[1536,9344]{1,0:T(8,128)(2,1)}) %all-gather.2.cloned.1.call-update) | async-done | bytes 28704784 | tf_op jit(solution)/shard_map/all_gather | solution.py:980
  190.4 1.6 fusion.3.refs_0_.refs_10_
  192.0 13.8 %shard_map.365 = (f32[512,768]{1,0:T(8,128)}, bf16[512,768]{1,0:T(8,128)(2,1)S(1)}, bf16[512,768]{1,0:T(8,128)(2,1)S(1)}, bf16[512,768]{1,0:T(8,128)(2,1)S(1)}, ...) custom-call(s32[4]{0:T(128)S(1)} %pad_add_fusion.scalars, f32[512,768]{1,0:T(8,128)} %fusion.3.refs_0_.refs_10_, ...), custom_call_target="tpu_custom_call" | custom-call | flops 3221225472 | bytes 30812160 | tf_op jit(solution)/shard_map/pallas_call | solution.py:122
  209.2 1.4 copy-done
  210.6 10.7 %shard_map.366 = (f32[512,768]{1,0:T(8,128)S(1)}, bf16[5,512,768]{2,1,0:T(8,128)(2,1)}, f32[4,512,768]{2,1,0:T(8,128)}) custom-call(s32[4]{0:T(128)S(1)} %pad_add_fusion.scalars, f32[512,768]{1,0:T(8,128)S(1)} %copy-done, f32[2,768]{1,0:T(2,128)S(1)} %get-tuple-element.518.refs_1_.refs_3_, bf16[16,2,48,9344]{3,2,1,0:T(8,128)(2,1)} %bitcast.29), custom_call_target="tpu_custom_call" | custom-call | flops 4831838208 | bytes 30283776 | tf_op jit(solution)/shard_map/pallas_call | solution.py:122
  222.4 14.4 %shard_map.367 = (f32[512,768]{1,0:T(8,128)}, bf16[512,768]{1,0:T(8,128)(2,1)S(1)}, bf16[512,768]{1,0:T(8,128)(2,1)S(1)}, bf16[512,768]{1,0:T(8,128)(2,1)S(1)}, ...) custom-call(s32[4]{0:T(128)S(1)} %pad_add_fusion.scalars, f32[512,768]{1,0:T(8,128)} %copy-done.1, ...), custom_call_target="tpu_custom_call" | custom-call | flops 3221225472 | bytes 30812160 | tf_op jit(solution)/shard_map/pallas_call | solution.py:122
  238.5 2.0 copy-done.2
  240.4 10.7 %shard_map.368 = (f32[512,768]{1,0:T(8,128)S(1)}, bf16[5,512,768]{2,1,0:T(8,128)(2,1)}, f32[4,512,768]{2,1,0:T(8,128)}) custom-call(s32[4]{0:T(128)S(1)} %pad_add_fusion.scalars, f32[512,768]{1,0:T(8,128)S(1)} %copy-done.2, f32[2,768]{1,0:T(2,128)S(1)} %get-tuple-element.516.refs_1_.refs_3_, bf16[16,2,48,9344]{3,2,1,0:T(8,128)(2,1)} %bitcast.31), custom_call_target="tpu_custom_call" | custom-call | flops 4831838208 | bytes 30283776 | tf_op jit(solution)/shard_map/pallas_call | solution.py:122
  252.3 1.6 fusion.18
  256.8 1.3 multiply_reduce_fusion.4
  259.1 2.3 multiply_reduce_fusion
  261.5 1.6 fusion.14
  265.0 8.5 %shard_map.369 = (bf16[384,768]{1,0:T(8,128)(2,1)S(1)}, bf16[384,768]{1,0:T(8,128)(2,1)S(1)}, f32[1,2,384,768]{3,2,1,0:T(8,128)}) custom-call(s32[4]{0:T(128)S(1)} %pad_add_fusion.scalars, bf16[5,512,768]{2,1,0:T(8,128)(2,1)} %get-tuple-element.247.refs_0_, bf16[512,384]{1,0:T(8,128)(2,1)S(1)} %get-tuple-element.515.refs_1_, ...), custom_call_target="tpu_custom_call" | custom-call | flops 2415919104 | bytes 8650752 | tf_op jit(solution)/shard_map/pallas_call | solution.py:122
  273.6 1.4 collective-permute-start.2
  275.8 1.3 collective-permute-done.6.refs_11_
  277.3 17.8 %shard_map.370 = (f32[512,768]{1,0:T(8,128)S(1)}, f32[2,768]{1,0:T(2,128)S(1)}, bf16[2,512,768]{2,1,0:T(8,128)(2,1)S(1)}, bf16[2,512,768]{2,1,0:T(8,128)(2,1)}) custom-call(s32[4]{0:T(128)S(1)} %pad_add_fusion.scalars, bf16[512,768]{1,0:T(8,128)(2,1)S(1)} %get-tuple-element.257.refs_0_, f32[512,768]{1,0:T(8,128)} %get-tuple-element.258.refs_1_, ...), custom_call_target="tpu_custom_call" | custom-call | flops 4831838208 | bytes 38934528 | tf_op jit(solution)/shard_map/pallas_call | solution.py:122
  295.1 1.2 copy-done.6
  299.6 3.5 collective-permute-done.7.refs_3_
  304.2 10.1 %shard_map.371 = (bf16[576,768]{1,0:T(8,128)(2,1)}, bf16[576,768]{1,0:T(8,128)(2,1)}, f32[1,2,384,768]{3,2,1,0:T(8,128)}, f32[1,2,192,768]{3,2,1,0:T(8,128)}) custom-call(s32[4]{0:T(128)S(1)} %pad_add_fusion.scalars, bf16[5,512,768]{2,1,0:T(8,128)(2,1)} %get-tuple-element.247.refs_0_, bf16[2,512,768]{2,1,0:T(8,128)(2,1)} %copy-done.7, ...), custom_call_target="tpu_custom_call" | custom-call | flops 2415919104 | bytes 14548992 | tf_op jit(solution)/shard_map/pallas_call | solution.py:122
  314.3 1.5 collective-permute-start.8
  318.8 21.5 %shard_map.372 = (f32[512,768]{1,0:T(8,128)}, bf16[512,768]{1,0:T(8,128)(2,1)S(1)}, bf16[512,384]{1,0:T(8,128)(2,1)S(1)}, bf16[512,384]{1,0:T(8,128)(2,1)S(1)}, ...) custom-call(s32[4]{0:T(128)S(1)} %pad_add_fusion.scalars, f32[512,768]{1,0:T(8,128)} %copy-done.6, ...), custom_call_target="tpu_custom_call" | custom-call | flops 4429185024 | bytes 34768896 | tf_op jit(solution)/shard_map/pallas_call | solution.py:122
  340.9 3.1 collective-permute-done.14.refs_7_
  345.8 16.6 %shard_map.373 = (bf16[960,768]{1,0:T(8,128)(2,1)}, bf16[960,768]{1,0:T(8,128)(2,1)}, f32[2,2,384,768]{3,2,1,0:T(8,128)}, f32[1,2,192,768]{3,2,1,0:T(8,128)}, f3...) custom-call(s32[4]{0:T(128)S(1)} %pad_add_fusion.scalars, ...), custom_call_target="tpu_custom_call" | custom-call | flops 4831838208 | bytes 20250624 | tf_op jit(solution)/shard_map/pallas_call | solution.py:122
  362.4 1.4 collective-permute-start.15
  364.4 1.9 collective-permute-start.18
  366.4 2.4 collective-permute-start.19
  368.8 17.4 %shard_map.374 = (f32[512,768]{1,0:T(8,128)S(1)}, f32[2,768]{1,0:T(2,128)S(1)}, bf16[2,512,768]{2,1,0:T(8,128)(2,1)S(1)}, bf16[2,512,768]{2,1,0:T(8,128)(2,1)}) custom-call(s32[4]{0:T(128)S(1)} %pad_add_fusion.scalars, bf16[512,768]{1,0:T(8,128)(2,1)S(1)} %get-tuple-element.311.refs_0_, f32[512,768]{1,0:T(8,128)} %get-tuple-element.312.refs_1_, ...), custom_call_target="tpu_custom_call" | custom-call | flops 4831838208 | bytes 38934528 | tf_op jit(solution)/shard_map/pallas_call | solution.py:122
  388.5 8.4 %collective-permute-done.15.refs_6_ = bf16[960,768]{1,0:T(8,128)(2,1)S(1)} collective-permute-done((bf16[960,768]{1,0:T(8,128)(2,1)}, bf16[960,768]{1,0:T(8,128)(2,1)S(1)}, u32[]{:S(2)}, u32[]{:S(2)}) %collective-permute-start.15) | collective-permute-done | bytes 1474592 | tf_op jit(solution)/shard_map/ppermute | solution.py:586
  398.1 3.6 collective-permute-done.20.refs_3_
  401.7 1.2 copy-done.64
  402.9 13.0 %shard_map.375 = (bf16[768,768]{1,0:T(8,128)(2,1)}, bf16[768,768]{1,0:T(8,128)(2,1)}, f32[1,2,384,768]{3,2,1,0:T(8,128)}, f32[2,2,192,768]{3,2,1,0:T(8,128)}, f3...) custom-call(s32[4]{0:T(128)S(1)} %pad_add_fusion.scalars, ...), custom_call_target="tpu_custom_call" | custom-call | flops 2415919104 | bytes 20597760 | tf_op jit(solution)/shard_map/pallas_call | solution.py:122
  420.6 1.5 collective-permute-start.22
  422.2 1.9 collective-permute-start.24
  424.2 2.4 collective-permute-start.25
  427.8 21.3 %shard_map.376 = (f32[512,768]{1,0:T(8,128)}, bf16[512,768]{1,0:T(8,128)(2,1)S(1)}, bf16[512,384]{1,0:T(8,128)(2,1)}, bf16[512,384]{1,0:T(8,128)(2,1)}, f32[2,76...) custom-call(s32[4]{0:T(128)S(1)} %pad_add_fusion.scalars, f32[512,768]{1,0:T(8,128)} %copy-done.5, ...), custom_call_target="tpu_custom_call" | custom-call | flops 4429185024 | bytes 34768896 | tf_op jit(solution)/shard_map/pallas_call | solution.py:122
  453.6 2.3 collective-permute-done.29.refs_15_
  462.9 12.0 %shard_map.377 = (bf16[640,768]{1,0:T(8,128)(2,1)}, bf16[576,768]{1,0:T(8,128)(2,1)}, f32[1,2,384,768]{3,2,1,0:T(8,128)}, f32[384,128]{1,0:T(8,128)S(1)}, f32[1,...) custom-call(s32[4]{0:T(128)S(1)} %pad_add_fusion.scalars, ...), custom_call_target="tpu_custom_call" | custom-call | flops 2415919104 | bytes 17841152 | tf_op jit(solution)/shard_map/pallas_call | solution.py:122
  475.5 1.4 collective-permute-start.31
  476.9 1.9 collective-permute-start.33
  478.8 2.4 collective-permute-start.34
  481.3 9.6 %collective-permute-done.32.refs_6_ = bf16[192,768]{1,0:T(8,128)(2,1)S(1)} collective-permute-done((bf16[192,768]{1,0:T(8,128)(2,1)S(1)}, bf16[192,768]{1,0:T(8,128)(2,1)S(1)}, u32[]{:S(2)}, u32[]{:S(2)}) %collective-permute-start.32) | collective-permute-done | bytes 294944 | tf_op jit(solution)/shard_map/ppermute | solution.py:586
  490.9 9.5 %collective-permute-done.33.refs_7_ = bf16[192,768]{1,0:T(8,128)(2,1)S(1)} collective-permute-done((bf16[192,768]{1,0:T(8,128)(2,1)S(1)}, bf16[192,768]{1,0:T(8,128)(2,1)S(1)}, u32[]{:S(2)}, u32[]{:S(2)}) %collective-permute-start.33) | collective-permute-done | bytes 294944 | tf_op jit(solution)/shard_map/ppermute | solution.py:586
  501.6 4.0 shard_map.378
  506.2 5.6 collective-permute-start.37
  511.7 1.4 collective-permute-start.35
  513.5 1.6 collective-permute-done.37.refs_5_
  515.1 1.9 collective-permute-start.39
  517.0 8.3 %collective-permute-done.38.refs_6_ = bf16[96,768]{1,0:T(8,128)(2,1)S(1)} collective-permute-done((bf16[96,768]{1,0:T(8,128)(2,1)S(1)}, bf16[96,768]{1,0:T(8,128)(2,1)S(1)}, u32[]{:S(2)}, u32[]{:S(2)}) %collective-permute-start.38) | collective-permute-done | bytes 147488 | tf_op jit(solution)/shard_map/ppermute | solution.py:586
  525.4 1.3 copy-done.11
  527.5 2.2 collective-permute-start.40
  530.2 1.9 collective-permute-start.42
  532.2 1.4 fusion.8.refs_6_
  533.5 4.0 collective-permute-done.40.refs_2_
  537.5 6.9 %collective-permute-done.41.refs_3_ = bf16[112,768]{1,0:T(8,128)(2,1)S(1)} collective-permute-done((bf16[112,768]{1,0:T(8,128)(2,1)S(1)}, bf16[112,768]{1,0:T(8,128)(2,1)S(1)}, u32[]{:S(2)}, u32[]{:S(2)}) %collective-permute-start.41) | collective-permute-done | bytes 172064 | tf_op jit(solution)/shard_map/ppermute | solution.py:586
  544.4 1.2 shard_map.380
  548.8 1.5 collective-permute-start.48
  551.5 1.8 collective-permute-done.48
  553.2 2.6 collective-permute-start.49
  556.5 2.0 collective-permute-start.51
  559.2 1.2 collective-permute-done.50
  560.4 1.5 collective-permute-done.51
  562.6 10.6 %shard_map.381 = (f32[1,1]{1,0:T(1,128)}, f32[2,48,2304]{2,1,0:T(8,128)}, f32[2,48,2304]{2,1,0:T(8,128)}, f32[2,48,2304]{2,1,0:T(8,128)}, f32[2,48,768]{2,1,0:T(...) custom-call(s32[4]{0:T(128)S(1)} %pad_add_fusion.scalars, ...), custom_call_target="tpu_custom_call" | custom-call | flops 53314560 | bytes 14251520 | tf_op jit(solution)/shard_map/pallas_call | solution.py:122
  (289 shorter events, 64.9 us)
Async XLA Ops:
  7.2 182.1 %all-gather.2.cloned.1.call-start = ((), (), s32[]{:S(2)}) async-start(), calls=%async_computation | async-start | bytes 29601792 | tf_op jit(solution)/shard_map/all_gather | solution.py:980
  17.1 188.8 %copy-start.77 = (s32[512]{0:T(512)}, s32[512]{0:T(512)S(1)}, u32[]{:S(2)}) copy-start(s32[512]{0:T(512)S(1)} %get-tuple-element.521) | copy-start | bytes 6148
  190.4 48.0 %copy-start.46 = (f32[2,768]{1,0:T(2,128)}, f32[2,768]{1,0:T(2,128)S(1)}, u32[]{:S(2)}) copy-start(f32[2,768]{1,0:T(2,128)S(1)} %get-tuple-element.516.refs_1_.refs_3_) | copy-start | bytes 18436
  251.2 12.9 %collective-permute-start = (bf16[5,512,768]{2,1,0:T(8,128)(2,1)}, bf16[5,512,768]{2,1,0:T(8,128)(2,1)}, u32[]{:S(2)}, u32[]{:S(2)}) collective-permute-start(bf16[5,512,768]{2,1,0:T(8,128)(2,1)} %get-tuple-element.247.refs_0_), channel_id=1, source_target_pairs={{0,1},{1,0},{2,3},{3,2},{4,5},{5,4},{6,7},{7,6},{8,9},{9,8},{10,11... | collective-permute-start | bytes 11796488 | tf_op jit(solution)/shard_map/ppermute | solution.py:582
  263.2 1.8 collective-permute-start.1
  263.5 76.8 %collective-permute-start.10 = (bf16[5,512,768]{2,1,0:T(8,128)(2,1)}, bf16[5,512,768]{2,1,0:T(8,128)(2,1)}, u32[]{:S(2)}, u32[]{:S(2)}) collective-permute-start(bf16[5,512,768]{2,1,0:T(8,128)(2,1)} %get-tuple-element.243.refs_4_.refs_0_), channel_id=1, source_target_pairs={{0,1},{1,0},{2,3},{3,2},{4,5},{5,4},{6,7},{7,6},{8,9},{9,8},{10,11... | collective-permute-start | bytes 11796488 | tf_op jit(solution)/shard_map/ppermute | solution.py:582
  263.8 34.9 %collective-permute-start.4 = (bf16[512,768]{1,0:T(8,128)(2,1)S(1)}, bf16[512,768]{1,0:T(8,128)(2,1)S(1)}, u32[]{:S(2)}, u32[]{:S(2)}) collective-permute-start(bf16[512,768]{1,0:T(8,128)(2,1)S(1)} %add_convert_fusion.refs_4_), channel_id=1, source_target_pairs={{0,1},{1,0},{2,3},{3,2},{4,5},{5,4},{6,7},{7,6},{8,9},{9,8},{10,11... | collective-permute-start | bytes 2359304 | tf_op jit(solution)/shard_map/ppermute | solution.py:582
  273.6 25.1 %collective-permute-start.2 = (bf16[384,768]{1,0:T(8,128)(2,1)S(1)}, bf16[384,768]{1,0:T(8,128)(2,1)S(1)}, u32[]{:S(2)}, u32[]{:S(2)}) collective-permute-start(bf16[384,768]{1,0:T(8,128)(2,1)S(1)} %get-tuple-element.255), channel_id=1, source_target_pairs={{0,2},{2,0},{4,6},{6,4},{8,10},{10,8},{12,14},{14,12},{16,18},{18,... | collective-permute-start | bytes 1769480 | tf_op jit(solution)/shard_map/ppermute | solution.py:586
  275.0 23.7 %collective-permute-start.3 = (bf16[384,768]{1,0:T(8,128)(2,1)S(1)}, bf16[384,768]{1,0:T(8,128)(2,1)S(1)}, u32[]{:S(2)}, u32[]{:S(2)}) collective-permute-start(bf16[384,768]{1,0:T(8,128)(2,1)S(1)} %get-tuple-element.256), channel_id=1, source_target_pairs={{0,4},{2,6},{4,0},{6,2},{8,12},{10,14},{12,8},{14,10},{16,20},{18,... | collective-permute-start | bytes 1769480 | tf_op jit(solution)/shard_map/ppermute | solution.py:586
  275.7 1.4 collective-permute-start.6
  277.1 20.9 %collective-permute-start.5 = (bf16[512,128]{1,0:T(8,128)(2,1)S(1)}, bf16[512,128]{1,0:T(8,128)(2,1)S(1)}, u32[]{:S(2)}, u32[]{:S(2)}) collective-permute-start(bf16[512,128]{1,0:T(8,128)(2,1)S(1)} %pad.18.refs_5_), channel_id=1, source_target_pairs={{0,1},{1,0},{2,3},{3,2},{4,5},{5,4},{6,7},{7,6},{8,9},{9,8},{10,11... | collective-permute-start | bytes 393224 | tf_op jit(solution)/shard_map/ppermute | solution.py:582
  298.7 4.4 collective-permute-start.7
  299.1 41.2 %collective-permute-start.12 = (bf16[2,512,768]{2,1,0:T(8,128)(2,1)}, bf16[2,512,768]{2,1,0:T(8,128)(2,1)}, u32[]{:S(2)}, u32[]{:S(2)}) collective-permute-start(bf16[2,512,768]{2,1,0:T(8,128)(2,1)} %get-tuple-element.245.refs_0_), channel_id=1, source_target_pairs={{0,1},{1,0},{2,3},{3,2},{4,5},{5,4},{6,7},{7,6},{8,9},{9,8},{10,11... | collective-permute-start | bytes 4718600 | tf_op jit(solution)/shard_map/ppermute | solution.py:582
  299.3 41.1 %collective-permute-start.11 = (bf16[2,512,768]{2,1,0:T(8,128)(2,1)}, bf16[2,512,768]{2,1,0:T(8,128)(2,1)}, u32[]{:S(2)}, u32[]{:S(2)}) collective-permute-start(bf16[2,512,768]{2,1,0:T(8,128)(2,1)} %get-tuple-element.241.refs_0_), channel_id=1, source_target_pairs={{0,1},{1,0},{2,3},{3,2},{4,5},{5,4},{6,7},{7,6},{8,9},{9,8},{10,11... | collective-permute-start | bytes 4718600 | tf_op jit(solution)/shard_map/ppermute | solution.py:582
  314.3 26.1 %collective-permute-start.8 = (bf16[576,768]{1,0:T(8,128)(2,1)}, bf16[576,768]{1,0:T(8,128)(2,1)S(1)}, u32[]{:S(2)}, u32[]{:S(2)}) collective-permute-start(bf16[576,768]{1,0:T(8,128)(2,1)} %get-tuple-element.273), channel_id=1, source_target_pairs={{0,2},{2,0},{4,6},{6,4},{8,10},{10,8},{12,14},{14,12},{16,18},{18,... | collective-permute-start | bytes 2654216 | tf_op jit(solution)/shard_map/ppermute | solution.py:586
  315.8 24.6 %collective-permute-start.9 = (bf16[576,768]{1,0:T(8,128)(2,1)}, bf16[576,768]{1,0:T(8,128)(2,1)}, u32[]{:S(2)}, u32[]{:S(2)}) collective-permute-start(bf16[576,768]{1,0:T(8,128)(2,1)} %get-tuple-element.274), channel_id=1, source_target_pairs={{0,4},{2,6},{4,0},{6,2},{8,12},{10,14},{12,8},{14,10},{16,20},{18,... | collective-permute-start | bytes 2654216 | tf_op jit(solution)/shard_map/ppermute | solution.py:586
  340.4 4.2 collective-permute-start.13
  340.4 3.6 collective-permute-start.14
  362.4 34.5 %collective-permute-start.15 = (bf16[960,768]{1,0:T(8,128)(2,1)}, bf16[960,768]{1,0:T(8,128)(2,1)S(1)}, u32[]{:S(2)}, u32[]{:S(2)}) collective-permute-start(bf16[960,768]{1,0:T(8,128)(2,1)} %get-tuple-element.306), channel_id=1, source_target_pairs={{0,2},{2,0},{4,6},{6,4},{8,10},{10,8},{12,14},{14,12},{16,18},{18,... | collective-permute-start | bytes 4423688 | tf_op jit(solution)/shard_map/ppermute | solution.py:586
  363.8 34.3 %collective-permute-start.16 = (bf16[960,768]{1,0:T(8,128)(2,1)}, bf16[960,768]{1,0:T(8,128)(2,1)S(1)}, u32[]{:S(2)}, u32[]{:S(2)}) collective-permute-start(bf16[960,768]{1,0:T(8,128)(2,1)} %get-tuple-element.307), channel_id=1, source_target_pairs={{0,4},{2,6},{4,0},{6,2},{8,12},{10,14},{12,8},{14,10},{16,20},{18,... | collective-permute-start | bytes 4423688 | tf_op jit(solution)/shard_map/ppermute | solution.py:586
  364.4 24.1 %collective-permute-start.17 = (bf16[96,768]{1,0:T(8,128)(2,1)S(1)}, bf16[96,768]{1,0:T(8,128)(2,1)S(1)}, u32[]{:S(2)}, u32[]{:S(2)}) collective-permute-start(bf16[96,768]{1,0:T(8,128)(2,1)S(1)} %get-tuple-element.308), channel_id=1, source_target_pairs={{0,8},{2,10},{4,12},{6,14},{8,0},{10,2},{12,4},{14,6},{16,24},{18,... | collective-permute-start | bytes 442376 | tf_op jit(solution)/shard_map/ppermute | solution.py:586
  364.4 24.1 %collective-permute-start.18 = (bf16[96,768]{1,0:T(8,128)(2,1)S(1)}, bf16[96,768]{1,0:T(8,128)(2,1)S(1)}, u32[]{:S(2)}, u32[]{:S(2)}) collective-permute-start(bf16[96,768]{1,0:T(8,128)(2,1)S(1)} %get-tuple-element.309), channel_id=1, source_target_pairs={{0,16},{2,18},{4,20},{6,22},{8,24},{10,26},{12,28},{14,30},{16,0},... | collective-permute-start | bytes 442376 | tf_op jit(solution)/shard_map/ppermute | solution.py:586
  366.4 22.1 %collective-permute-start.19 = (bf16[96,768]{1,0:T(8,128)(2,1)S(1)}, bf16[96,768]{1,0:T(8,128)(2,1)S(1)}, u32[]{:S(2)}, u32[]{:S(2)}) collective-permute-start(bf16[96,768]{1,0:T(8,128)(2,1)S(1)} %get-tuple-element.310), channel_id=1, source_target_pairs={{0,24},{2,26},{4,28},{6,30},{8,16},{10,18},{12,20},{14,22},{16,8},... | collective-permute-start | bytes 442376 | tf_op jit(solution)/shard_map/ppermute | solution.py:586
  398.1 3.6 collective-permute-start.20
  419.9 31.7 %collective-permute-start.21 = (bf16[768,768]{1,0:T(8,128)(2,1)}, bf16[768,768]{1,0:T(8,128)(2,1)}, u32[]{:S(2)}, u32[]{:S(2)}) collective-permute-start(bf16[768,768]{1,0:T(8,128)(2,1)} %get-tuple-element.339), channel_id=1, source_target_pairs={{0,2},{2,0},{4,6},{6,4},{8,10},{10,8},{12,14},{14,12},{16,18},{18,... | collective-permute-start | bytes 3538952 | tf_op jit(solution)/shard_map/ppermute | solution.py:586
  420.6 31.1 %collective-permute-start.22 = (bf16[768,768]{1,0:T(8,128)(2,1)}, bf16[768,768]{1,0:T(8,128)(2,1)}, u32[]{:S(2)}, u32[]{:S(2)}) collective-permute-start(bf16[768,768]{1,0:T(8,128)(2,1)} %get-tuple-element.340), channel_id=1, source_target_pairs={{0,4},{2,6},{4,0},{6,2},{8,12},{10,14},{12,8},{14,10},{16,20},{18,... | collective-permute-start | bytes 3538952 | tf_op jit(solution)/shard_map/ppermute | solution.py:586
  422.2 27.5 %collective-permute-start.23 = (bf16[96,768]{1,0:T(8,128)(2,1)}, bf16[96,768]{1,0:T(8,128)(2,1)S(1)}, u32[]{:S(2)}, u32[]{:S(2)}) collective-permute-start(bf16[96,768]{1,0:T(8,128)(2,1)} %copy-done.61), channel_id=1, source_target_pairs={{0,8},{2,10},{4,12},{6,14},{8,0},{10,2},{12,4},{14,6},{16,24},{18,... | collective-permute-start | bytes 442376 | tf_op jit(solution)/shard_map/ppermute | solution.py:586
  422.2 28.1 %collective-permute-start.24 = (bf16[96,768]{1,0:T(8,128)(2,1)}, bf16[96,768]{1,0:T(8,128)(2,1)S(1)}, u32[]{:S(2)}, u32[]{:S(2)}) collective-permute-start(bf16[96,768]{1,0:T(8,128)(2,1)} %copy-done.60), channel_id=1, source_target_pairs={{0,16},{2,18},{4,20},{6,22},{8,24},{10,26},{12,28},{14,30},{16,0},... | collective-permute-start | bytes 442376 | tf_op jit(solution)/shard_map/ppermute | solution.py:586
  424.2 26.8 %collective-permute-start.25 = (bf16[96,768]{1,0:T(8,128)(2,1)}, bf16[96,768]{1,0:T(8,128)(2,1)S(1)}, u32[]{:S(2)}, u32[]{:S(2)}) collective-permute-start(bf16[96,768]{1,0:T(8,128)(2,1)} %copy-done.59), channel_id=1, source_target_pairs={{0,24},{2,26},{4,28},{6,30},{8,16},{10,18},{12,20},{14,22},{16,8},... | collective-permute-start | bytes 442376 | tf_op jit(solution)/shard_map/ppermute | solution.py:586
  451.7 4.9 collective-permute-start.26
  451.7 4.4 collective-permute-start.27
  453.0 2.9 collective-permute-start.29
  453.1 2.9 collective-permute-start.28
  474.9 25.5 %collective-permute-start.30 = (bf16[640,768]{1,0:T(8,128)(2,1)}, bf16[640,768]{1,0:T(8,128)(2,1)S(1)}, u32[]{:S(2)}, u32[]{:S(2)}) collective-permute-start(bf16[640,768]{1,0:T(8,128)(2,1)} %get-tuple-element.385), channel_id=1, source_target_pairs={{0,2},{2,0},{4,6},{6,4},{8,10},{10,8},{12,14},{14,12},{16,18},{18,... | collective-permute-start | bytes 2949128 | tf_op jit(solution)/shard_map/ppermute | solution.py:586
  475.5 24.9 %collective-permute-start.31 = (bf16[576,768]{1,0:T(8,128)(2,1)}, bf16[576,768]{1,0:T(8,128)(2,1)S(1)}, u32[]{:S(2)}, u32[]{:S(2)}) collective-permute-start(bf16[576,768]{1,0:T(8,128)(2,1)} %get-tuple-element.386), channel_id=1, source_target_pairs={{0,4},{2,6},{4,0},{6,2},{8,12},{10,14},{12,8},{14,10},{16,20},{18,... | collective-permute-start | bytes 2654216 | tf_op jit(solution)/shard_map/ppermute | solution.py:586
  476.9 14.0 %collective-permute-start.32 = (bf16[192,768]{1,0:T(8,128)(2,1)S(1)}, bf16[192,768]{1,0:T(8,128)(2,1)S(1)}, u32[]{:S(2)}, u32[]{:S(2)}) collective-permute-start(bf16[192,768]{1,0:T(8,128)(2,1)S(1)} %get-tuple-element.387), channel_id=1, source_target_pairs={{0,8},{2,10},{4,12},{6,14},{8,0},{10,2},{12,4},{14,6},{16,24},{18,... | collective-permute-start | bytes 884744 | tf_op jit(solution)/shard_map/ppermute | solution.py:586
  476.9 23.5 %collective-permute-start.33 = (bf16[192,768]{1,0:T(8,128)(2,1)S(1)}, bf16[192,768]{1,0:T(8,128)(2,1)S(1)}, u32[]{:S(2)}, u32[]{:S(2)}) collective-permute-start(bf16[192,768]{1,0:T(8,128)(2,1)S(1)} %get-tuple-element.388), channel_id=1, source_target_pairs={{0,16},{2,18},{4,20},{6,22},{8,24},{10,26},{12,28},{14,30},{16,0},... | collective-permute-start | bytes 884744 | tf_op jit(solution)/shard_map/ppermute | solution.py:586
  478.8 21.5 %collective-permute-start.34 = (bf16[192,768]{1,0:T(8,128)(2,1)S(1)}, bf16[192,768]{1,0:T(8,128)(2,1)S(1)}, u32[]{:S(2)}, u32[]{:S(2)}) collective-permute-start(bf16[192,768]{1,0:T(8,128)(2,1)S(1)} %get-tuple-element.389), channel_id=1, source_target_pairs={{0,24},{2,26},{4,28},{6,30},{8,16},{10,18},{12,20},{14,22},{16,8},... | collective-permute-start | bytes 884744 | tf_op jit(solution)/shard_map/ppermute | solution.py:586
  505.6 40.1 %copy-start.23 = (f32[2,2,48,768]{3,2,1,0:T(8,128)}, f32[2,2,48,768]{3,2,1,0:T(8,128)S(1)}, u32[]{:S(2)}) copy-start(f32[2,2,48,768]{3,2,1,0:T(8,128)S(1)} %get-tuple-element.437.refs_5_) | copy-start | bytes 1769476
  505.6 19.8 %collective-permute-start.36 = (bf16[256,768]{1,0:T(8,128)(2,1)S(1)}, bf16[256,768]{1,0:T(8,128)(2,1)S(1)}, u32[]{:S(2)}, u32[]{:S(2)}) collective-permute-start(bf16[256,768]{1,0:T(8,128)(2,1)S(1)} %get-tuple-element.408), channel_id=1, source_target_pairs={{0,4},{2,6},{4,0},{6,2},{8,12},{10,14},{12,8},{14,10},{16,20},{18,... | collective-permute-start | bytes 1179656 | tf_op jit(solution)/shard_map/ppermute | solution.py:586
  506.2 8.9 %collective-permute-start.37 = (bf16[96,768]{1,0:T(8,128)(2,1)S(1)}, bf16[96,768]{1,0:T(8,128)(2,1)S(1)}, u32[]{:S(2)}, u32[]{:S(2)}) collective-permute-start(bf16[96,768]{1,0:T(8,128)(2,1)S(1)} %get-tuple-element.409), channel_id=1, source_target_pairs={{0,8},{2,10},{4,12},{6,14},{8,0},{10,2},{12,4},{14,6},{16,24},{18,... | collective-permute-start | bytes 442376 | tf_op jit(solution)/shard_map/ppermute | solution.py:586
  511.7 13.6 %collective-permute-start.35 = (bf16[192,768]{1,0:T(8,128)(2,1)S(1)}, bf16[192,768]{1,0:T(8,128)(2,1)S(1)}, u32[]{:S(2)}, u32[]{:S(2)}) collective-permute-start(bf16[192,768]{1,0:T(8,128)(2,1)S(1)} %get-tuple-element.407), channel_id=1, source_target_pairs={{0,2},{2,0},{4,6},{6,4},{8,10},{10,8},{12,14},{14,12},{16,18},{18,... | collective-permute-start | bytes 884744 | tf_op jit(solution)/shard_map/ppermute | solution.py:586
  513.2 12.2 %collective-permute-start.38 = (bf16[96,768]{1,0:T(8,128)(2,1)S(1)}, bf16[96,768]{1,0:T(8,128)(2,1)S(1)}, u32[]{:S(2)}, u32[]{:S(2)}) collective-permute-start(bf16[96,768]{1,0:T(8,128)(2,1)S(1)} %get-tuple-element.410), channel_id=1, source_target_pairs={{0,16},{2,18},{4,20},{6,22},{8,24},{10,26},{12,28},{14,30},{16,0},... | collective-permute-start | bytes 442376 | tf_op jit(solution)/shard_map/ppermute | solution.py:586
  513.5 18.7 %collective-permute-start.43 = (f32[1,2,48,768]{3,2,1,0:T(8,128)S(1)}, f32[1,2,48,768]{3,2,1,0:T(8,128)S(1)}, u32[]{:S(2)}, u32[]{:S(2)}) collective-permute-start(f32[1,2,48,768]{3,2,1,0:T(8,128)S(1)} %copy-done.27), channel_id=1, source_target_pairs={{0,1},{1,0},{2,3},{3,2},{4,5},{5,4},{6,7},{7,6},{8,9},{9,8},{10,11... | collective-permute-start | bytes 884744 | tf_op jit(solution)/shard_map/ppermute | solution.py:582
  515.1 10.3 %collective-permute-start.39 = (bf16[96,768]{1,0:T(8,128)(2,1)S(1)}, bf16[96,768]{1,0:T(8,128)(2,1)S(1)}, u32[]{:S(2)}, u32[]{:S(2)}) collective-permute-start(bf16[96,768]{1,0:T(8,128)(2,1)S(1)} %get-tuple-element.411), channel_id=1, source_target_pairs={{0,24},{2,26},{4,28},{6,30},{8,16},{10,18},{12,20},{14,22},{16,8},... | collective-permute-start | bytes 442376 | tf_op jit(solution)/shard_map/ppermute | solution.py:586
  525.3 8.2 %collective-permute-start.44 = (f32[1,2,48,768]{3,2,1,0:T(8,128)S(1)}, f32[1,2,48,768]{3,2,1,0:T(8,128)S(1)}, u32[]{:S(2)}, u32[]{:S(2)}) collective-permute-start(f32[1,2,48,768]{3,2,1,0:T(8,128)S(1)} %get-tuple-element.430.refs_4_), channel_id=1, source_target_pairs={{0,1},{1,0},{2,3},{3,2},{4,5},{5,4},{6,7},{7,6},{8,9},{9,8},{10,11... | collective-permute-start | bytes 884744 | tf_op jit(solution)/shard_map/ppermute | solution.py:582
  526.6 35.9 %copy-start.10 = (f32[2,48,768]{2,1,0:T(8,128)S(1)}, f32[2,48,768]{2,1,0:T(8,128)}, u32[]{:S(2)}) copy-start(f32[2,48,768]{2,1,0:T(8,128)} %refs_16_.1) | copy-start | bytes 884740
  526.6 35.9 %copy-start.24 = (f32[2,48,768]{2,1,0:T(8,128)S(1)}, f32[2,48,768]{2,1,0:T(8,128)}, u32[]{:S(2)}) copy-start(f32[2,48,768]{2,1,0:T(8,128)} %refs_17_.1) | copy-start | bytes 884740
  526.7 35.9 %copy-start.25 = (f32[2,48,768]{2,1,0:T(8,128)S(1)}, f32[2,48,768]{2,1,0:T(8,128)}, u32[]{:S(2)}) copy-start(f32[2,48,768]{2,1,0:T(8,128)} %refs_18_.1) | copy-start | bytes 884740
  526.7 35.9 %copy-start.49 = (f32[5,2,48]{2,1,0:T(2,128)S(1)}, f32[5,2,48]{2,1,0:T(2,128)}, u32[]{:S(2)}) copy-start(f32[5,2,48]{2,1,0:T(2,128)} %refs_28_.1) | copy-start | bytes 5764
  527.5 10.0 %collective-permute-start.40 = (bf16[112,768]{1,0:T(8,128)(2,1)S(1)}, bf16[112,768]{1,0:T(8,128)(2,1)S(1)}, u32[]{:S(2)}, u32[]{:S(2)}) collective-permute-start(bf16[112,768]{1,0:T(8,128)(2,1)S(1)} %get-tuple-element.426), channel_id=1, source_target_pairs={{0,8},{2,10},{4,12},{6,14},{8,0},{10,2},{12,4},{14,6},{16,24},{18,... | collective-permute-start | bytes 516104 | tf_op jit(solution)/shard_map/ppermute | solution.py:586
  529.7 14.7 %collective-permute-start.41 = (bf16[112,768]{1,0:T(8,128)(2,1)S(1)}, bf16[112,768]{1,0:T(8,128)(2,1)S(1)}, u32[]{:S(2)}, u32[]{:S(2)}) collective-permute-start(bf16[112,768]{1,0:T(8,128)(2,1)S(1)} %get-tuple-element.427), channel_id=1, source_target_pairs={{0,16},{2,18},{4,20},{6,22},{8,24},{10,26},{12,28},{14,30},{16,0},... | collective-permute-start | bytes 516104 | tf_op jit(solution)/shard_map/ppermute | solution.py:586
  530.2 14.2 %collective-permute-start.42 = (bf16[112,768]{1,0:T(8,128)(2,1)S(1)}, bf16[112,768]{1,0:T(8,128)(2,1)S(1)}, u32[]{:S(2)}, u32[]{:S(2)}) collective-permute-start(bf16[112,768]{1,0:T(8,128)(2,1)S(1)} %get-tuple-element.428), channel_id=1, source_target_pairs={{0,24},{2,26},{4,28},{6,30},{8,16},{10,18},{12,20},{14,22},{16,8},... | collective-permute-start | bytes 516104 | tf_op jit(solution)/shard_map/ppermute | solution.py:586
  532.2 30.3 %collective-permute-start.53 = (f32[2,2,48,768]{3,2,1,0:T(8,128)S(1)}, f32[2,2,48,768]{3,2,1,0:T(8,128)}, u32[]{:S(2)}, u32[]{:S(2)}) collective-permute-start(f32[2,2,48,768]{3,2,1,0:T(8,128)S(1)} %get-tuple-element.437.refs_5_), channel_id=1, source_target_pairs={{0,1},{1,0},{2,3},{3,2},{4,5},{5,4},{6,7},{7,6},{8,9},{9,8},{10,11... | collective-permute-start | bytes 1769480 | tf_op jit(solution)/shard_map/ppermute | solution.py:582
  545.7 1.1 collective-permute-start.45
  546.8 3.5 collective-permute-start.46
  547.9 3.5 collective-permute-start.47
  548.8 4.4 collective-permute-start.48
  553.2 5.4 collective-permute-start.49
  555.9 4.5 collective-permute-start.50
  556.5 5.4 collective-permute-start.51
  558.6 3.9 collective-permute-start.54
  558.7 3.8 collective-permute-start.55
  560.4 2.1 collective-permute-start.52
  (75 other events, 542.8 us)
Sparse Core Ops, SparseCore 0:
  14.9 174.2 all-gather.1

commit v11 on v10

--- a/solution.py
+++ b/solution.py
@@ -66,18 +66,9 @@
     )
 
 
-def granted(shapes, margin):
-    total = margin << 20
-    for shape, kind in shapes:
-        size = jnp.dtype(kind).itemsize
-        *lead, rows, lanes = (1,) + tuple(shape)
-        for n in lead:
-            size *= n
-        total += size * (-(-rows // 16) * 16) * (-(-lanes // 128) * 128)
-    return min(max(total, 50 << 20), 60 << 20)
-
-
+VMEM_LIMIT = 56 * 1024 * 1024
 LOW, FULL = jnp.bfloat16, jnp.float32
+SMALL = 128
 
 
 class Sent:
@@ -101,7 +92,7 @@
         self.copies.append(copy)
 
 
-def call(kernel, scalars, outs, ins, anys=(), scratch=(), flops=0, sent=(), margin=6):
+def call(kernel, scalars, outs, ins, anys=(), scratch=(), flops=0, sent=()):
     whole = pl.BlockSpec(memory_space=pltpu.VMEM)
     left = pl.BlockSpec(memory_space=pl.ANY)
 
@@ -117,8 +108,6 @@
             for copy in out_refs[i].copies:
                 copy.wait()
 
-    held = [(x.shape, x.dtype) for x in ins] + list(outs)
-    held += [(x.shape, x.dtype) for x in scratch if x.memory_space == pltpu.VMEM]
     return pl.pallas_call(
         body,
         out_shape=[jax.ShapeDtypeStruct(s, t) for s, t in outs],
@@ -129,7 +118,7 @@
         scratch_shapes=[pltpu.VMEM(*outs[i]) for i in sent]
         + list(scratch)
         + [pltpu.SemaphoreType.DMA((len(sent), 5))] * (len(sent) > 0),
-        compiler_params=pltpu.CompilerParams(vmem_limit_bytes=granted(held, margin)),
+        compiler_params=pltpu.CompilerParams(vmem_limit_bytes=VMEM_LIMIT),
         cost_estimate=pl.CostEstimate(
             flops=flops,
             bytes_accessed=sum(x.size * x.dtype.itemsize for x in list(ins) + list(anys)),
@@ -490,6 +479,50 @@
     )
 
 
+def head_kernel(place_of, ins, anys, outs):
+    resid, table, gains, codons, weight = ins
+    grad, branch, branch_own, branch_other, head_in, grad_logits, grad_gains, sums = outs
+    half = resid.shape[1] // 2
+    normed, unit, inverse = normalize(resid[...], gains[0:1], gains[1:2])
+    head_in[...] = normed.astype(LOW)
+    logits = dot_nt(head_in[...], table[...])
+    lane = lax.broadcasted_iota(jnp.int32, logits.shape, 1)
+    logits = jnp.where(lane < V, logits, -1e30)
+    top = jnp.max(logits, 1, keepdims=True)
+    lse = top + jnp.log(jnp.sum(jnp.exp(logits - top), 1, keepdims=True))
+    hot = jnp.where(lane == codons[...], 1.0, 0.0)
+    picked = jnp.sum(logits * hot, 1, keepdims=True)
+    loss = jnp.sum((lse - picked) * weight[...], 0, keepdims=True)
+    count = jnp.sum(weight[...], 0, keepdims=True)
+    lane = lax.broadcasted_iota(jnp.int32, sums.shape, 1)
+    sums[...] = jnp.where(lane == 0, loss, jnp.where(lane == 1, count, 0.0))
+    grad_logits[...] = ((jnp.exp(logits - lse) - hot) * weight[...]).astype(LOW)
+    back, gain, bias = normalize_back(
+        dot(grad_logits[...], table[...]), unit, inverse, gains[0:1]
+    )
+    grad[...] = back
+    back = back.astype(LOW)
+    branch[...] = back
+    first = place_of[0] == 0
+    branch_own[...] = jnp.where(first, back[:, :half], back[:, half:])
+    branch_other[...] = jnp.where(first, back[:, half:], back[:, :half])
+    grad_gains[0:1] = gain
+    grad_gains[1:2] = bias
+
+
+def head(place, resid, table, gains, codons, weight):
+    length, width = resid.shape
+    one, part = (length, width), (length, width // 2)
+    return call(
+        head_kernel,
+        place,
+        [(one, FULL), (one, LOW), (part, LOW), (part, LOW), (one, LOW)]
+        + [((length, SMALL), LOW), ((2, width), FULL), ((1, SMALL), FULL)],
+        [resid, table, gains, codons[:, None], weight[:, None]],
+        flops=4 * length * width * SMALL,
+    )
+
+
 def adam_step(master, grad, first, second, rate, decay):
     first = BETA_ONE * first + (1.0 - BETA_ONE) * grad
     second = BETA_TWO * second + (1.0 - BETA_TWO) * grad * grad
@@ -505,10 +538,13 @@
     return grad_norm, CLIP / jnp.maximum(grad_norm, CLIP) / count
 
 
-def optimizer_kernel(chunks, place_of, ins, anys, outs):
+def optimizer_kernel(chunks, place_of, ins, anys, outs, *scratch):
+    *masters, sems = scratch
+    copies = fetch(anys, masters, sems)
     totals, small_own, small_other, *rest = ins
-    n = (len(rest) - 18) // 2
-    own, other, masters = rest[:n], rest[n : 2 * n], rest[2 * n :]
+    n = (len(rest) - 6) // 2
+    own, other = rest[:n], rest[n : 2 * n]
+    masters += rest[2 * n :]
     layers = len(chunks)
     first = place_of[0] == 0
     grad_norm, scale = scale_of(totals[...])
@@ -524,26 +560,47 @@
         a, b = own[where[0]][where[1], s], other[where[0]][where[1], s]
         return jnp.where(first, a, b) if core == 0 else jnp.where(first, b, a)
 
+    def arrive(*which):
+        for copy in copies[3 * which[0] : 3 * which[-1] + 3]:
+            copy.wait()
+
+    def leave(which):
+        for i in range(3):
+            outs[1 + 3 * which + i].send()
+
     rows, width = own[0].shape[-2:]
     half = width // 2
+    arrive(0, 1)
     for l in range(layers):
-        mixer, up, down = chunks[l]
         for core in range(2):
             columns = lambda p: pl.ds(p * width + core * half, half)
-            value = tile(mixer, 0, core)
+            value = tile(chunks[l][0], 0, core)
             step(0, (l, slice(None), columns(0)), value[:, :half])
             step(0, (l, slice(None), columns(1)), value[:, half:])
-            value = tile(mixer, 1, core)
+            value = tile(chunks[l][0], 1, core)
             step(0, (l, slice(None), columns(2)), value[:, :half])
             step(1, (l, slice(None), columns(0)), value[:, half:])
+    leave(0)
+    leave(1)
+    arrive(2)
+    for l in range(layers):
+        for core in range(2):
             for s in range(2):
-                step(2, (l, slice(None), pl.ds((2 * core + s) * width, width)), tile(up, s, core))
-                value = tile(down, s, core)
+                at = (l, slice(None), pl.ds((2 * core + s) * width, width))
+                step(2, at, tile(chunks[l][1], s, core))
+    leave(2)
+    arrive(3)
+    for l in range(layers):
+        for core in range(2):
+            for s in range(2):
+                value = tile(chunks[l][2], s, core)
                 for j in range(2):
-                    at = (l, pl.ds((2 * s + j) * rows, rows), columns(0))
+                    at = (l, pl.ds((2 * s + j) * rows, rows), pl.ds(core * half, half))
                     step(3, at, value[:, j * half : (j + 1) * half])
-    small = jnp.where(first, small_own[...], small_other[...]).T
-    step(4, (slice(None), slice(None)), small[:V])
+    leave(3)
+    small = jnp.where(first, small_own[...], small_other[...])
+    step(4, (slice(None), slice(None)), small[:, :V])
+    small = small.T
     for n in range(masters[15].shape[0]):
         step(5, n, small[V + 2 * n : V + 2 * n + 2], RATE_VECTOR, 0.0)
 
@@ -553,8 +610,11 @@
         functools.partial(optimizer_kernel, chunks),
         place,
         [((1, 1), FULL)] + [(m.shape, m.dtype) for m in masters],
-        [totals, *small, *own, *other, *masters],
+        [totals, *small, *own, *other, *masters[12:]],
+        masters[:12],
+        [pltpu.VMEM(m.shape, m.dtype) for m in masters[:12]] + [pltpu.SemaphoreType.DMA((12,))],
         flops=20 * sum(m.size for m in masters),
+        sent=range(1, 13),
     )
 
 
@@ -605,9 +665,6 @@
 
 X, Y = 1, 2
 Z = (4, 8, 12)
-
-
-SMALL = 128
 
 
 def round_kernel(jobs, small_job, n_ins, counts, smalls, last, place_of, ins, anys, outs, *scratch):
@@ -988,15 +1045,13 @@
             quarter = quarter.reshape(2, 4, width, half).transpose(0, 2, 1, 3)
             columns.append(quarter.reshape(2, fsdp, rows, 2 * width).transpose(1, 0, 2, 3))
         weights = jnp.concatenate(columns, 3).transpose(1, 0, 2, 3).reshape(1, 2, width, -1)
-    small = weights[:, 0, :, : V + norms].reshape(width, V + norms).T
+    small = weights[:, 0, :, :SMALL].reshape(width, SMALL).T
     base = lambda l: weights.shape[3] - (layers - l) * 6 * width
-    table_low = small[:V]
-    gains = small[V:].astype(FULL).reshape(-1, 2, width)
+    gains = small[V : V + norms].astype(FULL).reshape(-1, 2, width)
 
     cosine, sine = rotary_tables(length)
-    vocab_ids = jnp.arange(V, dtype=jnp.int32)
     chosen = (inputs[:, None] == jnp.arange(SMALL, dtype=jnp.int32)[None, :]).astype(LOW)
-    resid = dot(chosen, jnp.pad(table_low, ((0, SMALL - V), (0, 0))))
+    resid = dot(chosen, small)
     kept = []
     for l in range(layers):
         gain = gains[2 * l : 2 * l + 2]
@@ -1006,27 +1061,12 @@
         output, pack_mid, hidden = hidden_forward(place, middle, weights, base(l), gain[1])
         kept.append((resid, query, keys, values, lse, pack, middle, hidden, pack_mid))
         resid = output
-    final_gain = gains[2 * layers]
-    normed_out, unit_out, inverse_out = normalize(resid, final_gain[0], final_gain[1])
-    head_in = normed_out.astype(LOW)
-    logits = jnp.einsum("sd,vd->sv", head_in, table_low, preferred_element_type=FULL)
-    top = jnp.max(logits, -1, keepdims=True)
-    lse_head = top + jnp.log(jnp.sum(jnp.exp(logits - top), -1, keepdims=True))
-    targets = (codons[:, None] == vocab_ids[None, :]).astype(FULL)
-    picked = jnp.sum(logits * targets, -1)
-    loss_local = jnp.sum((lse_head[:, 0] - picked) * weight)
-    grad_logits = ((jnp.exp(logits - lse_head) - targets) * weight[:, None]).astype(LOW)
-    grad_head = dot(grad_logits, table_low)
-    grad_logits = jnp.pad(grad_logits, ((0, 0), (0, SMALL - V)))
+    grad, branch, branch_own, branch_other, head_in, grad_logits, grad_norms, sums = head(
+        place, resid, small, gains[2 * layers], codons, weight
+    )
+    grad_norms = [grad_norms]
     early = (head_in, grad_logits, chosen)
     early_came = [swap_cores(v) for v in early]
-    sums = jnp.pad(jnp.stack([loss_local, jnp.sum(weight)]), (0, SMALL - 2))[None]
-    grad, grad_final_gain, grad_final_bias = normalize_back(
-        grad_head, unit_out, inverse_out, final_gain[0]
-    )
-    branch = grad.astype(LOW)
-    branch_own, branch_other = half_of(branch, core), half_of(branch, 1 - core)
-    grad_norms = [grad_final_gain, grad_final_bias]
     mid_came = [swap_cores(saved[-1]) for saved in kept]
     pack_came = [swap_cores(saved[5]) for saved in kept]
     grad, branch, mid_came[-1] = tie(grad, branch, mid_came[-1])
@@ -1169,9 +1209,11 @@
         chunks = [((at + 2, 0), (at + 1, 0), (at, pair)) for at, pair in places]
         own, other = zip(*shares)
         states = [v for group in zip(masters, firsts, seconds) for v in group]
+        states[12:15] = [v.T for v in states[12:15]]
         grad_norm, *values = optimizer(
             place, totals, (share_small, small_other), chunks, own, other, states
         )
+        values[12:15] = [v.T for v in values[12:15]]
     else:
         grad_norm, scale = scale_of(totals)
         share_small = share_small[:, : V + norms].T

time: 592 us -> 577 us (0.975)
  local copies, waits for them, and re-layouts: 47.7 us -> 19.4 us
  Pallas kernels: 207 us -> 229 us
  other arithmetic: 11.7 us -> 5.24 us
    unnamed x170 -> x122, local copies, waits for them, and re-layouts: 43.4 us -> 10.7 us
    pallas_call x18 -> x19, Pallas kernels: 207 us -> 229 us  [call(): pl.pallas_call(body, out_shape=[jax.ShapeDtypeStruct(s, t) for s, t in ou...]
  transfers between devices with their start and end apart: 57 -> 57, of which waited for: 24 -> 22; matrix products, arithmetic and copies ran while one was open for 3% -> 2% of each run, Pallas kernels for 17% -> 20%
where the time goes in v11:
time: 577 us; the launch traced here: 568 us
  waiting for transfers between devices  246 us (43%)
  Pallas kernels  229 us (40%)
  starting transfers between devices  52.1 us (9%)
  local copies, waits for them, and re-layouts  19.4 us (3%)
  between operations  15.1 us (3%)
    pallas_call x19, Pallas kernels, call(): pl.pallas_call(body, out_shape=[jax.ShapeDtypeStruct(s, t) for s, t in ou...  229 us
    all_gather x1, waiting for transfers between devices, body(): weights = lax.all_gather(weights, ('fsdp', 'dp'), axis=0, tiled=True)  171 us
    ppermute x33, waiting for transfers between devices, across(): return lax.ppermute(value, 'fsdp', [(i, i ^ mask) for i in range(size)])  56.4 us
    ppermute x33, starting transfers between devices, across(): return lax.ppermute(value, 'fsdp', [(i, i ^ mask) for i in range(size)])  47.6 us
    ppermute x23, waiting for transfers between devices, swap_cores(): return lax.ppermute(value, 'dp', [(0, 1), (1, 0)])  18.2 us
  transfers between devices with their start and end apart: 57, of which 22 were waited for; matrix products, arithmetic and copies ran while one was open for 2% of the time, Pallas kernels for 20%

profile of v11, /device:TPU:0, one launch (start us, length us, event | category | flops | bytes accessed | tf_op | source)
XLA Modules:
  0.0 568.0 jit_solution(13276961522564210188)
XLA Ops:
  10.1 3.1 shard_map.364
  15.1 1.3 pad_maximum_fusion
  16.4 171.3 %all-gather.2.cloned.1.call-done = bf16[1536,9344]{1,0:T(8,128)(2,1)} async-done(((bf16[48,9344]{1,0:T(8,128)(2,1)}), bf16[1536,9344]{1,0:T(8,128)(2,1)}) %all-gather.2.cloned.1.call-update) | async-done | bytes 28704784 | tf_op jit(solution)/shard_map/all_gather | solution.py:1037
  189.5 1.6 fusion.3.refs_0_.refs_10_
  191.0 14.0 %shard_map.365 = (f32[512,768]{1,0:T(8,128)}, bf16[512,768]{1,0:T(8,128)(2,1)}, bf16[512,768]{1,0:T(8,128)(2,1)}, bf16[512,768]{1,0:T(8,128)(2,1)}, f32[512,128]{1,0:T(8,128)}, /*index=5*/bf16[2,512,768]{2,1,0:T(8,128)(2,1)}) custom-call(s32[4]{0:T(128)} %pad_add_fusion.scalars, f32[512,768]{1,0:T(8,128)} %fusion.3.refs_0_.refs_10_, ...), custom_call_target="tpu_custom_call" | custom-call | flops 3221225472 | bytes 30812160 | tf_op jit(solution)/shard_map/pallas_call | solution.py:111
  205.1 12.7 %shard_map.366 = (f32[512,768]{1,0:T(8,128)}, bf16[5,512,768]{2,1,0:T(8,128)(2,1)}, f32[4,512,768]{2,1,0:T(8,128)}) custom-call(s32[4]{0:T(128)} %pad_add_fusion.scalars, f32[512,768]{1,0:T(8,128)} %get-tuple-element.250.refs_0_.refs_2_, f32[2,768]{1,0:T(2,128)} %get-tuple-element.480.refs_1_.refs_3_, bf16[16,2,48,9344]{3,2,1,0:T(8,128)(2,1)} %bitcast.27), custom_call_target="tpu_custom_call" | custom-call | flops 4831838208 | bytes 30283776 | tf_op jit(solution)/shard_map/pallas_call | solution.py:111
  217.8 14.1 %shard_map.367 = (f32[512,768]{1,0:T(8,128)}, bf16[512,768]{1,0:T(8,128)(2,1)}, bf16[512,768]{1,0:T(8,128)(2,1)}, bf16[512,768]{1,0:T(8,128)(2,1)}, f32[512,128]{1,0:T(8,128)}, /*index=5*/bf16[2,512,768]{2,1,0:T(8,128)(2,1)}) custom-call(s32[4]{0:T(128)} %pad_add_fusion.scalars, f32[512,768]{1,0:T(8,128)} %get-tuple-element.252.refs_0_.refs_10_, ...), custom_call_target="tpu_custom_call" | custom-call | flops 3221225472 | bytes 30812160 | tf_op jit(solution)/shard_map/pallas_call | solution.py:111
  231.9 12.7 %shard_map.368 = (f32[512,768]{1,0:T(8,128)}, bf16[5,512,768]{2,1,0:T(8,128)(2,1)}, f32[4,512,768]{2,1,0:T(8,128)}) custom-call(s32[4]{0:T(128)} %pad_add_fusion.scalars, f32[512,768]{1,0:T(8,128)} %get-tuple-element.254.refs_0_.refs_2_, f32[2,768]{1,0:T(2,128)} %get-tuple-element.478.refs_1_.refs_3_, bf16[16,2,48,9344]{3,2,1,0:T(8,128)(2,1)} %bitcast.29), custom_call_target="tpu_custom_call" | custom-call | flops 4831838208 | bytes 30283776 | tf_op jit(solution)/shard_map/pallas_call | solution.py:111
  246.7 5.8 %shard_map.369 = (f32[512,768]{1,0:T(8,128)}, bf16[512,768]{1,0:T(8,128)(2,1)}, bf16[512,384]{1,0:T(8,128)(2,1)}, bf16[512,384]{1,0:T(8,128)(2,1)}, bf16[512,768...) custom-call(s32[4]{0:T(128)} %pad_add_fusion.scalars, ...), custom_call_target="tpu_custom_call" | custom-call | flops 201326592 | bytes 1779712 | tf_op jit(solution)/shard_map/pallas_call | solution.py:111
  253.3 1.2 collective-permute-done.1.refs_3_
  255.2 8.8 %shard_map.370 = (bf16[384,768]{1,0:T(8,128)(2,1)}, bf16[384,768]{1,0:T(8,128)(2,1)}, f32[1,2,384,768]{3,2,1,0:T(8,128)}) custom-call(s32[4]{0:T(128)} %pad_add_fusion.scalars, bf16[5,512,768]{2,1,0:T(8,128)(2,1)} %get-tuple-element.255.refs_0_, bf16[512,384]{1,0:T(8,128)(2,1)} %get-tuple-element.257.refs_1_, ...), custom_call_target="tpu_custom_call" | custom-call | flops 2415919104 | bytes 8650752 | tf_op jit(solution)/shard_map/pallas_call | solution.py:111
  264.0 1.4 collective-permute-start.2
  266.2 1.3 collective-permute-done.6.refs_11_
  267.7 19.8 %shard_map.371 = (f32[512,768]{1,0:T(8,128)}, f32[2,768]{1,0:T(2,128)}, bf16[2,512,768]{2,1,0:T(8,128)(2,1)}, bf16[2,512,768]{2,1,0:T(8,128)(2,1)}) custom-call(s32[4]{0:T(128)} %pad_add_fusion.scalars, bf16[512,768]{1,0:T(8,128)(2,1)} %get-tuple-element.269.refs_0_, f32[512,768]{1,0:T(8,128)} %get-tuple-element.270.refs_1_, ...), custom_call_target="tpu_custom_call" | custom-call | flops 4831838208 | bytes 38934528 | tf_op jit(solution)/shard_map/pallas_call | solution.py:111
  289.4 3.5 collective-permute-done.7.refs_3_
  292.9 1.2 copy-done.4
  294.1 10.3 %shard_map.372 = (bf16[576,768]{1,0:T(8,128)(2,1)}, bf16[576,768]{1,0:T(8,128)(2,1)}, f32[1,2,384,768]{3,2,1,0:T(8,128)}, f32[1,2,192,768]{3,2,1,0:T(8,128)}) custom-call(s32[4]{0:T(128)} %pad_add_fusion.scalars, bf16[5,512,768]{2,1,0:T(8,128)(2,1)} %get-tuple-element.255.refs_0_, bf16[2,512,768]{2,1,0:T(8,128)(2,1)} %get-tuple-element.277.refs_1_, ...), custom_call_target="tpu_custom_call" | custom-call | flops 2415919104 | bytes 14548992 | tf_op jit(solution)/shard_map/pallas_call | solution.py:111
  304.3 1.5 collective-permute-start.8
  306.4 1.1 copy.52
  308.1 22.2 %shard_map.373 = (f32[512,768]{1,0:T(8,128)}, bf16[512,768]{1,0:T(8,128)(2,1)}, bf16[512,384]{1,0:T(8,128)(2,1)}, bf16[512,384]{1,0:T(8,128)(2,1)}, f32[2,768]{1...) custom-call(s32[4]{0:T(128)} %pad_add_fusion.scalars, f32[512,768]{1,0:T(8,128)} %get-tuple-element.289.refs_0_, ...), custom_call_target="tpu_custom_call" | custom-call | flops 4429185024 | bytes 34768896 | tf_op jit(solution)/shard_map/pallas_call | solution.py:111
  330.9 3.7 collective-permute-done.14.refs_7_
  335.3 1.2 copy-done.3
  336.5 16.9 %shard_map.374 = (bf16[960,768]{1,0:T(8,128)(2,1)}, bf16[960,768]{1,0:T(8,128)(2,1)}, f32[2,2,384,768]{3,2,1,0:T(8,128)}, f32[1,2,192,768]{3,2,1,0:T(8,128)}, f3...) custom-call(s32[4]{0:T(128)} %pad_add_fusion.scalars, ...), custom_call_target="tpu_custom_call" | custom-call | flops 4831838208 | bytes 20250624 | tf_op jit(solution)/shard_map/pallas_call | solution.py:111
  353.4 1.5 collective-permute-start.15
  355.8 1.9 collective-permute-start.18
  357.7 2.4 collective-permute-start.19
  360.1 19.3 %shard_map.375 = (f32[512,768]{1,0:T(8,128)}, f32[2,768]{1,0:T(2,128)}, bf16[2,512,768]{2,1,0:T(8,128)(2,1)}, bf16[2,512,768]{2,1,0:T(8,128)(2,1)}) custom-call(s32[4]{0:T(128)} %pad_add_fusion.scalars, bf16[512,768]{1,0:T(8,128)(2,1)} %get-tuple-element.325.refs_0_, f32[512,768]{1,0:T(8,128)} %get-tuple-element.326.refs_1_, ...), custom_call_target="tpu_custom_call" | custom-call | flops 4831838208 | bytes 38934528 | tf_op jit(solution)/shard_map/pallas_call | solution.py:111
  379.5 8.5 %collective-permute-done.15.refs_6_ = bf16[960,768]{1,0:T(8,128)(2,1)S(1)} collective-permute-done((bf16[960,768]{1,0:T(8,128)(2,1)}, bf16[960,768]{1,0:T(8,128)(2,1)S(1)}, u32[]{:S(2)}, u32[]{:S(2)}) %collective-permute-start.15) | collective-permute-done | bytes 1474592 | tf_op jit(solution)/shard_map/ppermute | solution.py:646
  388.0 1.4 collective-permute-done.16.refs_7_
  389.4 3.6 collective-permute-done.20.refs_3_
  394.2 13.1 %shard_map.376 = (bf16[768,768]{1,0:T(8,128)(2,1)}, bf16[768,768]{1,0:T(8,128)(2,1)}, f32[1,2,384,768]{3,2,1,0:T(8,128)}, f32[2,2,192,768]{3,2,1,0:T(8,128)}, f3...) custom-call(s32[4]{0:T(128)} %pad_add_fusion.scalars, ...), custom_call_target="tpu_custom_call" | custom-call | flops 2415919104 | bytes 20597760 | tf_op jit(solution)/shard_map/pallas_call | solution.py:111
  407.9 1.5 collective-permute-start.22
  410.1 1.9 collective-permute-start.24
  412.1 2.4 collective-permute-start.25
  414.5 22.1 %shard_map.377 = (f32[512,768]{1,0:T(8,128)}, bf16[512,768]{1,0:T(8,128)(2,1)}, bf16[512,384]{1,0:T(8,128)(2,1)}, bf16[512,384]{1,0:T(8,128)(2,1)}, f32[2,768]{1...) custom-call(s32[4]{0:T(128)} %pad_add_fusion.scalars, f32[512,768]{1,0:T(8,128)} %get-tuple-element.358.refs_0_, ...), custom_call_target="tpu_custom_call" | custom-call | flops 4429185024 | bytes 34768896 | tf_op jit(solution)/shard_map/pallas_call | solution.py:111
  438.0 2.3 collective-permute-done.29.refs_15_
  440.3 1.3 collective-permute-done.28.refs_13_
  443.1 13.2 %shard_map.378 = (bf16[640,768]{1,0:T(8,128)(2,1)}, bf16[576,768]{1,0:T(8,128)(2,1)}, f32[1,2,384,768]{3,2,1,0:T(8,128)}, f32[384,128]{1,0:T(8,128)}, f32[1,2,19...) custom-call(s32[4]{0:T(128)} %pad_add_fusion.scalars, ...), custom_call_target="tpu_custom_call" | custom-call | flops 2415919104 | bytes 17841152 | tf_op jit(solution)/shard_map/pallas_call | solution.py:111
  456.8 1.4 collective-permute-start.31
  458.3 1.9 collective-permute-start.33
  460.2 2.4 collective-permute-start.34
  462.7 9.7 %collective-permute-done.32.refs_6_ = bf16[192,768]{1,0:T(8,128)(2,1)S(1)} collective-permute-done((bf16[192,768]{1,0:T(8,128)(2,1)}, bf16[192,768]{1,0:T(8,128)(2,1)S(1)}, u32[]{:S(2)}, u32[]{:S(2)}) %collective-permute-start.32) | collective-permute-done | bytes 294944 | tf_op jit(solution)/shard_map/ppermute | solution.py:646
  472.4 9.6 %collective-permute-done.33.refs_7_ = bf16[192,768]{1,0:T(8,128)(2,1)S(1)} collective-permute-done((bf16[192,768]{1,0:T(8,128)(2,1)}, bf16[192,768]{1,0:T(8,128)(2,1)S(1)}, u32[]{:S(2)}, u32[]{:S(2)}) %collective-permute-start.33) | collective-permute-done | bytes 294944 | tf_op jit(solution)/shard_map/ppermute | solution.py:646
  483.4 4.9 shard_map.379
  488.9 5.4 collective-permute-start.37
  494.3 1.5 collective-permute-start.35
  496.1 1.9 collective-permute-done.37.refs_5_
  498.0 2.7 collective-permute-start.39
  500.7 7.6 %collective-permute-done.38.refs_6_ = bf16[96,768]{1,0:T(8,128)(2,1)S(1)} collective-permute-done((bf16[96,768]{1,0:T(8,128)(2,1)}, bf16[96,768]{1,0:T(8,128)(2,1)S(1)}, u32[]{:S(2)}, u32[]{:S(2)}) %collective-permute-start.38) | collective-permute-done | bytes 147488 | tf_op jit(solution)/shard_map/ppermute | solution.py:646
  509.2 2.8 shard_map.380
  512.0 2.3 collective-permute-start.40
  514.5 2.2 collective-permute-start.42
  516.8 5.1 collective-permute-done.40.refs_2_
  521.9 7.2 %collective-permute-done.41.refs_3_ = bf16[112,768]{1,0:T(8,128)(2,1)S(1)} collective-permute-done((bf16[112,768]{1,0:T(8,128)(2,1)}, bf16[112,768]{1,0:T(8,128)(2,1)S(1)}, u32[]{:S(2)}, u32[]{:S(2)}) %collective-permute-start.41) | collective-permute-done | bytes 172064 | tf_op jit(solution)/shard_map/ppermute | solution.py:646
  529.9 2.0 shard_map.381
  531.9 1.3 collective-permute-done.45
  534.5 1.2 collective-permute-start.47
  535.7 1.6 collective-permute-start.48
  538.1 2.1 collective-permute-done.48
  540.1 2.7 collective-permute-start.49
  543.0 2.3 collective-permute-start.51
  545.8 1.5 collective-permute-done.50
  547.3 1.1 collective-permute-done.51
  550.0 10.8 %shard_map.382 = (f32[1,1]{1,0:T(1,128)}, f32[2,48,2304]{2,1,0:T(8,128)}, f32[2,48,2304]{2,1,0:T(8,128)}, f32[2,48,2304]{2,1,0:T(8,128)}, f32[2,48,768]{2,1,0:T(...) custom-call(s32[4]{0:T(128)} %pad_add_fusion.scalars, ...), custom_call_target="tpu_custom_call" | custom-call | flops 53314560 | bytes 14251520 | tf_op jit(solution)/shard_map/pallas_call | solution.py:111
  (222 shorter events, 30.7 us)
Async XLA Ops:
  7.2 180.5 %all-gather.2.cloned.1.call-start = ((), (), s32[]{:S(2)}) async-start(), calls=%async_computation | async-start | bytes 29601792 | tf_op jit(solution)/shard_map/all_gather | solution.py:1037
  244.7 8.6 %collective-permute-start = (bf16[5,512,768]{2,1,0:T(8,128)(2,1)}, bf16[5,512,768]{2,1,0:T(8,128)(2,1)}, u32[]{:S(2)}, u32[]{:S(2)}) collective-permute-start(bf16[5,512,768]{2,1,0:T(8,128)(2,1)} %get-tuple-element.255.refs_0_), channel_id=1, source_target_pairs={{0,1},{1,0},{2,3},{3,2},{4,5},{5,4},{6,7},{7,6},{8,9},{9,8},{10,11... | collective-permute-start | bytes 11796488 | tf_op jit(solution)/shard_map/ppermute | solution.py:642
  252.5 1.9 collective-permute-start.1
  252.8 77.5 %collective-permute-start.10 = (bf16[5,512,768]{2,1,0:T(8,128)(2,1)}, bf16[5,512,768]{2,1,0:T(8,128)(2,1)}, u32[]{:S(2)}, u32[]{:S(2)}) collective-permute-start(bf16[5,512,768]{2,1,0:T(8,128)(2,1)} %get-tuple-element.251.refs_4_.refs_0_), channel_id=1, source_target_pairs={{0,1},{1,0},{2,3},{3,2},{4,5},{5,4},{6,7},{7,6},{8,9},{9,8},{10,11... | collective-permute-start | bytes 11796488 | tf_op jit(solution)/shard_map/ppermute | solution.py:642
  253.0 34.6 %collective-permute-start.4 = (bf16[512,768]{1,0:T(8,128)(2,1)}, bf16[512,768]{1,0:T(8,128)(2,1)S(1)}, u32[]{:S(2)}, u32[]{:S(2)}) collective-permute-start(bf16[512,768]{1,0:T(8,128)(2,1)} %get-tuple-element.275.refs_4_), channel_id=1, source_target_pairs={{0,1},{1,0},{2,3},{3,2},{4,5},{5,4},{6,7},{7,6},{8,9},{9,8},{10,11... | collective-permute-start | bytes 2359304 | tf_op jit(solution)/shard_map/ppermute | solution.py:642
  264.0 23.7 %collective-permute-start.2 = (bf16[384,768]{1,0:T(8,128)(2,1)}, bf16[384,768]{1,0:T(8,128)(2,1)S(1)}, u32[]{:S(2)}, u32[]{:S(2)}) collective-permute-start(bf16[384,768]{1,0:T(8,128)(2,1)} %get-tuple-element.267), channel_id=1, source_target_pairs={{0,2},{2,0},{4,6},{6,4},{8,10},{10,8},{12,14},{14,12},{16,18},{18,... | collective-permute-start | bytes 1769480 | tf_op jit(solution)/shard_map/ppermute | solution.py:646
  265.4 22.3 %collective-permute-start.3 = (bf16[384,768]{1,0:T(8,128)(2,1)}, bf16[384,768]{1,0:T(8,128)(2,1)S(1)}, u32[]{:S(2)}, u32[]{:S(2)}) collective-permute-start(bf16[384,768]{1,0:T(8,128)(2,1)} %get-tuple-element.268), channel_id=1, source_target_pairs={{0,4},{2,6},{4,0},{6,2},{8,12},{10,14},{12,8},{14,10},{16,20},{18,... | collective-permute-start | bytes 1769480 | tf_op jit(solution)/shard_map/ppermute | solution.py:646
  266.2 1.4 collective-permute-start.6
  267.6 20.0 %collective-permute-start.5 = (bf16[512,128]{1,0:T(8,128)(2,1)S(1)}, bf16[512,128]{1,0:T(8,128)(2,1)S(1)}, u32[]{:S(2)}, u32[]{:S(2)}) collective-permute-start(bf16[512,128]{1,0:T(8,128)(2,1)S(1)} %copy-done.45), channel_id=1, source_target_pairs={{0,1},{1,0},{2,3},{3,2},{4,5},{5,4},{6,7},{7,6},{8,9},{9,8},{10,11... | collective-permute-start | bytes 393224 | tf_op jit(solution)/shard_map/ppermute | solution.py:642
  288.5 4.4 collective-permute-start.7
  288.9 41.3 %collective-permute-start.12 = (bf16[2,512,768]{2,1,0:T(8,128)(2,1)}, bf16[2,512,768]{2,1,0:T(8,128)(2,1)}, u32[]{:S(2)}, u32[]{:S(2)}) collective-permute-start(bf16[2,512,768]{2,1,0:T(8,128)(2,1)} %get-tuple-element.253.refs_0_), channel_id=1, source_target_pairs={{0,1},{1,0},{2,3},{3,2},{4,5},{5,4},{6,7},{7,6},{8,9},{9,8},{10,11... | collective-permute-start | bytes 4718600 | tf_op jit(solution)/shard_map/ppermute | solution.py:642
  289.1 41.2 %collective-permute-start.11 = (bf16[2,512,768]{2,1,0:T(8,128)(2,1)S(1)}, bf16[2,512,768]{2,1,0:T(8,128)(2,1)S(1)}, u32[]{:S(2)}, u32[]{:S(2)}) collective-permute-start(bf16[2,512,768]{2,1,0:T(8,128)(2,1)S(1)} %copy-done), channel_id=1, source_target_pairs={{0,1},{1,0},{2,3},{3,2},{4,5},{5,4},{6,7},{7,6},{8,9},{9,8},{10,11... | collective-permute-start | bytes 4718600 | tf_op jit(solution)/shard_map/ppermute | solution.py:642
  304.3 25.9 %collective-permute-start.8 = (bf16[576,768]{1,0:T(8,128)(2,1)}, bf16[576,768]{1,0:T(8,128)(2,1)}, u32[]{:S(2)}, u32[]{:S(2)}) collective-permute-start(bf16[576,768]{1,0:T(8,128)(2,1)} %get-tuple-element.287), channel_id=1, source_target_pairs={{0,2},{2,0},{4,6},{6,4},{8,10},{10,8},{12,14},{14,12},{16,18},{18,... | collective-permute-start | bytes 2654216 | tf_op jit(solution)/shard_map/ppermute | solution.py:646
  305.8 24.5 %collective-permute-start.9 = (bf16[576,768]{1,0:T(8,128)(2,1)}, bf16[576,768]{1,0:T(8,128)(2,1)}, u32[]{:S(2)}, u32[]{:S(2)}) collective-permute-start(bf16[576,768]{1,0:T(8,128)(2,1)} %get-tuple-element.288), channel_id=1, source_target_pairs={{0,4},{2,6},{4,0},{6,2},{8,12},{10,14},{12,8},{14,10},{16,20},{18,... | collective-permute-start | bytes 2654216 | tf_op jit(solution)/shard_map/ppermute | solution.py:646
  330.3 23.2 %copy-start.1 = (bf16[2,512,768]{2,1,0:T(8,128)(2,1)}, bf16[2,512,768]{2,1,0:T(8,128)(2,1)S(1)}, u32[]{:S(2)}) copy-start(bf16[2,512,768]{2,1,0:T(8,128)(2,1)S(1)} %collective-permute-done.11.refs_2_) | copy-start | bytes 4718596
  330.3 4.3 collective-permute-start.13
  330.4 4.2 collective-permute-start.14
  353.4 34.6 %collective-permute-start.15 = (bf16[960,768]{1,0:T(8,128)(2,1)}, bf16[960,768]{1,0:T(8,128)(2,1)S(1)}, u32[]{:S(2)}, u32[]{:S(2)}) collective-permute-start(bf16[960,768]{1,0:T(8,128)(2,1)} %get-tuple-element.320), channel_id=1, source_target_pairs={{0,2},{2,0},{4,6},{6,4},{8,10},{10,8},{12,14},{14,12},{16,18},{18,... | collective-permute-start | bytes 4423688 | tf_op jit(solution)/shard_map/ppermute | solution.py:646
  354.9 34.5 %collective-permute-start.16 = (bf16[960,768]{1,0:T(8,128)(2,1)}, bf16[960,768]{1,0:T(8,128)(2,1)S(1)}, u32[]{:S(2)}, u32[]{:S(2)}) collective-permute-start(bf16[960,768]{1,0:T(8,128)(2,1)} %get-tuple-element.321), channel_id=1, source_target_pairs={{0,4},{2,6},{4,0},{6,2},{8,12},{10,14},{12,8},{14,10},{16,20},{18,... | collective-permute-start | bytes 4423688 | tf_op jit(solution)/shard_map/ppermute | solution.py:646
  355.8 23.7 %collective-permute-start.17 = (bf16[96,768]{1,0:T(8,128)(2,1)}, bf16[96,768]{1,0:T(8,128)(2,1)S(1)}, u32[]{:S(2)}, u32[]{:S(2)}) collective-permute-start(bf16[96,768]{1,0:T(8,128)(2,1)} %get-tuple-element.322), channel_id=1, source_target_pairs={{0,8},{2,10},{4,12},{6,14},{8,0},{10,2},{12,4},{14,6},{16,24},{18,... | collective-permute-start | bytes 442376 | tf_op jit(solution)/shard_map/ppermute | solution.py:646
  355.8 23.7 %collective-permute-start.18 = (bf16[96,768]{1,0:T(8,128)(2,1)}, bf16[96,768]{1,0:T(8,128)(2,1)S(1)}, u32[]{:S(2)}, u32[]{:S(2)}) collective-permute-start(bf16[96,768]{1,0:T(8,128)(2,1)} %get-tuple-element.323), channel_id=1, source_target_pairs={{0,16},{2,18},{4,20},{6,22},{8,24},{10,26},{12,28},{14,30},{16,0},... | collective-permute-start | bytes 442376 | tf_op jit(solution)/shard_map/ppermute | solution.py:646
  357.7 21.8 %collective-permute-start.19 = (bf16[96,768]{1,0:T(8,128)(2,1)}, bf16[96,768]{1,0:T(8,128)(2,1)S(1)}, u32[]{:S(2)}, u32[]{:S(2)}) collective-permute-start(bf16[96,768]{1,0:T(8,128)(2,1)} %get-tuple-element.324), channel_id=1, source_target_pairs={{0,24},{2,26},{4,28},{6,30},{8,16},{10,18},{12,20},{14,22},{16,8},... | collective-permute-start | bytes 442376 | tf_op jit(solution)/shard_map/ppermute | solution.py:646
  389.4 3.6 collective-permute-start.20
  407.2 29.5 %collective-permute-start.21 = (bf16[768,768]{1,0:T(8,128)(2,1)}, bf16[768,768]{1,0:T(8,128)(2,1)S(1)}, u32[]{:S(2)}, u32[]{:S(2)}) collective-permute-start(bf16[768,768]{1,0:T(8,128)(2,1)} %get-tuple-element.353), channel_id=1, source_target_pairs={{0,2},{2,0},{4,6},{6,4},{8,10},{10,8},{12,14},{14,12},{16,18},{18,... | collective-permute-start | bytes 3538952 | tf_op jit(solution)/shard_map/ppermute | solution.py:646
  407.9 28.8 %collective-permute-start.22 = (bf16[768,768]{1,0:T(8,128)(2,1)}, bf16[768,768]{1,0:T(8,128)(2,1)S(1)}, u32[]{:S(2)}, u32[]{:S(2)}) collective-permute-start(bf16[768,768]{1,0:T(8,128)(2,1)} %get-tuple-element.354), channel_id=1, source_target_pairs={{0,4},{2,6},{4,0},{6,2},{8,12},{10,14},{12,8},{14,10},{16,20},{18,... | collective-permute-start | bytes 3538952 | tf_op jit(solution)/shard_map/ppermute | solution.py:646
  410.1 26.5 %collective-permute-start.23 = (bf16[96,768]{1,0:T(8,128)(2,1)}, bf16[96,768]{1,0:T(8,128)(2,1)S(1)}, u32[]{:S(2)}, u32[]{:S(2)}) collective-permute-start(bf16[96,768]{1,0:T(8,128)(2,1)} %get-tuple-element.355), channel_id=1, source_target_pairs={{0,8},{2,10},{4,12},{6,14},{8,0},{10,2},{12,4},{14,6},{16,24},{18,... | collective-permute-start | bytes 442376 | tf_op jit(solution)/shard_map/ppermute | solution.py:646
  410.1 26.5 %collective-permute-start.24 = (bf16[96,768]{1,0:T(8,128)(2,1)}, bf16[96,768]{1,0:T(8,128)(2,1)S(1)}, u32[]{:S(2)}, u32[]{:S(2)}) collective-permute-start(bf16[96,768]{1,0:T(8,128)(2,1)} %get-tuple-element.356), channel_id=1, source_target_pairs={{0,16},{2,18},{4,20},{6,22},{8,24},{10,26},{12,28},{14,30},{16,0},... | collective-permute-start | bytes 442376 | tf_op jit(solution)/shard_map/ppermute | solution.py:646
  412.1 24.6 %collective-permute-start.25 = (bf16[96,768]{1,0:T(8,128)(2,1)}, bf16[96,768]{1,0:T(8,128)(2,1)S(1)}, u32[]{:S(2)}, u32[]{:S(2)}) collective-permute-start(bf16[96,768]{1,0:T(8,128)(2,1)} %get-tuple-element.357), channel_id=1, source_target_pairs={{0,24},{2,26},{4,28},{6,30},{8,16},{10,18},{12,20},{14,22},{16,8},... | collective-permute-start | bytes 442376 | tf_op jit(solution)/shard_map/ppermute | solution.py:646
  414.5 22.8 %copy-start.57 = (f32[2,768]{1,0:T(2,128)S(1)}, f32[2,768]{1,0:T(2,128)}, u32[]{:S(2)}) copy-start(f32[2,768]{1,0:T(2,128)} %get-tuple-element.376) | copy-start | bytes 18436
  414.5 22.8 %copy-start.58 = (f32[2,768]{1,0:T(2,128)S(1)}, f32[2,768]{1,0:T(2,128)}, u32[]{:S(2)}) copy-start(f32[2,768]{1,0:T(2,128)} %get-tuple-element.375) | copy-start | bytes 18436
  436.8 4.9 collective-permute-start.26
  436.9 4.8 collective-permute-start.27
  437.4 2.9 collective-permute-start.29
  437.5 4.1 collective-permute-start.28
  456.2 25.8 %collective-permute-start.30 = (bf16[640,768]{1,0:T(8,128)(2,1)}, bf16[640,768]{1,0:T(8,128)(2,1)S(1)}, u32[]{:S(2)}, u32[]{:S(2)}) collective-permute-start(bf16[640,768]{1,0:T(8,128)(2,1)} %get-tuple-element.400), channel_id=1, source_target_pairs={{0,2},{2,0},{4,6},{6,4},{8,10},{10,8},{12,14},{14,12},{16,18},{18,... | collective-permute-start | bytes 2949128 | tf_op jit(solution)/shard_map/ppermute | solution.py:646
  456.8 25.1 %collective-permute-start.31 = (bf16[576,768]{1,0:T(8,128)(2,1)}, bf16[576,768]{1,0:T(8,128)(2,1)S(1)}, u32[]{:S(2)}, u32[]{:S(2)}) collective-permute-start(bf16[576,768]{1,0:T(8,128)(2,1)} %get-tuple-element.401), channel_id=1, source_target_pairs={{0,4},{2,6},{4,0},{6,2},{8,12},{10,14},{12,8},{14,10},{16,20},{18,... | collective-permute-start | bytes 2654216 | tf_op jit(solution)/shard_map/ppermute | solution.py:646
  458.3 14.1 %collective-permute-start.32 = (bf16[192,768]{1,0:T(8,128)(2,1)}, bf16[192,768]{1,0:T(8,128)(2,1)S(1)}, u32[]{:S(2)}, u32[]{:S(2)}) collective-permute-start(bf16[192,768]{1,0:T(8,128)(2,1)} %get-tuple-element.402), channel_id=1, source_target_pairs={{0,8},{2,10},{4,12},{6,14},{8,0},{10,2},{12,4},{14,6},{16,24},{18,... | collective-permute-start | bytes 884744 | tf_op jit(solution)/shard_map/ppermute | solution.py:646
  458.3 23.7 %collective-permute-start.33 = (bf16[192,768]{1,0:T(8,128)(2,1)}, bf16[192,768]{1,0:T(8,128)(2,1)S(1)}, u32[]{:S(2)}, u32[]{:S(2)}) collective-permute-start(bf16[192,768]{1,0:T(8,128)(2,1)} %get-tuple-element.403), channel_id=1, source_target_pairs={{0,16},{2,18},{4,20},{6,22},{8,24},{10,26},{12,28},{14,30},{16,0},... | collective-permute-start | bytes 884744 | tf_op jit(solution)/shard_map/ppermute | solution.py:646
  460.2 21.7 %collective-permute-start.34 = (bf16[192,768]{1,0:T(8,128)(2,1)}, bf16[192,768]{1,0:T(8,128)(2,1)S(1)}, u32[]{:S(2)}, u32[]{:S(2)}) collective-permute-start(bf16[192,768]{1,0:T(8,128)(2,1)} %get-tuple-element.404), channel_id=1, source_target_pairs={{0,24},{2,26},{4,28},{6,30},{8,16},{10,18},{12,20},{14,22},{16,8},... | collective-permute-start | bytes 884744 | tf_op jit(solution)/shard_map/ppermute | solution.py:646
  483.4 24.9 %copy-start.27 = (f32[1,2,48,768]{3,2,1,0:T(8,128)S(1)}, f32[1,2,48,768]{3,2,1,0:T(8,128)}, u32[]{:S(2)}) copy-start(f32[1,2,48,768]{3,2,1,0:T(8,128)} %get-tuple-element.445.refs_4_) | copy-start | bytes 884740
  488.3 28.4 %copy-start.15 = (f32[2,2,48,768]{3,2,1,0:T(8,128)S(1)}, f32[2,2,48,768]{3,2,1,0:T(8,128)}, u32[]{:S(2)}) copy-start(f32[2,2,48,768]{3,2,1,0:T(8,128)} %get-tuple-element.453.refs_5_) | copy-start | bytes 1769476
  488.3 20.1 %collective-permute-start.36 = (bf16[256,768]{1,0:T(8,128)(2,1)}, bf16[256,768]{1,0:T(8,128)(2,1)S(1)}, u32[]{:S(2)}, u32[]{:S(2)}) collective-permute-start(bf16[256,768]{1,0:T(8,128)(2,1)} %get-tuple-element.423), channel_id=1, source_target_pairs={{0,4},{2,6},{4,0},{6,2},{8,12},{10,14},{12,8},{14,10},{16,20},{18,... | collective-permute-start | bytes 1179656 | tf_op jit(solution)/shard_map/ppermute | solution.py:646
  488.9 9.0 %collective-permute-start.37 = (bf16[96,768]{1,0:T(8,128)(2,1)}, bf16[96,768]{1,0:T(8,128)(2,1)S(1)}, u32[]{:S(2)}, u32[]{:S(2)}) collective-permute-start(bf16[96,768]{1,0:T(8,128)(2,1)} %get-tuple-element.424), channel_id=1, source_target_pairs={{0,8},{2,10},{4,12},{6,14},{8,0},{10,2},{12,4},{14,6},{16,24},{18,... | collective-permute-start | bytes 442376 | tf_op jit(solution)/shard_map/ppermute | solution.py:646
  494.3 14.0 %collective-permute-start.35 = (bf16[192,768]{1,0:T(8,128)(2,1)}, bf16[192,768]{1,0:T(8,128)(2,1)S(1)}, u32[]{:S(2)}, u32[]{:S(2)}) collective-permute-start(bf16[192,768]{1,0:T(8,128)(2,1)} %get-tuple-element.422), channel_id=1, source_target_pairs={{0,2},{2,0},{4,6},{6,4},{8,10},{10,8},{12,14},{14,12},{16,18},{18,... | collective-permute-start | bytes 884744 | tf_op jit(solution)/shard_map/ppermute | solution.py:646
  495.8 12.5 %collective-permute-start.38 = (bf16[96,768]{1,0:T(8,128)(2,1)}, bf16[96,768]{1,0:T(8,128)(2,1)S(1)}, u32[]{:S(2)}, u32[]{:S(2)}) collective-permute-start(bf16[96,768]{1,0:T(8,128)(2,1)} %get-tuple-element.425), channel_id=1, source_target_pairs={{0,16},{2,18},{4,20},{6,22},{8,24},{10,26},{12,28},{14,30},{16,0},... | collective-permute-start | bytes 442376 | tf_op jit(solution)/shard_map/ppermute | solution.py:646
  496.1 20.6 %collective-permute-start.43 = (f32[1,2,48,768]{3,2,1,0:T(8,128)S(1)}, f32[1,2,48,768]{3,2,1,0:T(8,128)S(1)}, u32[]{:S(2)}, u32[]{:S(2)}) collective-permute-start(f32[1,2,48,768]{3,2,1,0:T(8,128)S(1)} %copy-done.26), channel_id=1, source_target_pairs={{0,1},{1,0},{2,3},{3,2},{4,5},{5,4},{6,7},{7,6},{8,9},{9,8},{10,11... | collective-permute-start | bytes 884744 | tf_op jit(solution)/shard_map/ppermute | solution.py:642
  498.0 10.3 %collective-permute-start.39 = (bf16[96,768]{1,0:T(8,128)(2,1)}, bf16[96,768]{1,0:T(8,128)(2,1)S(1)}, u32[]{:S(2)}, u32[]{:S(2)}) collective-permute-start(bf16[96,768]{1,0:T(8,128)(2,1)} %get-tuple-element.426), channel_id=1, source_target_pairs={{0,24},{2,26},{4,28},{6,30},{8,16},{10,18},{12,20},{14,22},{16,8},... | collective-permute-start | bytes 442376 | tf_op jit(solution)/shard_map/ppermute | solution.py:646
  508.3 8.5 %collective-permute-start.44 = (f32[1,2,48,768]{3,2,1,0:T(8,128)S(1)}, f32[1,2,48,768]{3,2,1,0:T(8,128)S(1)}, u32[]{:S(2)}, u32[]{:S(2)}) collective-permute-start(f32[1,2,48,768]{3,2,1,0:T(8,128)S(1)} %copy-done.27), channel_id=1, source_target_pairs={{0,1},{1,0},{2,3},{3,2},{4,5},{5,4},{6,7},{7,6},{8,9},{9,8},{10,11... | collective-permute-start | bytes 884744 | tf_op jit(solution)/shard_map/ppermute | solution.py:642
  512.0 9.9 %collective-permute-start.40 = (bf16[112,768]{1,0:T(8,128)(2,1)}, bf16[112,768]{1,0:T(8,128)(2,1)S(1)}, u32[]{:S(2)}, u32[]{:S(2)}) collective-permute-start(bf16[112,768]{1,0:T(8,128)(2,1)} %get-tuple-element.441), channel_id=1, source_target_pairs={{0,8},{2,10},{4,12},{6,14},{8,0},{10,2},{12,4},{14,6},{16,24},{18,... | collective-permute-start | bytes 516104 | tf_op jit(solution)/shard_map/ppermute | solution.py:646
  514.3 14.9 %collective-permute-start.41 = (bf16[112,768]{1,0:T(8,128)(2,1)}, bf16[112,768]{1,0:T(8,128)(2,1)S(1)}, u32[]{:S(2)}, u32[]{:S(2)}) collective-permute-start(bf16[112,768]{1,0:T(8,128)(2,1)} %get-tuple-element.442), channel_id=1, source_target_pairs={{0,16},{2,18},{4,20},{6,22},{8,24},{10,26},{12,28},{14,30},{16,0},... | collective-permute-start | bytes 516104 | tf_op jit(solution)/shard_map/ppermute | solution.py:646
  514.5 14.7 %collective-permute-start.42 = (bf16[112,768]{1,0:T(8,128)(2,1)}, bf16[112,768]{1,0:T(8,128)(2,1)S(1)}, u32[]{:S(2)}, u32[]{:S(2)}) collective-permute-start(bf16[112,768]{1,0:T(8,128)(2,1)} %get-tuple-element.443), channel_id=1, source_target_pairs={{0,24},{2,26},{4,28},{6,30},{8,16},{10,18},{12,20},{14,22},{16,8},... | collective-permute-start | bytes 516104 | tf_op jit(solution)/shard_map/ppermute | solution.py:646
  516.7 32.3 %copy-start.28 = (f32[1,2,48,768]{3,2,1,0:T(8,128)}, f32[1,2,48,768]{3,2,1,0:T(8,128)S(1)}, u32[]{:S(2)}) copy-start(f32[1,2,48,768]{3,2,1,0:T(8,128)S(1)} %collective-permute-done.43.refs_8_) | copy-start | bytes 884740
  516.7 32.3 %collective-permute-start.53 = (f32[2,2,48,768]{3,2,1,0:T(8,128)S(1)}, f32[2,2,48,768]{3,2,1,0:T(8,128)S(1)}, u32[]{:S(2)}, u32[]{:S(2)}) collective-permute-start(f32[2,2,48,768]{3,2,1,0:T(8,128)S(1)} %copy-done.15), channel_id=1, source_target_pairs={{0,1},{1,0},{2,3},{3,2},{4,5},{5,4},{6,7},{7,6},{8,9},{9,8},{10,11... | collective-permute-start | bytes 1769480 | tf_op jit(solution)/shard_map/ppermute | solution.py:642
  516.8 32.2 %copy-start.29 = (f32[1,2,48,768]{3,2,1,0:T(8,128)}, f32[1,2,48,768]{3,2,1,0:T(8,128)S(1)}, u32[]{:S(2)}) copy-start(f32[1,2,48,768]{3,2,1,0:T(8,128)S(1)} %collective-permute-done.44.refs_9_) | copy-start | bytes 884740
  531.9 1.3 collective-permute-start.45
  533.8 3.5 collective-permute-start.46
  534.5 3.5 collective-permute-start.47
  535.7 4.4 collective-permute-start.48
  540.1 5.1 collective-permute-start.49
  542.8 4.4 collective-permute-start.50
  543.0 5.3 collective-permute-start.51
  545.3 3.7 collective-permute-start.54
  545.3 3.7 collective-permute-start.55
  547.3 1.7 collective-permute-start.52
  (54 other events, 317.0 us)
Sparse Core Ops, SparseCore 0:
  13.4 174.2 all-gather.1

commit v12 on v11

--- a/solution.py
+++ b/solution.py
@@ -147,8 +147,20 @@
 
 
 def tile_scratch(count, weights):
-    blocks, _, rows, _ = weights.shape
+    blocks, rows = (weights.shape[0], weights.shape[2])
     return pltpu.VMEM((count, blocks, rows, blocks * rows), LOW)
+
+
+def mixer_tile(anys, cores, place, t, base, width):
+    if len(anys) == 2:
+        return anys[place].at[t]
+    return tile_of(anys[0], cores[place], base + t * width)
+
+
+def mixer_scratch(weights):
+    w = weights[0]
+    blocks, rows = (w.shape[1], w.shape[2]) if len(weights) == 2 else (w.shape[0], w.shape[2])
+    return [pltpu.VMEM((2, blocks, rows, blocks * rows), LOW)] * 2
 
 
 def swap_halves(value):
@@ -172,12 +184,11 @@
 def attention_forward_kernel(base, place_of, ins, anys, outs, w_a, w_b, mixed, bias, sems):
     resid, seg_col, seg_row, cosine, sine, gains = ins
     middle, query, keys, values, lse, pack = outs
-    (weights,) = anys
     width = resid.shape[1]
     half = width // 2
     cores = (place_of[0], 1 - place_of[0])
     copies = fetch(
-        [tile_of(weights, c, base + t * width) for t in range(2) for c in cores],
+        [mixer_tile(anys, cores, p, t, base, width) for t in range(2) for p in range(2)],
         [w.at[place] for w in (w_a, w_b) for place in range(2)],
         sems,
     )
@@ -235,10 +246,9 @@
         place,
         [(one, FULL)] + [(one, LOW)] * 3 + [((length, 128), FULL), ((2,) + one, LOW)],
         [resid, segments[:, None], segments[None, :], cosine, sine, gains],
-        [weights],
-        [
-            tile_scratch(2, weights),
-            tile_scratch(2, weights),
+        weights,
+        mixer_scratch(weights)
+        + [
             pltpu.VMEM(one, FULL),
             pltpu.VMEM((length, length), FULL),
             pltpu.SemaphoreType.DMA((4,)),
@@ -251,15 +261,17 @@
 GELU_CUBE = 0.044715
 
 
-def fetch_hidden(weights, base, order, ups, downs, sems):
+def fetch_hidden(weights, base, order, ups, downs, sems, between=lambda t: None, down_first=False):
     blocks, _, rows, _ = weights.shape
     width = blocks * rows
     half, some = width // 2, max(blocks // 4, 1)
     copies = {}
     for t, (core_of, within) in enumerate(order):
-        copies[0, t] = fetch(
+        up = lambda: fetch(
             [tile_of(weights, core_of, base + (2 + within) * width)], [ups.at[t]], sems, t
         )
+        if not down_first:
+            copies[0, t] = up()
         if blocks >= 4 or t == 0:
             sources, targets = [], []
             first = (2 * core_of + within) * some if blocks >= 4 else 0
@@ -271,6 +283,9 @@
                         downs.at[pl.ds(t * some, some), j, :, core * half : (core + 1) * half]
                     )
             copies[1, t] = fetch(sources, targets, sems, 4 + 8 * t)
+        between(t)
+        if down_first:
+            copies[0, t] = up()
 
     def wait(which, t):
         for copy in copies.pop((which, t), []):
@@ -339,10 +354,13 @@
     hidden, weights = anys
     grad_middle, grad_gains, grad_own, grad_other = outs
     order = [(core, t) for core in (place_of[0], 1 - place_of[0]) for t in range(2)]
-    wait = fetch_hidden(weights, base, order, ups, downs, sems)
-    copies = fetch(
-        [hidden.at[2 * core + t] for core, t in order], [hidden_here.at[t] for t in range(4)], own_sems
-    )
+    copies = []
+
+    def fetch_values(t):
+        source = hidden.at[2 * order[t][0] + order[t][1]]
+        copies.extend(fetch([source], [hidden_here.at[t]], own_sems, t))
+
+    wait = fetch_hidden(weights, base, order, ups, downs, sems, fetch_values, down_first=True)
     for t in range(4):
         wait(1, t)
         grad_active = dot_nt(branch[...], rows_of(downs, t, order))
@@ -385,13 +403,12 @@
 
 def attention_back_kernel(base, place_of, ins, anys, outs, w_a, w_b, bias, ga, gq, gk, gv, sems):
     grad_middle, query, keys, values, lse, seg_col, seg_row, cosine, sine, gains, resid = ins
-    (weights,) = anys
     grad, branch, branch_own, branch_other, grad_gains, grad_own, grad_other = outs
     width = resid.shape[1]
     half = width // 2
     cores = (place_of[0], 1 - place_of[0])
     copies = fetch(
-        [tile_of(weights, c, base + t * width) for t in (1, 0) for c in cores],
+        [mixer_tile(anys, cores, p, t, base, width) for t in (1, 0) for p in range(2)],
         [w.at[place] for w in (w_b, w_a) for place in range(2)],
         sems,
     )
@@ -467,10 +484,9 @@
         + [((2,) + one, LOW)] * 2,
         [grad_middle, query, keys, values, lse.T[: width // HD]]
         + [segments[:, None], segments[None, :], cosine, sine, gains, resid],
-        [weights],
-        [
-            tile_scratch(2, weights),
-            tile_scratch(2, weights),
+        weights,
+        mixer_scratch(weights)
+        + [
             pltpu.VMEM((length, length), FULL),
         ]
         + [pltpu.VMEM(one, LOW)] * 4
@@ -620,21 +636,31 @@
 
 def pack_kernel(layers, place_of, ins, anys, outs):
     inward, outward, expand, shrink, small = ins
-    (out,) = outs
+    out, *early = outs
     first = place_of[0] == 0
     rows = inward.shape[1]
     width = inward.shape[2] // 3
     half = width // 2
-    at = small.shape[1]
-    out[:, :at] = small[...]
+    at = 0
+    if early:
+        early[0][rows : rows + 16] = jnp.zeros((16, width), LOW)
+        for q in range(rows // 16):
+            early[0][rows : rows + 16, q * SMALL : (q + 1) * SMALL] = small[q * 16 : (q + 1) * 16]
+    else:
+        at = small.shape[1]
+        out[:, :at] = small[...]
     for l in range(layers):
         sources = [inward[l, :, p * width : (p + 1) * width] for p in range(3)] + [outward[l]]
         sources.append(expand[l])
         sources += [shrink[l, j * rows : (j + 1) * rows] for j in range(shrink.shape[1] // rows)]
-        for value in sources:
+        for n, value in enumerate(sources):
             part = value.shape[1] // 2
-            value = jnp.where(first, value[:, :part], value[:, part:])
-            out[:, at : at + part] = value.astype(LOW)
+            value = jnp.where(first, value[:, :part], value[:, part:]).astype(LOW)
+            if early and l == 0 and n < 4:
+                start = 0 if n < 2 else rows + 16
+                early[0][start : start + rows, (n % 2) * half : (n % 2 + 1) * half] = value
+                continue
+            out[:, at : at + part] = value
             at += part
 
 
@@ -661,6 +687,69 @@
             value = value + across(value, bit, size)
         bit *= 4
     return value
+
+
+def arrange_kernel(parts, place_of, ins, anys, outs, sems):
+    copies, at = [], 0
+    for h in range(2):
+        for piece in anys:
+            copies += fetch(
+                [piece.at[h * parts[0] : h * parts[0] + parts[h]]],
+                [outs[0].at[at : at + parts[h]]],
+                sems,
+                len(copies),
+            )
+            at += parts[h]
+    for copy in copies:
+        copy.wait()
+
+
+def place_kernel(parts, rows, place_of, ins, anys, outs, sems):
+    quarter, from_x, from_y, far_a, far_b = anys
+    tiles, small = outs
+    x, y, z = place_of[1], place_of[2], place_of[3]
+    for n in range(16):
+        xor_z, xor_y, xor_x = n // 4, n // 2 % 2, n % 2
+        index = jnp.bitwise_xor(z, xor_z) * 4 + jnp.bitwise_xor(y, xor_y) * 2 + jnp.bitwise_xor(x, xor_x)
+        for h in range(2):
+            at = xor_z * parts[h]
+            if xor_x and xor_y:
+                source = (far_a, far_b)[h]
+            else:
+                source = from_x if xor_x else from_y if xor_y else quarter
+                at += h * 4 * parts[0]
+            fetch([source.at[at : at + rows]], [tiles.at[h, index]], sems, h)
+            if h == 0:
+                fetch([source.at[at + rows : at + parts[0]]], [small.at[index]], sems, 2)
+    for n, target in enumerate((tiles.at[0], tiles.at[1], small)):
+        pltpu.make_async_copy(target, target, sems.at[n]).wait()
+
+
+def gather_first(place, shard, rows, width):
+    parts = (rows + 16, rows)
+    got = [across(shard, mask, 16) for mask in Z]
+    (quarter,) = call(
+        functools.partial(arrange_kernel, parts),
+        place,
+        [((4 * sum(parts), width), LOW)],
+        [],
+        [shard] + got,
+        [pltpu.SemaphoreType.DMA((8,))],
+    )
+    from_x, from_y = across(quarter, X, 16), across(quarter, Y, 16)
+    cut = 4 * parts[0]
+    far_a, far_b = across(from_y[:cut], X, 16), across(from_x[cut:], Y, 16)
+    own, small = call(
+        functools.partial(place_kernel, parts, rows),
+        place,
+        [((2, 16, rows, width), LOW), ((16, 16, width), LOW)],
+        [],
+        [quarter, from_x, from_y, far_a, far_b],
+        [pltpu.SemaphoreType.DMA((3,))],
+    )
+    small = small[:, :, : rows // 16 * SMALL].reshape(16, 16, rows // 16, SMALL)
+    small = small.transpose(0, 2, 1, 3).reshape(width, SMALL)
+    return [own, swap_cores(own)], small
 
 
 X, Y = 1, 2
@@ -1028,10 +1117,14 @@
         [codon_table.astype(LOW), norm_params.astype(LOW).reshape(norms, rows)], 0
     )
     small = jnp.pad(small.T, ((0, 0), (0, -small.shape[0] % 128)))
-    (weights,) = call(
+    columns = small.shape[1] + layers * 6 * width
+    shapes = [(rows, columns)]
+    if fast:
+        shapes = [(rows, layers * 6 * width - 2 * width), (2 * rows + 16, width)]
+    weights, *early = call(
         functools.partial(pack_kernel, layers),
         place,
-        [((rows, small.shape[1] + layers * 6 * width), LOW)],
+        [(shape, LOW) for shape in shapes],
         [inward, outward, expand, shrink, small],
     )
     weights = lax.all_gather(weights, ("fsdp", "dp"), axis=0, tiled=True)
@@ -1045,7 +1138,12 @@
             quarter = quarter.reshape(2, 4, width, half).transpose(0, 2, 1, 3)
             columns.append(quarter.reshape(2, fsdp, rows, 2 * width).transpose(1, 0, 2, 3))
         weights = jnp.concatenate(columns, 3).transpose(1, 0, 2, 3).reshape(1, 2, width, -1)
-    small = weights[:, 0, :, :SMALL].reshape(width, SMALL).T
+    mixers = [[weights]] * layers
+    if fast:
+        mixers[0], small = gather_first(place, early[0], rows, width)
+        small = small.T
+    else:
+        small = weights[:, 0, :, :SMALL].reshape(width, SMALL).T
     base = lambda l: weights.shape[3] - (layers - l) * 6 * width
     gains = small[V : V + norms].astype(FULL).reshape(-1, 2, width)
 
@@ -1056,7 +1154,7 @@
     for l in range(layers):
         gain = gains[2 * l : 2 * l + 2]
         middle, query, keys, values, lse, pack = attention_forward(
-            place, resid, weights, base(l), gain[0], cosine, sine, segments
+            place, resid, mixers[l], base(l), gain[0], cosine, sine, segments
         )
         output, pack_mid, hidden = hidden_forward(place, middle, weights, base(l), gain[1])
         kept.append((resid, query, keys, values, lse, pack, middle, hidden, pack_mid))
@@ -1113,7 +1211,7 @@
             grad_middle,
         )
         grad, branch, branch_own, branch_other, gains_in, mix_own, mix_other = attention_back(
-            place, grad_middle, resid, weights, base(l), gain[0], cosine, sine, segments,
+            place, grad_middle, resid, mixers[l], base(l), gain[0], cosine, sine, segments,
             query, keys, values, lse,
         )
         grad_norms = [gains_in, gains_mid] + grad_norms

time: 577 us -> 553 us (0.958)
  waiting for transfers between devices: 246 us -> 204 us
  starting transfers between devices: 52.1 us -> 62.8 us
    all_gather x1, waiting for transfers between devices: 171 us -> 84.4 us  [body(): weights = lax.all_gather(weights, ('fsdp', 'dp'), axis=0, tiled=True)]
    ppermute x33 -> x40, waiting for transfers between devices: 56.4 us -> 101 us  [across(): return lax.ppermute(value, 'fsdp', [(i, i ^ mask) for i in range(size)])]
    ppermute x33 -> x40, starting transfers between devices: 47.6 us -> 58.2 us  [across(): return lax.ppermute(value, 'fsdp', [(i, i ^ mask) for i in range(size)])]
    unnamed x122 -> x140, local copies, waits for them, and re-layouts: 10.7 us -> 14.5 us
    pallas_call x19 -> x21, Pallas kernels: 229 us -> 232 us  [call(): pl.pallas_call(body, out_shape=[jax.ShapeDtypeStruct(s, t) for s, t in ou...]
    ppermute x23 -> x24, waiting for transfers between devices: 18.2 us -> 18.2 us  [swap_cores(): return lax.ppermute(value, 'dp', [(0, 1), (1, 0)])]
  transfers between devices with their start and end apart: 57 -> 65, of which waited for: 22 -> 28; matrix products, arithmetic and copies ran while one was open for 2% -> 2% of each run, Pallas kernels for 20% -> 24%
where the time goes in v12:
time: 553 us; the launch traced here: 543 us
  Pallas kernels  232 us (42%)
  waiting for transfers between devices  204 us (37%)
  starting transfers between devices  62.8 us (11%)
  local copies, waits for them, and re-layouts  22.4 us (4%)
  between operations  15.2 us (3%)
    pallas_call x21, Pallas kernels, call(): pl.pallas_call(body, out_shape=[jax.ShapeDtypeStruct(s, t) for s, t in ou...  232 us
    ppermute x40, waiting for transfers between devices, across(): return lax.ppermute(value, 'fsdp', [(i, i ^ mask) for i in range(size)])  101 us
    all_gather x1, waiting for transfers between devices, body(): weights = lax.all_gather(weights, ('fsdp', 'dp'), axis=0, tiled=True)  84.4 us
    ppermute x40, starting transfers between devices, across(): return lax.ppermute(value, 'fsdp', [(i, i ^ mask) for i in range(size)])  58.2 us
    ppermute x24, waiting for transfers between devices, swap_cores(): return lax.ppermute(value, 'dp', [(0, 1), (1, 0)])  18.2 us
    unnamed x140, local copies, waits for them, and re-layouts  14.5 us
  transfers between devices with their start and end apart: 65, of which 28 were waited for; matrix products, arithmetic and copies ran while one was open for 2% of the time, Pallas kernels for 24%

profile of v12, /device:TPU:0, one launch (start us, length us, event | category | flops | bytes accessed | tf_op | source)
XLA Modules:
  0.0 543.5 jit_solution(10862124263831193330)
XLA Ops:
  10.1 3.0 shard_map.364
  13.1 3.1 collective-permute-start
  16.2 2.6 collective-permute-start.1
  18.8 4.7 collective-permute-done.refs_1_
  23.5 13.3 %collective-permute-done.1.refs_2_ = bf16[112,768]{1,0:T(8,128)(2,1)S(1)} collective-permute-done((bf16[112,768]{1,0:T(8,128)(2,1)}, bf16[112,768]{1,0:T(8,128)(2,1)S(1)}, u32[]{:S(2)}, u32[]{:S(2)}) %collective-permute-start.1) | collective-permute-done | bytes 172064 | tf_op jit(solution)/shard_map/ppermute | solution.py:672
  38.1 2.8 shard_map.365.refs_0_
  40.9 1.6 collective-permute-start.4
  42.5 1.5 collective-permute-start.3
  44.0 11.3 %collective-permute-done.4.refs_2_ = bf16[448,768]{1,0:T(8,128)(2,1)S(1)} collective-permute-done((bf16[448,768]{1,0:T(8,128)(2,1)}, bf16[448,768]{1,0:T(8,128)(2,1)S(1)}, u32[]{:S(2)}, u32[]{:S(2)}) %collective-permute-start.4) | collective-permute-done | bytes 688160 | tf_op jit(solution)/shard_map/ppermute | solution.py:672
  55.3 1.6 collective-permute-start.5
  58.5 12.3 %collective-permute-done.6.refs_4_ = bf16[192,768]{1,0:T(8,128)(2,1)S(1)} collective-permute-done((bf16[192,768]{1,0:T(8,128)(2,1)S(1)}, bf16[192,768]{1,0:T(8,128)(2,1)S(1)}, u32[]{:S(2)}, u32[]{:S(2)}) %collective-permute-start.6) | collective-permute-done | bytes 294944 | tf_op jit(solution)/shard_map/ppermute | solution.py:672
  72.3 4.1 shard_map.366
  80.6 1.6 fusion.3.refs_0_.refs_10_
  82.2 1.5 copy-done.68
  83.7 14.4 %shard_map.367 = (f32[512,768]{1,0:T(8,128)}, bf16[512,768]{1,0:T(8,128)(2,1)}, bf16[512,768]{1,0:T(8,128)(2,1)}, bf16[512,768]{1,0:T(8,128)(2,1)}, f32[512,128]{1,0:T(8,128)}, /*index=5*/bf16[2,512,768]{2,1,0:T(8,128)(2,1)}) custom-call(s32[4]{0:T(128)} %pad_add_fusion.scalars, f32[512,768]{1,0:T(8,128)} %fusion.3.refs_0_.refs_10_, ...), custom_call_target="tpu_custom_call" | custom-call | flops 3221225472 | bytes 6825984 | tf_op jit(solution)/shard_map/pallas_call | solution.py:111
  98.1 84.4 %all-gather.2.cloned.1.call-done = bf16[1536,7680]{1,0:T(8,128)(2,1)} async-done(((bf16[48,7680]{1,0:T(8,128)(2,1)}), bf16[1536,7680]{1,0:T(8,128)(2,1)}) %all-gather.2.cloned.1.call-update) | async-done | bytes 23592976 | tf_op jit(solution)/shard_map/all_gather | solution.py:1130
  182.5 12.7 %shard_map.368 = (f32[512,768]{1,0:T(8,128)}, bf16[5,512,768]{2,1,0:T(8,128)(2,1)}, f32[4,512,768]{2,1,0:T(8,128)}) custom-call(s32[4]{0:T(128)} %pad_add_fusion.scalars, f32[512,768]{1,0:T(8,128)} %get-tuple-element.257.refs_0_.refs_2_, f32[2,768]{1,0:T(2,128)} %get-tuple-element.488.refs_1_.refs_3_, bf16[16,2,48,7680]{3,2,1,0:T(8,128)(2,1)} %bitcast.26), custom_call_target="tpu_custom_call" | custom-call | flops 4831838208 | bytes 25171968 | tf_op jit(solution)/shard_map/pallas_call | solution.py:111
  195.2 14.2 %shard_map.369 = (f32[512,768]{1,0:T(8,128)}, bf16[512,768]{1,0:T(8,128)(2,1)}, bf16[512,768]{1,0:T(8,128)(2,1)}, bf16[512,768]{1,0:T(8,128)(2,1)}, f32[512,128]{1,0:T(8,128)}, /*index=5*/bf16[2,512,768]{2,1,0:T(8,128)(2,1)}) custom-call(s32[4]{0:T(128)} %pad_add_fusion.scalars, f32[512,768]{1,0:T(8,128)} %get-tuple-element.260.refs_0_.refs_10_, ...), custom_call_target="tpu_custom_call" | custom-call | flops 3221225472 | bytes 25700352 | tf_op jit(solution)/shard_map/pallas_call | solution.py:111
  209.4 12.7 %shard_map.370 = (f32[512,768]{1,0:T(8,128)}, bf16[5,512,768]{2,1,0:T(8,128)(2,1)}, f32[4,512,768]{2,1,0:T(8,128)}) custom-call(s32[4]{0:T(128)} %pad_add_fusion.scalars, f32[512,768]{1,0:T(8,128)} %get-tuple-element.262.refs_0_.refs_2_, f32[2,768]{1,0:T(2,128)} %get-tuple-element.486.refs_1_.refs_3_, bf16[16,2,48,7680]{3,2,1,0:T(8,128)(2,1)} %bitcast.28), custom_call_target="tpu_custom_call" | custom-call | flops 4831838208 | bytes 25171968 | tf_op jit(solution)/shard_map/pallas_call | solution.py:111
  224.1 5.8 %shard_map.371 = (f32[512,768]{1,0:T(8,128)}, bf16[512,768]{1,0:T(8,128)(2,1)}, bf16[512,384]{1,0:T(8,128)(2,1)}, bf16[512,384]{1,0:T(8,128)(2,1)}, bf16[512,768...) custom-call(s32[4]{0:T(128)} %pad_add_fusion.scalars, ...), custom_call_target="tpu_custom_call" | custom-call | flops 201326592 | bytes 1779712 | tf_op jit(solution)/shard_map/pallas_call | solution.py:111
  232.7 8.8 %shard_map.372 = (bf16[384,768]{1,0:T(8,128)(2,1)}, bf16[384,768]{1,0:T(8,128)(2,1)}, f32[1,2,384,768]{3,2,1,0:T(8,128)}) custom-call(s32[4]{0:T(128)} %pad_add_fusion.scalars, bf16[5,512,768]{2,1,0:T(8,128)(2,1)} %get-tuple-element.263.refs_0_, bf16[512,384]{1,0:T(8,128)(2,1)} %get-tuple-element.265.refs_1_, ...), custom_call_target="tpu_custom_call" | custom-call | flops 2415919104 | bytes 8650752 | tf_op jit(solution)/shard_map/pallas_call | solution.py:111
  241.4 1.4 collective-permute-start.10
  245.2 17.9 %shard_map.373 = (f32[512,768]{1,0:T(8,128)}, f32[2,768]{1,0:T(2,128)}, bf16[2,512,768]{2,1,0:T(8,128)(2,1)}, bf16[2,512,768]{2,1,0:T(8,128)(2,1)}) custom-call(s32[4]{0:T(128)} %pad_add_fusion.scalars, bf16[512,768]{1,0:T(8,128)(2,1)} %get-tuple-element.277.refs_0_, f32[512,768]{1,0:T(8,128)} %get-tuple-element.278.refs_1_, ...), custom_call_target="tpu_custom_call" | custom-call | flops 4831838208 | bytes 33822720 | tf_op jit(solution)/shard_map/pallas_call | solution.py:111
  265.0 3.5 collective-permute-done.15.refs_3_
  269.6 10.2 %shard_map.374 = (bf16[576,768]{1,0:T(8,128)(2,1)}, bf16[576,768]{1,0:T(8,128)(2,1)}, f32[1,2,384,768]{3,2,1,0:T(8,128)}, f32[1,2,192,768]{3,2,1,0:T(8,128)}) custom-call(s32[4]{0:T(128)} %pad_add_fusion.scalars, bf16[5,512,768]{2,1,0:T(8,128)(2,1)} %get-tuple-element.263.refs_0_, bf16[2,512,768]{2,1,0:T(8,128)(2,1)} %get-tuple-element.285.refs_1_, ...), custom_call_target="tpu_custom_call" | custom-call | flops 2415919104 | bytes 14548992 | tf_op jit(solution)/shard_map/pallas_call | solution.py:111
  279.8 1.5 collective-permute-start.16
  283.6 22.2 %shard_map.375 = (f32[512,768]{1,0:T(8,128)}, bf16[512,768]{1,0:T(8,128)(2,1)}, bf16[512,384]{1,0:T(8,128)(2,1)}, bf16[512,384]{1,0:T(8,128)(2,1)}, f32[2,768]{1...) custom-call(s32[4]{0:T(128)} %pad_add_fusion.scalars, f32[512,768]{1,0:T(8,128)} %get-tuple-element.297.refs_0_, ...), custom_call_target="tpu_custom_call" | custom-call | flops 4429185024 | bytes 29657088 | tf_op jit(solution)/shard_map/pallas_call | solution.py:111
  306.4 3.7 collective-permute-done.22.refs_7_
  312.0 17.2 %shard_map.376 = (bf16[960,768]{1,0:T(8,128)(2,1)}, bf16[960,768]{1,0:T(8,128)(2,1)}, f32[2,2,384,768]{3,2,1,0:T(8,128)}, f32[1,2,192,768]{3,2,1,0:T(8,128)}, f3...) custom-call(s32[4]{0:T(128)} %pad_add_fusion.scalars, ...), custom_call_target="tpu_custom_call" | custom-call | flops 4831838208 | bytes 20250624 | tf_op jit(solution)/shard_map/pallas_call | solution.py:111
  329.2 1.4 collective-permute-start.23
  331.3 1.9 collective-permute-start.26
  333.2 2.4 collective-permute-start.27
  335.6 17.4 %shard_map.377 = (f32[512,768]{1,0:T(8,128)}, f32[2,768]{1,0:T(2,128)}, bf16[2,512,768]{2,1,0:T(8,128)(2,1)}, bf16[2,512,768]{2,1,0:T(8,128)(2,1)}) custom-call(s32[4]{0:T(128)} %pad_add_fusion.scalars, bf16[512,768]{1,0:T(8,128)(2,1)} %get-tuple-element.333.refs_0_, f32[512,768]{1,0:T(8,128)} %get-tuple-element.334.refs_1_, ...), custom_call_target="tpu_custom_call" | custom-call | flops 4831838208 | bytes 33822720 | tf_op jit(solution)/shard_map/pallas_call | solution.py:111
  353.1 10.7 %collective-permute-done.23.refs_6_ = bf16[960,768]{1,0:T(8,128)(2,1)S(1)} collective-permute-done((bf16[960,768]{1,0:T(8,128)(2,1)}, bf16[960,768]{1,0:T(8,128)(2,1)S(1)}, u32[]{:S(2)}, u32[]{:S(2)}) %collective-permute-start.23) | collective-permute-done | bytes 1474592 | tf_op jit(solution)/shard_map/ppermute | solution.py:672
  364.9 3.6 collective-permute-done.28.refs_3_
  369.7 13.4 %shard_map.378 = (bf16[768,768]{1,0:T(8,128)(2,1)}, bf16[768,768]{1,0:T(8,128)(2,1)}, f32[1,2,384,768]{3,2,1,0:T(8,128)}, f32[2,2,192,768]{3,2,1,0:T(8,128)}, f3...) custom-call(s32[4]{0:T(128)} %pad_add_fusion.scalars, ...), custom_call_target="tpu_custom_call" | custom-call | flops 2415919104 | bytes 20597760 | tf_op jit(solution)/shard_map/pallas_call | solution.py:111
  386.0 1.9 collective-permute-start.32
  387.9 2.4 collective-permute-start.33
  390.4 22.1 %shard_map.379 = (f32[512,768]{1,0:T(8,128)}, bf16[512,768]{1,0:T(8,128)(2,1)}, bf16[512,384]{1,0:T(8,128)(2,1)}, bf16[512,384]{1,0:T(8,128)(2,1)}, f32[2,768]{1...) custom-call(s32[4]{0:T(128)} %pad_add_fusion.scalars, f32[512,768]{1,0:T(8,128)} %get-tuple-element.366.refs_0_, ...), custom_call_target="tpu_custom_call" | custom-call | flops 4429185024 | bytes 10782720 | tf_op jit(solution)/shard_map/pallas_call | solution.py:111
  413.8 2.3 collective-permute-done.37.refs_15_
  418.9 13.1 %shard_map.380 = (bf16[640,768]{1,0:T(8,128)(2,1)}, bf16[576,768]{1,0:T(8,128)(2,1)}, f32[1,2,384,768]{3,2,1,0:T(8,128)}, f32[384,128]{1,0:T(8,128)}, f32[1,2,19...) custom-call(s32[4]{0:T(128)} %pad_add_fusion.scalars, ...), custom_call_target="tpu_custom_call" | custom-call | flops 2415919104 | bytes 17841152 | tf_op jit(solution)/shard_map/pallas_call | solution.py:111
  432.6 1.4 collective-permute-start.39
  434.0 1.9 collective-permute-start.41
  436.0 2.4 collective-permute-start.42
  438.4 9.7 %collective-permute-done.40.refs_6_ = bf16[192,768]{1,0:T(8,128)(2,1)S(1)} collective-permute-done((bf16[192,768]{1,0:T(8,128)(2,1)}, bf16[192,768]{1,0:T(8,128)(2,1)S(1)}, u32[]{:S(2)}, u32[]{:S(2)}) %collective-permute-start.40) | collective-permute-done | bytes 294944 | tf_op jit(solution)/shard_map/ppermute | solution.py:672
  448.1 9.6 %collective-permute-done.41.refs_7_ = bf16[192,768]{1,0:T(8,128)(2,1)S(1)} collective-permute-done((bf16[192,768]{1,0:T(8,128)(2,1)}, bf16[192,768]{1,0:T(8,128)(2,1)S(1)}, u32[]{:S(2)}, u32[]{:S(2)}) %collective-permute-start.41) | collective-permute-done | bytes 294944 | tf_op jit(solution)/shard_map/ppermute | solution.py:672
  459.1 4.9 shard_map.381
  464.7 5.4 collective-permute-start.45
  470.1 1.5 collective-permute-start.43
  471.9 1.9 collective-permute-done.45.refs_5_
  473.7 2.7 collective-permute-start.47
  476.4 7.7 %collective-permute-done.46.refs_6_ = bf16[96,768]{1,0:T(8,128)(2,1)S(1)} collective-permute-done((bf16[96,768]{1,0:T(8,128)(2,1)}, bf16[96,768]{1,0:T(8,128)(2,1)S(1)}, u32[]{:S(2)}, u32[]{:S(2)}) %collective-permute-start.46) | collective-permute-done | bytes 147488 | tf_op jit(solution)/shard_map/ppermute | solution.py:672
  485.1 2.8 shard_map.382
  487.8 2.1 collective-permute-start.48
  490.2 2.2 collective-permute-start.50
  492.5 5.2 collective-permute-done.48.refs_2_
  497.7 7.2 %collective-permute-done.49.refs_3_ = bf16[112,768]{1,0:T(8,128)(2,1)S(1)} collective-permute-done((bf16[112,768]{1,0:T(8,128)(2,1)}, bf16[112,768]{1,0:T(8,128)(2,1)S(1)}, u32[]{:S(2)}, u32[]{:S(2)}) %collective-permute-start.49) | collective-permute-done | bytes 172064 | tf_op jit(solution)/shard_map/ppermute | solution.py:672
  505.7 2.0 shard_map.383
  511.5 1.6 collective-permute-start.56
  513.8 2.1 collective-permute-done.56
  516.0 2.6 collective-permute-start.57
  518.8 2.2 collective-permute-start.59
  521.5 1.5 collective-permute-done.58
  525.8 10.6 %shard_map.384 = (f32[1,1]{1,0:T(1,128)}, f32[2,48,2304]{2,1,0:T(8,128)}, f32[2,48,2304]{2,1,0:T(8,128)}, f32[2,48,2304]{2,1,0:T(8,128)}, f32[2,48,768]{2,1,0:T(...) custom-call(s32[4]{0:T(128)} %pad_add_fusion.scalars, ...), custom_call_target="tpu_custom_call" | custom-call | flops 53314560 | bytes 14251520 | tf_op jit(solution)/shard_map/pallas_call | solution.py:111
  (262 shorter events, 48.8 us)
Async XLA Ops:
  7.2 175.3 %all-gather.2.cloned.1.call-start = ((), (), s32[]{:S(2)}) async-start(), calls=%async_computation | async-start | bytes 24330240 | tf_op jit(solution)/shard_map/all_gather | solution.py:1130
  13.1 10.4 %collective-permute-start = (bf16[112,768]{1,0:T(8,128)(2,1)}, bf16[112,768]{1,0:T(8,128)(2,1)S(1)}, u32[]{:S(2)}, u32[]{:S(2)}) collective-permute-start(bf16[112,768]{1,0:T(8,128)(2,1)} %get-tuple-element.253.refs_0_), channel_id=1, source_target_pairs={{0,8},{2,10},{4,12},{6,14},{8,0},{10,2},{12,4},{14,6},{16,24},{18,... | collective-permute-start | bytes 516104 | tf_op jit(solution)/shard_map/ppermute | solution.py:672
  16.2 20.6 %collective-permute-start.1 = (bf16[112,768]{1,0:T(8,128)(2,1)}, bf16[112,768]{1,0:T(8,128)(2,1)S(1)}, u32[]{:S(2)}, u32[]{:S(2)}) collective-permute-start(bf16[112,768]{1,0:T(8,128)(2,1)} %get-tuple-element.253.refs_0_), channel_id=1, source_target_pairs={{0,16},{2,18},{4,20},{6,22},{8,24},{10,26},{12,28},{14,30},{16,0},... | collective-permute-start | bytes 516104 | tf_op jit(solution)/shard_map/ppermute | solution.py:672
  18.8 18.0 %collective-permute-start.2 = (bf16[112,768]{1,0:T(8,128)(2,1)}, bf16[112,768]{1,0:T(8,128)(2,1)S(1)}, u32[]{:S(2)}, u32[]{:S(2)}) collective-permute-start(bf16[112,768]{1,0:T(8,128)(2,1)} %get-tuple-element.253.refs_0_), channel_id=1, source_target_pairs={{0,24},{2,26},{4,28},{6,30},{8,16},{10,18},{12,20},{14,22},{16,8},... | collective-permute-start | bytes 516104 | tf_op jit(solution)/shard_map/ppermute | solution.py:672
  40.9 14.4 %collective-permute-start.4 = (bf16[448,768]{1,0:T(8,128)(2,1)}, bf16[448,768]{1,0:T(8,128)(2,1)S(1)}, u32[]{:S(2)}, u32[]{:S(2)}) collective-permute-start(bf16[448,768]{1,0:T(8,128)(2,1)} %shard_map.365.refs_0_), channel_id=1, source_target_pairs={{0,4},{2,6},{4,0},{6,2},{8,12},{10,14},{12,8},{14,10},{16,20},{18,... | collective-permute-start | bytes 2064392 | tf_op jit(solution)/shard_map/ppermute | solution.py:672
  42.5 15.2 %collective-permute-start.3 = (bf16[448,768]{1,0:T(8,128)(2,1)}, bf16[448,768]{1,0:T(8,128)(2,1)S(1)}, u32[]{:S(2)}, u32[]{:S(2)}) collective-permute-start(bf16[448,768]{1,0:T(8,128)(2,1)} %shard_map.365.refs_0_), channel_id=1, source_target_pairs={{0,2},{2,0},{4,6},{6,4},{8,10},{10,8},{12,14},{14,12},{16,18},{18,... | collective-permute-start | bytes 2064392 | tf_op jit(solution)/shard_map/ppermute | solution.py:672
  55.3 15.9 %collective-permute-start.5 = (bf16[256,768]{1,0:T(8,128)(2,1)S(1)}, bf16[256,768]{1,0:T(8,128)(2,1)S(1)}, u32[]{:S(2)}, u32[]{:S(2)}) collective-permute-start(bf16[256,768]{1,0:T(8,128)(2,1)S(1)} %slice.71), channel_id=1, source_target_pairs={{0,2},{2,0},{4,6},{6,4},{8,10},{10,8},{12,14},{14,12},{16,18},{18,... | collective-permute-start | bytes 1179656 | tf_op jit(solution)/shard_map/ppermute | solution.py:672
  57.7 13.1 %collective-permute-start.6 = (bf16[192,768]{1,0:T(8,128)(2,1)S(1)}, bf16[192,768]{1,0:T(8,128)(2,1)S(1)}, u32[]{:S(2)}, u32[]{:S(2)}) collective-permute-start(bf16[192,768]{1,0:T(8,128)(2,1)S(1)} %slice.72), channel_id=1, source_target_pairs={{0,4},{2,6},{4,0},{6,2},{8,12},{10,14},{12,8},{14,10},{16,20},{18,... | collective-permute-start | bytes 884744 | tf_op jit(solution)/shard_map/ppermute | solution.py:672
  76.4 5.8 %collective-permute-start.7 = (bf16[2,16,48,768]{3,2,1,0:T(8,128)(2,1)}, bf16[2,16,48,768]{3,2,1,0:T(8,128)(2,1)S(1)}, u32[]{:S(2)}, u32[]{:S(2)}) collective-permute-start(bf16[2,16,48,768]{3,2,1,0:T(8,128)(2,1)} %get-tuple-element.255.refs_6_.refs_11_), channel_id=1, source_target_pairs={{0,1},{1,0},{2,3},{3,2},{4,5},{5,4},{6,7},{7,6},{8,9},{9,8},{10,11... | collective-permute-start | bytes 7077896 | tf_op jit(solution)/shard_map/ppermute | solution.py:668
  222.1 8.6 %collective-permute-start.8 = (bf16[5,512,768]{2,1,0:T(8,128)(2,1)}, bf16[5,512,768]{2,1,0:T(8,128)(2,1)}, u32[]{:S(2)}, u32[]{:S(2)}) collective-permute-start(bf16[5,512,768]{2,1,0:T(8,128)(2,1)} %get-tuple-element.263.refs_0_), channel_id=1, source_target_pairs={{0,1},{1,0},{2,3},{3,2},{4,5},{5,4},{6,7},{7,6},{8,9},{9,8},{10,11... | collective-permute-start | bytes 11796488 | tf_op jit(solution)/shard_map/ppermute | solution.py:668
  229.9 1.9 collective-permute-start.9
  230.2 75.6 %collective-permute-start.18 = (bf16[5,512,768]{2,1,0:T(8,128)(2,1)}, bf16[5,512,768]{2,1,0:T(8,128)(2,1)}, u32[]{:S(2)}, u32[]{:S(2)}) collective-permute-start(bf16[5,512,768]{2,1,0:T(8,128)(2,1)} %get-tuple-element.259.refs_4_.refs_0_), channel_id=1, source_target_pairs={{0,1},{1,0},{2,3},{3,2},{4,5},{5,4},{6,7},{7,6},{8,9},{9,8},{10,11... | collective-permute-start | bytes 11796488 | tf_op jit(solution)/shard_map/ppermute | solution.py:668
  230.4 32.7 %collective-permute-start.12 = (bf16[512,768]{1,0:T(8,128)(2,1)}, bf16[512,768]{1,0:T(8,128)(2,1)S(1)}, u32[]{:S(2)}, u32[]{:S(2)}) collective-permute-start(bf16[512,768]{1,0:T(8,128)(2,1)} %get-tuple-element.283.refs_4_), channel_id=1, source_target_pairs={{0,1},{1,0},{2,3},{3,2},{4,5},{5,4},{6,7},{7,6},{8,9},{9,8},{10,11... | collective-permute-start | bytes 2359304 | tf_op jit(solution)/shard_map/ppermute | solution.py:668
  241.4 21.7 %collective-permute-start.10 = (bf16[384,768]{1,0:T(8,128)(2,1)}, bf16[384,768]{1,0:T(8,128)(2,1)S(1)}, u32[]{:S(2)}, u32[]{:S(2)}) collective-permute-start(bf16[384,768]{1,0:T(8,128)(2,1)} %get-tuple-element.275), channel_id=1, source_target_pairs={{0,2},{2,0},{4,6},{6,4},{8,10},{10,8},{12,14},{14,12},{16,18},{18,... | collective-permute-start | bytes 1769480 | tf_op jit(solution)/shard_map/ppermute | solution.py:672
  242.8 20.3 %collective-permute-start.11 = (bf16[384,768]{1,0:T(8,128)(2,1)}, bf16[384,768]{1,0:T(8,128)(2,1)S(1)}, u32[]{:S(2)}, u32[]{:S(2)}) collective-permute-start(bf16[384,768]{1,0:T(8,128)(2,1)} %get-tuple-element.276), channel_id=1, source_target_pairs={{0,4},{2,6},{4,0},{6,2},{8,12},{10,14},{12,8},{14,10},{16,20},{18,... | collective-permute-start | bytes 1769480 | tf_op jit(solution)/shard_map/ppermute | solution.py:672
  243.6 1.4 collective-permute-start.14
  245.0 18.1 %collective-permute-start.13 = (bf16[512,128]{1,0:T(8,128)(2,1)S(1)}, bf16[512,128]{1,0:T(8,128)(2,1)S(1)}, u32[]{:S(2)}, u32[]{:S(2)}) collective-permute-start(bf16[512,128]{1,0:T(8,128)(2,1)S(1)} %copy-done.52), channel_id=1, source_target_pairs={{0,1},{1,0},{2,3},{3,2},{4,5},{5,4},{6,7},{7,6},{8,9},{9,8},{10,11... | collective-permute-start | bytes 393224 | tf_op jit(solution)/shard_map/ppermute | solution.py:668
  264.1 4.3 collective-permute-start.15
  264.5 41.3 %collective-permute-start.19 = (bf16[2,512,768]{2,1,0:T(8,128)(2,1)S(1)}, bf16[2,512,768]{2,1,0:T(8,128)(2,1)S(1)}, u32[]{:S(2)}, u32[]{:S(2)}) collective-permute-start(bf16[2,512,768]{2,1,0:T(8,128)(2,1)S(1)} %copy-done.1), channel_id=1, source_target_pairs={{0,1},{1,0},{2,3},{3,2},{4,5},{5,4},{6,7},{7,6},{8,9},{9,8},{10,11... | collective-permute-start | bytes 4718600 | tf_op jit(solution)/shard_map/ppermute | solution.py:668
  264.6 41.2 %collective-permute-start.20 = (bf16[2,512,768]{2,1,0:T(8,128)(2,1)}, bf16[2,512,768]{2,1,0:T(8,128)(2,1)}, u32[]{:S(2)}, u32[]{:S(2)}) collective-permute-start(bf16[2,512,768]{2,1,0:T(8,128)(2,1)} %get-tuple-element.261.refs_0_), channel_id=1, source_target_pairs={{0,1},{1,0},{2,3},{3,2},{4,5},{5,4},{6,7},{7,6},{8,9},{9,8},{10,11... | collective-permute-start | bytes 4718600 | tf_op jit(solution)/shard_map/ppermute | solution.py:668
  279.8 26.0 %collective-permute-start.16 = (bf16[576,768]{1,0:T(8,128)(2,1)}, bf16[576,768]{1,0:T(8,128)(2,1)}, u32[]{:S(2)}, u32[]{:S(2)}) collective-permute-start(bf16[576,768]{1,0:T(8,128)(2,1)} %get-tuple-element.295), channel_id=1, source_target_pairs={{0,2},{2,0},{4,6},{6,4},{8,10},{10,8},{12,14},{14,12},{16,18},{18,... | collective-permute-start | bytes 2654216 | tf_op jit(solution)/shard_map/ppermute | solution.py:672
  281.3 24.5 %collective-permute-start.17 = (bf16[576,768]{1,0:T(8,128)(2,1)}, bf16[576,768]{1,0:T(8,128)(2,1)}, u32[]{:S(2)}, u32[]{:S(2)}) collective-permute-start(bf16[576,768]{1,0:T(8,128)(2,1)} %get-tuple-element.296), channel_id=1, source_target_pairs={{0,4},{2,6},{4,0},{6,2},{8,12},{10,14},{12,8},{14,10},{16,20},{18,... | collective-permute-start | bytes 2654216 | tf_op jit(solution)/shard_map/ppermute | solution.py:672
  305.8 4.3 collective-permute-start.21
  305.9 4.2 collective-permute-start.22
  329.2 34.6 %collective-permute-start.23 = (bf16[960,768]{1,0:T(8,128)(2,1)}, bf16[960,768]{1,0:T(8,128)(2,1)S(1)}, u32[]{:S(2)}, u32[]{:S(2)}) collective-permute-start(bf16[960,768]{1,0:T(8,128)(2,1)} %get-tuple-element.328), channel_id=1, source_target_pairs={{0,2},{2,0},{4,6},{6,4},{8,10},{10,8},{12,14},{14,12},{16,18},{18,... | collective-permute-start | bytes 4423688 | tf_op jit(solution)/shard_map/ppermute | solution.py:672
  330.6 34.3 %collective-permute-start.24 = (bf16[960,768]{1,0:T(8,128)(2,1)}, bf16[960,768]{1,0:T(8,128)(2,1)S(1)}, u32[]{:S(2)}, u32[]{:S(2)}) collective-permute-start(bf16[960,768]{1,0:T(8,128)(2,1)} %get-tuple-element.329), channel_id=1, source_target_pairs={{0,4},{2,6},{4,0},{6,2},{8,12},{10,14},{12,8},{14,10},{16,20},{18,... | collective-permute-start | bytes 4423688 | tf_op jit(solution)/shard_map/ppermute | solution.py:672
  331.3 21.8 %collective-permute-start.25 = (bf16[96,768]{1,0:T(8,128)(2,1)}, bf16[96,768]{1,0:T(8,128)(2,1)S(1)}, u32[]{:S(2)}, u32[]{:S(2)}) collective-permute-start(bf16[96,768]{1,0:T(8,128)(2,1)} %get-tuple-element.330), channel_id=1, source_target_pairs={{0,8},{2,10},{4,12},{6,14},{8,0},{10,2},{12,4},{14,6},{16,24},{18,... | collective-permute-start | bytes 442376 | tf_op jit(solution)/shard_map/ppermute | solution.py:672
  331.3 21.8 %collective-permute-start.26 = (bf16[96,768]{1,0:T(8,128)(2,1)}, bf16[96,768]{1,0:T(8,128)(2,1)S(1)}, u32[]{:S(2)}, u32[]{:S(2)}) collective-permute-start(bf16[96,768]{1,0:T(8,128)(2,1)} %get-tuple-element.331), channel_id=1, source_target_pairs={{0,16},{2,18},{4,20},{6,22},{8,24},{10,26},{12,28},{14,30},{16,0},... | collective-permute-start | bytes 442376 | tf_op jit(solution)/shard_map/ppermute | solution.py:672
  333.2 19.9 %collective-permute-start.27 = (bf16[96,768]{1,0:T(8,128)(2,1)}, bf16[96,768]{1,0:T(8,128)(2,1)S(1)}, u32[]{:S(2)}, u32[]{:S(2)}) collective-permute-start(bf16[96,768]{1,0:T(8,128)(2,1)} %get-tuple-element.332), channel_id=1, source_target_pairs={{0,24},{2,26},{4,28},{6,30},{8,16},{10,18},{12,20},{14,22},{16,8},... | collective-permute-start | bytes 442376 | tf_op jit(solution)/shard_map/ppermute | solution.py:672
  364.9 3.6 collective-permute-start.28
  383.1 29.5 %collective-permute-start.29 = (bf16[768,768]{1,0:T(8,128)(2,1)}, bf16[768,768]{1,0:T(8,128)(2,1)S(1)}, u32[]{:S(2)}, u32[]{:S(2)}) collective-permute-start(bf16[768,768]{1,0:T(8,128)(2,1)} %get-tuple-element.361), channel_id=1, source_target_pairs={{0,2},{2,0},{4,6},{6,4},{8,10},{10,8},{12,14},{14,12},{16,18},{18,... | collective-permute-start | bytes 3538952 | tf_op jit(solution)/shard_map/ppermute | solution.py:672
  383.8 28.8 %collective-permute-start.30 = (bf16[768,768]{1,0:T(8,128)(2,1)}, bf16[768,768]{1,0:T(8,128)(2,1)S(1)}, u32[]{:S(2)}, u32[]{:S(2)}) collective-permute-start(bf16[768,768]{1,0:T(8,128)(2,1)} %get-tuple-element.362), channel_id=1, source_target_pairs={{0,4},{2,6},{4,0},{6,2},{8,12},{10,14},{12,8},{14,10},{16,20},{18,... | collective-permute-start | bytes 3538952 | tf_op jit(solution)/shard_map/ppermute | solution.py:672
  386.0 26.6 %collective-permute-start.31 = (bf16[96,768]{1,0:T(8,128)(2,1)}, bf16[96,768]{1,0:T(8,128)(2,1)S(1)}, u32[]{:S(2)}, u32[]{:S(2)}) collective-permute-start(bf16[96,768]{1,0:T(8,128)(2,1)} %get-tuple-element.363), channel_id=1, source_target_pairs={{0,8},{2,10},{4,12},{6,14},{8,0},{10,2},{12,4},{14,6},{16,24},{18,... | collective-permute-start | bytes 442376 | tf_op jit(solution)/shard_map/ppermute | solution.py:672
  386.0 26.6 %collective-permute-start.32 = (bf16[96,768]{1,0:T(8,128)(2,1)}, bf16[96,768]{1,0:T(8,128)(2,1)S(1)}, u32[]{:S(2)}, u32[]{:S(2)}) collective-permute-start(bf16[96,768]{1,0:T(8,128)(2,1)} %get-tuple-element.364), channel_id=1, source_target_pairs={{0,16},{2,18},{4,20},{6,22},{8,24},{10,26},{12,28},{14,30},{16,0},... | collective-permute-start | bytes 442376 | tf_op jit(solution)/shard_map/ppermute | solution.py:672
  387.9 24.7 %collective-permute-start.33 = (bf16[96,768]{1,0:T(8,128)(2,1)}, bf16[96,768]{1,0:T(8,128)(2,1)S(1)}, u32[]{:S(2)}, u32[]{:S(2)}) collective-permute-start(bf16[96,768]{1,0:T(8,128)(2,1)} %get-tuple-element.365), channel_id=1, source_target_pairs={{0,24},{2,26},{4,28},{6,30},{8,16},{10,18},{12,20},{14,22},{16,8},... | collective-permute-start | bytes 442376 | tf_op jit(solution)/shard_map/ppermute | solution.py:672
  412.6 4.9 collective-permute-start.34
  412.7 4.8 collective-permute-start.35
  413.2 2.9 collective-permute-start.37
  413.4 4.1 collective-permute-start.36
  432.0 25.8 %collective-permute-start.38 = (bf16[640,768]{1,0:T(8,128)(2,1)}, bf16[640,768]{1,0:T(8,128)(2,1)S(1)}, u32[]{:S(2)}, u32[]{:S(2)}) collective-permute-start(bf16[640,768]{1,0:T(8,128)(2,1)} %get-tuple-element.408), channel_id=1, source_target_pairs={{0,2},{2,0},{4,6},{6,4},{8,10},{10,8},{12,14},{14,12},{16,18},{18,... | collective-permute-start | bytes 2949128 | tf_op jit(solution)/shard_map/ppermute | solution.py:672
  432.6 25.1 %collective-permute-start.39 = (bf16[576,768]{1,0:T(8,128)(2,1)}, bf16[576,768]{1,0:T(8,128)(2,1)S(1)}, u32[]{:S(2)}, u32[]{:S(2)}) collective-permute-start(bf16[576,768]{1,0:T(8,128)(2,1)} %get-tuple-element.409), channel_id=1, source_target_pairs={{0,4},{2,6},{4,0},{6,2},{8,12},{10,14},{12,8},{14,10},{16,20},{18,... | collective-permute-start | bytes 2654216 | tf_op jit(solution)/shard_map/ppermute | solution.py:672
  434.0 14.1 %collective-permute-start.40 = (bf16[192,768]{1,0:T(8,128)(2,1)}, bf16[192,768]{1,0:T(8,128)(2,1)S(1)}, u32[]{:S(2)}, u32[]{:S(2)}) collective-permute-start(bf16[192,768]{1,0:T(8,128)(2,1)} %get-tuple-element.410), channel_id=1, source_target_pairs={{0,8},{2,10},{4,12},{6,14},{8,0},{10,2},{12,4},{14,6},{16,24},{18,... | collective-permute-start | bytes 884744 | tf_op jit(solution)/shard_map/ppermute | solution.py:672
  434.0 23.7 %collective-permute-start.41 = (bf16[192,768]{1,0:T(8,128)(2,1)}, bf16[192,768]{1,0:T(8,128)(2,1)S(1)}, u32[]{:S(2)}, u32[]{:S(2)}) collective-permute-start(bf16[192,768]{1,0:T(8,128)(2,1)} %get-tuple-element.411), channel_id=1, source_target_pairs={{0,16},{2,18},{4,20},{6,22},{8,24},{10,26},{12,28},{14,30},{16,0},... | collective-permute-start | bytes 884744 | tf_op jit(solution)/shard_map/ppermute | solution.py:672
  436.0 21.7 %collective-permute-start.42 = (bf16[192,768]{1,0:T(8,128)(2,1)}, bf16[192,768]{1,0:T(8,128)(2,1)S(1)}, u32[]{:S(2)}, u32[]{:S(2)}) collective-permute-start(bf16[192,768]{1,0:T(8,128)(2,1)} %get-tuple-element.412), channel_id=1, source_target_pairs={{0,24},{2,26},{4,28},{6,30},{8,16},{10,18},{12,20},{14,22},{16,8},... | collective-permute-start | bytes 884744 | tf_op jit(solution)/shard_map/ppermute | solution.py:672
  464.0 20.1 %collective-permute-start.44 = (bf16[256,768]{1,0:T(8,128)(2,1)}, bf16[256,768]{1,0:T(8,128)(2,1)S(1)}, u32[]{:S(2)}, u32[]{:S(2)}) collective-permute-start(bf16[256,768]{1,0:T(8,128)(2,1)} %get-tuple-element.431), channel_id=1, source_target_pairs={{0,4},{2,6},{4,0},{6,2},{8,12},{10,14},{12,8},{14,10},{16,20},{18,... | collective-permute-start | bytes 1179656 | tf_op jit(solution)/shard_map/ppermute | solution.py:672
  464.7 9.0 %collective-permute-start.45 = (bf16[96,768]{1,0:T(8,128)(2,1)}, bf16[96,768]{1,0:T(8,128)(2,1)S(1)}, u32[]{:S(2)}, u32[]{:S(2)}) collective-permute-start(bf16[96,768]{1,0:T(8,128)(2,1)} %get-tuple-element.432), channel_id=1, source_target_pairs={{0,8},{2,10},{4,12},{6,14},{8,0},{10,2},{12,4},{14,6},{16,24},{18,... | collective-permute-start | bytes 442376 | tf_op jit(solution)/shard_map/ppermute | solution.py:672
  470.1 14.1 %collective-permute-start.43 = (bf16[192,768]{1,0:T(8,128)(2,1)}, bf16[192,768]{1,0:T(8,128)(2,1)S(1)}, u32[]{:S(2)}, u32[]{:S(2)}) collective-permute-start(bf16[192,768]{1,0:T(8,128)(2,1)} %get-tuple-element.430), channel_id=1, source_target_pairs={{0,2},{2,0},{4,6},{6,4},{8,10},{10,8},{12,14},{14,12},{16,18},{18,... | collective-permute-start | bytes 884744 | tf_op jit(solution)/shard_map/ppermute | solution.py:672
  471.5 12.6 %collective-permute-start.46 = (bf16[96,768]{1,0:T(8,128)(2,1)}, bf16[96,768]{1,0:T(8,128)(2,1)S(1)}, u32[]{:S(2)}, u32[]{:S(2)}) collective-permute-start(bf16[96,768]{1,0:T(8,128)(2,1)} %get-tuple-element.433), channel_id=1, source_target_pairs={{0,16},{2,18},{4,20},{6,22},{8,24},{10,26},{12,28},{14,30},{16,0},... | collective-permute-start | bytes 442376 | tf_op jit(solution)/shard_map/ppermute | solution.py:672
  471.9 20.6 %collective-permute-start.51 = (f32[1,2,48,768]{3,2,1,0:T(8,128)S(1)}, f32[1,2,48,768]{3,2,1,0:T(8,128)S(1)}, u32[]{:S(2)}, u32[]{:S(2)}) collective-permute-start(f32[1,2,48,768]{3,2,1,0:T(8,128)S(1)} %copy-done.30), channel_id=1, source_target_pairs={{0,1},{1,0},{2,3},{3,2},{4,5},{5,4},{6,7},{7,6},{8,9},{9,8},{10,11... | collective-permute-start | bytes 884744 | tf_op jit(solution)/shard_map/ppermute | solution.py:668
  473.7 10.4 %collective-permute-start.47 = (bf16[96,768]{1,0:T(8,128)(2,1)}, bf16[96,768]{1,0:T(8,128)(2,1)S(1)}, u32[]{:S(2)}, u32[]{:S(2)}) collective-permute-start(bf16[96,768]{1,0:T(8,128)(2,1)} %get-tuple-element.434), channel_id=1, source_target_pairs={{0,24},{2,26},{4,28},{6,30},{8,16},{10,18},{12,20},{14,22},{16,8},... | collective-permute-start | bytes 442376 | tf_op jit(solution)/shard_map/ppermute | solution.py:672
  484.1 8.4 %collective-permute-start.52 = (f32[1,2,48,768]{3,2,1,0:T(8,128)S(1)}, f32[1,2,48,768]{3,2,1,0:T(8,128)S(1)}, u32[]{:S(2)}, u32[]{:S(2)}) collective-permute-start(f32[1,2,48,768]{3,2,1,0:T(8,128)S(1)} %copy-done.31), channel_id=1, source_target_pairs={{0,1},{1,0},{2,3},{3,2},{4,5},{5,4},{6,7},{7,6},{8,9},{9,8},{10,11... | collective-permute-start | bytes 884744 | tf_op jit(solution)/shard_map/ppermute | solution.py:668
  487.8 9.9 %collective-permute-start.48 = (bf16[112,768]{1,0:T(8,128)(2,1)}, bf16[112,768]{1,0:T(8,128)(2,1)S(1)}, u32[]{:S(2)}, u32[]{:S(2)}) collective-permute-start(bf16[112,768]{1,0:T(8,128)(2,1)} %get-tuple-element.449), channel_id=1, source_target_pairs={{0,8},{2,10},{4,12},{6,14},{8,0},{10,2},{12,4},{14,6},{16,24},{18,... | collective-permute-start | bytes 516104 | tf_op jit(solution)/shard_map/ppermute | solution.py:672
  490.0 15.0 %collective-permute-start.49 = (bf16[112,768]{1,0:T(8,128)(2,1)}, bf16[112,768]{1,0:T(8,128)(2,1)S(1)}, u32[]{:S(2)}, u32[]{:S(2)}) collective-permute-start(bf16[112,768]{1,0:T(8,128)(2,1)} %get-tuple-element.450), channel_id=1, source_target_pairs={{0,16},{2,18},{4,20},{6,22},{8,24},{10,26},{12,28},{14,30},{16,0},... | collective-permute-start | bytes 516104 | tf_op jit(solution)/shard_map/ppermute | solution.py:672
  490.2 14.7 %collective-permute-start.50 = (bf16[112,768]{1,0:T(8,128)(2,1)}, bf16[112,768]{1,0:T(8,128)(2,1)S(1)}, u32[]{:S(2)}, u32[]{:S(2)}) collective-permute-start(bf16[112,768]{1,0:T(8,128)(2,1)} %get-tuple-element.451), channel_id=1, source_target_pairs={{0,24},{2,26},{4,28},{6,30},{8,16},{10,18},{12,20},{14,22},{16,8},... | collective-permute-start | bytes 516104 | tf_op jit(solution)/shard_map/ppermute | solution.py:672
  492.4 32.3 %collective-permute-start.61 = (f32[2,2,48,768]{3,2,1,0:T(8,128)S(1)}, f32[2,2,48,768]{3,2,1,0:T(8,128)S(1)}, u32[]{:S(2)}, u32[]{:S(2)}) collective-permute-start(f32[2,2,48,768]{3,2,1,0:T(8,128)S(1)} %copy-done.17), channel_id=1, source_target_pairs={{0,1},{1,0},{2,3},{3,2},{4,5},{5,4},{6,7},{7,6},{8,9},{9,8},{10,11... | collective-permute-start | bytes 1769480 | tf_op jit(solution)/shard_map/ppermute | solution.py:668
  509.7 3.5 collective-permute-start.54
  510.3 3.5 collective-permute-start.55
  511.5 4.4 collective-permute-start.56
  516.0 5.0 collective-permute-start.57
  518.6 4.4 collective-permute-start.58
  518.8 5.3 collective-permute-start.59
  521.0 3.8 collective-permute-start.62
  521.0 3.8 collective-permute-start.63
  523.0 1.7 collective-permute-start.60
  (71 other events, 591.9 us)
Sparse Core Ops, SparseCore 0:
  13.3 169.1 all-gather.1

commit v13 on v12

--- a/solution.py
+++ b/solution.py
@@ -144,11 +144,6 @@
 def matrix(ref, place, low=None, high=None):
     value = ref[place] if low is None else ref[place, :, :, low:high]
     return value.reshape(-1, value.shape[-1])
-
-
-def tile_scratch(count, weights):
-    blocks, rows = (weights.shape[0], weights.shape[2])
-    return pltpu.VMEM((count, blocks, rows, blocks * rows), LOW)
 
 
 def mixer_tile(anys, cores, place, t, base, width):
@@ -261,27 +256,34 @@
 GELU_CUBE = 0.044715
 
 
-def fetch_hidden(weights, base, order, ups, downs, sems, between=lambda t: None, down_first=False):
-    blocks, _, rows, _ = weights.shape
-    width = blocks * rows
+def fetch_hidden(anys, base, cores, ups, downs, sems, between=lambda t: None, down_first=False):
+    blocks, parts, rows, width = downs.shape
     half, some = width // 2, max(blocks // 4, 1)
     copies = {}
-    for t, (core_of, within) in enumerate(order):
-        up = lambda: fetch(
-            [tile_of(weights, core_of, base + (2 + within) * width)], [ups.at[t]], sems, t
-        )
+
+    def up_source(place, within):
+        if len(anys) == 2:
+            return anys[place].at[2 * within]
+        return tile_of(anys[0], cores[place], base + (2 + within) * width)
+
+    def down_source(place, first, j):
+        if len(anys) == 2:
+            return anys[place].at[1 + j // 2 * 2, pl.ds(first, some), :, j % 2 * half : (j % 2 + 1) * half]
+        at = base + 4 * width + j * half
+        return anys[0].at[pl.ds(first, some), cores[place], :, at : at + half]
+
+    for t in range(4):
+        up = lambda: fetch([up_source(t // 2, t % 2)], [ups.at[t]], sems, t)
         if not down_first:
             copies[0, t] = up()
         if blocks >= 4 or t == 0:
             sources, targets = [], []
-            first = (2 * core_of + within) * some if blocks >= 4 else 0
-            for core in range(2):
+            first = (2 * cores[t // 2] + t % 2) * some if blocks >= 4 else 0
+            for place in range(2):
+                columns = pl.ds(pl.multiple_of(cores[place] * half, 128), half)
                 for j in range(4):
-                    at = base + 4 * width + j * half
-                    sources.append(weights.at[pl.ds(first, some), core, :, at : at + half])
-                    targets.append(
-                        downs.at[pl.ds(t * some, some), j, :, core * half : (core + 1) * half]
-                    )
+                    sources.append(down_source(place, first, j))
+                    targets.append(downs.at[pl.ds(t * some, some), j, :, columns])
             copies[1, t] = fetch(sources, targets, sems, 4 + 8 * t)
         between(t)
         if down_first:
@@ -294,18 +296,19 @@
     return wait
 
 
-def rows_of(downs, t, order):
+def rows_of(downs, t, cores):
     blocks, parts, rows, width = downs.shape
     if blocks >= 4:
         some = blocks // 4
         return downs[t * some : (t + 1) * some].reshape(some * parts * rows, width)
-    return downs[0, 2 * order[t][0] + order[t][1]]
+    return downs[0, 2 * cores[t // 2] + t % 2]
 
 
 def hidden_scratch(weights):
-    blocks, _, rows, _ = weights.shape
+    w = weights[0]
+    blocks, rows = (w.shape[1], w.shape[2]) if len(weights) == 2 else (w.shape[0], w.shape[2])
     return [
-        tile_scratch(4, weights),
+        pltpu.VMEM((4, blocks, rows, blocks * rows), LOW),
         pltpu.VMEM((blocks, 4, rows, blocks * rows), LOW),
         pltpu.SemaphoreType.DMA((36,)),
     ]
@@ -314,23 +317,24 @@
 def hidden_forward_kernel(base, place_of, ins, anys, outs, ups, downs, sems):
     middle, gains = ins
     output, pack, hidden = outs
-    order = [(t // 2, t % 2) for t in range(4)]
-    wait = fetch_hidden(anys[0], base, order, ups, downs, sems)
+    cores = (place_of[0], 1 - place_of[0])
+    wait = fetch_hidden(anys, base, cores, ups, downs, sems)
     normed, _, _ = normalize(middle[...], gains[0:1], gains[1:2])
     pack[0] = normed.astype(LOW)
     pack.send(0)
     for t in range(4):
         wait(0, t)
+        index = 2 * cores[t // 2] + t % 2
         x = dot(pack[0], matrix(ups, t))
-        hidden[t] = x
-        hidden.send(t)
+        hidden[index] = x
+        hidden.send(index)
         inner = jnp.tanh(x * (GELU_SCALE + (GELU_SCALE * GELU_CUBE) * (x * x)))
         value = x * 0.5
         value = (value + value * inner).astype(LOW)
-        pack[1 + t] = value
-        pack.send(1 + t)
+        pack[1 + index] = value
+        pack.send(1 + index)
         wait(1, t)
-        product = dot(value, rows_of(downs, t, order))
+        product = dot(value, rows_of(downs, t, cores))
         output[...] = (middle[...] if t == 0 else output[...]) + product
 
 
@@ -342,7 +346,7 @@
         place,
         [(one, FULL), ((5,) + one, LOW), ((4,) + one, FULL)],
         [middle, gains],
-        [weights],
+        weights,
         hidden_scratch(weights),
         16 * length * width * width,
         sent=(1, 2),
@@ -351,19 +355,19 @@
 
 def hidden_back_kernel(base, place_of, ins, anys, outs, ups, downs, sems, hidden_here, total, own_sems):
     branch, grad, middle, gains = ins
-    hidden, weights = anys
+    hidden, *weights = anys
     grad_middle, grad_gains, grad_own, grad_other = outs
-    order = [(core, t) for core in (place_of[0], 1 - place_of[0]) for t in range(2)]
+    cores = (place_of[0], 1 - place_of[0])
     copies = []
 
     def fetch_values(t):
-        source = hidden.at[2 * order[t][0] + order[t][1]]
+        source = hidden.at[2 * cores[t // 2] + t % 2]
         copies.extend(fetch([source], [hidden_here.at[t]], own_sems, t))
 
-    wait = fetch_hidden(weights, base, order, ups, downs, sems, fetch_values, down_first=True)
+    wait = fetch_hidden(weights, base, cores, ups, downs, sems, fetch_values, down_first=True)
     for t in range(4):
         wait(1, t)
-        grad_active = dot_nt(branch[...], rows_of(downs, t, order))
+        grad_active = dot_nt(branch[...], rows_of(downs, t, cores))
         copies[t].wait()
         x = hidden_here[t]
         square = x * x
@@ -390,7 +394,7 @@
         place,
         [(one, FULL), ((2, width), FULL), ((2,) + one, LOW), ((2,) + one, LOW)],
         [branch, grad, middle, gains],
-        [hidden, weights],
+        [hidden] + weights,
         hidden_scratch(weights)
         + [
             pltpu.VMEM((4,) + one, FULL),
@@ -659,9 +663,16 @@
             if early and l == 0 and n < 4:
                 start = 0 if n < 2 else rows + 16
                 early[0][start : start + rows, (n % 2) * half : (n % 2 + 1) * half] = value
-                continue
-            out[:, at : at + part] = value
-            at += part
+            elif early and l == layers - 1 and n == 4:
+                for t in range(2):
+                    early[1][2 * t * rows : (2 * t + 1) * rows] = value[:, t * width : (t + 1) * width]
+            elif early and l == layers - 1 and n > 4:
+                start = (2 * ((n - 5) // 2) + 1) * rows
+                lanes = (n - 5) % 2 * half
+                early[1][start : start + rows, lanes : lanes + half] = value
+            else:
+                out[:, at : at + part] = value
+                at += part
 
 
 def swap_cores(value):
@@ -706,7 +717,8 @@
 
 def place_kernel(parts, rows, place_of, ins, anys, outs, sems):
     quarter, from_x, from_y, far_a, far_b = anys
-    tiles, small = outs
+    tiles, *small = outs
+    count = tiles.shape[0] // 2
     x, y, z = place_of[1], place_of[2], place_of[3]
     for n in range(16):
         xor_z, xor_y, xor_x = n // 4, n // 2 % 2, n % 2
@@ -718,38 +730,55 @@
             else:
                 source = from_x if xor_x else from_y if xor_y else quarter
                 at += h * 4 * parts[0]
-            fetch([source.at[at : at + rows]], [tiles.at[h, index]], sems, h)
-            if h == 0:
-                fetch([source.at[at + rows : at + parts[0]]], [small.at[index]], sems, 2)
-    for n, target in enumerate((tiles.at[0], tiles.at[1], small)):
+            for t in range(count):
+                here = source.at[at + t * rows : at + (t + 1) * rows]
+                fetch([here], [tiles.at[h * count + t, index]], sems, h * count + t)
+            if h == 0 and small:
+                here = source.at[at + count * rows : at + parts[0]]
+                fetch([here], [small[0].at[index]], sems, 2 * count)
+    targets = [tiles.at[t] for t in range(2 * count)] + small
+    for n, target in enumerate(targets):
         pltpu.make_async_copy(target, target, sems.at[n]).wait()
 
 
-def gather_first(place, shard, rows, width):
-    parts = (rows + 16, rows)
-    got = [across(shard, mask, 16) for mask in Z]
-    (quarter,) = call(
-        functools.partial(arrange_kernel, parts),
-        place,
-        [((4 * sum(parts), width), LOW)],
-        [],
-        [shard] + got,
-        [pltpu.SemaphoreType.DMA((8,))],
-    )
-    from_x, from_y = across(quarter, X, 16), across(quarter, Y, 16)
-    cut = 4 * parts[0]
-    far_a, far_b = across(from_y[:cut], X, 16), across(from_x[cut:], Y, 16)
-    own, small = call(
-        functools.partial(place_kernel, parts, rows),
-        place,
-        [((2, 16, rows, width), LOW), ((16, 16, width), LOW)],
-        [],
-        [quarter, from_x, from_y, far_a, far_b],
-        [pltpu.SemaphoreType.DMA((3,))],
-    )
-    small = small[:, :, : rows // 16 * SMALL].reshape(16, 16, rows // 16, SMALL)
-    small = small.transpose(0, 2, 1, 3).reshape(width, SMALL)
-    return [own, swap_cores(own)], small
+class Gather:
+    def __init__(self, place, shard, parts, rows):
+        self.place, self.shard, self.parts, self.rows = place, shard, parts, rows
+
+    def along_z(self):
+        self.got = [across(self.shard, mask, 16) for mask in Z]
+
+    def in_plane(self):
+        width = self.shard.shape[1]
+        (quarter,) = call(
+            functools.partial(arrange_kernel, self.parts),
+            self.place,
+            [((4 * sum(self.parts), width), LOW)],
+            [],
+            [self.shard] + self.got,
+            [pltpu.SemaphoreType.DMA((8,))],
+        )
+        self.quarter, self.near = quarter, [across(quarter, X, 16), across(quarter, Y, 16)]
+
+    def forward(self):
+        cut = 4 * self.parts[0]
+        from_x, from_y = self.near
+        self.far = [across(from_y[:cut], X, 16), across(from_x[cut:], Y, 16)]
+
+    def result(self):
+        width = self.shard.shape[1]
+        count, more = divmod(self.parts[0], self.rows)
+        outs = [((2 * count, 16, self.rows, width), LOW)]
+        if more:
+            outs.append(((16, more, width), LOW))
+        return call(
+            functools.partial(place_kernel, self.parts, self.rows),
+            self.place,
+            outs,
+            [],
+            [self.quarter] + self.near + self.far,
+            [pltpu.SemaphoreType.DMA((2 * count + 1,))],
+        )
 
 
 X, Y = 1, 2
@@ -1105,7 +1134,7 @@
     rows = inward.shape[1]
     width = rows * fsdp
     half = width // 2
-    fast = fsdp == 16 and rows == 48
+    fast = fsdp == 16 and rows == 48 and layers > 1
     core, index = lax.axis_index("dp"), lax.axis_index("fsdp")
     bit = lambda b: lax.rem(lax.div(index, b), 2)
     place = jnp.stack([core, bit(1), bit(2), lax.div(index, 4)]).astype(jnp.int32)
@@ -1120,7 +1149,7 @@
     columns = small.shape[1] + layers * 6 * width
     shapes = [(rows, columns)]
     if fast:
-        shapes = [(rows, layers * 6 * width - 2 * width), (2 * rows + 16, width)]
+        shapes = [(rows, (layers - 1) * 6 * width), (2 * rows + 16, width), (4 * rows, width)]
     weights, *early = call(
         functools.partial(pack_kernel, layers),
         place,
@@ -1138,13 +1167,27 @@
             quarter = quarter.reshape(2, 4, width, half).transpose(0, 2, 1, 3)
             columns.append(quarter.reshape(2, fsdp, rows, 2 * width).transpose(1, 0, 2, 3))
         weights = jnp.concatenate(columns, 3).transpose(1, 0, 2, 3).reshape(1, 2, width, -1)
-    mixers = [[weights]] * layers
+    mixers, hiddens = [[weights]] * layers, [[weights]] * layers
     if fast:
-        mixers[0], small = gather_first(place, early[0], rows, width)
-        small = small.T
+        first = Gather(place, early[0], (rows + 16, rows), rows)
+        last = Gather(place, early[1], (2 * rows, 2 * rows), rows)
+        first.along_z()
+        first.got, last.shard = tie(first.got, last.shard)
+        first.in_plane()
+        last.along_z()
+        first.near, last.got = tie(first.near, last.got)
+        first.forward()
+        (first.far,) = tie(first.far)
+        own, small = first.result()
+        mixers[0] = [own, swap_cores(own)]
+        own, last.got = tie(own, last.got)
+        last.in_plane()
+        small = small[:, :, : rows // 16 * SMALL].reshape(16, 16, rows // 16, SMALL)
+        small = small.transpose(0, 2, 1, 3).reshape(width, SMALL).T
     else:
         small = weights[:, 0, :, :SMALL].reshape(width, SMALL).T
-    base = lambda l: weights.shape[3] - (layers - l) * 6 * width
+    start = -2 * width if fast else weights.shape[3] - layers * 6 * width
+    base = lambda l: start + l * 6 * width
     gains = small[V : V + norms].astype(FULL).reshape(-1, 2, width)
 
     cosine, sine = rotary_tables(length)
@@ -1156,7 +1199,13 @@
         middle, query, keys, values, lse, pack = attention_forward(
             place, resid, mixers[l], base(l), gain[0], cosine, sine, segments
         )
-        output, pack_mid, hidden = hidden_forward(place, middle, weights, base(l), gain[1])
+        if fast and l == 0:
+            middle, last.near = tie(middle, last.near)
+            last.forward()
+            (own,) = last.result()
+            hiddens[-1] = [own, swap_cores(own)]
+            middle, hiddens[-1][0] = tie(middle, own)
+        output, pack_mid, hidden = hidden_forward(place, middle, hiddens[l], base(l), gain[1])
         kept.append((resid, query, keys, values, lse, pack, middle, hidden, pack_mid))
         resid = output
     grad, branch, branch_own, branch_other, head_in, grad_logits, grad_norms, sums = head(
@@ -1190,7 +1239,7 @@
         )
         grad, branch = rounds.step(chunk, grad, branch)
         grad_middle, gains_mid, up_own, up_other = hidden_back(
-            place, grad, branch, middle, hidden, weights, base(l), gain[1]
+            place, grad, branch, middle, hidden, hiddens[l], base(l), gain[1]
         )
         grad_middle, up_own, up_other, early_came = rounds.finish(
             grad_middle, up_own, up_other, early_came

time: 553 us -> 548 us (level)
  waiting for transfers between devices: 204 us -> 163 us
  starting transfers between devices: 62.8 us -> 91.3 us
  Pallas kernels: 232 us -> 241 us
    all_gather x1, waiting for transfers between devices: 84.4 us -> 0.02 us  [body(): weights = lax.all_gather(weights, ('fsdp', 'dp'), axis=0, tiled=True)]
    ppermute x40 -> x47, waiting for transfers between devices: 101 us -> 145 us  [across(): return lax.ppermute(value, 'fsdp', [(i, i ^ mask) for i in range(size)])]
    ppermute x40 -> x47, starting transfers between devices: 58.2 us -> 86.6 us  [across(): return lax.ppermute(value, 'fsdp', [(i, i ^ mask) for i in range(size)])]
    pallas_call x21 -> x23, Pallas kernels: 232 us -> 241 us  [call(): pl.pallas_call(body, out_shape=[jax.ShapeDtypeStruct(s, t) for s, t in ou...]
    unnamed x140 -> x154, local copies, waits for them, and re-layouts: 14.5 us -> 13 us
    ppermute x24 -> x25, waiting for transfers between devices: 18.2 us -> 18.3 us  [swap_cores(): return lax.ppermute(value, 'dp', [(0, 1), (1, 0)])]
  transfers between devices with their start and end apart: 65 -> 73, of which waited for: 28 -> 30; matrix products, arithmetic and copies ran while one was open for 2% -> 2% of each run, Pallas kernels for 24% -> 31%
where the time goes in v13:
time: 548 us; the launch traced here: 538 us
  Pallas kernels  241 us (44%)
  waiting for transfers between devices  163 us (30%)
  starting transfers between devices  91.3 us (17%)
  local copies, waits for them, and re-layouts  21 us (4%)
  between operations  15.4 us (3%)
    pallas_call x23, Pallas kernels, call(): pl.pallas_call(body, out_shape=[jax.ShapeDtypeStruct(s, t) for s, t in ou...  241 us
    ppermute x47, waiting for transfers between devices, across(): return lax.ppermute(value, 'fsdp', [(i, i ^ mask) for i in range(size)])  145 us
    ppermute x47, starting transfers between devices, across(): return lax.ppermute(value, 'fsdp', [(i, i ^ mask) for i in range(size)])  86.6 us
    ppermute x25, waiting for transfers between devices, swap_cores(): return lax.ppermute(value, 'dp', [(0, 1), (1, 0)])  18.3 us
    unnamed x154, local copies, waits for them, and re-layouts  13 us
  transfers between devices with their start and end apart: 73, of which 30 were waited for; matrix products, arithmetic and copies ran while one was open for 2% of the time, Pallas kernels for 31%

profile of v13, /device:TPU:0, one launch (start us, length us, event | category | flops | bytes accessed | tf_op | source)
XLA Modules:
  0.0 538.2 jit_solution(9532838251654965529)
XLA Ops:
  10.1 3.0 shard_map.364
  13.1 3.1 collective-permute-start
  16.2 2.6 collective-permute-start.1
  18.8 4.7 collective-permute-done.refs_1_
  23.5 12.3 %collective-permute-done.1.refs_2_ = bf16[112,768]{1,0:T(8,128)(2,1)S(1)} collective-permute-done((bf16[112,768]{1,0:T(8,128)(2,1)}, bf16[112,768]{1,0:T(8,128)(2,1)S(1)}, u32[]{:S(2)}, u32[]{:S(2)}) %collective-permute-start.1) | collective-permute-done | bytes 172064 | tf_op jit(solution)/shard_map/ppermute | solution.py:683
  36.5 2.7 shard_map.365.refs_0_
  39.3 1.6 collective-permute-start.3
  40.8 1.5 collective-permute-start.4
  42.4 8.5 %collective-permute-start.5 = (bf16[192,768]{1,0:T(8,128)(2,1)S(1)}, bf16[192,768]{1,0:T(8,128)(2,1)S(1)}, u32[]{:S(2)}, u32[]{:S(2)}) collective-permute-start(bf16[192,768]{1,0:T(8,128)(2,1)S(1)} %copy-done.29), channel_id=1, source_target_pairs={{0,8},{2,10},{4,12},{6,14},{8,0},{10,2},{12,4},{14,6},{16,24},{18,... | collective-permute-start | bytes 884744 | tf_op jit(solution)/shard_map/ppermute | solution.py:683
  53.3 11.2 %collective-permute-done.5.refs_1_ = bf16[192,768]{1,0:T(8,128)(2,1)S(1)} collective-permute-done((bf16[192,768]{1,0:T(8,128)(2,1)S(1)}, bf16[192,768]{1,0:T(8,128)(2,1)S(1)}, u32[]{:S(2)}, u32[]{:S(2)}) %collective-permute-start.5) | collective-permute-done | bytes 294944 | tf_op jit(solution)/shard_map/ppermute | solution.py:683
  64.5 22.8 %collective-permute-done.6.refs_2_ = bf16[192,768]{1,0:T(8,128)(2,1)S(1)} collective-permute-done((bf16[192,768]{1,0:T(8,128)(2,1)S(1)}, bf16[192,768]{1,0:T(8,128)(2,1)S(1)}, u32[]{:S(2)}, u32[]{:S(2)}) %collective-permute-start.6) | collective-permute-done | bytes 294944 | tf_op jit(solution)/shard_map/ppermute | solution.py:683
  87.6 6.7 %collective-permute-done.9.refs_4_ = bf16[192,768]{1,0:T(8,128)(2,1)S(1)} collective-permute-done((bf16[192,768]{1,0:T(8,128)(2,1)S(1)}, bf16[192,768]{1,0:T(8,128)(2,1)S(1)}, u32[]{:S(2)}, u32[]{:S(2)}) %collective-permute-start.9) | collective-permute-done | bytes 294944 | tf_op jit(solution)/shard_map/ppermute | solution.py:683
  96.0 4.0 shard_map.366
  101.2 3.2 shard_map.368.refs_0_
  104.5 1.8 collective-permute-start.11
  110.3 1.6 fusion.3.refs_0_.refs_10_
  112.0 14.4 %shard_map.367 = (f32[512,768]{1,0:T(8,128)}, bf16[512,768]{1,0:T(8,128)(2,1)}, bf16[512,768]{1,0:T(8,128)(2,1)}, bf16[512,768]{1,0:T(8,128)(2,1)}, f32[512,128]{1,0:T(8,128)}, /*index=5*/bf16[2,512,768]{2,1,0:T(8,128)(2,1)}) custom-call(s32[4]{0:T(128)} %pad_add_fusion.scalars, f32[512,768]{1,0:T(8,128)} %fusion.3.refs_0_.refs_10_, ...), custom_call_target="tpu_custom_call" | custom-call | flops 3221225472 | bytes 6825984 | tf_op jit(solution)/shard_map/pallas_call | solution.py:111
  126.3 21.2 %collective-permute-done.11.refs_1_ = bf16[768,768]{1,0:T(8,128)(2,1)S(1)} collective-permute-done((bf16[768,768]{1,0:T(8,128)(2,1)}, bf16[768,768]{1,0:T(8,128)(2,1)S(1)}, u32[]{:S(2)}, u32[]{:S(2)}) %collective-permute-start.11) | collective-permute-done | bytes 1179680 | tf_op jit(solution)/shard_map/ppermute | solution.py:683
  147.6 1.5 collective-permute-start.13
  149.8 13.1 %collective-permute-done.13.refs_3_ = bf16[384,768]{1,0:T(8,128)(2,1)S(1)} collective-permute-done((bf16[384,768]{1,0:T(8,128)(2,1)S(1)}, bf16[384,768]{1,0:T(8,128)(2,1)S(1)}, u32[]{:S(2)}, u32[]{:S(2)}) %collective-permute-start.13) | collective-permute-done | bytes 589856 | tf_op jit(solution)/shard_map/ppermute | solution.py:683
  165.0 5.2 shard_map.369.refs_2_.refs_5_
  170.4 12.8 %shard_map.370 = (f32[512,768]{1,0:T(8,128)}, bf16[5,512,768]{2,1,0:T(8,128)(2,1)}, f32[4,512,768]{2,1,0:T(8,128)}) custom-call(s32[4]{0:T(128)} %pad_add_fusion.scalars, f32[512,768]{1,0:T(8,128)} %get-tuple-element.296.refs_0_.refs_2_, f32[2,768]{1,0:T(2,128)} %get-tuple-element.528.refs_1_.refs_3_, bf16[16,2,48,4608]{3,2,1,0:T(8,128)(2,1)} %bitcast.26), custom_call_target="tpu_custom_call" | custom-call | flops 4831838208 | bytes 15734784 | tf_op jit(solution)/shard_map/pallas_call | solution.py:111
  183.2 14.2 %shard_map.371 = (f32[512,768]{1,0:T(8,128)}, bf16[512,768]{1,0:T(8,128)(2,1)}, bf16[512,768]{1,0:T(8,128)(2,1)}, bf16[512,768]{1,0:T(8,128)(2,1)}, f32[512,128]{1,0:T(8,128)}, /*index=5*/bf16[2,512,768]{2,1,0:T(8,128)(2,1)}) custom-call(s32[4]{0:T(128)} %pad_add_fusion.scalars, f32[512,768]{1,0:T(8,128)} %get-tuple-element.299.refs_0_.refs_10_, ...), custom_call_target="tpu_custom_call" | custom-call | flops 3221225472 | bytes 16263168 | tf_op jit(solution)/shard_map/pallas_call | solution.py:111
  197.4 12.7 %shard_map.372 = (f32[512,768]{1,0:T(8,128)}, bf16[5,512,768]{2,1,0:T(8,128)(2,1)}, f32[4,512,768]{2,1,0:T(8,128)}) custom-call(s32[4]{0:T(128)} %pad_add_fusion.scalars, f32[512,768]{1,0:T(8,128)} %get-tuple-element.301.refs_0_.refs_2_, f32[2,768]{1,0:T(2,128)} %get-tuple-element.526.refs_1_.refs_3_, bf16[4,16,48,768]{3,2,1,0:T(8,128)(2,1)} %shard_map.369.refs_2_.refs_5_, ...), custom_call_target="tpu_custom_call" | custom-call | flops 4831838208 | bytes 11016192 | tf_op jit(solution)/shard_map/pallas_call | solution.py:111
  212.3 5.6 %shard_map.373 = (f32[512,768]{1,0:T(8,128)}, bf16[512,768]{1,0:T(8,128)(2,1)}, bf16[512,384]{1,0:T(8,128)(2,1)}, bf16[512,384]{1,0:T(8,128)(2,1)}, bf16[512,768...) custom-call(s32[4]{0:T(128)} %pad_add_fusion.scalars, ...), custom_call_target="tpu_custom_call" | custom-call | flops 201326592 | bytes 1779712 | tf_op jit(solution)/shard_map/pallas_call | solution.py:111
  220.6 8.8 %shard_map.374 = (bf16[384,768]{1,0:T(8,128)(2,1)}, bf16[384,768]{1,0:T(8,128)(2,1)}, f32[1,2,384,768]{3,2,1,0:T(8,128)}) custom-call(s32[4]{0:T(128)} %pad_add_fusion.scalars, bf16[5,512,768]{2,1,0:T(8,128)(2,1)} %get-tuple-element.303.refs_0_, bf16[512,384]{1,0:T(8,128)(2,1)} %get-tuple-element.305.refs_1_, ...), custom_call_target="tpu_custom_call" | custom-call | flops 2415919104 | bytes 8650752 | tf_op jit(solution)/shard_map/pallas_call | solution.py:111
  233.2 17.9 %shard_map.375 = (f32[512,768]{1,0:T(8,128)}, f32[2,768]{1,0:T(2,128)}, bf16[2,512,768]{2,1,0:T(8,128)(2,1)}, bf16[2,512,768]{2,1,0:T(8,128)(2,1)}) custom-call(s32[4]{0:T(128)} %pad_add_fusion.scalars, bf16[512,768]{1,0:T(8,128)(2,1)} %get-tuple-element.317.refs_0_, f32[512,768]{1,0:T(8,128)} %get-tuple-element.318.refs_1_, ...), custom_call_target="tpu_custom_call" | custom-call | flops 4831838208 | bytes 19666944 | tf_op jit(solution)/shard_map/pallas_call | solution.py:111
  253.0 3.4 collective-permute-done.23.refs_3_
  257.5 10.4 %shard_map.376 = (bf16[576,768]{1,0:T(8,128)(2,1)}, bf16[576,768]{1,0:T(8,128)(2,1)}, f32[1,2,384,768]{3,2,1,0:T(8,128)}, f32[1,2,192,768]{3,2,1,0:T(8,128)}) custom-call(s32[4]{0:T(128)} %pad_add_fusion.scalars, bf16[5,512,768]{2,1,0:T(8,128)(2,1)} %get-tuple-element.303.refs_0_, bf16[2,512,768]{2,1,0:T(8,128)(2,1)} %get-tuple-element.325.refs_1_, ...), custom_call_target="tpu_custom_call" | custom-call | flops 2415919104 | bytes 14548992 | tf_op jit(solution)/shard_map/pallas_call | solution.py:111
  271.6 22.1 %shard_map.377 = (f32[512,768]{1,0:T(8,128)}, bf16[512,768]{1,0:T(8,128)(2,1)}, bf16[512,384]{1,0:T(8,128)(2,1)}, bf16[512,384]{1,0:T(8,128)(2,1)}, f32[2,768]{1...) custom-call(s32[4]{0:T(128)} %pad_add_fusion.scalars, f32[512,768]{1,0:T(8,128)} %get-tuple-element.337.refs_0_, ...), custom_call_target="tpu_custom_call" | custom-call | flops 4429185024 | bytes 20219904 | tf_op jit(solution)/shard_map/pallas_call | solution.py:111
  294.4 3.7 collective-permute-done.30.refs_7_
  300.0 17.3 %shard_map.378 = (bf16[960,768]{1,0:T(8,128)(2,1)}, bf16[960,768]{1,0:T(8,128)(2,1)}, f32[2,2,384,768]{3,2,1,0:T(8,128)}, f32[1,2,192,768]{3,2,1,0:T(8,128)}, f3...) custom-call(s32[4]{0:T(128)} %pad_add_fusion.scalars, ...), custom_call_target="tpu_custom_call" | custom-call | flops 4831838208 | bytes 20250624 | tf_op jit(solution)/shard_map/pallas_call | solution.py:111
  319.4 6.2 %collective-permute-start.33 = (bf16[96,768]{1,0:T(8,128)(2,1)}, bf16[96,768]{1,0:T(8,128)(2,1)S(1)}, u32[]{:S(2)}, u32[]{:S(2)}) collective-permute-start(bf16[96,768]{1,0:T(8,128)(2,1)} %get-tuple-element.370), channel_id=1, source_target_pairs={{0,8},{2,10},{4,12},{6,14},{8,0},{10,2},{12,4},{14,6},{16,24},{18,... | collective-permute-start | bytes 442376 | tf_op jit(solution)/shard_map/ppermute | solution.py:683
  325.6 1.9 collective-permute-start.34
  329.0 17.4 %shard_map.379 = (f32[512,768]{1,0:T(8,128)}, f32[2,768]{1,0:T(2,128)}, bf16[2,512,768]{2,1,0:T(8,128)(2,1)}, bf16[2,512,768]{2,1,0:T(8,128)(2,1)}) custom-call(s32[4]{0:T(128)} %pad_add_fusion.scalars, bf16[512,768]{1,0:T(8,128)(2,1)} %get-tuple-element.373.refs_0_, f32[512,768]{1,0:T(8,128)} %get-tuple-element.374.refs_1_, ...), custom_call_target="tpu_custom_call" | custom-call | flops 4831838208 | bytes 24385536 | tf_op jit(solution)/shard_map/pallas_call | solution.py:111
  346.5 5.4 %collective-permute-done.31.refs_6_ = bf16[960,768]{1,0:T(8,128)(2,1)S(1)} collective-permute-done((bf16[960,768]{1,0:T(8,128)(2,1)}, bf16[960,768]{1,0:T(8,128)(2,1)S(1)}, u32[]{:S(2)}, u32[]{:S(2)}) %collective-permute-start.31) | collective-permute-done | bytes 1474592 | tf_op jit(solution)/shard_map/ppermute | solution.py:683
  352.5 3.6 collective-permute-done.36.refs_3_
  357.4 13.4 %shard_map.380 = (bf16[768,768]{1,0:T(8,128)(2,1)}, bf16[768,768]{1,0:T(8,128)(2,1)}, f32[1,2,384,768]{3,2,1,0:T(8,128)}, f32[2,2,192,768]{3,2,1,0:T(8,128)}, f3...) custom-call(s32[4]{0:T(128)} %pad_add_fusion.scalars, ...), custom_call_target="tpu_custom_call" | custom-call | flops 2415919104 | bytes 20597760 | tf_op jit(solution)/shard_map/pallas_call | solution.py:111
  373.7 6.2 %collective-permute-start.39 = (bf16[96,768]{1,0:T(8,128)(2,1)}, bf16[96,768]{1,0:T(8,128)(2,1)S(1)}, u32[]{:S(2)}, u32[]{:S(2)}) collective-permute-start(bf16[96,768]{1,0:T(8,128)(2,1)} %get-tuple-element.403), channel_id=1, source_target_pairs={{0,8},{2,10},{4,12},{6,14},{8,0},{10,2},{12,4},{14,6},{16,24},{18,... | collective-permute-start | bytes 442376 | tf_op jit(solution)/shard_map/ppermute | solution.py:683
  379.9 1.9 collective-permute-start.40
  381.8 1.5 collective-permute-start.41
  383.3 22.1 %shard_map.381 = (f32[512,768]{1,0:T(8,128)}, bf16[512,768]{1,0:T(8,128)(2,1)}, bf16[512,384]{1,0:T(8,128)(2,1)}, bf16[512,384]{1,0:T(8,128)(2,1)}, f32[2,768]{1...) custom-call(s32[4]{0:T(128)} %pad_add_fusion.scalars, f32[512,768]{1,0:T(8,128)} %get-tuple-element.406.refs_0_, ...), custom_call_target="tpu_custom_call" | custom-call | flops 4429185024 | bytes 10782720 | tf_op jit(solution)/shard_map/pallas_call | solution.py:111
  406.8 2.3 collective-permute-done.45.refs_15_
  411.8 13.1 %shard_map.382 = (bf16[640,768]{1,0:T(8,128)(2,1)}, bf16[576,768]{1,0:T(8,128)(2,1)}, f32[1,2,384,768]{3,2,1,0:T(8,128)}, f32[384,128]{1,0:T(8,128)}, f32[1,2,19...) custom-call(s32[4]{0:T(128)} %pad_add_fusion.scalars, ...), custom_call_target="tpu_custom_call" | custom-call | flops 2415919104 | bytes 17841152 | tf_op jit(solution)/shard_map/pallas_call | solution.py:111
  428.0 2.3 collective-permute-start.49
  431.8 10.0 %collective-permute-done.48.refs_6_ = bf16[192,768]{1,0:T(8,128)(2,1)S(1)} collective-permute-done((bf16[192,768]{1,0:T(8,128)(2,1)}, bf16[192,768]{1,0:T(8,128)(2,1)S(1)}, u32[]{:S(2)}, u32[]{:S(2)}) %collective-permute-start.48) | collective-permute-done | bytes 294944 | tf_op jit(solution)/shard_map/ppermute | solution.py:683
  441.8 9.9 %collective-permute-done.49.refs_7_ = bf16[192,768]{1,0:T(8,128)(2,1)S(1)} collective-permute-done((bf16[192,768]{1,0:T(8,128)(2,1)}, bf16[192,768]{1,0:T(8,128)(2,1)S(1)}, u32[]{:S(2)}, u32[]{:S(2)}) %collective-permute-start.49) | collective-permute-done | bytes 294944 | tf_op jit(solution)/shard_map/ppermute | solution.py:683
  453.2 4.9 shard_map.383
  459.0 5.2 collective-permute-start.53
  465.3 1.8 collective-permute-start.54
  467.1 2.0 collective-permute-done.53.refs_5_
  469.0 2.8 collective-permute-start.55
  471.8 4.6 collective-permute-done.54.refs_6_
  477.3 2.8 shard_map.384
  480.1 3.5 collective-permute-start.56
  486.5 3.3 collective-permute-done.56.refs_2_
  489.8 9.1 %collective-permute-done.57.refs_3_ = bf16[112,768]{1,0:T(8,128)(2,1)S(1)} collective-permute-done((bf16[112,768]{1,0:T(8,128)(2,1)}, bf16[112,768]{1,0:T(8,128)(2,1)S(1)}, u32[]{:S(2)}, u32[]{:S(2)}) %collective-permute-start.57) | collective-permute-done | bytes 172064 | tf_op jit(solution)/shard_map/ppermute | solution.py:683
  499.6 2.2 shard_map.385
  505.6 1.7 collective-permute-start.64
  508.3 1.7 collective-permute-done.64
  510.0 3.3 collective-permute-start.65
  513.5 2.3 collective-permute-start.67
  516.3 1.5 collective-permute-done.66
  520.5 10.6 %shard_map.386 = (f32[1,1]{1,0:T(1,128)}, f32[2,48,2304]{2,1,0:T(8,128)}, f32[2,48,2304]{2,1,0:T(8,128)}, f32[2,48,2304]{2,1,0:T(8,128)}, f32[2,48,768]{2,1,0:T(...) custom-call(s32[4]{0:T(128)} %pad_add_fusion.scalars, ...), custom_call_target="tpu_custom_call" | custom-call | flops 53314560 | bytes 14251520 | tf_op jit(solution)/shard_map/pallas_call | solution.py:111
  (296 shorter events, 66.5 us)
Async XLA Ops:
  7.2 163.2 %all-gather.2.cloned.1.call-start = ((), (), s32[]{:S(2)}) async-start(), calls=%async_computation | async-start | bytes 14598144 | tf_op jit(solution)/shard_map/all_gather | solution.py:1159
  13.1 10.4 %collective-permute-start = (bf16[112,768]{1,0:T(8,128)(2,1)}, bf16[112,768]{1,0:T(8,128)(2,1)S(1)}, u32[]{:S(2)}, u32[]{:S(2)}) collective-permute-start(bf16[112,768]{1,0:T(8,128)(2,1)} %get-tuple-element.273.refs_0_), channel_id=1, source_target_pairs={{0,8},{2,10},{4,12},{6,14},{8,0},{10,2},{12,4},{14,6},{16,24},{18,... | collective-permute-start | bytes 516104 | tf_op jit(solution)/shard_map/ppermute | solution.py:683
  16.2 19.6 %collective-permute-start.1 = (bf16[112,768]{1,0:T(8,128)(2,1)}, bf16[112,768]{1,0:T(8,128)(2,1)S(1)}, u32[]{:S(2)}, u32[]{:S(2)}) collective-permute-start(bf16[112,768]{1,0:T(8,128)(2,1)} %get-tuple-element.273.refs_0_), channel_id=1, source_target_pairs={{0,16},{2,18},{4,20},{6,22},{8,24},{10,26},{12,28},{14,30},{16,0},... | collective-permute-start | bytes 516104 | tf_op jit(solution)/shard_map/ppermute | solution.py:683
  18.8 17.0 %collective-permute-start.2 = (bf16[112,768]{1,0:T(8,128)(2,1)}, bf16[112,768]{1,0:T(8,128)(2,1)S(1)}, u32[]{:S(2)}, u32[]{:S(2)}) collective-permute-start(bf16[112,768]{1,0:T(8,128)(2,1)} %get-tuple-element.273.refs_0_), channel_id=1, source_target_pairs={{0,24},{2,26},{4,28},{6,30},{8,16},{10,18},{12,20},{14,22},{16,8},... | collective-permute-start | bytes 516104 | tf_op jit(solution)/shard_map/ppermute | solution.py:683
  39.3 48.1 %collective-permute-start.3 = (bf16[448,768]{1,0:T(8,128)(2,1)}, bf16[448,768]{1,0:T(8,128)(2,1)S(1)}, u32[]{:S(2)}, u32[]{:S(2)}) collective-permute-start(bf16[448,768]{1,0:T(8,128)(2,1)} %shard_map.365.refs_0_), channel_id=1, source_target_pairs={{0,2},{2,0},{4,6},{6,4},{8,10},{10,8},{12,14},{14,12},{16,18},{18,... | collective-permute-start | bytes 2064392 | tf_op jit(solution)/shard_map/ppermute | solution.py:683
  40.8 46.5 %collective-permute-start.4 = (bf16[448,768]{1,0:T(8,128)(2,1)}, bf16[448,768]{1,0:T(8,128)(2,1)S(1)}, u32[]{:S(2)}, u32[]{:S(2)}) collective-permute-start(bf16[448,768]{1,0:T(8,128)(2,1)} %shard_map.365.refs_0_), channel_id=1, source_target_pairs={{0,4},{2,6},{4,0},{6,2},{8,12},{10,14},{12,8},{14,10},{16,20},{18,... | collective-permute-start | bytes 2064392 | tf_op jit(solution)/shard_map/ppermute | solution.py:683
  42.4 22.2 %collective-permute-start.5 = (bf16[192,768]{1,0:T(8,128)(2,1)S(1)}, bf16[192,768]{1,0:T(8,128)(2,1)S(1)}, u32[]{:S(2)}, u32[]{:S(2)}) collective-permute-start(bf16[192,768]{1,0:T(8,128)(2,1)S(1)} %copy-done.29), channel_id=1, source_target_pairs={{0,8},{2,10},{4,12},{6,14},{8,0},{10,2},{12,4},{14,6},{16,24},{18,... | collective-permute-start | bytes 884744 | tf_op jit(solution)/shard_map/ppermute | solution.py:683
  50.9 36.5 %collective-permute-start.6 = (bf16[192,768]{1,0:T(8,128)(2,1)S(1)}, bf16[192,768]{1,0:T(8,128)(2,1)S(1)}, u32[]{:S(2)}, u32[]{:S(2)}) collective-permute-start(bf16[192,768]{1,0:T(8,128)(2,1)S(1)} %copy-done.29), channel_id=1, source_target_pairs={{0,16},{2,18},{4,20},{6,22},{8,24},{10,26},{12,28},{14,30},{16,0},... | collective-permute-start | bytes 884744 | tf_op jit(solution)/shard_map/ppermute | solution.py:683
  51.8 35.5 %collective-permute-start.7 = (bf16[192,768]{1,0:T(8,128)(2,1)S(1)}, bf16[192,768]{1,0:T(8,128)(2,1)S(1)}, u32[]{:S(2)}, u32[]{:S(2)}) collective-permute-start(bf16[192,768]{1,0:T(8,128)(2,1)S(1)} %copy-done.29), channel_id=1, source_target_pairs={{0,24},{2,26},{4,28},{6,30},{8,16},{10,18},{12,20},{14,22},{16,8},... | collective-permute-start | bytes 884744 | tf_op jit(solution)/shard_map/ppermute | solution.py:683
  87.4 7.8 %collective-permute-start.8 = (bf16[256,768]{1,0:T(8,128)(2,1)S(1)}, bf16[256,768]{1,0:T(8,128)(2,1)S(1)}, u32[]{:S(2)}, u32[]{:S(2)}) collective-permute-start(bf16[256,768]{1,0:T(8,128)(2,1)S(1)} %slice.64), channel_id=1, source_target_pairs={{0,2},{2,0},{4,6},{6,4},{8,10},{10,8},{12,14},{14,12},{16,18},{18,... | collective-permute-start | bytes 1179656 | tf_op jit(solution)/shard_map/ppermute | solution.py:683
  87.5 6.8 %collective-permute-start.9 = (bf16[192,768]{1,0:T(8,128)(2,1)S(1)}, bf16[192,768]{1,0:T(8,128)(2,1)S(1)}, u32[]{:S(2)}, u32[]{:S(2)}) collective-permute-start(bf16[192,768]{1,0:T(8,128)(2,1)S(1)} %slice.65), channel_id=1, source_target_pairs={{0,4},{2,6},{4,0},{6,2},{8,12},{10,14},{12,8},{14,10},{16,20},{18,... | collective-permute-start | bytes 884744 | tf_op jit(solution)/shard_map/ppermute | solution.py:683
  100.1 11.9 %collective-permute-start.10 = (bf16[2,16,48,768]{3,2,1,0:T(8,128)(2,1)}, bf16[2,16,48,768]{3,2,1,0:T(8,128)(2,1)}, u32[]{:S(2)}, u32[]{:S(2)}) collective-permute-start(bf16[2,16,48,768]{3,2,1,0:T(8,128)(2,1)} %get-tuple-element.284.refs_6_.refs_11_), channel_id=1, source_target_pairs={{0,1},{1,0},{2,3},{3,2},{4,5},{5,4},{6,7},{7,6},{8,9},{9,8},{10,11... | collective-permute-start | bytes 7077896 | tf_op jit(solution)/shard_map/ppermute | solution.py:679
  104.5 43.1 %collective-permute-start.11 = (bf16[768,768]{1,0:T(8,128)(2,1)}, bf16[768,768]{1,0:T(8,128)(2,1)S(1)}, u32[]{:S(2)}, u32[]{:S(2)}) collective-permute-start(bf16[768,768]{1,0:T(8,128)(2,1)} %shard_map.368.refs_0_), channel_id=1, source_target_pairs={{0,2},{2,0},{4,6},{6,4},{8,10},{10,8},{12,14},{14,12},{16,18},{18,... | collective-permute-start | bytes 3538952 | tf_op jit(solution)/shard_map/ppermute | solution.py:683
  106.3 41.3 %collective-permute-start.12 = (bf16[768,768]{1,0:T(8,128)(2,1)}, bf16[768,768]{1,0:T(8,128)(2,1)S(1)}, u32[]{:S(2)}, u32[]{:S(2)}) collective-permute-start(bf16[768,768]{1,0:T(8,128)(2,1)} %shard_map.368.refs_0_), channel_id=1, source_target_pairs={{0,4},{2,6},{4,0},{6,2},{8,12},{10,14},{12,8},{14,10},{16,20},{18,... | collective-permute-start | bytes 3538952 | tf_op jit(solution)/shard_map/ppermute | solution.py:683
  147.6 15.3 %collective-permute-start.13 = (bf16[384,768]{1,0:T(8,128)(2,1)S(1)}, bf16[384,768]{1,0:T(8,128)(2,1)S(1)}, u32[]{:S(2)}, u32[]{:S(2)}) collective-permute-start(bf16[384,768]{1,0:T(8,128)(2,1)S(1)} %slice.69), channel_id=1, source_target_pairs={{0,2},{2,0},{4,6},{6,4},{8,10},{10,8},{12,14},{14,12},{16,18},{18,... | collective-permute-start | bytes 1769480 | tf_op jit(solution)/shard_map/ppermute | solution.py:683
  149.2 15.0 %collective-permute-start.14 = (bf16[384,768]{1,0:T(8,128)(2,1)S(1)}, bf16[384,768]{1,0:T(8,128)(2,1)S(1)}, u32[]{:S(2)}, u32[]{:S(2)}) collective-permute-start(bf16[384,768]{1,0:T(8,128)(2,1)S(1)} %slice.70), channel_id=1, source_target_pairs={{0,4},{2,6},{4,0},{6,2},{8,12},{10,14},{12,8},{14,10},{16,20},{18,... | collective-permute-start | bytes 1769480 | tf_op jit(solution)/shard_map/ppermute | solution.py:683
  170.3 27.1 %collective-permute-start.15 = (bf16[4,16,48,768]{3,2,1,0:T(8,128)(2,1)}, bf16[4,16,48,768]{3,2,1,0:T(8,128)(2,1)}, u32[]{:S(2)}, u32[]{:S(2)}) collective-permute-start(bf16[4,16,48,768]{3,2,1,0:T(8,128)(2,1)} %shard_map.369.refs_2_.refs_5_), channel_id=1, source_target_pairs={{0,1},{1,0},{2,3},{3,2},{4,5},{5,4},{6,7},{7,6},{8,9},{9,8},{10,11... | collective-permute-start | bytes 14155784 | tf_op jit(solution)/shard_map/ppermute | solution.py:679
  210.1 8.4 %collective-permute-start.16 = (bf16[5,512,768]{2,1,0:T(8,128)(2,1)}, bf16[5,512,768]{2,1,0:T(8,128)(2,1)}, u32[]{:S(2)}, u32[]{:S(2)}) collective-permute-start(bf16[5,512,768]{2,1,0:T(8,128)(2,1)} %get-tuple-element.303.refs_0_), channel_id=1, source_target_pairs={{0,1},{1,0},{2,3},{3,2},{4,5},{5,4},{6,7},{7,6},{8,9},{9,8},{10,11... | collective-permute-start | bytes 11796488 | tf_op jit(solution)/shard_map/ppermute | solution.py:679
  218.0 75.8 %collective-permute-start.26 = (bf16[5,512,768]{2,1,0:T(8,128)(2,1)}, bf16[5,512,768]{2,1,0:T(8,128)(2,1)}, u32[]{:S(2)}, u32[]{:S(2)}) collective-permute-start(bf16[5,512,768]{2,1,0:T(8,128)(2,1)} %get-tuple-element.298.refs_4_.refs_0_), channel_id=1, source_target_pairs={{0,1},{1,0},{2,3},{3,2},{4,5},{5,4},{6,7},{7,6},{8,9},{9,8},{10,11... | collective-permute-start | bytes 11796488 | tf_op jit(solution)/shard_map/ppermute | solution.py:679
  218.4 32.8 %collective-permute-start.20 = (bf16[512,768]{1,0:T(8,128)(2,1)}, bf16[512,768]{1,0:T(8,128)(2,1)S(1)}, u32[]{:S(2)}, u32[]{:S(2)}) collective-permute-start(bf16[512,768]{1,0:T(8,128)(2,1)} %get-tuple-element.323.refs_4_), channel_id=1, source_target_pairs={{0,1},{1,0},{2,3},{3,2},{4,5},{5,4},{6,7},{7,6},{8,9},{9,8},{10,11... | collective-permute-start | bytes 2359304 | tf_op jit(solution)/shard_map/ppermute | solution.py:679
  229.4 21.8 %collective-permute-start.18 = (bf16[384,768]{1,0:T(8,128)(2,1)}, bf16[384,768]{1,0:T(8,128)(2,1)S(1)}, u32[]{:S(2)}, u32[]{:S(2)}) collective-permute-start(bf16[384,768]{1,0:T(8,128)(2,1)} %get-tuple-element.315), channel_id=1, source_target_pairs={{0,2},{2,0},{4,6},{6,4},{8,10},{10,8},{12,14},{14,12},{16,18},{18,... | collective-permute-start | bytes 1769480 | tf_op jit(solution)/shard_map/ppermute | solution.py:683
  230.3 20.9 %collective-permute-start.19 = (bf16[384,768]{1,0:T(8,128)(2,1)}, bf16[384,768]{1,0:T(8,128)(2,1)S(1)}, u32[]{:S(2)}, u32[]{:S(2)}) collective-permute-start(bf16[384,768]{1,0:T(8,128)(2,1)} %get-tuple-element.316), channel_id=1, source_target_pairs={{0,4},{2,6},{4,0},{6,2},{8,12},{10,14},{12,8},{14,10},{16,20},{18,... | collective-permute-start | bytes 1769480 | tf_op jit(solution)/shard_map/ppermute | solution.py:683
  233.1 18.1 %collective-permute-start.21 = (bf16[512,128]{1,0:T(8,128)(2,1)S(1)}, bf16[512,128]{1,0:T(8,128)(2,1)S(1)}, u32[]{:S(2)}, u32[]{:S(2)}) collective-permute-start(bf16[512,128]{1,0:T(8,128)(2,1)S(1)} %copy-done.60), channel_id=1, source_target_pairs={{0,1},{1,0},{2,3},{3,2},{4,5},{5,4},{6,7},{7,6},{8,9},{9,8},{10,11... | collective-permute-start | bytes 393224 | tf_op jit(solution)/shard_map/ppermute | solution.py:679
  252.1 4.3 collective-permute-start.23
  252.5 41.3 %collective-permute-start.27 = (bf16[2,512,768]{2,1,0:T(8,128)(2,1)S(1)}, bf16[2,512,768]{2,1,0:T(8,128)(2,1)S(1)}, u32[]{:S(2)}, u32[]{:S(2)}) collective-permute-start(bf16[2,512,768]{2,1,0:T(8,128)(2,1)S(1)} %copy-done.3), channel_id=1, source_target_pairs={{0,1},{1,0},{2,3},{3,2},{4,5},{5,4},{6,7},{7,6},{8,9},{9,8},{10,11... | collective-permute-start | bytes 4718600 | tf_op jit(solution)/shard_map/ppermute | solution.py:679
  252.6 41.1 %collective-permute-start.28 = (bf16[2,512,768]{2,1,0:T(8,128)(2,1)}, bf16[2,512,768]{2,1,0:T(8,128)(2,1)}, u32[]{:S(2)}, u32[]{:S(2)}) collective-permute-start(bf16[2,512,768]{2,1,0:T(8,128)(2,1)} %get-tuple-element.300.refs_0_), channel_id=1, source_target_pairs={{0,1},{1,0},{2,3},{3,2},{4,5},{5,4},{6,7},{7,6},{8,9},{9,8},{10,11... | collective-permute-start | bytes 4718600 | tf_op jit(solution)/shard_map/ppermute | solution.py:679
  267.9 25.9 %collective-permute-start.24 = (bf16[576,768]{1,0:T(8,128)(2,1)}, bf16[576,768]{1,0:T(8,128)(2,1)}, u32[]{:S(2)}, u32[]{:S(2)}) collective-permute-start(bf16[576,768]{1,0:T(8,128)(2,1)} %get-tuple-element.335), channel_id=1, source_target_pairs={{0,2},{2,0},{4,6},{6,4},{8,10},{10,8},{12,14},{14,12},{16,18},{18,... | collective-permute-start | bytes 2654216 | tf_op jit(solution)/shard_map/ppermute | solution.py:683
  268.9 24.9 %collective-permute-start.25 = (bf16[576,768]{1,0:T(8,128)(2,1)}, bf16[576,768]{1,0:T(8,128)(2,1)}, u32[]{:S(2)}, u32[]{:S(2)}) collective-permute-start(bf16[576,768]{1,0:T(8,128)(2,1)} %get-tuple-element.336), channel_id=1, source_target_pairs={{0,4},{2,6},{4,0},{6,2},{8,12},{10,14},{12,8},{14,10},{16,20},{18,... | collective-permute-start | bytes 2654216 | tf_op jit(solution)/shard_map/ppermute | solution.py:683
  293.8 4.3 collective-permute-start.29
  293.9 4.2 collective-permute-start.30
  317.3 34.6 %collective-permute-start.31 = (bf16[960,768]{1,0:T(8,128)(2,1)}, bf16[960,768]{1,0:T(8,128)(2,1)S(1)}, u32[]{:S(2)}, u32[]{:S(2)}) collective-permute-start(bf16[960,768]{1,0:T(8,128)(2,1)} %get-tuple-element.368), channel_id=1, source_target_pairs={{0,2},{2,0},{4,6},{6,4},{8,10},{10,8},{12,14},{14,12},{16,18},{18,... | collective-permute-start | bytes 4423688 | tf_op jit(solution)/shard_map/ppermute | solution.py:683
  318.3 34.3 %collective-permute-start.32 = (bf16[960,768]{1,0:T(8,128)(2,1)}, bf16[960,768]{1,0:T(8,128)(2,1)S(1)}, u32[]{:S(2)}, u32[]{:S(2)}) collective-permute-start(bf16[960,768]{1,0:T(8,128)(2,1)} %get-tuple-element.369), channel_id=1, source_target_pairs={{0,4},{2,6},{4,0},{6,2},{8,12},{10,14},{12,8},{14,10},{16,20},{18,... | collective-permute-start | bytes 4423688 | tf_op jit(solution)/shard_map/ppermute | solution.py:683
  319.4 27.0 %collective-permute-start.33 = (bf16[96,768]{1,0:T(8,128)(2,1)}, bf16[96,768]{1,0:T(8,128)(2,1)S(1)}, u32[]{:S(2)}, u32[]{:S(2)}) collective-permute-start(bf16[96,768]{1,0:T(8,128)(2,1)} %get-tuple-element.370), channel_id=1, source_target_pairs={{0,8},{2,10},{4,12},{6,14},{8,0},{10,2},{12,4},{14,6},{16,24},{18,... | collective-permute-start | bytes 442376 | tf_op jit(solution)/shard_map/ppermute | solution.py:683
  325.6 20.8 %collective-permute-start.34 = (bf16[96,768]{1,0:T(8,128)(2,1)}, bf16[96,768]{1,0:T(8,128)(2,1)S(1)}, u32[]{:S(2)}, u32[]{:S(2)}) collective-permute-start(bf16[96,768]{1,0:T(8,128)(2,1)} %get-tuple-element.371), channel_id=1, source_target_pairs={{0,16},{2,18},{4,20},{6,22},{8,24},{10,26},{12,28},{14,30},{16,0},... | collective-permute-start | bytes 442376 | tf_op jit(solution)/shard_map/ppermute | solution.py:683
  327.6 18.9 %collective-permute-start.35 = (bf16[96,768]{1,0:T(8,128)(2,1)}, bf16[96,768]{1,0:T(8,128)(2,1)S(1)}, u32[]{:S(2)}, u32[]{:S(2)}) collective-permute-start(bf16[96,768]{1,0:T(8,128)(2,1)} %get-tuple-element.372), channel_id=1, source_target_pairs={{0,24},{2,26},{4,28},{6,30},{8,16},{10,18},{12,20},{14,22},{16,8},... | collective-permute-start | bytes 442376 | tf_op jit(solution)/shard_map/ppermute | solution.py:683
  370.7 34.8 %collective-permute-start.37 = (bf16[768,768]{1,0:T(8,128)(2,1)}, bf16[768,768]{1,0:T(8,128)(2,1)S(1)}, u32[]{:S(2)}, u32[]{:S(2)}) collective-permute-start(bf16[768,768]{1,0:T(8,128)(2,1)} %get-tuple-element.401), channel_id=1, source_target_pairs={{0,2},{2,0},{4,6},{6,4},{8,10},{10,8},{12,14},{14,12},{16,18},{18,... | collective-permute-start | bytes 3538952 | tf_op jit(solution)/shard_map/ppermute | solution.py:683
  371.9 33.6 %collective-permute-start.38 = (bf16[768,768]{1,0:T(8,128)(2,1)}, bf16[768,768]{1,0:T(8,128)(2,1)S(1)}, u32[]{:S(2)}, u32[]{:S(2)}) collective-permute-start(bf16[768,768]{1,0:T(8,128)(2,1)} %get-tuple-element.402), channel_id=1, source_target_pairs={{0,4},{2,6},{4,0},{6,2},{8,12},{10,14},{12,8},{14,10},{16,20},{18,... | collective-permute-start | bytes 3538952 | tf_op jit(solution)/shard_map/ppermute | solution.py:683
  373.7 31.7 %collective-permute-start.39 = (bf16[96,768]{1,0:T(8,128)(2,1)}, bf16[96,768]{1,0:T(8,128)(2,1)S(1)}, u32[]{:S(2)}, u32[]{:S(2)}) collective-permute-start(bf16[96,768]{1,0:T(8,128)(2,1)} %get-tuple-element.403), channel_id=1, source_target_pairs={{0,8},{2,10},{4,12},{6,14},{8,0},{10,2},{12,4},{14,6},{16,24},{18,... | collective-permute-start | bytes 442376 | tf_op jit(solution)/shard_map/ppermute | solution.py:683
  379.9 25.6 %collective-permute-start.40 = (bf16[96,768]{1,0:T(8,128)(2,1)}, bf16[96,768]{1,0:T(8,128)(2,1)S(1)}, u32[]{:S(2)}, u32[]{:S(2)}) collective-permute-start(bf16[96,768]{1,0:T(8,128)(2,1)} %get-tuple-element.404), channel_id=1, source_target_pairs={{0,16},{2,18},{4,20},{6,22},{8,24},{10,26},{12,28},{14,30},{16,0},... | collective-permute-start | bytes 442376 | tf_op jit(solution)/shard_map/ppermute | solution.py:683
  381.8 23.7 %collective-permute-start.41 = (bf16[96,768]{1,0:T(8,128)(2,1)}, bf16[96,768]{1,0:T(8,128)(2,1)S(1)}, u32[]{:S(2)}, u32[]{:S(2)}) collective-permute-start(bf16[96,768]{1,0:T(8,128)(2,1)} %get-tuple-element.405), channel_id=1, source_target_pairs={{0,24},{2,26},{4,28},{6,30},{8,16},{10,18},{12,20},{14,22},{16,8},... | collective-permute-start | bytes 442376 | tf_op jit(solution)/shard_map/ppermute | solution.py:683
  405.5 4.9 collective-permute-start.42
  405.6 4.8 collective-permute-start.43
  406.3 4.1 collective-permute-start.44
  424.9 26.9 %collective-permute-start.46 = (bf16[640,768]{1,0:T(8,128)(2,1)}, bf16[640,768]{1,0:T(8,128)(2,1)S(1)}, u32[]{:S(2)}, u32[]{:S(2)}) collective-permute-start(bf16[640,768]{1,0:T(8,128)(2,1)} %get-tuple-element.448), channel_id=1, source_target_pairs={{0,2},{2,0},{4,6},{6,4},{8,10},{10,8},{12,14},{14,12},{16,18},{18,... | collective-permute-start | bytes 2949128 | tf_op jit(solution)/shard_map/ppermute | solution.py:683
  426.0 25.7 %collective-permute-start.47 = (bf16[576,768]{1,0:T(8,128)(2,1)}, bf16[576,768]{1,0:T(8,128)(2,1)S(1)}, u32[]{:S(2)}, u32[]{:S(2)}) collective-permute-start(bf16[576,768]{1,0:T(8,128)(2,1)} %get-tuple-element.449), channel_id=1, source_target_pairs={{0,4},{2,6},{4,0},{6,2},{8,12},{10,14},{12,8},{14,10},{16,20},{18,... | collective-permute-start | bytes 2654216 | tf_op jit(solution)/shard_map/ppermute | solution.py:683
  427.4 14.3 %collective-permute-start.48 = (bf16[192,768]{1,0:T(8,128)(2,1)}, bf16[192,768]{1,0:T(8,128)(2,1)S(1)}, u32[]{:S(2)}, u32[]{:S(2)}) collective-permute-start(bf16[192,768]{1,0:T(8,128)(2,1)} %get-tuple-element.450), channel_id=1, source_target_pairs={{0,8},{2,10},{4,12},{6,14},{8,0},{10,2},{12,4},{14,6},{16,24},{18,... | collective-permute-start | bytes 884744 | tf_op jit(solution)/shard_map/ppermute | solution.py:683
  428.0 23.7 %collective-permute-start.49 = (bf16[192,768]{1,0:T(8,128)(2,1)}, bf16[192,768]{1,0:T(8,128)(2,1)S(1)}, u32[]{:S(2)}, u32[]{:S(2)}) collective-permute-start(bf16[192,768]{1,0:T(8,128)(2,1)} %get-tuple-element.451), channel_id=1, source_target_pairs={{0,16},{2,18},{4,20},{6,22},{8,24},{10,26},{12,28},{14,30},{16,0},... | collective-permute-start | bytes 884744 | tf_op jit(solution)/shard_map/ppermute | solution.py:683
  430.4 21.4 %collective-permute-start.50 = (bf16[192,768]{1,0:T(8,128)(2,1)}, bf16[192,768]{1,0:T(8,128)(2,1)S(1)}, u32[]{:S(2)}, u32[]{:S(2)}) collective-permute-start(bf16[192,768]{1,0:T(8,128)(2,1)} %get-tuple-element.452), channel_id=1, source_target_pairs={{0,24},{2,26},{4,28},{6,30},{8,16},{10,18},{12,20},{14,22},{16,8},... | collective-permute-start | bytes 884744 | tf_op jit(solution)/shard_map/ppermute | solution.py:683
  458.0 18.4 %collective-permute-start.52 = (bf16[256,768]{1,0:T(8,128)(2,1)}, bf16[256,768]{1,0:T(8,128)(2,1)S(1)}, u32[]{:S(2)}, u32[]{:S(2)}) collective-permute-start(bf16[256,768]{1,0:T(8,128)(2,1)} %get-tuple-element.471), channel_id=1, source_target_pairs={{0,4},{2,6},{4,0},{6,2},{8,12},{10,14},{12,8},{14,10},{16,20},{18,... | collective-permute-start | bytes 1179656 | tf_op jit(solution)/shard_map/ppermute | solution.py:683
  459.0 10.0 %collective-permute-start.53 = (bf16[96,768]{1,0:T(8,128)(2,1)}, bf16[96,768]{1,0:T(8,128)(2,1)S(1)}, u32[]{:S(2)}, u32[]{:S(2)}) collective-permute-start(bf16[96,768]{1,0:T(8,128)(2,1)} %get-tuple-element.472), channel_id=1, source_target_pairs={{0,8},{2,10},{4,12},{6,14},{8,0},{10,2},{12,4},{14,6},{16,24},{18,... | collective-permute-start | bytes 442376 | tf_op jit(solution)/shard_map/ppermute | solution.py:683
  464.2 12.2 %collective-permute-start.51 = (bf16[192,768]{1,0:T(8,128)(2,1)}, bf16[192,768]{1,0:T(8,128)(2,1)S(1)}, u32[]{:S(2)}, u32[]{:S(2)}) collective-permute-start(bf16[192,768]{1,0:T(8,128)(2,1)} %get-tuple-element.470), channel_id=1, source_target_pairs={{0,2},{2,0},{4,6},{6,4},{8,10},{10,8},{12,14},{14,12},{16,18},{18,... | collective-permute-start | bytes 884744 | tf_op jit(solution)/shard_map/ppermute | solution.py:683
  465.3 11.1 %collective-permute-start.54 = (bf16[96,768]{1,0:T(8,128)(2,1)}, bf16[96,768]{1,0:T(8,128)(2,1)S(1)}, u32[]{:S(2)}, u32[]{:S(2)}) collective-permute-start(bf16[96,768]{1,0:T(8,128)(2,1)} %get-tuple-element.473), channel_id=1, source_target_pairs={{0,16},{2,18},{4,20},{6,22},{8,24},{10,26},{12,28},{14,30},{16,0},... | collective-permute-start | bytes 442376 | tf_op jit(solution)/shard_map/ppermute | solution.py:683
  467.1 19.4 %collective-permute-start.59 = (f32[1,2,48,768]{3,2,1,0:T(8,128)S(1)}, f32[1,2,48,768]{3,2,1,0:T(8,128)S(1)}, u32[]{:S(2)}, u32[]{:S(2)}) collective-permute-start(f32[1,2,48,768]{3,2,1,0:T(8,128)S(1)} %copy-done.38), channel_id=1, source_target_pairs={{0,1},{1,0},{2,3},{3,2},{4,5},{5,4},{6,7},{7,6},{8,9},{9,8},{10,11... | collective-permute-start | bytes 884744 | tf_op jit(solution)/shard_map/ppermute | solution.py:679
  469.0 7.4 %collective-permute-start.55 = (bf16[96,768]{1,0:T(8,128)(2,1)}, bf16[96,768]{1,0:T(8,128)(2,1)S(1)}, u32[]{:S(2)}, u32[]{:S(2)}) collective-permute-start(bf16[96,768]{1,0:T(8,128)(2,1)} %get-tuple-element.474), channel_id=1, source_target_pairs={{0,24},{2,26},{4,28},{6,30},{8,16},{10,18},{12,20},{14,22},{16,8},... | collective-permute-start | bytes 442376 | tf_op jit(solution)/shard_map/ppermute | solution.py:683
  476.4 10.1 %collective-permute-start.60 = (f32[1,2,48,768]{3,2,1,0:T(8,128)S(1)}, f32[1,2,48,768]{3,2,1,0:T(8,128)S(1)}, u32[]{:S(2)}, u32[]{:S(2)}) collective-permute-start(f32[1,2,48,768]{3,2,1,0:T(8,128)S(1)} %copy-done.39), channel_id=1, source_target_pairs={{0,1},{1,0},{2,3},{3,2},{4,5},{5,4},{6,7},{7,6},{8,9},{9,8},{10,11... | collective-permute-start | bytes 884744 | tf_op jit(solution)/shard_map/ppermute | solution.py:679
  480.1 9.7 %collective-permute-start.56 = (bf16[112,768]{1,0:T(8,128)(2,1)}, bf16[112,768]{1,0:T(8,128)(2,1)S(1)}, u32[]{:S(2)}, u32[]{:S(2)}) collective-permute-start(bf16[112,768]{1,0:T(8,128)(2,1)} %get-tuple-element.489), channel_id=1, source_target_pairs={{0,8},{2,10},{4,12},{6,14},{8,0},{10,2},{12,4},{14,6},{16,24},{18,... | collective-permute-start | bytes 516104 | tf_op jit(solution)/shard_map/ppermute | solution.py:683
  483.7 15.3 %collective-permute-start.57 = (bf16[112,768]{1,0:T(8,128)(2,1)}, bf16[112,768]{1,0:T(8,128)(2,1)S(1)}, u32[]{:S(2)}, u32[]{:S(2)}) collective-permute-start(bf16[112,768]{1,0:T(8,128)(2,1)} %get-tuple-element.490), channel_id=1, source_target_pairs={{0,16},{2,18},{4,20},{6,22},{8,24},{10,26},{12,28},{14,30},{16,0},... | collective-permute-start | bytes 516104 | tf_op jit(solution)/shard_map/ppermute | solution.py:683
  485.0 13.9 %collective-permute-start.58 = (bf16[112,768]{1,0:T(8,128)(2,1)}, bf16[112,768]{1,0:T(8,128)(2,1)S(1)}, u32[]{:S(2)}, u32[]{:S(2)}) collective-permute-start(bf16[112,768]{1,0:T(8,128)(2,1)} %get-tuple-element.491), channel_id=1, source_target_pairs={{0,24},{2,26},{4,28},{6,30},{8,16},{10,18},{12,20},{14,22},{16,8},... | collective-permute-start | bytes 516104 | tf_op jit(solution)/shard_map/ppermute | solution.py:683
  486.4 32.9 %collective-permute-start.69 = (f32[2,2,48,768]{3,2,1,0:T(8,128)S(1)}, f32[2,2,48,768]{3,2,1,0:T(8,128)S(1)}, u32[]{:S(2)}, u32[]{:S(2)}) collective-permute-start(f32[2,2,48,768]{3,2,1,0:T(8,128)S(1)} %copy-done.19), channel_id=1, source_target_pairs={{0,1},{1,0},{2,3},{3,2},{4,5},{5,4},{6,7},{7,6},{8,9},{9,8},{10,11... | collective-permute-start | bytes 1769480 | tf_op jit(solution)/shard_map/ppermute | solution.py:679
  505.6 4.4 collective-permute-start.64
  510.0 5.7 %collective-permute-start.65 = (f32[1,128]{1,0:T(1,128)S(1)}, f32[1,128]{1,0:T(1,128)S(1)}, u32[]{:S(2)}, u32[]{:S(2)}) collective-permute-start(f32[1,128]{1,0:T(1,128)S(1)} %add_add_fusion.1), channel_id=1, source_target_pairs={{0,8},{2,10},{4,12},{6,14},{8,0},{10,2},{12,4},{14,6},{16,24},{18,... | collective-permute-start | bytes 1544 | tf_op jit(solution)/shard_map/ppermute | solution.py:683
  513.3 4.4 collective-permute-start.66
  513.5 5.3 collective-permute-start.67
  515.8 3.7 collective-permute-start.71
  (86 other events, 704.3 us)
Sparse Core Ops, SparseCore 0:
  13.2 138.1 all-gather.1

commit v14 on v13

--- a/solution.py
+++ b/solution.py
@@ -92,7 +92,7 @@
         self.copies.append(copy)
 
 
-def call(kernel, scalars, outs, ins, anys=(), scratch=(), flops=0, sent=()):
+def call(kernel, scalars, outs, ins, anys=(), scratch=(), flops=0, sent=(), limit=VMEM_LIMIT):
     whole = pl.BlockSpec(memory_space=pltpu.VMEM)
     left = pl.BlockSpec(memory_space=pl.ANY)
 
@@ -118,7 +118,7 @@
         scratch_shapes=[pltpu.VMEM(*outs[i]) for i in sent]
         + list(scratch)
         + [pltpu.SemaphoreType.DMA((len(sent), 5))] * (len(sent) > 0),
-        compiler_params=pltpu.CompilerParams(vmem_limit_bytes=VMEM_LIMIT),
+        compiler_params=pltpu.CompilerParams(vmem_limit_bytes=limit),
         cost_estimate=pl.CostEstimate(
             flops=flops,
             bytes_accessed=sum(x.size * x.dtype.itemsize for x in list(ins) + list(anys)),
@@ -176,7 +176,9 @@
     return (lane < HD) if head == 0 else (lane >= HD)
 
 
-def attention_forward_kernel(base, place_of, ins, anys, outs, w_a, w_b, mixed, bias, sems):
+def attention_forward_kernel(
+    base, place_of, ins, anys, outs, w_a, w_b, mixed, bias, columns_of_lse, sems
+):
     resid, seg_col, seg_row, cosine, sine, gains = ins
     middle, query, keys, values, lse, pack = outs
     width = resid.shape[1]
@@ -207,7 +209,7 @@
             normed_low[...], matrix(w_b, place, 0, half)
         ).astype(LOW)
 
-    lse[...] = jnp.zeros_like(lse)
+    columns_of_lse[...] = jnp.zeros_like(columns_of_lse)
 
     for p in range(width // 128):
         columns = slice(p * 128, (p + 1) * 128)
@@ -221,9 +223,12 @@
             total = jnp.sum(expo, -1, keepdims=True)
             probs = (expo * (1.0 / total)).astype(LOW)
             out.append(dot(probs, v))
-            lane = lax.broadcasted_iota(jnp.int32, lse.shape, 1)
-            lse[...] = jnp.where(lane == 2 * p + head, top + jnp.log(total), lse[...])
+            lane = lax.broadcasted_iota(jnp.int32, columns_of_lse.shape, 1)
+            columns_of_lse[...] = jnp.where(
+                lane == 2 * p + head, top + jnp.log(total), columns_of_lse[...]
+            )
         attended[:, columns] = jnp.where(head_mask(out[0].shape, 0), out[0], out[1]).astype(LOW)
+    lse[...] = columns_of_lse[...].T[: lse.shape[0]]
     attended[...] = ordered(first, attended[:, :half], attended[:, half:])
     out = ordered(
         first,
@@ -239,13 +244,14 @@
     return call(
         functools.partial(attention_forward_kernel, base),
         place,
-        [(one, FULL)] + [(one, LOW)] * 3 + [((length, 128), FULL), ((2,) + one, LOW)],
-        [resid, segments[:, None], segments[None, :], cosine, sine, gains],
+        [(one, FULL)] + [(one, LOW)] * 3 + [((16, length), FULL), ((2,) + one, LOW)],
+        [resid, *segments, cosine, sine, gains],
         weights,
         mixer_scratch(weights)
         + [
             pltpu.VMEM(one, FULL),
             pltpu.VMEM((length, length), FULL),
+            pltpu.VMEM((length, 128), FULL),
             pltpu.SemaphoreType.DMA((4,)),
         ],
         8 * length * width * width + 4 * length * length * width,
@@ -486,8 +492,8 @@
         + [((length, width // 2), LOW)] * 2
         + [((2, width), FULL)]
         + [((2,) + one, LOW)] * 2,
-        [grad_middle, query, keys, values, lse.T[: width // HD]]
-        + [segments[:, None], segments[None, :], cosine, sine, gains, resid],
+        [grad_middle, query, keys, values, lse]
+        + [*segments, cosine, sine, gains, resid],
         weights,
         mixer_scratch(weights)
         + [
@@ -538,7 +544,7 @@
         place,
         [(one, FULL), (one, LOW), (part, LOW), (part, LOW), (one, LOW)]
         + [((length, SMALL), LOW), ((2, width), FULL), ((1, SMALL), FULL)],
-        [resid, table, gains, codons[:, None], weight[:, None]],
+        [resid, table, gains, codons, weight],
         flops=4 * length * width * SMALL,
     )
 
@@ -1022,6 +1028,7 @@
                 [],
                 scratch,
                 4 * new * length * width * width,
+                limit=VMEM_LIMIT if new else 24 << 20,
             )
         )
         if last:
@@ -1035,7 +1042,7 @@
         self.kept, self.small_kept = [None] * 3, [None] * 3
         if last:
             return ties
-        got, ties = tie(got, ties)
+        got, ties, self.shares = tie(got, ties, self.shares)
         to = [got.pop(0) for _ in range(2)] if new or once else []
         for stage in range(3):
             if counts[stage]:
@@ -1172,7 +1179,8 @@
         first = Gather(place, early[0], (rows + 16, rows), rows)
         last = Gather(place, early[1], (2 * rows, 2 * rows), rows)
         first.along_z()
-        first.got, last.shard = tie(first.got, last.shard)
+        columns = (codons[:, None], weight[:, None], segments[:, None])
+        first.got, last.shard, columns = tie(first.got, last.shard, columns)
         first.in_plane()
         last.along_z()
         first.near, last.got = tie(first.near, last.got)
@@ -1185,6 +1193,7 @@
         small = small[:, :, : rows // 16 * SMALL].reshape(16, 16, rows // 16, SMALL)
         small = small.transpose(0, 2, 1, 3).reshape(width, SMALL).T
     else:
+        columns = (codons[:, None], weight[:, None], segments[:, None])
         small = weights[:, 0, :, :SMALL].reshape(width, SMALL).T
     start = -2 * width if fast else weights.shape[3] - layers * 6 * width
     base = lambda l: start + l * 6 * width
@@ -1197,19 +1206,21 @@
     for l in range(layers):
         gain = gains[2 * l : 2 * l + 2]
         middle, query, keys, values, lse, pack = attention_forward(
-            place, resid, mixers[l], base(l), gain[0], cosine, sine, segments
+            place, resid, mixers[l], base(l), gain[0], cosine, sine, (columns[2], segments[None, :])
         )
         if fast and l == 0:
             middle, last.near = tie(middle, last.near)
             last.forward()
+        output, pack_mid, hidden = hidden_forward(place, middle, hiddens[l], base(l), gain[1])
+        if fast and l == 0:
+            output, last.far = tie(output, last.far)
             (own,) = last.result()
             hiddens[-1] = [own, swap_cores(own)]
-            middle, hiddens[-1][0] = tie(middle, own)
-        output, pack_mid, hidden = hidden_forward(place, middle, hiddens[l], base(l), gain[1])
+            output, hiddens[-1][0] = tie(output, own)
         kept.append((resid, query, keys, values, lse, pack, middle, hidden, pack_mid))
         resid = output
     grad, branch, branch_own, branch_other, head_in, grad_logits, grad_norms, sums = head(
-        place, resid, small, gains[2 * layers], codons, weight
+        place, resid, small, gains[2 * layers], columns[0], columns[1]
     )
     grad_norms = [grad_norms]
     early = (head_in, grad_logits, chosen)
@@ -1260,7 +1271,8 @@
             grad_middle,
         )
         grad, branch, branch_own, branch_other, gains_in, mix_own, mix_other = attention_back(
-            place, grad_middle, resid, mixers[l], base(l), gain[0], cosine, sine, segments,
+            place, grad_middle, resid, mixers[l], base(l), gain[0], cosine, sine,
+            (columns[2], segments[None, :]),
             query, keys, values, lse,
         )
         grad_norms = [gains_in, gains_mid] + grad_norms

time: 548 us -> 531 us (0.969)
  waiting for transfers between devices: 163 us -> 154 us
  Pallas kernels: 241 us -> 234 us
    ppermute x47, waiting for transfers between devices: 145 us -> 135 us  [across(): return lax.ppermute(value, 'fsdp', [(i, i ^ mask) for i in range(size)])]
    pallas_call x23, Pallas kernels: 241 us -> 234 us  [call(): pl.pallas_call(body, out_shape=[jax.ShapeDtypeStruct(s, t) for s, t in ou...]
    unnamed x154 -> x148, local copies, waits for them, and re-layouts: 13 us -> 15.5 us
  transfers between devices with their start and end apart: 73 -> 73, of which waited for: 30 -> 31; matrix products, arithmetic and copies ran while one was open for 2% -> 2% of each run, Pallas kernels for 31% -> 30%
where the time goes in v14:
time: 531 us; the launch traced here: 522 us
  Pallas kernels  234 us (44%)
  waiting for transfers between devices  154 us (29%)
  starting transfers between devices  89.6 us (17%)
  local copies, waits for them, and re-layouts  22.8 us (4%)
  between operations  15.4 us (3%)
    pallas_call x23, Pallas kernels, call(): pl.pallas_call(body, out_shape=[jax.ShapeDtypeStruct(s, t) for s, t in ou...  234 us
    ppermute x47, waiting for transfers between devices, across(): return lax.ppermute(value, 'fsdp', [(i, i ^ mask) for i in range(size)])  135 us
    ppermute x47, starting transfers between devices, across(): return lax.ppermute(value, 'fsdp', [(i, i ^ mask) for i in range(size)])  84.2 us
    ppermute x25, waiting for transfers between devices, swap_cores(): return lax.ppermute(value, 'dp', [(0, 1), (1, 0)])  17.2 us
    unnamed x148, local copies, waits for them, and re-layouts  15.5 us
  transfers between devices with their start and end apart: 73, of which 31 were waited for; matrix products, arithmetic and copies ran while one was open for 2% of the time, Pallas kernels for 30%

profile of v14, /device:TPU:0, one launch (start us, length us, event | category | flops | bytes accessed | tf_op | source)
XLA Modules:
  0.0 521.6 jit_solution(7890739369549355461)
XLA Ops:
  10.2 3.0 shard_map.364
  13.2 3.1 collective-permute-start
  16.3 2.6 collective-permute-start.1
  18.9 4.7 collective-permute-done.refs_1_
  23.6 12.3 %collective-permute-done.1.refs_2_ = bf16[112,768]{1,0:T(8,128)(2,1)S(1)} collective-permute-done((bf16[112,768]{1,0:T(8,128)(2,1)}, bf16[112,768]{1,0:T(8,128)(2,1)S(1)}, u32[]{:S(2)}, u32[]{:S(2)}) %collective-permute-start.1) | collective-permute-done | bytes 172064 | tf_op jit(solution)/shard_map/ppermute | solution.py:689
  36.6 2.7 shard_map.365.refs_0_
  39.4 1.6 collective-permute-start.3
  40.9 1.5 collective-permute-start.4
  42.4 8.5 %collective-permute-start.5 = (bf16[192,768]{1,0:T(8,128)(2,1)S(1)}, bf16[192,768]{1,0:T(8,128)(2,1)S(1)}, u32[]{:S(2)}, u32[]{:S(2)}) collective-permute-start(bf16[192,768]{1,0:T(8,128)(2,1)S(1)} %copy-done.37), channel_id=1, source_target_pairs={{0,8},{2,10},{4,12},{6,14},{8,0},{10,2},{12,4},{14,6},{16,24},{18,... | collective-permute-start | bytes 884744 | tf_op jit(solution)/shard_map/ppermute | solution.py:689
  51.9 1.5 collective-permute-start.7
  53.3 11.2 %collective-permute-done.5.refs_1_ = bf16[192,768]{1,0:T(8,128)(2,1)S(1)} collective-permute-done((bf16[192,768]{1,0:T(8,128)(2,1)S(1)}, bf16[192,768]{1,0:T(8,128)(2,1)S(1)}, u32[]{:S(2)}, u32[]{:S(2)}) %collective-permute-start.5) | collective-permute-done | bytes 294944 | tf_op jit(solution)/shard_map/ppermute | solution.py:689
  64.6 22.8 %collective-permute-done.6.refs_2_ = bf16[192,768]{1,0:T(8,128)(2,1)S(1)} collective-permute-done((bf16[192,768]{1,0:T(8,128)(2,1)S(1)}, bf16[192,768]{1,0:T(8,128)(2,1)S(1)}, u32[]{:S(2)}, u32[]{:S(2)}) %collective-permute-start.6) | collective-permute-done | bytes 294944 | tf_op jit(solution)/shard_map/ppermute | solution.py:689
  87.7 6.7 %collective-permute-done.9.refs_4_ = bf16[192,768]{1,0:T(8,128)(2,1)S(1)} collective-permute-done((bf16[192,768]{1,0:T(8,128)(2,1)S(1)}, bf16[192,768]{1,0:T(8,128)(2,1)S(1)}, u32[]{:S(2)}, u32[]{:S(2)}) %collective-permute-start.9) | collective-permute-done | bytes 294944 | tf_op jit(solution)/shard_map/ppermute | solution.py:689
  96.1 4.0 shard_map.366
  100.3 3.1 shard_map.368.refs_0_
  103.4 1.8 collective-permute-start.11
  110.2 1.6 fusion.3.refs_0_.refs_10_
  111.8 14.4 %shard_map.367 = (f32[512,768]{1,0:T(8,128)}, bf16[512,768]{1,0:T(8,128)(2,1)}, bf16[512,768]{1,0:T(8,128)(2,1)}, bf16[512,768]{1,0:T(8,128)(2,1)}, f32[16,512]{1,0:T(8,128)}, /*index=5*/bf16[2,512,768]{2,1,0:T(8,128)(2,1)}) custom-call(s32[4]{0:T(128)} %pad_add_fusion.scalars, f32[512,768]{1,0:T(8,128)} %fusion.3.refs_0_.refs_10_, ...), custom_call_target="tpu_custom_call" | custom-call | flops 3221225472 | bytes 6825984 | tf_op jit(solution)/shard_map/pallas_call | solution.py:111
  126.3 21.3 %collective-permute-done.11.refs_1_ = bf16[768,768]{1,0:T(8,128)(2,1)S(1)} collective-permute-done((bf16[768,768]{1,0:T(8,128)(2,1)}, bf16[768,768]{1,0:T(8,128)(2,1)S(1)}, u32[]{:S(2)}, u32[]{:S(2)}) %collective-permute-start.11) | collective-permute-done | bytes 1179680 | tf_op jit(solution)/shard_map/ppermute | solution.py:689
  152.6 12.8 %shard_map.369 = (f32[512,768]{1,0:T(8,128)}, bf16[5,512,768]{2,1,0:T(8,128)(2,1)}, f32[4,512,768]{2,1,0:T(8,128)}) custom-call(s32[4]{0:T(128)} %pad_add_fusion.scalars, f32[512,768]{1,0:T(8,128)} %get-tuple-element.310.refs_0_.refs_2_, f32[2,768]{1,0:T(2,128)} %get-tuple-element.560.refs_1_.refs_3_, bf16[16,2,48,4608]{3,2,1,0:T(8,128)(2,1)} %bitcast.24), custom_call_target="tpu_custom_call" | custom-call | flops 4831838208 | bytes 15734784 | tf_op jit(solution)/shard_map/pallas_call | solution.py:111
  166.9 5.2 %shard_map.370.refs_2_.refs_5_ = bf16[4,16,48,768]{3,2,1,0:T(8,128)(2,1)} custom-call(s32[4]{0:T(128)} %pad_add_fusion.scalars, bf16[768,768]{1,0:T(8,128)(2,1)} %shard_map.368.refs_0_, bf16[768,768]{1,0:T(8,128)(2,1)} %copy-done.13, bf16[768,768]{1,0:T(8,128)(2,1)} %copy-done.14, bf16[384,768]{1,0:T(8,128)(2,1)} %copy-done.33, bf16[384,768]{1,0:T(8,128)(2,1)} %copy-done.34), custom_call_target="tpu_custom_call" | custom-call | bytes 4718592 | tf_op jit(solution)/shard_map/pallas_call | solution.py:111
  172.2 14.3 %shard_map.371 = (f32[512,768]{1,0:T(8,128)}, bf16[512,768]{1,0:T(8,128)(2,1)}, bf16[512,768]{1,0:T(8,128)(2,1)}, bf16[512,768]{1,0:T(8,128)(2,1)}, f32[16,512]{1,0:T(8,128)}, /*index=5*/bf16[2,512,768]{2,1,0:T(8,128)(2,1)}) custom-call(s32[4]{0:T(128)} %pad_add_fusion.scalars, f32[512,768]{1,0:T(8,128)} %get-tuple-element.319.refs_0_.refs_10_, ...), custom_call_target="tpu_custom_call" | custom-call | flops 3221225472 | bytes 16263168 | tf_op jit(solution)/shard_map/pallas_call | solution.py:111
  186.5 2.2 copy-done.12
  188.7 12.9 %shard_map.372 = (f32[512,768]{1,0:T(8,128)}, bf16[5,512,768]{2,1,0:T(8,128)(2,1)}, f32[4,512,768]{2,1,0:T(8,128)}) custom-call(s32[4]{0:T(128)} %pad_add_fusion.scalars, f32[512,768]{1,0:T(8,128)} %get-tuple-element.321.refs_0_.refs_2_, f32[2,768]{1,0:T(2,128)} %get-tuple-element.558.refs_1_.refs_3_, bf16[4,16,48,768]{3,2,1,0:T(8,128)(2,1)} %shard_map.370.refs_2_.refs_5_, ...), custom_call_target="tpu_custom_call" | custom-call | flops 4831838208 | bytes 11016192 | tf_op jit(solution)/shard_map/pallas_call | solution.py:111
  203.9 5.6 %shard_map.373 = (f32[512,768]{1,0:T(8,128)}, bf16[512,768]{1,0:T(8,128)(2,1)}, bf16[512,384]{1,0:T(8,128)(2,1)}, bf16[512,384]{1,0:T(8,128)(2,1)}, bf16[512,768...) custom-call(s32[4]{0:T(128)} %pad_add_fusion.scalars, ...), custom_call_target="tpu_custom_call" | custom-call | flops 201326592 | bytes 1779712 | tf_op jit(solution)/shard_map/pallas_call | solution.py:111
  212.2 8.8 %shard_map.374 = (bf16[384,768]{1,0:T(8,128)(2,1)}, bf16[384,768]{1,0:T(8,128)(2,1)}, f32[1,2,384,768]{3,2,1,0:T(8,128)}) custom-call(s32[4]{0:T(128)} %pad_add_fusion.scalars, bf16[5,512,768]{2,1,0:T(8,128)(2,1)} %get-tuple-element.323.refs_0_, bf16[512,384]{1,0:T(8,128)(2,1)} %get-tuple-element.327.refs_1_, ...), custom_call_target="tpu_custom_call" | custom-call | flops 2415919104 | bytes 8650752 | tf_op jit(solution)/shard_map/pallas_call | solution.py:111
  221.7 1.5 collective-permute-start.19
  224.9 17.9 %shard_map.375 = (f32[512,768]{1,0:T(8,128)}, f32[2,768]{1,0:T(2,128)}, bf16[2,512,768]{2,1,0:T(8,128)(2,1)}, bf16[2,512,768]{2,1,0:T(8,128)(2,1)}) custom-call(s32[4]{0:T(128)} %pad_add_fusion.scalars, bf16[512,768]{1,0:T(8,128)(2,1)} %get-tuple-element.339.refs_0_, f32[512,768]{1,0:T(8,128)} %get-tuple-element.340.refs_1_, ...), custom_call_target="tpu_custom_call" | custom-call | flops 4831838208 | bytes 19666944 | tf_op jit(solution)/shard_map/pallas_call | solution.py:111
  244.3 2.4 collective-permute-done.23.refs_3_
  246.7 10.3 %shard_map.376 = (bf16[576,768]{1,0:T(8,128)(2,1)}, bf16[576,768]{1,0:T(8,128)(2,1)}, f32[1,2,384,768]{3,2,1,0:T(8,128)}, f32[1,2,192,768]{3,2,1,0:T(8,128)}) custom-call(s32[4]{0:T(128)} %pad_add_fusion.scalars, bf16[5,512,768]{2,1,0:T(8,128)(2,1)} %get-tuple-element.323.refs_0_, bf16[2,512,768]{2,1,0:T(8,128)(2,1)} %get-tuple-element.347.refs_1_, ...), custom_call_target="tpu_custom_call" | custom-call | flops 2415919104 | bytes 14548992 | tf_op jit(solution)/shard_map/pallas_call | solution.py:111
  258.9 22.1 %shard_map.377 = (f32[512,768]{1,0:T(8,128)}, bf16[512,768]{1,0:T(8,128)(2,1)}, bf16[512,384]{1,0:T(8,128)(2,1)}, bf16[512,384]{1,0:T(8,128)(2,1)}, f32[2,768]{1...) custom-call(s32[4]{0:T(128)} %pad_add_fusion.scalars, f32[512,768]{1,0:T(8,128)} %get-tuple-element.359.refs_0_, ...), custom_call_target="tpu_custom_call" | custom-call | flops 4429185024 | bytes 20228096 | tf_op jit(solution)/shard_map/pallas_call | solution.py:111
  281.7 3.4 collective-permute-done.30.refs_7_
  286.5 17.3 %shard_map.378 = (bf16[960,768]{1,0:T(8,128)(2,1)}, bf16[960,768]{1,0:T(8,128)(2,1)}, f32[2,2,384,768]{3,2,1,0:T(8,128)}, f32[1,2,192,768]{3,2,1,0:T(8,128)}, f3...) custom-call(s32[4]{0:T(128)} %pad_add_fusion.scalars, ...), custom_call_target="tpu_custom_call" | custom-call | flops 4831838208 | bytes 20250624 | tf_op jit(solution)/shard_map/pallas_call | solution.py:111
  304.5 1.5 collective-permute-start.32
  306.0 6.3 %collective-permute-start.33 = (bf16[96,768]{1,0:T(8,128)(2,1)}, bf16[96,768]{1,0:T(8,128)(2,1)S(1)}, u32[]{:S(2)}, u32[]{:S(2)}) collective-permute-start(bf16[96,768]{1,0:T(8,128)(2,1)} %get-tuple-element.392), channel_id=1, source_target_pairs={{0,8},{2,10},{4,12},{6,14},{8,0},{10,2},{12,4},{14,6},{16,24},{18,... | collective-permute-start | bytes 442376 | tf_op jit(solution)/shard_map/ppermute | solution.py:689
  312.3 1.9 collective-permute-start.34
  314.2 1.5 collective-permute-start.35
  315.7 17.3 %shard_map.379 = (f32[512,768]{1,0:T(8,128)}, f32[2,768]{1,0:T(2,128)}, bf16[2,512,768]{2,1,0:T(8,128)(2,1)}, bf16[2,512,768]{2,1,0:T(8,128)(2,1)}) custom-call(s32[4]{0:T(128)} %pad_add_fusion.scalars, bf16[512,768]{1,0:T(8,128)(2,1)} %get-tuple-element.395.refs_0_, f32[512,768]{1,0:T(8,128)} %get-tuple-element.396.refs_1_, ...), custom_call_target="tpu_custom_call" | custom-call | flops 4831838208 | bytes 24385536 | tf_op jit(solution)/shard_map/pallas_call | solution.py:111
  333.1 5.3 %collective-permute-done.31.refs_6_ = bf16[960,768]{1,0:T(8,128)(2,1)S(1)} collective-permute-done((bf16[960,768]{1,0:T(8,128)(2,1)}, bf16[960,768]{1,0:T(8,128)(2,1)S(1)}, u32[]{:S(2)}, u32[]{:S(2)}) %collective-permute-start.31) | collective-permute-done | bytes 1474592 | tf_op jit(solution)/shard_map/ppermute | solution.py:689
  338.7 3.6 collective-permute-done.36.refs_3_
  343.6 13.3 %shard_map.380 = (bf16[768,768]{1,0:T(8,128)(2,1)}, bf16[768,768]{1,0:T(8,128)(2,1)}, f32[1,2,384,768]{3,2,1,0:T(8,128)}, f32[2,2,192,768]{3,2,1,0:T(8,128)}, f3...) custom-call(s32[4]{0:T(128)} %pad_add_fusion.scalars, ...), custom_call_target="tpu_custom_call" | custom-call | flops 2415919104 | bytes 20597760 | tf_op jit(solution)/shard_map/pallas_call | solution.py:111
  359.6 6.9 %collective-permute-start.39 = (bf16[96,768]{1,0:T(8,128)(2,1)}, bf16[96,768]{1,0:T(8,128)(2,1)S(1)}, u32[]{:S(2)}, u32[]{:S(2)}) collective-permute-start(bf16[96,768]{1,0:T(8,128)(2,1)} %get-tuple-element.426), channel_id=1, source_target_pairs={{0,8},{2,10},{4,12},{6,14},{8,0},{10,2},{12,4},{14,6},{16,24},{18,... | collective-permute-start | bytes 442376 | tf_op jit(solution)/shard_map/ppermute | solution.py:689
  367.2 1.7 collective-permute-start.41
  368.9 22.1 %shard_map.381 = (f32[512,768]{1,0:T(8,128)}, bf16[512,768]{1,0:T(8,128)(2,1)}, bf16[512,384]{1,0:T(8,128)(2,1)}, bf16[512,384]{1,0:T(8,128)(2,1)}, f32[2,768]{1...) custom-call(s32[4]{0:T(128)} %pad_add_fusion.scalars, f32[512,768]{1,0:T(8,128)} %get-tuple-element.429.refs_0_, ...), custom_call_target="tpu_custom_call" | custom-call | flops 4429185024 | bytes 10790912 | tf_op jit(solution)/shard_map/pallas_call | solution.py:111
  392.3 2.3 collective-permute-done.45.refs_15_
  397.4 13.1 %shard_map.382 = (bf16[640,768]{1,0:T(8,128)(2,1)}, bf16[576,768]{1,0:T(8,128)(2,1)}, f32[1,2,384,768]{3,2,1,0:T(8,128)}, f32[384,128]{1,0:T(8,128)}, f32[1,2,19...) custom-call(s32[4]{0:T(128)} %pad_add_fusion.scalars, ...), custom_call_target="tpu_custom_call" | custom-call | flops 2415919104 | bytes 17841152 | tf_op jit(solution)/shard_map/pallas_call | solution.py:111
  414.1 2.0 collective-permute-start.49
  417.6 10.1 %collective-permute-done.48.refs_6_ = bf16[192,768]{1,0:T(8,128)(2,1)S(1)} collective-permute-done((bf16[192,768]{1,0:T(8,128)(2,1)}, bf16[192,768]{1,0:T(8,128)(2,1)S(1)}, u32[]{:S(2)}, u32[]{:S(2)}) %collective-permute-start.48) | collective-permute-done | bytes 294944 | tf_op jit(solution)/shard_map/ppermute | solution.py:689
  427.7 10.1 %collective-permute-done.49.refs_7_ = bf16[192,768]{1,0:T(8,128)(2,1)S(1)} collective-permute-done((bf16[192,768]{1,0:T(8,128)(2,1)}, bf16[192,768]{1,0:T(8,128)(2,1)S(1)}, u32[]{:S(2)}, u32[]{:S(2)}) %collective-permute-start.49) | collective-permute-done | bytes 294944 | tf_op jit(solution)/shard_map/ppermute | solution.py:689
  437.8 1.7 copy-done
  444.6 1.5 collective-permute-start.52
  446.6 5.3 %collective-permute-start.53 = (bf16[96,768]{1,0:T(8,128)(2,1)S(1)}, bf16[96,768]{1,0:T(8,128)(2,1)S(1)}, u32[]{:S(2)}, u32[]{:S(2)}) collective-permute-start(bf16[96,768]{1,0:T(8,128)(2,1)S(1)} %get-tuple-element.500), channel_id=1, source_target_pairs={{0,8},{2,10},{4,12},{6,14},{8,0},{10,2},{12,4},{14,6},{16,24},{18,... | collective-permute-start | bytes 442376 | tf_op jit(solution)/shard_map/ppermute | solution.py:689
  451.9 1.8 collective-permute-start.54
  456.2 8.4 %collective-permute-done.54.refs_6_ = bf16[96,768]{1,0:T(8,128)(2,1)S(1)} collective-permute-done((bf16[96,768]{1,0:T(8,128)(2,1)S(1)}, bf16[96,768]{1,0:T(8,128)(2,1)S(1)}, u32[]{:S(2)}, u32[]{:S(2)}) %collective-permute-start.54) | collective-permute-done | bytes 147488 | tf_op jit(solution)/shard_map/ppermute | solution.py:689
  466.0 2.1 collective-permute-start.56
  469.2 1.5 collective-permute-start.58
  470.6 5.1 collective-permute-done.56.refs_2_
  475.7 7.9 %collective-permute-done.57.refs_3_ = bf16[112,768]{1,0:T(8,128)(2,1)S(1)} collective-permute-done((bf16[112,768]{1,0:T(8,128)(2,1)S(1)}, bf16[112,768]{1,0:T(8,128)(2,1)S(1)}, u32[]{:S(2)}, u32[]{:S(2)}) %collective-permute-start.57) | collective-permute-done | bytes 172064 | tf_op jit(solution)/shard_map/ppermute | solution.py:689
  486.0 1.6 collective-permute-start.62
  488.3 1.5 collective-permute-start.64
  491.2 1.5 collective-permute-done.64
  492.7 3.1 collective-permute-start.65
  500.3 2.0 collective-permute-done.67
  503.9 10.6 %shard_map.386 = (f32[1,1]{1,0:T(1,128)}, f32[2,48,2304]{2,1,0:T(8,128)}, f32[2,48,2304]{2,1,0:T(8,128)}, f32[2,48,2304]{2,1,0:T(8,128)}, f32[2,48,768]{2,1,0:T(...) custom-call(s32[4]{0:T(128)} %pad_add_fusion.scalars, ...), custom_call_target="tpu_custom_call" | custom-call | flops 53314560 | bytes 14251520 | tf_op jit(solution)/shard_map/pallas_call | solution.py:111
  (286 shorter events, 66.3 us)
Async XLA Ops:
  7.2 145.4 %all-gather.2.cloned.1.call-start = ((), (), s32[]{:S(2)}) async-start(), calls=%async_computation | async-start | bytes 14598144 | tf_op jit(solution)/shard_map/all_gather | solution.py:1166
  13.2 10.4 %collective-permute-start = (bf16[112,768]{1,0:T(8,128)(2,1)}, bf16[112,768]{1,0:T(8,128)(2,1)S(1)}, u32[]{:S(2)}, u32[]{:S(2)}) collective-permute-start(bf16[112,768]{1,0:T(8,128)(2,1)} %get-tuple-element.289.refs_0_), channel_id=1, source_target_pairs={{0,8},{2,10},{4,12},{6,14},{8,0},{10,2},{12,4},{14,6},{16,24},{18,... | collective-permute-start | bytes 516104 | tf_op jit(solution)/shard_map/ppermute | solution.py:689
  16.3 19.6 %collective-permute-start.1 = (bf16[112,768]{1,0:T(8,128)(2,1)}, bf16[112,768]{1,0:T(8,128)(2,1)S(1)}, u32[]{:S(2)}, u32[]{:S(2)}) collective-permute-start(bf16[112,768]{1,0:T(8,128)(2,1)} %get-tuple-element.289.refs_0_), channel_id=1, source_target_pairs={{0,16},{2,18},{4,20},{6,22},{8,24},{10,26},{12,28},{14,30},{16,0},... | collective-permute-start | bytes 516104 | tf_op jit(solution)/shard_map/ppermute | solution.py:689
  18.9 17.0 %collective-permute-start.2 = (bf16[112,768]{1,0:T(8,128)(2,1)}, bf16[112,768]{1,0:T(8,128)(2,1)S(1)}, u32[]{:S(2)}, u32[]{:S(2)}) collective-permute-start(bf16[112,768]{1,0:T(8,128)(2,1)} %get-tuple-element.289.refs_0_), channel_id=1, source_target_pairs={{0,24},{2,26},{4,28},{6,30},{8,16},{10,18},{12,20},{14,22},{16,8},... | collective-permute-start | bytes 516104 | tf_op jit(solution)/shard_map/ppermute | solution.py:689
  39.4 48.1 %collective-permute-start.3 = (bf16[448,768]{1,0:T(8,128)(2,1)}, bf16[448,768]{1,0:T(8,128)(2,1)S(1)}, u32[]{:S(2)}, u32[]{:S(2)}) collective-permute-start(bf16[448,768]{1,0:T(8,128)(2,1)} %shard_map.365.refs_0_), channel_id=1, source_target_pairs={{0,2},{2,0},{4,6},{6,4},{8,10},{10,8},{12,14},{14,12},{16,18},{18,... | collective-permute-start | bytes 2064392 | tf_op jit(solution)/shard_map/ppermute | solution.py:689
  40.9 46.5 %collective-permute-start.4 = (bf16[448,768]{1,0:T(8,128)(2,1)}, bf16[448,768]{1,0:T(8,128)(2,1)S(1)}, u32[]{:S(2)}, u32[]{:S(2)}) collective-permute-start(bf16[448,768]{1,0:T(8,128)(2,1)} %shard_map.365.refs_0_), channel_id=1, source_target_pairs={{0,4},{2,6},{4,0},{6,2},{8,12},{10,14},{12,8},{14,10},{16,20},{18,... | collective-permute-start | bytes 2064392 | tf_op jit(solution)/shard_map/ppermute | solution.py:689
  42.4 22.2 %collective-permute-start.5 = (bf16[192,768]{1,0:T(8,128)(2,1)S(1)}, bf16[192,768]{1,0:T(8,128)(2,1)S(1)}, u32[]{:S(2)}, u32[]{:S(2)}) collective-permute-start(bf16[192,768]{1,0:T(8,128)(2,1)S(1)} %copy-done.37), channel_id=1, source_target_pairs={{0,8},{2,10},{4,12},{6,14},{8,0},{10,2},{12,4},{14,6},{16,24},{18,... | collective-permute-start | bytes 884744 | tf_op jit(solution)/shard_map/ppermute | solution.py:689
  50.9 36.5 %collective-permute-start.6 = (bf16[192,768]{1,0:T(8,128)(2,1)S(1)}, bf16[192,768]{1,0:T(8,128)(2,1)S(1)}, u32[]{:S(2)}, u32[]{:S(2)}) collective-permute-start(bf16[192,768]{1,0:T(8,128)(2,1)S(1)} %copy-done.37), channel_id=1, source_target_pairs={{0,16},{2,18},{4,20},{6,22},{8,24},{10,26},{12,28},{14,30},{16,0},... | collective-permute-start | bytes 884744 | tf_op jit(solution)/shard_map/ppermute | solution.py:689
  51.9 35.5 %collective-permute-start.7 = (bf16[192,768]{1,0:T(8,128)(2,1)S(1)}, bf16[192,768]{1,0:T(8,128)(2,1)S(1)}, u32[]{:S(2)}, u32[]{:S(2)}) collective-permute-start(bf16[192,768]{1,0:T(8,128)(2,1)S(1)} %copy-done.37), channel_id=1, source_target_pairs={{0,24},{2,26},{4,28},{6,30},{8,16},{10,18},{12,20},{14,22},{16,8},... | collective-permute-start | bytes 884744 | tf_op jit(solution)/shard_map/ppermute | solution.py:689
  87.5 7.8 %collective-permute-start.8 = (bf16[256,768]{1,0:T(8,128)(2,1)S(1)}, bf16[256,768]{1,0:T(8,128)(2,1)S(1)}, u32[]{:S(2)}, u32[]{:S(2)}) collective-permute-start(bf16[256,768]{1,0:T(8,128)(2,1)S(1)} %slice.58), channel_id=1, source_target_pairs={{0,2},{2,0},{4,6},{6,4},{8,10},{10,8},{12,14},{14,12},{16,18},{18,... | collective-permute-start | bytes 1179656 | tf_op jit(solution)/shard_map/ppermute | solution.py:689
  87.6 6.8 %collective-permute-start.9 = (bf16[192,768]{1,0:T(8,128)(2,1)S(1)}, bf16[192,768]{1,0:T(8,128)(2,1)S(1)}, u32[]{:S(2)}, u32[]{:S(2)}) collective-permute-start(bf16[192,768]{1,0:T(8,128)(2,1)S(1)} %slice.59), channel_id=1, source_target_pairs={{0,4},{2,6},{4,0},{6,2},{8,12},{10,14},{12,8},{14,10},{16,20},{18,... | collective-permute-start | bytes 884744 | tf_op jit(solution)/shard_map/ppermute | solution.py:689
  100.2 11.7 %collective-permute-start.10 = (bf16[2,16,48,768]{3,2,1,0:T(8,128)(2,1)}, bf16[2,16,48,768]{3,2,1,0:T(8,128)(2,1)}, u32[]{:S(2)}, u32[]{:S(2)}) collective-permute-start(bf16[2,16,48,768]{3,2,1,0:T(8,128)(2,1)} %get-tuple-element.301.refs_6_.refs_11_), channel_id=1, source_target_pairs={{0,1},{1,0},{2,3},{3,2},{4,5},{5,4},{6,7},{7,6},{8,9},{9,8},{10,11... | collective-permute-start | bytes 7077896 | tf_op jit(solution)/shard_map/ppermute | solution.py:685
  103.4 44.2 %collective-permute-start.11 = (bf16[768,768]{1,0:T(8,128)(2,1)}, bf16[768,768]{1,0:T(8,128)(2,1)S(1)}, u32[]{:S(2)}, u32[]{:S(2)}) collective-permute-start(bf16[768,768]{1,0:T(8,128)(2,1)} %shard_map.368.refs_0_), channel_id=1, source_target_pairs={{0,2},{2,0},{4,6},{6,4},{8,10},{10,8},{12,14},{14,12},{16,18},{18,... | collective-permute-start | bytes 3538952 | tf_op jit(solution)/shard_map/ppermute | solution.py:689
  105.2 42.4 %collective-permute-start.12 = (bf16[768,768]{1,0:T(8,128)(2,1)}, bf16[768,768]{1,0:T(8,128)(2,1)S(1)}, u32[]{:S(2)}, u32[]{:S(2)}) collective-permute-start(bf16[768,768]{1,0:T(8,128)(2,1)} %shard_map.368.refs_0_), channel_id=1, source_target_pairs={{0,4},{2,6},{4,0},{6,2},{8,12},{10,14},{12,8},{14,10},{16,20},{18,... | collective-permute-start | bytes 3538952 | tf_op jit(solution)/shard_map/ppermute | solution.py:689
  148.6 16.7 %collective-permute-start.13 = (bf16[384,768]{1,0:T(8,128)(2,1)}, bf16[384,768]{1,0:T(8,128)(2,1)S(1)}, u32[]{:S(2)}, u32[]{:S(2)}) collective-permute-start(bf16[384,768]{1,0:T(8,128)(2,1)} %slice.64), channel_id=1, source_target_pairs={{0,2},{2,0},{4,6},{6,4},{8,10},{10,8},{12,14},{14,12},{16,18},{18,... | collective-permute-start | bytes 1769480 | tf_op jit(solution)/shard_map/ppermute | solution.py:689
  150.9 15.2 %collective-permute-start.14 = (bf16[384,768]{1,0:T(8,128)(2,1)}, bf16[384,768]{1,0:T(8,128)(2,1)S(1)}, u32[]{:S(2)}, u32[]{:S(2)}) collective-permute-start(bf16[384,768]{1,0:T(8,128)(2,1)} %slice.65), channel_id=1, source_target_pairs={{0,4},{2,6},{4,0},{6,2},{8,12},{10,14},{12,8},{14,10},{16,20},{18,... | collective-permute-start | bytes 1769480 | tf_op jit(solution)/shard_map/ppermute | solution.py:689
  172.1 14.4 %collective-permute-start.15 = (bf16[4,16,48,768]{3,2,1,0:T(8,128)(2,1)}, bf16[4,16,48,768]{3,2,1,0:T(8,128)(2,1)S(1)}, u32[]{:S(2)}, u32[]{:S(2)}) collective-permute-start(bf16[4,16,48,768]{3,2,1,0:T(8,128)(2,1)} %shard_map.370.refs_2_.refs_5_), channel_id=1, source_target_pairs={{0,1},{1,0},{2,3},{3,2},{4,5},{5,4},{6,7},{7,6},{8,9},{9,8},{10,11... | collective-permute-start | bytes 14155784 | tf_op jit(solution)/shard_map/ppermute | solution.py:685
  201.6 8.5 %collective-permute-start.16 = (bf16[5,512,768]{2,1,0:T(8,128)(2,1)}, bf16[5,512,768]{2,1,0:T(8,128)(2,1)}, u32[]{:S(2)}, u32[]{:S(2)}) collective-permute-start(bf16[5,512,768]{2,1,0:T(8,128)(2,1)} %get-tuple-element.323.refs_0_), channel_id=1, source_target_pairs={{0,1},{1,0},{2,3},{3,2},{4,5},{5,4},{6,7},{7,6},{8,9},{9,8},{10,11... | collective-permute-start | bytes 11796488 | tf_op jit(solution)/shard_map/ppermute | solution.py:685
  209.6 71.5 %collective-permute-start.26 = (bf16[5,512,768]{2,1,0:T(8,128)(2,1)}, bf16[5,512,768]{2,1,0:T(8,128)(2,1)S(1)}, u32[]{:S(2)}, u32[]{:S(2)}) collective-permute-start(bf16[5,512,768]{2,1,0:T(8,128)(2,1)} %get-tuple-element.312.refs_4_.refs_0_), channel_id=1, source_target_pairs={{0,1},{1,0},{2,3},{3,2},{4,5},{5,4},{6,7},{7,6},{8,9},{9,8},{10,11... | collective-permute-start | bytes 11796488 | tf_op jit(solution)/shard_map/ppermute | solution.py:685
  210.0 32.8 %collective-permute-start.20 = (bf16[512,768]{1,0:T(8,128)(2,1)}, bf16[512,768]{1,0:T(8,128)(2,1)S(1)}, u32[]{:S(2)}, u32[]{:S(2)}) collective-permute-start(bf16[512,768]{1,0:T(8,128)(2,1)} %get-tuple-element.345.refs_4_), channel_id=1, source_target_pairs={{0,1},{1,0},{2,3},{3,2},{4,5},{5,4},{6,7},{7,6},{8,9},{9,8},{10,11... | collective-permute-start | bytes 2359304 | tf_op jit(solution)/shard_map/ppermute | solution.py:685
  221.0 21.8 %collective-permute-start.18 = (bf16[384,768]{1,0:T(8,128)(2,1)}, bf16[384,768]{1,0:T(8,128)(2,1)S(1)}, u32[]{:S(2)}, u32[]{:S(2)}) collective-permute-start(bf16[384,768]{1,0:T(8,128)(2,1)} %get-tuple-element.337), channel_id=1, source_target_pairs={{0,2},{2,0},{4,6},{6,4},{8,10},{10,8},{12,14},{14,12},{16,18},{18,... | collective-permute-start | bytes 1769480 | tf_op jit(solution)/shard_map/ppermute | solution.py:689
  221.7 21.2 %collective-permute-start.19 = (bf16[384,768]{1,0:T(8,128)(2,1)}, bf16[384,768]{1,0:T(8,128)(2,1)S(1)}, u32[]{:S(2)}, u32[]{:S(2)}) collective-permute-start(bf16[384,768]{1,0:T(8,128)(2,1)} %get-tuple-element.338), channel_id=1, source_target_pairs={{0,4},{2,6},{4,0},{6,2},{8,12},{10,14},{12,8},{14,10},{16,20},{18,... | collective-permute-start | bytes 1769480 | tf_op jit(solution)/shard_map/ppermute | solution.py:689
  224.8 18.1 %collective-permute-start.21 = (bf16[512,128]{1,0:T(8,128)(2,1)S(1)}, bf16[512,128]{1,0:T(8,128)(2,1)S(1)}, u32[]{:S(2)}, u32[]{:S(2)}) collective-permute-start(bf16[512,128]{1,0:T(8,128)(2,1)S(1)} %copy-done.57), channel_id=1, source_target_pairs={{0,1},{1,0},{2,3},{3,2},{4,5},{5,4},{6,7},{7,6},{8,9},{9,8},{10,11... | collective-permute-start | bytes 393224 | tf_op jit(solution)/shard_map/ppermute | solution.py:685
  243.7 37.2 %collective-permute-start.27 = (bf16[2,512,768]{2,1,0:T(8,128)(2,1)S(1)}, bf16[2,512,768]{2,1,0:T(8,128)(2,1)S(1)}, u32[]{:S(2)}, u32[]{:S(2)}) collective-permute-start(bf16[2,512,768]{2,1,0:T(8,128)(2,1)S(1)} %copy-done.16), channel_id=1, source_target_pairs={{0,1},{1,0},{2,3},{3,2},{4,5},{5,4},{6,7},{7,6},{8,9},{9,8},{10,11... | collective-permute-start | bytes 4718600 | tf_op jit(solution)/shard_map/ppermute | solution.py:685
  244.1 36.9 %collective-permute-start.28 = (bf16[2,512,768]{2,1,0:T(8,128)(2,1)}, bf16[2,512,768]{2,1,0:T(8,128)(2,1)}, u32[]{:S(2)}, u32[]{:S(2)}) collective-permute-start(bf16[2,512,768]{2,1,0:T(8,128)(2,1)} %get-tuple-element.320.refs_0_), channel_id=1, source_target_pairs={{0,1},{1,0},{2,3},{3,2},{4,5},{5,4},{6,7},{7,6},{8,9},{9,8},{10,11... | collective-permute-start | bytes 4718600 | tf_op jit(solution)/shard_map/ppermute | solution.py:685
  257.0 24.1 %collective-permute-start.24 = (bf16[576,768]{1,0:T(8,128)(2,1)}, bf16[576,768]{1,0:T(8,128)(2,1)S(1)}, u32[]{:S(2)}, u32[]{:S(2)}) collective-permute-start(bf16[576,768]{1,0:T(8,128)(2,1)} %get-tuple-element.357), channel_id=1, source_target_pairs={{0,2},{2,0},{4,6},{6,4},{8,10},{10,8},{12,14},{14,12},{16,18},{18,... | collective-permute-start | bytes 2654216 | tf_op jit(solution)/shard_map/ppermute | solution.py:689
  258.1 23.0 %collective-permute-start.25 = (bf16[576,768]{1,0:T(8,128)(2,1)}, bf16[576,768]{1,0:T(8,128)(2,1)}, u32[]{:S(2)}, u32[]{:S(2)}) collective-permute-start(bf16[576,768]{1,0:T(8,128)(2,1)} %get-tuple-element.358), channel_id=1, source_target_pairs={{0,4},{2,6},{4,0},{6,2},{8,12},{10,14},{12,8},{14,10},{16,20},{18,... | collective-permute-start | bytes 2654216 | tf_op jit(solution)/shard_map/ppermute | solution.py:689
  281.1 4.2 collective-permute-start.29
  281.2 3.9 collective-permute-start.30
  303.8 34.6 %collective-permute-start.31 = (bf16[960,768]{1,0:T(8,128)(2,1)}, bf16[960,768]{1,0:T(8,128)(2,1)S(1)}, u32[]{:S(2)}, u32[]{:S(2)}) collective-permute-start(bf16[960,768]{1,0:T(8,128)(2,1)} %get-tuple-element.390), channel_id=1, source_target_pairs={{0,2},{2,0},{4,6},{6,4},{8,10},{10,8},{12,14},{14,12},{16,18},{18,... | collective-permute-start | bytes 4423688 | tf_op jit(solution)/shard_map/ppermute | solution.py:689
  304.5 34.3 %collective-permute-start.32 = (bf16[960,768]{1,0:T(8,128)(2,1)}, bf16[960,768]{1,0:T(8,128)(2,1)S(1)}, u32[]{:S(2)}, u32[]{:S(2)}) collective-permute-start(bf16[960,768]{1,0:T(8,128)(2,1)} %get-tuple-element.391), channel_id=1, source_target_pairs={{0,4},{2,6},{4,0},{6,2},{8,12},{10,14},{12,8},{14,10},{16,20},{18,... | collective-permute-start | bytes 4423688 | tf_op jit(solution)/shard_map/ppermute | solution.py:689
  306.0 27.0 %collective-permute-start.33 = (bf16[96,768]{1,0:T(8,128)(2,1)}, bf16[96,768]{1,0:T(8,128)(2,1)S(1)}, u32[]{:S(2)}, u32[]{:S(2)}) collective-permute-start(bf16[96,768]{1,0:T(8,128)(2,1)} %get-tuple-element.392), channel_id=1, source_target_pairs={{0,8},{2,10},{4,12},{6,14},{8,0},{10,2},{12,4},{14,6},{16,24},{18,... | collective-permute-start | bytes 442376 | tf_op jit(solution)/shard_map/ppermute | solution.py:689
  312.3 20.7 %collective-permute-start.34 = (bf16[96,768]{1,0:T(8,128)(2,1)}, bf16[96,768]{1,0:T(8,128)(2,1)S(1)}, u32[]{:S(2)}, u32[]{:S(2)}) collective-permute-start(bf16[96,768]{1,0:T(8,128)(2,1)} %get-tuple-element.393), channel_id=1, source_target_pairs={{0,16},{2,18},{4,20},{6,22},{8,24},{10,26},{12,28},{14,30},{16,0},... | collective-permute-start | bytes 442376 | tf_op jit(solution)/shard_map/ppermute | solution.py:689
  314.2 18.9 %collective-permute-start.35 = (bf16[96,768]{1,0:T(8,128)(2,1)}, bf16[96,768]{1,0:T(8,128)(2,1)S(1)}, u32[]{:S(2)}, u32[]{:S(2)}) collective-permute-start(bf16[96,768]{1,0:T(8,128)(2,1)} %get-tuple-element.394), channel_id=1, source_target_pairs={{0,24},{2,26},{4,28},{6,30},{8,16},{10,18},{12,20},{14,22},{16,8},... | collective-permute-start | bytes 442376 | tf_op jit(solution)/shard_map/ppermute | solution.py:689
  356.9 34.2 %collective-permute-start.37 = (bf16[768,768]{1,0:T(8,128)(2,1)}, bf16[768,768]{1,0:T(8,128)(2,1)S(1)}, u32[]{:S(2)}, u32[]{:S(2)}) collective-permute-start(bf16[768,768]{1,0:T(8,128)(2,1)} %get-tuple-element.424), channel_id=1, source_target_pairs={{0,2},{2,0},{4,6},{6,4},{8,10},{10,8},{12,14},{14,12},{16,18},{18,... | collective-permute-start | bytes 3538952 | tf_op jit(solution)/shard_map/ppermute | solution.py:689
  358.3 32.8 %collective-permute-start.38 = (bf16[768,768]{1,0:T(8,128)(2,1)}, bf16[768,768]{1,0:T(8,128)(2,1)S(1)}, u32[]{:S(2)}, u32[]{:S(2)}) collective-permute-start(bf16[768,768]{1,0:T(8,128)(2,1)} %get-tuple-element.425), channel_id=1, source_target_pairs={{0,4},{2,6},{4,0},{6,2},{8,12},{10,14},{12,8},{14,10},{16,20},{18,... | collective-permute-start | bytes 3538952 | tf_op jit(solution)/shard_map/ppermute | solution.py:689
  359.6 31.4 %collective-permute-start.39 = (bf16[96,768]{1,0:T(8,128)(2,1)}, bf16[96,768]{1,0:T(8,128)(2,1)S(1)}, u32[]{:S(2)}, u32[]{:S(2)}) collective-permute-start(bf16[96,768]{1,0:T(8,128)(2,1)} %get-tuple-element.426), channel_id=1, source_target_pairs={{0,8},{2,10},{4,12},{6,14},{8,0},{10,2},{12,4},{14,6},{16,24},{18,... | collective-permute-start | bytes 442376 | tf_op jit(solution)/shard_map/ppermute | solution.py:689
  366.5 24.5 %collective-permute-start.40 = (bf16[96,768]{1,0:T(8,128)(2,1)}, bf16[96,768]{1,0:T(8,128)(2,1)S(1)}, u32[]{:S(2)}, u32[]{:S(2)}) collective-permute-start(bf16[96,768]{1,0:T(8,128)(2,1)} %get-tuple-element.427), channel_id=1, source_target_pairs={{0,16},{2,18},{4,20},{6,22},{8,24},{10,26},{12,28},{14,30},{16,0},... | collective-permute-start | bytes 442376 | tf_op jit(solution)/shard_map/ppermute | solution.py:689
  367.2 23.8 %collective-permute-start.41 = (bf16[96,768]{1,0:T(8,128)(2,1)}, bf16[96,768]{1,0:T(8,128)(2,1)S(1)}, u32[]{:S(2)}, u32[]{:S(2)}) collective-permute-start(bf16[96,768]{1,0:T(8,128)(2,1)} %get-tuple-element.428), channel_id=1, source_target_pairs={{0,24},{2,26},{4,28},{6,30},{8,16},{10,18},{12,20},{14,22},{16,8},... | collective-permute-start | bytes 442376 | tf_op jit(solution)/shard_map/ppermute | solution.py:689
  391.1 4.9 collective-permute-start.42
  391.2 4.8 collective-permute-start.43
  391.9 4.1 collective-permute-start.44
  410.4 27.4 %collective-permute-start.46 = (bf16[640,768]{1,0:T(8,128)(2,1)}, bf16[640,768]{1,0:T(8,128)(2,1)S(1)}, u32[]{:S(2)}, u32[]{:S(2)}) collective-permute-start(bf16[640,768]{1,0:T(8,128)(2,1)} %get-tuple-element.473), channel_id=1, source_target_pairs={{0,2},{2,0},{4,6},{6,4},{8,10},{10,8},{12,14},{14,12},{16,18},{18,... | collective-permute-start | bytes 2949128 | tf_op jit(solution)/shard_map/ppermute | solution.py:689
  411.8 26.0 %collective-permute-start.47 = (bf16[576,768]{1,0:T(8,128)(2,1)}, bf16[576,768]{1,0:T(8,128)(2,1)S(1)}, u32[]{:S(2)}, u32[]{:S(2)}) collective-permute-start(bf16[576,768]{1,0:T(8,128)(2,1)} %get-tuple-element.474), channel_id=1, source_target_pairs={{0,4},{2,6},{4,0},{6,2},{8,12},{10,14},{12,8},{14,10},{16,20},{18,... | collective-permute-start | bytes 2654216 | tf_op jit(solution)/shard_map/ppermute | solution.py:689
  413.2 14.5 %collective-permute-start.48 = (bf16[192,768]{1,0:T(8,128)(2,1)}, bf16[192,768]{1,0:T(8,128)(2,1)S(1)}, u32[]{:S(2)}, u32[]{:S(2)}) collective-permute-start(bf16[192,768]{1,0:T(8,128)(2,1)} %get-tuple-element.475), channel_id=1, source_target_pairs={{0,8},{2,10},{4,12},{6,14},{8,0},{10,2},{12,4},{14,6},{16,24},{18,... | collective-permute-start | bytes 884744 | tf_op jit(solution)/shard_map/ppermute | solution.py:689
  414.1 23.7 %collective-permute-start.49 = (bf16[192,768]{1,0:T(8,128)(2,1)}, bf16[192,768]{1,0:T(8,128)(2,1)S(1)}, u32[]{:S(2)}, u32[]{:S(2)}) collective-permute-start(bf16[192,768]{1,0:T(8,128)(2,1)} %get-tuple-element.476), channel_id=1, source_target_pairs={{0,16},{2,18},{4,20},{6,22},{8,24},{10,26},{12,28},{14,30},{16,0},... | collective-permute-start | bytes 884744 | tf_op jit(solution)/shard_map/ppermute | solution.py:689
  416.1 21.7 %collective-permute-start.50 = (bf16[192,768]{1,0:T(8,128)(2,1)}, bf16[192,768]{1,0:T(8,128)(2,1)S(1)}, u32[]{:S(2)}, u32[]{:S(2)}) collective-permute-start(bf16[192,768]{1,0:T(8,128)(2,1)} %get-tuple-element.477), channel_id=1, source_target_pairs={{0,24},{2,26},{4,28},{6,30},{8,16},{10,18},{12,20},{14,22},{16,8},... | collective-permute-start | bytes 884744 | tf_op jit(solution)/shard_map/ppermute | solution.py:689
  444.6 20.0 %collective-permute-start.52 = (bf16[256,768]{1,0:T(8,128)(2,1)S(1)}, bf16[256,768]{1,0:T(8,128)(2,1)S(1)}, u32[]{:S(2)}, u32[]{:S(2)}) collective-permute-start(bf16[256,768]{1,0:T(8,128)(2,1)S(1)} %get-tuple-element.499), channel_id=1, source_target_pairs={{0,4},{2,6},{4,0},{6,2},{8,12},{10,14},{12,8},{14,10},{16,20},{18,... | collective-permute-start | bytes 1179656 | tf_op jit(solution)/shard_map/ppermute | solution.py:689
  446.0 18.5 %collective-permute-start.51 = (bf16[192,768]{1,0:T(8,128)(2,1)S(1)}, bf16[192,768]{1,0:T(8,128)(2,1)S(1)}, u32[]{:S(2)}, u32[]{:S(2)}) collective-permute-start(bf16[192,768]{1,0:T(8,128)(2,1)S(1)} %get-tuple-element.498), channel_id=1, source_target_pairs={{0,2},{2,0},{4,6},{6,4},{8,10},{10,8},{12,14},{14,12},{16,18},{18,... | collective-permute-start | bytes 884744 | tf_op jit(solution)/shard_map/ppermute | solution.py:689
  446.6 9.6 %collective-permute-start.53 = (bf16[96,768]{1,0:T(8,128)(2,1)S(1)}, bf16[96,768]{1,0:T(8,128)(2,1)S(1)}, u32[]{:S(2)}, u32[]{:S(2)}) collective-permute-start(bf16[96,768]{1,0:T(8,128)(2,1)S(1)} %get-tuple-element.500), channel_id=1, source_target_pairs={{0,8},{2,10},{4,12},{6,14},{8,0},{10,2},{12,4},{14,6},{16,24},{18,... | collective-permute-start | bytes 442376 | tf_op jit(solution)/shard_map/ppermute | solution.py:689
  451.9 12.6 %collective-permute-start.54 = (bf16[96,768]{1,0:T(8,128)(2,1)S(1)}, bf16[96,768]{1,0:T(8,128)(2,1)S(1)}, u32[]{:S(2)}, u32[]{:S(2)}) collective-permute-start(bf16[96,768]{1,0:T(8,128)(2,1)S(1)} %get-tuple-element.501), channel_id=1, source_target_pairs={{0,16},{2,18},{4,20},{6,22},{8,24},{10,26},{12,28},{14,30},{16,0},... | collective-permute-start | bytes 442376 | tf_op jit(solution)/shard_map/ppermute | solution.py:689
  453.7 10.8 %collective-permute-start.55 = (bf16[96,768]{1,0:T(8,128)(2,1)S(1)}, bf16[96,768]{1,0:T(8,128)(2,1)S(1)}, u32[]{:S(2)}, u32[]{:S(2)}) collective-permute-start(bf16[96,768]{1,0:T(8,128)(2,1)S(1)} %get-tuple-element.502), channel_id=1, source_target_pairs={{0,24},{2,26},{4,28},{6,30},{8,16},{10,18},{12,20},{14,22},{16,8},... | collective-permute-start | bytes 442376 | tf_op jit(solution)/shard_map/ppermute | solution.py:689
  465.4 18.3 %collective-permute-start.59 = (f32[1,2,48,768]{3,2,1,0:T(8,128)S(1)}, f32[1,2,48,768]{3,2,1,0:T(8,128)S(1)}, u32[]{:S(2)}, u32[]{:S(2)}) collective-permute-start(f32[1,2,48,768]{3,2,1,0:T(8,128)S(1)} %copy-done.42), channel_id=1, source_target_pairs={{0,1},{1,0},{2,3},{3,2},{4,5},{5,4},{6,7},{7,6},{8,9},{9,8},{10,11... | collective-permute-start | bytes 884744 | tf_op jit(solution)/shard_map/ppermute | solution.py:685
  465.5 18.2 %collective-permute-start.60 = (f32[1,2,48,768]{3,2,1,0:T(8,128)S(1)}, f32[1,2,48,768]{3,2,1,0:T(8,128)S(1)}, u32[]{:S(2)}, u32[]{:S(2)}) collective-permute-start(f32[1,2,48,768]{3,2,1,0:T(8,128)S(1)} %copy-done.43), channel_id=1, source_target_pairs={{0,1},{1,0},{2,3},{3,2},{4,5},{5,4},{6,7},{7,6},{8,9},{9,8},{10,11... | collective-permute-start | bytes 884744 | tf_op jit(solution)/shard_map/ppermute | solution.py:685
  466.0 9.8 %collective-permute-start.56 = (bf16[112,768]{1,0:T(8,128)(2,1)S(1)}, bf16[112,768]{1,0:T(8,128)(2,1)S(1)}, u32[]{:S(2)}, u32[]{:S(2)}) collective-permute-start(bf16[112,768]{1,0:T(8,128)(2,1)S(1)} %get-tuple-element.521), channel_id=1, source_target_pairs={{0,8},{2,10},{4,12},{6,14},{8,0},{10,2},{12,4},{14,6},{16,24},{18,... | collective-permute-start | bytes 516104 | tf_op jit(solution)/shard_map/ppermute | solution.py:689
  468.1 15.5 %collective-permute-start.57 = (bf16[112,768]{1,0:T(8,128)(2,1)S(1)}, bf16[112,768]{1,0:T(8,128)(2,1)S(1)}, u32[]{:S(2)}, u32[]{:S(2)}) collective-permute-start(bf16[112,768]{1,0:T(8,128)(2,1)S(1)} %get-tuple-element.522), channel_id=1, source_target_pairs={{0,16},{2,18},{4,20},{6,22},{8,24},{10,26},{12,28},{14,30},{16,0},... | collective-permute-start | bytes 516104 | tf_op jit(solution)/shard_map/ppermute | solution.py:689
  469.2 14.5 %collective-permute-start.58 = (bf16[112,768]{1,0:T(8,128)(2,1)S(1)}, bf16[112,768]{1,0:T(8,128)(2,1)S(1)}, u32[]{:S(2)}, u32[]{:S(2)}) collective-permute-start(bf16[112,768]{1,0:T(8,128)(2,1)S(1)} %get-tuple-element.523), channel_id=1, source_target_pairs={{0,24},{2,26},{4,28},{6,30},{8,16},{10,18},{12,20},{14,22},{16,8},... | collective-permute-start | bytes 516104 | tf_op jit(solution)/shard_map/ppermute | solution.py:689
  475.7 27.2 %collective-permute-start.69 = (f32[2,2,48,768]{3,2,1,0:T(8,128)S(1)}, f32[2,2,48,768]{3,2,1,0:T(8,128)S(1)}, u32[]{:S(2)}, u32[]{:S(2)}) collective-permute-start(f32[2,2,48,768]{3,2,1,0:T(8,128)S(1)} %get-tuple-element.533.refs_5_), channel_id=1, source_target_pairs={{0,1},{1,0},{2,3},{3,2},{4,5},{5,4},{6,7},{7,6},{8,9},{9,8},{10,11... | collective-permute-start | bytes 1769480 | tf_op jit(solution)/shard_map/ppermute | solution.py:685
  488.3 4.4 collective-permute-start.64
  492.7 5.6 %collective-permute-start.65 = (f32[1,128]{1,0:T(1,128)S(1)}, f32[1,128]{1,0:T(1,128)S(1)}, u32[]{:S(2)}, u32[]{:S(2)}) collective-permute-start(f32[1,128]{1,0:T(1,128)S(1)} %add_add_fusion.1), channel_id=1, source_target_pairs={{0,8},{2,10},{4,12},{6,14},{8,0},{10,2},{12,4},{14,6},{16,24},{18,... | collective-permute-start | bytes 1544 | tf_op jit(solution)/shard_map/ppermute | solution.py:689
  495.8 4.4 collective-permute-start.66
  497.0 5.3 %collective-permute-start.67 = (f32[1,128]{1,0:T(1,128)S(1)}, f32[1,128]{1,0:T(1,128)S(1)}, u32[]{:S(2)}, u32[]{:S(2)}) collective-permute-start(f32[1,128]{1,0:T(1,128)S(1)} %add_add_fusion.1), channel_id=1, source_target_pairs={{0,24},{2,26},{4,28},{6,30},{8,16},{10,18},{12,20},{14,22},{16,8},... | collective-permute-start | bytes 1544 | tf_op jit(solution)/shard_map/ppermute | solution.py:689
  498.4 4.5 collective-permute-start.70
  498.4 4.6 collective-permute-start.71
  (83 other events, 790.5 us)
Sparse Core Ops, SparseCore 0:
  13.3 139.2 all-gather.1

commit v15 on v14

--- a/solution.py
+++ b/solution.py
@@ -506,7 +506,7 @@
 
 
 def head_kernel(place_of, ins, anys, outs):
-    resid, table, gains, codons, weight = ins
+    resid, table, gains, hot, weight = ins
     grad, branch, branch_own, branch_other, head_in, grad_logits, grad_gains, sums = outs
     half = resid.shape[1] // 2
     normed, unit, inverse = normalize(resid[...], gains[0:1], gains[1:2])
@@ -516,13 +516,14 @@
     logits = jnp.where(lane < V, logits, -1e30)
     top = jnp.max(logits, 1, keepdims=True)
     lse = top + jnp.log(jnp.sum(jnp.exp(logits - top), 1, keepdims=True))
-    hot = jnp.where(lane == codons[...], 1.0, 0.0)
+    hot = hot[...].astype(FULL)
+    weight = weight[:, 0:1]
     picked = jnp.sum(logits * hot, 1, keepdims=True)
-    loss = jnp.sum((lse - picked) * weight[...], 0, keepdims=True)
-    count = jnp.sum(weight[...], 0, keepdims=True)
+    loss = jnp.sum((lse - picked) * weight, 0, keepdims=True)
+    count = jnp.sum(weight, 0, keepdims=True)
     lane = lax.broadcasted_iota(jnp.int32, sums.shape, 1)
     sums[...] = jnp.where(lane == 0, loss, jnp.where(lane == 1, count, 0.0))
-    grad_logits[...] = ((jnp.exp(logits - lse) - hot) * weight[...]).astype(LOW)
+    grad_logits[...] = ((jnp.exp(logits - lse) - hot) * weight).astype(LOW)
     back, gain, bias = normalize_back(
         dot(grad_logits[...], table[...]), unit, inverse, gains[0:1]
     )
@@ -536,7 +537,7 @@
     grad_gains[1:2] = bias
 
 
-def head(place, resid, table, gains, codons, weight):
+def head(place, resid, table, gains, hot, weight):
     length, width = resid.shape
     one, part = (length, width), (length, width // 2)
     return call(
@@ -544,7 +545,7 @@
         place,
         [(one, FULL), (one, LOW), (part, LOW), (part, LOW), (one, LOW)]
         + [((length, SMALL), LOW), ((2, width), FULL), ((1, SMALL), FULL)],
-        [resid, table, gains, codons, weight],
+        [resid, table, gains, hot, weight],
         flops=4 * length * width * SMALL,
     )
 
@@ -809,7 +810,7 @@
     to_z = pop(twice, 3)
     (share,), (small_share,), (squares,) = pop(done), pop(small_done), pop(done)
     (totals,) = pop(last)
-    (tile,), (unit,), (small_tile,) = pop(new), pop(new), pop(small_new)
+    (tile,), (unit,), (small_tile,), (flat,) = pop(new), pop(new), pop(small_new), pop(small_new)
     rows = (out_once if new else out_twice if once else out_done if twice else share).shape[-2]
     rows = rows // (8 if new else 4 if once else 1)
     bits, z = (place_of[1], place_of[2]), place_of[3]
@@ -871,13 +872,13 @@
                     out_once[p, s, block(at), :] = tile[s, block(index(bits[s])), :]
     if small_new:
         products, norms_at = small_job
-        total = summed(products)
-        norms = jnp.concatenate([ins[mine][...] + ins[theirs][...] for mine, theirs in norms_at], 0)
-        high = norms.astype(LOW)
-        shape = (norms.shape[0], SMALL)
-        column = lax.broadcasted_iota(jnp.int32, shape, 1) - V
-        pick = jnp.where(lax.broadcasted_iota(jnp.int32, shape, 0) == column, 1.0, 0.0).astype(LOW)
-        total = total + (cross(high, pick) + cross((norms - high.astype(FULL)).astype(LOW), pick))
+        flat[...] = summed([(right, left) for left, right in products])
+        at = V
+        for mine, theirs in norms_at:
+            count = ins[mine].shape[0]
+            flat[at : at + count] += ins[mine][...] + ins[theirs][...]
+            at += count
+        total = flat[...].T
         small_tile[...] = total
         for zz in range(4):
             for other in range(2):
@@ -1016,7 +1017,9 @@
         if new:
             scratch.append(pltpu.VMEM((2, 16 * rows, width), FULL))
             scratch.append(pltpu.VMEM((16 * rows, width // 2), FULL))
-        scratch += [pltpu.VMEM((16 * rows, SMALL), FULL)] * smalls[0]
+        if smalls[0]:
+            scratch.append(pltpu.VMEM((16 * rows, SMALL), FULL))
+            scratch.append(pltpu.VMEM((SMALL, width), FULL))
         got = list(
             call(
                 functools.partial(
@@ -1028,7 +1031,7 @@
                 [],
                 scratch,
                 4 * new * length * width * width,
-                limit=VMEM_LIMIT if new else 24 << 20,
+                limit=VMEM_LIMIT if new or once else 24 << 20,
             )
         )
         if last:
@@ -1174,26 +1177,25 @@
             quarter = quarter.reshape(2, 4, width, half).transpose(0, 2, 1, 3)
             columns.append(quarter.reshape(2, fsdp, rows, 2 * width).transpose(1, 0, 2, 3))
         weights = jnp.concatenate(columns, 3).transpose(1, 0, 2, 3).reshape(1, 2, width, -1)
+    hot = (codons[:, None] == jnp.arange(SMALL, dtype=jnp.int32)[None, :]).astype(LOW)
+    columns = (hot, jnp.broadcast_to(weight[:, None], (length, SMALL)), segments[:, None])
     mixers, hiddens = [[weights]] * layers, [[weights]] * layers
     if fast:
         first = Gather(place, early[0], (rows + 16, rows), rows)
         last = Gather(place, early[1], (2 * rows, 2 * rows), rows)
         first.along_z()
-        columns = (codons[:, None], weight[:, None], segments[:, None])
         first.got, last.shard, columns = tie(first.got, last.shard, columns)
         first.in_plane()
         last.along_z()
-        first.near, last.got = tie(first.near, last.got)
+        (first.near,) = tie(first.near)
         first.forward()
-        (first.far,) = tie(first.far)
+        first.far, last.got = tie(first.far, last.got)
         own, small = first.result()
         mixers[0] = [own, swap_cores(own)]
-        own, last.got = tie(own, last.got)
         last.in_plane()
         small = small[:, :, : rows // 16 * SMALL].reshape(16, 16, rows // 16, SMALL)
         small = small.transpose(0, 2, 1, 3).reshape(width, SMALL).T
     else:
-        columns = (codons[:, None], weight[:, None], segments[:, None])
         small = weights[:, 0, :, :SMALL].reshape(width, SMALL).T
     start = -2 * width if fast else weights.shape[3] - layers * 6 * width
     base = lambda l: start + l * 6 * width

time: 531 us -> 538 us (1.013)
  starting transfers between devices: 89.6 us -> 96.4 us
    ppermute x47, waiting for transfers between devices: 135 us -> 128 us  [across(): return lax.ppermute(value, 'fsdp', [(i, i ^ mask) for i in range(size)])]
    ppermute x47, starting transfers between devices: 84.2 us -> 90.8 us  [across(): return lax.ppermute(value, 'fsdp', [(i, i ^ mask) for i in range(size)])]
    unnamed x148 -> x146, local copies, waits for them, and re-layouts: 15.5 us -> 15.4 us
  transfers between devices with their start and end apart: 73 -> 73, of which waited for: 31 -> 29; matrix products, arithmetic and copies ran while one was open for 2% -> 2% of each run, Pallas kernels for 30% -> 30%
where the time goes in v15:
time: 538 us; the launch traced here: 529 us
  Pallas kernels  238 us (44%)
  waiting for transfers between devices  150 us (28%)
  starting transfers between devices  96.4 us (18%)
  local copies, waits for them, and re-layouts  21.9 us (4%)
  between operations  15.3 us (3%)
    pallas_call x23, Pallas kernels, call(): pl.pallas_call(body, out_shape=[jax.ShapeDtypeStruct(s, t) for s, t in ou...  238 us
    ppermute x47, waiting for transfers between devices, across(): return lax.ppermute(value, 'fsdp', [(i, i ^ mask) for i in range(size)])  128 us
    ppermute x47, starting transfers between devices, across(): return lax.ppermute(value, 'fsdp', [(i, i ^ mask) for i in range(size)])  90.8 us
    ppermute x25, waiting for transfers between devices, swap_cores(): return lax.ppermute(value, 'dp', [(0, 1), (1, 0)])  17.6 us
    unnamed x146, local copies, waits for them, and re-layouts  15.4 us
  transfers between devices with their start and end apart: 73, of which 29 were waited for; matrix products, arithmetic and copies ran while one was open for 2% of the time, Pallas kernels for 30%

profile of v15, /device:TPU:0, one launch (start us, length us, event | category | flops | bytes accessed | tf_op | source)
XLA Modules:
  0.0 528.7 jit_solution(17062714113393935320)
XLA Ops:
  10.1 3.0 shard_map.364
  13.1 3.1 collective-permute-start
  16.2 2.6 collective-permute-start.1
  19.6 3.9 collective-permute-done.refs_1_
  23.5 12.3 %collective-permute-done.1.refs_2_ = bf16[112,768]{1,0:T(8,128)(2,1)S(1)} collective-permute-done((bf16[112,768]{1,0:T(8,128)(2,1)}, bf16[112,768]{1,0:T(8,128)(2,1)S(1)}, u32[]{:S(2)}, u32[]{:S(2)}) %collective-permute-start.1) | collective-permute-done | bytes 172064 | tf_op jit(solution)/shard_map/ppermute | solution.py:690
  36.7 2.8 shard_map.365.refs_0_
  39.5 1.6 collective-permute-start.3
  42.5 16.2 %collective-permute-done.3.refs_1_ = bf16[448,768]{1,0:T(8,128)(2,1)S(1)} collective-permute-done((bf16[448,768]{1,0:T(8,128)(2,1)}, bf16[448,768]{1,0:T(8,128)(2,1)S(1)}, u32[]{:S(2)}, u32[]{:S(2)}) %collective-permute-start.3) | collective-permute-done | bytes 688160 | tf_op jit(solution)/shard_map/ppermute | solution.py:690
  58.8 2.4 collective-permute-start.5
  61.2 17.4 %collective-permute-start.7 = (bf16[192,768]{1,0:T(8,128)(2,1)S(1)}, bf16[192,768]{1,0:T(8,128)(2,1)S(1)}, u32[]{:S(2)}, u32[]{:S(2)}) collective-permute-start(bf16[192,768]{1,0:T(8,128)(2,1)S(1)} %copy-done.34), channel_id=1, source_target_pairs={{0,8},{2,10},{4,12},{6,14},{8,0},{10,2},{12,4},{14,6},{16,24},{18,... | collective-permute-start | bytes 884744 | tf_op jit(solution)/shard_map/ppermute | solution.py:690
  78.6 1.8 collective-permute-start.8
  83.3 7.0 %collective-permute-done.7.refs_1_ = bf16[192,768]{1,0:T(8,128)(2,1)S(1)} collective-permute-done((bf16[192,768]{1,0:T(8,128)(2,1)S(1)}, bf16[192,768]{1,0:T(8,128)(2,1)S(1)}, u32[]{:S(2)}, u32[]{:S(2)}) %collective-permute-start.7) | collective-permute-done | bytes 294944 | tf_op jit(solution)/shard_map/ppermute | solution.py:690
  90.3 7.4 %collective-permute-done.8.refs_2_ = bf16[192,768]{1,0:T(8,128)(2,1)S(1)} collective-permute-done((bf16[192,768]{1,0:T(8,128)(2,1)S(1)}, bf16[192,768]{1,0:T(8,128)(2,1)S(1)}, u32[]{:S(2)}, u32[]{:S(2)}) %collective-permute-start.8) | collective-permute-done | bytes 294944 | tf_op jit(solution)/shard_map/ppermute | solution.py:690
  99.3 5.0 shard_map.366
  104.4 3.1 shard_map.368.refs_0_
  108.9 2.1 collective-permute-start.12
  115.1 1.6 fusion.3.refs_0_.refs_10_
  116.7 14.4 %shard_map.367 = (f32[512,768]{1,0:T(8,128)}, bf16[512,768]{1,0:T(8,128)(2,1)}, bf16[512,768]{1,0:T(8,128)(2,1)}, bf16[512,768]{1,0:T(8,128)(2,1)}, f32[16,512]{1,0:T(8,128)}, /*index=5*/bf16[2,512,768]{2,1,0:T(8,128)(2,1)}) custom-call(s32[4]{0:T(128)} %pad_add_fusion.scalars, f32[512,768]{1,0:T(8,128)} %fusion.3.refs_0_.refs_10_, ...), custom_call_target="tpu_custom_call" | custom-call | flops 3221225472 | bytes 6825984 | tf_op jit(solution)/shard_map/pallas_call | solution.py:111
  131.1 21.8 %collective-permute-done.11.refs_1_ = bf16[768,768]{1,0:T(8,128)(2,1)S(1)} collective-permute-done((bf16[768,768]{1,0:T(8,128)(2,1)}, bf16[768,768]{1,0:T(8,128)(2,1)S(1)}, u32[]{:S(2)}, u32[]{:S(2)}) %collective-permute-start.11) | collective-permute-done | bytes 1179680 | tf_op jit(solution)/shard_map/ppermute | solution.py:690
  156.8 3.9 all-gather.2.cloned.1.call-done
  160.8 12.7 %shard_map.369 = (f32[512,768]{1,0:T(8,128)}, bf16[5,512,768]{2,1,0:T(8,128)(2,1)}, f32[4,512,768]{2,1,0:T(8,128)}) custom-call(s32[4]{0:T(128)} %pad_add_fusion.scalars, f32[512,768]{1,0:T(8,128)} %get-tuple-element.304.refs_0_.refs_2_, f32[2,768]{1,0:T(2,128)} %get-tuple-element.554.refs_1_.refs_3_, bf16[16,2,48,4608]{3,2,1,0:T(8,128)(2,1)} %bitcast.22), custom_call_target="tpu_custom_call" | custom-call | flops 4831838208 | bytes 15734784 | tf_op jit(solution)/shard_map/pallas_call | solution.py:111
  174.5 5.2 shard_map.370.refs_2_.refs_5_
  180.1 14.2 %shard_map.371 = (f32[512,768]{1,0:T(8,128)}, bf16[512,768]{1,0:T(8,128)(2,1)}, bf16[512,768]{1,0:T(8,128)(2,1)}, bf16[512,768]{1,0:T(8,128)(2,1)}, f32[16,512]{1,0:T(8,128)}, /*index=5*/bf16[2,512,768]{2,1,0:T(8,128)(2,1)}) custom-call(s32[4]{0:T(128)} %pad_add_fusion.scalars, f32[512,768]{1,0:T(8,128)} %get-tuple-element.313.refs_0_.refs_10_, ...), custom_call_target="tpu_custom_call" | custom-call | flops 3221225472 | bytes 16263168 | tf_op jit(solution)/shard_map/pallas_call | solution.py:111
  194.3 2.2 copy-done.11
  196.5 13.1 %shard_map.372 = (f32[512,768]{1,0:T(8,128)}, bf16[5,512,768]{2,1,0:T(8,128)(2,1)}, f32[4,512,768]{2,1,0:T(8,128)}) custom-call(s32[4]{0:T(128)} %pad_add_fusion.scalars, f32[512,768]{1,0:T(8,128)} %get-tuple-element.315.refs_0_.refs_2_, f32[2,768]{1,0:T(2,128)} %get-tuple-element.552.refs_1_.refs_3_, bf16[4,16,48,768]{3,2,1,0:T(8,128)(2,1)} %shard_map.370.refs_2_.refs_5_, ...), custom_call_target="tpu_custom_call" | custom-call | flops 4831838208 | bytes 11016192 | tf_op jit(solution)/shard_map/pallas_call | solution.py:111
  210.1 5.5 %shard_map.373 = (f32[512,768]{1,0:T(8,128)}, bf16[512,768]{1,0:T(8,128)(2,1)}, bf16[512,384]{1,0:T(8,128)(2,1)}, bf16[512,384]{1,0:T(8,128)(2,1)}, bf16[512,768...) custom-call(s32[4]{0:T(128)} %pad_add_fusion.scalars, ...), custom_call_target="tpu_custom_call" | custom-call | flops 201326592 | bytes 2168832 | tf_op jit(solution)/shard_map/pallas_call | solution.py:111
  218.3 8.8 %shard_map.374 = (bf16[384,768]{1,0:T(8,128)(2,1)}, bf16[384,768]{1,0:T(8,128)(2,1)}, f32[1,2,384,768]{3,2,1,0:T(8,128)}) custom-call(s32[4]{0:T(128)} %pad_add_fusion.scalars, bf16[5,512,768]{2,1,0:T(8,128)(2,1)} %get-tuple-element.317.refs_0_, bf16[512,384]{1,0:T(8,128)(2,1)} %get-tuple-element.321.refs_1_, ...), custom_call_target="tpu_custom_call" | custom-call | flops 2415919104 | bytes 8650752 | tf_op jit(solution)/shard_map/pallas_call | solution.py:111
  230.0 17.8 %shard_map.375 = (f32[512,768]{1,0:T(8,128)}, f32[2,768]{1,0:T(2,128)}, bf16[2,512,768]{2,1,0:T(8,128)(2,1)}, bf16[2,512,768]{2,1,0:T(8,128)(2,1)}) custom-call(s32[4]{0:T(128)} %pad_add_fusion.scalars, bf16[512,768]{1,0:T(8,128)(2,1)} %get-tuple-element.333.refs_0_, f32[512,768]{1,0:T(8,128)} %get-tuple-element.334.refs_1_, ...), custom_call_target="tpu_custom_call" | custom-call | flops 4831838208 | bytes 19666944 | tf_op jit(solution)/shard_map/pallas_call | solution.py:111
  248.8 2.9 collective-permute-done.23.refs_3_
  251.6 10.3 %shard_map.376 = (bf16[576,768]{1,0:T(8,128)(2,1)}, bf16[576,768]{1,0:T(8,128)(2,1)}, f32[1,2,384,768]{3,2,1,0:T(8,128)}, f32[1,2,192,768]{3,2,1,0:T(8,128)}) custom-call(s32[4]{0:T(128)} %pad_add_fusion.scalars, bf16[5,512,768]{2,1,0:T(8,128)(2,1)} %get-tuple-element.317.refs_0_, bf16[2,512,768]{2,1,0:T(8,128)(2,1)} %get-tuple-element.341.refs_1_, ...), custom_call_target="tpu_custom_call" | custom-call | flops 2415919104 | bytes 14548992 | tf_op jit(solution)/shard_map/pallas_call | solution.py:111
  261.9 2.0 collective-permute-start.24
  264.8 22.1 %shard_map.377 = (f32[512,768]{1,0:T(8,128)}, bf16[512,768]{1,0:T(8,128)(2,1)}, bf16[512,384]{1,0:T(8,128)(2,1)}, bf16[512,384]{1,0:T(8,128)(2,1)}, f32[2,768]{1...) custom-call(s32[4]{0:T(128)} %pad_add_fusion.scalars, f32[512,768]{1,0:T(8,128)} %get-tuple-element.353.refs_0_, ...), custom_call_target="tpu_custom_call" | custom-call | flops 4429185024 | bytes 20228096 | tf_op jit(solution)/shard_map/pallas_call | solution.py:111
  287.6 3.7 collective-permute-done.30.refs_7_
  293.1 17.4 %shard_map.378 = (bf16[960,768]{1,0:T(8,128)(2,1)}, bf16[960,768]{1,0:T(8,128)(2,1)}, f32[2,2,384,768]{3,2,1,0:T(8,128)}, f32[1,2,192,768]{3,2,1,0:T(8,128)}, f3...) custom-call(s32[4]{0:T(128)} %pad_add_fusion.scalars, ...), custom_call_target="tpu_custom_call" | custom-call | flops 4831838208 | bytes 20250624 | tf_op jit(solution)/shard_map/pallas_call | solution.py:111
  311.8 5.3 collective-permute-start.33
  317.8 1.7 collective-permute-start.35
  319.5 17.3 %shard_map.379 = (f32[512,768]{1,0:T(8,128)}, f32[2,768]{1,0:T(2,128)}, bf16[2,512,768]{2,1,0:T(8,128)(2,1)}, bf16[2,512,768]{2,1,0:T(8,128)(2,1)}) custom-call(s32[4]{0:T(128)} %pad_add_fusion.scalars, bf16[512,768]{1,0:T(8,128)(2,1)} %get-tuple-element.389.refs_0_, f32[512,768]{1,0:T(8,128)} %get-tuple-element.390.refs_1_, ...), custom_call_target="tpu_custom_call" | custom-call | flops 4831838208 | bytes 24385536 | tf_op jit(solution)/shard_map/pallas_call | solution.py:111
  336.9 8.3 %collective-permute-done.31.refs_6_ = bf16[960,768]{1,0:T(8,128)(2,1)S(1)} collective-permute-done((bf16[960,768]{1,0:T(8,128)(2,1)}, bf16[960,768]{1,0:T(8,128)(2,1)S(1)}, u32[]{:S(2)}, u32[]{:S(2)}) %collective-permute-start.31) | collective-permute-done | bytes 1474592 | tf_op jit(solution)/shard_map/ppermute | solution.py:690
  345.9 3.6 collective-permute-done.36.refs_3_
  350.6 13.5 %shard_map.380 = (bf16[768,768]{1,0:T(8,128)(2,1)}, bf16[768,768]{1,0:T(8,128)(2,1)}, f32[1,2,384,768]{3,2,1,0:T(8,128)}, f32[2,2,192,768]{3,2,1,0:T(8,128)}, f3...) custom-call(s32[4]{0:T(128)} %pad_add_fusion.scalars, ...), custom_call_target="tpu_custom_call" | custom-call | flops 2415919104 | bytes 20597760 | tf_op jit(solution)/shard_map/pallas_call | solution.py:111
  366.3 5.3 collective-permute-start.39
  372.3 1.7 collective-permute-start.41
  374.0 22.1 %shard_map.381 = (f32[512,768]{1,0:T(8,128)}, bf16[512,768]{1,0:T(8,128)(2,1)}, bf16[512,384]{1,0:T(8,128)(2,1)}, bf16[512,384]{1,0:T(8,128)(2,1)}, f32[2,768]{1...) custom-call(s32[4]{0:T(128)} %pad_add_fusion.scalars, f32[512,768]{1,0:T(8,128)} %get-tuple-element.423.refs_0_, ...), custom_call_target="tpu_custom_call" | custom-call | flops 4429185024 | bytes 10790912 | tf_op jit(solution)/shard_map/pallas_call | solution.py:111
  397.4 2.3 collective-permute-done.45.refs_15_
  402.5 12.7 %shard_map.382 = (bf16[640,768]{1,0:T(8,128)(2,1)}, bf16[576,768]{1,0:T(8,128)(2,1)}, f32[1,2,384,768]{3,2,1,0:T(8,128)}, f32[384,128]{1,0:T(8,128)}, f32[1,2,19...) custom-call(s32[4]{0:T(128)} %pad_add_fusion.scalars, ...), custom_call_target="tpu_custom_call" | custom-call | flops 2415919104 | bytes 17841152 | tf_op jit(solution)/shard_map/pallas_call | solution.py:111
  416.7 2.1 collective-permute-start.48
  419.5 1.7 collective-permute-start.50
  421.2 9.8 %collective-permute-done.48.refs_6_ = bf16[192,768]{1,0:T(8,128)(2,1)S(1)} collective-permute-done((bf16[192,768]{1,0:T(8,128)(2,1)}, bf16[192,768]{1,0:T(8,128)(2,1)S(1)}, u32[]{:S(2)}, u32[]{:S(2)}) %collective-permute-start.48) | collective-permute-done | bytes 294944 | tf_op jit(solution)/shard_map/ppermute | solution.py:690
  431.0 11.5 %collective-permute-done.49.refs_7_ = bf16[192,768]{1,0:T(8,128)(2,1)S(1)} collective-permute-done((bf16[192,768]{1,0:T(8,128)(2,1)}, bf16[192,768]{1,0:T(8,128)(2,1)S(1)}, u32[]{:S(2)}, u32[]{:S(2)}) %collective-permute-start.49) | collective-permute-done | bytes 294944 | tf_op jit(solution)/shard_map/ppermute | solution.py:690
  443.9 4.9 shard_map.383
  451.0 5.1 collective-permute-start.53
  456.8 1.7 collective-permute-start.55
  458.5 2.3 collective-permute-done.53.refs_5_
  460.7 7.7 %collective-permute-done.54.refs_6_ = bf16[96,768]{1,0:T(8,128)(2,1)S(1)} collective-permute-done((bf16[96,768]{1,0:T(8,128)(2,1)}, bf16[96,768]{1,0:T(8,128)(2,1)S(1)}, u32[]{:S(2)}, u32[]{:S(2)}) %collective-permute-start.54) | collective-permute-done | bytes 147488 | tf_op jit(solution)/shard_map/ppermute | solution.py:690
  473.6 2.2 collective-permute-start.56
  476.5 1.7 collective-permute-start.58
  478.2 5.2 collective-permute-done.56.refs_2_
  483.3 8.0 %collective-permute-done.57.refs_3_ = bf16[112,768]{1,0:T(8,128)(2,1)S(1)} collective-permute-done((bf16[112,768]{1,0:T(8,128)(2,1)S(1)}, bf16[112,768]{1,0:T(8,128)(2,1)S(1)}, u32[]{:S(2)}, u32[]{:S(2)}) %collective-permute-start.57) | collective-permute-done | bytes 172064 | tf_op jit(solution)/shard_map/ppermute | solution.py:690
  495.7 1.6 collective-permute-start.64
  498.4 1.7 collective-permute-done.64
  500.1 3.1 collective-permute-start.65
  504.0 1.7 collective-permute-start.67
  507.7 1.7 collective-permute-done.67
  511.0 10.6 %shard_map.386 = (f32[1,1]{1,0:T(1,128)}, f32[2,48,2304]{2,1,0:T(8,128)}, f32[2,48,2304]{2,1,0:T(8,128)}, f32[2,48,2304]{2,1,0:T(8,128)}, f32[2,48,768]{2,1,0:T(...) custom-call(s32[4]{0:T(128)} %pad_add_fusion.scalars, ...), custom_call_target="tpu_custom_call" | custom-call | flops 53314560 | bytes 14251520 | tf_op jit(solution)/shard_map/pallas_call | solution.py:111
  (284 shorter events, 64.3 us)
Async XLA Ops:
  7.2 153.6 %all-gather.2.cloned.1.call-start = ((), (), s32[]{:S(2)}) async-start(), calls=%async_computation | async-start | bytes 14598144 | tf_op jit(solution)/shard_map/all_gather | solution.py:1169
  13.1 10.4 %collective-permute-start = (bf16[112,768]{1,0:T(8,128)(2,1)}, bf16[112,768]{1,0:T(8,128)(2,1)S(1)}, u32[]{:S(2)}, u32[]{:S(2)}) collective-permute-start(bf16[112,768]{1,0:T(8,128)(2,1)} %get-tuple-element.286.refs_0_), channel_id=1, source_target_pairs={{0,8},{2,10},{4,12},{6,14},{8,0},{10,2},{12,4},{14,6},{16,24},{18,... | collective-permute-start | bytes 516104 | tf_op jit(solution)/shard_map/ppermute | solution.py:690
  16.2 19.6 %collective-permute-start.1 = (bf16[112,768]{1,0:T(8,128)(2,1)}, bf16[112,768]{1,0:T(8,128)(2,1)S(1)}, u32[]{:S(2)}, u32[]{:S(2)}) collective-permute-start(bf16[112,768]{1,0:T(8,128)(2,1)} %get-tuple-element.286.refs_0_), channel_id=1, source_target_pairs={{0,16},{2,18},{4,20},{6,22},{8,24},{10,26},{12,28},{14,30},{16,0},... | collective-permute-start | bytes 516104 | tf_op jit(solution)/shard_map/ppermute | solution.py:690
  18.8 17.0 %collective-permute-start.2 = (bf16[112,768]{1,0:T(8,128)(2,1)}, bf16[112,768]{1,0:T(8,128)(2,1)S(1)}, u32[]{:S(2)}, u32[]{:S(2)}) collective-permute-start(bf16[112,768]{1,0:T(8,128)(2,1)} %get-tuple-element.286.refs_0_), channel_id=1, source_target_pairs={{0,24},{2,26},{4,28},{6,30},{8,16},{10,18},{12,20},{14,22},{16,8},... | collective-permute-start | bytes 516104 | tf_op jit(solution)/shard_map/ppermute | solution.py:690
  39.5 19.3 %collective-permute-start.3 = (bf16[448,768]{1,0:T(8,128)(2,1)}, bf16[448,768]{1,0:T(8,128)(2,1)S(1)}, u32[]{:S(2)}, u32[]{:S(2)}) collective-permute-start(bf16[448,768]{1,0:T(8,128)(2,1)} %shard_map.365.refs_0_), channel_id=1, source_target_pairs={{0,2},{2,0},{4,6},{6,4},{8,10},{10,8},{12,14},{14,12},{16,18},{18,... | collective-permute-start | bytes 2064392 | tf_op jit(solution)/shard_map/ppermute | solution.py:690
  41.0 17.8 %collective-permute-start.4 = (bf16[448,768]{1,0:T(8,128)(2,1)}, bf16[448,768]{1,0:T(8,128)(2,1)S(1)}, u32[]{:S(2)}, u32[]{:S(2)}) collective-permute-start(bf16[448,768]{1,0:T(8,128)(2,1)} %shard_map.365.refs_0_), channel_id=1, source_target_pairs={{0,4},{2,6},{4,0},{6,2},{8,12},{10,14},{12,8},{14,10},{16,20},{18,... | collective-permute-start | bytes 2064392 | tf_op jit(solution)/shard_map/ppermute | solution.py:690
  58.8 39.0 %collective-permute-start.5 = (bf16[256,768]{1,0:T(8,128)(2,1)S(1)}, bf16[256,768]{1,0:T(8,128)(2,1)S(1)}, u32[]{:S(2)}, u32[]{:S(2)}) collective-permute-start(bf16[256,768]{1,0:T(8,128)(2,1)S(1)} %slice.58), channel_id=1, source_target_pairs={{0,2},{2,0},{4,6},{6,4},{8,10},{10,8},{12,14},{14,12},{16,18},{18,... | collective-permute-start | bytes 1179656 | tf_op jit(solution)/shard_map/ppermute | solution.py:690
  61.2 29.1 %collective-permute-start.7 = (bf16[192,768]{1,0:T(8,128)(2,1)S(1)}, bf16[192,768]{1,0:T(8,128)(2,1)S(1)}, u32[]{:S(2)}, u32[]{:S(2)}) collective-permute-start(bf16[192,768]{1,0:T(8,128)(2,1)S(1)} %copy-done.34), channel_id=1, source_target_pairs={{0,8},{2,10},{4,12},{6,14},{8,0},{10,2},{12,4},{14,6},{16,24},{18,... | collective-permute-start | bytes 884744 | tf_op jit(solution)/shard_map/ppermute | solution.py:690
  78.6 19.1 %collective-permute-start.8 = (bf16[192,768]{1,0:T(8,128)(2,1)S(1)}, bf16[192,768]{1,0:T(8,128)(2,1)S(1)}, u32[]{:S(2)}, u32[]{:S(2)}) collective-permute-start(bf16[192,768]{1,0:T(8,128)(2,1)S(1)} %copy-done.34), channel_id=1, source_target_pairs={{0,16},{2,18},{4,20},{6,22},{8,24},{10,26},{12,28},{14,30},{16,0},... | collective-permute-start | bytes 884744 | tf_op jit(solution)/shard_map/ppermute | solution.py:690
  80.4 17.4 %collective-permute-start.9 = (bf16[192,768]{1,0:T(8,128)(2,1)S(1)}, bf16[192,768]{1,0:T(8,128)(2,1)S(1)}, u32[]{:S(2)}, u32[]{:S(2)}) collective-permute-start(bf16[192,768]{1,0:T(8,128)(2,1)S(1)} %copy-done.34), channel_id=1, source_target_pairs={{0,24},{2,26},{4,28},{6,30},{8,16},{10,18},{12,20},{14,22},{16,8},... | collective-permute-start | bytes 884744 | tf_op jit(solution)/shard_map/ppermute | solution.py:690
  81.9 15.9 %collective-permute-start.6 = (bf16[192,768]{1,0:T(8,128)(2,1)S(1)}, bf16[192,768]{1,0:T(8,128)(2,1)S(1)}, u32[]{:S(2)}, u32[]{:S(2)}) collective-permute-start(bf16[192,768]{1,0:T(8,128)(2,1)S(1)} %slice.59), channel_id=1, source_target_pairs={{0,4},{2,6},{4,0},{6,2},{8,12},{10,14},{12,8},{14,10},{16,20},{18,... | collective-permute-start | bytes 884744 | tf_op jit(solution)/shard_map/ppermute | solution.py:690
  104.3 12.5 %collective-permute-start.10 = (bf16[2,16,48,768]{3,2,1,0:T(8,128)(2,1)}, bf16[2,16,48,768]{3,2,1,0:T(8,128)(2,1)}, u32[]{:S(2)}, u32[]{:S(2)}) collective-permute-start(bf16[2,16,48,768]{3,2,1,0:T(8,128)(2,1)} %get-tuple-element.298.refs_6_.refs_11_), channel_id=1, source_target_pairs={{0,1},{1,0},{2,3},{3,2},{4,5},{5,4},{6,7},{7,6},{8,9},{9,8},{10,11... | collective-permute-start | bytes 7077896 | tf_op jit(solution)/shard_map/ppermute | solution.py:686
  107.5 45.4 %collective-permute-start.11 = (bf16[768,768]{1,0:T(8,128)(2,1)}, bf16[768,768]{1,0:T(8,128)(2,1)S(1)}, u32[]{:S(2)}, u32[]{:S(2)}) collective-permute-start(bf16[768,768]{1,0:T(8,128)(2,1)} %shard_map.368.refs_0_), channel_id=1, source_target_pairs={{0,2},{2,0},{4,6},{6,4},{8,10},{10,8},{12,14},{14,12},{16,18},{18,... | collective-permute-start | bytes 3538952 | tf_op jit(solution)/shard_map/ppermute | solution.py:690
  108.9 44.1 %collective-permute-start.12 = (bf16[768,768]{1,0:T(8,128)(2,1)}, bf16[768,768]{1,0:T(8,128)(2,1)S(1)}, u32[]{:S(2)}, u32[]{:S(2)}) collective-permute-start(bf16[768,768]{1,0:T(8,128)(2,1)} %shard_map.368.refs_0_), channel_id=1, source_target_pairs={{0,4},{2,6},{4,0},{6,2},{8,12},{10,14},{12,8},{14,10},{16,20},{18,... | collective-permute-start | bytes 3538952 | tf_op jit(solution)/shard_map/ppermute | solution.py:690
  153.9 19.6 %collective-permute-start.13 = (bf16[384,768]{1,0:T(8,128)(2,1)}, bf16[384,768]{1,0:T(8,128)(2,1)S(1)}, u32[]{:S(2)}, u32[]{:S(2)}) collective-permute-start(bf16[384,768]{1,0:T(8,128)(2,1)} %slice.64), channel_id=1, source_target_pairs={{0,2},{2,0},{4,6},{6,4},{8,10},{10,8},{12,14},{14,12},{16,18},{18,... | collective-permute-start | bytes 1769480 | tf_op jit(solution)/shard_map/ppermute | solution.py:690
  156.2 17.3 %collective-permute-start.14 = (bf16[384,768]{1,0:T(8,128)(2,1)}, bf16[384,768]{1,0:T(8,128)(2,1)S(1)}, u32[]{:S(2)}, u32[]{:S(2)}) collective-permute-start(bf16[384,768]{1,0:T(8,128)(2,1)} %slice.65), channel_id=1, source_target_pairs={{0,4},{2,6},{4,0},{6,2},{8,12},{10,14},{12,8},{14,10},{16,20},{18,... | collective-permute-start | bytes 1769480 | tf_op jit(solution)/shard_map/ppermute | solution.py:690
  179.8 14.5 %collective-permute-start.15 = (bf16[4,16,48,768]{3,2,1,0:T(8,128)(2,1)}, bf16[4,16,48,768]{3,2,1,0:T(8,128)(2,1)S(1)}, u32[]{:S(2)}, u32[]{:S(2)}) collective-permute-start(bf16[4,16,48,768]{3,2,1,0:T(8,128)(2,1)} %shard_map.370.refs_2_.refs_5_), channel_id=1, source_target_pairs={{0,1},{1,0},{2,3},{3,2},{4,5},{5,4},{6,7},{7,6},{8,9},{9,8},{10,11... | collective-permute-start | bytes 14155784 | tf_op jit(solution)/shard_map/ppermute | solution.py:686
  209.7 7.2 %collective-permute-start.16 = (bf16[5,512,768]{2,1,0:T(8,128)(2,1)}, bf16[5,512,768]{2,1,0:T(8,128)(2,1)}, u32[]{:S(2)}, u32[]{:S(2)}) collective-permute-start(bf16[5,512,768]{2,1,0:T(8,128)(2,1)} %get-tuple-element.317.refs_0_), channel_id=1, source_target_pairs={{0,1},{1,0},{2,3},{3,2},{4,5},{5,4},{6,7},{7,6},{8,9},{9,8},{10,11... | collective-permute-start | bytes 11796488 | tf_op jit(solution)/shard_map/ppermute | solution.py:686
  215.7 71.2 %collective-permute-start.26 = (bf16[5,512,768]{2,1,0:T(8,128)(2,1)S(1)}, bf16[5,512,768]{2,1,0:T(8,128)(2,1)S(1)}, u32[]{:S(2)}, u32[]{:S(2)}) collective-permute-start(bf16[5,512,768]{2,1,0:T(8,128)(2,1)S(1)} %copy-done.9), channel_id=1, source_target_pairs={{0,1},{1,0},{2,3},{3,2},{4,5},{5,4},{6,7},{7,6},{8,9},{9,8},{10,11... | collective-permute-start | bytes 11796488 | tf_op jit(solution)/shard_map/ppermute | solution.py:686
  216.1 31.6 %collective-permute-start.20 = (bf16[512,768]{1,0:T(8,128)(2,1)}, bf16[512,768]{1,0:T(8,128)(2,1)}, u32[]{:S(2)}, u32[]{:S(2)}) collective-permute-start(bf16[512,768]{1,0:T(8,128)(2,1)} %get-tuple-element.339.refs_4_), channel_id=1, source_target_pairs={{0,1},{1,0},{2,3},{3,2},{4,5},{5,4},{6,7},{7,6},{8,9},{9,8},{10,11... | collective-permute-start | bytes 2359304 | tf_op jit(solution)/shard_map/ppermute | solution.py:686
  227.1 20.7 %collective-permute-start.18 = (bf16[384,768]{1,0:T(8,128)(2,1)}, bf16[384,768]{1,0:T(8,128)(2,1)}, u32[]{:S(2)}, u32[]{:S(2)}) collective-permute-start(bf16[384,768]{1,0:T(8,128)(2,1)} %get-tuple-element.331), channel_id=1, source_target_pairs={{0,2},{2,0},{4,6},{6,4},{8,10},{10,8},{12,14},{14,12},{16,18},{18,... | collective-permute-start | bytes 1769480 | tf_op jit(solution)/shard_map/ppermute | solution.py:690
  228.1 19.7 %collective-permute-start.19 = (bf16[384,768]{1,0:T(8,128)(2,1)}, bf16[384,768]{1,0:T(8,128)(2,1)}, u32[]{:S(2)}, u32[]{:S(2)}) collective-permute-start(bf16[384,768]{1,0:T(8,128)(2,1)} %get-tuple-element.332), channel_id=1, source_target_pairs={{0,4},{2,6},{4,0},{6,2},{8,12},{10,14},{12,8},{14,10},{16,20},{18,... | collective-permute-start | bytes 1769480 | tf_op jit(solution)/shard_map/ppermute | solution.py:690
  229.8 17.9 %collective-permute-start.21 = (bf16[512,128]{1,0:T(8,128)(2,1)S(1)}, bf16[512,128]{1,0:T(8,128)(2,1)}, u32[]{:S(2)}, u32[]{:S(2)}) collective-permute-start(bf16[512,128]{1,0:T(8,128)(2,1)S(1)} %copy-done.57), channel_id=1, source_target_pairs={{0,1},{1,0},{2,3},{3,2},{4,5},{5,4},{6,7},{7,6},{8,9},{9,8},{10,11... | collective-permute-start | bytes 393224 | tf_op jit(solution)/shard_map/ppermute | solution.py:686
  248.2 38.7 %collective-permute-start.27 = (bf16[2,512,768]{2,1,0:T(8,128)(2,1)}, bf16[2,512,768]{2,1,0:T(8,128)(2,1)}, u32[]{:S(2)}, u32[]{:S(2)}) collective-permute-start(bf16[2,512,768]{2,1,0:T(8,128)(2,1)} %get-tuple-element.299.refs_0_), channel_id=1, source_target_pairs={{0,1},{1,0},{2,3},{3,2},{4,5},{5,4},{6,7},{7,6},{8,9},{9,8},{10,11... | collective-permute-start | bytes 4718600 | tf_op jit(solution)/shard_map/ppermute | solution.py:686
  248.4 38.5 %collective-permute-start.28 = (bf16[2,512,768]{2,1,0:T(8,128)(2,1)}, bf16[2,512,768]{2,1,0:T(8,128)(2,1)}, u32[]{:S(2)}, u32[]{:S(2)}) collective-permute-start(bf16[2,512,768]{2,1,0:T(8,128)(2,1)} %get-tuple-element.314.refs_0_), channel_id=1, source_target_pairs={{0,1},{1,0},{2,3},{3,2},{4,5},{5,4},{6,7},{7,6},{8,9},{9,8},{10,11... | collective-permute-start | bytes 4718600 | tf_op jit(solution)/shard_map/ppermute | solution.py:686
  261.9 25.1 %collective-permute-start.24 = (bf16[576,768]{1,0:T(8,128)(2,1)}, bf16[576,768]{1,0:T(8,128)(2,1)}, u32[]{:S(2)}, u32[]{:S(2)}) collective-permute-start(bf16[576,768]{1,0:T(8,128)(2,1)} %get-tuple-element.351), channel_id=1, source_target_pairs={{0,2},{2,0},{4,6},{6,4},{8,10},{10,8},{12,14},{14,12},{16,18},{18,... | collective-permute-start | bytes 2654216 | tf_op jit(solution)/shard_map/ppermute | solution.py:690
  263.9 23.0 %collective-permute-start.25 = (bf16[576,768]{1,0:T(8,128)(2,1)}, bf16[576,768]{1,0:T(8,128)(2,1)}, u32[]{:S(2)}, u32[]{:S(2)}) collective-permute-start(bf16[576,768]{1,0:T(8,128)(2,1)} %get-tuple-element.352), channel_id=1, source_target_pairs={{0,4},{2,6},{4,0},{6,2},{8,12},{10,14},{12,8},{14,10},{16,20},{18,... | collective-permute-start | bytes 2654216 | tf_op jit(solution)/shard_map/ppermute | solution.py:690
  287.0 4.3 collective-permute-start.29
  287.1 4.2 collective-permute-start.30
  310.5 34.6 %collective-permute-start.31 = (bf16[960,768]{1,0:T(8,128)(2,1)}, bf16[960,768]{1,0:T(8,128)(2,1)S(1)}, u32[]{:S(2)}, u32[]{:S(2)}) collective-permute-start(bf16[960,768]{1,0:T(8,128)(2,1)} %get-tuple-element.384), channel_id=1, source_target_pairs={{0,2},{2,0},{4,6},{6,4},{8,10},{10,8},{12,14},{14,12},{16,18},{18,... | collective-permute-start | bytes 4423688 | tf_op jit(solution)/shard_map/ppermute | solution.py:690
  311.6 34.3 %collective-permute-start.32 = (bf16[960,768]{1,0:T(8,128)(2,1)}, bf16[960,768]{1,0:T(8,128)(2,1)S(1)}, u32[]{:S(2)}, u32[]{:S(2)}) collective-permute-start(bf16[960,768]{1,0:T(8,128)(2,1)} %get-tuple-element.385), channel_id=1, source_target_pairs={{0,4},{2,6},{4,0},{6,2},{8,12},{10,14},{12,8},{14,10},{16,20},{18,... | collective-permute-start | bytes 4423688 | tf_op jit(solution)/shard_map/ppermute | solution.py:690
  311.8 25.0 %collective-permute-start.33 = (bf16[96,768]{1,0:T(8,128)(2,1)}, bf16[96,768]{1,0:T(8,128)(2,1)S(1)}, u32[]{:S(2)}, u32[]{:S(2)}) collective-permute-start(bf16[96,768]{1,0:T(8,128)(2,1)} %get-tuple-element.386), channel_id=1, source_target_pairs={{0,8},{2,10},{4,12},{6,14},{8,0},{10,2},{12,4},{14,6},{16,24},{18,... | collective-permute-start | bytes 442376 | tf_op jit(solution)/shard_map/ppermute | solution.py:690
  317.1 19.7 %collective-permute-start.34 = (bf16[96,768]{1,0:T(8,128)(2,1)}, bf16[96,768]{1,0:T(8,128)(2,1)S(1)}, u32[]{:S(2)}, u32[]{:S(2)}) collective-permute-start(bf16[96,768]{1,0:T(8,128)(2,1)} %get-tuple-element.387), channel_id=1, source_target_pairs={{0,16},{2,18},{4,20},{6,22},{8,24},{10,26},{12,28},{14,30},{16,0},... | collective-permute-start | bytes 442376 | tf_op jit(solution)/shard_map/ppermute | solution.py:690
  317.8 19.1 %collective-permute-start.35 = (bf16[96,768]{1,0:T(8,128)(2,1)}, bf16[96,768]{1,0:T(8,128)(2,1)S(1)}, u32[]{:S(2)}, u32[]{:S(2)}) collective-permute-start(bf16[96,768]{1,0:T(8,128)(2,1)} %get-tuple-element.388), channel_id=1, source_target_pairs={{0,24},{2,26},{4,28},{6,30},{8,16},{10,18},{12,20},{14,22},{16,8},... | collective-permute-start | bytes 442376 | tf_op jit(solution)/shard_map/ppermute | solution.py:690
  364.1 32.0 %collective-permute-start.37 = (bf16[768,768]{1,0:T(8,128)(2,1)}, bf16[768,768]{1,0:T(8,128)(2,1)S(1)}, u32[]{:S(2)}, u32[]{:S(2)}) collective-permute-start(bf16[768,768]{1,0:T(8,128)(2,1)} %get-tuple-element.418), channel_id=1, source_target_pairs={{0,2},{2,0},{4,6},{6,4},{8,10},{10,8},{12,14},{14,12},{16,18},{18,... | collective-permute-start | bytes 3538952 | tf_op jit(solution)/shard_map/ppermute | solution.py:690
  365.2 31.0 %collective-permute-start.38 = (bf16[768,768]{1,0:T(8,128)(2,1)}, bf16[768,768]{1,0:T(8,128)(2,1)S(1)}, u32[]{:S(2)}, u32[]{:S(2)}) collective-permute-start(bf16[768,768]{1,0:T(8,128)(2,1)} %get-tuple-element.419), channel_id=1, source_target_pairs={{0,4},{2,6},{4,0},{6,2},{8,12},{10,14},{12,8},{14,10},{16,20},{18,... | collective-permute-start | bytes 3538952 | tf_op jit(solution)/shard_map/ppermute | solution.py:690
  366.3 29.8 %collective-permute-start.39 = (bf16[96,768]{1,0:T(8,128)(2,1)}, bf16[96,768]{1,0:T(8,128)(2,1)S(1)}, u32[]{:S(2)}, u32[]{:S(2)}) collective-permute-start(bf16[96,768]{1,0:T(8,128)(2,1)} %get-tuple-element.420), channel_id=1, source_target_pairs={{0,8},{2,10},{4,12},{6,14},{8,0},{10,2},{12,4},{14,6},{16,24},{18,... | collective-permute-start | bytes 442376 | tf_op jit(solution)/shard_map/ppermute | solution.py:690
  371.6 24.5 %collective-permute-start.40 = (bf16[96,768]{1,0:T(8,128)(2,1)}, bf16[96,768]{1,0:T(8,128)(2,1)S(1)}, u32[]{:S(2)}, u32[]{:S(2)}) collective-permute-start(bf16[96,768]{1,0:T(8,128)(2,1)} %get-tuple-element.421), channel_id=1, source_target_pairs={{0,16},{2,18},{4,20},{6,22},{8,24},{10,26},{12,28},{14,30},{16,0},... | collective-permute-start | bytes 442376 | tf_op jit(solution)/shard_map/ppermute | solution.py:690
  372.3 23.9 %collective-permute-start.41 = (bf16[96,768]{1,0:T(8,128)(2,1)}, bf16[96,768]{1,0:T(8,128)(2,1)S(1)}, u32[]{:S(2)}, u32[]{:S(2)}) collective-permute-start(bf16[96,768]{1,0:T(8,128)(2,1)} %get-tuple-element.422), channel_id=1, source_target_pairs={{0,24},{2,26},{4,28},{6,30},{8,16},{10,18},{12,20},{14,22},{16,8},... | collective-permute-start | bytes 442376 | tf_op jit(solution)/shard_map/ppermute | solution.py:690
  396.2 4.9 collective-permute-start.42
  396.3 4.8 collective-permute-start.43
  397.0 4.1 collective-permute-start.44
  415.1 27.4 %collective-permute-start.46 = (bf16[640,768]{1,0:T(8,128)(2,1)}, bf16[640,768]{1,0:T(8,128)(2,1)S(1)}, u32[]{:S(2)}, u32[]{:S(2)}) collective-permute-start(bf16[640,768]{1,0:T(8,128)(2,1)} %get-tuple-element.467), channel_id=1, source_target_pairs={{0,2},{2,0},{4,6},{6,4},{8,10},{10,8},{12,14},{14,12},{16,18},{18,... | collective-permute-start | bytes 2949128 | tf_op jit(solution)/shard_map/ppermute | solution.py:690
  415.5 27.0 %collective-permute-start.47 = (bf16[576,768]{1,0:T(8,128)(2,1)}, bf16[576,768]{1,0:T(8,128)(2,1)S(1)}, u32[]{:S(2)}, u32[]{:S(2)}) collective-permute-start(bf16[576,768]{1,0:T(8,128)(2,1)} %get-tuple-element.468), channel_id=1, source_target_pairs={{0,4},{2,6},{4,0},{6,2},{8,12},{10,14},{12,8},{14,10},{16,20},{18,... | collective-permute-start | bytes 2654216 | tf_op jit(solution)/shard_map/ppermute | solution.py:690
  416.7 14.3 %collective-permute-start.48 = (bf16[192,768]{1,0:T(8,128)(2,1)}, bf16[192,768]{1,0:T(8,128)(2,1)S(1)}, u32[]{:S(2)}, u32[]{:S(2)}) collective-permute-start(bf16[192,768]{1,0:T(8,128)(2,1)} %get-tuple-element.469), channel_id=1, source_target_pairs={{0,8},{2,10},{4,12},{6,14},{8,0},{10,2},{12,4},{14,6},{16,24},{18,... | collective-permute-start | bytes 884744 | tf_op jit(solution)/shard_map/ppermute | solution.py:690
  418.8 23.7 %collective-permute-start.49 = (bf16[192,768]{1,0:T(8,128)(2,1)}, bf16[192,768]{1,0:T(8,128)(2,1)S(1)}, u32[]{:S(2)}, u32[]{:S(2)}) collective-permute-start(bf16[192,768]{1,0:T(8,128)(2,1)} %get-tuple-element.470), channel_id=1, source_target_pairs={{0,16},{2,18},{4,20},{6,22},{8,24},{10,26},{12,28},{14,30},{16,0},... | collective-permute-start | bytes 884744 | tf_op jit(solution)/shard_map/ppermute | solution.py:690
  419.5 23.0 %collective-permute-start.50 = (bf16[192,768]{1,0:T(8,128)(2,1)}, bf16[192,768]{1,0:T(8,128)(2,1)S(1)}, u32[]{:S(2)}, u32[]{:S(2)}) collective-permute-start(bf16[192,768]{1,0:T(8,128)(2,1)} %get-tuple-element.471), channel_id=1, source_target_pairs={{0,24},{2,26},{4,28},{6,30},{8,16},{10,18},{12,20},{14,22},{16,8},... | collective-permute-start | bytes 884744 | tf_op jit(solution)/shard_map/ppermute | solution.py:690
  448.8 19.6 %collective-permute-start.52 = (bf16[256,768]{1,0:T(8,128)(2,1)}, bf16[256,768]{1,0:T(8,128)(2,1)S(1)}, u32[]{:S(2)}, u32[]{:S(2)}) collective-permute-start(bf16[256,768]{1,0:T(8,128)(2,1)} %get-tuple-element.493), channel_id=1, source_target_pairs={{0,4},{2,6},{4,0},{6,2},{8,12},{10,14},{12,8},{14,10},{16,20},{18,... | collective-permute-start | bytes 1179656 | tf_op jit(solution)/shard_map/ppermute | solution.py:690
  450.1 18.4 %collective-permute-start.51 = (bf16[192,768]{1,0:T(8,128)(2,1)}, bf16[192,768]{1,0:T(8,128)(2,1)S(1)}, u32[]{:S(2)}, u32[]{:S(2)}) collective-permute-start(bf16[192,768]{1,0:T(8,128)(2,1)} %get-tuple-element.492), channel_id=1, source_target_pairs={{0,2},{2,0},{4,6},{6,4},{8,10},{10,8},{12,14},{14,12},{16,18},{18,... | collective-permute-start | bytes 884744 | tf_op jit(solution)/shard_map/ppermute | solution.py:690
  451.0 9.7 %collective-permute-start.53 = (bf16[96,768]{1,0:T(8,128)(2,1)}, bf16[96,768]{1,0:T(8,128)(2,1)S(1)}, u32[]{:S(2)}, u32[]{:S(2)}) collective-permute-start(bf16[96,768]{1,0:T(8,128)(2,1)} %get-tuple-element.494), channel_id=1, source_target_pairs={{0,8},{2,10},{4,12},{6,14},{8,0},{10,2},{12,4},{14,6},{16,24},{18,... | collective-permute-start | bytes 442376 | tf_op jit(solution)/shard_map/ppermute | solution.py:690
  456.1 12.3 %collective-permute-start.54 = (bf16[96,768]{1,0:T(8,128)(2,1)}, bf16[96,768]{1,0:T(8,128)(2,1)S(1)}, u32[]{:S(2)}, u32[]{:S(2)}) collective-permute-start(bf16[96,768]{1,0:T(8,128)(2,1)} %get-tuple-element.495), channel_id=1, source_target_pairs={{0,16},{2,18},{4,20},{6,22},{8,24},{10,26},{12,28},{14,30},{16,0},... | collective-permute-start | bytes 442376 | tf_op jit(solution)/shard_map/ppermute | solution.py:690
  456.8 11.6 %collective-permute-start.55 = (bf16[96,768]{1,0:T(8,128)(2,1)}, bf16[96,768]{1,0:T(8,128)(2,1)S(1)}, u32[]{:S(2)}, u32[]{:S(2)}) collective-permute-start(bf16[96,768]{1,0:T(8,128)(2,1)} %get-tuple-element.496), channel_id=1, source_target_pairs={{0,24},{2,26},{4,28},{6,30},{8,16},{10,18},{12,20},{14,22},{16,8},... | collective-permute-start | bytes 442376 | tf_op jit(solution)/shard_map/ppermute | solution.py:690
  473.1 18.3 %collective-permute-start.59 = (f32[1,2,48,768]{3,2,1,0:T(8,128)S(1)}, f32[1,2,48,768]{3,2,1,0:T(8,128)S(1)}, u32[]{:S(2)}, u32[]{:S(2)}) collective-permute-start(f32[1,2,48,768]{3,2,1,0:T(8,128)S(1)} %copy-done.42), channel_id=1, source_target_pairs={{0,1},{1,0},{2,3},{3,2},{4,5},{5,4},{6,7},{7,6},{8,9},{9,8},{10,11... | collective-permute-start | bytes 884744 | tf_op jit(solution)/shard_map/ppermute | solution.py:686
  473.2 18.2 %collective-permute-start.60 = (f32[1,2,48,768]{3,2,1,0:T(8,128)S(1)}, f32[1,2,48,768]{3,2,1,0:T(8,128)S(1)}, u32[]{:S(2)}, u32[]{:S(2)}) collective-permute-start(f32[1,2,48,768]{3,2,1,0:T(8,128)S(1)} %copy-done.43), channel_id=1, source_target_pairs={{0,1},{1,0},{2,3},{3,2},{4,5},{5,4},{6,7},{7,6},{8,9},{9,8},{10,11... | collective-permute-start | bytes 884744 | tf_op jit(solution)/shard_map/ppermute | solution.py:686
  473.6 9.7 %collective-permute-start.56 = (bf16[112,768]{1,0:T(8,128)(2,1)S(1)}, bf16[112,768]{1,0:T(8,128)(2,1)S(1)}, u32[]{:S(2)}, u32[]{:S(2)}) collective-permute-start(bf16[112,768]{1,0:T(8,128)(2,1)S(1)} %get-tuple-element.515), channel_id=1, source_target_pairs={{0,8},{2,10},{4,12},{6,14},{8,0},{10,2},{12,4},{14,6},{16,24},{18,... | collective-permute-start | bytes 516104 | tf_op jit(solution)/shard_map/ppermute | solution.py:690
  475.8 15.5 %collective-permute-start.57 = (bf16[112,768]{1,0:T(8,128)(2,1)S(1)}, bf16[112,768]{1,0:T(8,128)(2,1)S(1)}, u32[]{:S(2)}, u32[]{:S(2)}) collective-permute-start(bf16[112,768]{1,0:T(8,128)(2,1)S(1)} %get-tuple-element.516), channel_id=1, source_target_pairs={{0,16},{2,18},{4,20},{6,22},{8,24},{10,26},{12,28},{14,30},{16,0},... | collective-permute-start | bytes 516104 | tf_op jit(solution)/shard_map/ppermute | solution.py:690
  476.5 14.9 %collective-permute-start.58 = (bf16[112,768]{1,0:T(8,128)(2,1)S(1)}, bf16[112,768]{1,0:T(8,128)(2,1)S(1)}, u32[]{:S(2)}, u32[]{:S(2)}) collective-permute-start(bf16[112,768]{1,0:T(8,128)(2,1)S(1)} %get-tuple-element.517), channel_id=1, source_target_pairs={{0,24},{2,26},{4,28},{6,30},{8,16},{10,18},{12,20},{14,22},{16,8},... | collective-permute-start | bytes 516104 | tf_op jit(solution)/shard_map/ppermute | solution.py:690
  483.3 26.6 %collective-permute-start.69 = (f32[2,2,48,768]{3,2,1,0:T(8,128)S(1)}, f32[2,2,48,768]{3,2,1,0:T(8,128)S(1)}, u32[]{:S(2)}, u32[]{:S(2)}) collective-permute-start(f32[2,2,48,768]{3,2,1,0:T(8,128)S(1)} %copy-done.27), channel_id=1, source_target_pairs={{0,1},{1,0},{2,3},{3,2},{4,5},{5,4},{6,7},{7,6},{8,9},{9,8},{10,11... | collective-permute-start | bytes 1769480 | tf_op jit(solution)/shard_map/ppermute | solution.py:686
  495.7 4.4 collective-permute-start.64
  500.1 5.8 %collective-permute-start.65 = (f32[1,128]{1,0:T(1,128)S(1)}, f32[1,128]{1,0:T(1,128)S(1)}, u32[]{:S(2)}, u32[]{:S(2)}) collective-permute-start(f32[1,128]{1,0:T(1,128)S(1)} %add_add_fusion.1), channel_id=1, source_target_pairs={{0,8},{2,10},{4,12},{6,14},{8,0},{10,2},{12,4},{14,6},{16,24},{18,... | collective-permute-start | bytes 1544 | tf_op jit(solution)/shard_map/ppermute | solution.py:690
  503.2 4.4 collective-permute-start.66
  504.0 5.3 %collective-permute-start.67 = (f32[1,128]{1,0:T(1,128)S(1)}, f32[1,128]{1,0:T(1,128)S(1)}, u32[]{:S(2)}, u32[]{:S(2)}) collective-permute-start(f32[1,128]{1,0:T(1,128)S(1)} %add_add_fusion.1), channel_id=1, source_target_pairs={{0,24},{2,26},{4,28},{6,30},{8,16},{10,18},{12,20},{14,22},{16,8},... | collective-permute-start | bytes 1544 | tf_op jit(solution)/shard_map/ppermute | solution.py:690
  505.7 4.3 collective-permute-start.70
  505.9 4.1 collective-permute-start.71
  (82 other events, 805.3 us)
Sparse Core Ops, SparseCore 0:
  13.2 147.4 all-gather.1

commit v16 on v15

--- a/solution.py
+++ b/solution.py
@@ -792,7 +792,7 @@
 Z = (4, 8, 12)
 
 
-def round_kernel(jobs, small_job, n_ins, counts, smalls, last, place_of, ins, anys, outs, *scratch):
+def round_kernel(jobs, small_job, n_ins, counts, smalls, last, split, place_of, ins, anys, outs, *scratch):
     new, once, twice, done = counts
     small_new, small_once, small_twice, small_done = smalls
     rest = list(ins[n_ins:]) + list(outs) + list(scratch)
@@ -800,6 +800,7 @@
     (keep_once,), (small_keep_once,) = pop(once), pop(small_once)
     (keep_twice,), (small_keep_twice,) = pop(twice), pop(small_twice)
     from_x, from_y = pop(once or twice, 2)
+    again_x, again_y = pop(split and twice, 2)
     (keep_done,), (small_keep_done,) = pop(done), pop(small_done)
     from_z = pop(done, 3)
     (squares_in,), (sums,) = pop(done), pop(last)
@@ -815,6 +816,9 @@
     rows = rows // (8 if new else 4 if once else 1)
     bits, z = (place_of[1], place_of[2]), place_of[3]
     to, came = (to_x, to_y), (from_x, from_y)
+    again, behind = (came, once * 8)
+    if split:
+        again, behind = (again_x, again_y), 0
 
     def block(index, size=rows):
         if isinstance(index, int):
@@ -897,7 +901,7 @@
                     else:
                         to[1 - s][block(new * 8 + p * 4 + zz), :] = value.astype(LOW)
     if small_once:
-        start = (once * 8 + twice * 4) * rows
+        start = (once * 8 + (0 if split else twice * 4)) * rows
         for zz in range(4):
             for bit in range(2):
                 other = bits[1] if bit else 1 - bits[1]
@@ -911,8 +915,8 @@
         for s in range(2):
             for xor in range(4):
                 at = jnp.bitwise_xor(z, xor)
-                value = keep_twice[p, s, block(at), :] + came[1 - s][
-                    block(once * 8 + p * 4 + at), :
+                value = keep_twice[p, s, block(at), :] + again[1 - s][
+                    block(behind + p * 4 + at), :
                 ].astype(FULL)
                 if xor == 0:
                     out_done[p, s] = value
@@ -955,16 +959,16 @@
         self.place, self.rows, self.width, self.sums = place, rows, width, sums
         self.counts, self.smalls = (0,) * 4, (False,) * 4
         self.kept, self.small_kept = [None] * 3, [None] * 3
-        self.came = self.came_z = self.totals = None
+        self.came = self.came_z = self.totals = self.again = None
         self.shares, self.others, self.small_share = [], [], None
         self.squares = jnp.zeros((1, width), FULL)
         self.flying, self.swapping = [], 0
 
-    def step(self, chunk, *ties, small=None):
+    def run(self, chunk, small, counts, smalls, limit):
         rows, width = self.rows, self.width
-        new, once, twice, done = counts = (len(chunk),) + self.counts[:3]
-        smalls = (small is not None,) + self.smalls[:3]
+        new, once, twice, done = counts
         last = not (new or once or twice)
+        split = self.again is not None
         arrays, jobs = [], []
 
         def number(spec):
@@ -993,6 +997,8 @@
             ins += [self.small_kept[stage]] * smalls[1 + stage]
         if once or twice:
             ins += self.came
+        if split and twice:
+            ins += self.again
         if done:
             ins += [self.kept[2]] + [self.small_kept[2]] * smalls[3] + self.came_z + [self.squares]
         ins += [self.sums] * last
@@ -1023,7 +1029,7 @@
         got = list(
             call(
                 functools.partial(
-                    round_kernel, jobs, small_job, len(arrays), counts, smalls, last
+                    round_kernel, jobs, small_job, len(arrays), counts, smalls, last, split
                 ),
                 self.place,
                 outs,
@@ -1031,7 +1037,7 @@
                 [],
                 scratch,
                 4 * new * length * width * width,
-                limit=VMEM_LIMIT if new or once else 24 << 20,
+                limit=limit,
             )
         )
         if last:
@@ -1041,19 +1047,47 @@
             if smalls[3]:
                 self.small_share = got.pop()
             self.shares.append(got.pop())
-        self.counts, self.smalls = counts, smalls
-        self.kept, self.small_kept = [None] * 3, [None] * 3
-        if last:
-            return ties
-        got, ties, self.shares = tie(got, ties, self.shares)
         to = [got.pop(0) for _ in range(2)] if new or once else []
+        kept, small_kept = [None] * 3, [None] * 3
         for stage in range(3):
             if counts[stage]:
-                self.kept[stage] = got.pop(0)
+                kept[stage] = got.pop(0)
             if smalls[stage]:
-                self.small_kept[stage] = got.pop(0)
-        self.flying = [across(v, mask, 16) for v, mask in zip(to, (X, Y))]
-        self.flying += [across(v, mask, 16) for v, mask in zip(got, Z)]
+                small_kept[stage] = got.pop(0)
+        return to, kept, small_kept, got
+
+    def step(self, chunk, *ties, small=None, split=False):
+        counts = (len(chunk),) + self.counts[:3]
+        smalls = (small is not None,) + self.smalls[:3]
+        again = None
+        plane = lambda to: [across(v, mask, 16) for v, mask in zip(to, (X, Y))]
+        line = lambda to: [across(v, mask, 16) for v, mask in zip(to, Z)]
+        if split:
+            to, kept, small_kept, to_z = self.run(
+                [], None, (0,) + counts[1:], (False,) + smalls[1:], VMEM_LIMIT
+            )
+            again, along_z = plane(to), line(to_z)
+            to, new_kept, new_small, _ = self.run(
+                chunk, small, (counts[0], 0, 0, 0), (smalls[0],) + (False,) * 3, VMEM_LIMIT
+            )
+            kept[0], small_kept[0] = new_kept[0], new_small[0]
+            again, to, kept, small_kept, ties, self.shares = tie(
+                again, to, kept, small_kept, ties, self.shares
+            )
+            self.flying = plane(to) + along_z
+        else:
+            limit = VMEM_LIMIT if chunk else 24 << 20
+            to, kept, small_kept, to_z = self.run(chunk, small, counts, smalls, limit)
+            if any(counts[:3]):
+                to, kept, small_kept, to_z, ties, self.shares = tie(
+                    to, kept, small_kept, to_z, ties, self.shares
+                )
+            self.flying = plane(to) + line(to_z)
+        self.again = again
+        self.counts, self.smalls = counts, smalls
+        self.kept, self.small_kept = kept, small_kept
+        if not any(counts[:3]):
+            return ties
         self.swapping = 0
         while len(self.flying) < 5 and len(self.others) + self.swapping < len(self.shares):
             self.flying.append(swap_cores(self.shares[len(self.others) + self.swapping]))
@@ -1081,7 +1115,7 @@
     def __init__(self):
         self.shares, self.squares = [], []
 
-    def step(self, chunk, *ties):
+    def step(self, chunk, *ties, split=False):
         def factor(spec):
             array, index, low, high = spec
             array = array if index is None else array[index]
@@ -1187,11 +1221,12 @@
         first.got, last.shard, columns = tie(first.got, last.shard, columns)
         first.in_plane()
         last.along_z()
-        (first.near,) = tie(first.near)
+        first.near, last.got = tie(first.near, last.got)
         first.forward()
-        first.far, last.got = tie(first.far, last.got)
+        (first.far,) = tie(first.far)
         own, small = first.result()
         mixers[0] = [own, swap_cores(own)]
+        own, last.got = tie(own, last.got)
         last.in_plane()
         small = small[:, :, : rows // 16 * SMALL].reshape(16, 16, rows // 16, SMALL)
         small = small.transpose(0, 2, 1, 3).reshape(width, SMALL).T
@@ -1250,7 +1285,7 @@
                 for t in range(4)
             ]
         )
-        grad, branch = rounds.step(chunk, grad, branch)
+        grad, branch = rounds.step(chunk, grad, branch, split=l == 0)
         grad_middle, gains_mid, up_own, up_other = hidden_back(
             place, grad, branch, middle, hidden, hiddens[l], base(l), gain[1]
         )
@@ -1299,7 +1334,7 @@
     products = [(whole(early[0]), whole(early[1])), (whole(early_came[0]), whole(early_came[1]))]
     products += [(whole(branch), whole(early[2])), (whole(branch_came), whole(early_came[2]))]
     if fast:
-        rounds.step(chunk, small=(products, [late, norms_early]))
+        rounds.step(chunk, small=(products, [late, norms_early]), split=True)
         while rounds.left():
             rounds.finish()
             rounds.step([])

time: 538 us -> 524 us (0.974)
  waiting for transfers between devices: 150 us -> 142 us
  starting transfers between devices: 96.4 us -> 90.9 us
    ppermute x47 -> x51, starting transfers between devices: 90.8 us -> 86 us  [across(): return lax.ppermute(value, 'fsdp', [(i, i ^ mask) for i in range(size)])]
    unnamed x146 -> x164, local copies, waits for them, and re-layouts: 15.4 us -> 13.7 us
    ppermute x47 -> x51, waiting for transfers between devices: 128 us -> 129 us  [across(): return lax.ppermute(value, 'fsdp', [(i, i ^ mask) for i in range(size)])]
    pallas_call x23 -> x25, Pallas kernels: 238 us -> 238 us  [call(): pl.pallas_call(body, out_shape=[jax.ShapeDtypeStruct(s, t) for s, t in ou...]
  transfers between devices with their start and end apart: 73 -> 77, of which waited for: 29 -> 27; matrix products, arithmetic and copies ran while one was open for 2% -> 2% of each run, Pallas kernels for 30% -> 37%
where the time goes in v16:
time: 524 us; the launch traced here: 514 us
  Pallas kernels  238 us (45%)
  waiting for transfers between devices  142 us (27%)
  starting transfers between devices  90.9 us (17%)
  local copies, waits for them, and re-layouts  20.6 us (4%)
  between operations  15.5 us (3%)
  other arithmetic  5.36 us (1%)
    pallas_call x25, Pallas kernels, call(): pl.pallas_call(body, out_shape=[jax.ShapeDtypeStruct(s, t) for s, t in ou...  238 us
    ppermute x51, waiting for transfers between devices, across(): return lax.ppermute(value, 'fsdp', [(i, i ^ mask) for i in range(size)])  129 us
    ppermute x51, starting transfers between devices, across(): return lax.ppermute(value, 'fsdp', [(i, i ^ mask) for i in range(size)])  86 us
    unnamed x164, local copies, waits for them, and re-layouts  13.7 us
    ppermute x25, waiting for transfers between devices, swap_cores(): return lax.ppermute(value, 'dp', [(0, 1), (1, 0)])  12.4 us
  transfers between devices with their start and end apart: 77, of which 27 were waited for; matrix products, arithmetic and copies ran while one was open for 2% of the time, Pallas kernels for 37%

profile of v16, /device:TPU:0, one launch (start us, length us, event | category | flops | bytes accessed | tf_op | source)
XLA Modules:
  0.0 514.2 jit_solution(14958649025743048502)
XLA Ops:
  10.1 3.0 shard_map.364
  13.1 3.1 collective-permute-start
  16.2 2.6 collective-permute-start.1
  19.6 3.9 collective-permute-done.refs_1_
  23.5 12.3 %collective-permute-done.1.refs_2_ = bf16[112,768]{1,0:T(8,128)(2,1)S(1)} collective-permute-done((bf16[112,768]{1,0:T(8,128)(2,1)}, bf16[112,768]{1,0:T(8,128)(2,1)S(1)}, u32[]{:S(2)}, u32[]{:S(2)}) %collective-permute-start.1) | collective-permute-done | bytes 172064 | tf_op jit(solution)/shard_map/ppermute | solution.py:690
  36.7 2.8 shard_map.365.refs_0_
  39.5 1.6 collective-permute-start.3
  41.0 1.5 collective-permute-start.4
  42.6 8.5 %collective-permute-start.5 = (bf16[192,768]{1,0:T(8,128)(2,1)S(1)}, bf16[192,768]{1,0:T(8,128)(2,1)S(1)}, u32[]{:S(2)}, u32[]{:S(2)}) collective-permute-start(bf16[192,768]{1,0:T(8,128)(2,1)S(1)} %copy-done.36), channel_id=1, source_target_pairs={{0,8},{2,10},{4,12},{6,14},{8,0},{10,2},{12,4},{14,6},{16,24},{18,... | collective-permute-start | bytes 884744 | tf_op jit(solution)/shard_map/ppermute | solution.py:690
  52.0 1.5 collective-permute-start.7
  53.5 12.3 %collective-permute-done.5.refs_1_ = bf16[192,768]{1,0:T(8,128)(2,1)S(1)} collective-permute-done((bf16[192,768]{1,0:T(8,128)(2,1)S(1)}, bf16[192,768]{1,0:T(8,128)(2,1)S(1)}, u32[]{:S(2)}, u32[]{:S(2)}) %collective-permute-start.5) | collective-permute-done | bytes 294944 | tf_op jit(solution)/shard_map/ppermute | solution.py:690
  65.8 22.0 %collective-permute-done.6.refs_2_ = bf16[192,768]{1,0:T(8,128)(2,1)S(1)} collective-permute-done((bf16[192,768]{1,0:T(8,128)(2,1)S(1)}, bf16[192,768]{1,0:T(8,128)(2,1)S(1)}, u32[]{:S(2)}, u32[]{:S(2)}) %collective-permute-start.6) | collective-permute-done | bytes 294944 | tf_op jit(solution)/shard_map/ppermute | solution.py:690
  88.0 6.7 %collective-permute-done.9.refs_4_ = bf16[192,768]{1,0:T(8,128)(2,1)S(1)} collective-permute-done((bf16[192,768]{1,0:T(8,128)(2,1)S(1)}, bf16[192,768]{1,0:T(8,128)(2,1)S(1)}, u32[]{:S(2)}, u32[]{:S(2)}) %collective-permute-start.9) | collective-permute-done | bytes 294944 | tf_op jit(solution)/shard_map/ppermute | solution.py:690
  96.4 4.0 shard_map.366
  100.6 3.1 shard_map.368.refs_0_
  103.7 1.8 collective-permute-start.11
  110.3 1.6 fusion.3.refs_0_.refs_10_
  112.0 14.4 %shard_map.367 = (f32[512,768]{1,0:T(8,128)}, bf16[512,768]{1,0:T(8,128)(2,1)}, bf16[512,768]{1,0:T(8,128)(2,1)}, bf16[512,768]{1,0:T(8,128)(2,1)}, f32[16,512]{1,0:T(8,128)}, /*index=5*/bf16[2,512,768]{2,1,0:T(8,128)(2,1)}) custom-call(s32[4]{0:T(128)} %pad_add_fusion.scalars, f32[512,768]{1,0:T(8,128)} %fusion.3.refs_0_.refs_10_, ...), custom_call_target="tpu_custom_call" | custom-call | flops 3221225472 | bytes 6825984 | tf_op jit(solution)/shard_map/pallas_call | solution.py:111
  126.4 21.3 %collective-permute-done.11.refs_1_ = bf16[768,768]{1,0:T(8,128)(2,1)S(1)} collective-permute-done((bf16[768,768]{1,0:T(8,128)(2,1)}, bf16[768,768]{1,0:T(8,128)(2,1)S(1)}, u32[]{:S(2)}, u32[]{:S(2)}) %collective-permute-start.11) | collective-permute-done | bytes 1179680 | tf_op jit(solution)/shard_map/ppermute | solution.py:690
  152.6 12.7 %shard_map.369 = (f32[512,768]{1,0:T(8,128)}, bf16[5,512,768]{2,1,0:T(8,128)(2,1)}, f32[4,512,768]{2,1,0:T(8,128)}) custom-call(s32[4]{0:T(128)} %pad_add_fusion.scalars, f32[512,768]{1,0:T(8,128)} %get-tuple-element.311.refs_0_.refs_2_, f32[2,768]{1,0:T(2,128)} %get-tuple-element.564.refs_1_.refs_3_, bf16[16,2,48,4608]{3,2,1,0:T(8,128)(2,1)} %bitcast.22), custom_call_target="tpu_custom_call" | custom-call | flops 4831838208 | bytes 15734784 | tf_op jit(solution)/shard_map/pallas_call | solution.py:111
  167.0 5.2 %shard_map.370.refs_2_.refs_5_ = bf16[4,16,48,768]{3,2,1,0:T(8,128)(2,1)} custom-call(s32[4]{0:T(128)} %pad_add_fusion.scalars, bf16[768,768]{1,0:T(8,128)(2,1)} %shard_map.368.refs_0_, bf16[768,768]{1,0:T(8,128)(2,1)} %copy-done.14, bf16[768,768]{1,0:T(8,128)(2,1)} %copy-done.15, bf16[384,768]{1,0:T(8,128)(2,1)} %copy-done.32, bf16[384,768]{1,0:T(8,128)(2,1)} %copy-done.33), custom_call_target="tpu_custom_call" | custom-call | bytes 4718592 | tf_op jit(solution)/shard_map/pallas_call | solution.py:111
  172.3 14.3 %shard_map.371 = (f32[512,768]{1,0:T(8,128)}, bf16[512,768]{1,0:T(8,128)(2,1)}, bf16[512,768]{1,0:T(8,128)(2,1)}, bf16[512,768]{1,0:T(8,128)(2,1)}, f32[16,512]{1,0:T(8,128)}, /*index=5*/bf16[2,512,768]{2,1,0:T(8,128)(2,1)}) custom-call(s32[4]{0:T(128)} %pad_add_fusion.scalars, f32[512,768]{1,0:T(8,128)} %get-tuple-element.320.refs_0_.refs_10_, ...), custom_call_target="tpu_custom_call" | custom-call | flops 3221225472 | bytes 16263168 | tf_op jit(solution)/shard_map/pallas_call | solution.py:111
  186.6 2.2 copy-done.11
  188.8 12.9 %shard_map.372 = (f32[512,768]{1,0:T(8,128)}, bf16[5,512,768]{2,1,0:T(8,128)(2,1)}, f32[4,512,768]{2,1,0:T(8,128)}) custom-call(s32[4]{0:T(128)} %pad_add_fusion.scalars, f32[512,768]{1,0:T(8,128)} %get-tuple-element.321.refs_0_.refs_2_, f32[2,768]{1,0:T(2,128)} %get-tuple-element.562.refs_1_.refs_3_, bf16[4,16,48,768]{3,2,1,0:T(8,128)(2,1)} %shard_map.370.refs_2_.refs_5_, ...), custom_call_target="tpu_custom_call" | custom-call | flops 4831838208 | bytes 11016192 | tf_op jit(solution)/shard_map/pallas_call | solution.py:111
  202.3 5.5 %shard_map.373 = (f32[512,768]{1,0:T(8,128)}, bf16[512,768]{1,0:T(8,128)(2,1)}, bf16[512,384]{1,0:T(8,128)(2,1)}, bf16[512,384]{1,0:T(8,128)(2,1)}, bf16[512,768...) custom-call(s32[4]{0:T(128)} %pad_add_fusion.scalars, ...), custom_call_target="tpu_custom_call" | custom-call | flops 201326592 | bytes 2168832 | tf_op jit(solution)/shard_map/pallas_call | solution.py:111
  211.0 8.7 %shard_map.374 = (bf16[384,768]{1,0:T(8,128)(2,1)}, bf16[384,768]{1,0:T(8,128)(2,1)}, f32[1,2,384,768]{3,2,1,0:T(8,128)}) custom-call(s32[4]{0:T(128)} %pad_add_fusion.scalars, bf16[5,512,768]{2,1,0:T(8,128)(2,1)} %get-tuple-element.323.refs_0_, bf16[512,384]{1,0:T(8,128)(2,1)} %get-tuple-element.327.refs_1_, bf16[5,512,768]{2,1,0:T(8,128)(2,1)} %copy-done.13, ...), custom_call_target="tpu_custom_call" | custom-call | flops 2415919104 | bytes 8650752 | tf_op jit(solution)/shard_map/pallas_call | solution.py:111
  220.3 1.5 collective-permute-start.19
  224.0 17.9 %shard_map.375 = (f32[512,768]{1,0:T(8,128)}, f32[2,768]{1,0:T(2,128)}, bf16[2,512,768]{2,1,0:T(8,128)(2,1)}, bf16[2,512,768]{2,1,0:T(8,128)(2,1)}) custom-call(s32[4]{0:T(128)} %pad_add_fusion.scalars, bf16[512,768]{1,0:T(8,128)(2,1)} %get-tuple-element.339.refs_0_, f32[512,768]{1,0:T(8,128)} %get-tuple-element.340.refs_1_, ...), custom_call_target="tpu_custom_call" | custom-call | flops 4831838208 | bytes 19666944 | tf_op jit(solution)/shard_map/pallas_call | solution.py:111
  243.1 2.7 collective-permute-done.23.refs_3_
  245.8 10.3 %shard_map.376 = (bf16[576,768]{1,0:T(8,128)(2,1)}, bf16[576,768]{1,0:T(8,128)(2,1)}, f32[1,2,384,768]{3,2,1,0:T(8,128)}, f32[1,2,192,768]{3,2,1,0:T(8,128)}) custom-call(s32[4]{0:T(128)} %pad_add_fusion.scalars, bf16[5,512,768]{2,1,0:T(8,128)(2,1)} %get-tuple-element.323.refs_0_, bf16[2,512,768]{2,1,0:T(8,128)(2,1)} %get-tuple-element.347.refs_1_, ...), custom_call_target="tpu_custom_call" | custom-call | flops 2415919104 | bytes 14548992 | tf_op jit(solution)/shard_map/pallas_call | solution.py:111
  258.1 22.1 %shard_map.377 = (f32[512,768]{1,0:T(8,128)}, bf16[512,768]{1,0:T(8,128)(2,1)}, bf16[512,384]{1,0:T(8,128)(2,1)}, bf16[512,384]{1,0:T(8,128)(2,1)}, f32[2,768]{1...) custom-call(s32[4]{0:T(128)} %pad_add_fusion.scalars, f32[512,768]{1,0:T(8,128)} %get-tuple-element.361.refs_0_, ...), custom_call_target="tpu_custom_call" | custom-call | flops 4429185024 | bytes 20228096 | tf_op jit(solution)/shard_map/pallas_call | solution.py:111
  281.2 5.4 %shard_map.378 = (bf16[192,768]{1,0:T(8,128)(2,1)}, bf16[192,768]{1,0:T(8,128)(2,1)}, f32[1,2,192,768]{3,2,1,0:T(8,128)}, f32[1,2,48,768]{3,2,1,0:T(8,128)}, bf1...) custom-call(s32[4]{0:T(128)} %pad_add_fusion.scalars, ...), custom_call_target="tpu_custom_call" | custom-call | bytes 5308416 | tf_op jit(solution)/shard_map/pallas_call | solution.py:111
  287.3 1.5 collective-permute-start.30
  289.5 15.0 %shard_map.379 = (bf16[768,768]{1,0:T(8,128)(2,1)}, bf16[768,768]{1,0:T(8,128)(2,1)}, f32[2,2,384,768]{3,2,1,0:T(8,128)}) custom-call(s32[4]{0:T(128)} %pad_add_fusion.scalars, bf16[2,512,768]{2,1,0:T(8,128)(2,1)} %get-tuple-element.373.refs_0_, bf16[2,512,768]{2,1,0:T(8,128)(2,1)} %get-tuple-element.378.refs_1_, ...), custom_call_target="tpu_custom_call" | custom-call | flops 4831838208 | bytes 14942208 | tf_op jit(solution)/shard_map/pallas_call | solution.py:111
  306.5 6.5 %collective-permute-start.35 = (bf16[96,768]{1,0:T(8,128)(2,1)S(1)}, bf16[96,768]{1,0:T(8,128)(2,1)S(1)}, u32[]{:S(2)}, u32[]{:S(2)}) collective-permute-start(bf16[96,768]{1,0:T(8,128)(2,1)S(1)} %copy-done.81), channel_id=1, source_target_pairs={{0,8},{2,10},{4,12},{6,14},{8,0},{10,2},{12,4},{14,6},{16,24},{18,... | collective-permute-start | bytes 442376 | tf_op jit(solution)/shard_map/ppermute | solution.py:690
  313.1 2.0 collective-permute-start.36
  315.0 1.5 collective-permute-start.37
  316.5 17.4 %shard_map.380 = (f32[512,768]{1,0:T(8,128)}, f32[2,768]{1,0:T(2,128)}, bf16[2,512,768]{2,1,0:T(8,128)(2,1)}, bf16[2,512,768]{2,1,0:T(8,128)(2,1)}) custom-call(s32[4]{0:T(128)} %pad_add_fusion.scalars, bf16[512,768]{1,0:T(8,128)(2,1)} %get-tuple-element.396.refs_0_, f32[512,768]{1,0:T(8,128)} %get-tuple-element.397.refs_1_, ...), custom_call_target="tpu_custom_call" | custom-call | flops 4831838208 | bytes 24385536 | tf_op jit(solution)/shard_map/pallas_call | solution.py:111
  334.1 3.6 collective-permute-done.38.refs_3_
  338.9 12.9 %shard_map.381 = (bf16[768,768]{1,0:T(8,128)(2,1)}, bf16[768,768]{1,0:T(8,128)(2,1)}, f32[1,2,384,768]{3,2,1,0:T(8,128)}, f32[2,2,192,768]{3,2,1,0:T(8,128)}, f3...) custom-call(s32[4]{0:T(128)} %pad_add_fusion.scalars, ...), custom_call_target="tpu_custom_call" | custom-call | flops 2415919104 | bytes 20597760 | tf_op jit(solution)/shard_map/pallas_call | solution.py:111
  353.8 5.2 %collective-permute-start.41 = (bf16[96,768]{1,0:T(8,128)(2,1)}, bf16[96,768]{1,0:T(8,128)(2,1)S(1)}, u32[]{:S(2)}, u32[]{:S(2)}) collective-permute-start(bf16[96,768]{1,0:T(8,128)(2,1)} %get-tuple-element.431), channel_id=1, source_target_pairs={{0,8},{2,10},{4,12},{6,14},{8,0},{10,2},{12,4},{14,6},{16,24},{18,... | collective-permute-start | bytes 442376 | tf_op jit(solution)/shard_map/ppermute | solution.py:690
  359.0 1.8 collective-permute-start.42
  362.3 22.1 %shard_map.382 = (f32[512,768]{1,0:T(8,128)}, bf16[512,768]{1,0:T(8,128)(2,1)}, bf16[512,384]{1,0:T(8,128)(2,1)}, bf16[512,384]{1,0:T(8,128)(2,1)}, f32[2,768]{1...) custom-call(s32[4]{0:T(128)} %pad_add_fusion.scalars, f32[512,768]{1,0:T(8,128)} %get-tuple-element.434.refs_0_, ...), custom_call_target="tpu_custom_call" | custom-call | flops 4429185024 | bytes 10790912 | tf_op jit(solution)/shard_map/pallas_call | solution.py:111
  386.0 5.1 shard_map.383
  397.0 9.3 %shard_map.384 = (bf16[448,768]{1,0:T(8,128)(2,1)}, bf16[384,768]{1,0:T(8,128)(2,1)}, f32[1,2,384,768]{3,2,1,0:T(8,128)}, f32[384,128]{1,0:T(8,128)}) custom-call(s32[4]{0:T(128)} %pad_add_fusion.scalars, bf16[2,512,768]{2,1,0:T(8,128)(2,1)} %get-tuple-element.372.refs_0_, bf16[2,512,768]{2,1,0:T(8,128)(2,1)} %get-tuple-element.452.refs_1_, ...), custom_call_target="tpu_custom_call" | custom-call | flops 2415919104 | bytes 10022912 | tf_op jit(solution)/shard_map/pallas_call | solution.py:111
  406.3 1.5 collective-permute-start.50
  410.0 2.1 collective-permute-start.53
  412.1 1.5 collective-permute-start.54
  413.6 9.9 %collective-permute-done.52.refs_8_ = bf16[192,768]{1,0:T(8,128)(2,1)S(1)} collective-permute-done((bf16[192,768]{1,0:T(8,128)(2,1)S(1)}, bf16[192,768]{1,0:T(8,128)(2,1)S(1)}, u32[]{:S(2)}, u32[]{:S(2)}) %collective-permute-start.52) | collective-permute-done | bytes 294944 | tf_op jit(solution)/shard_map/ppermute | solution.py:690
  423.5 10.0 %collective-permute-done.53.refs_9_ = bf16[192,768]{1,0:T(8,128)(2,1)S(1)} collective-permute-done((bf16[192,768]{1,0:T(8,128)(2,1)S(1)}, bf16[192,768]{1,0:T(8,128)(2,1)S(1)}, u32[]{:S(2)}, u32[]{:S(2)}) %collective-permute-start.53) | collective-permute-done | bytes 294944 | tf_op jit(solution)/shard_map/ppermute | solution.py:690
  433.5 1.7 copy-done
  439.2 5.2 %collective-permute-start.57 = (bf16[96,768]{1,0:T(8,128)(2,1)S(1)}, bf16[96,768]{1,0:T(8,128)(2,1)S(1)}, u32[]{:S(2)}, u32[]{:S(2)}) collective-permute-start(bf16[96,768]{1,0:T(8,128)(2,1)S(1)} %get-tuple-element.504), channel_id=1, source_target_pairs={{0,8},{2,10},{4,12},{6,14},{8,0},{10,2},{12,4},{14,6},{16,24},{18,... | collective-permute-start | bytes 442376 | tf_op jit(solution)/shard_map/ppermute | solution.py:690
  444.4 1.9 collective-permute-start.58
  446.3 1.5 collective-permute-start.59
  448.6 8.5 %collective-permute-done.58.refs_6_ = bf16[96,768]{1,0:T(8,128)(2,1)S(1)} collective-permute-done((bf16[96,768]{1,0:T(8,128)(2,1)S(1)}, bf16[96,768]{1,0:T(8,128)(2,1)S(1)}, u32[]{:S(2)}, u32[]{:S(2)}) %collective-permute-start.58) | collective-permute-done | bytes 147488 | tf_op jit(solution)/shard_map/ppermute | solution.py:690
  458.6 2.1 collective-permute-start.60
  461.8 1.5 collective-permute-start.62
  463.2 5.1 collective-permute-done.60.refs_2_
  468.3 7.9 %collective-permute-done.61.refs_3_ = bf16[112,768]{1,0:T(8,128)(2,1)S(1)} collective-permute-done((bf16[112,768]{1,0:T(8,128)(2,1)S(1)}, bf16[112,768]{1,0:T(8,128)(2,1)S(1)}, u32[]{:S(2)}, u32[]{:S(2)}) %collective-permute-start.61) | collective-permute-done | bytes 172064 | tf_op jit(solution)/shard_map/ppermute | solution.py:690
  480.8 1.5 collective-permute-start.68
  483.7 1.6 collective-permute-done.68
  485.3 3.1 collective-permute-start.69
  492.8 2.0 collective-permute-done.71
  496.5 10.6 %shard_map.388 = (f32[1,1]{1,0:T(1,128)}, f32[2,48,2304]{2,1,0:T(8,128)}, f32[2,48,2304]{2,1,0:T(8,128)}, f32[2,48,2304]{2,1,0:T(8,128)}, f32[2,48,768]{2,1,0:T(...) custom-call(s32[4]{0:T(128)} %pad_add_fusion.scalars, ...), custom_call_target="tpu_custom_call" | custom-call | flops 53314560 | bytes 14251520 | tf_op jit(solution)/shard_map/pallas_call | solution.py:111
  (312 shorter events, 66.4 us)
Async XLA Ops:
  7.2 145.4 %all-gather.2.cloned.1.call-start = ((), (), s32[]{:S(2)}) async-start(), calls=%async_computation | async-start | bytes 14598144 | tf_op jit(solution)/shard_map/all_gather | solution.py:1203
  13.1 10.4 %collective-permute-start = (bf16[112,768]{1,0:T(8,128)(2,1)}, bf16[112,768]{1,0:T(8,128)(2,1)S(1)}, u32[]{:S(2)}, u32[]{:S(2)}) collective-permute-start(bf16[112,768]{1,0:T(8,128)(2,1)} %get-tuple-element.291.refs_0_), channel_id=1, source_target_pairs={{0,8},{2,10},{4,12},{6,14},{8,0},{10,2},{12,4},{14,6},{16,24},{18,... | collective-permute-start | bytes 516104 | tf_op jit(solution)/shard_map/ppermute | solution.py:690
  16.2 19.6 %collective-permute-start.1 = (bf16[112,768]{1,0:T(8,128)(2,1)}, bf16[112,768]{1,0:T(8,128)(2,1)S(1)}, u32[]{:S(2)}, u32[]{:S(2)}) collective-permute-start(bf16[112,768]{1,0:T(8,128)(2,1)} %get-tuple-element.291.refs_0_), channel_id=1, source_target_pairs={{0,16},{2,18},{4,20},{6,22},{8,24},{10,26},{12,28},{14,30},{16,0},... | collective-permute-start | bytes 516104 | tf_op jit(solution)/shard_map/ppermute | solution.py:690
  18.8 17.0 %collective-permute-start.2 = (bf16[112,768]{1,0:T(8,128)(2,1)}, bf16[112,768]{1,0:T(8,128)(2,1)S(1)}, u32[]{:S(2)}, u32[]{:S(2)}) collective-permute-start(bf16[112,768]{1,0:T(8,128)(2,1)} %get-tuple-element.291.refs_0_), channel_id=1, source_target_pairs={{0,24},{2,26},{4,28},{6,30},{8,16},{10,18},{12,20},{14,22},{16,8},... | collective-permute-start | bytes 516104 | tf_op jit(solution)/shard_map/ppermute | solution.py:690
  39.5 48.3 %collective-permute-start.3 = (bf16[448,768]{1,0:T(8,128)(2,1)}, bf16[448,768]{1,0:T(8,128)(2,1)S(1)}, u32[]{:S(2)}, u32[]{:S(2)}) collective-permute-start(bf16[448,768]{1,0:T(8,128)(2,1)} %shard_map.365.refs_0_), channel_id=1, source_target_pairs={{0,2},{2,0},{4,6},{6,4},{8,10},{10,8},{12,14},{14,12},{16,18},{18,... | collective-permute-start | bytes 2064392 | tf_op jit(solution)/shard_map/ppermute | solution.py:690
  41.0 46.8 %collective-permute-start.4 = (bf16[448,768]{1,0:T(8,128)(2,1)}, bf16[448,768]{1,0:T(8,128)(2,1)S(1)}, u32[]{:S(2)}, u32[]{:S(2)}) collective-permute-start(bf16[448,768]{1,0:T(8,128)(2,1)} %shard_map.365.refs_0_), channel_id=1, source_target_pairs={{0,4},{2,6},{4,0},{6,2},{8,12},{10,14},{12,8},{14,10},{16,20},{18,... | collective-permute-start | bytes 2064392 | tf_op jit(solution)/shard_map/ppermute | solution.py:690
  42.6 23.2 %collective-permute-start.5 = (bf16[192,768]{1,0:T(8,128)(2,1)S(1)}, bf16[192,768]{1,0:T(8,128)(2,1)S(1)}, u32[]{:S(2)}, u32[]{:S(2)}) collective-permute-start(bf16[192,768]{1,0:T(8,128)(2,1)S(1)} %copy-done.36), channel_id=1, source_target_pairs={{0,8},{2,10},{4,12},{6,14},{8,0},{10,2},{12,4},{14,6},{16,24},{18,... | collective-permute-start | bytes 884744 | tf_op jit(solution)/shard_map/ppermute | solution.py:690
  51.1 36.7 %collective-permute-start.6 = (bf16[192,768]{1,0:T(8,128)(2,1)S(1)}, bf16[192,768]{1,0:T(8,128)(2,1)S(1)}, u32[]{:S(2)}, u32[]{:S(2)}) collective-permute-start(bf16[192,768]{1,0:T(8,128)(2,1)S(1)} %copy-done.36), channel_id=1, source_target_pairs={{0,16},{2,18},{4,20},{6,22},{8,24},{10,26},{12,28},{14,30},{16,0},... | collective-permute-start | bytes 884744 | tf_op jit(solution)/shard_map/ppermute | solution.py:690
  52.0 35.7 %collective-permute-start.7 = (bf16[192,768]{1,0:T(8,128)(2,1)S(1)}, bf16[192,768]{1,0:T(8,128)(2,1)S(1)}, u32[]{:S(2)}, u32[]{:S(2)}) collective-permute-start(bf16[192,768]{1,0:T(8,128)(2,1)S(1)} %copy-done.36), channel_id=1, source_target_pairs={{0,24},{2,26},{4,28},{6,30},{8,16},{10,18},{12,20},{14,22},{16,8},... | collective-permute-start | bytes 884744 | tf_op jit(solution)/shard_map/ppermute | solution.py:690
  87.8 7.8 %collective-permute-start.8 = (bf16[256,768]{1,0:T(8,128)(2,1)S(1)}, bf16[256,768]{1,0:T(8,128)(2,1)S(1)}, u32[]{:S(2)}, u32[]{:S(2)}) collective-permute-start(bf16[256,768]{1,0:T(8,128)(2,1)S(1)} %slice.58), channel_id=1, source_target_pairs={{0,2},{2,0},{4,6},{6,4},{8,10},{10,8},{12,14},{14,12},{16,18},{18,... | collective-permute-start | bytes 1179656 | tf_op jit(solution)/shard_map/ppermute | solution.py:690
  87.9 6.8 %collective-permute-start.9 = (bf16[192,768]{1,0:T(8,128)(2,1)S(1)}, bf16[192,768]{1,0:T(8,128)(2,1)S(1)}, u32[]{:S(2)}, u32[]{:S(2)}) collective-permute-start(bf16[192,768]{1,0:T(8,128)(2,1)S(1)} %slice.59), channel_id=1, source_target_pairs={{0,4},{2,6},{4,0},{6,2},{8,12},{10,14},{12,8},{14,10},{16,20},{18,... | collective-permute-start | bytes 884744 | tf_op jit(solution)/shard_map/ppermute | solution.py:690
  100.5 11.4 %collective-permute-start.10 = (bf16[2,16,48,768]{3,2,1,0:T(8,128)(2,1)}, bf16[2,16,48,768]{3,2,1,0:T(8,128)(2,1)}, u32[]{:S(2)}, u32[]{:S(2)}) collective-permute-start(bf16[2,16,48,768]{3,2,1,0:T(8,128)(2,1)} %get-tuple-element.303.refs_6_.refs_11_), channel_id=1, source_target_pairs={{0,1},{1,0},{2,3},{3,2},{4,5},{5,4},{6,7},{7,6},{8,9},{9,8},{10,11... | collective-permute-start | bytes 7077896 | tf_op jit(solution)/shard_map/ppermute | solution.py:686
  103.7 44.0 %collective-permute-start.11 = (bf16[768,768]{1,0:T(8,128)(2,1)}, bf16[768,768]{1,0:T(8,128)(2,1)S(1)}, u32[]{:S(2)}, u32[]{:S(2)}) collective-permute-start(bf16[768,768]{1,0:T(8,128)(2,1)} %shard_map.368.refs_0_), channel_id=1, source_target_pairs={{0,2},{2,0},{4,6},{6,4},{8,10},{10,8},{12,14},{14,12},{16,18},{18,... | collective-permute-start | bytes 3538952 | tf_op jit(solution)/shard_map/ppermute | solution.py:690
  105.6 42.2 %collective-permute-start.12 = (bf16[768,768]{1,0:T(8,128)(2,1)}, bf16[768,768]{1,0:T(8,128)(2,1)S(1)}, u32[]{:S(2)}, u32[]{:S(2)}) collective-permute-start(bf16[768,768]{1,0:T(8,128)(2,1)} %shard_map.368.refs_0_), channel_id=1, source_target_pairs={{0,4},{2,6},{4,0},{6,2},{8,12},{10,14},{12,8},{14,10},{16,20},{18,... | collective-permute-start | bytes 3538952 | tf_op jit(solution)/shard_map/ppermute | solution.py:690
  148.7 16.7 %collective-permute-start.13 = (bf16[384,768]{1,0:T(8,128)(2,1)}, bf16[384,768]{1,0:T(8,128)(2,1)S(1)}, u32[]{:S(2)}, u32[]{:S(2)}) collective-permute-start(bf16[384,768]{1,0:T(8,128)(2,1)} %slice.64), channel_id=1, source_target_pairs={{0,2},{2,0},{4,6},{6,4},{8,10},{10,8},{12,14},{14,12},{16,18},{18,... | collective-permute-start | bytes 1769480 | tf_op jit(solution)/shard_map/ppermute | solution.py:690
  151.0 15.2 %collective-permute-start.14 = (bf16[384,768]{1,0:T(8,128)(2,1)}, bf16[384,768]{1,0:T(8,128)(2,1)S(1)}, u32[]{:S(2)}, u32[]{:S(2)}) collective-permute-start(bf16[384,768]{1,0:T(8,128)(2,1)} %slice.65), channel_id=1, source_target_pairs={{0,4},{2,6},{4,0},{6,2},{8,12},{10,14},{12,8},{14,10},{16,20},{18,... | collective-permute-start | bytes 1769480 | tf_op jit(solution)/shard_map/ppermute | solution.py:690
  172.2 14.4 %collective-permute-start.15 = (bf16[4,16,48,768]{3,2,1,0:T(8,128)(2,1)}, bf16[4,16,48,768]{3,2,1,0:T(8,128)(2,1)S(1)}, u32[]{:S(2)}, u32[]{:S(2)}) collective-permute-start(bf16[4,16,48,768]{3,2,1,0:T(8,128)(2,1)} %shard_map.370.refs_2_.refs_5_), channel_id=1, source_target_pairs={{0,1},{1,0},{2,3},{3,2},{4,5},{5,4},{6,7},{7,6},{8,9},{9,8},{10,11... | collective-permute-start | bytes 14155784 | tf_op jit(solution)/shard_map/ppermute | solution.py:686
  201.6 7.3 %collective-permute-start.16 = (bf16[5,512,768]{2,1,0:T(8,128)(2,1)}, bf16[5,512,768]{2,1,0:T(8,128)(2,1)S(1)}, u32[]{:S(2)}, u32[]{:S(2)}) collective-permute-start(bf16[5,512,768]{2,1,0:T(8,128)(2,1)} %get-tuple-element.323.refs_0_), channel_id=1, source_target_pairs={{0,1},{1,0},{2,3},{3,2},{4,5},{5,4},{6,7},{7,6},{8,9},{9,8},{10,11... | collective-permute-start | bytes 11796488 | tf_op jit(solution)/shard_map/ppermute | solution.py:686
  207.8 72.4 %collective-permute-start.26 = (bf16[5,512,768]{2,1,0:T(8,128)(2,1)}, bf16[5,512,768]{2,1,0:T(8,128)(2,1)S(1)}, u32[]{:S(2)}, u32[]{:S(2)}) collective-permute-start(bf16[5,512,768]{2,1,0:T(8,128)(2,1)} %get-tuple-element.313.refs_4_.refs_0_), channel_id=1, source_target_pairs={{0,1},{1,0},{2,3},{3,2},{4,5},{5,4},{6,7},{7,6},{8,9},{9,8},{10,11... | collective-permute-start | bytes 11796488 | tf_op jit(solution)/shard_map/ppermute | solution.py:686
  208.3 33.6 %collective-permute-start.20 = (bf16[512,768]{1,0:T(8,128)(2,1)}, bf16[512,768]{1,0:T(8,128)(2,1)}, u32[]{:S(2)}, u32[]{:S(2)}) collective-permute-start(bf16[512,768]{1,0:T(8,128)(2,1)} %get-tuple-element.345.refs_4_), channel_id=1, source_target_pairs={{0,1},{1,0},{2,3},{3,2},{4,5},{5,4},{6,7},{7,6},{8,9},{9,8},{10,11... | collective-permute-start | bytes 2359304 | tf_op jit(solution)/shard_map/ppermute | solution.py:686
  219.7 22.2 %collective-permute-start.18 = (bf16[384,768]{1,0:T(8,128)(2,1)}, bf16[384,768]{1,0:T(8,128)(2,1)S(1)}, u32[]{:S(2)}, u32[]{:S(2)}) collective-permute-start(bf16[384,768]{1,0:T(8,128)(2,1)} %get-tuple-element.337), channel_id=1, source_target_pairs={{0,2},{2,0},{4,6},{6,4},{8,10},{10,8},{12,14},{14,12},{16,18},{18,... | collective-permute-start | bytes 1769480 | tf_op jit(solution)/shard_map/ppermute | solution.py:690
  220.3 21.6 %collective-permute-start.19 = (bf16[384,768]{1,0:T(8,128)(2,1)}, bf16[384,768]{1,0:T(8,128)(2,1)S(1)}, u32[]{:S(2)}, u32[]{:S(2)}) collective-permute-start(bf16[384,768]{1,0:T(8,128)(2,1)} %get-tuple-element.338), channel_id=1, source_target_pairs={{0,4},{2,6},{4,0},{6,2},{8,12},{10,14},{12,8},{14,10},{16,20},{18,... | collective-permute-start | bytes 1769480 | tf_op jit(solution)/shard_map/ppermute | solution.py:690
  223.4 18.5 %collective-permute-start.21 = (bf16[512,128]{1,0:T(8,128)(2,1)}, bf16[512,128]{1,0:T(8,128)(2,1)S(1)}, u32[]{:S(2)}, u32[]{:S(2)}) collective-permute-start(bf16[512,128]{1,0:T(8,128)(2,1)} %get-tuple-element.346.refs_5_), channel_id=1, source_target_pairs={{0,1},{1,0},{2,3},{3,2},{4,5},{5,4},{6,7},{7,6},{8,9},{9,8},{10,11... | collective-permute-start | bytes 393224 | tf_op jit(solution)/shard_map/ppermute | solution.py:686
  242.5 37.6 %collective-permute-start.27 = (bf16[2,512,768]{2,1,0:T(8,128)(2,1)S(1)}, bf16[2,512,768]{2,1,0:T(8,128)(2,1)S(1)}, u32[]{:S(2)}, u32[]{:S(2)}) collective-permute-start(bf16[2,512,768]{2,1,0:T(8,128)(2,1)S(1)} %copy-done.17), channel_id=1, source_target_pairs={{0,1},{1,0},{2,3},{3,2},{4,5},{5,4},{6,7},{7,6},{8,9},{9,8},{10,11... | collective-permute-start | bytes 4718600 | tf_op jit(solution)/shard_map/ppermute | solution.py:686
  242.7 37.5 %collective-permute-start.28 = (bf16[2,512,768]{2,1,0:T(8,128)(2,1)}, bf16[2,512,768]{2,1,0:T(8,128)(2,1)}, u32[]{:S(2)}, u32[]{:S(2)}) collective-permute-start(bf16[2,512,768]{2,1,0:T(8,128)(2,1)} %get-tuple-element.373.refs_0_), channel_id=1, source_target_pairs={{0,1},{1,0},{2,3},{3,2},{4,5},{5,4},{6,7},{7,6},{8,9},{9,8},{10,11... | collective-permute-start | bytes 4718600 | tf_op jit(solution)/shard_map/ppermute | solution.py:686
  256.1 24.1 %collective-permute-start.24 = (bf16[576,768]{1,0:T(8,128)(2,1)}, bf16[576,768]{1,0:T(8,128)(2,1)S(1)}, u32[]{:S(2)}, u32[]{:S(2)}) collective-permute-start(bf16[576,768]{1,0:T(8,128)(2,1)} %get-tuple-element.359), channel_id=1, source_target_pairs={{0,2},{2,0},{4,6},{6,4},{8,10},{10,8},{12,14},{14,12},{16,18},{18,... | collective-permute-start | bytes 2654216 | tf_op jit(solution)/shard_map/ppermute | solution.py:690
  257.2 23.0 %collective-permute-start.25 = (bf16[576,768]{1,0:T(8,128)(2,1)}, bf16[576,768]{1,0:T(8,128)(2,1)}, u32[]{:S(2)}, u32[]{:S(2)}) collective-permute-start(bf16[576,768]{1,0:T(8,128)(2,1)} %get-tuple-element.360), channel_id=1, source_target_pairs={{0,4},{2,6},{4,0},{6,2},{8,12},{10,14},{12,8},{14,10},{16,20},{18,... | collective-permute-start | bytes 2654216 | tf_op jit(solution)/shard_map/ppermute | solution.py:690
  280.3 8.5 %collective-permute-start.31 = (bf16[2,512,768]{2,1,0:T(8,128)(2,1)}, bf16[2,512,768]{2,1,0:T(8,128)(2,1)}, u32[]{:S(2)}, u32[]{:S(2)}) collective-permute-start(bf16[2,512,768]{2,1,0:T(8,128)(2,1)} %get-tuple-element.380), channel_id=1, source_target_pairs={{0,1},{1,0},{2,3},{3,2},{4,5},{5,4},{6,7},{7,6},{8,9},{9,8},{10,11... | collective-permute-start | bytes 4718600 | tf_op jit(solution)/shard_map/ppermute | solution.py:686
  280.3 8.4 %collective-permute-start.32 = (bf16[512,384]{1,0:T(8,128)(2,1)}, bf16[512,384]{1,0:T(8,128)(2,1)S(1)}, u32[]{:S(2)}, u32[]{:S(2)}) collective-permute-start(bf16[512,384]{1,0:T(8,128)(2,1)} %get-tuple-element.383), channel_id=1, source_target_pairs={{0,1},{1,0},{2,3},{3,2},{4,5},{5,4},{6,7},{7,6},{8,9},{9,8},{10,11... | collective-permute-start | bytes 1179656 | tf_op jit(solution)/shard_map/ppermute | solution.py:686
  286.6 17.9 %collective-permute-start.29 = (bf16[192,768]{1,0:T(8,128)(2,1)}, bf16[192,768]{1,0:T(8,128)(2,1)S(1)}, u32[]{:S(2)}, u32[]{:S(2)}) collective-permute-start(bf16[192,768]{1,0:T(8,128)(2,1)} %get-tuple-element.376), channel_id=1, source_target_pairs={{0,2},{2,0},{4,6},{6,4},{8,10},{10,8},{12,14},{14,12},{16,18},{18,... | collective-permute-start | bytes 884744 | tf_op jit(solution)/shard_map/ppermute | solution.py:690
  287.3 17.2 %collective-permute-start.30 = (bf16[192,768]{1,0:T(8,128)(2,1)}, bf16[192,768]{1,0:T(8,128)(2,1)S(1)}, u32[]{:S(2)}, u32[]{:S(2)}) collective-permute-start(bf16[192,768]{1,0:T(8,128)(2,1)} %get-tuple-element.377), channel_id=1, source_target_pairs={{0,4},{2,6},{4,0},{6,2},{8,12},{10,14},{12,8},{14,10},{16,20},{18,... | collective-permute-start | bytes 884744 | tf_op jit(solution)/shard_map/ppermute | solution.py:690
  304.5 29.4 %collective-permute-start.33 = (bf16[768,768]{1,0:T(8,128)(2,1)}, bf16[768,768]{1,0:T(8,128)(2,1)S(1)}, u32[]{:S(2)}, u32[]{:S(2)}) collective-permute-start(bf16[768,768]{1,0:T(8,128)(2,1)} %get-tuple-element.391), channel_id=1, source_target_pairs={{0,2},{2,0},{4,6},{6,4},{8,10},{10,8},{12,14},{14,12},{16,18},{18,... | collective-permute-start | bytes 3538952 | tf_op jit(solution)/shard_map/ppermute | solution.py:690
  305.7 28.3 %collective-permute-start.34 = (bf16[768,768]{1,0:T(8,128)(2,1)}, bf16[768,768]{1,0:T(8,128)(2,1)S(1)}, u32[]{:S(2)}, u32[]{:S(2)}) collective-permute-start(bf16[768,768]{1,0:T(8,128)(2,1)} %get-tuple-element.392), channel_id=1, source_target_pairs={{0,4},{2,6},{4,0},{6,2},{8,12},{10,14},{12,8},{14,10},{16,20},{18,... | collective-permute-start | bytes 3538952 | tf_op jit(solution)/shard_map/ppermute | solution.py:690
  306.5 27.4 %collective-permute-start.35 = (bf16[96,768]{1,0:T(8,128)(2,1)S(1)}, bf16[96,768]{1,0:T(8,128)(2,1)S(1)}, u32[]{:S(2)}, u32[]{:S(2)}) collective-permute-start(bf16[96,768]{1,0:T(8,128)(2,1)S(1)} %copy-done.81), channel_id=1, source_target_pairs={{0,8},{2,10},{4,12},{6,14},{8,0},{10,2},{12,4},{14,6},{16,24},{18,... | collective-permute-start | bytes 442376 | tf_op jit(solution)/shard_map/ppermute | solution.py:690
  313.1 20.9 %collective-permute-start.36 = (bf16[96,768]{1,0:T(8,128)(2,1)S(1)}, bf16[96,768]{1,0:T(8,128)(2,1)S(1)}, u32[]{:S(2)}, u32[]{:S(2)}) collective-permute-start(bf16[96,768]{1,0:T(8,128)(2,1)S(1)} %copy-done.80), channel_id=1, source_target_pairs={{0,16},{2,18},{4,20},{6,22},{8,24},{10,26},{12,28},{14,30},{16,0},... | collective-permute-start | bytes 442376 | tf_op jit(solution)/shard_map/ppermute | solution.py:690
  315.0 18.9 %collective-permute-start.37 = (bf16[96,768]{1,0:T(8,128)(2,1)S(1)}, bf16[96,768]{1,0:T(8,128)(2,1)S(1)}, u32[]{:S(2)}, u32[]{:S(2)}) collective-permute-start(bf16[96,768]{1,0:T(8,128)(2,1)S(1)} %copy-done.79), channel_id=1, source_target_pairs={{0,24},{2,26},{4,28},{6,30},{8,16},{10,18},{12,20},{14,22},{16,8},... | collective-permute-start | bytes 442376 | tf_op jit(solution)/shard_map/ppermute | solution.py:690
  351.8 32.7 %collective-permute-start.39 = (bf16[768,768]{1,0:T(8,128)(2,1)}, bf16[768,768]{1,0:T(8,128)(2,1)S(1)}, u32[]{:S(2)}, u32[]{:S(2)}) collective-permute-start(bf16[768,768]{1,0:T(8,128)(2,1)} %get-tuple-element.429), channel_id=1, source_target_pairs={{0,2},{2,0},{4,6},{6,4},{8,10},{10,8},{12,14},{14,12},{16,18},{18,... | collective-permute-start | bytes 3538952 | tf_op jit(solution)/shard_map/ppermute | solution.py:690
  353.1 31.4 %collective-permute-start.40 = (bf16[768,768]{1,0:T(8,128)(2,1)}, bf16[768,768]{1,0:T(8,128)(2,1)S(1)}, u32[]{:S(2)}, u32[]{:S(2)}) collective-permute-start(bf16[768,768]{1,0:T(8,128)(2,1)} %get-tuple-element.430), channel_id=1, source_target_pairs={{0,4},{2,6},{4,0},{6,2},{8,12},{10,14},{12,8},{14,10},{16,20},{18,... | collective-permute-start | bytes 3538952 | tf_op jit(solution)/shard_map/ppermute | solution.py:690
  353.8 30.6 %collective-permute-start.41 = (bf16[96,768]{1,0:T(8,128)(2,1)}, bf16[96,768]{1,0:T(8,128)(2,1)S(1)}, u32[]{:S(2)}, u32[]{:S(2)}) collective-permute-start(bf16[96,768]{1,0:T(8,128)(2,1)} %get-tuple-element.431), channel_id=1, source_target_pairs={{0,8},{2,10},{4,12},{6,14},{8,0},{10,2},{12,4},{14,6},{16,24},{18,... | collective-permute-start | bytes 442376 | tf_op jit(solution)/shard_map/ppermute | solution.py:690
  359.0 25.5 %collective-permute-start.42 = (bf16[96,768]{1,0:T(8,128)(2,1)}, bf16[96,768]{1,0:T(8,128)(2,1)S(1)}, u32[]{:S(2)}, u32[]{:S(2)}) collective-permute-start(bf16[96,768]{1,0:T(8,128)(2,1)} %get-tuple-element.432), channel_id=1, source_target_pairs={{0,16},{2,18},{4,20},{6,22},{8,24},{10,26},{12,28},{14,30},{16,0},... | collective-permute-start | bytes 442376 | tf_op jit(solution)/shard_map/ppermute | solution.py:690
  360.9 23.6 %collective-permute-start.43 = (bf16[96,768]{1,0:T(8,128)(2,1)}, bf16[96,768]{1,0:T(8,128)(2,1)S(1)}, u32[]{:S(2)}, u32[]{:S(2)}) collective-permute-start(bf16[96,768]{1,0:T(8,128)(2,1)} %get-tuple-element.433), channel_id=1, source_target_pairs={{0,24},{2,26},{4,28},{6,30},{8,16},{10,18},{12,20},{14,22},{16,8},... | collective-permute-start | bytes 442376 | tf_op jit(solution)/shard_map/ppermute | solution.py:690
  384.6 10.5 %collective-permute-start.46 = (bf16[2,512,768]{2,1,0:T(8,128)(2,1)}, bf16[2,512,768]{2,1,0:T(8,128)(2,1)S(1)}, u32[]{:S(2)}, u32[]{:S(2)}) collective-permute-start(bf16[2,512,768]{2,1,0:T(8,128)(2,1)} %get-tuple-element.454), channel_id=1, source_target_pairs={{0,1},{1,0},{2,3},{3,2},{4,5},{5,4},{6,7},{7,6},{8,9},{9,8},{10,11... | collective-permute-start | bytes 4718600 | tf_op jit(solution)/shard_map/ppermute | solution.py:686
  384.6 10.4 %collective-permute-start.47 = (bf16[512,768]{1,0:T(8,128)(2,1)}, bf16[512,768]{1,0:T(8,128)(2,1)S(1)}, u32[]{:S(2)}, u32[]{:S(2)}) collective-permute-start(bf16[512,768]{1,0:T(8,128)(2,1)} %get-tuple-element.457.refs_8_), channel_id=1, source_target_pairs={{0,1},{1,0},{2,3},{3,2},{4,5},{5,4},{6,7},{7,6},{8,9},{9,8},{10,11... | collective-permute-start | bytes 2359304 | tf_op jit(solution)/shard_map/ppermute | solution.py:686
  391.1 15.2 %collective-permute-start.44 = (bf16[192,768]{1,0:T(8,128)(2,1)}, bf16[192,768]{1,0:T(8,128)(2,1)S(1)}, u32[]{:S(2)}, u32[]{:S(2)}) collective-permute-start(bf16[192,768]{1,0:T(8,128)(2,1)} %get-tuple-element.450), channel_id=1, source_target_pairs={{0,2},{2,0},{4,6},{6,4},{8,10},{10,8},{12,14},{14,12},{16,18},{18,... | collective-permute-start | bytes 884744 | tf_op jit(solution)/shard_map/ppermute | solution.py:690
  391.9 14.5 %collective-permute-start.45 = (bf16[192,768]{1,0:T(8,128)(2,1)}, bf16[192,768]{1,0:T(8,128)(2,1)S(1)}, u32[]{:S(2)}, u32[]{:S(2)}) collective-permute-start(bf16[192,768]{1,0:T(8,128)(2,1)} %get-tuple-element.451), channel_id=1, source_target_pairs={{0,4},{2,6},{4,0},{6,2},{8,12},{10,14},{12,8},{14,10},{16,20},{18,... | collective-permute-start | bytes 884744 | tf_op jit(solution)/shard_map/ppermute | solution.py:690
  406.3 27.2 %collective-permute-start.50 = (bf16[448,768]{1,0:T(8,128)(2,1)}, bf16[448,768]{1,0:T(8,128)(2,1)S(1)}, u32[]{:S(2)}, u32[]{:S(2)}) collective-permute-start(bf16[448,768]{1,0:T(8,128)(2,1)} %get-tuple-element.475), channel_id=1, source_target_pairs={{0,2},{2,0},{4,6},{6,4},{8,10},{10,8},{12,14},{14,12},{16,18},{18,... | collective-permute-start | bytes 2064392 | tf_op jit(solution)/shard_map/ppermute | solution.py:690
  407.8 25.7 %collective-permute-start.51 = (bf16[384,768]{1,0:T(8,128)(2,1)}, bf16[384,768]{1,0:T(8,128)(2,1)S(1)}, u32[]{:S(2)}, u32[]{:S(2)}) collective-permute-start(bf16[384,768]{1,0:T(8,128)(2,1)} %get-tuple-element.476), channel_id=1, source_target_pairs={{0,4},{2,6},{4,0},{6,2},{8,12},{10,14},{12,8},{14,10},{16,20},{18,... | collective-permute-start | bytes 1769480 | tf_op jit(solution)/shard_map/ppermute | solution.py:690
  409.2 14.3 %collective-permute-start.52 = (bf16[192,768]{1,0:T(8,128)(2,1)S(1)}, bf16[192,768]{1,0:T(8,128)(2,1)S(1)}, u32[]{:S(2)}, u32[]{:S(2)}) collective-permute-start(bf16[192,768]{1,0:T(8,128)(2,1)S(1)} %copy-done.78), channel_id=1, source_target_pairs={{0,8},{2,10},{4,12},{6,14},{8,0},{10,2},{12,4},{14,6},{16,24},{18,... | collective-permute-start | bytes 884744 | tf_op jit(solution)/shard_map/ppermute | solution.py:690
  410.0 23.5 %collective-permute-start.53 = (bf16[192,768]{1,0:T(8,128)(2,1)S(1)}, bf16[192,768]{1,0:T(8,128)(2,1)S(1)}, u32[]{:S(2)}, u32[]{:S(2)}) collective-permute-start(bf16[192,768]{1,0:T(8,128)(2,1)S(1)} %copy-done.77), channel_id=1, source_target_pairs={{0,16},{2,18},{4,20},{6,22},{8,24},{10,26},{12,28},{14,30},{16,0},... | collective-permute-start | bytes 884744 | tf_op jit(solution)/shard_map/ppermute | solution.py:690
  412.1 21.4 %collective-permute-start.54 = (bf16[192,768]{1,0:T(8,128)(2,1)S(1)}, bf16[192,768]{1,0:T(8,128)(2,1)S(1)}, u32[]{:S(2)}, u32[]{:S(2)}) collective-permute-start(bf16[192,768]{1,0:T(8,128)(2,1)S(1)} %copy-done.76), channel_id=1, source_target_pairs={{0,24},{2,26},{4,28},{6,30},{8,16},{10,18},{12,20},{14,22},{16,8},... | collective-permute-start | bytes 884744 | tf_op jit(solution)/shard_map/ppermute | solution.py:690
  437.3 19.9 %collective-permute-start.56 = (bf16[256,768]{1,0:T(8,128)(2,1)S(1)}, bf16[256,768]{1,0:T(8,128)(2,1)S(1)}, u32[]{:S(2)}, u32[]{:S(2)}) collective-permute-start(bf16[256,768]{1,0:T(8,128)(2,1)S(1)} %get-tuple-element.503), channel_id=1, source_target_pairs={{0,4},{2,6},{4,0},{6,2},{8,12},{10,14},{12,8},{14,10},{16,20},{18,... | collective-permute-start | bytes 1179656 | tf_op jit(solution)/shard_map/ppermute | solution.py:690
  438.5 18.7 %collective-permute-start.55 = (bf16[192,768]{1,0:T(8,128)(2,1)S(1)}, bf16[192,768]{1,0:T(8,128)(2,1)S(1)}, u32[]{:S(2)}, u32[]{:S(2)}) collective-permute-start(bf16[192,768]{1,0:T(8,128)(2,1)S(1)} %get-tuple-element.502), channel_id=1, source_target_pairs={{0,2},{2,0},{4,6},{6,4},{8,10},{10,8},{12,14},{14,12},{16,18},{18,... | collective-permute-start | bytes 884744 | tf_op jit(solution)/shard_map/ppermute | solution.py:690
  439.2 9.5 %collective-permute-start.57 = (bf16[96,768]{1,0:T(8,128)(2,1)S(1)}, bf16[96,768]{1,0:T(8,128)(2,1)S(1)}, u32[]{:S(2)}, u32[]{:S(2)}) collective-permute-start(bf16[96,768]{1,0:T(8,128)(2,1)S(1)} %get-tuple-element.504), channel_id=1, source_target_pairs={{0,8},{2,10},{4,12},{6,14},{8,0},{10,2},{12,4},{14,6},{16,24},{18,... | collective-permute-start | bytes 442376 | tf_op jit(solution)/shard_map/ppermute | solution.py:690
  444.4 12.8 %collective-permute-start.58 = (bf16[96,768]{1,0:T(8,128)(2,1)S(1)}, bf16[96,768]{1,0:T(8,128)(2,1)S(1)}, u32[]{:S(2)}, u32[]{:S(2)}) collective-permute-start(bf16[96,768]{1,0:T(8,128)(2,1)S(1)} %get-tuple-element.505), channel_id=1, source_target_pairs={{0,16},{2,18},{4,20},{6,22},{8,24},{10,26},{12,28},{14,30},{16,0},... | collective-permute-start | bytes 442376 | tf_op jit(solution)/shard_map/ppermute | solution.py:690
  446.3 10.9 %collective-permute-start.59 = (bf16[96,768]{1,0:T(8,128)(2,1)S(1)}, bf16[96,768]{1,0:T(8,128)(2,1)S(1)}, u32[]{:S(2)}, u32[]{:S(2)}) collective-permute-start(bf16[96,768]{1,0:T(8,128)(2,1)S(1)} %get-tuple-element.506), channel_id=1, source_target_pairs={{0,24},{2,26},{4,28},{6,30},{8,16},{10,18},{12,20},{14,22},{16,8},... | collective-permute-start | bytes 442376 | tf_op jit(solution)/shard_map/ppermute | solution.py:690
  458.0 18.3 %collective-permute-start.63 = (f32[1,2,48,768]{3,2,1,0:T(8,128)S(1)}, f32[1,2,48,768]{3,2,1,0:T(8,128)S(1)}, u32[]{:S(2)}, u32[]{:S(2)}) collective-permute-start(f32[1,2,48,768]{3,2,1,0:T(8,128)S(1)} %copy-done.41), channel_id=1, source_target_pairs={{0,1},{1,0},{2,3},{3,2},{4,5},{5,4},{6,7},{7,6},{8,9},{9,8},{10,11... | collective-permute-start | bytes 884744 | tf_op jit(solution)/shard_map/ppermute | solution.py:686
  458.1 18.2 %collective-permute-start.64 = (f32[1,2,48,768]{3,2,1,0:T(8,128)S(1)}, f32[1,2,48,768]{3,2,1,0:T(8,128)S(1)}, u32[]{:S(2)}, u32[]{:S(2)}) collective-permute-start(f32[1,2,48,768]{3,2,1,0:T(8,128)S(1)} %copy-done.42), channel_id=1, source_target_pairs={{0,1},{1,0},{2,3},{3,2},{4,5},{5,4},{6,7},{7,6},{8,9},{9,8},{10,11... | collective-permute-start | bytes 884744 | tf_op jit(solution)/shard_map/ppermute | solution.py:686
  458.6 9.8 %collective-permute-start.60 = (bf16[112,768]{1,0:T(8,128)(2,1)S(1)}, bf16[112,768]{1,0:T(8,128)(2,1)S(1)}, u32[]{:S(2)}, u32[]{:S(2)}) collective-permute-start(bf16[112,768]{1,0:T(8,128)(2,1)S(1)} %get-tuple-element.525), channel_id=1, source_target_pairs={{0,8},{2,10},{4,12},{6,14},{8,0},{10,2},{12,4},{14,6},{16,24},{18,... | collective-permute-start | bytes 516104 | tf_op jit(solution)/shard_map/ppermute | solution.py:690
  460.7 15.5 %collective-permute-start.61 = (bf16[112,768]{1,0:T(8,128)(2,1)S(1)}, bf16[112,768]{1,0:T(8,128)(2,1)S(1)}, u32[]{:S(2)}, u32[]{:S(2)}) collective-permute-start(bf16[112,768]{1,0:T(8,128)(2,1)S(1)} %get-tuple-element.526), channel_id=1, source_target_pairs={{0,16},{2,18},{4,20},{6,22},{8,24},{10,26},{12,28},{14,30},{16,0},... | collective-permute-start | bytes 516104 | tf_op jit(solution)/shard_map/ppermute | solution.py:690
  461.8 14.5 %collective-permute-start.62 = (bf16[112,768]{1,0:T(8,128)(2,1)S(1)}, bf16[112,768]{1,0:T(8,128)(2,1)S(1)}, u32[]{:S(2)}, u32[]{:S(2)}) collective-permute-start(bf16[112,768]{1,0:T(8,128)(2,1)S(1)} %get-tuple-element.527), channel_id=1, source_target_pairs={{0,24},{2,26},{4,28},{6,30},{8,16},{10,18},{12,20},{14,22},{16,8},... | collective-permute-start | bytes 516104 | tf_op jit(solution)/shard_map/ppermute | solution.py:690
  468.3 27.1 %collective-permute-start.73 = (f32[2,2,48,768]{3,2,1,0:T(8,128)S(1)}, f32[2,2,48,768]{3,2,1,0:T(8,128)S(1)}, u32[]{:S(2)}, u32[]{:S(2)}) collective-permute-start(f32[2,2,48,768]{3,2,1,0:T(8,128)S(1)} %get-tuple-element.537.refs_5_), channel_id=1, source_target_pairs={{0,1},{1,0},{2,3},{3,2},{4,5},{5,4},{6,7},{7,6},{8,9},{9,8},{10,11... | collective-permute-start | bytes 1769480 | tf_op jit(solution)/shard_map/ppermute | solution.py:686
  485.3 5.6 %collective-permute-start.69 = (f32[1,128]{1,0:T(1,128)S(1)}, f32[1,128]{1,0:T(1,128)S(1)}, u32[]{:S(2)}, u32[]{:S(2)}) collective-permute-start(f32[1,128]{1,0:T(1,128)S(1)} %add_add_fusion.1), channel_id=1, source_target_pairs={{0,8},{2,10},{4,12},{6,14},{8,0},{10,2},{12,4},{14,6},{16,24},{18,... | collective-permute-start | bytes 1544 | tf_op jit(solution)/shard_map/ppermute | solution.py:690
  489.5 5.3 %collective-permute-start.71 = (f32[1,128]{1,0:T(1,128)S(1)}, f32[1,128]{1,0:T(1,128)S(1)}, u32[]{:S(2)}, u32[]{:S(2)}) collective-permute-start(f32[1,128]{1,0:T(1,128)S(1)} %add_add_fusion.1), channel_id=1, source_target_pairs={{0,24},{2,26},{4,28},{6,30},{8,16},{10,18},{12,20},{14,22},{16,8},... | collective-permute-start | bytes 1544 | tf_op jit(solution)/shard_map/ppermute | solution.py:690
  490.9 4.6 collective-permute-start.75
  (95 other events, 959.7 us)
Sparse Core Ops, SparseCore 0:
  13.2 139.3 all-gather.1

commit v17 on v16

--- a/solution.py
+++ b/solution.py
@@ -746,6 +746,8 @@
     targets = [tiles.at[t] for t in range(2 * count)] + small
     for n, target in enumerate(targets):
         pltpu.make_async_copy(target, target, sems.at[n]).wait()
+        if n < 2 * count:
+            tiles.send(n)
 
 
 class Gather:
@@ -785,6 +787,7 @@
             [],
             [self.quarter] + self.near + self.far,
             [pltpu.SemaphoreType.DMA((2 * count + 1,))],
+            sent=(0,),
         )
 
 
@@ -874,6 +877,7 @@
                     index = lambda bit: zz * 4 + (other * 2 + bit if s == 0 else bit * 2 + other)
                     to[s][block(p * 8 + at), :] = tile[s, block(index(1 - bits[s])), :].astype(LOW)
                     out_once[p, s, block(at), :] = tile[s, block(index(bits[s])), :]
+            out_once.send((p, s))
     if small_new:
         products, norms_at = small_job
         flat[...] = summed([(right, left) for left, right in products])
@@ -1037,6 +1041,7 @@
                 [],
                 scratch,
                 4 * new * length * width * width,
+                sent=(2,) if new else (),
                 limit=limit,
             )
         )

time: 524 us -> 527 us (level)
  transfers between devices with their start and end apart: 77 -> 77, of which waited for: 27 -> 28; matrix products, arithmetic and copies ran while one was open for 2% -> 2% of each run, Pallas kernels for 37% -> 38%
where the time goes in v17:
time: 527 us; the launch traced here: 517 us
  Pallas kernels  241 us (46%)
  waiting for transfers between devices  142 us (27%)
  starting transfers between devices  91.6 us (17%)
  local copies, waits for them, and re-layouts  20.7 us (4%)
  between operations  15.5 us (3%)
  other arithmetic  5.36 us (1%)
    pallas_call x25, Pallas kernels, call(): pl.pallas_call(body, out_shape=[jax.ShapeDtypeStruct(s, t) for s, t in ou...  241 us
    ppermute x51, waiting for transfers between devices, across(): return lax.ppermute(value, 'fsdp', [(i, i ^ mask) for i in range(size)])  129 us
    ppermute x51, starting transfers between devices, across(): return lax.ppermute(value, 'fsdp', [(i, i ^ mask) for i in range(size)])  86.3 us
    unnamed x164, local copies, waits for them, and re-layouts  14.2 us
    ppermute x25, waiting for transfers between devices, swap_cores(): return lax.ppermute(value, 'dp', [(0, 1), (1, 0)])  12.4 us
  transfers between devices with their start and end apart: 77, of which 28 were waited for; matrix products, arithmetic and copies ran while one was open for 2% of the time, Pallas kernels for 38%

profile of v17, /device:TPU:0, one launch (start us, length us, event | category | flops | bytes accessed | tf_op | source)
XLA Modules:
  0.0 517.4 jit_solution(13041547693096924815)
XLA Ops:
  10.1 3.0 shard_map.364
  13.1 3.1 collective-permute-start
  16.2 2.6 collective-permute-start.1
  19.6 3.9 collective-permute-done.refs_1_
  23.5 12.3 %collective-permute-done.1.refs_2_ = bf16[112,768]{1,0:T(8,128)(2,1)S(1)} collective-permute-done((bf16[112,768]{1,0:T(8,128)(2,1)}, bf16[112,768]{1,0:T(8,128)(2,1)S(1)}, u32[]{:S(2)}, u32[]{:S(2)}) %collective-permute-start.1) | collective-permute-done | bytes 172064 | tf_op jit(solution)/shard_map/ppermute | solution.py:690
  36.7 2.8 shard_map.365.refs_0_
  39.5 1.6 collective-permute-start.3
  41.0 1.5 collective-permute-start.4
  42.6 8.5 %collective-permute-start.5 = (bf16[192,768]{1,0:T(8,128)(2,1)S(1)}, bf16[192,768]{1,0:T(8,128)(2,1)S(1)}, u32[]{:S(2)}, u32[]{:S(2)}) collective-permute-start(bf16[192,768]{1,0:T(8,128)(2,1)S(1)} %copy-done.36), channel_id=1, source_target_pairs={{0,8},{2,10},{4,12},{6,14},{8,0},{10,2},{12,4},{14,6},{16,24},{18,... | collective-permute-start | bytes 884744 | tf_op jit(solution)/shard_map/ppermute | solution.py:690
  52.0 1.5 collective-permute-start.7
  53.5 12.3 %collective-permute-done.5.refs_1_ = bf16[192,768]{1,0:T(8,128)(2,1)S(1)} collective-permute-done((bf16[192,768]{1,0:T(8,128)(2,1)S(1)}, bf16[192,768]{1,0:T(8,128)(2,1)S(1)}, u32[]{:S(2)}, u32[]{:S(2)}) %collective-permute-start.5) | collective-permute-done | bytes 294944 | tf_op jit(solution)/shard_map/ppermute | solution.py:690
  65.8 22.0 %collective-permute-done.6.refs_2_ = bf16[192,768]{1,0:T(8,128)(2,1)S(1)} collective-permute-done((bf16[192,768]{1,0:T(8,128)(2,1)S(1)}, bf16[192,768]{1,0:T(8,128)(2,1)S(1)}, u32[]{:S(2)}, u32[]{:S(2)}) %collective-permute-start.6) | collective-permute-done | bytes 294944 | tf_op jit(solution)/shard_map/ppermute | solution.py:690
  88.0 6.7 %collective-permute-done.9.refs_4_ = bf16[192,768]{1,0:T(8,128)(2,1)S(1)} collective-permute-done((bf16[192,768]{1,0:T(8,128)(2,1)S(1)}, bf16[192,768]{1,0:T(8,128)(2,1)S(1)}, u32[]{:S(2)}, u32[]{:S(2)}) %collective-permute-start.9) | collective-permute-done | bytes 294944 | tf_op jit(solution)/shard_map/ppermute | solution.py:690
  96.4 4.7 shard_map.366
  101.2 3.1 shard_map.368.refs_0_
  104.4 1.8 collective-permute-start.11
  110.9 1.6 fusion.3.refs_0_.refs_10_
  112.6 14.5 %shard_map.367 = (f32[512,768]{1,0:T(8,128)}, bf16[512,768]{1,0:T(8,128)(2,1)}, bf16[512,768]{1,0:T(8,128)(2,1)}, bf16[512,768]{1,0:T(8,128)(2,1)}, f32[16,512]{1,0:T(8,128)}, /*index=5*/bf16[2,512,768]{2,1,0:T(8,128)(2,1)}) custom-call(s32[4]{0:T(128)} %pad_add_fusion.scalars, f32[512,768]{1,0:T(8,128)} %fusion.3.refs_0_.refs_10_, ...), custom_call_target="tpu_custom_call" | custom-call | flops 3221225472 | bytes 6825984 | tf_op jit(solution)/shard_map/pallas_call | solution.py:111
  127.1 20.7 %collective-permute-done.11.refs_1_ = bf16[768,768]{1,0:T(8,128)(2,1)S(1)} collective-permute-done((bf16[768,768]{1,0:T(8,128)(2,1)}, bf16[768,768]{1,0:T(8,128)(2,1)S(1)}, u32[]{:S(2)}, u32[]{:S(2)}) %collective-permute-start.11) | collective-permute-done | bytes 1179680 | tf_op jit(solution)/shard_map/ppermute | solution.py:690
  152.0 12.7 %shard_map.369 = (f32[512,768]{1,0:T(8,128)}, bf16[5,512,768]{2,1,0:T(8,128)(2,1)}, f32[4,512,768]{2,1,0:T(8,128)}) custom-call(s32[4]{0:T(128)} %pad_add_fusion.scalars, f32[512,768]{1,0:T(8,128)} %get-tuple-element.311.refs_0_.refs_2_, f32[2,768]{1,0:T(2,128)} %get-tuple-element.564.refs_1_.refs_3_, bf16[16,2,48,4608]{3,2,1,0:T(8,128)(2,1)} %bitcast.22), custom_call_target="tpu_custom_call" | custom-call | flops 4831838208 | bytes 15734784 | tf_op jit(solution)/shard_map/pallas_call | solution.py:111
  167.0 5.2 %shard_map.370.refs_2_.refs_5_ = bf16[4,16,48,768]{3,2,1,0:T(8,128)(2,1)} custom-call(s32[4]{0:T(128)} %pad_add_fusion.scalars, bf16[768,768]{1,0:T(8,128)(2,1)} %shard_map.368.refs_0_, bf16[768,768]{1,0:T(8,128)(2,1)} %copy-done.14, bf16[768,768]{1,0:T(8,128)(2,1)} %copy-done.15, bf16[384,768]{1,0:T(8,128)(2,1)} %copy-done.32, bf16[384,768]{1,0:T(8,128)(2,1)} %copy-done.33), custom_call_target="tpu_custom_call" | custom-call | bytes 4718592 | tf_op jit(solution)/shard_map/pallas_call | solution.py:111
  172.2 14.3 %shard_map.371 = (f32[512,768]{1,0:T(8,128)}, bf16[512,768]{1,0:T(8,128)(2,1)}, bf16[512,768]{1,0:T(8,128)(2,1)}, bf16[512,768]{1,0:T(8,128)(2,1)}, f32[16,512]{1,0:T(8,128)}, /*index=5*/bf16[2,512,768]{2,1,0:T(8,128)(2,1)}) custom-call(s32[4]{0:T(128)} %pad_add_fusion.scalars, f32[512,768]{1,0:T(8,128)} %get-tuple-element.320.refs_0_.refs_10_, ...), custom_call_target="tpu_custom_call" | custom-call | flops 3221225472 | bytes 16263168 | tf_op jit(solution)/shard_map/pallas_call | solution.py:111
  186.6 2.2 copy-done.11
  188.7 12.9 %shard_map.372 = (f32[512,768]{1,0:T(8,128)}, bf16[5,512,768]{2,1,0:T(8,128)(2,1)}, f32[4,512,768]{2,1,0:T(8,128)}) custom-call(s32[4]{0:T(128)} %pad_add_fusion.scalars, f32[512,768]{1,0:T(8,128)} %get-tuple-element.321.refs_0_.refs_2_, f32[2,768]{1,0:T(2,128)} %get-tuple-element.562.refs_1_.refs_3_, bf16[4,16,48,768]{3,2,1,0:T(8,128)(2,1)} %shard_map.370.refs_2_.refs_5_, ...), custom_call_target="tpu_custom_call" | custom-call | flops 4831838208 | bytes 11016192 | tf_op jit(solution)/shard_map/pallas_call | solution.py:111
  202.3 5.5 %shard_map.373 = (f32[512,768]{1,0:T(8,128)}, bf16[512,768]{1,0:T(8,128)(2,1)}, bf16[512,384]{1,0:T(8,128)(2,1)}, bf16[512,384]{1,0:T(8,128)(2,1)}, bf16[512,768...) custom-call(s32[4]{0:T(128)} %pad_add_fusion.scalars, ...), custom_call_target="tpu_custom_call" | custom-call | flops 201326592 | bytes 2168832 | tf_op jit(solution)/shard_map/pallas_call | solution.py:111
  210.9 9.5 %shard_map.374 = (bf16[384,768]{1,0:T(8,128)(2,1)}, bf16[384,768]{1,0:T(8,128)(2,1)}, f32[1,2,384,768]{3,2,1,0:T(8,128)}) custom-call(s32[4]{0:T(128)} %pad_add_fusion.scalars, bf16[5,512,768]{2,1,0:T(8,128)(2,1)} %get-tuple-element.323.refs_0_, bf16[512,384]{1,0:T(8,128)(2,1)} %get-tuple-element.327.refs_1_, bf16[5,512,768]{2,1,0:T(8,128)(2,1)} %copy-done.13, ...), custom_call_target="tpu_custom_call" | custom-call | flops 2415919104 | bytes 8650752 | tf_op jit(solution)/shard_map/pallas_call | solution.py:111
  221.1 1.5 collective-permute-start.19
  224.8 17.8 %shard_map.375 = (f32[512,768]{1,0:T(8,128)}, f32[2,768]{1,0:T(2,128)}, bf16[2,512,768]{2,1,0:T(8,128)(2,1)}, bf16[2,512,768]{2,1,0:T(8,128)(2,1)}) custom-call(s32[4]{0:T(128)} %pad_add_fusion.scalars, bf16[512,768]{1,0:T(8,128)(2,1)} %get-tuple-element.339.refs_0_, f32[512,768]{1,0:T(8,128)} %get-tuple-element.340.refs_1_, ...), custom_call_target="tpu_custom_call" | custom-call | flops 4831838208 | bytes 19666944 | tf_op jit(solution)/shard_map/pallas_call | solution.py:111
  243.8 2.7 collective-permute-done.23.refs_3_
  246.6 11.0 %shard_map.376 = (bf16[576,768]{1,0:T(8,128)(2,1)}, bf16[576,768]{1,0:T(8,128)(2,1)}, f32[1,2,384,768]{3,2,1,0:T(8,128)}, f32[1,2,192,768]{3,2,1,0:T(8,128)}) custom-call(s32[4]{0:T(128)} %pad_add_fusion.scalars, bf16[5,512,768]{2,1,0:T(8,128)(2,1)} %get-tuple-element.323.refs_0_, bf16[2,512,768]{2,1,0:T(8,128)(2,1)} %get-tuple-element.347.refs_1_, ...), custom_call_target="tpu_custom_call" | custom-call | flops 2415919104 | bytes 14548992 | tf_op jit(solution)/shard_map/pallas_call | solution.py:111
  259.6 22.1 %shard_map.377 = (f32[512,768]{1,0:T(8,128)}, bf16[512,768]{1,0:T(8,128)(2,1)}, bf16[512,384]{1,0:T(8,128)(2,1)}, bf16[512,384]{1,0:T(8,128)(2,1)}, f32[2,768]{1...) custom-call(s32[4]{0:T(128)} %pad_add_fusion.scalars, f32[512,768]{1,0:T(8,128)} %get-tuple-element.361.refs_0_, ...), custom_call_target="tpu_custom_call" | custom-call | flops 4429185024 | bytes 20228096 | tf_op jit(solution)/shard_map/pallas_call | solution.py:111
  282.7 5.4 %shard_map.378 = (bf16[192,768]{1,0:T(8,128)(2,1)}, bf16[192,768]{1,0:T(8,128)(2,1)}, f32[1,2,192,768]{3,2,1,0:T(8,128)}, f32[1,2,48,768]{3,2,1,0:T(8,128)}, bf1...) custom-call(s32[4]{0:T(128)} %pad_add_fusion.scalars, ...), custom_call_target="tpu_custom_call" | custom-call | bytes 5308416 | tf_op jit(solution)/shard_map/pallas_call | solution.py:111
  288.8 1.5 collective-permute-start.30
  291.0 14.9 %shard_map.379 = (bf16[768,768]{1,0:T(8,128)(2,1)}, bf16[768,768]{1,0:T(8,128)(2,1)}, f32[2,2,384,768]{3,2,1,0:T(8,128)}) custom-call(s32[4]{0:T(128)} %pad_add_fusion.scalars, bf16[2,512,768]{2,1,0:T(8,128)(2,1)} %get-tuple-element.373.refs_0_, bf16[2,512,768]{2,1,0:T(8,128)(2,1)} %get-tuple-element.378.refs_1_, ...), custom_call_target="tpu_custom_call" | custom-call | flops 4831838208 | bytes 14942208 | tf_op jit(solution)/shard_map/pallas_call | solution.py:111
  307.9 6.5 %collective-permute-start.35 = (bf16[96,768]{1,0:T(8,128)(2,1)S(1)}, bf16[96,768]{1,0:T(8,128)(2,1)S(1)}, u32[]{:S(2)}, u32[]{:S(2)}) collective-permute-start(bf16[96,768]{1,0:T(8,128)(2,1)S(1)} %copy-done.81), channel_id=1, source_target_pairs={{0,8},{2,10},{4,12},{6,14},{8,0},{10,2},{12,4},{14,6},{16,24},{18,... | collective-permute-start | bytes 442376 | tf_op jit(solution)/shard_map/ppermute | solution.py:690
  314.5 1.9 collective-permute-start.36
  316.3 1.5 collective-permute-start.37
  317.8 17.4 %shard_map.380 = (f32[512,768]{1,0:T(8,128)}, f32[2,768]{1,0:T(2,128)}, bf16[2,512,768]{2,1,0:T(8,128)(2,1)}, bf16[2,512,768]{2,1,0:T(8,128)(2,1)}) custom-call(s32[4]{0:T(128)} %pad_add_fusion.scalars, bf16[512,768]{1,0:T(8,128)(2,1)} %get-tuple-element.396.refs_0_, f32[512,768]{1,0:T(8,128)} %get-tuple-element.397.refs_1_, ...), custom_call_target="tpu_custom_call" | custom-call | flops 4831838208 | bytes 24385536 | tf_op jit(solution)/shard_map/pallas_call | solution.py:111
  335.8 3.6 collective-permute-done.38.refs_3_
  340.6 13.5 %shard_map.381 = (bf16[768,768]{1,0:T(8,128)(2,1)}, bf16[768,768]{1,0:T(8,128)(2,1)}, f32[1,2,384,768]{3,2,1,0:T(8,128)}, f32[2,2,192,768]{3,2,1,0:T(8,128)}, f3...) custom-call(s32[4]{0:T(128)} %pad_add_fusion.scalars, ...), custom_call_target="tpu_custom_call" | custom-call | flops 2415919104 | bytes 20597760 | tf_op jit(solution)/shard_map/pallas_call | solution.py:111
  354.1 1.5 collective-permute-start.39
  356.2 5.3 %collective-permute-start.41 = (bf16[96,768]{1,0:T(8,128)(2,1)}, bf16[96,768]{1,0:T(8,128)(2,1)S(1)}, u32[]{:S(2)}, u32[]{:S(2)}) collective-permute-start(bf16[96,768]{1,0:T(8,128)(2,1)} %get-tuple-element.431), channel_id=1, source_target_pairs={{0,8},{2,10},{4,12},{6,14},{8,0},{10,2},{12,4},{14,6},{16,24},{18,... | collective-permute-start | bytes 442376 | tf_op jit(solution)/shard_map/ppermute | solution.py:690
  361.5 1.8 collective-permute-start.42
  363.3 1.5 collective-permute-start.43
  364.8 22.1 %shard_map.382 = (f32[512,768]{1,0:T(8,128)}, bf16[512,768]{1,0:T(8,128)(2,1)}, bf16[512,384]{1,0:T(8,128)(2,1)}, bf16[512,384]{1,0:T(8,128)(2,1)}, f32[2,768]{1...) custom-call(s32[4]{0:T(128)} %pad_add_fusion.scalars, f32[512,768]{1,0:T(8,128)} %get-tuple-element.434.refs_0_, ...), custom_call_target="tpu_custom_call" | custom-call | flops 4429185024 | bytes 10790912 | tf_op jit(solution)/shard_map/pallas_call | solution.py:111
  388.5 5.1 shard_map.383
  399.5 10.1 %shard_map.384 = (bf16[448,768]{1,0:T(8,128)(2,1)}, bf16[384,768]{1,0:T(8,128)(2,1)}, f32[1,2,384,768]{3,2,1,0:T(8,128)}, f32[384,128]{1,0:T(8,128)}) custom-call(s32[4]{0:T(128)} %pad_add_fusion.scalars, bf16[2,512,768]{2,1,0:T(8,128)(2,1)} %get-tuple-element.372.refs_0_, bf16[2,512,768]{2,1,0:T(8,128)(2,1)} %get-tuple-element.452.refs_1_, ...), custom_call_target="tpu_custom_call" | custom-call | flops 2415919104 | bytes 10022912 | tf_op jit(solution)/shard_map/pallas_call | solution.py:111
  413.1 2.3 collective-permute-start.53
  415.4 1.5 collective-permute-start.54
  416.9 9.9 %collective-permute-done.52.refs_8_ = bf16[192,768]{1,0:T(8,128)(2,1)S(1)} collective-permute-done((bf16[192,768]{1,0:T(8,128)(2,1)S(1)}, bf16[192,768]{1,0:T(8,128)(2,1)S(1)}, u32[]{:S(2)}, u32[]{:S(2)}) %collective-permute-start.52) | collective-permute-done | bytes 294944 | tf_op jit(solution)/shard_map/ppermute | solution.py:690
  426.8 9.8 %collective-permute-done.53.refs_9_ = bf16[192,768]{1,0:T(8,128)(2,1)S(1)} collective-permute-done((bf16[192,768]{1,0:T(8,128)(2,1)S(1)}, bf16[192,768]{1,0:T(8,128)(2,1)S(1)}, u32[]{:S(2)}, u32[]{:S(2)}) %collective-permute-start.53) | collective-permute-done | bytes 294944 | tf_op jit(solution)/shard_map/ppermute | solution.py:690
  436.6 1.7 copy-done
  442.4 5.2 %collective-permute-start.57 = (bf16[96,768]{1,0:T(8,128)(2,1)S(1)}, bf16[96,768]{1,0:T(8,128)(2,1)S(1)}, u32[]{:S(2)}, u32[]{:S(2)}) collective-permute-start(bf16[96,768]{1,0:T(8,128)(2,1)S(1)} %get-tuple-element.504), channel_id=1, source_target_pairs={{0,8},{2,10},{4,12},{6,14},{8,0},{10,2},{12,4},{14,6},{16,24},{18,... | collective-permute-start | bytes 442376 | tf_op jit(solution)/shard_map/ppermute | solution.py:690
  447.7 1.8 collective-permute-start.58
  451.9 8.4 %collective-permute-done.58.refs_6_ = bf16[96,768]{1,0:T(8,128)(2,1)S(1)} collective-permute-done((bf16[96,768]{1,0:T(8,128)(2,1)S(1)}, bf16[96,768]{1,0:T(8,128)(2,1)S(1)}, u32[]{:S(2)}, u32[]{:S(2)}) %collective-permute-start.58) | collective-permute-done | bytes 147488 | tf_op jit(solution)/shard_map/ppermute | solution.py:690
  461.7 2.1 collective-permute-start.60
  466.4 5.1 collective-permute-done.60.refs_2_
  471.5 7.9 %collective-permute-done.61.refs_3_ = bf16[112,768]{1,0:T(8,128)(2,1)S(1)} collective-permute-done((bf16[112,768]{1,0:T(8,128)(2,1)S(1)}, bf16[112,768]{1,0:T(8,128)(2,1)S(1)}, u32[]{:S(2)}, u32[]{:S(2)}) %collective-permute-start.61) | collective-permute-done | bytes 172064 | tf_op jit(solution)/shard_map/ppermute | solution.py:690
  481.8 1.6 collective-permute-start.66
  484.0 1.5 collective-permute-start.68
  487.0 1.5 collective-permute-done.68
  488.5 3.1 collective-permute-start.69
  496.0 2.0 collective-permute-done.71
  499.7 10.6 %shard_map.388 = (f32[1,1]{1,0:T(1,128)}, f32[2,48,2304]{2,1,0:T(8,128)}, f32[2,48,2304]{2,1,0:T(8,128)}, f32[2,48,2304]{2,1,0:T(8,128)}, f32[2,48,768]{2,1,0:T(...) custom-call(s32[4]{0:T(128)} %pad_add_fusion.scalars, ...), custom_call_target="tpu_custom_call" | custom-call | flops 53314560 | bytes 14251520 | tf_op jit(solution)/shard_map/pallas_call | solution.py:111
  (312 shorter events, 67.0 us)
Async XLA Ops:
  7.2 144.9 %all-gather.2.cloned.1.call-start = ((), (), s32[]{:S(2)}) async-start(), calls=%async_computation | async-start | bytes 14598144 | tf_op jit(solution)/shard_map/all_gather | solution.py:1208
  13.1 10.4 %collective-permute-start = (bf16[112,768]{1,0:T(8,128)(2,1)}, bf16[112,768]{1,0:T(8,128)(2,1)S(1)}, u32[]{:S(2)}, u32[]{:S(2)}) collective-permute-start(bf16[112,768]{1,0:T(8,128)(2,1)} %get-tuple-element.291.refs_0_), channel_id=1, source_target_pairs={{0,8},{2,10},{4,12},{6,14},{8,0},{10,2},{12,4},{14,6},{16,24},{18,... | collective-permute-start | bytes 516104 | tf_op jit(solution)/shard_map/ppermute | solution.py:690
  16.2 19.6 %collective-permute-start.1 = (bf16[112,768]{1,0:T(8,128)(2,1)}, bf16[112,768]{1,0:T(8,128)(2,1)S(1)}, u32[]{:S(2)}, u32[]{:S(2)}) collective-permute-start(bf16[112,768]{1,0:T(8,128)(2,1)} %get-tuple-element.291.refs_0_), channel_id=1, source_target_pairs={{0,16},{2,18},{4,20},{6,22},{8,24},{10,26},{12,28},{14,30},{16,0},... | collective-permute-start | bytes 516104 | tf_op jit(solution)/shard_map/ppermute | solution.py:690
  18.8 17.0 %collective-permute-start.2 = (bf16[112,768]{1,0:T(8,128)(2,1)}, bf16[112,768]{1,0:T(8,128)(2,1)S(1)}, u32[]{:S(2)}, u32[]{:S(2)}) collective-permute-start(bf16[112,768]{1,0:T(8,128)(2,1)} %get-tuple-element.291.refs_0_), channel_id=1, source_target_pairs={{0,24},{2,26},{4,28},{6,30},{8,16},{10,18},{12,20},{14,22},{16,8},... | collective-permute-start | bytes 516104 | tf_op jit(solution)/shard_map/ppermute | solution.py:690
  39.5 48.3 %collective-permute-start.3 = (bf16[448,768]{1,0:T(8,128)(2,1)}, bf16[448,768]{1,0:T(8,128)(2,1)S(1)}, u32[]{:S(2)}, u32[]{:S(2)}) collective-permute-start(bf16[448,768]{1,0:T(8,128)(2,1)} %shard_map.365.refs_0_), channel_id=1, source_target_pairs={{0,2},{2,0},{4,6},{6,4},{8,10},{10,8},{12,14},{14,12},{16,18},{18,... | collective-permute-start | bytes 2064392 | tf_op jit(solution)/shard_map/ppermute | solution.py:690
  41.0 46.8 %collective-permute-start.4 = (bf16[448,768]{1,0:T(8,128)(2,1)}, bf16[448,768]{1,0:T(8,128)(2,1)S(1)}, u32[]{:S(2)}, u32[]{:S(2)}) collective-permute-start(bf16[448,768]{1,0:T(8,128)(2,1)} %shard_map.365.refs_0_), channel_id=1, source_target_pairs={{0,4},{2,6},{4,0},{6,2},{8,12},{10,14},{12,8},{14,10},{16,20},{18,... | collective-permute-start | bytes 2064392 | tf_op jit(solution)/shard_map/ppermute | solution.py:690
  42.6 23.2 %collective-permute-start.5 = (bf16[192,768]{1,0:T(8,128)(2,1)S(1)}, bf16[192,768]{1,0:T(8,128)(2,1)S(1)}, u32[]{:S(2)}, u32[]{:S(2)}) collective-permute-start(bf16[192,768]{1,0:T(8,128)(2,1)S(1)} %copy-done.36), channel_id=1, source_target_pairs={{0,8},{2,10},{4,12},{6,14},{8,0},{10,2},{12,4},{14,6},{16,24},{18,... | collective-permute-start | bytes 884744 | tf_op jit(solution)/shard_map/ppermute | solution.py:690
  51.1 36.7 %collective-permute-start.6 = (bf16[192,768]{1,0:T(8,128)(2,1)S(1)}, bf16[192,768]{1,0:T(8,128)(2,1)S(1)}, u32[]{:S(2)}, u32[]{:S(2)}) collective-permute-start(bf16[192,768]{1,0:T(8,128)(2,1)S(1)} %copy-done.36), channel_id=1, source_target_pairs={{0,16},{2,18},{4,20},{6,22},{8,24},{10,26},{12,28},{14,30},{16,0},... | collective-permute-start | bytes 884744 | tf_op jit(solution)/shard_map/ppermute | solution.py:690
  52.0 35.7 %collective-permute-start.7 = (bf16[192,768]{1,0:T(8,128)(2,1)S(1)}, bf16[192,768]{1,0:T(8,128)(2,1)S(1)}, u32[]{:S(2)}, u32[]{:S(2)}) collective-permute-start(bf16[192,768]{1,0:T(8,128)(2,1)S(1)} %copy-done.36), channel_id=1, source_target_pairs={{0,24},{2,26},{4,28},{6,30},{8,16},{10,18},{12,20},{14,22},{16,8},... | collective-permute-start | bytes 884744 | tf_op jit(solution)/shard_map/ppermute | solution.py:690
  87.8 7.8 %collective-permute-start.8 = (bf16[256,768]{1,0:T(8,128)(2,1)S(1)}, bf16[256,768]{1,0:T(8,128)(2,1)S(1)}, u32[]{:S(2)}, u32[]{:S(2)}) collective-permute-start(bf16[256,768]{1,0:T(8,128)(2,1)S(1)} %slice.58), channel_id=1, source_target_pairs={{0,2},{2,0},{4,6},{6,4},{8,10},{10,8},{12,14},{14,12},{16,18},{18,... | collective-permute-start | bytes 1179656 | tf_op jit(solution)/shard_map/ppermute | solution.py:690
  87.9 6.8 %collective-permute-start.9 = (bf16[192,768]{1,0:T(8,128)(2,1)S(1)}, bf16[192,768]{1,0:T(8,128)(2,1)S(1)}, u32[]{:S(2)}, u32[]{:S(2)}) collective-permute-start(bf16[192,768]{1,0:T(8,128)(2,1)S(1)} %slice.59), channel_id=1, source_target_pairs={{0,4},{2,6},{4,0},{6,2},{8,12},{10,14},{12,8},{14,10},{16,20},{18,... | collective-permute-start | bytes 884744 | tf_op jit(solution)/shard_map/ppermute | solution.py:690
  101.1 11.4 %collective-permute-start.10 = (bf16[2,16,48,768]{3,2,1,0:T(8,128)(2,1)}, bf16[2,16,48,768]{3,2,1,0:T(8,128)(2,1)}, u32[]{:S(2)}, u32[]{:S(2)}) collective-permute-start(bf16[2,16,48,768]{3,2,1,0:T(8,128)(2,1)} %get-tuple-element.303.refs_6_.refs_11_), channel_id=1, source_target_pairs={{0,1},{1,0},{2,3},{3,2},{4,5},{5,4},{6,7},{7,6},{8,9},{9,8},{10,11... | collective-permute-start | bytes 7077896 | tf_op jit(solution)/shard_map/ppermute | solution.py:686
  104.4 43.3 %collective-permute-start.11 = (bf16[768,768]{1,0:T(8,128)(2,1)}, bf16[768,768]{1,0:T(8,128)(2,1)S(1)}, u32[]{:S(2)}, u32[]{:S(2)}) collective-permute-start(bf16[768,768]{1,0:T(8,128)(2,1)} %shard_map.368.refs_0_), channel_id=1, source_target_pairs={{0,2},{2,0},{4,6},{6,4},{8,10},{10,8},{12,14},{14,12},{16,18},{18,... | collective-permute-start | bytes 3538952 | tf_op jit(solution)/shard_map/ppermute | solution.py:690
  106.2 41.6 %collective-permute-start.12 = (bf16[768,768]{1,0:T(8,128)(2,1)}, bf16[768,768]{1,0:T(8,128)(2,1)S(1)}, u32[]{:S(2)}, u32[]{:S(2)}) collective-permute-start(bf16[768,768]{1,0:T(8,128)(2,1)} %shard_map.368.refs_0_), channel_id=1, source_target_pairs={{0,4},{2,6},{4,0},{6,2},{8,12},{10,14},{12,8},{14,10},{16,20},{18,... | collective-permute-start | bytes 3538952 | tf_op jit(solution)/shard_map/ppermute | solution.py:690
  148.7 16.1 %collective-permute-start.13 = (bf16[384,768]{1,0:T(8,128)(2,1)}, bf16[384,768]{1,0:T(8,128)(2,1)S(1)}, u32[]{:S(2)}, u32[]{:S(2)}) collective-permute-start(bf16[384,768]{1,0:T(8,128)(2,1)} %slice.64), channel_id=1, source_target_pairs={{0,2},{2,0},{4,6},{6,4},{8,10},{10,8},{12,14},{14,12},{16,18},{18,... | collective-permute-start | bytes 1769480 | tf_op jit(solution)/shard_map/ppermute | solution.py:690
  151.0 15.1 %collective-permute-start.14 = (bf16[384,768]{1,0:T(8,128)(2,1)}, bf16[384,768]{1,0:T(8,128)(2,1)S(1)}, u32[]{:S(2)}, u32[]{:S(2)}) collective-permute-start(bf16[384,768]{1,0:T(8,128)(2,1)} %slice.65), channel_id=1, source_target_pairs={{0,4},{2,6},{4,0},{6,2},{8,12},{10,14},{12,8},{14,10},{16,20},{18,... | collective-permute-start | bytes 1769480 | tf_op jit(solution)/shard_map/ppermute | solution.py:690
  172.2 14.4 %collective-permute-start.15 = (bf16[4,16,48,768]{3,2,1,0:T(8,128)(2,1)}, bf16[4,16,48,768]{3,2,1,0:T(8,128)(2,1)S(1)}, u32[]{:S(2)}, u32[]{:S(2)}) collective-permute-start(bf16[4,16,48,768]{3,2,1,0:T(8,128)(2,1)} %shard_map.370.refs_2_.refs_5_), channel_id=1, source_target_pairs={{0,1},{1,0},{2,3},{3,2},{4,5},{5,4},{6,7},{7,6},{8,9},{9,8},{10,11... | collective-permute-start | bytes 14155784 | tf_op jit(solution)/shard_map/ppermute | solution.py:686
  201.6 7.3 %collective-permute-start.16 = (bf16[5,512,768]{2,1,0:T(8,128)(2,1)}, bf16[5,512,768]{2,1,0:T(8,128)(2,1)S(1)}, u32[]{:S(2)}, u32[]{:S(2)}) collective-permute-start(bf16[5,512,768]{2,1,0:T(8,128)(2,1)} %get-tuple-element.323.refs_0_), channel_id=1, source_target_pairs={{0,1},{1,0},{2,3},{3,2},{4,5},{5,4},{6,7},{7,6},{8,9},{9,8},{10,11... | collective-permute-start | bytes 11796488 | tf_op jit(solution)/shard_map/ppermute | solution.py:686
  207.8 73.9 %collective-permute-start.26 = (bf16[5,512,768]{2,1,0:T(8,128)(2,1)}, bf16[5,512,768]{2,1,0:T(8,128)(2,1)S(1)}, u32[]{:S(2)}, u32[]{:S(2)}) collective-permute-start(bf16[5,512,768]{2,1,0:T(8,128)(2,1)} %get-tuple-element.313.refs_4_.refs_0_), channel_id=1, source_target_pairs={{0,1},{1,0},{2,3},{3,2},{4,5},{5,4},{6,7},{7,6},{8,9},{9,8},{10,11... | collective-permute-start | bytes 11796488 | tf_op jit(solution)/shard_map/ppermute | solution.py:686
  208.3 34.4 %collective-permute-start.20 = (bf16[512,768]{1,0:T(8,128)(2,1)}, bf16[512,768]{1,0:T(8,128)(2,1)}, u32[]{:S(2)}, u32[]{:S(2)}) collective-permute-start(bf16[512,768]{1,0:T(8,128)(2,1)} %get-tuple-element.345.refs_4_), channel_id=1, source_target_pairs={{0,1},{1,0},{2,3},{3,2},{4,5},{5,4},{6,7},{7,6},{8,9},{9,8},{10,11... | collective-permute-start | bytes 2359304 | tf_op jit(solution)/shard_map/ppermute | solution.py:686
  220.4 22.3 %collective-permute-start.18 = (bf16[384,768]{1,0:T(8,128)(2,1)}, bf16[384,768]{1,0:T(8,128)(2,1)S(1)}, u32[]{:S(2)}, u32[]{:S(2)}) collective-permute-start(bf16[384,768]{1,0:T(8,128)(2,1)} %get-tuple-element.337), channel_id=1, source_target_pairs={{0,2},{2,0},{4,6},{6,4},{8,10},{10,8},{12,14},{14,12},{16,18},{18,... | collective-permute-start | bytes 1769480 | tf_op jit(solution)/shard_map/ppermute | solution.py:690
  221.1 21.6 %collective-permute-start.19 = (bf16[384,768]{1,0:T(8,128)(2,1)}, bf16[384,768]{1,0:T(8,128)(2,1)S(1)}, u32[]{:S(2)}, u32[]{:S(2)}) collective-permute-start(bf16[384,768]{1,0:T(8,128)(2,1)} %get-tuple-element.338), channel_id=1, source_target_pairs={{0,4},{2,6},{4,0},{6,2},{8,12},{10,14},{12,8},{14,10},{16,20},{18,... | collective-permute-start | bytes 1769480 | tf_op jit(solution)/shard_map/ppermute | solution.py:690
  224.1 18.5 %collective-permute-start.21 = (bf16[512,128]{1,0:T(8,128)(2,1)}, bf16[512,128]{1,0:T(8,128)(2,1)S(1)}, u32[]{:S(2)}, u32[]{:S(2)}) collective-permute-start(bf16[512,128]{1,0:T(8,128)(2,1)} %get-tuple-element.346.refs_5_), channel_id=1, source_target_pairs={{0,1},{1,0},{2,3},{3,2},{4,5},{5,4},{6,7},{7,6},{8,9},{9,8},{10,11... | collective-permute-start | bytes 393224 | tf_op jit(solution)/shard_map/ppermute | solution.py:686
  243.3 38.3 %collective-permute-start.27 = (bf16[2,512,768]{2,1,0:T(8,128)(2,1)S(1)}, bf16[2,512,768]{2,1,0:T(8,128)(2,1)S(1)}, u32[]{:S(2)}, u32[]{:S(2)}) collective-permute-start(bf16[2,512,768]{2,1,0:T(8,128)(2,1)S(1)} %copy-done.17), channel_id=1, source_target_pairs={{0,1},{1,0},{2,3},{3,2},{4,5},{5,4},{6,7},{7,6},{8,9},{9,8},{10,11... | collective-permute-start | bytes 4718600 | tf_op jit(solution)/shard_map/ppermute | solution.py:686
  243.5 38.2 %collective-permute-start.28 = (bf16[2,512,768]{2,1,0:T(8,128)(2,1)}, bf16[2,512,768]{2,1,0:T(8,128)(2,1)}, u32[]{:S(2)}, u32[]{:S(2)}) collective-permute-start(bf16[2,512,768]{2,1,0:T(8,128)(2,1)} %get-tuple-element.373.refs_0_), channel_id=1, source_target_pairs={{0,1},{1,0},{2,3},{3,2},{4,5},{5,4},{6,7},{7,6},{8,9},{9,8},{10,11... | collective-permute-start | bytes 4718600 | tf_op jit(solution)/shard_map/ppermute | solution.py:686
  257.6 24.1 %collective-permute-start.24 = (bf16[576,768]{1,0:T(8,128)(2,1)}, bf16[576,768]{1,0:T(8,128)(2,1)S(1)}, u32[]{:S(2)}, u32[]{:S(2)}) collective-permute-start(bf16[576,768]{1,0:T(8,128)(2,1)} %get-tuple-element.359), channel_id=1, source_target_pairs={{0,2},{2,0},{4,6},{6,4},{8,10},{10,8},{12,14},{14,12},{16,18},{18,... | collective-permute-start | bytes 2654216 | tf_op jit(solution)/shard_map/ppermute | solution.py:690
  258.2 23.5 %collective-permute-start.25 = (bf16[576,768]{1,0:T(8,128)(2,1)}, bf16[576,768]{1,0:T(8,128)(2,1)}, u32[]{:S(2)}, u32[]{:S(2)}) collective-permute-start(bf16[576,768]{1,0:T(8,128)(2,1)} %get-tuple-element.360), channel_id=1, source_target_pairs={{0,4},{2,6},{4,0},{6,2},{8,12},{10,14},{12,8},{14,10},{16,20},{18,... | collective-permute-start | bytes 2654216 | tf_op jit(solution)/shard_map/ppermute | solution.py:690
  281.7 8.5 %collective-permute-start.31 = (bf16[2,512,768]{2,1,0:T(8,128)(2,1)}, bf16[2,512,768]{2,1,0:T(8,128)(2,1)}, u32[]{:S(2)}, u32[]{:S(2)}) collective-permute-start(bf16[2,512,768]{2,1,0:T(8,128)(2,1)} %get-tuple-element.380), channel_id=1, source_target_pairs={{0,1},{1,0},{2,3},{3,2},{4,5},{5,4},{6,7},{7,6},{8,9},{9,8},{10,11... | collective-permute-start | bytes 4718600 | tf_op jit(solution)/shard_map/ppermute | solution.py:686
  281.8 8.4 %collective-permute-start.32 = (bf16[512,384]{1,0:T(8,128)(2,1)}, bf16[512,384]{1,0:T(8,128)(2,1)S(1)}, u32[]{:S(2)}, u32[]{:S(2)}) collective-permute-start(bf16[512,384]{1,0:T(8,128)(2,1)} %get-tuple-element.383), channel_id=1, source_target_pairs={{0,1},{1,0},{2,3},{3,2},{4,5},{5,4},{6,7},{7,6},{8,9},{9,8},{10,11... | collective-permute-start | bytes 1179656 | tf_op jit(solution)/shard_map/ppermute | solution.py:686
  288.1 17.8 %collective-permute-start.29 = (bf16[192,768]{1,0:T(8,128)(2,1)}, bf16[192,768]{1,0:T(8,128)(2,1)S(1)}, u32[]{:S(2)}, u32[]{:S(2)}) collective-permute-start(bf16[192,768]{1,0:T(8,128)(2,1)} %get-tuple-element.376), channel_id=1, source_target_pairs={{0,2},{2,0},{4,6},{6,4},{8,10},{10,8},{12,14},{14,12},{16,18},{18,... | collective-permute-start | bytes 884744 | tf_op jit(solution)/shard_map/ppermute | solution.py:690
  288.8 17.1 %collective-permute-start.30 = (bf16[192,768]{1,0:T(8,128)(2,1)}, bf16[192,768]{1,0:T(8,128)(2,1)S(1)}, u32[]{:S(2)}, u32[]{:S(2)}) collective-permute-start(bf16[192,768]{1,0:T(8,128)(2,1)} %get-tuple-element.377), channel_id=1, source_target_pairs={{0,4},{2,6},{4,0},{6,2},{8,12},{10,14},{12,8},{14,10},{16,20},{18,... | collective-permute-start | bytes 884744 | tf_op jit(solution)/shard_map/ppermute | solution.py:690
  305.9 29.3 %collective-permute-start.33 = (bf16[768,768]{1,0:T(8,128)(2,1)}, bf16[768,768]{1,0:T(8,128)(2,1)S(1)}, u32[]{:S(2)}, u32[]{:S(2)}) collective-permute-start(bf16[768,768]{1,0:T(8,128)(2,1)} %get-tuple-element.391), channel_id=1, source_target_pairs={{0,2},{2,0},{4,6},{6,4},{8,10},{10,8},{12,14},{14,12},{16,18},{18,... | collective-permute-start | bytes 3538952 | tf_op jit(solution)/shard_map/ppermute | solution.py:690
  306.6 28.7 %collective-permute-start.34 = (bf16[768,768]{1,0:T(8,128)(2,1)}, bf16[768,768]{1,0:T(8,128)(2,1)S(1)}, u32[]{:S(2)}, u32[]{:S(2)}) collective-permute-start(bf16[768,768]{1,0:T(8,128)(2,1)} %get-tuple-element.392), channel_id=1, source_target_pairs={{0,4},{2,6},{4,0},{6,2},{8,12},{10,14},{12,8},{14,10},{16,20},{18,... | collective-permute-start | bytes 3538952 | tf_op jit(solution)/shard_map/ppermute | solution.py:690
  307.9 27.3 %collective-permute-start.35 = (bf16[96,768]{1,0:T(8,128)(2,1)S(1)}, bf16[96,768]{1,0:T(8,128)(2,1)S(1)}, u32[]{:S(2)}, u32[]{:S(2)}) collective-permute-start(bf16[96,768]{1,0:T(8,128)(2,1)S(1)} %copy-done.81), channel_id=1, source_target_pairs={{0,8},{2,10},{4,12},{6,14},{8,0},{10,2},{12,4},{14,6},{16,24},{18,... | collective-permute-start | bytes 442376 | tf_op jit(solution)/shard_map/ppermute | solution.py:690
  314.5 20.8 %collective-permute-start.36 = (bf16[96,768]{1,0:T(8,128)(2,1)S(1)}, bf16[96,768]{1,0:T(8,128)(2,1)S(1)}, u32[]{:S(2)}, u32[]{:S(2)}) collective-permute-start(bf16[96,768]{1,0:T(8,128)(2,1)S(1)} %copy-done.80), channel_id=1, source_target_pairs={{0,16},{2,18},{4,20},{6,22},{8,24},{10,26},{12,28},{14,30},{16,0},... | collective-permute-start | bytes 442376 | tf_op jit(solution)/shard_map/ppermute | solution.py:690
  316.3 18.9 %collective-permute-start.37 = (bf16[96,768]{1,0:T(8,128)(2,1)S(1)}, bf16[96,768]{1,0:T(8,128)(2,1)S(1)}, u32[]{:S(2)}, u32[]{:S(2)}) collective-permute-start(bf16[96,768]{1,0:T(8,128)(2,1)S(1)} %copy-done.79), channel_id=1, source_target_pairs={{0,24},{2,26},{4,28},{6,30},{8,16},{10,18},{12,20},{14,22},{16,8},... | collective-permute-start | bytes 442376 | tf_op jit(solution)/shard_map/ppermute | solution.py:690
  354.1 32.9 %collective-permute-start.39 = (bf16[768,768]{1,0:T(8,128)(2,1)}, bf16[768,768]{1,0:T(8,128)(2,1)S(1)}, u32[]{:S(2)}, u32[]{:S(2)}) collective-permute-start(bf16[768,768]{1,0:T(8,128)(2,1)} %get-tuple-element.429), channel_id=1, source_target_pairs={{0,2},{2,0},{4,6},{6,4},{8,10},{10,8},{12,14},{14,12},{16,18},{18,... | collective-permute-start | bytes 3538952 | tf_op jit(solution)/shard_map/ppermute | solution.py:690
  355.6 31.4 %collective-permute-start.40 = (bf16[768,768]{1,0:T(8,128)(2,1)}, bf16[768,768]{1,0:T(8,128)(2,1)S(1)}, u32[]{:S(2)}, u32[]{:S(2)}) collective-permute-start(bf16[768,768]{1,0:T(8,128)(2,1)} %get-tuple-element.430), channel_id=1, source_target_pairs={{0,4},{2,6},{4,0},{6,2},{8,12},{10,14},{12,8},{14,10},{16,20},{18,... | collective-permute-start | bytes 3538952 | tf_op jit(solution)/shard_map/ppermute | solution.py:690
  356.2 30.7 %collective-permute-start.41 = (bf16[96,768]{1,0:T(8,128)(2,1)}, bf16[96,768]{1,0:T(8,128)(2,1)S(1)}, u32[]{:S(2)}, u32[]{:S(2)}) collective-permute-start(bf16[96,768]{1,0:T(8,128)(2,1)} %get-tuple-element.431), channel_id=1, source_target_pairs={{0,8},{2,10},{4,12},{6,14},{8,0},{10,2},{12,4},{14,6},{16,24},{18,... | collective-permute-start | bytes 442376 | tf_op jit(solution)/shard_map/ppermute | solution.py:690
  361.5 25.4 %collective-permute-start.42 = (bf16[96,768]{1,0:T(8,128)(2,1)}, bf16[96,768]{1,0:T(8,128)(2,1)S(1)}, u32[]{:S(2)}, u32[]{:S(2)}) collective-permute-start(bf16[96,768]{1,0:T(8,128)(2,1)} %get-tuple-element.432), channel_id=1, source_target_pairs={{0,16},{2,18},{4,20},{6,22},{8,24},{10,26},{12,28},{14,30},{16,0},... | collective-permute-start | bytes 442376 | tf_op jit(solution)/shard_map/ppermute | solution.py:690
  363.3 23.7 %collective-permute-start.43 = (bf16[96,768]{1,0:T(8,128)(2,1)}, bf16[96,768]{1,0:T(8,128)(2,1)S(1)}, u32[]{:S(2)}, u32[]{:S(2)}) collective-permute-start(bf16[96,768]{1,0:T(8,128)(2,1)} %get-tuple-element.433), channel_id=1, source_target_pairs={{0,24},{2,26},{4,28},{6,30},{8,16},{10,18},{12,20},{14,22},{16,8},... | collective-permute-start | bytes 442376 | tf_op jit(solution)/shard_map/ppermute | solution.py:690
  387.0 10.5 %collective-permute-start.46 = (bf16[2,512,768]{2,1,0:T(8,128)(2,1)}, bf16[2,512,768]{2,1,0:T(8,128)(2,1)S(1)}, u32[]{:S(2)}, u32[]{:S(2)}) collective-permute-start(bf16[2,512,768]{2,1,0:T(8,128)(2,1)} %get-tuple-element.454), channel_id=1, source_target_pairs={{0,1},{1,0},{2,3},{3,2},{4,5},{5,4},{6,7},{7,6},{8,9},{9,8},{10,11... | collective-permute-start | bytes 4718600 | tf_op jit(solution)/shard_map/ppermute | solution.py:686
  387.1 10.4 %collective-permute-start.47 = (bf16[512,768]{1,0:T(8,128)(2,1)}, bf16[512,768]{1,0:T(8,128)(2,1)S(1)}, u32[]{:S(2)}, u32[]{:S(2)}) collective-permute-start(bf16[512,768]{1,0:T(8,128)(2,1)} %get-tuple-element.457.refs_8_), channel_id=1, source_target_pairs={{0,1},{1,0},{2,3},{3,2},{4,5},{5,4},{6,7},{7,6},{8,9},{9,8},{10,11... | collective-permute-start | bytes 2359304 | tf_op jit(solution)/shard_map/ppermute | solution.py:686
  393.6 16.0 %collective-permute-start.44 = (bf16[192,768]{1,0:T(8,128)(2,1)}, bf16[192,768]{1,0:T(8,128)(2,1)S(1)}, u32[]{:S(2)}, u32[]{:S(2)}) collective-permute-start(bf16[192,768]{1,0:T(8,128)(2,1)} %get-tuple-element.450), channel_id=1, source_target_pairs={{0,2},{2,0},{4,6},{6,4},{8,10},{10,8},{12,14},{14,12},{16,18},{18,... | collective-permute-start | bytes 884744 | tf_op jit(solution)/shard_map/ppermute | solution.py:690
  394.2 15.4 %collective-permute-start.45 = (bf16[192,768]{1,0:T(8,128)(2,1)}, bf16[192,768]{1,0:T(8,128)(2,1)S(1)}, u32[]{:S(2)}, u32[]{:S(2)}) collective-permute-start(bf16[192,768]{1,0:T(8,128)(2,1)} %get-tuple-element.451), channel_id=1, source_target_pairs={{0,4},{2,6},{4,0},{6,2},{8,12},{10,14},{12,8},{14,10},{16,20},{18,... | collective-permute-start | bytes 884744 | tf_op jit(solution)/shard_map/ppermute | solution.py:690
  409.6 26.9 %collective-permute-start.50 = (bf16[448,768]{1,0:T(8,128)(2,1)}, bf16[448,768]{1,0:T(8,128)(2,1)S(1)}, u32[]{:S(2)}, u32[]{:S(2)}) collective-permute-start(bf16[448,768]{1,0:T(8,128)(2,1)} %get-tuple-element.475), channel_id=1, source_target_pairs={{0,2},{2,0},{4,6},{6,4},{8,10},{10,8},{12,14},{14,12},{16,18},{18,... | collective-permute-start | bytes 2064392 | tf_op jit(solution)/shard_map/ppermute | solution.py:690
  411.0 25.5 %collective-permute-start.51 = (bf16[384,768]{1,0:T(8,128)(2,1)}, bf16[384,768]{1,0:T(8,128)(2,1)S(1)}, u32[]{:S(2)}, u32[]{:S(2)}) collective-permute-start(bf16[384,768]{1,0:T(8,128)(2,1)} %get-tuple-element.476), channel_id=1, source_target_pairs={{0,4},{2,6},{4,0},{6,2},{8,12},{10,14},{12,8},{14,10},{16,20},{18,... | collective-permute-start | bytes 1769480 | tf_op jit(solution)/shard_map/ppermute | solution.py:690
  412.5 14.3 %collective-permute-start.52 = (bf16[192,768]{1,0:T(8,128)(2,1)S(1)}, bf16[192,768]{1,0:T(8,128)(2,1)S(1)}, u32[]{:S(2)}, u32[]{:S(2)}) collective-permute-start(bf16[192,768]{1,0:T(8,128)(2,1)S(1)} %copy-done.78), channel_id=1, source_target_pairs={{0,8},{2,10},{4,12},{6,14},{8,0},{10,2},{12,4},{14,6},{16,24},{18,... | collective-permute-start | bytes 884744 | tf_op jit(solution)/shard_map/ppermute | solution.py:690
  413.1 23.5 %collective-permute-start.53 = (bf16[192,768]{1,0:T(8,128)(2,1)S(1)}, bf16[192,768]{1,0:T(8,128)(2,1)S(1)}, u32[]{:S(2)}, u32[]{:S(2)}) collective-permute-start(bf16[192,768]{1,0:T(8,128)(2,1)S(1)} %copy-done.77), channel_id=1, source_target_pairs={{0,16},{2,18},{4,20},{6,22},{8,24},{10,26},{12,28},{14,30},{16,0},... | collective-permute-start | bytes 884744 | tf_op jit(solution)/shard_map/ppermute | solution.py:690
  415.4 21.2 %collective-permute-start.54 = (bf16[192,768]{1,0:T(8,128)(2,1)S(1)}, bf16[192,768]{1,0:T(8,128)(2,1)S(1)}, u32[]{:S(2)}, u32[]{:S(2)}) collective-permute-start(bf16[192,768]{1,0:T(8,128)(2,1)S(1)} %copy-done.76), channel_id=1, source_target_pairs={{0,24},{2,26},{4,28},{6,30},{8,16},{10,18},{12,20},{14,22},{16,8},... | collective-permute-start | bytes 884744 | tf_op jit(solution)/shard_map/ppermute | solution.py:690
  440.3 20.0 %collective-permute-start.56 = (bf16[256,768]{1,0:T(8,128)(2,1)S(1)}, bf16[256,768]{1,0:T(8,128)(2,1)S(1)}, u32[]{:S(2)}, u32[]{:S(2)}) collective-permute-start(bf16[256,768]{1,0:T(8,128)(2,1)S(1)} %get-tuple-element.503), channel_id=1, source_target_pairs={{0,4},{2,6},{4,0},{6,2},{8,12},{10,14},{12,8},{14,10},{16,20},{18,... | collective-permute-start | bytes 1179656 | tf_op jit(solution)/shard_map/ppermute | solution.py:690
  441.8 18.6 %collective-permute-start.55 = (bf16[192,768]{1,0:T(8,128)(2,1)S(1)}, bf16[192,768]{1,0:T(8,128)(2,1)S(1)}, u32[]{:S(2)}, u32[]{:S(2)}) collective-permute-start(bf16[192,768]{1,0:T(8,128)(2,1)S(1)} %get-tuple-element.502), channel_id=1, source_target_pairs={{0,2},{2,0},{4,6},{6,4},{8,10},{10,8},{12,14},{14,12},{16,18},{18,... | collective-permute-start | bytes 884744 | tf_op jit(solution)/shard_map/ppermute | solution.py:690
  442.4 9.5 %collective-permute-start.57 = (bf16[96,768]{1,0:T(8,128)(2,1)S(1)}, bf16[96,768]{1,0:T(8,128)(2,1)S(1)}, u32[]{:S(2)}, u32[]{:S(2)}) collective-permute-start(bf16[96,768]{1,0:T(8,128)(2,1)S(1)} %get-tuple-element.504), channel_id=1, source_target_pairs={{0,8},{2,10},{4,12},{6,14},{8,0},{10,2},{12,4},{14,6},{16,24},{18,... | collective-permute-start | bytes 442376 | tf_op jit(solution)/shard_map/ppermute | solution.py:690
  447.7 12.7 %collective-permute-start.58 = (bf16[96,768]{1,0:T(8,128)(2,1)S(1)}, bf16[96,768]{1,0:T(8,128)(2,1)S(1)}, u32[]{:S(2)}, u32[]{:S(2)}) collective-permute-start(bf16[96,768]{1,0:T(8,128)(2,1)S(1)} %get-tuple-element.505), channel_id=1, source_target_pairs={{0,16},{2,18},{4,20},{6,22},{8,24},{10,26},{12,28},{14,30},{16,0},... | collective-permute-start | bytes 442376 | tf_op jit(solution)/shard_map/ppermute | solution.py:690
  449.5 10.9 %collective-permute-start.59 = (bf16[96,768]{1,0:T(8,128)(2,1)S(1)}, bf16[96,768]{1,0:T(8,128)(2,1)S(1)}, u32[]{:S(2)}, u32[]{:S(2)}) collective-permute-start(bf16[96,768]{1,0:T(8,128)(2,1)S(1)} %get-tuple-element.506), channel_id=1, source_target_pairs={{0,24},{2,26},{4,28},{6,30},{8,16},{10,18},{12,20},{14,22},{16,8},... | collective-permute-start | bytes 442376 | tf_op jit(solution)/shard_map/ppermute | solution.py:690
  461.2 18.3 %collective-permute-start.63 = (f32[1,2,48,768]{3,2,1,0:T(8,128)S(1)}, f32[1,2,48,768]{3,2,1,0:T(8,128)S(1)}, u32[]{:S(2)}, u32[]{:S(2)}) collective-permute-start(f32[1,2,48,768]{3,2,1,0:T(8,128)S(1)} %copy-done.41), channel_id=1, source_target_pairs={{0,1},{1,0},{2,3},{3,2},{4,5},{5,4},{6,7},{7,6},{8,9},{9,8},{10,11... | collective-permute-start | bytes 884744 | tf_op jit(solution)/shard_map/ppermute | solution.py:686
  461.2 18.2 %collective-permute-start.64 = (f32[1,2,48,768]{3,2,1,0:T(8,128)S(1)}, f32[1,2,48,768]{3,2,1,0:T(8,128)S(1)}, u32[]{:S(2)}, u32[]{:S(2)}) collective-permute-start(f32[1,2,48,768]{3,2,1,0:T(8,128)S(1)} %copy-done.42), channel_id=1, source_target_pairs={{0,1},{1,0},{2,3},{3,2},{4,5},{5,4},{6,7},{7,6},{8,9},{9,8},{10,11... | collective-permute-start | bytes 884744 | tf_op jit(solution)/shard_map/ppermute | solution.py:686
  461.7 9.8 %collective-permute-start.60 = (bf16[112,768]{1,0:T(8,128)(2,1)S(1)}, bf16[112,768]{1,0:T(8,128)(2,1)S(1)}, u32[]{:S(2)}, u32[]{:S(2)}) collective-permute-start(bf16[112,768]{1,0:T(8,128)(2,1)S(1)} %get-tuple-element.525), channel_id=1, source_target_pairs={{0,8},{2,10},{4,12},{6,14},{8,0},{10,2},{12,4},{14,6},{16,24},{18,... | collective-permute-start | bytes 516104 | tf_op jit(solution)/shard_map/ppermute | solution.py:690
  463.9 15.5 %collective-permute-start.61 = (bf16[112,768]{1,0:T(8,128)(2,1)S(1)}, bf16[112,768]{1,0:T(8,128)(2,1)S(1)}, u32[]{:S(2)}, u32[]{:S(2)}) collective-permute-start(bf16[112,768]{1,0:T(8,128)(2,1)S(1)} %get-tuple-element.526), channel_id=1, source_target_pairs={{0,16},{2,18},{4,20},{6,22},{8,24},{10,26},{12,28},{14,30},{16,0},... | collective-permute-start | bytes 516104 | tf_op jit(solution)/shard_map/ppermute | solution.py:690
  464.9 14.5 %collective-permute-start.62 = (bf16[112,768]{1,0:T(8,128)(2,1)S(1)}, bf16[112,768]{1,0:T(8,128)(2,1)S(1)}, u32[]{:S(2)}, u32[]{:S(2)}) collective-permute-start(bf16[112,768]{1,0:T(8,128)(2,1)S(1)} %get-tuple-element.527), channel_id=1, source_target_pairs={{0,24},{2,26},{4,28},{6,30},{8,16},{10,18},{12,20},{14,22},{16,8},... | collective-permute-start | bytes 516104 | tf_op jit(solution)/shard_map/ppermute | solution.py:690
  471.5 27.2 %collective-permute-start.73 = (f32[2,2,48,768]{3,2,1,0:T(8,128)S(1)}, f32[2,2,48,768]{3,2,1,0:T(8,128)S(1)}, u32[]{:S(2)}, u32[]{:S(2)}) collective-permute-start(f32[2,2,48,768]{3,2,1,0:T(8,128)S(1)} %get-tuple-element.537.refs_5_), channel_id=1, source_target_pairs={{0,1},{1,0},{2,3},{3,2},{4,5},{5,4},{6,7},{7,6},{8,9},{9,8},{10,11... | collective-permute-start | bytes 1769480 | tf_op jit(solution)/shard_map/ppermute | solution.py:686
  488.5 5.6 %collective-permute-start.69 = (f32[1,128]{1,0:T(1,128)S(1)}, f32[1,128]{1,0:T(1,128)S(1)}, u32[]{:S(2)}, u32[]{:S(2)}) collective-permute-start(f32[1,128]{1,0:T(1,128)S(1)} %add_add_fusion.1), channel_id=1, source_target_pairs={{0,8},{2,10},{4,12},{6,14},{8,0},{10,2},{12,4},{14,6},{16,24},{18,... | collective-permute-start | bytes 1544 | tf_op jit(solution)/shard_map/ppermute | solution.py:690
  492.7 5.3 %collective-permute-start.71 = (f32[1,128]{1,0:T(1,128)S(1)}, f32[1,128]{1,0:T(1,128)S(1)}, u32[]{:S(2)}, u32[]{:S(2)}) collective-permute-start(f32[1,128]{1,0:T(1,128)S(1)} %add_add_fusion.1), channel_id=1, source_target_pairs={{0,24},{2,26},{4,28},{6,30},{8,16},{10,18},{12,20},{14,22},{16,8},... | collective-permute-start | bytes 1544 | tf_op jit(solution)/shard_map/ppermute | solution.py:690
  494.1 4.6 collective-permute-start.75
  (95 other events, 965.2 us)
Sparse Core Ops, SparseCore 0:
  13.2 138.7 all-gather.1
